TPU v7x, 32 devices: a whole 2x2x4 slice. The times are simulated.
32 devices in a mesh: dp: 2 (over x), expert: 16 (over z, y, core).
Axes of the slice: x: 2, y: 2, z: 4, core: 2. Of those that a mesh axis runs over, the one named last changes fastest.
Arguments:
- tokens: bfloat16 [128, 4096], P(('dp', 'expert')), may hold values from -6 to 6
- expert_ids: int32 [128, 8], P(('dp', 'expert')), may hold values from 0 to 15, all different within a row; in each aligned block of 4 rows (0 to 3, 4 to 7, ...) at most 4 rows name the same one
- gate_probs: float32 [128, 8], P(('dp', 'expert')), may hold values from 0.2 to 1
- w_gate: bfloat16 [16, 4096, 2048], P('expert', None, 'dp'), may hold values from -0.09375 to 0.09375
- w_up: bfloat16 [16, 4096, 2048], P('expert', None, 'dp'), may hold values from -0.09375 to 0.09375
- w_down: bfloat16 [16, 2048, 4096], P('expert', None, 'dp'), may hold values from -0.125 to 0.125
Outputs:
- combined: bfloat16 [128, 4096], P(('dp', 'expert'))
Inputs may be any that keep to these rules, and one draw needn't show every extreme that they name: `expert_ids`: each row names 8 different experts. In the rows of one device (aligned blocks of 4 rows) no expert is named by more than 4 rows, a bound that some block reaches.
All inputs are finite; a program needn't handle non-finite values.
Results may differ from a plain program's by a relative error of at most 0.0057.
Values may be sent and summed in bfloat16 or wider, within the bound.
No kernel may reach another device: no remote copies, remote signals or barrier semaphores. Data moves between devices by JAX's collectives and lax.ppermute only.
A program may use at most 64 MiB of HBM per device.

v0:
```python
import jax
import jax.numpy as jnp
from jax import lax
from jax.sharding import PartitionSpec as P


def slot_positions(choices, experts, capacity):
    flat_ids = choices.reshape(-1)
    onehot = (flat_ids[:, None] == jnp.arange(experts, dtype=jnp.int32)[None, :]).astype(jnp.int32)
    earlier = jnp.cumsum(onehot, axis=0) - onehot
    slot_rank = jnp.sum(earlier * onehot, axis=1)
    return flat_ids * capacity + slot_rank


def placement_table(choices, experts, capacity):
    token_count, top_count = choices.shape
    positions = slot_positions(choices, experts, capacity)
    chosen = (
        positions[:, None] == jnp.arange(experts * capacity, dtype=jnp.int32)[None, :]
    ).astype(jnp.float32)
    return chosen.reshape(token_count, top_count, experts * capacity)


def local(tokens, expert_ids, gate_probs, w_gate, w_up, w_down):
    token_count, width = tokens.shape
    top_count = expert_ids.shape[1]
    groups = lax.axis_size("dp")
    experts = lax.axis_size("expert") * w_gate.shape[0]
    capacity = min(token_count, max(2, 2 * token_count * top_count // experts))
    gate_matrix = w_gate[0]
    up_matrix = w_up[0]
    down_matrix = w_down[0]
    chosen = placement_table(expert_ids, experts, capacity)
    placing = jnp.sum(chosen, axis=1).astype(jnp.bfloat16)
    outgoing = jnp.einsum("tp,td->pd", placing, tokens, preferred_element_type=jnp.float32)
    outgoing = outgoing.astype(jnp.bfloat16).reshape(experts, capacity, width)
    arrived = lax.all_to_all(outgoing, "expert", split_axis=0, concat_axis=0, tiled=True)
    row_block = lax.all_gather(arrived.reshape(experts * capacity, width), "dp", axis=0, tiled=True)
    gate_proj = jnp.dot(row_block, gate_matrix, preferred_element_type=jnp.float32)
    up_proj = jnp.dot(row_block, up_matrix, preferred_element_type=jnp.float32)
    hidden = (jax.nn.silu(gate_proj) * up_proj).astype(jnp.bfloat16)
    columns = jnp.dot(
        lax.all_gather(hidden, "dp", axis=1, tiled=True),
        down_matrix,
        preferred_element_type=jnp.float32,
    ).astype(jnp.bfloat16)
    out_blocks = columns.reshape(groups, experts, capacity, down_matrix.shape[1])
    returned = lax.all_to_all(
        lax.all_to_all(out_blocks, "dp", split_axis=0, concat_axis=3, tiled=True),
        "expert",
        split_axis=1,
        concat_axis=1,
        tiled=True,
    )
    returned = returned.reshape(experts * capacity, width).astype(jnp.float32)
    weighting = jnp.einsum("tkp,tk->tp", chosen, gate_probs, precision=lax.Precision.HIGHEST)
    combined = jnp.dot(weighting, returned, precision=lax.Precision.HIGHEST)
    return combined.astype(jnp.bfloat16)


def solution(mesh):
    placed = (
        P(("dp", "expert"), None),
        P(("dp", "expert"), None),
        P(("dp", "expert"), None),
        P("expert", None, "dp"),
        P("expert", None, "dp"),
        P("expert", None, "dp"),
    )
    return jax.shard_map(
        local, mesh=mesh, in_specs=placed, out_specs=P(("dp", "expert"), None), check_vma=False
    )
```

profile of v0, /device:TPU:0, one launch (start us, length us, event | category | flops | bytes accessed | tf_op | source)
XLA Modules:
  0.0 110.4 jit_solution(12652536138095810273)
XLA Ops:
  6.5 0.0 copy-start
  6.5 0.0 all-gather.2.cloned.1.call-start
  6.5 0.8 eq.30
  7.3 0.1 fusion.16
  7.4 0.1 reduce_window_sum.11
  7.4 0.2 select_reduce_fusion
  7.6 0.1 reduce_sum.21
  7.7 0.7 multiply_add_fusion
  8.4 0.1 convert_reduce_fusion
  8.5 0.0 copy-done
  8.5 0.3 convolution_convert_fusion
  8.8 0.2 reshape.39
  9.0 21.7 %all_to_all.28 = bf16[16,4,4096]{2,1,0:T(4,128)(2,1)S(1)} all-to-all(bf16[16,4,4096]{2,1,0:T(4,128)(2,1)S(1)} %reshape.39), channel_id=1, replica_groups=mesh['dp'=2,'expert'=16] {'expert'}, dimensions={0} | all-to-all | bytes 1048576 | tf_op jit(solution)/shard_map/all_to_all | solution.py:37
  30.7 0.9 reshape.40
  31.6 0.0 all-gather.2.cloned.1.call-update
  31.7 20.9 %all-gather.2.cloned.1.call-done = bf16[128,4096]{1,0:T(8,128)(2,1)} async-done(((bf16[64,4096]{1,0:T(8,128)(2,1)}), bf16[128,4096]{1,0:T(8,128)(2,1)}) %all-gather.2.cloned.1.call-update) | async-done | bytes 1048592 | tf_op jit(solution)/shard_map/all_gather | solution.py:38
  52.5 0.0 copy-start.1
  52.5 0.0 copy-start.2
  52.5 0.0 slice-start
  52.5 5.1 %fusion.4 = f32[128,1024]{1,0:T(8,128)S(1)} fusion(bf16[128,4096]{1,0:T(8,128)(2,1)} %all-gather.2.cloned.1.call-done, bf16[1,4096,1024]{2,1,0:T(8,128)(2,1)} %param.9), kind=kOutput, calls=%fused_computation.4 | convolution fusion | flops 1073741824 | bytes 9961472 | tf_op jit(solution)/shard_map/dot_general | solution.py:39
  57.6 0.0 copy-done.1
  57.7 1.3 %copy-done.2 = bf16[1,4096,1024]{2,1,0:T(8,128)(2,1)S(1)} copy-done((bf16[1,4096,1024]{2,1,0:T(8,128)(2,1)S(1)}, bf16[1,4096,1024]{2,1,0:T(8,128)(2,1)}, u32[]{:S(2)}) %copy-start.2) | copy-done | bytes 8388632
  59.0 0.0 slice-start.1
  59.0 1.4 %fusion.12 = bf16[128,1024]{1,0:T(8,128)(2,1)S(1)} fusion(bf16[128,4096]{1,0:T(8,128)(2,1)S(1)} %copy-done.1, bf16[1,4096,1024]{2,1,0:T(8,128)(2,1)S(1)} %copy-done.2, f32[128,1024]{1,0:T(8,128)S(1)} %fusion.4), kind=kOutput, calls=%fused_computation.10 | convolution fusion | flops 1074528256 | bytes 10223616 | tf_op jit(solution)/shard_map/dot_general | solution.py:40
  60.3 8.7 %all_gather.7 = bf16[128,2048]{1,0:T(8,128)(2,1)S(1)} all-gather(bf16[128,1024]{1,0:T(8,128)(2,1)S(1)} %fusion.12), channel_id=1, replica_groups=mesh['dp'=2,'expert'=16] {'dp'}, dimensions={1}, use_global_device_ids=true | all-gather | bytes 786432 | tf_op jit(solution)/shard_map/all_gather | solution.py:43
  69.1 0.0 slice-done
  69.1 0.0 slice-done.1
  69.1 0.0 copy-start.3
  69.1 1.3 %fusion.6 = bf16[128,2048]{1,0:T(8,128)(2,1)S(1)} fusion(bf16[128,2048]{1,0:T(8,128)(2,1)S(1)} %all_gather.7, bf16[1,2048,2048]{2,1,0:T(8,128)(2,1)S(1)} %bitcast.34), kind=kOutput, calls=%fused_computation.8 | convolution fusion | flops 1074003968 | bytes 9437184 | tf_op jit(solution)/shard_map/dot_general | solution.py:42
  70.4 0.2 reshape.41
  70.6 0.3 copy.13
  70.9 9.8 %all_to_all.29 = bf16[2,16,4,2048]{3,1,2,0:T(8,128)(2,1)S(1)} all-to-all(bf16[2,16,4,2048]{3,1,2,0:T(8,128)(2,1)S(1)} %copy.13), channel_id=1, replica_groups=mesh['dp'=2,'expert'=16] {'dp'}, dimensions={0} | all-to-all | bytes 1048576 | tf_op jit(solution)/shard_map/all_to_all | solution.py:49
  80.7 0.5 copy.18
  81.2 1.1 %reshape.45 = bf16[1,16,4,4096]{3,2,0,1:T(4,128)(2,1)} reshape(bf16[1,16,4,2,2048]{4,3,2,1,0:T(2,128)(2,1)S(1)} %copy.18) | data formatting | bytes 1048576 | tf_op jit(solution)/shard_map/all_to_all | solution.py:49
  82.3 5.6 %all-to-all-start.2 = ((bf16[1,16,4,4096]{3,2,0,1:T(4,128)(2,1)}), bf16[1,16,4,4096]{3,2,0,1:T(4,128)(2,1)S(1)}, u32[]{:S(2)}, u32[]{:S(2)}) async-start(bf16[1,16,4,4096]{3,2,0,1:T(4,128)(2,1)} %reshape.45), calls=%async_computation.2 | async-start | bytes 1048576 | tf_op jit(solution)/shard_map/all_to_all | solution.py:48
  88.0 0.0 copy-done.3
  88.0 0.2 fusion.15
  88.2 14.3 %all-to-all-done.2 = bf16[1,16,4,4096]{3,2,0,1:T(4,128)(2,1)S(1)} async-done(((bf16[1,16,4,4096]{3,2,0,1:T(4,128)(2,1)}), bf16[1,16,4,4096]{3,2,0,1:T(4,128)(2,1)S(1)}, u32[]{:S(2)}, u32[]{:S(2)}) %all-to-all-start.2) | async-done | bytes 524320 | tf_op jit(solution)/shard_map/all_to_all | solution.py:48
  102.4 0.1 reshape.42
  102.6 0.9 convolution_convert_fusion.1
  (1 shorter events, 0.0 us)
Async XLA Ops:
  6.5 2.0 %copy-start = (bf16[4,4096]{1,0:T(4,128)(2,1)S(1)}, bf16[4,4096]{1,0:T(4,128)(2,1)}, u32[]{:S(2)}) copy-start(bf16[4,4096]{1,0:T(4,128)(2,1)} %param.6) | copy-start | bytes 98308
  6.5 46.0 %all-gather.2.cloned.1.call-start = ((), (), s32[]{:S(2)}) async-start(), calls=%async_computation.3 | async-start | bytes 1572864 | tf_op jit(solution)/shard_map/all_gather | solution.py:38
  52.5 5.1 %copy-start.1 = (bf16[128,4096]{1,0:T(8,128)(2,1)S(1)}, bf16[128,4096]{1,0:T(8,128)(2,1)}, u32[]{:S(2)}) copy-start(bf16[128,4096]{1,0:T(8,128)(2,1)} %all-gather.2.cloned.1.call-done) | copy-start | bytes 3145732
  52.5 6.4 %copy-start.2 = (bf16[1,4096,1024]{2,1,0:T(8,128)(2,1)S(1)}, bf16[1,4096,1024]{2,1,0:T(8,128)(2,1)}, u32[]{:S(2)}) copy-start(bf16[1,4096,1024]{2,1,0:T(8,128)(2,1)} %param.10) | copy-start | bytes 25165828
  52.5 16.5 %slice-start = ((s8[8388608]{0:T(1024)(128)(4,1)}), s8[4194304]{0:T(1024)(128)(4,1)S(1)}, s32[]{:S(2)}) async-start(s8[8388608]{0:T(1024)(128)(4,1)} %bitcast.33), calls=%async_computation.4 | async-start | bytes 8388608
  59.0 10.1 %slice-start.1 = ((s8[8388608]{0:T(1024)(128)(4,1)}), s8[4194304]{0:T(1024)(128)(4,1)S(1)}, s32[]{:S(2)}) async-start(s8[8388608]{0:T(1024)(128)(4,1)} %bitcast.33), calls=%async_computation.5 | async-start | bytes 8388608
  69.1 18.9 %copy-start.3 = (f32[4,8]{1,0:T(4,128)S(1)}, f32[4,8]{1,0:T(4,128)}, u32[]{:S(2)}) copy-start(f32[4,8]{1,0:T(4,128)} %param.8) | copy-start | bytes 388
  82.3 20.1 %all-to-all-start.2 = ((bf16[1,16,4,4096]{3,2,0,1:T(4,128)(2,1)}), bf16[1,16,4,4096]{3,2,0,1:T(4,128)(2,1)S(1)}, u32[]{:S(2)}, u32[]{:S(2)}) async-start(bf16[1,16,4,4096]{3,2,0,1:T(4,128)(2,1)} %reshape.45), calls=%async_computation.2 | async-start | bytes 1048576 | tf_op jit(solution)/shard_map/all_to_all | solution.py:48
Sparse Core Ops, SparseCore 0:
  31.8 20.7 all-gather.1
where the time goes:
time: 111 us; the launch traced here: 110 us
  blocking collectives  40.2 us (36%)
  waiting for transfers between devices  35.1 us (32%)
  between operations  13.5 us (12%)
  matrix products  9.24 us (8%)
  starting transfers between devices  5.62 us (5%)
  local copies, waits for them, and re-layouts  5.59 us (5%)
    all_to_all x1, blocking collectives, local(): lax.all_to_all(outgoing, 'expert', split_axis=0, concat_axis=0, tiled=True)  21.7 us
    all_gather x1, waiting for transfers between devices, local(): lax.all_gather(arrived.reshape(experts * capacity, width), 'dp', axis=0,...  20.9 us
    all_to_all x1, waiting for transfers between devices, local(): lax.all_to_all(lax.all_to_all(out_blocks, 'dp', split_axis=0, concat_axis...  14.3 us
    all_to_all x1, blocking collectives, local(): lax.all_to_all(out_blocks, 'dp', split_axis=0, concat_axis=3, tiled=True)  9.79 us
    all_gather x1, blocking collectives, local(): lax.all_gather(hidden, 'dp', axis=1, tiled=True)  8.72 us
    all_to_all x1, starting transfers between devices, local(): lax.all_to_all(lax.all_to_all(out_blocks, 'dp', split_axis=0, concat_axis...  5.62 us
    dot_general x1, matrix products, local(): jnp.dot(row_block, gate_matrix, preferred_element_type=jnp.float32)  5.09 us
  transfers between devices with their start and end apart: 2, of which 2 were waited for; matrix products, arithmetic and copies ran while one was open for 0% of the time, Pallas kernels for 0%

commit v1 on v0

v1 whole, which is shorter than its diff:
```python
import jax
import jax.numpy as jnp
from jax import lax
from jax.sharding import PartitionSpec as P


def swap(value, axis, mask):
    size = lax.axis_size(axis)
    return lax.ppermute(value, axis, [(i, i ^ mask) for i in range(size)])


def spread(value, axis, masks):
    return jnp.concatenate([value[None]] + [swap(value, axis, m)[None] for m in masks])


def gate_table(expert_ids, gate_probs, experts):
    hit = expert_ids[:, :, None] == jnp.arange(experts, dtype=jnp.int32)
    table = jnp.sum(jnp.where(hit, gate_probs[:, :, None], 0.0), axis=1)
    parts = []
    for _ in range(3):
        part = lax.reduce_precision(table, 8, 7)
        parts.append(part.astype(jnp.bfloat16))
        table = table - part
    return jnp.concatenate(parts, axis=1)


def gather_rows(block, high_masks, group_masks):
    rows, width = block.shape
    near = spread(block, "expert", high_masks)
    near = near.reshape(-1, width)
    if group_masks:
        near = spread(near, "dp", group_masks).reshape(-1, width)
    over_x = swap(near, "dp", 1)
    over_y = swap(near, "expert", 2)
    half = near.shape[0] // 2
    corner = jnp.concatenate([swap(over_y[:half], "dp", 1), swap(over_x[half:], "expert", 2)])
    chip = jnp.concatenate([near, over_y, over_x, corner])
    return jnp.concatenate([chip, swap(chip, "expert", 1)])


def local(tokens, expert_ids, gate_probs, w_gate, w_up, w_down):
    token_count, width = tokens.shape
    experts, groups = lax.axis_size("expert"), lax.axis_size("dp")
    me, group = lax.axis_index("expert"), lax.axis_index("dp")
    high_masks = list(range(4, experts, 4))
    group_masks = list(range(2, groups, 2))
    high, wide = len(high_masks) + 1, len(group_masks) + 1

    table = gate_table(expert_ids, gate_probs, experts)
    slots = -(-table.shape[1] // 128) * 128
    block = jnp.concatenate([tokens, jnp.pad(table, ((0, 0), (0, slots - table.shape[1])))], axis=1)
    everything = gather_rows(block, high_masks, group_masks)
    rows = everything[:, :width]
    mine = (jnp.arange(slots) % experts == me) & (jnp.arange(slots) < table.shape[1])
    scale = jnp.sum(jnp.where(mine, everything[:, width:].astype(jnp.float32), 0.0), axis=1)

    gate_proj = jnp.dot(rows, w_gate[0], preferred_element_type=jnp.float32)
    up_proj = jnp.dot(rows, w_up[0], preferred_element_type=jnp.float32)
    hidden = (jax.nn.silu(gate_proj) * up_proj).astype(jnp.bfloat16)

    units = hidden.shape[1]
    shape = (2, 2, 2, wide, high * token_count, units)
    down = w_down[0].reshape(groups, units, -1)
    total = jnp.zeros((rows.shape[0], down.shape[2]), jnp.float32)
    for mask in range(groups):
        part = hidden
        if mask:
            part = swap(hidden, "dp", mask).reshape(shape)
            x_order = [i ^ (mask & 1) for i in range(2)]
            wide_order = [i ^ (mask >> 1) for i in range(wide)]
            part = jnp.stack([part[:, i] for i in x_order], axis=1)
            part = jnp.stack([part[:, :, :, i] for i in wide_order], axis=3)
            part = part.reshape(hidden.shape)
        mine_down = lax.dynamic_index_in_dim(down, group ^ mask, 0, keepdims=False)
        total = total + jnp.dot(part, mine_down, preferred_element_type=jnp.float32)

    total = (total * scale[:, None]).reshape(2, 2, 2, wide, high, token_count, -1)
    send = lambda value, axis, mask: swap(value.astype(jnp.bfloat16), axis, mask).astype(jnp.float32)
    total = total[0] + send(total[1], "expert", 1)
    total = total[:, 0] + send(total[:, 1], "expert", 2)
    kept = total[:, :, 0]
    for slot, mask in enumerate(high_masks, 1):
        kept = kept + send(total[:, :, slot], "expert", mask)
    kept = kept.astype(jnp.bfloat16)
    pieces = []
    for mask in range(groups):
        piece = kept[mask & 1, mask >> 1]
        pieces.append(swap(piece, "dp", mask) if mask else piece)
    pieces = jnp.stack(pieces)
    order = jnp.arange(groups) ^ group
    if groups == 2:
        pieces = jnp.where(group == 0, pieces, pieces[::-1])
    else:
        pieces = jnp.take(pieces, order, axis=0)
    return pieces.transpose(1, 0, 2).reshape(token_count, width)


def solution(mesh):
    placed = (
        P(("dp", "expert"), None),
        P(("dp", "expert"), None),
        P(("dp", "expert"), None),
        P("expert", None, "dp"),
        P("expert", None, "dp"),
        P("expert", None, "dp"),
    )
    return jax.shard_map(
        local, mesh=mesh, in_specs=placed, out_specs=P(("dp", "expert"), None), check_vma=False
    )
```

time: 111 us -> 67.5 us (0.61)
  blocking collectives: 40.2 us -> 0 us
  starting transfers between devices: 5.62 us -> 20.5 us
  between operations: 13.5 us -> 0.2 us
  waiting for transfers between devices: 35.1 us -> 30 us
  local copies, waits for them, and re-layouts: 5.59 us -> 1.65 us
  matrix products: 9.24 us -> 12.1 us
  other arithmetic: 1.1 us -> 2.75 us
    all_to_all x2 -> x0, blocking collectives: 31.5 us -> none  [the longest x1 21.7 us: local(): lax.all_to_all(outgoing, 'expert', split_axis=0, concat_axis=0, tiled=True)]
    ppermute x0 -> x15, waiting for transfers between devices: none -> 30 us  [swap(): return lax.ppermute(value, axis, [(i, i ^ mask) for i in range(size)])]
    all_gather x1 -> x0, waiting for transfers between devices: 20.9 us -> none  [local(): lax.all_gather(arrived.reshape(experts * capacity, width), 'dp', axis=0,...]
    ppermute x0 -> x15, starting transfers between devices: none -> 20.5 us  [swap(): return lax.ppermute(value, axis, [(i, i ^ mask) for i in range(size)])]
    all_to_all x1 -> x0, waiting for transfers between devices: 14.3 us -> none  [local(): lax.all_to_all(lax.all_to_all(out_blocks, 'dp', split_axis=0, concat_axis...]
    all_gather x1 -> x0, blocking collectives: 8.72 us -> none  [local(): lax.all_gather(hidden, 'dp', axis=1, tiled=True)]
    all_to_all x1 -> x0, starting transfers between devices: 5.62 us -> none  [local(): lax.all_to_all(lax.all_to_all(out_blocks, 'dp', split_axis=0, concat_axis...]
    dot_general x6 -> x4, matrix products: 9.24 us -> 12.1 us  [the longest x2 5.89 us: local(): total = total + jnp.dot(part, mine_down, preferred_element_type=jnp.float32)]
  transfers between devices with their start and end apart: 2 -> 15, of which waited for: 2 -> 13; matrix products, arithmetic and copies ran while one was open for 0% -> 1% of each run, Pallas kernels for 0% -> 0%
where the time goes in v1:
time: 67.5 us; the launch traced here: 67.2 us
  waiting for transfers between devices  30 us (44%)
  starting transfers between devices  20.5 us (30%)
  matrix products  12.1 us (18%)
  other arithmetic  2.75 us (4%)
  local copies, waits for them, and re-layouts  1.65 us (2%)
    ppermute x15, waiting for transfers between devices, swap(): return lax.ppermute(value, axis, [(i, i ^ mask) for i in range(size)])  30 us
    ppermute x15, starting transfers between devices, swap(): return lax.ppermute(value, axis, [(i, i ^ mask) for i in range(size)])  20.5 us
    dot_general x2, matrix products, local(): total = total + jnp.dot(part, mine_down, preferred_element_type=jnp.float32)  5.89 us
    dot_general x1, matrix products, local(): gate_proj = jnp.dot(rows, w_gate[0], preferred_element_type=jnp.float32)  4.78 us
    dot_general x1, matrix products, local(): up_proj = jnp.dot(rows, w_up[0], preferred_element_type=jnp.float32)  1.42 us
  transfers between devices with their start and end apart: 15, of which 13 were waited for; matrix products, arithmetic and copies ran while one was open for 1% of the time, Pallas kernels for 0%

profile of v1, /device:TPU:0, one launch (start us, length us, event | category | flops | bytes accessed | tf_op | source)
XLA Modules:
  0.0 67.2 jit_solution(467165985969283567)
XLA Ops:
  0.0 0.8 %select_reduce_fusion.1 = f32[4,16]{1,0:T(4,128)S(1)} fusion(f32[4,8]{1,0:T(4,128)} %param.8, s32[4,8]{1,0:T(4,128)} %param.7), kind=kLoop, calls=%fused_computation.48 | loop fusion | flops 1472 | bytes 512 | tf_op jit(solution)/shard_map/reduce_sum | solution.py:18
  0.8 0.1 fusion.30
  0.9 0.8 %fusion.33 = (bf16[1,4,4224]{2,1,0:T(4,128)(2,1)S(1)}, bf16[4,4224]{1,0:T(4,128)(2,1)S(1)}) fusion(bf16[4,128]{1,0:T(4,128)(2,1)S(1)} %fusion.30, bf16[4,4096]{1,0:T(4,128)(2,1)} %param.6), kind=kLoop, calls=%fused_computation.66 | loop fusion | flops 67584 | bytes 101376 | tf_op jit(solution)/shard_map/broadcast_in_dim | solution.py:13
  1.7 3.1 %collective-permute-start = (bf16[4,4224]{1,0:T(4,128)(2,1)S(1)}, bf16[4,4224]{1,0:T(4,128)(2,1)S(1)}, u32[]{:S(2)}, u32[]{:S(2)}) collective-permute-start(bf16[4,4224]{1,0:T(4,128)(2,1)S(1)} %get-tuple-element.23), channel_id=1, source_target_pairs={{0,4},{1,5},{2,6},{3,7},{4,0},{5,1},{6,2},{7,3},{8,12},{9,13},{10,... | collective-permute-start | bytes 101384 | tf_op jit(solution)/shard_map/ppermute | solution.py:9
  4.8 2.6 %collective-permute-start.1 = (bf16[4,4224]{1,0:T(4,128)(2,1)S(1)}, bf16[4,4224]{1,0:T(4,128)(2,1)S(1)}, u32[]{:S(2)}, u32[]{:S(2)}) collective-permute-start(bf16[4,4224]{1,0:T(4,128)(2,1)S(1)} %get-tuple-element.23), channel_id=1, source_target_pairs={{0,8},{1,9},{2,10},{3,11},{4,12},{5,13},{6,14},{7,15},{8,0},{9,1},... | collective-permute-start | bytes 101384 | tf_op jit(solution)/shard_map/ppermute | solution.py:9
  7.3 0.0 collective-permute-start.2
  7.3 0.0 collective-permute-done
  7.3 2.8 %collective-permute-done.1 = bf16[4,4224]{1,0:T(4,128)(2,1)S(1)} collective-permute-done((bf16[4,4224]{1,0:T(4,128)(2,1)S(1)}, bf16[4,4224]{1,0:T(4,128)(2,1)S(1)}, u32[]{:S(2)}, u32[]{:S(2)}) %collective-permute-start.1) | collective-permute-done | bytes 33824 | tf_op jit(solution)/shard_map/ppermute | solution.py:9
  10.2 2.9 %collective-permute-done.2 = bf16[4,4224]{1,0:T(4,128)(2,1)S(1)} collective-permute-done((bf16[4,4224]{1,0:T(4,128)(2,1)S(1)}, bf16[4,4224]{1,0:T(4,128)(2,1)S(1)}, u32[]{:S(2)}, u32[]{:S(2)}) %collective-permute-start.2) | collective-permute-done | bytes 33824 | tf_op jit(solution)/shard_map/ppermute | solution.py:9
  13.1 0.1 pad_maximum_fusion.1
  13.2 1.6 %collective-permute-start.3 = (bf16[16,4224]{1,0:T(8,128)(2,1)S(1)}, bf16[16,4224]{1,0:T(8,128)(2,1)S(1)}, u32[]{:S(2)}, u32[]{:S(2)}) collective-permute-start(bf16[16,4224]{1,0:T(8,128)(2,1)S(1)} %reshape.82), channel_id=1, source_target_pairs={{0,2},{1,3},{2,0},{3,1},{4,6},{5,7},{6,4},{7,5},{8,10},{9,11},{10,... | collective-permute-start | bytes 405512 | tf_op jit(solution)/shard_map/ppermute | solution.py:9
  14.8 1.5 %collective-permute-start.4 = (bf16[16,4224]{1,0:T(8,128)(2,1)S(1)}, bf16[16,4224]{1,0:T(8,128)(2,1)S(1)}, u32[]{:S(2)}, u32[]{:S(2)}) collective-permute-start(bf16[16,4224]{1,0:T(8,128)(2,1)S(1)} %reshape.82), channel_id=1, source_target_pairs={{0,16},{16,0},{1,17},{17,1},{2,18},{18,2},{3,19},{19,3},{4,20},{20... | collective-permute-start | bytes 405512 | tf_op jit(solution)/shard_map/ppermute | solution.py:9
  16.3 2.0 %collective-permute-done.3 = bf16[16,4224]{1,0:T(8,128)(2,1)S(1)} collective-permute-done((bf16[16,4224]{1,0:T(8,128)(2,1)S(1)}, bf16[16,4224]{1,0:T(8,128)(2,1)S(1)}, u32[]{:S(2)}, u32[]{:S(2)}) %collective-permute-start.3) | collective-permute-done | bytes 135200 | tf_op jit(solution)/shard_map/ppermute | solution.py:9
  18.3 1.5 %collective-permute-start.5 = (bf16[8,4224]{1,0:T(8,128)(2,1)S(1)}, bf16[8,4224]{1,0:T(8,128)(2,1)S(1)}, u32[]{:S(2)}, u32[]{:S(2)}) collective-permute-start(bf16[8,4224]{1,0:T(8,128)(2,1)S(1)} %slice.71), channel_id=1, source_target_pairs={{0,16},{16,0},{1,17},{17,1},{2,18},{18,2},{3,19},{19,3},{4,20},{20... | collective-permute-start | bytes 202760 | tf_op jit(solution)/shard_map/ppermute | solution.py:9
  19.8 0.4 collective-permute-done.4
  20.2 1.2 %collective-permute-start.6 = (bf16[8,4224]{1,0:T(8,128)(2,1)S(1)}, bf16[8,4224]{1,0:T(8,128)(2,1)S(1)}, u32[]{:S(2)}, u32[]{:S(2)}) collective-permute-start(bf16[8,4224]{1,0:T(8,128)(2,1)S(1)} %slice.72), channel_id=1, source_target_pairs={{0,2},{1,3},{2,0},{3,1},{4,6},{5,7},{6,4},{7,5},{8,10},{9,11},{10,... | collective-permute-start | bytes 202760 | tf_op jit(solution)/shard_map/ppermute | solution.py:9
  21.5 1.1 %collective-permute-done.5 = bf16[8,4224]{1,0:T(8,128)(2,1)S(1)} collective-permute-done((bf16[8,4224]{1,0:T(8,128)(2,1)S(1)}, bf16[8,4224]{1,0:T(8,128)(2,1)S(1)}, u32[]{:S(2)}, u32[]{:S(2)}) %collective-permute-start.5) | collective-permute-done | bytes 67616 | tf_op jit(solution)/shard_map/ppermute | solution.py:9
  22.6 1.8 %collective-permute-done.6 = bf16[8,4224]{1,0:T(8,128)(2,1)S(1)} collective-permute-done((bf16[8,4224]{1,0:T(8,128)(2,1)S(1)}, bf16[8,4224]{1,0:T(8,128)(2,1)S(1)}, u32[]{:S(2)}, u32[]{:S(2)}) %collective-permute-start.6) | collective-permute-done | bytes 67616 | tf_op jit(solution)/shard_map/ppermute | solution.py:9
  24.5 0.1 collective-permute-start.7
  24.5 1.9 %collective-permute-done.7 = bf16[64,4224]{1,0:T(8,128)(2,1)S(1)} collective-permute-done((bf16[64,4224]{1,0:T(8,128)(2,1)S(1)}, bf16[64,4224]{1,0:T(8,128)(2,1)S(1)}, u32[]{:S(2)}, u32[]{:S(2)}) %collective-permute-start.7) | collective-permute-done | bytes 540704 | tf_op jit(solution)/shard_map/ppermute | solution.py:9
  26.5 0.0 slice-start
  26.5 0.0 slice-start.1
  26.5 4.8 %fusion.2 = f32[128,1024]{1,0:T(8,128)S(1)} fusion(bf16[1,4096,1024]{2,1,0:T(8,128)(2,1)} %param.9, bf16[128,4224]{1,0:T(8,128)(2,1)S(1)} %constant_dynamic-update-slice_fusion.5), kind=kOutput, calls=%fused_computation.2 | convolution fusion | flops 1073741824 | bytes 9961472 | tf_op jit(solution)/shard_map/dot_general | solution.py:57
  31.3 0.0 slice-done
  31.3 1.0 %slice-done.1 = s8[4194304]{0:T(1024)(128)(4,1)S(1)} async-done(((s8[8388608]{0:T(1024)(128)(4,1)}), s8[4194304]{0:T(1024)(128)(4,1)S(1)}, s32[]{:S(2)}) %slice-start.1) | async-done | bytes 4194328
  32.3 1.4 %multiply_convert_fusion = bf16[128,1024]{1,0:T(8,128)(2,1)S(1)} fusion(f32[128,1024]{1,0:T(8,128)S(1)} %fusion.2, bf16[1,4096,1024]{2,1,0:T(8,128)(2,1)S(1)} %bitcast.85, bf16[128,4224]{1,0:T(8,128)(2,1)S(1)} %constant_dynamic-update-slice_fusion.5), kind=kOutput, calls=%fused_computation.16 | convolution fusion | flops 1074528256 | bytes 10223616 | tf_op jit(solution)/shard_map/dot_general | solution.py:58
  33.8 1.6 %collective-permute-start.8 = (bf16[128,1024]{1,0:T(8,128)(2,1)S(1)}, bf16[128,1024]{1,0:T(8,128)(2,1)S(1)}, u32[]{:S(2)}, u32[]{:S(2)}) collective-permute-start(bf16[128,1024]{1,0:T(8,128)(2,1)S(1)} %multiply_convert_fusion), channel_id=1, source_target_pairs={{0,16},{16,0},{1,17},{17,1},{2,18},{18,2},{3,19},{19,3},{4,20},{20... | collective-permute-start | bytes 786440 | tf_op jit(solution)/shard_map/ppermute | solution.py:9
  35.3 0.1 select_reduce_fusion
  35.4 6.7 %collective-permute-done.8 = bf16[128,1024]{1,0:T(8,128)(2,1)S(1)} collective-permute-done((bf16[128,1024]{1,0:T(8,128)(2,1)S(1)}, bf16[128,1024]{1,0:T(8,128)(2,1)S(1)}, u32[]{:S(2)}, u32[]{:S(2)}) %collective-permute-start.8) | collective-permute-done | bytes 262176 | tf_op jit(solution)/shard_map/ppermute | solution.py:9
  42.2 2.9 %fusion.4 = f32[128,2048]{1,0:T(8,128)S(1)} fusion(bf16[128,1024]{1,0:T(8,128)(2,1)S(1)} %bitcast.76, bf16[2,1024,2048]{2,1,0:T(8,128)(2,1)} %bitcast.71, s32[]{:T(128)S(6)} %select_n.33), kind=kOutput, calls=%fused_computation.4 | convolution fusion | flops 536870912 | bytes 5505028 | tf_op jit(solution)/shard_map/dot_general | solution.py:75
  45.2 3.0 %fusion.13 = f32[128,2048]{1,0:T(8,128)S(1)} fusion(f32[128,2048]{1,0:T(8,128)S(1)} %fusion.4, bf16[128,1024]{1,0:T(8,128)(2,1)S(1)} %multiply_convert_fusion, bf16[2,1024,2048]{2,1,0:T(8,128)(2,1)} %bitcast.72, s32[]{:T(128)S(6)} %select_n.32, f32[128]{0:T(128)S(1)} %select_reduce_fusion), kind=kOutput, calls=%fused_computation.11 | convolution fusion | flops 537395200 | bytes 6554116 | tf_op jit(solution)/shard_map/dot_general | solution.py:75
  48.2 0.1 convert_element_type.100
  48.3 0.1 collective-permute-start.9
  48.4 0.1 squeeze.34
  48.6 1.3 %collective-permute-done.9 = bf16[2,2,1,4,4,2048]{5,4,3,1,0,2:T(4,128)(2,1)S(1)} collective-permute-done((bf16[2,2,1,4,4,2048]{5,4,3,1,0,2:T(4,128)(2,1)S(1)}, bf16[2,2,1,4,4,2048]{5,4,3,1,0,2:T(4,128)(2,1)S(1)}, u32[]{:S(2)}, u32[]{:S(2)}) %collective-permute-start.9) | collective-permute-done | bytes 262176 | tf_op jit(solution)/shard_map/ppermute | solution.py:9
  50.0 1.3 %collective-permute-start.10 = (bf16[2,1,4,4,2048]{4,3,2,0,1:T(4,128)(2,1)S(1)}, bf16[2,1,4,4,2048]{4,3,2,0,1:T(4,128)(2,1)S(1)}, u32[]{:S(2)}, u32[]{:S(2)}) collective-permute-start(bf16[2,1,4,4,2048]{4,3,2,0,1:T(4,128)(2,1)S(1)} %fusion.19), channel_id=1, source_target_pairs={{0,2},{1,3},{2,0},{3,1},{4,6},{5,7},{6,4},{7,5},{8,10},{9,11},{10,... | collective-permute-start | bytes 393224 | tf_op jit(solution)/shard_map/ppermute | solution.py:9
  51.3 4.3 %collective-permute-done.10 = bf16[2,1,4,4,2048]{4,3,2,0,1:T(4,128)(2,1)S(1)} collective-permute-done((bf16[2,1,4,4,2048]{4,3,2,0,1:T(4,128)(2,1)S(1)}, bf16[2,1,4,4,2048]{4,3,2,0,1:T(4,128)(2,1)S(1)}, u32[]{:S(2)}, u32[]{:S(2)}) %collective-permute-start.10) | collective-permute-done | bytes 131104 | tf_op jit(solution)/shard_map/ppermute | solution.py:9
  55.6 0.1 fusion.34
  55.8 0.1 collective-permute-start.11
  55.8 1.1 %collective-permute-start.12 = (bf16[2,1,4,2048]{3,2,0,1:T(4,128)(2,1)S(1)}, bf16[2,1,4,2048]{3,2,0,1:T(4,128)(2,1)S(1)}, u32[]{:S(2)}, u32[]{:S(2)}) collective-permute-start(bf16[2,1,4,2048]{3,2,0,1:T(4,128)(2,1)S(1)} %get-tuple-element.17), channel_id=1, source_target_pairs={{0,8},{1,9},{2,10},{3,11},{4,12},{5,13},{6,14},{7,15},{8,0},{9,1},... | collective-permute-start | bytes 98312 | tf_op jit(solution)/shard_map/ppermute | solution.py:9
  56.9 3.3 %collective-permute-start.13 = (bf16[2,1,4,2048]{3,2,0,1:T(4,128)(2,1)S(1)}, bf16[2,1,4,2048]{3,2,0,1:T(4,128)(2,1)S(1)}, u32[]{:S(2)}, u32[]{:S(2)}) collective-permute-start(bf16[2,1,4,2048]{3,2,0,1:T(4,128)(2,1)S(1)} %get-tuple-element.16), channel_id=1, source_target_pairs={{0,12},{1,13},{2,14},{3,15},{4,8},{5,9},{6,10},{7,11},{8,4},{9,5},... | collective-permute-start | bytes 98312 | tf_op jit(solution)/shard_map/ppermute | solution.py:9
  60.2 0.0 collective-permute-done.11
  60.2 0.6 collective-permute-done.12
  60.9 1.8 %collective-permute-done.13 = bf16[2,1,4,2048]{3,2,0,1:T(4,128)(2,1)S(1)} collective-permute-done((bf16[2,1,4,2048]{3,2,0,1:T(4,128)(2,1)S(1)}, bf16[2,1,4,2048]{3,2,0,1:T(4,128)(2,1)S(1)}, u32[]{:S(2)}, u32[]{:S(2)}) %collective-permute-start.13) | collective-permute-done | bytes 32800 | tf_op jit(solution)/shard_map/ppermute | solution.py:9
  62.7 1.6 %collective-permute-start.14 = (bf16[4,2048]{1,0:T(4,128)(2,1)S(1)}, bf16[4,2048]{1,0:T(4,128)(2,1)S(1)}, u32[]{:S(2)}, u32[]{:S(2)}) collective-permute-start(bf16[4,2048]{1,0:T(4,128)(2,1)S(1)} %slice_bitcast_fusion.5), channel_id=1, source_target_pairs={{0,16},{16,0},{1,17},{17,1},{2,18},{18,2},{3,19},{19,3},{4,20},{20... | collective-permute-start | bytes 49160 | tf_op jit(solution)/shard_map/ppermute | solution.py:9
  64.3 2.2 %collective-permute-done.14 = bf16[4,2048]{1,0:T(4,128)(2,1)S(1)} collective-permute-done((bf16[4,2048]{1,0:T(4,128)(2,1)S(1)}, bf16[4,2048]{1,0:T(4,128)(2,1)S(1)}, u32[]{:S(2)}, u32[]{:S(2)}) %collective-permute-start.14) | collective-permute-done | bytes 16416 | tf_op jit(solution)/shard_map/ppermute | solution.py:9
  66.6 0.6 reverse_select_fusion
  (23 shorter events, 0.5 us)
Async XLA Ops:
  1.7 5.7 %collective-permute-start = (bf16[4,4224]{1,0:T(4,128)(2,1)S(1)}, bf16[4,4224]{1,0:T(4,128)(2,1)S(1)}, u32[]{:S(2)}, u32[]{:S(2)}) collective-permute-start(bf16[4,4224]{1,0:T(4,128)(2,1)S(1)} %get-tuple-element.23), channel_id=1, source_target_pairs={{0,4},{1,5},{2,6},{3,7},{4,0},{5,1},{6,2},{7,3},{8,12},{9,13},{10,... | collective-permute-start | bytes 101384 | tf_op jit(solution)/shard_map/ppermute | solution.py:9
  4.8 5.4 %collective-permute-start.1 = (bf16[4,4224]{1,0:T(4,128)(2,1)S(1)}, bf16[4,4224]{1,0:T(4,128)(2,1)S(1)}, u32[]{:S(2)}, u32[]{:S(2)}) collective-permute-start(bf16[4,4224]{1,0:T(4,128)(2,1)S(1)} %get-tuple-element.23), channel_id=1, source_target_pairs={{0,8},{1,9},{2,10},{3,11},{4,12},{5,13},{6,14},{7,15},{8,0},{9,1},... | collective-permute-start | bytes 101384 | tf_op jit(solution)/shard_map/ppermute | solution.py:9
  7.3 5.7 %collective-permute-start.2 = (bf16[4,4224]{1,0:T(4,128)(2,1)S(1)}, bf16[4,4224]{1,0:T(4,128)(2,1)S(1)}, u32[]{:S(2)}, u32[]{:S(2)}) collective-permute-start(bf16[4,4224]{1,0:T(4,128)(2,1)S(1)} %get-tuple-element.23), channel_id=1, source_target_pairs={{0,12},{1,13},{2,14},{3,15},{4,8},{5,9},{6,10},{7,11},{8,4},{9,5},... | collective-permute-start | bytes 101384 | tf_op jit(solution)/shard_map/ppermute | solution.py:9
  13.2 5.1 %collective-permute-start.3 = (bf16[16,4224]{1,0:T(8,128)(2,1)S(1)}, bf16[16,4224]{1,0:T(8,128)(2,1)S(1)}, u32[]{:S(2)}, u32[]{:S(2)}) collective-permute-start(bf16[16,4224]{1,0:T(8,128)(2,1)S(1)} %reshape.82), channel_id=1, source_target_pairs={{0,2},{1,3},{2,0},{3,1},{4,6},{5,7},{6,4},{7,5},{8,10},{9,11},{10,... | collective-permute-start | bytes 405512 | tf_op jit(solution)/shard_map/ppermute | solution.py:9
  14.8 5.3 %collective-permute-start.4 = (bf16[16,4224]{1,0:T(8,128)(2,1)S(1)}, bf16[16,4224]{1,0:T(8,128)(2,1)S(1)}, u32[]{:S(2)}, u32[]{:S(2)}) collective-permute-start(bf16[16,4224]{1,0:T(8,128)(2,1)S(1)} %reshape.82), channel_id=1, source_target_pairs={{0,16},{16,0},{1,17},{17,1},{2,18},{18,2},{3,19},{19,3},{4,20},{20... | collective-permute-start | bytes 405512 | tf_op jit(solution)/shard_map/ppermute | solution.py:9
  18.3 4.3 %collective-permute-start.5 = (bf16[8,4224]{1,0:T(8,128)(2,1)S(1)}, bf16[8,4224]{1,0:T(8,128)(2,1)S(1)}, u32[]{:S(2)}, u32[]{:S(2)}) collective-permute-start(bf16[8,4224]{1,0:T(8,128)(2,1)S(1)} %slice.71), channel_id=1, source_target_pairs={{0,16},{16,0},{1,17},{17,1},{2,18},{18,2},{3,19},{19,3},{4,20},{20... | collective-permute-start | bytes 202760 | tf_op jit(solution)/shard_map/ppermute | solution.py:9
  20.2 4.3 %collective-permute-start.6 = (bf16[8,4224]{1,0:T(8,128)(2,1)S(1)}, bf16[8,4224]{1,0:T(8,128)(2,1)S(1)}, u32[]{:S(2)}, u32[]{:S(2)}) collective-permute-start(bf16[8,4224]{1,0:T(8,128)(2,1)S(1)} %slice.72), channel_id=1, source_target_pairs={{0,2},{1,3},{2,0},{3,1},{4,6},{5,7},{6,4},{7,5},{8,10},{9,11},{10,... | collective-permute-start | bytes 202760 | tf_op jit(solution)/shard_map/ppermute | solution.py:9
  24.5 2.0 %collective-permute-start.7 = (bf16[64,4224]{1,0:T(8,128)(2,1)S(1)}, bf16[64,4224]{1,0:T(8,128)(2,1)S(1)}, u32[]{:S(2)}, u32[]{:S(2)}) collective-permute-start(bf16[64,4224]{1,0:T(8,128)(2,1)S(1)} %get-tuple-element.18), channel_id=1, source_target_pairs={{0,1},{1,0},{2,3},{3,2},{4,5},{5,4},{6,7},{7,6},{8,9},{9,8},{10,11... | collective-permute-start | bytes 1622024 | tf_op jit(solution)/shard_map/ppermute | solution.py:9
  26.5 4.9 %slice-start = ((s8[8388608]{0:T(1024)(128)(4,1)}), s8[4194304]{0:T(1024)(128)(4,1)S(1)}, s32[]{:S(2)}) async-start(s8[8388608]{0:T(1024)(128)(4,1)} %bitcast.84), calls=%async_computation | async-start | bytes 8388608
  26.5 5.8 %slice-start.1 = ((s8[8388608]{0:T(1024)(128)(4,1)}), s8[4194304]{0:T(1024)(128)(4,1)S(1)}, s32[]{:S(2)}) async-start(s8[8388608]{0:T(1024)(128)(4,1)} %bitcast.84), calls=%async_computation.1 | async-start | bytes 8388608
  33.8 8.4 %collective-permute-start.8 = (bf16[128,1024]{1,0:T(8,128)(2,1)S(1)}, bf16[128,1024]{1,0:T(8,128)(2,1)S(1)}, u32[]{:S(2)}, u32[]{:S(2)}) collective-permute-start(bf16[128,1024]{1,0:T(8,128)(2,1)S(1)} %multiply_convert_fusion), channel_id=1, source_target_pairs={{0,16},{16,0},{1,17},{17,1},{2,18},{18,2},{3,19},{19,3},{4,20},{20... | collective-permute-start | bytes 786440 | tf_op jit(solution)/shard_map/ppermute | solution.py:9
  48.3 1.6 %collective-permute-start.9 = (bf16[2,2,1,4,4,2048]{5,4,3,1,0,2:T(4,128)(2,1)S(1)}, bf16[2,2,1,4,4,2048]{5,4,3,1,0,2:T(4,128)(2,1)S(1)}, u32[]{:S(2)}, u32[]{:S(2)}) collective-permute-start(bf16[2,2,1,4,4,2048]{5,4,3,1,0,2:T(4,128)(2,1)S(1)} %convert_element_type.100), channel_id=1, source_target_pairs={{0,1},{1,0},{2,3},{3,2},{4,5},{5,4},{6,7},{7,6},{8,9},{9,8},{10,11... | collective-permute-start | bytes 786440 | tf_op jit(solution)/shard_map/ppermute | solution.py:9
  50.0 5.6 %collective-permute-start.10 = (bf16[2,1,4,4,2048]{4,3,2,0,1:T(4,128)(2,1)S(1)}, bf16[2,1,4,4,2048]{4,3,2,0,1:T(4,128)(2,1)S(1)}, u32[]{:S(2)}, u32[]{:S(2)}) collective-permute-start(bf16[2,1,4,4,2048]{4,3,2,0,1:T(4,128)(2,1)S(1)} %fusion.19), channel_id=1, source_target_pairs={{0,2},{1,3},{2,0},{3,1},{4,6},{5,7},{6,4},{7,5},{8,10},{9,11},{10,... | collective-permute-start | bytes 393224 | tf_op jit(solution)/shard_map/ppermute | solution.py:9
  55.8 4.5 %collective-permute-start.11 = (bf16[2,1,4,2048]{3,2,0,1:T(4,128)(2,1)S(1)}, bf16[2,1,4,2048]{3,2,0,1:T(4,128)(2,1)S(1)}, u32[]{:S(2)}, u32[]{:S(2)}) collective-permute-start(bf16[2,1,4,2048]{3,2,0,1:T(4,128)(2,1)S(1)} %get-tuple-element.15), channel_id=1, source_target_pairs={{0,4},{1,5},{2,6},{3,7},{4,0},{5,1},{6,2},{7,3},{8,12},{9,13},{10,... | collective-permute-start | bytes 98312 | tf_op jit(solution)/shard_map/ppermute | solution.py:9
  55.8 5.0 %collective-permute-start.12 = (bf16[2,1,4,2048]{3,2,0,1:T(4,128)(2,1)S(1)}, bf16[2,1,4,2048]{3,2,0,1:T(4,128)(2,1)S(1)}, u32[]{:S(2)}, u32[]{:S(2)}) collective-permute-start(bf16[2,1,4,2048]{3,2,0,1:T(4,128)(2,1)S(1)} %get-tuple-element.17), channel_id=1, source_target_pairs={{0,8},{1,9},{2,10},{3,11},{4,12},{5,13},{6,14},{7,15},{8,0},{9,1},... | collective-permute-start | bytes 98312 | tf_op jit(solution)/shard_map/ppermute | solution.py:9
  56.9 5.7 %collective-permute-start.13 = (bf16[2,1,4,2048]{3,2,0,1:T(4,128)(2,1)S(1)}, bf16[2,1,4,2048]{3,2,0,1:T(4,128)(2,1)S(1)}, u32[]{:S(2)}, u32[]{:S(2)}) collective-permute-start(bf16[2,1,4,2048]{3,2,0,1:T(4,128)(2,1)S(1)} %get-tuple-element.16), channel_id=1, source_target_pairs={{0,12},{1,13},{2,14},{3,15},{4,8},{5,9},{6,10},{7,11},{8,4},{9,5},... | collective-permute-start | bytes 98312 | tf_op jit(solution)/shard_map/ppermute | solution.py:9
  62.7 3.8 %collective-permute-start.14 = (bf16[4,2048]{1,0:T(4,128)(2,1)S(1)}, bf16[4,2048]{1,0:T(4,128)(2,1)S(1)}, u32[]{:S(2)}, u32[]{:S(2)}) collective-permute-start(bf16[4,2048]{1,0:T(4,128)(2,1)S(1)} %slice_bitcast_fusion.5), channel_id=1, source_target_pairs={{0,16},{16,0},{1,17},{17,1},{2,18},{18,2},{3,19},{19,3},{4,20},{20... | collective-permute-start | bytes 49160 | tf_op jit(solution)/shard_map/ppermute | solution.py:9

commit v2 on v1

--- a/solution.py
+++ b/solution.py
@@ -1,7 +1,12 @@
 import jax
 import jax.numpy as jnp
 from jax import lax
+from jax.experimental import pallas as pl
+from jax.experimental.pallas import tpu as pltpu
 from jax.sharding import PartitionSpec as P
+
+
+CHUNKS = 2
 
 
 def swap(value, axis, mask):
@@ -11,6 +16,38 @@
 
 def spread(value, axis, masks):
     return jnp.concatenate([value[None]] + [swap(value, axis, m)[None] for m in masks])
+
+
+def fetch(weights, after, cuts, name):
+    weights, _ = lax.optimization_barrier((weights, after))
+    weights = pltpu.with_memory_space_constraint(weights, pltpu.HBM)
+
+    def body(rows_from, source, *rest):
+        pieces, arrived = rest[:-1], rest[-1]
+        copies = []
+        for i, (_, rows, column, columns) in enumerate(cuts):
+            start = pl.multiple_of(rows_from[i], 128)
+            part = source.at[pl.ds(start, rows), pl.ds(column, columns)]
+            copies.append(pltpu.make_async_copy(part, pieces[i], arrived.at[i]))
+        for copy in copies:
+            copy.start()
+        for copy in copies:
+            copy.wait()
+
+    size = sum(rows * columns for _, rows, _, columns in cuts) * weights.dtype.itemsize
+    return pl.pallas_call(
+        body,
+        out_shape=[pltpu.VMEM((rows, columns), weights.dtype) for _, rows, _, columns in cuts],
+        in_specs=[
+            pl.BlockSpec(memory_space=pltpu.SMEM),
+            pl.BlockSpec(memory_space=pltpu.HBM),
+        ],
+        out_specs=[pl.BlockSpec(memory_space=pltpu.VMEM)] * len(cuts),
+        scratch_shapes=[pltpu.SemaphoreType.DMA((len(cuts),))],
+        cost_estimate=pl.CostEstimate(flops=0, bytes_accessed=size, transcendentals=0),
+        compiler_params=pltpu.CompilerParams(vmem_limit_bytes=1 << 20),
+        name=name,
+    )(jnp.stack([jnp.asarray(row, jnp.int32) for row, _, _, _ in cuts]), weights)
 
 
 def gate_table(expert_ids, gate_probs, experts):
@@ -24,18 +61,24 @@
     return jnp.concatenate(parts, axis=1)
 
 
-def gather_rows(block, high_masks, group_masks):
+def gather_rows(block, high_masks, group_masks, fetches):
     rows, width = block.shape
     near = spread(block, "expert", high_masks)
     near = near.reshape(-1, width)
     if group_masks:
         near = spread(near, "dp", group_masks).reshape(-1, width)
+    parts = [fetches[0](block)]
+    near, parts[0] = lax.optimization_barrier((near, parts[0]))
     over_x = swap(near, "dp", 1)
     over_y = swap(near, "expert", 2)
+    parts.append(fetches[1](near))
+    over_x, over_y, parts[1] = lax.optimization_barrier((over_x, over_y, parts[1]))
     half = near.shape[0] // 2
     corner = jnp.concatenate([swap(over_y[:half], "dp", 1), swap(over_x[half:], "expert", 2)])
+    parts.append(fetches[2](over_x))
+    corner, parts[2] = lax.optimization_barrier((corner, parts[2]))
     chip = jnp.concatenate([near, over_y, over_x, corner])
-    return jnp.concatenate([chip, swap(chip, "expert", 1)])
+    return jnp.concatenate([chip, swap(chip, "expert", 1)]), parts
 
 
 def local(tokens, expert_ids, gate_probs, w_gate, w_up, w_down):
@@ -49,30 +92,45 @@
     table = gate_table(expert_ids, gate_probs, experts)
     slots = -(-table.shape[1] // 128) * 128
     block = jnp.concatenate([tokens, jnp.pad(table, ((0, 0), (0, slots - table.shape[1])))], axis=1)
-    everything = gather_rows(block, high_masks, group_masks)
+    units = w_gate.shape[2]
+    chunks = CHUNKS if units % (128 * CHUNKS) == 0 else 1
+    step = units // chunks
+    columns = [(0, width, i * step, step) for i in range(chunks)]
+    down_rows = [
+        ((group ^ mask) * units + i * step, step, 0, w_down.shape[2])
+        for mask in range(groups)
+        for i in range(chunks)
+    ]
+    fetches = (
+        lambda after: fetch(w_gate[0], after, columns, "fetch_gate"),
+        lambda after: fetch(w_up[0], after, columns, "fetch_up"),
+        lambda after: fetch(w_down[0], after, down_rows, "fetch_down"),
+    )
+    everything, parts = gather_rows(block, high_masks, group_masks, fetches)
+    gate_parts, up_parts, down_parts = parts
     rows = everything[:, :width]
     mine = (jnp.arange(slots) % experts == me) & (jnp.arange(slots) < table.shape[1])
     scale = jnp.sum(jnp.where(mine, everything[:, width:].astype(jnp.float32), 0.0), axis=1)
 
-    gate_proj = jnp.dot(rows, w_gate[0], preferred_element_type=jnp.float32)
-    up_proj = jnp.dot(rows, w_up[0], preferred_element_type=jnp.float32)
-    hidden = (jax.nn.silu(gate_proj) * up_proj).astype(jnp.bfloat16)
+    shape = (2, 2, 2, wide, high * token_count, step)
 
-    units = hidden.shape[1]
-    shape = (2, 2, 2, wide, high * token_count, units)
-    down = w_down[0].reshape(groups, units, -1)
-    total = jnp.zeros((rows.shape[0], down.shape[2]), jnp.float32)
-    for mask in range(groups):
-        part = hidden
-        if mask:
-            part = swap(hidden, "dp", mask).reshape(shape)
-            x_order = [i ^ (mask & 1) for i in range(2)]
-            wide_order = [i ^ (mask >> 1) for i in range(wide)]
-            part = jnp.stack([part[:, i] for i in x_order], axis=1)
-            part = jnp.stack([part[:, :, :, i] for i in wide_order], axis=3)
-            part = part.reshape(hidden.shape)
-        mine_down = lax.dynamic_index_in_dim(down, group ^ mask, 0, keepdims=False)
-        total = total + jnp.dot(part, mine_down, preferred_element_type=jnp.float32)
+    def from_group(value, mask):
+        value = swap(value, "dp", mask).reshape(shape)
+        value = jnp.stack([value[:, i ^ (mask & 1)] for i in range(2)], axis=1)
+        value = jnp.stack([value[:, :, :, i ^ (mask >> 1)] for i in range(wide)], axis=3)
+        return value.reshape(-1, step)
+
+    own, others = [], [[] for _ in range(1, groups)]
+    for gate_part, up_part in zip(gate_parts, up_parts):
+        gate_proj = jnp.dot(rows, gate_part, preferred_element_type=jnp.float32)
+        up_proj = jnp.dot(rows, up_part, preferred_element_type=jnp.float32)
+        hidden = (jax.nn.silu(gate_proj) * up_proj).astype(jnp.bfloat16)
+        own.append(hidden)
+        for mask in range(1, groups):
+            others[mask - 1].append(from_group(hidden, mask))
+    total = jnp.zeros((rows.shape[0], w_down.shape[2]), jnp.float32)
+    for part, down_part in zip(sum(others, own), down_parts):
+        total = total + jnp.dot(part, down_part, preferred_element_type=jnp.float32)
 
     total = (total * scale[:, None]).reshape(2, 2, 2, wide, high, token_count, -1)
     send = lambda value, axis, mask: swap(value.astype(jnp.bfloat16), axis, mask).astype(jnp.float32)

time: 67.5 us -> 65 us (0.963)
  Pallas kernels: 0 us -> 12.4 us
  waiting for transfers between devices: 30 us -> 18.7 us
  matrix products: 12.1 us -> 4.71 us
  local copies, waits for them, and re-layouts: 1.65 us -> 6 us
  starting transfers between devices: 20.5 us -> 19.7 us
    pallas_call x0 -> x3, Pallas kernels: none -> 12.4 us  [fetch(): pl.pallas_call(body, out_shape=[pltpu.VMEM((rows, columns), weights.dtype...]
    ppermute x15 -> x16, waiting for transfers between devices: 30 us -> 18.7 us  [swap(): return lax.ppermute(value, axis, [(i, i ^ mask) for i in range(size)])]
    dot_general x4 -> x8, matrix products: 12.1 us -> 4.71 us  [the longest x4 1.86 us: local(): total = total + jnp.dot(part, down_part, preferred_element_type=jnp.float32)]
    unnamed x8 -> x12, local copies, waits for them, and re-layouts: 1.09 us -> 5.46 us
    ppermute x15 -> x16, starting transfers between devices: 20.5 us -> 19.7 us  [swap(): return lax.ppermute(value, axis, [(i, i ^ mask) for i in range(size)])]
  transfers between devices with their start and end apart: 15 -> 16, of which waited for: 13 -> 8; matrix products, arithmetic and copies ran while one was open for 1% -> 3% of each run, Pallas kernels for 0% -> 19%
where the time goes in v2:
time: 65 us; the launch traced here: 64.8 us
  starting transfers between devices  19.7 us (30%)
  waiting for transfers between devices  18.7 us (29%)
  Pallas kernels  12.4 us (19%)
  local copies, waits for them, and re-layouts  6 us (9%)
  matrix products  4.71 us (7%)
  other arithmetic  2.89 us (4%)
    ppermute x16, starting transfers between devices, swap(): return lax.ppermute(value, axis, [(i, i ^ mask) for i in range(size)])  19.7 us
    ppermute x16, waiting for transfers between devices, swap(): return lax.ppermute(value, axis, [(i, i ^ mask) for i in range(size)])  18.7 us
    pallas_call x3, Pallas kernels, fetch(): pl.pallas_call(body, out_shape=[pltpu.VMEM((rows, columns), weights.dtype...  12.4 us
    unnamed x12, local copies, waits for them, and re-layouts  5.46 us
    dot_general x4, matrix products, local(): total = total + jnp.dot(part, down_part, preferred_element_type=jnp.float32)  1.86 us
    dot_general x2, matrix products, local(): up_proj = jnp.dot(rows, up_part, preferred_element_type=jnp.float32)  1.44 us
    dot_general x2, matrix products, local(): gate_proj = jnp.dot(rows, gate_part, preferred_element_type=jnp.float32)  1.41 us
  transfers between devices with their start and end apart: 16, of which 8 were waited for; matrix products, arithmetic and copies ran while one was open for 3% of the time, Pallas kernels for 19%

profile of v2, /device:TPU:0, one launch (start us, length us, event | category | flops | bytes accessed | tf_op | source)
XLA Modules:
  0.0 64.8 jit_solution(11593296071282130184)
XLA Ops:
  0.0 0.8 %select_reduce_fusion.1 = f32[4,16]{1,0:T(4,128)S(1)} fusion(f32[4,8]{1,0:T(4,128)} %param.8, s32[4,8]{1,0:T(4,128)} %param.7), kind=kLoop, calls=%fused_computation.39 | loop fusion | flops 1472 | bytes 512 | tf_op jit(solution)/shard_map/reduce_sum | solution.py:55
  0.8 0.1 fusion.21
  0.9 0.8 %fusion.22 = (bf16[1,4,4224]{2,1,0:T(4,128)(2,1)S(1)}, bf16[4,4224]{1,0:T(4,128)(2,1)S(1)}) fusion(bf16[4,128]{1,0:T(4,128)(2,1)S(1)} %fusion.21, bf16[4,4096]{1,0:T(4,128)(2,1)} %param.6), kind=kLoop, calls=%fused_computation.61 | loop fusion | flops 67584 | bytes 101376 | tf_op jit(solution)/shard_map/broadcast_in_dim | solution.py:18
  1.7 5.1 %collective-permute-start.2 = (bf16[4,4224]{1,0:T(4,128)(2,1)S(1)}, bf16[4,4224]{1,0:T(4,128)(2,1)S(1)}, u32[]{:S(2)}, u32[]{:S(2)}) collective-permute-start(bf16[4,4224]{1,0:T(4,128)(2,1)S(1)} %get-tuple-element.61), channel_id=1, source_target_pairs={{0,12},{1,13},{2,14},{3,15},{4,8},{5,9},{6,10},{7,11},{8,4},{9,5},... | collective-permute-start | bytes 101384 | tf_op jit(solution)/shard_map/ppermute | solution.py:14
  6.8 0.6 collective-permute-start
  7.4 0.1 pad_add_fusion.rows_from
  7.5 4.0 %fetch_gate.1 = (bf16[4096,512]{1,0:T(8,128)(2,1)S(1)}, bf16[4096,512]{1,0:T(8,128)(2,1)S(1)}) custom-call(s32[2]{0:T(128)S(1)} %broadcast_5_rows_from.2.rows_from, bf16[4096,1024]{1,0:T(8,128)(2,1)} %bitcast.71), custom_call_target="tpu_custom_call" | custom-call | bytes 8388608 | tf_op jit(solution)/shard_map/fetch_gate/pallas_call | solution.py:38
  11.6 1.9 %copy-done = bf16[4096,512]{1,0:T(8,128)(2,1)} copy-done((bf16[4096,512]{1,0:T(8,128)(2,1)}, bf16[4096,512]{1,0:T(8,128)(2,1)S(1)}, u32[]{:S(2)}) %copy-start) | copy-done | bytes 4194328
  13.5 2.0 %copy-done.2 = bf16[4096,512]{1,0:T(8,128)(2,1)} copy-done((bf16[4096,512]{1,0:T(8,128)(2,1)}, bf16[4096,512]{1,0:T(8,128)(2,1)S(1)}, u32[]{:S(2)}) %copy-start.2) | copy-done | bytes 4194328
  15.5 0.0 collective-permute-done.1
  15.5 0.1 pad_maximum_fusion.1
  15.7 1.7 %collective-permute-start.4 = (bf16[16,4224]{1,0:T(8,128)(2,1)S(1)}, bf16[16,4224]{1,0:T(8,128)(2,1)S(1)}, u32[]{:S(2)}, u32[]{:S(2)}) collective-permute-start(bf16[16,4224]{1,0:T(8,128)(2,1)S(1)} %reshape.85), channel_id=1, source_target_pairs={{0,2},{1,3},{2,0},{3,1},{4,6},{5,7},{6,4},{7,5},{8,10},{9,11},{10,... | collective-permute-start | bytes 405512 | tf_op jit(solution)/shard_map/ppermute | solution.py:14
  17.4 1.5 %collective-permute-start.3 = (bf16[16,4224]{1,0:T(8,128)(2,1)S(1)}, bf16[16,4224]{1,0:T(8,128)(2,1)S(1)}, u32[]{:S(2)}, u32[]{:S(2)}) collective-permute-start(bf16[16,4224]{1,0:T(8,128)(2,1)S(1)} %reshape.85), channel_id=1, source_target_pairs={{0,16},{16,0},{1,17},{17,1},{2,18},{18,2},{3,19},{19,3},{4,20},{20... | collective-permute-start | bytes 405512 | tf_op jit(solution)/shard_map/ppermute | solution.py:14
  18.9 4.0 %fetch_up.1 = (bf16[4096,512]{1,0:T(8,128)(2,1)S(1)}, bf16[4096,512]{1,0:T(8,128)(2,1)S(1)}) custom-call(s32[2]{0:T(128)S(1)} %broadcast_5_rows_from.2.rows_from, bf16[4096,1024]{1,0:T(8,128)(2,1)} %bitcast.72), custom_call_target="tpu_custom_call" | custom-call | bytes 8388608 | tf_op jit(solution)/shard_map/fetch_up/pallas_call | solution.py:38
  23.0 0.6 collective-permute-start.6
  23.6 0.9 %collective-permute-start.5 = (bf16[8,4224]{1,0:T(8,128)(2,1)S(1)}, bf16[8,4224]{1,0:T(8,128)(2,1)S(1)}, u32[]{:S(2)}, u32[]{:S(2)}) collective-permute-start(bf16[8,4224]{1,0:T(8,128)(2,1)S(1)} %slice.61), channel_id=1, source_target_pairs={{0,16},{16,0},{1,17},{17,1},{2,18},{18,2},{3,19},{19,3},{4,20},{20... | collective-permute-start | bytes 202760 | tf_op jit(solution)/shard_map/ppermute | solution.py:14
  24.5 4.3 %fetch_down.1 = (bf16[512,2048]{1,0:T(8,128)(2,1)S(1)}, bf16[512,2048]{1,0:T(8,128)(2,1)S(1)}, bf16[512,2048]{1,0:T(8,128)(2,1)S(1)}, bf16[512,2048]{1,0:T(8,128)(2,1)S(1)}) custom-call(s32[4]{0:T(128)S(1)} %pad_add_fusion.rows_from, bf16[2048,2048]{1,0:T(8,128)(2,1)} %bitcast.73), custom_call_target="tpu_custom_call" | custom-call | bytes 8388608 | tf_op jit(solution)/shard_map/fetch_down/pallas_call | solution.py:38
  28.9 0.1 collective-permute-start.7
  29.0 1.9 %collective-permute-done.7 = bf16[64,4224]{1,0:T(8,128)(2,1)S(1)} collective-permute-done((bf16[64,4224]{1,0:T(8,128)(2,1)S(1)}, bf16[64,4224]{1,0:T(8,128)(2,1)S(1)}, u32[]{:S(2)}, u32[]{:S(2)}) %collective-permute-start.7) | collective-permute-done | bytes 540704 | tf_op jit(solution)/shard_map/ppermute | solution.py:14
  31.0 0.7 %fusion.3 = f32[128,512]{1,0:T(8,128)S(1)} fusion(bf16[4096,512]{1,0:T(8,128)(2,1)S(1)} %copy-done.3, bf16[128,4224]{1,0:T(8,128)(2,1)S(1)} %constant_dynamic-update-slice_fusion), kind=kOutput, calls=%fused_computation.6 | convolution fusion | flops 536870912 | bytes 5505024 | tf_op jit(solution)/shard_map/dot_general | solution.py:125
  31.7 1.5 %copy-done.1 = bf16[4096,512]{1,0:T(8,128)(2,1)S(1)} copy-done((bf16[4096,512]{1,0:T(8,128)(2,1)S(1)}, bf16[4096,512]{1,0:T(8,128)(2,1)}, u32[]{:S(2)}) %copy-start.1) | copy-done | bytes 4194328
  33.2 0.7 %fusion.7 = f32[128,512]{1,0:T(8,128)S(1)} fusion(bf16[4096,512]{1,0:T(8,128)(2,1)S(1)} %copy-done.1, bf16[128,4224]{1,0:T(8,128)(2,1)S(1)} %constant_dynamic-update-slice_fusion), kind=kOutput, calls=%fused_computation.10 | convolution fusion | flops 536870912 | bytes 5505024 | tf_op jit(solution)/shard_map/dot_general | solution.py:125
  33.9 0.7 %multiply_convert_fusion.1 = bf16[128,512]{1,0:T(8,128)(2,1)S(1)} fusion(f32[128,512]{1,0:T(8,128)S(1)} %fusion.7, bf16[4096,512]{1,0:T(8,128)(2,1)S(1)} %get-tuple-element.44, bf16[128,4224]{1,0:T(8,128)(2,1)S(1)} %constant_dynamic-update-slice_fusion), kind=kOutput, calls=%fused_computation.19 | convolution fusion | flops 537264128 | bytes 5636096 | tf_op jit(solution)/shard_map/dot_general | solution.py:126
  34.6 1.2 %collective-permute-start.8 = (bf16[128,512]{1,0:T(8,128)(2,1)S(1)}, bf16[128,512]{1,0:T(8,128)(2,1)S(1)}, u32[]{:S(2)}, u32[]{:S(2)}) collective-permute-start(bf16[128,512]{1,0:T(8,128)(2,1)S(1)} %multiply_convert_fusion.1), channel_id=1, source_target_pairs={{0,16},{16,0},{1,17},{17,1},{2,18},{18,2},{3,19},{19,3},{4,20},{20... | collective-permute-start | bytes 393224 | tf_op jit(solution)/shard_map/ppermute | solution.py:14
  35.8 0.4 fusion.27
  36.2 0.7 %multiply_convert_fusion = bf16[128,512]{1,0:T(8,128)(2,1)S(1)} fusion(f32[128,512]{1,0:T(8,128)S(1)} %fusion.3, bf16[4096,512]{1,0:T(8,128)(2,1)S(1)} %get-tuple-element.47, bf16[128,4224]{1,0:T(8,128)(2,1)S(1)} %constant_dynamic-update-slice_fusion), kind=kOutput, calls=%fused_computation.18 | convolution fusion | flops 537264128 | bytes 5636096 | tf_op jit(solution)/shard_map/dot_general | solution.py:126
  37.0 1.0 %collective-permute-start.9 = (bf16[128,512]{1,0:T(8,128)(2,1)S(1)}, bf16[128,512]{1,0:T(8,128)(2,1)S(1)}, u32[]{:S(2)}, u32[]{:S(2)}) collective-permute-start(bf16[128,512]{1,0:T(8,128)(2,1)S(1)} %multiply_convert_fusion), channel_id=1, source_target_pairs={{0,16},{16,0},{1,17},{17,1},{2,18},{18,2},{3,19},{19,3},{4,20},{20... | collective-permute-start | bytes 393224 | tf_op jit(solution)/shard_map/ppermute | solution.py:14
  37.9 0.4 convolution_add_fusion.2
  38.4 0.1 select_reduce_fusion
  38.5 2.4 %collective-permute-done.8 = bf16[128,512]{1,0:T(8,128)(2,1)S(1)} collective-permute-done((bf16[128,512]{1,0:T(8,128)(2,1)S(1)}, bf16[128,512]{1,0:T(8,128)(2,1)S(1)}, u32[]{:S(2)}, u32[]{:S(2)}) %collective-permute-start.8) | collective-permute-done | bytes 131104 | tf_op jit(solution)/shard_map/ppermute | solution.py:14
  41.0 2.1 %collective-permute-done.9 = bf16[128,512]{1,0:T(8,128)(2,1)S(1)} collective-permute-done((bf16[128,512]{1,0:T(8,128)(2,1)S(1)}, bf16[128,512]{1,0:T(8,128)(2,1)S(1)}, u32[]{:S(2)}, u32[]{:S(2)}) %collective-permute-start.9) | collective-permute-done | bytes 131104 | tf_op jit(solution)/shard_map/ppermute | solution.py:14
  43.1 0.5 convolution_add_fusion.1
  43.6 0.5 fusion
  44.1 0.1 convert_element_type.104
  44.2 0.1 collective-permute-start.10
  44.4 0.1 squeeze.29
  44.5 1.3 %collective-permute-done.10 = bf16[2,2,1,4,4,2048]{5,4,3,1,0,2:T(4,128)(2,1)S(1)} collective-permute-done((bf16[2,2,1,4,4,2048]{5,4,3,1,0,2:T(4,128)(2,1)S(1)}, bf16[2,2,1,4,4,2048]{5,4,3,1,0,2:T(4,128)(2,1)S(1)}, u32[]{:S(2)}, u32[]{:S(2)}) %collective-permute-start.10) | collective-permute-done | bytes 262176 | tf_op jit(solution)/shard_map/ppermute | solution.py:14
  45.9 1.6 %collective-permute-start.11 = (bf16[2,1,4,4,2048]{4,3,2,0,1:T(4,128)(2,1)S(1)}, bf16[2,1,4,4,2048]{4,3,2,0,1:T(4,128)(2,1)S(1)}, u32[]{:S(2)}, u32[]{:S(2)}) collective-permute-start(bf16[2,1,4,4,2048]{4,3,2,0,1:T(4,128)(2,1)S(1)} %fusion.10), channel_id=1, source_target_pairs={{0,2},{1,3},{2,0},{3,1},{4,6},{5,7},{6,4},{7,5},{8,10},{9,11},{10,... | collective-permute-start | bytes 393224 | tf_op jit(solution)/shard_map/ppermute | solution.py:14
  47.5 4.0 %collective-permute-done.11 = bf16[2,1,4,4,2048]{4,3,2,0,1:T(4,128)(2,1)S(1)} collective-permute-done((bf16[2,1,4,4,2048]{4,3,2,0,1:T(4,128)(2,1)S(1)}, bf16[2,1,4,4,2048]{4,3,2,0,1:T(4,128)(2,1)S(1)}, u32[]{:S(2)}, u32[]{:S(2)}) %collective-permute-start.11) | collective-permute-done | bytes 131104 | tf_op jit(solution)/shard_map/ppermute | solution.py:14
  51.6 0.1 fusion.23
  51.7 1.3 %collective-permute-start.12 = (bf16[2,1,4,2048]{3,2,0,1:T(4,128)(2,1)S(1)}, bf16[2,1,4,2048]{3,2,0,1:T(4,128)(2,1)S(1)}, u32[]{:S(2)}, u32[]{:S(2)}) collective-permute-start(bf16[2,1,4,2048]{3,2,0,1:T(4,128)(2,1)S(1)} %get-tuple-element.53), channel_id=1, source_target_pairs={{0,4},{1,5},{2,6},{3,7},{4,0},{5,1},{6,2},{7,3},{8,12},{9,13},{10,... | collective-permute-start | bytes 98312 | tf_op jit(solution)/shard_map/ppermute | solution.py:14
  53.0 2.4 %collective-permute-start.14 = (bf16[2,1,4,2048]{3,2,0,1:T(4,128)(2,1)S(1)}, bf16[2,1,4,2048]{3,2,0,1:T(4,128)(2,1)S(1)}, u32[]{:S(2)}, u32[]{:S(2)}) collective-permute-start(bf16[2,1,4,2048]{3,2,0,1:T(4,128)(2,1)S(1)} %get-tuple-element.54), channel_id=1, source_target_pairs={{0,12},{1,13},{2,14},{3,15},{4,8},{5,9},{6,10},{7,11},{8,4},{9,5},... | collective-permute-start | bytes 98312 | tf_op jit(solution)/shard_map/ppermute | solution.py:14
  55.4 0.5 collective-permute-start.13
  55.9 3.0 %collective-permute-done.14 = bf16[2,1,4,2048]{3,2,0,1:T(4,128)(2,1)S(1)} collective-permute-done((bf16[2,1,4,2048]{3,2,0,1:T(4,128)(2,1)S(1)}, bf16[2,1,4,2048]{3,2,0,1:T(4,128)(2,1)S(1)}, u32[]{:S(2)}, u32[]{:S(2)}) %collective-permute-start.14) | collective-permute-done | bytes 32800 | tf_op jit(solution)/shard_map/ppermute | solution.py:14
  59.0 1.3 %collective-permute-done.13 = bf16[2,1,4,2048]{3,2,0,1:T(4,128)(2,1)S(1)} collective-permute-done((bf16[2,1,4,2048]{3,2,0,1:T(4,128)(2,1)S(1)}, bf16[2,1,4,2048]{3,2,0,1:T(4,128)(2,1)S(1)}, u32[]{:S(2)}, u32[]{:S(2)}) %collective-permute-start.13) | collective-permute-done | bytes 32800 | tf_op jit(solution)/shard_map/ppermute | solution.py:14
  60.3 1.2 %collective-permute-start.15 = (bf16[4,2048]{1,0:T(4,128)(2,1)S(1)}, bf16[4,2048]{1,0:T(4,128)(2,1)S(1)}, u32[]{:S(2)}, u32[]{:S(2)}) collective-permute-start(bf16[4,2048]{1,0:T(4,128)(2,1)S(1)} %slice_bitcast_fusion.5), channel_id=1, source_target_pairs={{0,16},{16,0},{1,17},{17,1},{2,18},{18,2},{3,19},{19,3},{4,20},{20... | collective-permute-start | bytes 49160 | tf_op jit(solution)/shard_map/ppermute | solution.py:14
  61.5 2.6 %collective-permute-done.15 = bf16[4,2048]{1,0:T(4,128)(2,1)S(1)} collective-permute-done((bf16[4,2048]{1,0:T(4,128)(2,1)S(1)}, bf16[4,2048]{1,0:T(4,128)(2,1)S(1)}, u32[]{:S(2)}, u32[]{:S(2)}) %collective-permute-start.15) | collective-permute-done | bytes 16416 | tf_op jit(solution)/shard_map/ppermute | solution.py:14
  64.1 0.6 reverse_select_fusion
  (39 shorter events, 0.6 us)
Async XLA Ops:
  1.7 13.8 %collective-permute-start.2 = (bf16[4,4224]{1,0:T(4,128)(2,1)S(1)}, bf16[4,4224]{1,0:T(4,128)(2,1)S(1)}, u32[]{:S(2)}, u32[]{:S(2)}) collective-permute-start(bf16[4,4224]{1,0:T(4,128)(2,1)S(1)} %get-tuple-element.61), channel_id=1, source_target_pairs={{0,12},{1,13},{2,14},{3,15},{4,8},{5,9},{6,10},{7,11},{8,4},{9,5},... | collective-permute-start | bytes 101384 | tf_op jit(solution)/shard_map/ppermute | solution.py:14
  6.8 8.7 %collective-permute-start.1 = (bf16[4,4224]{1,0:T(4,128)(2,1)S(1)}, bf16[4,4224]{1,0:T(4,128)(2,1)S(1)}, u32[]{:S(2)}, u32[]{:S(2)}) collective-permute-start(bf16[4,4224]{1,0:T(4,128)(2,1)S(1)} %get-tuple-element.61), channel_id=1, source_target_pairs={{0,8},{1,9},{2,10},{3,11},{4,12},{5,13},{6,14},{7,15},{8,0},{9,1},... | collective-permute-start | bytes 101384 | tf_op jit(solution)/shard_map/ppermute | solution.py:14
  6.8 8.7 %collective-permute-start = (bf16[4,4224]{1,0:T(4,128)(2,1)S(1)}, bf16[4,4224]{1,0:T(4,128)(2,1)S(1)}, u32[]{:S(2)}, u32[]{:S(2)}) collective-permute-start(bf16[4,4224]{1,0:T(4,128)(2,1)S(1)} %get-tuple-element.61), channel_id=1, source_target_pairs={{0,4},{1,5},{2,6},{3,7},{4,0},{5,1},{6,2},{7,3},{8,12},{9,13},{10,... | collective-permute-start | bytes 101384 | tf_op jit(solution)/shard_map/ppermute | solution.py:14
  11.5 1.9 %copy-start = (bf16[4096,512]{1,0:T(8,128)(2,1)}, bf16[4096,512]{1,0:T(8,128)(2,1)S(1)}, u32[]{:S(2)}) copy-start(bf16[4096,512]{1,0:T(8,128)(2,1)S(1)} %get-tuple-element.43) | copy-start | bytes 12582916
  13.5 2.0 %copy-start.2 = (bf16[4096,512]{1,0:T(8,128)(2,1)}, bf16[4096,512]{1,0:T(8,128)(2,1)S(1)}, u32[]{:S(2)}) copy-start(bf16[4096,512]{1,0:T(8,128)(2,1)S(1)} %get-tuple-element.46) | copy-start | bytes 12582916
  15.7 7.3 %collective-permute-start.4 = (bf16[16,4224]{1,0:T(8,128)(2,1)S(1)}, bf16[16,4224]{1,0:T(8,128)(2,1)S(1)}, u32[]{:S(2)}, u32[]{:S(2)}) collective-permute-start(bf16[16,4224]{1,0:T(8,128)(2,1)S(1)} %reshape.85), channel_id=1, source_target_pairs={{0,2},{1,3},{2,0},{3,1},{4,6},{5,7},{6,4},{7,5},{8,10},{9,11},{10,... | collective-permute-start | bytes 405512 | tf_op jit(solution)/shard_map/ppermute | solution.py:14
  17.4 5.6 %collective-permute-start.3 = (bf16[16,4224]{1,0:T(8,128)(2,1)S(1)}, bf16[16,4224]{1,0:T(8,128)(2,1)S(1)}, u32[]{:S(2)}, u32[]{:S(2)}) collective-permute-start(bf16[16,4224]{1,0:T(8,128)(2,1)S(1)} %reshape.85), channel_id=1, source_target_pairs={{0,16},{16,0},{1,17},{17,1},{2,18},{18,2},{3,19},{19,3},{4,20},{20... | collective-permute-start | bytes 405512 | tf_op jit(solution)/shard_map/ppermute | solution.py:14
  23.0 5.8 %collective-permute-start.6 = (bf16[8,4224]{1,0:T(8,128)(2,1)S(1)}, bf16[8,4224]{1,0:T(8,128)(2,1)S(1)}, u32[]{:S(2)}, u32[]{:S(2)}) collective-permute-start(bf16[8,4224]{1,0:T(8,128)(2,1)S(1)} %slice.62), channel_id=1, source_target_pairs={{0,2},{1,3},{2,0},{3,1},{4,6},{5,7},{6,4},{7,5},{8,10},{9,11},{10,... | collective-permute-start | bytes 202760 | tf_op jit(solution)/shard_map/ppermute | solution.py:14
  23.6 5.3 %collective-permute-start.5 = (bf16[8,4224]{1,0:T(8,128)(2,1)S(1)}, bf16[8,4224]{1,0:T(8,128)(2,1)S(1)}, u32[]{:S(2)}, u32[]{:S(2)}) collective-permute-start(bf16[8,4224]{1,0:T(8,128)(2,1)S(1)} %slice.61), channel_id=1, source_target_pairs={{0,16},{16,0},{1,17},{17,1},{2,18},{18,2},{3,19},{19,3},{4,20},{20... | collective-permute-start | bytes 202760 | tf_op jit(solution)/shard_map/ppermute | solution.py:14
  24.5 6.5 %copy-start.3 = (bf16[4096,512]{1,0:T(8,128)(2,1)S(1)}, bf16[4096,512]{1,0:T(8,128)(2,1)}, u32[]{:S(2)}) copy-start(bf16[4096,512]{1,0:T(8,128)(2,1)} %copy-done.2) | copy-start | bytes 12582916
  28.9 2.0 %collective-permute-start.7 = (bf16[64,4224]{1,0:T(8,128)(2,1)S(1)}, bf16[64,4224]{1,0:T(8,128)(2,1)S(1)}, u32[]{:S(2)}, u32[]{:S(2)}) collective-permute-start(bf16[64,4224]{1,0:T(8,128)(2,1)S(1)} %pad_maximum_fusion), channel_id=1, source_target_pairs={{0,1},{1,0},{2,3},{3,2},{4,5},{5,4},{6,7},{7,6},{8,9},{9,8},{10,11... | collective-permute-start | bytes 1622024 | tf_op jit(solution)/shard_map/ppermute | solution.py:14
  31.0 2.2 %copy-start.1 = (bf16[4096,512]{1,0:T(8,128)(2,1)S(1)}, bf16[4096,512]{1,0:T(8,128)(2,1)}, u32[]{:S(2)}) copy-start(bf16[4096,512]{1,0:T(8,128)(2,1)} %copy-done) | copy-start | bytes 12582916
  34.6 6.3 %collective-permute-start.8 = (bf16[128,512]{1,0:T(8,128)(2,1)S(1)}, bf16[128,512]{1,0:T(8,128)(2,1)S(1)}, u32[]{:S(2)}, u32[]{:S(2)}) collective-permute-start(bf16[128,512]{1,0:T(8,128)(2,1)S(1)} %multiply_convert_fusion.1), channel_id=1, source_target_pairs={{0,16},{16,0},{1,17},{17,1},{2,18},{18,2},{3,19},{19,3},{4,20},{20... | collective-permute-start | bytes 393224 | tf_op jit(solution)/shard_map/ppermute | solution.py:14
  37.0 6.1 %collective-permute-start.9 = (bf16[128,512]{1,0:T(8,128)(2,1)S(1)}, bf16[128,512]{1,0:T(8,128)(2,1)S(1)}, u32[]{:S(2)}, u32[]{:S(2)}) collective-permute-start(bf16[128,512]{1,0:T(8,128)(2,1)S(1)} %multiply_convert_fusion), channel_id=1, source_target_pairs={{0,16},{16,0},{1,17},{17,1},{2,18},{18,2},{3,19},{19,3},{4,20},{20... | collective-permute-start | bytes 393224 | tf_op jit(solution)/shard_map/ppermute | solution.py:14
  44.2 1.6 %collective-permute-start.10 = (bf16[2,2,1,4,4,2048]{5,4,3,1,0,2:T(4,128)(2,1)S(1)}, bf16[2,2,1,4,4,2048]{5,4,3,1,0,2:T(4,128)(2,1)S(1)}, u32[]{:S(2)}, u32[]{:S(2)}) collective-permute-start(bf16[2,2,1,4,4,2048]{5,4,3,1,0,2:T(4,128)(2,1)S(1)} %convert_element_type.104), channel_id=1, source_target_pairs={{0,1},{1,0},{2,3},{3,2},{4,5},{5,4},{6,7},{7,6},{8,9},{9,8},{10,11... | collective-permute-start | bytes 786440 | tf_op jit(solution)/shard_map/ppermute | solution.py:14
  45.9 5.6 %collective-permute-start.11 = (bf16[2,1,4,4,2048]{4,3,2,0,1:T(4,128)(2,1)S(1)}, bf16[2,1,4,4,2048]{4,3,2,0,1:T(4,128)(2,1)S(1)}, u32[]{:S(2)}, u32[]{:S(2)}) collective-permute-start(bf16[2,1,4,4,2048]{4,3,2,0,1:T(4,128)(2,1)S(1)} %fusion.10), channel_id=1, source_target_pairs={{0,2},{1,3},{2,0},{3,1},{4,6},{5,7},{6,4},{7,5},{8,10},{9,11},{10,... | collective-permute-start | bytes 393224 | tf_op jit(solution)/shard_map/ppermute | solution.py:14
  51.7 4.2 %collective-permute-start.12 = (bf16[2,1,4,2048]{3,2,0,1:T(4,128)(2,1)S(1)}, bf16[2,1,4,2048]{3,2,0,1:T(4,128)(2,1)S(1)}, u32[]{:S(2)}, u32[]{:S(2)}) collective-permute-start(bf16[2,1,4,2048]{3,2,0,1:T(4,128)(2,1)S(1)} %get-tuple-element.53), channel_id=1, source_target_pairs={{0,4},{1,5},{2,6},{3,7},{4,0},{5,1},{6,2},{7,3},{8,12},{9,13},{10,... | collective-permute-start | bytes 98312 | tf_op jit(solution)/shard_map/ppermute | solution.py:14
  53.0 6.0 %collective-permute-start.14 = (bf16[2,1,4,2048]{3,2,0,1:T(4,128)(2,1)S(1)}, bf16[2,1,4,2048]{3,2,0,1:T(4,128)(2,1)S(1)}, u32[]{:S(2)}, u32[]{:S(2)}) collective-permute-start(bf16[2,1,4,2048]{3,2,0,1:T(4,128)(2,1)S(1)} %get-tuple-element.54), channel_id=1, source_target_pairs={{0,12},{1,13},{2,14},{3,15},{4,8},{5,9},{6,10},{7,11},{8,4},{9,5},... | collective-permute-start | bytes 98312 | tf_op jit(solution)/shard_map/ppermute | solution.py:14
  55.4 4.8 %collective-permute-start.13 = (bf16[2,1,4,2048]{3,2,0,1:T(4,128)(2,1)S(1)}, bf16[2,1,4,2048]{3,2,0,1:T(4,128)(2,1)S(1)}, u32[]{:S(2)}, u32[]{:S(2)}) collective-permute-start(bf16[2,1,4,2048]{3,2,0,1:T(4,128)(2,1)S(1)} %get-tuple-element.55), channel_id=1, source_target_pairs={{0,8},{1,9},{2,10},{3,11},{4,12},{5,13},{6,14},{7,15},{8,0},{9,1},... | collective-permute-start | bytes 98312 | tf_op jit(solution)/shard_map/ppermute | solution.py:14
  60.3 3.8 %collective-permute-start.15 = (bf16[4,2048]{1,0:T(4,128)(2,1)S(1)}, bf16[4,2048]{1,0:T(4,128)(2,1)S(1)}, u32[]{:S(2)}, u32[]{:S(2)}) collective-permute-start(bf16[4,2048]{1,0:T(4,128)(2,1)S(1)} %slice_bitcast_fusion.5), channel_id=1, source_target_pairs={{0,16},{16,0},{1,17},{17,1},{2,18},{18,2},{3,19},{19,3},{4,20},{20... | collective-permute-start | bytes 49160 | tf_op jit(solution)/shard_map/ppermute | solution.py:14

commit v3 on v0

v3 whole, which is shorter than its diff:
```python
import jax
import jax.numpy as jnp
from jax import lax
from jax.experimental import pallas as pl
from jax.experimental.pallas import tpu as pltpu
from jax.sharding import Mesh
from jax.sharding import PartitionSpec as P

CHUNKS = 2
TILE = 256
BATCH = 128


def swap(value, axis, offset):
    size = lax.axis_size(axis)
    return lax.ppermute(value, axis, [((i + offset) % size, i) for i in range(size)])


def in_vmem(weights):
    return pltpu.with_memory_space_constraint(weights, pltpu.VMEM)


def row_batches(count, step):
    batch = min(BATCH, count)
    if count == batch:
        step(0, batch)
    else:

        @pl.loop(0, count // batch)
        def _(i):
            step(pl.multiple_of(i * batch, batch), batch)


def expand_rows(rows, w_gate, w_up, start, columns):
    count, depth = rows.shape[0], w_gate.shape[0]

    def body(rows_ref, gate_ref, up_ref, hidden_ref):
        def step(first, batch):
            x = rows_ref[pl.ds(first, batch), :depth]
            tile = min(TILE, columns)
            for i in range(0, columns, tile):
                cut = slice(start + i, start + i + tile)
                gate = jnp.dot(x, gate_ref[:, cut], preferred_element_type=jnp.float32)
                up = jnp.dot(x, up_ref[:, cut], preferred_element_type=jnp.float32)
                value = gate / (1.0 + jnp.exp(-gate)) * up
                hidden_ref[pl.ds(first, batch), i : i + tile] = value.astype(hidden_ref.dtype)

        row_batches(count, step)

    return pl.pallas_call(
        body,
        out_shape=jax.ShapeDtypeStruct((count, columns), rows.dtype),
        in_specs=[pl.BlockSpec(memory_space=pltpu.VMEM)] * 3,
        out_specs=pl.BlockSpec(memory_space=pltpu.VMEM),
        cost_estimate=pl.CostEstimate(flops=0, bytes_accessed=count * columns, transcendentals=0),
        compiler_params=pltpu.CompilerParams(vmem_limit_bytes=24 << 20),
        name="expand_rows",
    )(rows, w_gate, w_up)


def contract_hidden(parts, first_units, w_down, before=None, scale=None):
    count, width = parts[0].shape[0], w_down.shape[1]
    def body(first_ref, down_ref, *refs):
        parts_refs = refs[: len(parts)]

        def step(first, batch):
            here = pl.ds(first, batch)
            tile = min(2 * TILE, width)
            for i in range(0, width, tile):
                cut = slice(i, i + tile)
                total = 0.0 if before is None else refs[len(parts)][here, cut]
                for j, part in enumerate(parts_refs):
                    units = pl.ds(pl.multiple_of(first_ref[j], 128), part.shape[1])
                    total = total + jnp.dot(
                        part[here, :], down_ref[units, cut], preferred_element_type=jnp.float32
                    )
                if scale is not None:
                    total = total.astype(w_down.dtype).astype(jnp.float32)
                    total = total * refs[len(parts) + 1][here, :]
                refs[-1][here, cut] = total

        row_batches(count, step)

    extra = [value for value in (before, scale) if value is not None]
    return pl.pallas_call(
        body,
        out_shape=jax.ShapeDtypeStruct((count, width), jnp.float32),
        in_specs=[pl.BlockSpec(memory_space=pltpu.SMEM)]
        + [pl.BlockSpec(memory_space=pltpu.VMEM)] * (1 + len(parts) + len(extra)),
        out_specs=pl.BlockSpec(memory_space=pltpu.VMEM),
        cost_estimate=pl.CostEstimate(flops=0, bytes_accessed=count * width, transcendentals=0),
        compiler_params=pltpu.CompilerParams(vmem_limit_bytes=24 << 20),
        name="contract_hidden",
    )(jnp.stack(first_units), w_down, *parts, *extra)


def gate_table(expert_ids, gate_probs, experts):
    hit = expert_ids[:, :, None] == jnp.arange(experts, dtype=jnp.int32)
    table = jnp.sum(jnp.where(hit, gate_probs[:, :, None], 0.0), axis=1)
    parts = []
    for _ in range(3):
        part = lax.reduce_precision(table, 8, 7)
        parts.append(part.astype(jnp.bfloat16))
        table = table - part
    table = jnp.concatenate(parts, axis=1)
    return jnp.pad(table, ((0, 0), (0, -table.shape[1] % 128)))


def local(tokens, expert_ids, gate_probs, w_gate, w_up, w_down):
    token_count, width = tokens.shape
    groups, cores = lax.axis_size("dp"), lax.axis_size("core")
    experts = lax.axis_size("far") * cores
    me, group = lax.axis_index(("far", "core")), lax.axis_index("dp")
    w_gate, w_up, w_down = in_vmem(w_gate[0]), in_vmem(w_up[0]), in_vmem(w_down[0])

    table = gate_table(expert_ids, gate_probs, experts)
    block = jnp.concatenate([tokens, table], axis=1)
    rows = lax.all_gather(block, ("dp", "far"), axis=1, tiled=True)
    rows = rows.reshape(token_count, -1, block.shape[1]).transpose(1, 0, 2)
    rows = rows.reshape(-1, block.shape[1])
    rows = jnp.concatenate([rows] + [swap(rows, "core", i) for i in range(1, cores)])
    tables = rows[:, width:]
    slot = jnp.arange(table.shape[1])
    mine = (slot % experts == me) & (slot < 3 * experts)
    scale = jnp.sum(
        jnp.where(mine, tables.astype(jnp.float32), 0.0), axis=1, keepdims=True
    )

    units = w_gate.shape[1]
    chunks = CHUNKS if units % (128 * CHUNKS) == 0 else 1
    step = units // chunks
    total, others, other_units = None, [], []
    for i in range(chunks):
        if total is not None:
            rows, total = lax.optimization_barrier((rows, total))
        hidden = expand_rows(rows, w_gate, w_up, i * step, step)
        for offset in range(1, groups):
            others.append(swap(hidden, "dp", offset))
            other_units.append((group + offset) % groups * units + i * step)
        total = contract_hidden([hidden], [group * units + i * step], w_down, total)
    total = contract_hidden(others, other_units, w_down, total, scale)

    total = total.reshape(cores, -1, w_down.shape[1])
    kept = total[0]
    for i in range(1, cores):
        kept = kept + swap(total[cores - i].astype(jnp.bfloat16), "core", i).astype(jnp.float32)
    blocks = kept.astype(jnp.bfloat16).reshape(-1, token_count, w_down.shape[1])
    blocks = lax.all_to_all(blocks, ("dp", "far"), split_axis=0, concat_axis=0, tiled=True)
    blocks = blocks.reshape(groups, -1, token_count, w_down.shape[1]).astype(jnp.float32)
    combined = jnp.sum(blocks, axis=1).astype(jnp.bfloat16)
    return combined.transpose(1, 0, 2).reshape(token_count, width)


def solution(mesh):
    groups, experts = mesh.devices.shape
    split = Mesh(mesh.devices.reshape(groups, experts // 2, 2), ("dp", "far", "core"))
    row, expert = P(("dp", "far", "core"), None), P(("far", "core"), None, "dp")
    return jax.shard_map(
        local,
        mesh=split,
        in_specs=(row, row, row, expert, expert, expert),
        out_specs=row,
        check_vma=False,
    )
```

time: 111 us -> 92.8 us (0.84)
  waiting for transfers between devices: 35.1 us -> 3.45 us
  blocking collectives: 40.2 us -> 58.4 us
  local copies, waits for them, and re-layouts: 5.59 us -> 20.5 us
  between operations: 13.5 us -> 0.18 us
  matrix products: 9.24 us -> 0 us
  Pallas kernels: 0 us -> 4.95 us
  starting transfers between devices: 5.62 us -> 2.31 us
  other arithmetic: 1.1 us -> 2.63 us
    all_gather x1, blocking collectives: 8.72 us -> 45.3 us  [local(): rows = lax.all_gather(block, ('dp', 'far'), axis=1, tiled=True)]
    all_gather x1 -> x0, waiting for transfers between devices: 20.9 us -> none  [local(): lax.all_gather(arrived.reshape(experts * capacity, width), 'dp', axis=0,...]
    unnamed x12 -> x17, local copies, waits for them, and re-layouts: 1.32 us -> 20.1 us
    all_to_all x2 -> x1, blocking collectives: 31.5 us -> 13 us  [local(): lax.all_to_all(blocks, ('dp', 'far'), split_axis=0, concat_axis=0, tiled=...]
    all_to_all x1 -> x0, waiting for transfers between devices: 14.3 us -> none  [local(): lax.all_to_all(lax.all_to_all(out_blocks, 'dp', split_axis=0, concat_axis...]
    dot_general x6 -> x0, matrix products: 9.24 us -> none  [the longest x1 5.09 us: local(): jnp.dot(row_block, gate_matrix, preferred_element_type=jnp.float32)]
    all_to_all x1 -> x0, starting transfers between devices: 5.62 us -> none  [local(): lax.all_to_all(lax.all_to_all(out_blocks, 'dp', split_axis=0, concat_axis...]
    pallas_call x0 -> x5, Pallas kernels: none -> 4.95 us  [the longest x2 2.73 us: expand_rows(): pl.pallas_call(body, out_shape=jax.ShapeDtypeStruct((count, columns), row...]
  transfers between devices with their start and end apart: 2 -> 4, of which waited for: 2 -> 3; matrix products, arithmetic and copies ran while one was open for 0% -> 0% of each run, Pallas kernels for 0% -> 2%
where the time goes in v3:
time: 92.8 us; the launch traced here: 92.4 us
  blocking collectives  58.4 us (63%)
  local copies, waits for them, and re-layouts  20.5 us (22%)
  Pallas kernels  4.95 us (5%)
  waiting for transfers between devices  3.45 us (4%)
  other arithmetic  2.63 us (3%)
  starting transfers between devices  2.31 us (2%)
    all_gather x1, blocking collectives, local(): rows = lax.all_gather(block, ('dp', 'far'), axis=1, tiled=True)  45.3 us
    unnamed x17, local copies, waits for them, and re-layouts  20.1 us
    all_to_all x1, blocking collectives, local(): lax.all_to_all(blocks, ('dp', 'far'), split_axis=0, concat_axis=0, tiled=...  13 us
    ppermute x4, waiting for transfers between devices, swap(): lax.ppermute(value, axis, [((i + offset) % size, i) for i in range(size)])  3.45 us
    pallas_call x2, Pallas kernels, expand_rows(): pl.pallas_call(body, out_shape=jax.ShapeDtypeStruct((count, columns), row...  2.73 us
    ppermute x4, starting transfers between devices, swap(): lax.ppermute(value, axis, [((i + offset) % size, i) for i in range(size)])  2.31 us
    pallas_call x3, Pallas kernels, contract_hidden(): pl.pallas_call(body, out_shape=jax.ShapeDtypeStruct((count, width), jnp.f...  2.21 us
  transfers between devices with their start and end apart: 4, of which 3 were waited for; matrix products, arithmetic and copies ran while one was open for 0% of the time, Pallas kernels for 2%

profile of v3, /device:TPU:0, one launch (start us, length us, event | category | flops | bytes accessed | tf_op | source)
XLA Modules:
  0.0 92.4 jit_solution(7635419554397519903)
XLA Ops:
  0.0 0.8 select_reduce_fusion.1
  0.8 0.1 fusion.7
  0.9 0.8 pad_maximum_fusion
  1.7 45.3 %all_gather.3 = bf16[4,67584]{1,0:T(4,128)(2,1)S(1)} all-gather(bf16[4,4224]{1,0:T(4,128)(2,1)S(1)} %pad_maximum_fusion), channel_id=1, replica_groups=mesh['dp'=2,'far'=8,'core'=2] {'dp','far'}, dimensions={1}, use_global_device_ids=true | all-gather | bytes 574464 | tf_op jit(solution)/shard_map/all_gather | solution.py:118
  47.0 0.1 reshape.23
  47.1 0.1 collective-permute-start
  47.3 1.8 %collective-permute-done = bf16[64,4224]{1,0:T(8,128)(2,1)S(1)} collective-permute-done((bf16[64,4224]{1,0:T(8,128)(2,1)S(1)}, bf16[64,4224]{1,0:T(8,128)(2,1)S(1)}, u32[]{:S(2)}, u32[]{:S(2)}) %collective-permute-start) | collective-permute-done | bytes 540704 | tf_op jit(solution)/shard_map/ppermute | solution.py:16
  49.2 0.0 slice-start
  49.2 0.0 copy-start.2
  49.2 3.5 %copy-done.2 = bf16[1,4096,1024]{2,1,0:T(8,128)(2,1)S(1)} copy-done((bf16[1,4096,1024]{2,1,0:T(8,128)(2,1)S(1)}, bf16[1,4096,1024]{2,1,0:T(8,128)(2,1)}, u32[]{:S(2)}) %copy-start.2) | copy-done | bytes 8388632
  52.7 0.0 copy-start.4
  52.7 3.5 %copy-done.4 = bf16[1,4096,1024]{2,1,0:T(8,128)(2,1)S(1)} copy-done((bf16[1,4096,1024]{2,1,0:T(8,128)(2,1)S(1)}, bf16[1,4096,1024]{2,1,0:T(8,128)(2,1)}, u32[]{:S(2)}) %copy-start.4) | copy-done | bytes 8388632
  56.2 0.0 slice-start.1
  56.2 1.4 %expand_rows.2.refs_0_ = bf16[128,512]{1,0:T(8,128)(2,1)S(1)} custom-call(bf16[128,4224]{1,0:T(8,128)(2,1)S(1)} %constant_dynamic-update-slice_fusion.rows_ref, bf16[4096,1024]{1,0:T(8,128)(2,1)S(1)} %bitcast.21, bf16[4096,1024]{1,0:T(8,128)(2,1)S(1)} %bitcast.23), custom_call_target="tpu_custom_call" | custom-call | bytes 65536 | tf_op jit(solution)/shard_map/expand_rows/pallas_call | solution.py:50
  57.6 1.0 %collective-permute-start.1 = (bf16[128,512]{1,0:T(8,128)(2,1)S(1)}, bf16[128,512]{1,0:T(8,128)(2,1)S(1)}, u32[]{:S(2)}, u32[]{:S(2)}) collective-permute-start(bf16[128,512]{1,0:T(8,128)(2,1)S(1)} %expand_rows.2.refs_0_), channel_id=1, source_target_pairs={{16,0},{0,16},{17,1},{1,17},{18,2},{2,18},{19,3},{3,19},{20,4},{4,... | collective-permute-start | bytes 393224 | tf_op jit(solution)/shard_map/ppermute | solution.py:16
  58.6 0.0 slice-done
  58.6 0.0 slice-done.1
  58.6 0.0 copy-start.3
  58.6 0.4 contract_hidden.3.refs_1_
  59.1 2.9 %copy-done.3 = bf16[1,4096,1024]{2,1,0:T(8,128)(2,1)S(1)} copy-done((bf16[1,4096,1024]{2,1,0:T(8,128)(2,1)S(1)}, bf16[1,4096,1024]{2,1,0:T(8,128)(2,1)}, u32[]{:S(2)}) %copy-start.3) | copy-done | bytes 8388632
  62.0 0.0 copy-start.5
  62.0 3.4 %copy-done.5 = bf16[1,4096,1024]{2,1,0:T(8,128)(2,1)S(1)} copy-done((bf16[1,4096,1024]{2,1,0:T(8,128)(2,1)S(1)}, bf16[1,4096,1024]{2,1,0:T(8,128)(2,1)}, u32[]{:S(2)}) %copy-start.5) | copy-done | bytes 8388632
  65.4 1.4 %expand_rows.3.refs_0_ = bf16[128,512]{1,0:T(8,128)(2,1)S(1)} custom-call(bf16[128,4224]{1,0:T(8,128)(2,1)S(1)} %constant_dynamic-update-slice_fusion.rows_ref, bf16[4096,1024]{1,0:T(8,128)(2,1)S(1)} %bitcast.22, bf16[4096,1024]{1,0:T(8,128)(2,1)S(1)} %bitcast.24), custom_call_target="tpu_custom_call" | custom-call | bytes 65536 | tf_op jit(solution)/shard_map/expand_rows/pallas_call | solution.py:50
  66.8 1.1 %collective-permute-start.2 = (bf16[128,512]{1,0:T(8,128)(2,1)S(1)}, bf16[128,512]{1,0:T(8,128)(2,1)S(1)}, u32[]{:S(2)}, u32[]{:S(2)}) collective-permute-start(bf16[128,512]{1,0:T(8,128)(2,1)S(1)} %expand_rows.3.refs_0_), channel_id=1, source_target_pairs={{16,0},{0,16},{17,1},{1,17},{18,2},{2,18},{19,3},{3,19},{20,4},{4,... | collective-permute-start | bytes 393224 | tf_op jit(solution)/shard_map/ppermute | solution.py:16
  67.9 0.1 pad_add_fusion.first_ref
  68.0 0.1 select_reduce_fusion
  68.1 0.1 copy.12.refs_3_
  68.2 0.0 copy-start
  68.2 3.4 %copy-done = bf16[1,2048,2048]{2,1,0:T(8,128)(2,1)S(1)} copy-done((bf16[1,2048,2048]{2,1,0:T(8,128)(2,1)S(1)}, bf16[1,2048,2048]{2,1,0:T(8,128)(2,1)}, u32[]{:S(2)}) %copy-start) | copy-done | bytes 8388632
  71.6 0.4 contract_hidden.4.refs_2_
  72.0 0.0 collective-permute-done.1.refs_0_
  72.1 0.1 collective-permute-done.2.refs_1_
  72.1 0.0 copy-start.1
  72.1 3.4 %copy-done.1 = bf16[1,2048,2048]{2,1,0:T(8,128)(2,1)S(1)} copy-done((bf16[1,2048,2048]{2,1,0:T(8,128)(2,1)S(1)}, bf16[1,2048,2048]{2,1,0:T(8,128)(2,1)}, u32[]{:S(2)}) %copy-start.1) | copy-done | bytes 8388632
  75.5 1.3 %contract_hidden.5 = f32[128,2048]{1,0:T(8,128)S(1)} custom-call(s32[2]{0:T(128)S(1)} %pad_add_fusion.first_ref, bf16[2048,2048]{1,0:T(8,128)(2,1)S(1)} %bitcast.20, bf16[128,512]{1,0:T(8,128)(2,1)S(1)} %collective-permute-done.1.refs_0_, bf16[128,512]{1,0:T(8,128)(2,1)S(1)} %collective-permute-done.2.refs_1_, f32[128,2048]{1,0:T(8,128)S(1)} %contract_hidden.4.refs_2_, ...), custom_call_target="tpu_custom_call" | custom-call | bytes 262144 | tf_op jit(solution)/shard_map/contract_hidden/pallas_call | solution.py:85
  76.9 0.1 collective-permute-start.3
  77.0 1.5 %collective-permute-done.3 = bf16[64,2048]{1,0:T(8,128)(2,1)S(1)} collective-permute-done((bf16[64,2048]{1,0:T(8,128)(2,1)S(1)}, bf16[64,2048]{1,0:T(8,128)(2,1)S(1)}, u32[]{:S(2)}, u32[]{:S(2)}) %collective-permute-start.3) | collective-permute-done | bytes 262176 | tf_op jit(solution)/shard_map/ppermute | solution.py:16
  78.5 0.1 fusion
  78.6 0.1 reshape.24
  78.7 13.0 %all_to_all.5 = bf16[16,4,2048]{2,1,0:T(4,128)(2,1)S(1)} all-to-all(bf16[16,4,2048]{2,1,0:T(4,128)(2,1)S(1)} %reshape.24), channel_id=1, replica_groups=mesh['dp'=2,'far'=8,'core'=2] {'dp','far'}, dimensions={0} | all-to-all | bytes 524288 | tf_op jit(solution)/shard_map/all_to_all | solution.py:148
  91.7 0.7 bitcast_reduce_fusion
  (6 shorter events, 0.1 us)
Async XLA Ops:
  47.1 2.0 %collective-permute-start = (bf16[64,4224]{1,0:T(8,128)(2,1)S(1)}, bf16[64,4224]{1,0:T(8,128)(2,1)S(1)}, u32[]{:S(2)}, u32[]{:S(2)}) collective-permute-start(bf16[64,4224]{1,0:T(8,128)(2,1)S(1)} %reshape.23), channel_id=1, source_target_pairs={{1,0},{0,1},{3,2},{2,3},{5,4},{4,5},{7,6},{6,7},{9,8},{8,9},{11,10... | collective-permute-start | bytes 1622024 | tf_op jit(solution)/shard_map/ppermute | solution.py:16
  49.2 9.4 %slice-start = ((s8[8388608]{0:T(1024)(128)(4,1)}), s8[4194304]{0:T(1024)(128)(4,1)S(1)}, s32[]{:S(2)}) async-start(s8[8388608]{0:T(1024)(128)(4,1)} %bitcast.16), calls=%async_computation.1 | async-start | bytes 8388608
  49.2 3.5 %copy-start.2 = (bf16[1,4096,1024]{2,1,0:T(8,128)(2,1)S(1)}, bf16[1,4096,1024]{2,1,0:T(8,128)(2,1)}, u32[]{:S(2)}) copy-start(bf16[1,4096,1024]{2,1,0:T(8,128)(2,1)} %param.9) | copy-start | bytes 25165828
  52.7 3.5 %copy-start.4 = (bf16[1,4096,1024]{2,1,0:T(8,128)(2,1)S(1)}, bf16[1,4096,1024]{2,1,0:T(8,128)(2,1)}, u32[]{:S(2)}) copy-start(bf16[1,4096,1024]{2,1,0:T(8,128)(2,1)} %param.10) | copy-start | bytes 25165828
  56.2 2.4 %slice-start.1 = ((s8[8388608]{0:T(1024)(128)(4,1)}), s8[4194304]{0:T(1024)(128)(4,1)S(1)}, s32[]{:S(2)}) async-start(s8[8388608]{0:T(1024)(128)(4,1)} %bitcast.16), calls=%async_computation.2 | async-start | bytes 8388608
  57.6 14.5 %collective-permute-start.1 = (bf16[128,512]{1,0:T(8,128)(2,1)S(1)}, bf16[128,512]{1,0:T(8,128)(2,1)S(1)}, u32[]{:S(2)}, u32[]{:S(2)}) collective-permute-start(bf16[128,512]{1,0:T(8,128)(2,1)S(1)} %expand_rows.2.refs_0_), channel_id=1, source_target_pairs={{16,0},{0,16},{17,1},{1,17},{18,2},{2,18},{19,3},{3,19},{20,4},{4,... | collective-permute-start | bytes 393224 | tf_op jit(solution)/shard_map/ppermute | solution.py:16
  58.6 3.4 %copy-start.3 = (bf16[1,4096,1024]{2,1,0:T(8,128)(2,1)S(1)}, bf16[1,4096,1024]{2,1,0:T(8,128)(2,1)}, u32[]{:S(2)}) copy-start(bf16[1,4096,1024]{2,1,0:T(8,128)(2,1)} %param.9) | copy-start | bytes 25165828
  62.0 3.4 %copy-start.5 = (bf16[1,4096,1024]{2,1,0:T(8,128)(2,1)S(1)}, bf16[1,4096,1024]{2,1,0:T(8,128)(2,1)}, u32[]{:S(2)}) copy-start(bf16[1,4096,1024]{2,1,0:T(8,128)(2,1)} %param.10) | copy-start | bytes 25165828
  66.8 5.4 %collective-permute-start.2 = (bf16[128,512]{1,0:T(8,128)(2,1)S(1)}, bf16[128,512]{1,0:T(8,128)(2,1)S(1)}, u32[]{:S(2)}, u32[]{:S(2)}) collective-permute-start(bf16[128,512]{1,0:T(8,128)(2,1)S(1)} %expand_rows.3.refs_0_), channel_id=1, source_target_pairs={{16,0},{0,16},{17,1},{1,17},{18,2},{2,18},{19,3},{3,19},{20,4},{4,... | collective-permute-start | bytes 393224 | tf_op jit(solution)/shard_map/ppermute | solution.py:16
  68.2 3.4 %copy-start = (bf16[1,2048,2048]{2,1,0:T(8,128)(2,1)S(1)}, bf16[1,2048,2048]{2,1,0:T(8,128)(2,1)}, u32[]{:S(2)}) copy-start(bf16[1,2048,2048]{2,1,0:T(8,128)(2,1)} %param.11) | copy-start | bytes 25165828
  72.1 3.4 %copy-start.1 = (bf16[1,2048,2048]{2,1,0:T(8,128)(2,1)S(1)}, bf16[1,2048,2048]{2,1,0:T(8,128)(2,1)}, u32[]{:S(2)}) copy-start(bf16[1,2048,2048]{2,1,0:T(8,128)(2,1)} %param.11) | copy-start | bytes 25165828
  76.9 1.6 %collective-permute-start.3 = (bf16[64,2048]{1,0:T(8,128)(2,1)S(1)}, bf16[64,2048]{1,0:T(8,128)(2,1)S(1)}, u32[]{:S(2)}, u32[]{:S(2)}) collective-permute-start(bf16[64,2048]{1,0:T(8,128)(2,1)S(1)} %slice.23), channel_id=1, source_target_pairs={{1,0},{0,1},{3,2},{2,3},{5,4},{4,5},{7,6},{6,7},{9,8},{8,9},{11,10... | collective-permute-start | bytes 786440 | tf_op jit(solution)/shard_map/ppermute | solution.py:16

commit v4 on v3

v4 whole, which is shorter than its diff:
```python
import jax
import jax.numpy as jnp
from jax import lax
from jax.experimental import pallas as pl
from jax.experimental.pallas import tpu as pltpu
from jax.sharding import PartitionSpec as P

CHUNKS = 2
TILE = 256
BATCH = 128
COPIES = 8
LANES = 128


def swap(value, group_mask, expert_mask):
    groups, experts = lax.axis_size("dp"), lax.axis_size("expert")
    pairs = [
        (g * experts + e, (g ^ group_mask) * experts + (e ^ expert_mask))
        for g in range(groups)
        for e in range(experts)
    ]
    return lax.ppermute(value, ("dp", "expert"), pairs)


def row_batches(count, step):
    batch = min(BATCH, count)
    if count == batch:
        step(0, batch)
    else:

        @pl.loop(0, count // batch)
        def _(i):
            step(pl.multiple_of(i * batch, batch), batch)


def pack_block(tokens, expert_ids, gate_probs, experts):
    count, width = tokens.shape
    top = expert_ids.shape[1]

    def body(tokens_ref, ids_ref, probs_ref, block_ref):
        block_ref[:, :width] = tokens_ref[...]
        lane = lax.broadcasted_iota(jnp.int32, (count, LANES), 1)
        table = jnp.zeros((count, LANES), jnp.float32)
        for k in range(top):
            hit = ids_ref[:, k : k + 1] == lax.rem(lane, experts)
            table = jnp.where(hit, probs_ref[:, k : k + 1], table)
        packed = jnp.zeros((count, LANES), jnp.float32)
        for i in range(3):
            part = table.astype(jnp.bfloat16).astype(jnp.float32)
            packed = jnp.where(lane // experts == i, part, packed)
            table = table - part
        block_ref[:, width:] = packed.astype(block_ref.dtype)

    return pl.pallas_call(
        body,
        out_shape=jax.ShapeDtypeStruct((count, width + LANES), tokens.dtype),
        in_specs=[pl.BlockSpec(memory_space=pltpu.VMEM)] * 3,
        out_specs=pl.BlockSpec(memory_space=pltpu.VMEM),
        compiler_params=pltpu.CompilerParams(vmem_limit_bytes=1 << 20),
        name="pack_block",
    )(tokens, expert_ids, gate_probs)


def fetch(weights, after, name):
    weights, _ = lax.optimization_barrier((weights, after))
    weights = pltpu.with_memory_space_constraint(weights, pltpu.HBM)
    piece = weights.shape[0] // COPIES

    def body(source, target, arrived):
        copies = []
        for i in range(COPIES):
            part = pl.ds(i * piece, piece)
            copies.append(pltpu.make_async_copy(source.at[part], target.at[part], arrived.at[i]))
        for copy in copies:
            copy.start()
        for copy in copies:
            copy.wait()

    return pl.pallas_call(
        body,
        out_shape=pltpu.VMEM(weights.shape, weights.dtype),
        in_specs=[pl.BlockSpec(memory_space=pltpu.HBM)],
        out_specs=pl.BlockSpec(memory_space=pltpu.VMEM),
        scratch_shapes=[pltpu.SemaphoreType.DMA((COPIES,))],
        cost_estimate=pl.CostEstimate(flops=0, bytes_accessed=weights.nbytes, transcendentals=0),
        compiler_params=pltpu.CompilerParams(vmem_limit_bytes=1 << 20),
        name=name,
    )(weights)


def in_vmem(value):
    return pltpu.with_memory_space_constraint(value, pltpu.VMEM)


def expand_rows(rows, w_gate, w_up, start, columns):
    count, depth = rows.shape[0], w_gate.shape[0]

    def body(rows_ref, gate_ref, up_ref, hidden_ref):
        def step(first, batch):
            x = rows_ref[pl.ds(first, batch), :depth]
            tile = min(TILE, columns)
            for i in range(0, columns, tile):
                cut = slice(start + i, start + i + tile)
                gate = jnp.dot(x, gate_ref[:, cut], preferred_element_type=jnp.float32)
                up = jnp.dot(x, up_ref[:, cut], preferred_element_type=jnp.float32)
                value = gate / (1.0 + jnp.exp(-gate)) * up
                hidden_ref[pl.ds(first, batch), i : i + tile] = value.astype(hidden_ref.dtype)

        row_batches(count, step)

    return pl.pallas_call(
        body,
        out_shape=jax.ShapeDtypeStruct((count, columns), rows.dtype),
        in_specs=[pl.BlockSpec(memory_space=pltpu.VMEM)] * 3,
        out_specs=pl.BlockSpec(memory_space=pltpu.VMEM),
        cost_estimate=pl.CostEstimate(flops=0, bytes_accessed=count * columns, transcendentals=0),
        compiler_params=pltpu.CompilerParams(vmem_limit_bytes=rows.nbytes + (6 << 20)),
        name="expand_rows",
    )(rows, in_vmem(w_gate), in_vmem(w_up))


def contract_hidden(parts, first_units, w_down, before=None, scale=None):
    count, width = parts[0].shape[0], w_down.shape[1]

    def body(first_ref, down_ref, *refs):
        parts_refs = refs[: len(parts)]

        def step(first, batch):
            here = pl.ds(first, batch)
            tile = min(2 * TILE, width)
            for i in range(0, width, tile):
                cut = slice(i, i + tile)
                total = 0.0 if before is None else refs[len(parts)][here, cut]
                for j, part in enumerate(parts_refs):
                    units = pl.ds(pl.multiple_of(first_ref[j], 128), part.shape[1])
                    total = total + jnp.dot(
                        part[here, :], down_ref[units, cut], preferred_element_type=jnp.float32
                    )
                if scale is not None:
                    total = total.astype(w_down.dtype).astype(jnp.float32)
                    total = total * refs[len(parts) + 1][here, :]
                refs[-1][here, cut] = total

        row_batches(count, step)

    extra = [value for value in (before, scale) if value is not None]
    return pl.pallas_call(
        body,
        out_shape=jax.ShapeDtypeStruct((count, width), jnp.float32),
        in_specs=[pl.BlockSpec(memory_space=pltpu.SMEM)]
        + [pl.BlockSpec(memory_space=pltpu.VMEM)] * (1 + len(parts) + len(extra)),
        out_specs=pl.BlockSpec(memory_space=pltpu.VMEM),
        cost_estimate=pl.CostEstimate(flops=0, bytes_accessed=count * width, transcendentals=0),
        compiler_params=pltpu.CompilerParams(vmem_limit_bytes=8 * count * width + (6 << 20)),
        name="contract_hidden",
    )(jnp.stack(first_units), in_vmem(w_down), *parts, *extra)


def local(tokens, expert_ids, gate_probs, w_gate, w_up, w_down):
    token_count, width = tokens.shape
    groups, experts = lax.axis_size("dp"), lax.axis_size("expert")
    group, me = lax.axis_index("dp"), lax.axis_index("expert")
    wide, high = groups // 2, experts // 4

    block = pack_block(tokens, expert_ids, gate_probs, experts)
    near = jnp.stack([block] + [swap(block, 0, 4 * i) for i in range(1, high)])
    near = near.reshape(-1, block.shape[1])
    gate_weights = fetch(w_gate[0], block, "fetch_gate")
    near, gate_weights = lax.optimization_barrier((near, gate_weights))
    if wide > 1:
        near = jnp.concatenate([near] + [swap(near, 2 * i, 0) for i in range(1, wide)])
    chip = [near, swap(near, 0, 2), swap(near, 1, 0), swap(near, 1, 2)]
    up_weights = fetch(w_up[0], near, "fetch_up")
    down_weights = fetch(w_down[0], near, "fetch_down")
    chip[3], up_weights, down_weights = lax.optimization_barrier(
        (chip[3], up_weights, down_weights)
    )
    chip = jnp.concatenate(chip)
    rows = jnp.concatenate([chip, swap(chip, 0, 1)])
    lane = jnp.arange(LANES)
    mine = (lane % experts == me) & (lane < 3 * experts)
    scale = jnp.where(mine, rows[:, width:].astype(jnp.float32), 0.0)
    scale = jnp.sum(scale, axis=1, keepdims=True)

    units = gate_weights.shape[1]
    chunks = CHUNKS if units % (LANES * CHUNKS) == 0 else 1
    step = units // chunks

    def from_group(value, mask):
        value = swap(value, mask, 0).reshape(2, 2, 2, wide, high * token_count, step)
        if mask & 1:
            value = jnp.concatenate([value[:, 1:], value[:, :1]], axis=1)
        if mask > 1:
            value = jnp.stack([value[:, :, :, i ^ (mask >> 1)] for i in range(wide)], axis=3)
        return value.reshape(-1, step)

    total, others, other_units = None, [], []
    for i in range(chunks):
        if total is not None:
            rows, total = lax.optimization_barrier((rows, total))
        hidden = expand_rows(rows, gate_weights, up_weights, i * step, step)
        for mask in range(1, groups):
            others.append(from_group(hidden, mask))
            other_units.append((group ^ mask) * units + i * step)
        total = contract_hidden([hidden], [group * units + i * step], down_weights, total)
    total = contract_hidden(others, other_units, down_weights, total, scale)

    columns = total.shape[1]
    send = lambda value, g, e: swap(value.astype(jnp.bfloat16), g, e).astype(jnp.float32)
    total = total.reshape(2, -1, columns)
    total = total[0] + send(total[1], 0, 1)
    part = total.shape[0] // 4
    near, over_y, over_x, corner = (total[i * part : (i + 1) * part] for i in range(4))
    total = jnp.concatenate(
        [near + send(over_y, 0, 2), send(over_x, 1, 0) + send(corner, 1, 2)], axis=1
    )
    part = part // wide
    total = jnp.concatenate(
        [total[:part]]
        + [send(total[i * part : (i + 1) * part], 2 * i, 0) for i in range(1, wide)],
        axis=1,
    )
    combined = total[:token_count]
    for i in range(1, high):
        combined = combined + send(total[i * token_count : (i + 1) * token_count], 0, 4 * i)
    combined = combined.astype(jnp.bfloat16)
    if groups == 2:
        swapped = jnp.concatenate([combined[:, columns:], combined[:, :columns]], axis=1)
        return jnp.where(group == 0, combined, swapped)
    combined = combined.reshape(token_count, groups, columns)
    combined = jnp.take(combined, jnp.arange(groups) ^ group, axis=1)
    return combined.reshape(token_count, width)


def solution(mesh):
    row, expert = P(("dp", "expert"), None), P("expert", None, "dp")
    return jax.shard_map(
        local,
        mesh=mesh,
        in_specs=(row, row, row, expert, expert, expert),
        out_specs=row,
        check_vma=False,
    )
```

time: 92.8 us -> 78.4 us (0.84)
  blocking collectives: 58.4 us -> 0 us
  starting transfers between devices: 2.31 us -> 19.6 us
  Pallas kernels: 4.95 us -> 18.5 us
  waiting for transfers between devices: 3.45 us -> 11.9 us
  local copies, waits for them, and re-layouts: 20.5 us -> 26.5 us
  other arithmetic: 2.63 us -> 1.18 us
    all_gather x1 -> x0, blocking collectives: 45.3 us -> none  [local(): rows = lax.all_gather(block, ('dp', 'far'), axis=1, tiled=True)]
    ppermute x4 -> x16, starting transfers between devices: 2.31 us -> 19.6 us  [swap(): return lax.ppermute(value, ('dp', 'expert'), pairs)]
    pallas_call x0 -> x4, Pallas kernels: none -> 13.6 us  [the longest x3 13.5 us: fetch(): pl.pallas_call(body, out_shape=pltpu.VMEM(weights.shape, weights.dtype),...]
    all_to_all x1 -> x0, blocking collectives: 13 us -> none  [local(): lax.all_to_all(blocks, ('dp', 'far'), split_axis=0, concat_axis=0, tiled=...]
    ppermute x4 -> x16, waiting for transfers between devices: 3.45 us -> 11.9 us  [swap(): return lax.ppermute(value, ('dp', 'expert'), pairs)]
    unnamed x17 -> x30, local copies, waits for them, and re-layouts: 20.1 us -> 26.2 us
    reduce_sum x3 -> x1, other arithmetic: 1.62 us -> 0.1 us  [local(): scale = jnp.sum(scale, axis=1, keepdims=True)]
  transfers between devices with their start and end apart: 4 -> 16, of which waited for: 3 -> 8; matrix products, arithmetic and copies ran while one was open for 0% -> 0% of each run, Pallas kernels for 2% -> 20%
where the time goes in v4:
time: 78.4 us; the launch traced here: 78 us
  local copies, waits for them, and re-layouts  26.5 us (34%)
  starting transfers between devices  19.6 us (25%)
  Pallas kernels  18.5 us (24%)
  waiting for transfers between devices  11.9 us (15%)
  other arithmetic  1.18 us (2%)
    unnamed x30, local copies, waits for them, and re-layouts  26.2 us
    ppermute x16, starting transfers between devices, swap(): return lax.ppermute(value, ('dp', 'expert'), pairs)  19.6 us
    pallas_call x3, Pallas kernels, fetch(): pl.pallas_call(body, out_shape=pltpu.VMEM(weights.shape, weights.dtype),...  13.5 us
    ppermute x16, waiting for transfers between devices, swap(): return lax.ppermute(value, ('dp', 'expert'), pairs)  11.9 us
    pallas_call x2, Pallas kernels, expand_rows(): pl.pallas_call(body, out_shape=jax.ShapeDtypeStruct((count, columns), row...  2.7 us
    pallas_call x3, Pallas kernels, contract_hidden(): pl.pallas_call(body, out_shape=jax.ShapeDtypeStruct((count, width), jnp.f...  2.24 us
  transfers between devices with their start and end apart: 16, of which 8 were waited for; matrix products, arithmetic and copies ran while one was open for 0% of the time, Pallas kernels for 20%

profile of v4, /device:TPU:0, one launch (start us, length us, event | category | flops | bytes accessed | tf_op | source)
XLA Modules:
  0.0 78.0 jit_solution(14303677785912272030)
XLA Ops:
  0.0 0.8 copy-done.8
  0.8 0.7 copy-done.9
  1.4 0.7 copy-done.10
  2.1 0.1 pack_block.1
  2.2 5.1 %collective-permute-start.2 = (bf16[4,4224]{1,0:T(4,128)(2,1)S(1)}, bf16[4,4224]{1,0:T(4,128)(2,1)S(1)}, u32[]{:S(2)}, u32[]{:S(2)}) collective-permute-start(bf16[4,4224]{1,0:T(4,128)(2,1)S(1)} %pack_block.1), channel_id=1, source_target_pairs={{0,12},{1,13},{2,14},{3,15},{4,8},{5,9},{6,10},{7,11},{8,4},{9,5},... | collective-permute-start | bytes 101384 | tf_op jit(solution)/shard_map/ppermute | solution.py:22
  7.3 0.0 collective-permute-start.1
  7.3 0.6 collective-permute-start
  8.0 3.5 %fetch_gate.1.gate_ref = bf16[4096,1024]{1,0:T(8,128)(2,1)S(1)} custom-call(bf16[4096,1024]{1,0:T(8,128)(2,1)} %bitcast.21), custom_call_target="tpu_custom_call" | custom-call | bytes 8388608 | tf_op jit(solution)/shard_map/fetch_gate/pallas_call | solution.py:79
  11.5 3.3 %copy-done.4 = bf16[4096,1024]{1,0:T(8,128)(2,1)} copy-done((bf16[4096,1024]{1,0:T(8,128)(2,1)}, bf16[4096,1024]{1,0:T(8,128)(2,1)S(1)}, u32[]{:S(2)}) %copy-start.4) | copy-done | bytes 8388632
  14.7 0.1 pad_maximum_fusion.2
  14.9 2.7 %collective-permute-start.3 = (bf16[16,4224]{1,0:T(8,128)(2,1)S(1)}, bf16[16,4224]{1,0:T(8,128)(2,1)S(1)}, u32[]{:S(2)}, u32[]{:S(2)}) collective-permute-start(bf16[16,4224]{1,0:T(8,128)(2,1)S(1)} %reshape.20), channel_id=1, source_target_pairs={{0,18},{1,19},{2,16},{3,17},{4,22},{5,23},{6,20},{7,21},{8,26},{9,... | collective-permute-start | bytes 405512 | tf_op jit(solution)/shard_map/ppermute | solution.py:22
  17.6 0.5 collective-permute-start.4
  18.1 0.4 collective-permute-start.5
  18.5 3.5 %fetch_up.1.up_ref = bf16[4096,1024]{1,0:T(8,128)(2,1)S(1)} custom-call(bf16[4096,1024]{1,0:T(8,128)(2,1)} %bitcast.22), custom_call_target="tpu_custom_call" | custom-call | bytes 8388608 | tf_op jit(solution)/shard_map/fetch_up/pallas_call | solution.py:79
  22.0 6.5 %fetch_down.1.down_ref = bf16[2048,2048]{1,0:T(8,128)(2,1)S(1)} custom-call(bf16[2048,2048]{1,0:T(8,128)(2,1)} %bitcast.23), custom_call_target="tpu_custom_call" | custom-call | bytes 8388608 | tf_op jit(solution)/shard_map/fetch_down/pallas_call | solution.py:79
  28.5 4.2 %copy-done = bf16[2048,2048]{1,0:T(8,128)(2,1)} copy-done((bf16[2048,2048]{1,0:T(8,128)(2,1)}, bf16[2048,2048]{1,0:T(8,128)(2,1)S(1)}, u32[]{:S(2)}) %copy-start) | copy-done | bytes 8388632
  32.9 0.1 collective-permute-start.6
  33.0 1.9 %collective-permute-done.6 = bf16[64,4224]{1,0:T(8,128)(2,1)S(1)} collective-permute-done((bf16[64,4224]{1,0:T(8,128)(2,1)S(1)}, bf16[64,4224]{1,0:T(8,128)(2,1)S(1)}, u32[]{:S(2)}, u32[]{:S(2)}) %collective-permute-start.6) | collective-permute-done | bytes 540704 | tf_op jit(solution)/shard_map/ppermute | solution.py:22
  34.9 1.3 %expand_rows.2.refs_0_ = bf16[128,512]{1,0:T(8,128)(2,1)S(1)} custom-call(bf16[128,4224]{1,0:T(8,128)(2,1)S(1)} %constant_dynamic-update-slice_fusion.rows_ref, bf16[4096,1024]{1,0:T(8,128)(2,1)S(1)} %bitcast.17, bf16[4096,1024]{1,0:T(8,128)(2,1)S(1)} %fetch_up.1.up_ref), custom_call_target="tpu_custom_call" | custom-call | bytes 65536 | tf_op jit(solution)/shard_map/expand_rows/pallas_call | solution.py:111
  36.3 1.7 %collective-permute-start.7 = (bf16[128,512]{1,0:T(8,128)(2,1)S(1)}, bf16[128,512]{1,0:T(8,128)(2,1)S(1)}, u32[]{:S(2)}, u32[]{:S(2)}) collective-permute-start(bf16[128,512]{1,0:T(8,128)(2,1)S(1)} %expand_rows.2.refs_0_), channel_id=1, source_target_pairs={{0,16},{1,17},{2,18},{3,19},{4,20},{5,21},{6,22},{7,23},{8,24},{9,... | collective-permute-start | bytes 393224 | tf_op jit(solution)/shard_map/ppermute | solution.py:22
  38.0 0.1 pad_add_fusion.first_ref
  38.1 3.4 %copy-done.1 = bf16[2048,2048]{1,0:T(8,128)(2,1)S(1)} copy-done((bf16[2048,2048]{1,0:T(8,128)(2,1)S(1)}, bf16[2048,2048]{1,0:T(8,128)(2,1)}, u32[]{:S(2)}) %copy-start.1) | copy-done | bytes 8388632
  41.4 0.4 contract_hidden.3.refs_1_
  41.9 2.9 %copy-done.7 = bf16[4096,1024]{1,0:T(8,128)(2,1)S(1)} copy-done((bf16[4096,1024]{1,0:T(8,128)(2,1)S(1)}, bf16[4096,1024]{1,0:T(8,128)(2,1)}, u32[]{:S(2)}) %copy-start.7) | copy-done | bytes 8388632
  44.8 3.4 %copy-done.5 = bf16[4096,1024]{1,0:T(8,128)(2,1)S(1)} copy-done((bf16[4096,1024]{1,0:T(8,128)(2,1)S(1)}, bf16[4096,1024]{1,0:T(8,128)(2,1)}, u32[]{:S(2)}) %copy-start.5) | copy-done | bytes 8388632
  48.2 1.4 %expand_rows.3.refs_0_ = bf16[128,512]{1,0:T(8,128)(2,1)S(1)} custom-call(bf16[128,4224]{1,0:T(8,128)(2,1)S(1)} %constant_dynamic-update-slice_fusion.rows_ref, bf16[4096,1024]{1,0:T(8,128)(2,1)S(1)} %copy-done.5, bf16[4096,1024]{1,0:T(8,128)(2,1)S(1)} %copy-done.7), custom_call_target="tpu_custom_call" | custom-call | bytes 65536 | tf_op jit(solution)/shard_map/expand_rows/pallas_call | solution.py:111
  49.6 0.5 collective-permute-start.8
  50.0 0.1 select_reduce_fusion
  50.1 0.1 copy.7.refs_3_
  50.3 3.4 %copy-done.2 = bf16[2048,2048]{1,0:T(8,128)(2,1)S(1)} copy-done((bf16[2048,2048]{1,0:T(8,128)(2,1)S(1)}, bf16[2048,2048]{1,0:T(8,128)(2,1)}, u32[]{:S(2)}) %copy-start.2) | copy-done | bytes 8388632
  53.7 0.4 contract_hidden.4.refs_2_
  54.1 0.8 collective-permute-done.8
  55.0 3.4 %copy-done.3 = bf16[2048,2048]{1,0:T(8,128)(2,1)S(1)} copy-done((bf16[2048,2048]{1,0:T(8,128)(2,1)S(1)}, bf16[2048,2048]{1,0:T(8,128)(2,1)}, u32[]{:S(2)}) %copy-start.3) | copy-done | bytes 8388632
  58.3 1.4 %contract_hidden.5 = f32[128,2048]{1,0:T(8,128)S(1)} custom-call(s32[2]{0:T(128)S(1)} %pad_add_fusion.first_ref, bf16[2048,2048]{1,0:T(8,128)(2,1)S(1)} %copy-done.3, bf16[128,512]{1,0:T(8,128)(2,1)S(1)} %bitcast.18, bf16[128,512]{1,0:T(8,128)(2,1)S(1)} %bitcast.19, f32[128,2048]{1,0:T(8,128)S(1)} %contract_hidden.4.refs_2_, f32[128,1]{1,0:T(8,128)S(1)} %copy.7.refs_3_), custom_call_target="tpu_custom_call" | custom-call | bytes 262144 | tf_op jit(solution)/shard_map/contract_hidden/pallas_call | solution.py:147
  59.7 0.1 collective-permute-start.9
  59.8 1.5 %collective-permute-done.9 = bf16[64,2048]{1,0:T(8,128)(2,1)S(1)} collective-permute-done((bf16[64,2048]{1,0:T(8,128)(2,1)S(1)}, bf16[64,2048]{1,0:T(8,128)(2,1)S(1)}, u32[]{:S(2)}, u32[]{:S(2)}) %collective-permute-start.9) | collective-permute-done | bytes 262176 | tf_op jit(solution)/shard_map/ppermute | solution.py:22
  61.3 0.1 fusion.6
  61.4 1.9 %collective-permute-start.12 = (bf16[16,2048]{1,0:T(8,128)(2,1)S(1)}, bf16[16,2048]{1,0:T(8,128)(2,1)S(1)}, u32[]{:S(2)}, u32[]{:S(2)}) collective-permute-start(bf16[16,2048]{1,0:T(8,128)(2,1)S(1)} %get-tuple-element.28), channel_id=1, source_target_pairs={{0,18},{1,19},{2,16},{3,17},{4,22},{5,23},{6,20},{7,21},{8,26},{9,... | collective-permute-start | bytes 196616 | tf_op jit(solution)/shard_map/ppermute | solution.py:22
  63.3 1.2 %collective-permute-start.11 = (bf16[16,2048]{1,0:T(8,128)(2,1)S(1)}, bf16[16,2048]{1,0:T(8,128)(2,1)S(1)}, u32[]{:S(2)}, u32[]{:S(2)}) collective-permute-start(bf16[16,2048]{1,0:T(8,128)(2,1)S(1)} %get-tuple-element.29), channel_id=1, source_target_pairs={{0,16},{1,17},{2,18},{3,19},{4,20},{5,21},{6,22},{7,23},{8,24},{9,... | collective-permute-start | bytes 196616 | tf_op jit(solution)/shard_map/ppermute | solution.py:22
  64.5 0.5 collective-permute-start.10
  65.0 2.3 %collective-permute-done.12 = bf16[16,2048]{1,0:T(8,128)(2,1)S(1)} collective-permute-done((bf16[16,2048]{1,0:T(8,128)(2,1)S(1)}, bf16[16,2048]{1,0:T(8,128)(2,1)S(1)}, u32[]{:S(2)}, u32[]{:S(2)}) %collective-permute-start.12) | collective-permute-done | bytes 65568 | tf_op jit(solution)/shard_map/ppermute | solution.py:22
  67.3 0.7 collective-permute-done.11
  68.0 0.7 collective-permute-done.10
  68.9 3.7 %collective-permute-start.15 = (bf16[4,4096]{1,0:T(4,128)(2,1)S(1)}, bf16[4,4096]{1,0:T(4,128)(2,1)S(1)}, u32[]{:S(2)}, u32[]{:S(2)}) collective-permute-start(bf16[4,4096]{1,0:T(4,128)(2,1)S(1)} %get-tuple-element.31), channel_id=1, source_target_pairs={{0,12},{1,13},{2,14},{3,15},{4,8},{5,9},{6,10},{7,11},{8,4},{9,5},... | collective-permute-start | bytes 98312 | tf_op jit(solution)/shard_map/ppermute | solution.py:22
  72.5 0.8 %collective-permute-start.13 = (bf16[4,4096]{1,0:T(4,128)(2,1)S(1)}, bf16[4,4096]{1,0:T(4,128)(2,1)S(1)}, u32[]{:S(2)}, u32[]{:S(2)}) collective-permute-start(bf16[4,4096]{1,0:T(4,128)(2,1)S(1)} %get-tuple-element.30), channel_id=1, source_target_pairs={{0,4},{1,5},{2,6},{3,7},{4,0},{5,1},{6,2},{7,3},{8,12},{9,13},{10,... | collective-permute-start | bytes 98312 | tf_op jit(solution)/shard_map/ppermute | solution.py:22
  73.3 1.3 %collective-permute-done.15 = bf16[4,4096]{1,0:T(4,128)(2,1)S(1)} collective-permute-done((bf16[4,4096]{1,0:T(4,128)(2,1)S(1)}, bf16[4,4096]{1,0:T(4,128)(2,1)S(1)}, u32[]{:S(2)}, u32[]{:S(2)}) %collective-permute-start.15) | collective-permute-done | bytes 32800 | tf_op jit(solution)/shard_map/ppermute | solution.py:22
  74.6 2.7 %collective-permute-done.14 = bf16[4,4096]{1,0:T(4,128)(2,1)S(1)} collective-permute-done((bf16[4,4096]{1,0:T(4,128)(2,1)S(1)}, bf16[4,4096]{1,0:T(4,128)(2,1)S(1)}, u32[]{:S(2)}, u32[]{:S(2)}) %collective-permute-start.14) | collective-permute-done | bytes 32800 | tf_op jit(solution)/shard_map/ppermute | solution.py:22
  77.4 0.6 maximum_select_fusion
  (46 shorter events, 0.5 us)
Async XLA Ops:
  0.0 0.8 copy-start.8
  0.8 0.7 copy-start.9
  1.4 0.7 copy-start.10
  2.2 12.5 %collective-permute-start.2 = (bf16[4,4224]{1,0:T(4,128)(2,1)S(1)}, bf16[4,4224]{1,0:T(4,128)(2,1)S(1)}, u32[]{:S(2)}, u32[]{:S(2)}) collective-permute-start(bf16[4,4224]{1,0:T(4,128)(2,1)S(1)} %pack_block.1), channel_id=1, source_target_pairs={{0,12},{1,13},{2,14},{3,15},{4,8},{5,9},{6,10},{7,11},{8,4},{9,5},... | collective-permute-start | bytes 101384 | tf_op jit(solution)/shard_map/ppermute | solution.py:22
  7.3 7.4 %collective-permute-start.1 = (bf16[4,4224]{1,0:T(4,128)(2,1)S(1)}, bf16[4,4224]{1,0:T(4,128)(2,1)S(1)}, u32[]{:S(2)}, u32[]{:S(2)}) collective-permute-start(bf16[4,4224]{1,0:T(4,128)(2,1)S(1)} %pack_block.1), channel_id=1, source_target_pairs={{0,8},{1,9},{2,10},{3,11},{4,12},{5,13},{6,14},{7,15},{8,0},{9,1},... | collective-permute-start | bytes 101384 | tf_op jit(solution)/shard_map/ppermute | solution.py:22
  7.3 7.4 %collective-permute-start = (bf16[4,4224]{1,0:T(4,128)(2,1)S(1)}, bf16[4,4224]{1,0:T(4,128)(2,1)S(1)}, u32[]{:S(2)}, u32[]{:S(2)}) collective-permute-start(bf16[4,4224]{1,0:T(4,128)(2,1)S(1)} %pack_block.1), channel_id=1, source_target_pairs={{0,4},{1,5},{2,6},{3,7},{4,0},{5,1},{6,2},{7,3},{8,12},{9,13},{10,... | collective-permute-start | bytes 101384 | tf_op jit(solution)/shard_map/ppermute | solution.py:22
  11.5 3.3 %copy-start.4 = (bf16[4096,1024]{1,0:T(8,128)(2,1)}, bf16[4096,1024]{1,0:T(8,128)(2,1)S(1)}, u32[]{:S(2)}) copy-start(bf16[4096,1024]{1,0:T(8,128)(2,1)S(1)} %fetch_gate.1.gate_ref) | copy-start | bytes 25165828
  14.9 17.9 %collective-permute-start.3 = (bf16[16,4224]{1,0:T(8,128)(2,1)S(1)}, bf16[16,4224]{1,0:T(8,128)(2,1)S(1)}, u32[]{:S(2)}, u32[]{:S(2)}) collective-permute-start(bf16[16,4224]{1,0:T(8,128)(2,1)S(1)} %reshape.20), channel_id=1, source_target_pairs={{0,18},{1,19},{2,16},{3,17},{4,22},{5,23},{6,20},{7,21},{8,26},{9,... | collective-permute-start | bytes 405512 | tf_op jit(solution)/shard_map/ppermute | solution.py:22
  17.6 15.2 %collective-permute-start.4 = (bf16[16,4224]{1,0:T(8,128)(2,1)S(1)}, bf16[16,4224]{1,0:T(8,128)(2,1)S(1)}, u32[]{:S(2)}, u32[]{:S(2)}) collective-permute-start(bf16[16,4224]{1,0:T(8,128)(2,1)S(1)} %reshape.20), channel_id=1, source_target_pairs={{0,2},{1,3},{2,0},{3,1},{4,6},{5,7},{6,4},{7,5},{8,10},{9,11},{10,... | collective-permute-start | bytes 405512 | tf_op jit(solution)/shard_map/ppermute | solution.py:22
  18.1 14.7 %collective-permute-start.5 = (bf16[16,4224]{1,0:T(8,128)(2,1)S(1)}, bf16[16,4224]{1,0:T(8,128)(2,1)S(1)}, u32[]{:S(2)}, u32[]{:S(2)}) collective-permute-start(bf16[16,4224]{1,0:T(8,128)(2,1)S(1)} %reshape.20), channel_id=1, source_target_pairs={{0,16},{1,17},{2,18},{3,19},{4,20},{5,21},{6,22},{7,23},{8,24},{9,... | collective-permute-start | bytes 405512 | tf_op jit(solution)/shard_map/ppermute | solution.py:22
  22.0 12.9 %copy-start.6 = (bf16[4096,1024]{1,0:T(8,128)(2,1)}, bf16[4096,1024]{1,0:T(8,128)(2,1)S(1)}, u32[]{:S(2)}) copy-start(bf16[4096,1024]{1,0:T(8,128)(2,1)S(1)} %fetch_up.1.up_ref) | copy-start | bytes 25165828
  22.0 12.9 %slice-start = ((s8[8388608]{0:T(1024)(128)(4,1)}), s8[4194304]{0:T(1024)(128)(4,1)S(1)}, s32[]{:S(2)}) async-start(s8[8388608]{0:T(1024)(128)(4,1)} %bitcast.16), calls=%async_computation | async-start | bytes 8388608
  22.0 12.9 %slice-start.1 = ((s8[8388608]{0:T(1024)(128)(4,1)}), s8[4194304]{0:T(1024)(128)(4,1)S(1)}, s32[]{:S(2)}) async-start(s8[8388608]{0:T(1024)(128)(4,1)} %bitcast.16), calls=%async_computation.1 | async-start | bytes 8388608
  28.5 4.3 %copy-start = (bf16[2048,2048]{1,0:T(8,128)(2,1)}, bf16[2048,2048]{1,0:T(8,128)(2,1)S(1)}, u32[]{:S(2)}) copy-start(bf16[2048,2048]{1,0:T(8,128)(2,1)S(1)} %fetch_down.1.down_ref) | copy-start | bytes 25165828
  32.9 2.0 %collective-permute-start.6 = (bf16[64,4224]{1,0:T(8,128)(2,1)S(1)}, bf16[64,4224]{1,0:T(8,128)(2,1)S(1)}, u32[]{:S(2)}, u32[]{:S(2)}) collective-permute-start(bf16[64,4224]{1,0:T(8,128)(2,1)S(1)} %pad_maximum_fusion), channel_id=1, source_target_pairs={{0,1},{1,0},{2,3},{3,2},{4,5},{5,4},{6,7},{7,6},{8,9},{9,8},{10,11... | collective-permute-start | bytes 1622024 | tf_op jit(solution)/shard_map/ppermute | solution.py:22
  36.3 17.8 %collective-permute-start.7 = (bf16[128,512]{1,0:T(8,128)(2,1)S(1)}, bf16[128,512]{1,0:T(8,128)(2,1)S(1)}, u32[]{:S(2)}, u32[]{:S(2)}) collective-permute-start(bf16[128,512]{1,0:T(8,128)(2,1)S(1)} %expand_rows.2.refs_0_), channel_id=1, source_target_pairs={{0,16},{1,17},{2,18},{3,19},{4,20},{5,21},{6,22},{7,23},{8,24},{9,... | collective-permute-start | bytes 393224 | tf_op jit(solution)/shard_map/ppermute | solution.py:22
  38.1 3.4 %copy-start.1 = (bf16[2048,2048]{1,0:T(8,128)(2,1)S(1)}, bf16[2048,2048]{1,0:T(8,128)(2,1)}, u32[]{:S(2)}) copy-start(bf16[2048,2048]{1,0:T(8,128)(2,1)} %copy-done) | copy-start | bytes 25165828
  41.4 3.4 %copy-start.7 = (bf16[4096,1024]{1,0:T(8,128)(2,1)S(1)}, bf16[4096,1024]{1,0:T(8,128)(2,1)}, u32[]{:S(2)}) copy-start(bf16[4096,1024]{1,0:T(8,128)(2,1)} %copy-done.6) | copy-start | bytes 25165828
  44.8 3.4 %copy-start.5 = (bf16[4096,1024]{1,0:T(8,128)(2,1)S(1)}, bf16[4096,1024]{1,0:T(8,128)(2,1)}, u32[]{:S(2)}) copy-start(bf16[4096,1024]{1,0:T(8,128)(2,1)} %copy-done.4) | copy-start | bytes 25165828
  49.6 5.3 %collective-permute-start.8 = (bf16[128,512]{1,0:T(8,128)(2,1)S(1)}, bf16[128,512]{1,0:T(8,128)(2,1)S(1)}, u32[]{:S(2)}, u32[]{:S(2)}) collective-permute-start(bf16[128,512]{1,0:T(8,128)(2,1)S(1)} %expand_rows.3.refs_0_), channel_id=1, source_target_pairs={{0,16},{1,17},{2,18},{3,19},{4,20},{5,21},{6,22},{7,23},{8,24},{9,... | collective-permute-start | bytes 393224 | tf_op jit(solution)/shard_map/ppermute | solution.py:22
  50.3 3.4 %copy-start.2 = (bf16[2048,2048]{1,0:T(8,128)(2,1)S(1)}, bf16[2048,2048]{1,0:T(8,128)(2,1)}, u32[]{:S(2)}) copy-start(bf16[2048,2048]{1,0:T(8,128)(2,1)} %copy-done) | copy-start | bytes 25165828
  55.0 3.4 %copy-start.3 = (bf16[2048,2048]{1,0:T(8,128)(2,1)S(1)}, bf16[2048,2048]{1,0:T(8,128)(2,1)}, u32[]{:S(2)}) copy-start(bf16[2048,2048]{1,0:T(8,128)(2,1)} %copy-done) | copy-start | bytes 25165828
  59.7 1.6 %collective-permute-start.9 = (bf16[64,2048]{1,0:T(8,128)(2,1)S(1)}, bf16[64,2048]{1,0:T(8,128)(2,1)S(1)}, u32[]{:S(2)}, u32[]{:S(2)}) collective-permute-start(bf16[64,2048]{1,0:T(8,128)(2,1)S(1)} %slice.115), channel_id=1, source_target_pairs={{0,1},{1,0},{2,3},{3,2},{4,5},{5,4},{6,7},{7,6},{8,9},{9,8},{10,11... | collective-permute-start | bytes 786440 | tf_op jit(solution)/shard_map/ppermute | solution.py:22
  61.4 5.9 %collective-permute-start.12 = (bf16[16,2048]{1,0:T(8,128)(2,1)S(1)}, bf16[16,2048]{1,0:T(8,128)(2,1)S(1)}, u32[]{:S(2)}, u32[]{:S(2)}) collective-permute-start(bf16[16,2048]{1,0:T(8,128)(2,1)S(1)} %get-tuple-element.28), channel_id=1, source_target_pairs={{0,18},{1,19},{2,16},{3,17},{4,22},{5,23},{6,20},{7,21},{8,26},{9,... | collective-permute-start | bytes 196616 | tf_op jit(solution)/shard_map/ppermute | solution.py:22
  63.3 4.7 %collective-permute-start.11 = (bf16[16,2048]{1,0:T(8,128)(2,1)S(1)}, bf16[16,2048]{1,0:T(8,128)(2,1)S(1)}, u32[]{:S(2)}, u32[]{:S(2)}) collective-permute-start(bf16[16,2048]{1,0:T(8,128)(2,1)S(1)} %get-tuple-element.29), channel_id=1, source_target_pairs={{0,16},{1,17},{2,18},{3,19},{4,20},{5,21},{6,22},{7,23},{8,24},{9,... | collective-permute-start | bytes 196616 | tf_op jit(solution)/shard_map/ppermute | solution.py:22
  64.5 4.3 %collective-permute-start.10 = (bf16[16,2048]{1,0:T(8,128)(2,1)S(1)}, bf16[16,2048]{1,0:T(8,128)(2,1)S(1)}, u32[]{:S(2)}, u32[]{:S(2)}) collective-permute-start(bf16[16,2048]{1,0:T(8,128)(2,1)S(1)} %get-tuple-element.27), channel_id=1, source_target_pairs={{0,2},{1,3},{2,0},{3,1},{4,6},{5,7},{6,4},{7,5},{8,10},{9,11},{10,... | collective-permute-start | bytes 196616 | tf_op jit(solution)/shard_map/ppermute | solution.py:22
  68.9 5.8 %collective-permute-start.15 = (bf16[4,4096]{1,0:T(4,128)(2,1)S(1)}, bf16[4,4096]{1,0:T(4,128)(2,1)S(1)}, u32[]{:S(2)}, u32[]{:S(2)}) collective-permute-start(bf16[4,4096]{1,0:T(4,128)(2,1)S(1)} %get-tuple-element.31), channel_id=1, source_target_pairs={{0,12},{1,13},{2,14},{3,15},{4,8},{5,9},{6,10},{7,11},{8,4},{9,5},... | collective-permute-start | bytes 98312 | tf_op jit(solution)/shard_map/ppermute | solution.py:22
  72.5 4.8 %collective-permute-start.14 = (bf16[4,4096]{1,0:T(4,128)(2,1)S(1)}, bf16[4,4096]{1,0:T(4,128)(2,1)S(1)}, u32[]{:S(2)}, u32[]{:S(2)}) collective-permute-start(bf16[4,4096]{1,0:T(4,128)(2,1)S(1)} %get-tuple-element.32), channel_id=1, source_target_pairs={{0,8},{1,9},{2,10},{3,11},{4,12},{5,13},{6,14},{7,15},{8,0},{9,1},... | collective-permute-start | bytes 98312 | tf_op jit(solution)/shard_map/ppermute | solution.py:22
  72.5 4.8 %collective-permute-start.13 = (bf16[4,4096]{1,0:T(4,128)(2,1)S(1)}, bf16[4,4096]{1,0:T(4,128)(2,1)S(1)}, u32[]{:S(2)}, u32[]{:S(2)}) collective-permute-start(bf16[4,4096]{1,0:T(4,128)(2,1)S(1)} %get-tuple-element.30), channel_id=1, source_target_pairs={{0,4},{1,5},{2,6},{3,7},{4,0},{5,1},{6,2},{7,3},{8,12},{9,13},{10,... | collective-permute-start | bytes 98312 | tf_op jit(solution)/shard_map/ppermute | solution.py:22

commit v5 on v4

--- a/solution.py
+++ b/solution.py
@@ -20,6 +20,14 @@
         for e in range(experts)
     ]
     return lax.ppermute(value, ("dp", "expert"), pairs)
+
+
+def in_vmem(value):
+    return pltpu.with_memory_space_constraint(value, pltpu.VMEM)
+
+
+def in_hbm(value):
+    return pltpu.with_memory_space_constraint(value, pltpu.HBM)
 
 
 def row_batches(count, step):
@@ -58,19 +66,42 @@
         out_specs=pl.BlockSpec(memory_space=pltpu.VMEM),
         compiler_params=pltpu.CompilerParams(vmem_limit_bytes=1 << 20),
         name="pack_block",
-    )(tokens, expert_ids, gate_probs)
-
-
-def fetch(weights, after, name):
+    )(in_hbm(tokens), in_hbm(expert_ids), in_hbm(gate_probs))
+
+
+def stack_blocks(blocks):
+    count, width = blocks[0].shape
+
+    def body(*refs):
+        values = [ref[...].astype(jnp.float32) for ref in refs[:-1]]
+        refs[-1][...] = jnp.concatenate(values).astype(refs[-1].dtype)
+
+    return pl.pallas_call(
+        body,
+        out_shape=jax.ShapeDtypeStruct((len(blocks) * count, width), blocks[0].dtype),
+        in_specs=[pl.BlockSpec(memory_space=pltpu.VMEM)] * len(blocks),
+        out_specs=pl.BlockSpec(memory_space=pltpu.VMEM),
+        compiler_params=pltpu.CompilerParams(vmem_limit_bytes=4 << 20),
+        name="stack_blocks",
+    )(*blocks)
+
+
+def fetch(weights, after, name, rows=None, part=None):
     weights, _ = lax.optimization_barrier((weights, after))
-    weights = pltpu.with_memory_space_constraint(weights, pltpu.HBM)
-    piece = weights.shape[0] // COPIES
+    rows = rows or weights.shape[0]
+    piece = rows // COPIES
+    size = rows * weights.shape[1] * weights.dtype.itemsize
 
     def body(source, target, arrived):
+        first = 0 if part is None else (lax.axis_index("dp") ^ part) * rows
         copies = []
         for i in range(COPIES):
-            part = pl.ds(i * piece, piece)
-            copies.append(pltpu.make_async_copy(source.at[part], target.at[part], arrived.at[i]))
+            here = pl.ds(pl.multiple_of(first + i * piece, piece), piece)
+            copies.append(
+                pltpu.make_async_copy(
+                    source.at[here], target.at[pl.ds(i * piece, piece)], arrived.at[i]
+                )
+            )
         for copy in copies:
             copy.start()
         for copy in copies:
@@ -78,18 +109,14 @@
 
     return pl.pallas_call(
         body,
-        out_shape=pltpu.VMEM(weights.shape, weights.dtype),
+        out_shape=pltpu.VMEM((rows, weights.shape[1]), weights.dtype),
         in_specs=[pl.BlockSpec(memory_space=pltpu.HBM)],
         out_specs=pl.BlockSpec(memory_space=pltpu.VMEM),
         scratch_shapes=[pltpu.SemaphoreType.DMA((COPIES,))],
-        cost_estimate=pl.CostEstimate(flops=0, bytes_accessed=weights.nbytes, transcendentals=0),
+        cost_estimate=pl.CostEstimate(flops=0, bytes_accessed=size, transcendentals=0),
         compiler_params=pltpu.CompilerParams(vmem_limit_bytes=1 << 20),
         name=name,
-    )(weights)
-
-
-def in_vmem(value):
-    return pltpu.with_memory_space_constraint(value, pltpu.VMEM)
+    )(in_hbm(weights))
 
 
 def expand_rows(rows, w_gate, w_up, start, columns):
@@ -119,93 +146,109 @@
     )(rows, in_vmem(w_gate), in_vmem(w_up))
 
 
-def contract_hidden(parts, first_units, w_down, before=None, scale=None):
-    count, width = parts[0].shape[0], w_down.shape[1]
-
-    def body(first_ref, down_ref, *refs):
-        parts_refs = refs[: len(parts)]
+def contract_hidden(parts, downs, before=None, rows=None, half=None):
+    count, width = parts[0][0].shape[0], downs[0].shape[1]
+    experts = lax.axis_size("expert")
+    operands = [part for part, _, _ in parts] + [in_vmem(down) for down in downs]
+    operands += [value for value in (before, rows) if value is not None]
+
+    def body(*refs):
+        part_refs, down_refs = refs[: len(parts)], refs[len(parts) : len(parts) + len(downs)]
+        rest = list(refs[len(parts) + len(downs) : -1])
+        before_ref = rest.pop(0) if before is not None else None
+        rows_ref = rest.pop(0) if rows is not None else None
+        me = lax.axis_index("expert")
 
         def step(first, batch):
             here = pl.ds(first, batch)
+            lefts = [ref[here, :] for ref in part_refs]
+            if half is not None:
+                order = [i ^ 1 for i in range(count // half)]
+                lefts = [
+                    jnp.concatenate([left[i * half : (i + 1) * half] for i in order])
+                    for left in lefts
+                ]
+            if rows is not None:
+                table = rows_ref[here, rows.shape[1] - LANES :].astype(jnp.float32)
+                lane = lax.broadcasted_iota(jnp.int32, table.shape, 1)
+                mine = (lax.rem(lane, experts) == me) & (lane < 3 * experts)
+                scale = jnp.sum(jnp.where(mine, table, 0.0), axis=1, keepdims=True)
             tile = min(2 * TILE, width)
             for i in range(0, width, tile):
                 cut = slice(i, i + tile)
-                total = 0.0 if before is None else refs[len(parts)][here, cut]
-                for j, part in enumerate(parts_refs):
-                    units = pl.ds(pl.multiple_of(first_ref[j], 128), part.shape[1])
-                    total = total + jnp.dot(
-                        part[here, :], down_ref[units, cut], preferred_element_type=jnp.float32
-                    )
-                if scale is not None:
-                    total = total.astype(w_down.dtype).astype(jnp.float32)
-                    total = total * refs[len(parts) + 1][here, :]
+                total = 0.0 if before is None else before_ref[here, cut]
+                for left, (_, j, unit) in zip(lefts, parts):
+                    right = down_refs[j][unit : unit + left.shape[1], cut]
+                    total = total + jnp.dot(left, right, preferred_element_type=jnp.float32)
+                if rows is not None:
+                    total = total.astype(jnp.bfloat16).astype(jnp.float32) * scale
                 refs[-1][here, cut] = total
 
         row_batches(count, step)
 
-    extra = [value for value in (before, scale) if value is not None]
     return pl.pallas_call(
         body,
         out_shape=jax.ShapeDtypeStruct((count, width), jnp.float32),
-        in_specs=[pl.BlockSpec(memory_space=pltpu.SMEM)]
-        + [pl.BlockSpec(memory_space=pltpu.VMEM)] * (1 + len(parts) + len(extra)),
+        in_specs=[pl.BlockSpec(memory_space=pltpu.VMEM)] * len(operands),
         out_specs=pl.BlockSpec(memory_space=pltpu.VMEM),
         cost_estimate=pl.CostEstimate(flops=0, bytes_accessed=count * width, transcendentals=0),
-        compiler_params=pltpu.CompilerParams(vmem_limit_bytes=8 * count * width + (6 << 20)),
+        compiler_params=pltpu.CompilerParams(
+            vmem_limit_bytes=8 * count * width
+            + (6 << 20)
+            + (0 if rows is None else rows.nbytes)
+        ),
         name="contract_hidden",
-    )(jnp.stack(first_units), in_vmem(w_down), *parts, *extra)
+    )(*operands)
 
 
 def local(tokens, expert_ids, gate_probs, w_gate, w_up, w_down):
     token_count, width = tokens.shape
     groups, experts = lax.axis_size("dp"), lax.axis_size("expert")
-    group, me = lax.axis_index("dp"), lax.axis_index("expert")
     wide, high = groups // 2, experts // 4
 
     block = pack_block(tokens, expert_ids, gate_probs, experts)
-    near = jnp.stack([block] + [swap(block, 0, 4 * i) for i in range(1, high)])
-    near = near.reshape(-1, block.shape[1])
+    near = stack_blocks([block] + [swap(block, 0, 4 * i) for i in range(1, high)])
     gate_weights = fetch(w_gate[0], block, "fetch_gate")
     near, gate_weights = lax.optimization_barrier((near, gate_weights))
     if wide > 1:
         near = jnp.concatenate([near] + [swap(near, 2 * i, 0) for i in range(1, wide)])
     chip = [near, swap(near, 0, 2), swap(near, 1, 0), swap(near, 1, 2)]
     up_weights = fetch(w_up[0], near, "fetch_up")
-    down_weights = fetch(w_down[0], near, "fetch_down")
-    chip[3], up_weights, down_weights = lax.optimization_barrier(
-        (chip[3], up_weights, down_weights)
-    )
+    units = up_weights.shape[1]
+    own_down = fetch(w_down[0], near, "fetch_down", units, 0)
+    chip[3], up_weights, own_down = lax.optimization_barrier((chip[3], up_weights, own_down))
     chip = jnp.concatenate(chip)
     rows = jnp.concatenate([chip, swap(chip, 0, 1)])
-    lane = jnp.arange(LANES)
-    mine = (lane % experts == me) & (lane < 3 * experts)
-    scale = jnp.where(mine, rows[:, width:].astype(jnp.float32), 0.0)
-    scale = jnp.sum(scale, axis=1, keepdims=True)
-
-    units = gate_weights.shape[1]
+
     chunks = CHUNKS if units % (LANES * CHUNKS) == 0 else 1
     step = units // chunks
+    half = rows.shape[0] // 4 if groups == 2 and rows.shape[0] <= BATCH else None
 
     def from_group(value, mask):
-        value = swap(value, mask, 0).reshape(2, 2, 2, wide, high * token_count, step)
-        if mask & 1:
-            value = jnp.concatenate([value[:, 1:], value[:, :1]], axis=1)
-        if mask > 1:
-            value = jnp.stack([value[:, :, :, i ^ (mask >> 1)] for i in range(wide)], axis=3)
+        value = swap(value, mask, 0)
+        if half is not None:
+            return value
+        value = value.reshape(2, 2, 2, wide, high * token_count, step)
+        value = jnp.stack([value[:, i ^ (mask & 1)] for i in range(2)], axis=1)
+        value = jnp.stack([value[:, :, :, i ^ (mask >> 1)] for i in range(wide)], axis=3)
         return value.reshape(-1, step)
 
-    total, others, other_units = None, [], []
+    total, others = None, [[] for _ in range(chunks)]
     for i in range(chunks):
         if total is not None:
             rows, total = lax.optimization_barrier((rows, total))
         hidden = expand_rows(rows, gate_weights, up_weights, i * step, step)
         for mask in range(1, groups):
-            others.append(from_group(hidden, mask))
-            other_units.append((group ^ mask) * units + i * step)
-        total = contract_hidden([hidden], [group * units + i * step], down_weights, total)
-    total = contract_hidden(others, other_units, down_weights, total, scale)
-
-    columns = total.shape[1]
+            others[i].append((from_group(hidden, mask), mask - 1, i * step))
+        total = contract_hidden([(hidden, 0, i * step)], [own_down], total)
+    downs = [
+        fetch(w_down[0], hidden, "fetch_down", units, mask) for mask in range(1, groups)
+    ]
+    for i in range(chunks):
+        weigh = rows if i == chunks - 1 else None
+        total = contract_hidden(others[i], downs, total, weigh, half)
+
+    columns = w_down.shape[2]
     send = lambda value, g, e: swap(value.astype(jnp.bfloat16), g, e).astype(jnp.float32)
     total = total.reshape(2, -1, columns)
     total = total[0] + send(total[1], 0, 1)
@@ -224,6 +267,7 @@
     for i in range(1, high):
         combined = combined + send(total[i * token_count : (i + 1) * token_count], 0, 4 * i)
     combined = combined.astype(jnp.bfloat16)
+    group = lax.axis_index("dp")
     if groups == 2:
         swapped = jnp.concatenate([combined[:, columns:], combined[:, :columns]], axis=1)
         return jnp.where(group == 0, combined, swapped)

time: 78.4 us -> 51 us (0.65)
  local copies, waits for them, and re-layouts: 26.5 us -> 0.21 us
  Pallas kernels: 18.5 us -> 16.8 us
  waiting for transfers between devices: 11.9 us -> 13.2 us
    unnamed x30 -> x4, local copies, waits for them, and re-layouts: 26.2 us -> 0.06 us
    pallas_call x3 -> x5, Pallas kernels: 13.5 us -> 11.4 us  [the longest x4 11.4 us: fetch(): pl.pallas_call(body, out_shape=pltpu.VMEM((rows, weights.shape[1]), weigh...]
    ppermute x16, waiting for transfers between devices: 11.9 us -> 13.2 us  [swap(): return lax.ppermute(value, ('dp', 'expert'), pairs)]
    pallas_call x3 -> x4, Pallas kernels: 2.24 us -> 1.82 us  [contract_hidden(): pl.pallas_call(body, out_shape=jax.ShapeDtypeStruct((count, width), jnp.f...]
  transfers between devices with their start and end apart: 16 -> 16, of which waited for: 8 -> 10; matrix products, arithmetic and copies ran while one was open for 0% -> 0% of each run, Pallas kernels for 20% -> 28%
where the time goes in v5:
time: 51 us; the launch traced here: 50.8 us
  starting transfers between devices  19.5 us (38%)
  Pallas kernels  16.8 us (33%)
  waiting for transfers between devices  13.2 us (26%)
  other arithmetic  0.84 us (2%)
    ppermute x16, starting transfers between devices, swap(): return lax.ppermute(value, ('dp', 'expert'), pairs)  19.5 us
    ppermute x16, waiting for transfers between devices, swap(): return lax.ppermute(value, ('dp', 'expert'), pairs)  13.2 us
    pallas_call x4, Pallas kernels, fetch(): pl.pallas_call(body, out_shape=pltpu.VMEM((rows, weights.shape[1]), weigh...  11.4 us
    pallas_call x2, Pallas kernels, expand_rows(): pl.pallas_call(body, out_shape=jax.ShapeDtypeStruct((count, columns), row...  2.71 us
    pallas_call x4, Pallas kernels, contract_hidden(): pl.pallas_call(body, out_shape=jax.ShapeDtypeStruct((count, width), jnp.f...  1.82 us
  transfers between devices with their start and end apart: 16, of which 10 were waited for; matrix products, arithmetic and copies ran while one was open for 0% of the time, Pallas kernels for 28%

profile of v5, /device:TPU:0, one launch (start us, length us, event | category | flops | bytes accessed | tf_op | source)
XLA Modules:
  0.0 50.8 jit_solution(16182025505562739597)
XLA Ops:
  0.0 0.9 %pack_block.1.refs_0_ = bf16[4,4224]{1,0:T(4,128)(2,1)S(1)} custom-call(bf16[4,4096]{1,0:T(4,128)(2,1)} %tokens_ref.1, s32[4,8]{1,0:T(4,128)} %ids_ref.1, f32[4,8]{1,0:T(4,128)} %probs_ref.1), custom_call_target="tpu_custom_call" | custom-call | tf_op jit(solution)/shard_map/pack_block/pallas_call | solution.py:62
  0.9 3.1 %collective-permute-start = (bf16[4,4224]{1,0:T(4,128)(2,1)S(1)}, bf16[4,4224]{1,0:T(4,128)(2,1)S(1)}, u32[]{:S(2)}, u32[]{:S(2)}) collective-permute-start(bf16[4,4224]{1,0:T(4,128)(2,1)S(1)} %pack_block.1.refs_0_), channel_id=1, source_target_pairs={{0,4},{1,5},{2,6},{3,7},{4,0},{5,1},{6,2},{7,3},{8,12},{9,13},{10,... | collective-permute-start | bytes 101384 | tf_op jit(solution)/shard_map/ppermute | solution.py:22
  4.0 2.6 %collective-permute-start.1 = (bf16[4,4224]{1,0:T(4,128)(2,1)S(1)}, bf16[4,4224]{1,0:T(4,128)(2,1)S(1)}, u32[]{:S(2)}, u32[]{:S(2)}) collective-permute-start(bf16[4,4224]{1,0:T(4,128)(2,1)S(1)} %pack_block.1.refs_0_), channel_id=1, source_target_pairs={{0,8},{1,9},{2,10},{3,11},{4,12},{5,13},{6,14},{7,15},{8,0},{9,1},... | collective-permute-start | bytes 101384 | tf_op jit(solution)/shard_map/ppermute | solution.py:22
  6.6 0.0 collective-permute-start.2
  6.6 3.5 %fetch_gate.1.gate_ref = bf16[4096,1024]{1,0:T(8,128)(2,1)S(1)} custom-call(bf16[4096,1024]{1,0:T(8,128)(2,1)} %bitcast.5), custom_call_target="tpu_custom_call" | custom-call | bytes 8388608 | tf_op jit(solution)/shard_map/fetch_gate/pallas_call | solution.py:110
  10.0 0.0 collective-permute-done.refs_1_
  10.0 0.0 collective-permute-done.1.refs_2_
  10.1 2.2 %collective-permute-done.2.refs_3_ = bf16[4,4224]{1,0:T(4,128)(2,1)S(1)} collective-permute-done((bf16[4,4224]{1,0:T(4,128)(2,1)S(1)}, bf16[4,4224]{1,0:T(4,128)(2,1)S(1)}, u32[]{:S(2)}, u32[]{:S(2)}) %collective-permute-start.2) | collective-permute-done | bytes 33824 | tf_op jit(solution)/shard_map/ppermute | solution.py:22
  12.3 1.6 %collective-permute-start.3 = (bf16[16,4224]{1,0:T(8,128)(2,1)S(1)}, bf16[16,4224]{1,0:T(8,128)(2,1)S(1)}, u32[]{:S(2)}, u32[]{:S(2)}) collective-permute-start(bf16[16,4224]{1,0:T(8,128)(2,1)S(1)} %stack_blocks.1), channel_id=1, source_target_pairs={{0,2},{1,3},{2,0},{3,1},{4,6},{5,7},{6,4},{7,5},{8,10},{9,11},{10,... | collective-permute-start | bytes 405512 | tf_op jit(solution)/shard_map/ppermute | solution.py:22
  13.9 1.5 %collective-permute-start.4 = (bf16[16,4224]{1,0:T(8,128)(2,1)S(1)}, bf16[16,4224]{1,0:T(8,128)(2,1)S(1)}, u32[]{:S(2)}, u32[]{:S(2)}) collective-permute-start(bf16[16,4224]{1,0:T(8,128)(2,1)S(1)} %stack_blocks.1), channel_id=1, source_target_pairs={{0,16},{1,17},{2,18},{3,19},{4,20},{5,21},{6,22},{7,23},{8,24},{9,... | collective-permute-start | bytes 405512 | tf_op jit(solution)/shard_map/ppermute | solution.py:22
  15.4 0.5 collective-permute-start.5
  15.9 3.5 %fetch_up.1.up_ref = bf16[4096,1024]{1,0:T(8,128)(2,1)S(1)} custom-call(bf16[4096,1024]{1,0:T(8,128)(2,1)} %bitcast.6), custom_call_target="tpu_custom_call" | custom-call | bytes 8388608 | tf_op jit(solution)/shard_map/fetch_up/pallas_call | solution.py:110
  19.4 2.2 %fetch_down.2.refs_1_ = bf16[1024,2048]{1,0:T(8,128)(2,1)S(1)} custom-call(bf16[2048,2048]{1,0:T(8,128)(2,1)} %bitcast.3), custom_call_target="tpu_custom_call" | custom-call | bytes 4194304 | tf_op jit(solution)/shard_map/fetch_down/pallas_call | solution.py:110
  21.6 0.0 collective-permute-done.5
  21.6 0.0 collective-permute-done.3
  21.6 0.0 collective-permute-done.4
  21.6 0.1 pad_maximum_fusion
  21.7 0.1 collective-permute-start.6
  21.8 1.9 %collective-permute-done.6 = bf16[64,4224]{1,0:T(8,128)(2,1)S(1)} collective-permute-done((bf16[64,4224]{1,0:T(8,128)(2,1)S(1)}, bf16[64,4224]{1,0:T(8,128)(2,1)S(1)}, u32[]{:S(2)}, u32[]{:S(2)}) %collective-permute-start.6) | collective-permute-done | bytes 540704 | tf_op jit(solution)/shard_map/ppermute | solution.py:22
  23.7 1.3 %expand_rows.2.refs_0_ = bf16[128,512]{1,0:T(8,128)(2,1)S(1)} custom-call(bf16[128,4224]{1,0:T(8,128)(2,1)S(1)} %constant_dynamic-update-slice_fusion.rows_ref.refs_3_, bf16[4096,1024]{1,0:T(8,128)(2,1)S(1)} %fetch_gate.1.gate_ref, bf16[4096,1024]{1,0:T(8,128)(2,1)S(1)} %fetch_up.1.up_ref), custom_call_target="tpu_custom_call" | custom-call | bytes 65536 | tf_op jit(solution)/shard_map/expand_rows/pallas_call | solution.py:138
  25.1 1.6 %collective-permute-start.8 = (bf16[128,512]{1,0:T(8,128)(2,1)S(1)}, bf16[128,512]{1,0:T(8,128)(2,1)S(1)}, u32[]{:S(2)}, u32[]{:S(2)}) collective-permute-start(bf16[128,512]{1,0:T(8,128)(2,1)S(1)} %expand_rows.2.refs_0_), channel_id=1, source_target_pairs={{0,16},{1,17},{2,18},{3,19},{4,20},{5,21},{6,22},{7,23},{8,24},{9,... | collective-permute-start | bytes 393224 | tf_op jit(solution)/shard_map/ppermute | solution.py:22
  26.6 0.4 contract_hidden.4.refs_2_
  27.1 1.4 %expand_rows.3.refs_0_ = bf16[128,512]{1,0:T(8,128)(2,1)S(1)} custom-call(bf16[128,4224]{1,0:T(8,128)(2,1)S(1)} %constant_dynamic-update-slice_fusion.rows_ref.refs_3_, bf16[4096,1024]{1,0:T(8,128)(2,1)S(1)} %fetch_gate.1.gate_ref, bf16[4096,1024]{1,0:T(8,128)(2,1)S(1)} %fetch_up.1.up_ref), custom_call_target="tpu_custom_call" | custom-call | bytes 65536 | tf_op jit(solution)/shard_map/expand_rows/pallas_call | solution.py:138
  28.5 0.6 %collective-permute-start.7 = (bf16[128,512]{1,0:T(8,128)(2,1)S(1)}, bf16[128,512]{1,0:T(8,128)(2,1)S(1)}, u32[]{:S(2)}, u32[]{:S(2)}) collective-permute-start(bf16[128,512]{1,0:T(8,128)(2,1)S(1)} %expand_rows.3.refs_0_), channel_id=1, source_target_pairs={{0,16},{1,17},{2,18},{3,19},{4,20},{5,21},{6,22},{7,23},{8,24},{9,... | collective-permute-start | bytes 393224 | tf_op jit(solution)/shard_map/ppermute | solution.py:22
  29.1 2.2 %fetch_down.3.refs_1_ = bf16[1024,2048]{1,0:T(8,128)(2,1)S(1)} custom-call(bf16[2048,2048]{1,0:T(8,128)(2,1)} %bitcast.4), custom_call_target="tpu_custom_call" | custom-call | bytes 4194304 | tf_op jit(solution)/shard_map/fetch_down/pallas_call | solution.py:110
  31.3 0.5 contract_hidden.5.refs_2_
  31.8 0.0 collective-permute-done.8.refs_0_
  31.8 0.5 contract_hidden.6.refs_2_
  32.2 1.6 %collective-permute-done.7.refs_0_ = bf16[128,512]{1,0:T(8,128)(2,1)S(1)} collective-permute-done((bf16[128,512]{1,0:T(8,128)(2,1)S(1)}, bf16[128,512]{1,0:T(8,128)(2,1)S(1)}, u32[]{:S(2)}, u32[]{:S(2)}) %collective-permute-start.7) | collective-permute-done | bytes 131104 | tf_op jit(solution)/shard_map/ppermute | solution.py:22
  33.8 0.5 contract_hidden.7
  34.3 0.1 collective-permute-start.9
  34.4 1.5 %collective-permute-done.9 = bf16[64,2048]{1,0:T(8,128)(2,1)S(1)} collective-permute-done((bf16[64,2048]{1,0:T(8,128)(2,1)S(1)}, bf16[64,2048]{1,0:T(8,128)(2,1)S(1)}, u32[]{:S(2)}, u32[]{:S(2)}) %collective-permute-start.9) | collective-permute-done | bytes 262176 | tf_op jit(solution)/shard_map/ppermute | solution.py:22
  35.9 0.1 fusion.6
  36.0 2.2 %collective-permute-start.12 = (bf16[16,2048]{1,0:T(8,128)(2,1)S(1)}, bf16[16,2048]{1,0:T(8,128)(2,1)S(1)}, u32[]{:S(2)}, u32[]{:S(2)}) collective-permute-start(bf16[16,2048]{1,0:T(8,128)(2,1)S(1)} %get-tuple-element.30), channel_id=1, source_target_pairs={{0,18},{1,19},{2,16},{3,17},{4,22},{5,23},{6,20},{7,21},{8,26},{9,... | collective-permute-start | bytes 196616 | tf_op jit(solution)/shard_map/ppermute | solution.py:22
  38.2 0.8 %collective-permute-start.11 = (bf16[16,2048]{1,0:T(8,128)(2,1)S(1)}, bf16[16,2048]{1,0:T(8,128)(2,1)S(1)}, u32[]{:S(2)}, u32[]{:S(2)}) collective-permute-start(bf16[16,2048]{1,0:T(8,128)(2,1)S(1)} %get-tuple-element.31), channel_id=1, source_target_pairs={{0,16},{1,17},{2,18},{3,19},{4,20},{5,21},{6,22},{7,23},{8,24},{9,... | collective-permute-start | bytes 196616 | tf_op jit(solution)/shard_map/ppermute | solution.py:22
  39.1 0.5 collective-permute-start.10
  39.6 2.3 %collective-permute-done.12 = bf16[16,2048]{1,0:T(8,128)(2,1)S(1)} collective-permute-done((bf16[16,2048]{1,0:T(8,128)(2,1)S(1)}, bf16[16,2048]{1,0:T(8,128)(2,1)S(1)}, u32[]{:S(2)}, u32[]{:S(2)}) %collective-permute-start.12) | collective-permute-done | bytes 65568 | tf_op jit(solution)/shard_map/ppermute | solution.py:22
  41.9 0.8 %collective-permute-done.11 = bf16[16,2048]{1,0:T(8,128)(2,1)S(1)} collective-permute-done((bf16[16,2048]{1,0:T(8,128)(2,1)S(1)}, bf16[16,2048]{1,0:T(8,128)(2,1)S(1)}, u32[]{:S(2)}, u32[]{:S(2)}) %collective-permute-start.11) | collective-permute-done | bytes 65568 | tf_op jit(solution)/shard_map/ppermute | solution.py:22
  42.7 0.6 %collective-permute-done.10 = bf16[16,2048]{1,0:T(8,128)(2,1)S(1)} collective-permute-done((bf16[16,2048]{1,0:T(8,128)(2,1)S(1)}, bf16[16,2048]{1,0:T(8,128)(2,1)S(1)}, u32[]{:S(2)}, u32[]{:S(2)}) %collective-permute-start.10) | collective-permute-done | bytes 65568 | tf_op jit(solution)/shard_map/ppermute | solution.py:22
  43.4 1.7 %collective-permute-start.15 = (bf16[4,4096]{1,0:T(4,128)(2,1)S(1)}, bf16[4,4096]{1,0:T(4,128)(2,1)S(1)}, u32[]{:S(2)}, u32[]{:S(2)}) collective-permute-start(bf16[4,4096]{1,0:T(4,128)(2,1)S(1)} %get-tuple-element.33), channel_id=1, source_target_pairs={{0,12},{1,13},{2,14},{3,15},{4,8},{5,9},{6,10},{7,11},{8,4},{9,5},... | collective-permute-start | bytes 98312 | tf_op jit(solution)/shard_map/ppermute | solution.py:22
  45.1 0.0 collective-permute-start.14
  45.1 2.8 %collective-permute-start.13 = (bf16[4,4096]{1,0:T(4,128)(2,1)S(1)}, bf16[4,4096]{1,0:T(4,128)(2,1)S(1)}, u32[]{:S(2)}, u32[]{:S(2)}) collective-permute-start(bf16[4,4096]{1,0:T(4,128)(2,1)S(1)} %get-tuple-element.32), channel_id=1, source_target_pairs={{0,4},{1,5},{2,6},{3,7},{4,0},{5,1},{6,2},{7,3},{8,12},{9,13},{10,... | collective-permute-start | bytes 98312 | tf_op jit(solution)/shard_map/ppermute | solution.py:22
  47.9 1.4 %collective-permute-done.15 = bf16[4,4096]{1,0:T(4,128)(2,1)S(1)} collective-permute-done((bf16[4,4096]{1,0:T(4,128)(2,1)S(1)}, bf16[4,4096]{1,0:T(4,128)(2,1)S(1)}, u32[]{:S(2)}, u32[]{:S(2)}) %collective-permute-start.15) | collective-permute-done | bytes 32800 | tf_op jit(solution)/shard_map/ppermute | solution.py:22
  49.2 0.8 %collective-permute-done.14 = bf16[4,4096]{1,0:T(4,128)(2,1)S(1)} collective-permute-done((bf16[4,4096]{1,0:T(4,128)(2,1)S(1)}, bf16[4,4096]{1,0:T(4,128)(2,1)S(1)}, u32[]{:S(2)}, u32[]{:S(2)}) %collective-permute-start.14) | collective-permute-done | bytes 32800 | tf_op jit(solution)/shard_map/ppermute | solution.py:22
  50.0 0.1 collective-permute-done.13
  50.2 0.6 %maximum_select_fusion = bf16[4,4096]{1,0:T(4,128)(2,1)} fusion(bf16[4,4096]{1,0:T(4,128)(2,1)S(1)} %fusion.5, bf16[4,2048]{1,0:T(4,128)(2,1)S(1)} %get-tuple-element.36, bf16[4,2048]{1,0:T(4,128)(2,1)S(1)} %get-tuple-element.35, pred[]{:T(512)S(6)} %eq.3), kind=kLoop, calls=%fused_computation.14 | loop fusion | flops 81920 | bytes 98305 | tf_op jit(solution)/shard_map/jit(_where)/select_n | solution.py:273
  (14 shorter events, 0.3 us)
Async XLA Ops:
  0.9 9.2 %collective-permute-start = (bf16[4,4224]{1,0:T(4,128)(2,1)S(1)}, bf16[4,4224]{1,0:T(4,128)(2,1)S(1)}, u32[]{:S(2)}, u32[]{:S(2)}) collective-permute-start(bf16[4,4224]{1,0:T(4,128)(2,1)S(1)} %pack_block.1.refs_0_), channel_id=1, source_target_pairs={{0,4},{1,5},{2,6},{3,7},{4,0},{5,1},{6,2},{7,3},{8,12},{9,13},{10,... | collective-permute-start | bytes 101384 | tf_op jit(solution)/shard_map/ppermute | solution.py:22
  4.0 6.1 %collective-permute-start.1 = (bf16[4,4224]{1,0:T(4,128)(2,1)S(1)}, bf16[4,4224]{1,0:T(4,128)(2,1)S(1)}, u32[]{:S(2)}, u32[]{:S(2)}) collective-permute-start(bf16[4,4224]{1,0:T(4,128)(2,1)S(1)} %pack_block.1.refs_0_), channel_id=1, source_target_pairs={{0,8},{1,9},{2,10},{3,11},{4,12},{5,13},{6,14},{7,15},{8,0},{9,1},... | collective-permute-start | bytes 101384 | tf_op jit(solution)/shard_map/ppermute | solution.py:22
  6.6 5.7 %collective-permute-start.2 = (bf16[4,4224]{1,0:T(4,128)(2,1)S(1)}, bf16[4,4224]{1,0:T(4,128)(2,1)S(1)}, u32[]{:S(2)}, u32[]{:S(2)}) collective-permute-start(bf16[4,4224]{1,0:T(4,128)(2,1)S(1)} %pack_block.1.refs_0_), channel_id=1, source_target_pairs={{0,12},{1,13},{2,14},{3,15},{4,8},{5,9},{6,10},{7,11},{8,4},{9,5},... | collective-permute-start | bytes 101384 | tf_op jit(solution)/shard_map/ppermute | solution.py:22
  12.3 9.3 %collective-permute-start.3 = (bf16[16,4224]{1,0:T(8,128)(2,1)S(1)}, bf16[16,4224]{1,0:T(8,128)(2,1)S(1)}, u32[]{:S(2)}, u32[]{:S(2)}) collective-permute-start(bf16[16,4224]{1,0:T(8,128)(2,1)S(1)} %stack_blocks.1), channel_id=1, source_target_pairs={{0,2},{1,3},{2,0},{3,1},{4,6},{5,7},{6,4},{7,5},{8,10},{9,11},{10,... | collective-permute-start | bytes 405512 | tf_op jit(solution)/shard_map/ppermute | solution.py:22
  13.9 7.7 %collective-permute-start.4 = (bf16[16,4224]{1,0:T(8,128)(2,1)S(1)}, bf16[16,4224]{1,0:T(8,128)(2,1)S(1)}, u32[]{:S(2)}, u32[]{:S(2)}) collective-permute-start(bf16[16,4224]{1,0:T(8,128)(2,1)S(1)} %stack_blocks.1), channel_id=1, source_target_pairs={{0,16},{1,17},{2,18},{3,19},{4,20},{5,21},{6,22},{7,23},{8,24},{9,... | collective-permute-start | bytes 405512 | tf_op jit(solution)/shard_map/ppermute | solution.py:22
  15.4 6.2 %collective-permute-start.5 = (bf16[16,4224]{1,0:T(8,128)(2,1)S(1)}, bf16[16,4224]{1,0:T(8,128)(2,1)S(1)}, u32[]{:S(2)}, u32[]{:S(2)}) collective-permute-start(bf16[16,4224]{1,0:T(8,128)(2,1)S(1)} %stack_blocks.1), channel_id=1, source_target_pairs={{0,18},{1,19},{2,16},{3,17},{4,22},{5,23},{6,20},{7,21},{8,26},{9,... | collective-permute-start | bytes 405512 | tf_op jit(solution)/shard_map/ppermute | solution.py:22
  21.7 2.0 %collective-permute-start.6 = (bf16[64,4224]{1,0:T(8,128)(2,1)S(1)}, bf16[64,4224]{1,0:T(8,128)(2,1)S(1)}, u32[]{:S(2)}, u32[]{:S(2)}) collective-permute-start(bf16[64,4224]{1,0:T(8,128)(2,1)S(1)} %pad_maximum_fusion), channel_id=1, source_target_pairs={{0,1},{1,0},{2,3},{3,2},{4,5},{5,4},{6,7},{7,6},{8,9},{9,8},{10,11... | collective-permute-start | bytes 1622024 | tf_op jit(solution)/shard_map/ppermute | solution.py:22
  25.1 6.7 %collective-permute-start.8 = (bf16[128,512]{1,0:T(8,128)(2,1)S(1)}, bf16[128,512]{1,0:T(8,128)(2,1)S(1)}, u32[]{:S(2)}, u32[]{:S(2)}) collective-permute-start(bf16[128,512]{1,0:T(8,128)(2,1)S(1)} %expand_rows.2.refs_0_), channel_id=1, source_target_pairs={{0,16},{1,17},{2,18},{3,19},{4,20},{5,21},{6,22},{7,23},{8,24},{9,... | collective-permute-start | bytes 393224 | tf_op jit(solution)/shard_map/ppermute | solution.py:22
  28.5 5.3 %collective-permute-start.7 = (bf16[128,512]{1,0:T(8,128)(2,1)S(1)}, bf16[128,512]{1,0:T(8,128)(2,1)S(1)}, u32[]{:S(2)}, u32[]{:S(2)}) collective-permute-start(bf16[128,512]{1,0:T(8,128)(2,1)S(1)} %expand_rows.3.refs_0_), channel_id=1, source_target_pairs={{0,16},{1,17},{2,18},{3,19},{4,20},{5,21},{6,22},{7,23},{8,24},{9,... | collective-permute-start | bytes 393224 | tf_op jit(solution)/shard_map/ppermute | solution.py:22
  34.3 1.6 %collective-permute-start.9 = (bf16[64,2048]{1,0:T(8,128)(2,1)S(1)}, bf16[64,2048]{1,0:T(8,128)(2,1)S(1)}, u32[]{:S(2)}, u32[]{:S(2)}) collective-permute-start(bf16[64,2048]{1,0:T(8,128)(2,1)S(1)} %slice.89), channel_id=1, source_target_pairs={{0,1},{1,0},{2,3},{3,2},{4,5},{5,4},{6,7},{7,6},{8,9},{9,8},{10,11... | collective-permute-start | bytes 786440 | tf_op jit(solution)/shard_map/ppermute | solution.py:22
  36.0 5.9 %collective-permute-start.12 = (bf16[16,2048]{1,0:T(8,128)(2,1)S(1)}, bf16[16,2048]{1,0:T(8,128)(2,1)S(1)}, u32[]{:S(2)}, u32[]{:S(2)}) collective-permute-start(bf16[16,2048]{1,0:T(8,128)(2,1)S(1)} %get-tuple-element.30), channel_id=1, source_target_pairs={{0,18},{1,19},{2,16},{3,17},{4,22},{5,23},{6,20},{7,21},{8,26},{9,... | collective-permute-start | bytes 196616 | tf_op jit(solution)/shard_map/ppermute | solution.py:22
  38.2 4.5 %collective-permute-start.11 = (bf16[16,2048]{1,0:T(8,128)(2,1)S(1)}, bf16[16,2048]{1,0:T(8,128)(2,1)S(1)}, u32[]{:S(2)}, u32[]{:S(2)}) collective-permute-start(bf16[16,2048]{1,0:T(8,128)(2,1)S(1)} %get-tuple-element.31), channel_id=1, source_target_pairs={{0,16},{1,17},{2,18},{3,19},{4,20},{5,21},{6,22},{7,23},{8,24},{9,... | collective-permute-start | bytes 196616 | tf_op jit(solution)/shard_map/ppermute | solution.py:22
  39.1 4.3 %collective-permute-start.10 = (bf16[16,2048]{1,0:T(8,128)(2,1)S(1)}, bf16[16,2048]{1,0:T(8,128)(2,1)S(1)}, u32[]{:S(2)}, u32[]{:S(2)}) collective-permute-start(bf16[16,2048]{1,0:T(8,128)(2,1)S(1)} %get-tuple-element.29), channel_id=1, source_target_pairs={{0,2},{1,3},{2,0},{3,1},{4,6},{5,7},{6,4},{7,5},{8,10},{9,11},{10,... | collective-permute-start | bytes 196616 | tf_op jit(solution)/shard_map/ppermute | solution.py:22
  43.4 5.8 %collective-permute-start.15 = (bf16[4,4096]{1,0:T(4,128)(2,1)S(1)}, bf16[4,4096]{1,0:T(4,128)(2,1)S(1)}, u32[]{:S(2)}, u32[]{:S(2)}) collective-permute-start(bf16[4,4096]{1,0:T(4,128)(2,1)S(1)} %get-tuple-element.33), channel_id=1, source_target_pairs={{0,12},{1,13},{2,14},{3,15},{4,8},{5,9},{6,10},{7,11},{8,4},{9,5},... | collective-permute-start | bytes 98312 | tf_op jit(solution)/shard_map/ppermute | solution.py:22
  45.1 5.0 %collective-permute-start.14 = (bf16[4,4096]{1,0:T(4,128)(2,1)S(1)}, bf16[4,4096]{1,0:T(4,128)(2,1)S(1)}, u32[]{:S(2)}, u32[]{:S(2)}) collective-permute-start(bf16[4,4096]{1,0:T(4,128)(2,1)S(1)} %get-tuple-element.34), channel_id=1, source_target_pairs={{0,8},{1,9},{2,10},{3,11},{4,12},{5,13},{6,14},{7,15},{8,0},{9,1},... | collective-permute-start | bytes 98312 | tf_op jit(solution)/shard_map/ppermute | solution.py:22
  45.1 5.0 %collective-permute-start.13 = (bf16[4,4096]{1,0:T(4,128)(2,1)S(1)}, bf16[4,4096]{1,0:T(4,128)(2,1)S(1)}, u32[]{:S(2)}, u32[]{:S(2)}) collective-permute-start(bf16[4,4096]{1,0:T(4,128)(2,1)S(1)} %get-tuple-element.32), channel_id=1, source_target_pairs={{0,4},{1,5},{2,6},{3,7},{4,0},{5,1},{6,2},{7,3},{8,12},{9,13},{10,... | collective-permute-start | bytes 98312 | tf_op jit(solution)/shard_map/ppermute | solution.py:22

commit v6 on v5

--- a/solution.py
+++ b/solution.py
@@ -3,23 +3,25 @@
 from jax import lax
 from jax.experimental import pallas as pl
 from jax.experimental.pallas import tpu as pltpu
+from jax.sharding import Mesh
 from jax.sharding import PartitionSpec as P
 
 CHUNKS = 2
 TILE = 256
 BATCH = 128
-COPIES = 8
+COPY_BYTES = 1 << 20
 LANES = 128
+EXPERT = ("far", "core")
 
 
 def swap(value, group_mask, expert_mask):
-    groups, experts = lax.axis_size("dp"), lax.axis_size("expert")
+    groups, experts = lax.axis_size("dp"), lax.axis_size(EXPERT)
     pairs = [
         (g * experts + e, (g ^ group_mask) * experts + (e ^ expert_mask))
         for g in range(groups)
         for e in range(experts)
     ]
-    return lax.ppermute(value, ("dp", "expert"), pairs)
+    return lax.ppermute(value, ("dp",) + EXPERT, pairs)
 
 
 def in_vmem(value):
@@ -86,22 +88,24 @@
     )(*blocks)
 
 
-def fetch(weights, after, name, rows=None, part=None):
-    weights, _ = lax.optimization_barrier((weights, after))
-    rows = rows or weights.shape[0]
-    piece = rows // COPIES
-    size = rows * weights.shape[1] * weights.dtype.itemsize
-
-    def body(source, target, arrived):
-        first = 0 if part is None else (lax.axis_index("dp") ^ part) * rows
+def fetch(pieces, after, units, name):
+    shapes = [(w.shape[0] if mask is None else units, w.shape[1]) for w, mask in pieces]
+    parts = []
+    for i, (rows, columns) in enumerate(shapes):
+        step = max(16, min(rows, COPY_BYTES // (2 * columns)))
+        parts += [(i, first, step) for first in range(0, rows, step)]
+    operands, _ = lax.optimization_barrier(([w for w, _ in pieces], after))
+
+    def body(*refs):
+        sources, targets = refs[: len(pieces)], refs[len(pieces) : -1]
+        group = lax.axis_index("dp")
         copies = []
-        for i in range(COPIES):
-            here = pl.ds(pl.multiple_of(first + i * piece, piece), piece)
-            copies.append(
-                pltpu.make_async_copy(
-                    source.at[here], target.at[pl.ds(i * piece, piece)], arrived.at[i]
-                )
-            )
+        for j, (i, first, step) in enumerate(parts):
+            mask = pieces[i][1]
+            start = first if mask is None else pl.multiple_of((group ^ mask) * units + first, 16)
+            source = sources[i].at[pl.ds(start, step)]
+            target = targets[i].at[pl.ds(first, step)]
+            copies.append(pltpu.make_async_copy(source, target, refs[-1].at[j]))
         for copy in copies:
             copy.start()
         for copy in copies:
@@ -109,14 +113,16 @@
 
     return pl.pallas_call(
         body,
-        out_shape=pltpu.VMEM((rows, weights.shape[1]), weights.dtype),
-        in_specs=[pl.BlockSpec(memory_space=pltpu.HBM)],
-        out_specs=pl.BlockSpec(memory_space=pltpu.VMEM),
-        scratch_shapes=[pltpu.SemaphoreType.DMA((COPIES,))],
-        cost_estimate=pl.CostEstimate(flops=0, bytes_accessed=size, transcendentals=0),
+        out_shape=[pltpu.VMEM(shape, w.dtype) for shape, (w, _) in zip(shapes, pieces)],
+        in_specs=[pl.BlockSpec(memory_space=pltpu.HBM)] * len(pieces),
+        out_specs=[pl.BlockSpec(memory_space=pltpu.VMEM)] * len(pieces),
+        scratch_shapes=[pltpu.SemaphoreType.DMA((len(parts),))],
+        cost_estimate=pl.CostEstimate(
+            flops=0, bytes_accessed=sum(2 * r * c for r, c in shapes), transcendentals=0
+        ),
         compiler_params=pltpu.CompilerParams(vmem_limit_bytes=1 << 20),
         name=name,
-    )(in_hbm(weights))
+    )(*[in_hbm(w) for w in operands])
 
 
 def expand_rows(rows, w_gate, w_up, start, columns):
@@ -148,7 +154,7 @@
 
 def contract_hidden(parts, downs, before=None, rows=None, half=None):
     count, width = parts[0][0].shape[0], downs[0].shape[1]
-    experts = lax.axis_size("expert")
+    experts = lax.axis_size(EXPERT)
     operands = [part for part, _, _ in parts] + [in_vmem(down) for down in downs]
     operands += [value for value in (before, rows) if value is not None]
 
@@ -157,7 +163,7 @@
         rest = list(refs[len(parts) + len(downs) : -1])
         before_ref = rest.pop(0) if before is not None else None
         rows_ref = rest.pop(0) if rows is not None else None
-        me = lax.axis_index("expert")
+        me = lax.axis_index(EXPERT)
 
         def step(first, batch):
             here = pl.ds(first, batch)
@@ -201,21 +207,44 @@
     )(*operands)
 
 
+def add_and_order(total, received, wide, high):
+    count, width = received.shape
+    blocks = 4 * wide * high
+    tokens, far_size = count // blocks, 2 * high
+
+    def body(total_ref, received_ref, out_ref):
+        group, far = lax.axis_index("dp"), lax.axis_index("far")
+        for i in range(blocks):
+            x, y, w, h = i // (blocks // 2), i // (wide * high) % 2, i // high % wide, i % high
+            slot = (group ^ (x + 2 * w)) * far_size + (far ^ (y + 2 * h))
+            here = slice(i * tokens, (i + 1) * tokens)
+            value = total_ref[here, :] + received_ref[here, :].astype(jnp.float32)
+            out_ref[slot] = value.astype(out_ref.dtype)
+
+    return pl.pallas_call(
+        body,
+        out_shape=jax.ShapeDtypeStruct((blocks, tokens, width), received.dtype),
+        in_specs=[pl.BlockSpec(memory_space=pltpu.VMEM)] * 2,
+        out_specs=pl.BlockSpec(memory_space=pltpu.VMEM),
+        compiler_params=pltpu.CompilerParams(vmem_limit_bytes=12 * total.size + (6 << 20)),
+        name="add_and_order",
+    )(total, received)
+
+
 def local(tokens, expert_ids, gate_probs, w_gate, w_up, w_down):
     token_count, width = tokens.shape
-    groups, experts = lax.axis_size("dp"), lax.axis_size("expert")
+    groups, experts = lax.axis_size("dp"), lax.axis_size(EXPERT)
     wide, high = groups // 2, experts // 4
 
     block = pack_block(tokens, expert_ids, gate_probs, experts)
     near = stack_blocks([block] + [swap(block, 0, 4 * i) for i in range(1, high)])
-    gate_weights = fetch(w_gate[0], block, "fetch_gate")
+    units = w_up.shape[2]
+    (gate_weights,) = fetch([(w_gate[0], None)], block, units, "fetch_gate")
     near, gate_weights = lax.optimization_barrier((near, gate_weights))
     if wide > 1:
         near = jnp.concatenate([near] + [swap(near, 2 * i, 0) for i in range(1, wide)])
     chip = [near, swap(near, 0, 2), swap(near, 1, 0), swap(near, 1, 2)]
-    up_weights = fetch(w_up[0], near, "fetch_up")
-    units = up_weights.shape[1]
-    own_down = fetch(w_down[0], near, "fetch_down", units, 0)
+    up_weights, own_down = fetch([(w_up[0], None), (w_down[0], 0)], near, units, "fetch_up")
     chip[3], up_weights, own_down = lax.optimization_barrier((chip[3], up_weights, own_down))
     chip = jnp.concatenate(chip)
     rows = jnp.concatenate([chip, swap(chip, 0, 1)])
@@ -241,46 +270,28 @@
         for mask in range(1, groups):
             others[i].append((from_group(hidden, mask), mask - 1, i * step))
         total = contract_hidden([(hidden, 0, i * step)], [own_down], total)
-    downs = [
-        fetch(w_down[0], hidden, "fetch_down", units, mask) for mask in range(1, groups)
-    ]
+    pieces = [(w_down[0], mask) for mask in range(1, groups)]
+    downs = fetch(pieces, hidden, units, "fetch_down")
     for i in range(chunks):
         weigh = rows if i == chunks - 1 else None
         total = contract_hidden(others[i], downs, total, weigh, half)
 
-    columns = w_down.shape[2]
-    send = lambda value, g, e: swap(value.astype(jnp.bfloat16), g, e).astype(jnp.float32)
-    total = total.reshape(2, -1, columns)
-    total = total[0] + send(total[1], 0, 1)
-    part = total.shape[0] // 4
-    near, over_y, over_x, corner = (total[i * part : (i + 1) * part] for i in range(4))
-    total = jnp.concatenate(
-        [near + send(over_y, 0, 2), send(over_x, 1, 0) + send(corner, 1, 2)], axis=1
-    )
-    part = part // wide
-    total = jnp.concatenate(
-        [total[:part]]
-        + [send(total[i * part : (i + 1) * part], 2 * i, 0) for i in range(1, wide)],
-        axis=1,
-    )
-    combined = total[:token_count]
-    for i in range(1, high):
-        combined = combined + send(total[i * token_count : (i + 1) * token_count], 0, 4 * i)
-    combined = combined.astype(jnp.bfloat16)
-    group = lax.axis_index("dp")
-    if groups == 2:
-        swapped = jnp.concatenate([combined[:, columns:], combined[:, :columns]], axis=1)
-        return jnp.where(group == 0, combined, swapped)
-    combined = combined.reshape(token_count, groups, columns)
-    combined = jnp.take(combined, jnp.arange(groups) ^ group, axis=1)
-    return combined.reshape(token_count, width)
+    count, columns = rows.shape[0] // 2, w_down.shape[2]
+    received = swap(total[count:].astype(jnp.bfloat16), 0, 1)
+    blocks = add_and_order(total, received, wide, high)
+    blocks = lax.all_to_all(blocks, ("dp", "far"), split_axis=0, concat_axis=0, tiled=True)
+    blocks = blocks.reshape(groups, -1, token_count, columns).astype(jnp.float32)
+    combined = jnp.sum(blocks, axis=1).astype(jnp.bfloat16)
+    return combined.transpose(1, 0, 2).reshape(token_count, width)
 
 
 def solution(mesh):
-    row, expert = P(("dp", "expert"), None), P("expert", None, "dp")
+    groups, experts = mesh.devices.shape
+    split = Mesh(mesh.devices.reshape(groups, experts // 2, 2), ("dp", "far", "core"))
+    row, expert = P(("dp", "far", "core"), None), P(EXPERT, None, "dp")
     return jax.shard_map(
         local,
-        mesh=mesh,
+        mesh=split,
         in_specs=(row, row, row, expert, expert, expert),
         out_specs=row,
         check_vma=False,

time: 51 us -> 50.5 us (level)
  blocking collectives: 0 us -> 16 us
  starting transfers between devices: 19.5 us -> 11.6 us
  waiting for transfers between devices: 13.2 us -> 5.65 us
  Pallas kernels: 16.8 us -> 16 us
    all_to_all x0 -> x1, blocking collectives: none -> 16 us  [local(): lax.all_to_all(blocks, ('dp', 'far'), split_axis=0, concat_axis=0, tiled=...]
    ppermute x16 -> x10, starting transfers between devices: 19.5 us -> 11.6 us  [swap(): return lax.ppermute(value, ('dp',) + EXPERT, pairs)]
    ppermute x16 -> x10, waiting for transfers between devices: 13.2 us -> 5.65 us  [swap(): return lax.ppermute(value, ('dp',) + EXPERT, pairs)]
    pallas_call x4, Pallas kernels: 11.4 us -> 10.5 us  [the longest x3 10.4 us: fetch(): pl.pallas_call(body, out_shape=[pltpu.VMEM(shape, w.dtype) for shape, (w,...]
    reduce_sum x0 -> x1, other arithmetic: none -> 0.73 us  [local(): combined = jnp.sum(blocks, axis=1).astype(jnp.bfloat16)]
    select_n x1 -> x0, other arithmetic: 0.65 us -> none  [local(): return jnp.where(group == 0, combined, swapped)]
  transfers between devices with their start and end apart: 16 -> 10, of which waited for: 10 -> 4; matrix products, arithmetic and copies ran while one was open for 0% -> 0% of each run, Pallas kernels for 28% -> 26%
where the time goes in v6:
time: 50.5 us; the launch traced here: 50.3 us
  Pallas kernels  16 us (32%)
  blocking collectives  16 us (32%)
  starting transfers between devices  11.6 us (23%)
  waiting for transfers between devices  5.65 us (11%)
  other arithmetic  0.77 us (2%)
    all_to_all x1, blocking collectives, local(): lax.all_to_all(blocks, ('dp', 'far'), split_axis=0, concat_axis=0, tiled=...  16 us
    ppermute x10, starting transfers between devices, swap(): return lax.ppermute(value, ('dp',) + EXPERT, pairs)  11.6 us
    pallas_call x3, Pallas kernels, fetch(): pl.pallas_call(body, out_shape=[pltpu.VMEM(shape, w.dtype) for shape, (w,...  10.4 us
    ppermute x10, waiting for transfers between devices, swap(): return lax.ppermute(value, ('dp',) + EXPERT, pairs)  5.65 us
    pallas_call x2, Pallas kernels, expand_rows(): pl.pallas_call(body, out_shape=jax.ShapeDtypeStruct((count, columns), row...  2.72 us
    pallas_call x4, Pallas kernels, contract_hidden(): pl.pallas_call(body, out_shape=jax.ShapeDtypeStruct((count, width), jnp.f...  1.82 us
  transfers between devices with their start and end apart: 10, of which 4 were waited for; matrix products, arithmetic and copies ran while one was open for 0% of the time, Pallas kernels for 26%

profile of v6, /device:TPU:0, one launch (start us, length us, event | category | flops | bytes accessed | tf_op | source)
XLA Modules:
  0.0 50.3 jit_solution(8358104691640749292)
XLA Ops:
  0.0 0.9 %pack_block.1.refs_0_ = bf16[4,4224]{1,0:T(4,128)(2,1)S(1)} custom-call(bf16[4,4096]{1,0:T(4,128)(2,1)} %tokens_ref.1, s32[4,8]{1,0:T(4,128)} %ids_ref.1, f32[4,8]{1,0:T(4,128)} %probs_ref.1), custom_call_target="tpu_custom_call" | custom-call | tf_op jit(solution)/shard_map/pack_block/pallas_call | solution.py:64
  0.9 5.1 %collective-permute-start.2 = (bf16[4,4224]{1,0:T(4,128)(2,1)S(1)}, bf16[4,4224]{1,0:T(4,128)(2,1)S(1)}, u32[]{:S(2)}, u32[]{:S(2)}) collective-permute-start(bf16[4,4224]{1,0:T(4,128)(2,1)S(1)} %pack_block.1.refs_0_), channel_id=1, source_target_pairs={{0,12},{1,13},{2,14},{3,15},{4,8},{5,9},{6,10},{7,11},{8,4},{9,5},... | collective-permute-start | bytes 101384 | tf_op jit(solution)/shard_map/ppermute | solution.py:24
  6.0 0.0 collective-permute-start.1
  6.0 0.6 %collective-permute-start = (bf16[4,4224]{1,0:T(4,128)(2,1)S(1)}, bf16[4,4224]{1,0:T(4,128)(2,1)S(1)}, u32[]{:S(2)}, u32[]{:S(2)}) collective-permute-start(bf16[4,4224]{1,0:T(4,128)(2,1)S(1)} %pack_block.1.refs_0_), channel_id=1, source_target_pairs={{0,4},{1,5},{2,6},{3,7},{4,0},{5,1},{6,2},{7,3},{8,12},{9,13},{10,... | collective-permute-start | bytes 101384 | tf_op jit(solution)/shard_map/ppermute | solution.py:24
  6.6 3.5 %fetch_gate.1.gate_ref = bf16[4096,1024]{1,0:T(8,128)(2,1)S(1)} custom-call(bf16[4096,1024]{1,0:T(8,128)(2,1)} %bitcast.10), custom_call_target="tpu_custom_call" | custom-call | bytes 8388608 | tf_op jit(solution)/shard_map/fetch_gate/pallas_call | solution.py:114
  10.1 0.0 collective-permute-done.2.refs_3_
  10.1 0.7 %collective-permute-done.1.refs_2_ = bf16[4,4224]{1,0:T(4,128)(2,1)S(1)} collective-permute-done((bf16[4,4224]{1,0:T(4,128)(2,1)S(1)}, bf16[4,4224]{1,0:T(4,128)(2,1)S(1)}, u32[]{:S(2)}, u32[]{:S(2)}) %collective-permute-start.1) | collective-permute-done | bytes 33824 | tf_op jit(solution)/shard_map/ppermute | solution.py:24
  10.8 0.0 collective-permute-done.refs_1_
  10.9 2.5 %collective-permute-start.5 = (bf16[16,4224]{1,0:T(8,128)(2,1)S(1)}, bf16[16,4224]{1,0:T(8,128)(2,1)S(1)}, u32[]{:S(2)}, u32[]{:S(2)}) collective-permute-start(bf16[16,4224]{1,0:T(8,128)(2,1)S(1)} %stack_blocks.1), channel_id=1, source_target_pairs={{0,18},{1,19},{2,16},{3,17},{4,22},{5,23},{6,20},{7,21},{8,26},{9,... | collective-permute-start | bytes 405512 | tf_op jit(solution)/shard_map/ppermute | solution.py:24
  13.4 0.5 %collective-permute-start.4 = (bf16[16,4224]{1,0:T(8,128)(2,1)S(1)}, bf16[16,4224]{1,0:T(8,128)(2,1)S(1)}, u32[]{:S(2)}, u32[]{:S(2)}) collective-permute-start(bf16[16,4224]{1,0:T(8,128)(2,1)S(1)} %stack_blocks.1), channel_id=1, source_target_pairs={{0,16},{1,17},{2,18},{3,19},{4,20},{5,21},{6,22},{7,23},{8,24},{9,... | collective-permute-start | bytes 405512 | tf_op jit(solution)/shard_map/ppermute | solution.py:24
  13.9 0.5 %collective-permute-start.3 = (bf16[16,4224]{1,0:T(8,128)(2,1)S(1)}, bf16[16,4224]{1,0:T(8,128)(2,1)S(1)}, u32[]{:S(2)}, u32[]{:S(2)}) collective-permute-start(bf16[16,4224]{1,0:T(8,128)(2,1)S(1)} %stack_blocks.1), channel_id=1, source_target_pairs={{0,2},{1,3},{2,0},{3,1},{4,6},{5,7},{6,4},{7,5},{8,10},{9,11},{10,... | collective-permute-start | bytes 405512 | tf_op jit(solution)/shard_map/ppermute | solution.py:24
  14.4 4.7 %fetch_up.1 = (bf16[4096,1024]{1,0:T(8,128)(2,1)S(1)}, bf16[1024,2048]{1,0:T(8,128)(2,1)S(1)}) custom-call(bf16[4096,1024]{1,0:T(8,128)(2,1)} %bitcast.11, bf16[2048,2048]{1,0:T(8,128)(2,1)} %bitcast.8), custom_call_target="tpu_custom_call" | custom-call | bytes 12582912 | tf_op jit(solution)/shard_map/fetch_up/pallas_call | solution.py:114
  19.1 0.0 collective-permute-done.5
  19.1 0.0 collective-permute-done.4
  19.2 0.0 collective-permute-done.3
  19.2 0.1 collective-permute-start.6
  19.4 1.9 %collective-permute-done.6 = bf16[64,4224]{1,0:T(8,128)(2,1)S(1)} collective-permute-done((bf16[64,4224]{1,0:T(8,128)(2,1)S(1)}, bf16[64,4224]{1,0:T(8,128)(2,1)S(1)}, u32[]{:S(2)}, u32[]{:S(2)}) %collective-permute-start.6) | collective-permute-done | bytes 540704 | tf_op jit(solution)/shard_map/ppermute | solution.py:24
  21.3 1.3 %expand_rows.2.refs_0_ = bf16[128,512]{1,0:T(8,128)(2,1)S(1)} custom-call(bf16[128,4224]{1,0:T(8,128)(2,1)S(1)} %constant_dynamic-update-slice_fusion.rows_ref.refs_3_, bf16[4096,1024]{1,0:T(8,128)(2,1)S(1)} %fetch_gate.1.gate_ref, bf16[4096,1024]{1,0:T(8,128)(2,1)S(1)} %get-tuple-element.26.up_ref), custom_call_target="tpu_custom_call" | custom-call | bytes 65536 | tf_op jit(solution)/shard_map/expand_rows/pallas_call | solution.py:144
  22.6 1.6 %collective-permute-start.8 = (bf16[128,512]{1,0:T(8,128)(2,1)S(1)}, bf16[128,512]{1,0:T(8,128)(2,1)S(1)}, u32[]{:S(2)}, u32[]{:S(2)}) collective-permute-start(bf16[128,512]{1,0:T(8,128)(2,1)S(1)} %expand_rows.2.refs_0_), channel_id=1, source_target_pairs={{0,16},{1,17},{2,18},{3,19},{4,20},{5,21},{6,22},{7,23},{8,24},{9,... | collective-permute-start | bytes 393224 | tf_op jit(solution)/shard_map/ppermute | solution.py:24
  24.2 0.4 contract_hidden.4.refs_2_
  24.6 1.4 %expand_rows.3.refs_0_ = bf16[128,512]{1,0:T(8,128)(2,1)S(1)} custom-call(bf16[128,4224]{1,0:T(8,128)(2,1)S(1)} %constant_dynamic-update-slice_fusion.rows_ref.refs_3_, bf16[4096,1024]{1,0:T(8,128)(2,1)S(1)} %fetch_gate.1.gate_ref, bf16[4096,1024]{1,0:T(8,128)(2,1)S(1)} %get-tuple-element.26.up_ref), custom_call_target="tpu_custom_call" | custom-call | bytes 65536 | tf_op jit(solution)/shard_map/expand_rows/pallas_call | solution.py:144
  26.0 0.6 %collective-permute-start.7 = (bf16[128,512]{1,0:T(8,128)(2,1)S(1)}, bf16[128,512]{1,0:T(8,128)(2,1)S(1)}, u32[]{:S(2)}, u32[]{:S(2)}) collective-permute-start(bf16[128,512]{1,0:T(8,128)(2,1)S(1)} %expand_rows.3.refs_0_), channel_id=1, source_target_pairs={{0,16},{1,17},{2,18},{3,19},{4,20},{5,21},{6,22},{7,23},{8,24},{9,... | collective-permute-start | bytes 393224 | tf_op jit(solution)/shard_map/ppermute | solution.py:24
  26.6 0.5 contract_hidden.5.refs_2_
  27.1 2.2 %fetch_down.1.refs_1_ = bf16[1024,2048]{1,0:T(8,128)(2,1)S(1)} custom-call(bf16[2048,2048]{1,0:T(8,128)(2,1)} %bitcast.9), custom_call_target="tpu_custom_call" | custom-call | bytes 4194304 | tf_op jit(solution)/shard_map/fetch_down/pallas_call | solution.py:114
  29.3 0.0 collective-permute-done.8.refs_0_
  29.3 0.5 contract_hidden.6.refs_2_
  29.8 1.6 %collective-permute-done.7.refs_0_ = bf16[128,512]{1,0:T(8,128)(2,1)S(1)} collective-permute-done((bf16[128,512]{1,0:T(8,128)(2,1)S(1)}, bf16[128,512]{1,0:T(8,128)(2,1)S(1)}, u32[]{:S(2)}, u32[]{:S(2)}) %collective-permute-start.7) | collective-permute-done | bytes 131104 | tf_op jit(solution)/shard_map/ppermute | solution.py:24
  31.3 0.5 contract_hidden.7.total_ref
  31.8 0.1 collective-permute-start.9
  31.9 1.5 %collective-permute-done.9.received_ref = bf16[64,2048]{1,0:T(8,128)(2,1)S(1)} collective-permute-done((bf16[64,2048]{1,0:T(8,128)(2,1)S(1)}, bf16[64,2048]{1,0:T(8,128)(2,1)S(1)}, u32[]{:S(2)}, u32[]{:S(2)}) %collective-permute-start.9) | collective-permute-done | bytes 262176 | tf_op jit(solution)/shard_map/ppermute | solution.py:24
  33.4 0.1 add_and_order.1
  33.6 16.0 %all_to_all.5 = bf16[16,4,2048]{2,1,0:T(4,128)(2,1)S(1)} all-to-all(bf16[16,4,2048]{2,1,0:T(4,128)(2,1)S(1)} %add_and_order.1), channel_id=1, replica_groups=mesh['dp'=2,'far'=8,'core'=2] {'dp','far'}, dimensions={0} | all-to-all | bytes 524288 | tf_op jit(solution)/shard_map/all_to_all | solution.py:282
  49.6 0.7 %bitcast_reduce_fusion = bf16[2,4,2048]{2,1,0:T(4,128)(2,1)} fusion(bf16[16,4,2048]{2,1,0:T(4,128)(2,1)S(1)} %all_to_all.5), kind=kLoop, calls=%fused_computation.2 | loop fusion | flops 114688 | bytes 294912 | tf_op jit(solution)/shard_map/reduce_sum | solution.py:284
  (8 shorter events, 0.2 us)
Async XLA Ops:
  0.9 9.2 %collective-permute-start.2 = (bf16[4,4224]{1,0:T(4,128)(2,1)S(1)}, bf16[4,4224]{1,0:T(4,128)(2,1)S(1)}, u32[]{:S(2)}, u32[]{:S(2)}) collective-permute-start(bf16[4,4224]{1,0:T(4,128)(2,1)S(1)} %pack_block.1.refs_0_), channel_id=1, source_target_pairs={{0,12},{1,13},{2,14},{3,15},{4,8},{5,9},{6,10},{7,11},{8,4},{9,5},... | collective-permute-start | bytes 101384 | tf_op jit(solution)/shard_map/ppermute | solution.py:24
  6.0 4.8 %collective-permute-start.1 = (bf16[4,4224]{1,0:T(4,128)(2,1)S(1)}, bf16[4,4224]{1,0:T(4,128)(2,1)S(1)}, u32[]{:S(2)}, u32[]{:S(2)}) collective-permute-start(bf16[4,4224]{1,0:T(4,128)(2,1)S(1)} %pack_block.1.refs_0_), channel_id=1, source_target_pairs={{0,8},{1,9},{2,10},{3,11},{4,12},{5,13},{6,14},{7,15},{8,0},{9,1},... | collective-permute-start | bytes 101384 | tf_op jit(solution)/shard_map/ppermute | solution.py:24
  6.0 4.8 %collective-permute-start = (bf16[4,4224]{1,0:T(4,128)(2,1)S(1)}, bf16[4,4224]{1,0:T(4,128)(2,1)S(1)}, u32[]{:S(2)}, u32[]{:S(2)}) collective-permute-start(bf16[4,4224]{1,0:T(4,128)(2,1)S(1)} %pack_block.1.refs_0_), channel_id=1, source_target_pairs={{0,4},{1,5},{2,6},{3,7},{4,0},{5,1},{6,2},{7,3},{8,12},{9,13},{10,... | collective-permute-start | bytes 101384 | tf_op jit(solution)/shard_map/ppermute | solution.py:24
  10.9 8.3 %collective-permute-start.5 = (bf16[16,4224]{1,0:T(8,128)(2,1)S(1)}, bf16[16,4224]{1,0:T(8,128)(2,1)S(1)}, u32[]{:S(2)}, u32[]{:S(2)}) collective-permute-start(bf16[16,4224]{1,0:T(8,128)(2,1)S(1)} %stack_blocks.1), channel_id=1, source_target_pairs={{0,18},{1,19},{2,16},{3,17},{4,22},{5,23},{6,20},{7,21},{8,26},{9,... | collective-permute-start | bytes 405512 | tf_op jit(solution)/shard_map/ppermute | solution.py:24
  13.4 5.8 %collective-permute-start.4 = (bf16[16,4224]{1,0:T(8,128)(2,1)S(1)}, bf16[16,4224]{1,0:T(8,128)(2,1)S(1)}, u32[]{:S(2)}, u32[]{:S(2)}) collective-permute-start(bf16[16,4224]{1,0:T(8,128)(2,1)S(1)} %stack_blocks.1), channel_id=1, source_target_pairs={{0,16},{1,17},{2,18},{3,19},{4,20},{5,21},{6,22},{7,23},{8,24},{9,... | collective-permute-start | bytes 405512 | tf_op jit(solution)/shard_map/ppermute | solution.py:24
  13.9 5.3 %collective-permute-start.3 = (bf16[16,4224]{1,0:T(8,128)(2,1)S(1)}, bf16[16,4224]{1,0:T(8,128)(2,1)S(1)}, u32[]{:S(2)}, u32[]{:S(2)}) collective-permute-start(bf16[16,4224]{1,0:T(8,128)(2,1)S(1)} %stack_blocks.1), channel_id=1, source_target_pairs={{0,2},{1,3},{2,0},{3,1},{4,6},{5,7},{6,4},{7,5},{8,10},{9,11},{10,... | collective-permute-start | bytes 405512 | tf_op jit(solution)/shard_map/ppermute | solution.py:24
  19.2 2.0 %collective-permute-start.6 = (bf16[64,4224]{1,0:T(8,128)(2,1)S(1)}, bf16[64,4224]{1,0:T(8,128)(2,1)S(1)}, u32[]{:S(2)}, u32[]{:S(2)}) collective-permute-start(bf16[64,4224]{1,0:T(8,128)(2,1)S(1)} %pad_maximum_fusion), channel_id=1, source_target_pairs={{0,1},{1,0},{2,3},{3,2},{4,5},{5,4},{6,7},{7,6},{8,9},{9,8},{10,11... | collective-permute-start | bytes 1622024 | tf_op jit(solution)/shard_map/ppermute | solution.py:24
  22.6 6.7 %collective-permute-start.8 = (bf16[128,512]{1,0:T(8,128)(2,1)S(1)}, bf16[128,512]{1,0:T(8,128)(2,1)S(1)}, u32[]{:S(2)}, u32[]{:S(2)}) collective-permute-start(bf16[128,512]{1,0:T(8,128)(2,1)S(1)} %expand_rows.2.refs_0_), channel_id=1, source_target_pairs={{0,16},{1,17},{2,18},{3,19},{4,20},{5,21},{6,22},{7,23},{8,24},{9,... | collective-permute-start | bytes 393224 | tf_op jit(solution)/shard_map/ppermute | solution.py:24
  26.0 5.3 %collective-permute-start.7 = (bf16[128,512]{1,0:T(8,128)(2,1)S(1)}, bf16[128,512]{1,0:T(8,128)(2,1)S(1)}, u32[]{:S(2)}, u32[]{:S(2)}) collective-permute-start(bf16[128,512]{1,0:T(8,128)(2,1)S(1)} %expand_rows.3.refs_0_), channel_id=1, source_target_pairs={{0,16},{1,17},{2,18},{3,19},{4,20},{5,21},{6,22},{7,23},{8,24},{9,... | collective-permute-start | bytes 393224 | tf_op jit(solution)/shard_map/ppermute | solution.py:24
  31.8 1.6 %collective-permute-start.9 = (bf16[64,2048]{1,0:T(8,128)(2,1)S(1)}, bf16[64,2048]{1,0:T(8,128)(2,1)S(1)}, u32[]{:S(2)}, u32[]{:S(2)}) collective-permute-start(bf16[64,2048]{1,0:T(8,128)(2,1)S(1)} %slice.7), channel_id=1, source_target_pairs={{0,1},{1,0},{2,3},{3,2},{4,5},{5,4},{6,7},{7,6},{8,9},{9,8},{10,11... | collective-permute-start | bytes 786440 | tf_op jit(solution)/shard_map/ppermute | solution.py:24

commit v7 on v6

--- a/solution.py
+++ b/solution.py
@@ -9,7 +9,6 @@
 CHUNKS = 2
 TILE = 256
 BATCH = 128
-COPY_BYTES = 1 << 20
 LANES = 128
 EXPERT = ("far", "core")
 
@@ -66,6 +65,7 @@
         out_shape=jax.ShapeDtypeStruct((count, width + LANES), tokens.dtype),
         in_specs=[pl.BlockSpec(memory_space=pltpu.VMEM)] * 3,
         out_specs=pl.BlockSpec(memory_space=pltpu.VMEM),
+        cost_estimate=pl.CostEstimate(flops=20 * 10**9, bytes_accessed=0, transcendentals=0),
         compiler_params=pltpu.CompilerParams(vmem_limit_bytes=1 << 20),
         name="pack_block",
     )(in_hbm(tokens), in_hbm(expert_ids), in_hbm(gate_probs))
@@ -86,43 +86,6 @@
         compiler_params=pltpu.CompilerParams(vmem_limit_bytes=4 << 20),
         name="stack_blocks",
     )(*blocks)
-
-
-def fetch(pieces, after, units, name):
-    shapes = [(w.shape[0] if mask is None else units, w.shape[1]) for w, mask in pieces]
-    parts = []
-    for i, (rows, columns) in enumerate(shapes):
-        step = max(16, min(rows, COPY_BYTES // (2 * columns)))
-        parts += [(i, first, step) for first in range(0, rows, step)]
-    operands, _ = lax.optimization_barrier(([w for w, _ in pieces], after))
-
-    def body(*refs):
-        sources, targets = refs[: len(pieces)], refs[len(pieces) : -1]
-        group = lax.axis_index("dp")
-        copies = []
-        for j, (i, first, step) in enumerate(parts):
-            mask = pieces[i][1]
-            start = first if mask is None else pl.multiple_of((group ^ mask) * units + first, 16)
-            source = sources[i].at[pl.ds(start, step)]
-            target = targets[i].at[pl.ds(first, step)]
-            copies.append(pltpu.make_async_copy(source, target, refs[-1].at[j]))
-        for copy in copies:
-            copy.start()
-        for copy in copies:
-            copy.wait()
-
-    return pl.pallas_call(
-        body,
-        out_shape=[pltpu.VMEM(shape, w.dtype) for shape, (w, _) in zip(shapes, pieces)],
-        in_specs=[pl.BlockSpec(memory_space=pltpu.HBM)] * len(pieces),
-        out_specs=[pl.BlockSpec(memory_space=pltpu.VMEM)] * len(pieces),
-        scratch_shapes=[pltpu.SemaphoreType.DMA((len(parts),))],
-        cost_estimate=pl.CostEstimate(
-            flops=0, bytes_accessed=sum(2 * r * c for r, c in shapes), transcendentals=0
-        ),
-        compiler_params=pltpu.CompilerParams(vmem_limit_bytes=1 << 20),
-        name=name,
-    )(*[in_hbm(w) for w in operands])
 
 
 def expand_rows(rows, w_gate, w_up, start, columns):
@@ -152,18 +115,18 @@
     )(rows, in_vmem(w_gate), in_vmem(w_up))
 
 
-def contract_hidden(parts, downs, before=None, rows=None, half=None):
-    count, width = parts[0][0].shape[0], downs[0].shape[1]
+def contract_hidden(parts, w_down, units, before=None, rows=None, half=None):
+    count, width = parts[0][0].shape[0], w_down.shape[1]
     experts = lax.axis_size(EXPERT)
-    operands = [part for part, _, _ in parts] + [in_vmem(down) for down in downs]
+    operands = [part for part, _, _ in parts] + [in_vmem(w_down)]
     operands += [value for value in (before, rows) if value is not None]
 
     def body(*refs):
-        part_refs, down_refs = refs[: len(parts)], refs[len(parts) : len(parts) + len(downs)]
-        rest = list(refs[len(parts) + len(downs) : -1])
+        part_refs, down_ref = refs[: len(parts)], refs[len(parts)]
+        rest = list(refs[len(parts) + 1 : -1])
         before_ref = rest.pop(0) if before is not None else None
         rows_ref = rest.pop(0) if rows is not None else None
-        me = lax.axis_index(EXPERT)
+        me, group = lax.axis_index(EXPERT), lax.axis_index("dp")
 
         def step(first, batch):
             here = pl.ds(first, batch)
@@ -183,8 +146,9 @@
             for i in range(0, width, tile):
                 cut = slice(i, i + tile)
                 total = 0.0 if before is None else before_ref[here, cut]
-                for left, (_, j, unit) in zip(lefts, parts):
-                    right = down_refs[j][unit : unit + left.shape[1], cut]
+                for left, (_, mask, unit) in zip(lefts, parts):
+                    start = pl.multiple_of((group ^ mask) * units + unit, LANES)
+                    right = down_ref[pl.ds(start, left.shape[1]), cut]
                     total = total + jnp.dot(left, right, preferred_element_type=jnp.float32)
                 if rows is not None:
                     total = total.astype(jnp.bfloat16).astype(jnp.float32) * scale
@@ -237,15 +201,13 @@
     wide, high = groups // 2, experts // 4
 
     block = pack_block(tokens, expert_ids, gate_probs, experts)
+    units = w_up.shape[2]
+    weights = lax.optimization_barrier((block, w_gate[0], w_up[0], w_down[0]))
+    block, gate_weights, up_weights, down_weights = weights
     near = stack_blocks([block] + [swap(block, 0, 4 * i) for i in range(1, high)])
-    units = w_up.shape[2]
-    (gate_weights,) = fetch([(w_gate[0], None)], block, units, "fetch_gate")
-    near, gate_weights = lax.optimization_barrier((near, gate_weights))
     if wide > 1:
         near = jnp.concatenate([near] + [swap(near, 2 * i, 0) for i in range(1, wide)])
     chip = [near, swap(near, 0, 2), swap(near, 1, 0), swap(near, 1, 2)]
-    up_weights, own_down = fetch([(w_up[0], None), (w_down[0], 0)], near, units, "fetch_up")
-    chip[3], up_weights, own_down = lax.optimization_barrier((chip[3], up_weights, own_down))
     chip = jnp.concatenate(chip)
     rows = jnp.concatenate([chip, swap(chip, 0, 1)])
 
@@ -268,13 +230,11 @@
             rows, total = lax.optimization_barrier((rows, total))
         hidden = expand_rows(rows, gate_weights, up_weights, i * step, step)
         for mask in range(1, groups):
-            others[i].append((from_group(hidden, mask), mask - 1, i * step))
-        total = contract_hidden([(hidden, 0, i * step)], [own_down], total)
-    pieces = [(w_down[0], mask) for mask in range(1, groups)]
-    downs = fetch(pieces, hidden, units, "fetch_down")
+            others[i].append((from_group(hidden, mask), mask, i * step))
+        total = contract_hidden([(hidden, 0, i * step)], down_weights, units, total)
     for i in range(chunks):
         weigh = rows if i == chunks - 1 else None
-        total = contract_hidden(others[i], downs, total, weigh, half)
+        total = contract_hidden(others[i], down_weights, units, total, weigh, half)
 
     count, columns = rows.shape[0] // 2, w_down.shape[2]
     received = swap(total[count:].astype(jnp.bfloat16), 0, 1)

time: 50.5 us -> 50.2 us (level)
  Pallas kernels: 16 us -> 5.81 us
  waiting for transfers between devices: 5.65 us -> 15.2 us
  blocking collectives: 16 us -> 15 us
  starting transfers between devices: 11.6 us -> 12.5 us
    pallas_call x3 -> x0, Pallas kernels: 10.4 us -> none  [fetch(): pl.pallas_call(body, out_shape=[pltpu.VMEM(shape, w.dtype) for shape, (w,...]
    ppermute x10, waiting for transfers between devices: 5.65 us -> 15.2 us  [swap(): return lax.ppermute(value, ('dp',) + EXPERT, pairs)]
    all_to_all x1, blocking collectives: 16 us -> 15 us  [local(): lax.all_to_all(blocks, ('dp', 'far'), split_axis=0, concat_axis=0, tiled=...]
    ppermute x10, starting transfers between devices: 11.6 us -> 12.5 us  [swap(): return lax.ppermute(value, ('dp',) + EXPERT, pairs)]
  transfers between devices with their start and end apart: 10 -> 10, of which waited for: 4 -> 8; matrix products, arithmetic and copies ran while one was open for 0% -> 0% of each run, Pallas kernels for 26% -> 6%
where the time goes in v7:
time: 50.2 us; the launch traced here: 50 us
  waiting for transfers between devices  15.2 us (30%)
  blocking collectives  15 us (30%)
  starting transfers between devices  12.5 us (25%)
  Pallas kernels  5.81 us (12%)
  other arithmetic  0.77 us (2%)
  local copies, waits for them, and re-layouts  0.59 us (1%)
    ppermute x10, waiting for transfers between devices, swap(): return lax.ppermute(value, ('dp',) + EXPERT, pairs)  15.2 us
    all_to_all x1, blocking collectives, local(): lax.all_to_all(blocks, ('dp', 'far'), split_axis=0, concat_axis=0, tiled=...  15 us
    ppermute x10, starting transfers between devices, swap(): return lax.ppermute(value, ('dp',) + EXPERT, pairs)  12.5 us
    pallas_call x2, Pallas kernels, expand_rows(): pl.pallas_call(body, out_shape=jax.ShapeDtypeStruct((count, columns), row...  2.8 us
    pallas_call x4, Pallas kernels, contract_hidden(): pl.pallas_call(body, out_shape=jax.ShapeDtypeStruct((count, width), jnp.f...  1.85 us
    pallas_call x1, Pallas kernels, pack_block(): pl.pallas_call(body, out_shape=jax.ShapeDtypeStruct((count, width + LANES...  1.02 us
  transfers between devices with their start and end apart: 10, of which 8 were waited for; matrix products, arithmetic and copies ran while one was open for 0% of the time, Pallas kernels for 6%

profile of v7, /device:TPU:0, one launch (start us, length us, event | category | flops | bytes accessed | tf_op | source)
XLA Modules:
  0.0 50.0 jit_solution(16215078268248763067)
XLA Ops:
  0.0 0.0 copy-start
  0.0 0.0 copy-start.1
  0.0 1.0 %pack_block.1.refs_0_ = bf16[4,4224]{1,0:T(4,128)(2,1)S(1)} custom-call(bf16[4,4096]{1,0:T(4,128)(2,1)} %tokens_ref.1, s32[4,8]{1,0:T(4,128)} %ids_ref.1, f32[4,8]{1,0:T(4,128)} %probs_ref.1), custom_call_target="tpu_custom_call" | custom-call | flops 20000000000 | tf_op jit(solution)/shard_map/pack_block/pallas_call | solution.py:63
  1.0 5.1 %collective-permute-start.2 = (bf16[4,4224]{1,0:T(4,128)(2,1)S(1)}, bf16[4,4224]{1,0:T(4,128)(2,1)S(1)}, u32[]{:S(2)}, u32[]{:S(2)}) collective-permute-start(bf16[4,4224]{1,0:T(4,128)(2,1)S(1)} %pack_block.1.refs_0_), channel_id=1, source_target_pairs={{0,12},{1,13},{2,14},{3,15},{4,8},{5,9},{6,10},{7,11},{8,4},{9,5},... | collective-permute-start | bytes 101384 | tf_op jit(solution)/shard_map/ppermute | solution.py:23
  6.1 0.0 collective-permute-start.1
  6.1 0.6 %collective-permute-start = (bf16[4,4224]{1,0:T(4,128)(2,1)S(1)}, bf16[4,4224]{1,0:T(4,128)(2,1)S(1)}, u32[]{:S(2)}, u32[]{:S(2)}) collective-permute-start(bf16[4,4224]{1,0:T(4,128)(2,1)S(1)} %pack_block.1.refs_0_), channel_id=1, source_target_pairs={{0,4},{1,5},{2,6},{3,7},{4,0},{5,1},{6,2},{7,3},{8,12},{9,13},{10,... | collective-permute-start | bytes 101384 | tf_op jit(solution)/shard_map/ppermute | solution.py:23
  6.8 1.3 %collective-permute-done.2.refs_3_ = bf16[4,4224]{1,0:T(4,128)(2,1)S(1)} collective-permute-done((bf16[4,4224]{1,0:T(4,128)(2,1)S(1)}, bf16[4,4224]{1,0:T(4,128)(2,1)S(1)}, u32[]{:S(2)}, u32[]{:S(2)}) %collective-permute-start.2) | collective-permute-done | bytes 33824 | tf_op jit(solution)/shard_map/ppermute | solution.py:23
  8.0 2.9 %collective-permute-done.1.refs_2_ = bf16[4,4224]{1,0:T(4,128)(2,1)S(1)} collective-permute-done((bf16[4,4224]{1,0:T(4,128)(2,1)S(1)}, bf16[4,4224]{1,0:T(4,128)(2,1)S(1)}, u32[]{:S(2)}, u32[]{:S(2)}) %collective-permute-start.1) | collective-permute-done | bytes 33824 | tf_op jit(solution)/shard_map/ppermute | solution.py:23
  11.0 0.0 collective-permute-done.refs_1_
  11.0 2.5 %collective-permute-start.5 = (bf16[16,4224]{1,0:T(8,128)(2,1)S(1)}, bf16[16,4224]{1,0:T(8,128)(2,1)S(1)}, u32[]{:S(2)}, u32[]{:S(2)}) collective-permute-start(bf16[16,4224]{1,0:T(8,128)(2,1)S(1)} %stack_blocks.1), channel_id=1, source_target_pairs={{0,18},{1,19},{2,16},{3,17},{4,22},{5,23},{6,20},{7,21},{8,26},{9,... | collective-permute-start | bytes 405512 | tf_op jit(solution)/shard_map/ppermute | solution.py:23
  13.5 0.5 %collective-permute-start.4 = (bf16[16,4224]{1,0:T(8,128)(2,1)S(1)}, bf16[16,4224]{1,0:T(8,128)(2,1)S(1)}, u32[]{:S(2)}, u32[]{:S(2)}) collective-permute-start(bf16[16,4224]{1,0:T(8,128)(2,1)S(1)} %stack_blocks.1), channel_id=1, source_target_pairs={{0,16},{1,17},{2,18},{3,19},{4,20},{5,21},{6,22},{7,23},{8,24},{9,... | collective-permute-start | bytes 405512 | tf_op jit(solution)/shard_map/ppermute | solution.py:23
  14.1 0.5 %collective-permute-start.3 = (bf16[16,4224]{1,0:T(8,128)(2,1)S(1)}, bf16[16,4224]{1,0:T(8,128)(2,1)S(1)}, u32[]{:S(2)}, u32[]{:S(2)}) collective-permute-start(bf16[16,4224]{1,0:T(8,128)(2,1)S(1)} %stack_blocks.1), channel_id=1, source_target_pairs={{0,2},{1,3},{2,0},{3,1},{4,6},{5,7},{6,4},{7,5},{8,10},{9,11},{10,... | collective-permute-start | bytes 405512 | tf_op jit(solution)/shard_map/ppermute | solution.py:23
  14.6 2.8 %collective-permute-done.5 = bf16[16,4224]{1,0:T(8,128)(2,1)S(1)} collective-permute-done((bf16[16,4224]{1,0:T(8,128)(2,1)S(1)}, bf16[16,4224]{1,0:T(8,128)(2,1)S(1)}, u32[]{:S(2)}, u32[]{:S(2)}) %collective-permute-start.5) | collective-permute-done | bytes 135200 | tf_op jit(solution)/shard_map/ppermute | solution.py:23
  17.4 1.4 %collective-permute-done.4 = bf16[16,4224]{1,0:T(8,128)(2,1)S(1)} collective-permute-done((bf16[16,4224]{1,0:T(8,128)(2,1)S(1)}, bf16[16,4224]{1,0:T(8,128)(2,1)S(1)}, u32[]{:S(2)}, u32[]{:S(2)}) %collective-permute-start.4) | collective-permute-done | bytes 135200 | tf_op jit(solution)/shard_map/ppermute | solution.py:23
  18.8 0.2 collective-permute-done.3
  19.1 0.1 collective-permute-start.6
  19.3 1.9 %collective-permute-done.6 = bf16[64,4224]{1,0:T(8,128)(2,1)S(1)} collective-permute-done((bf16[64,4224]{1,0:T(8,128)(2,1)S(1)}, bf16[64,4224]{1,0:T(8,128)(2,1)S(1)}, u32[]{:S(2)}, u32[]{:S(2)}) %collective-permute-start.6) | collective-permute-done | bytes 540704 | tf_op jit(solution)/shard_map/ppermute | solution.py:23
  21.1 0.0 slice-start
  21.2 0.0 copy-done
  21.2 0.0 copy-done.1
  21.2 0.0 slice-start.1
  21.2 1.4 %expand_rows.2.refs_0_ = bf16[128,512]{1,0:T(8,128)(2,1)S(1)} custom-call(bf16[128,4224]{1,0:T(8,128)(2,1)S(1)} %constant_dynamic-update-slice_fusion.rows_ref.refs_3_, bf16[4096,1024]{1,0:T(8,128)(2,1)S(1)} %bitcast.14, bf16[4096,1024]{1,0:T(8,128)(2,1)S(1)} %bitcast.16), custom_call_target="tpu_custom_call" | custom-call | bytes 65536 | tf_op jit(solution)/shard_map/expand_rows/pallas_call | solution.py:107
  22.6 1.5 %collective-permute-start.8 = (bf16[128,512]{1,0:T(8,128)(2,1)S(1)}, bf16[128,512]{1,0:T(8,128)(2,1)S(1)}, u32[]{:S(2)}, u32[]{:S(2)}) collective-permute-start(bf16[128,512]{1,0:T(8,128)(2,1)S(1)} %expand_rows.2.refs_0_), channel_id=1, source_target_pairs={{0,16},{1,17},{2,18},{3,19},{4,20},{5,21},{6,22},{7,23},{8,24},{9,... | collective-permute-start | bytes 393224 | tf_op jit(solution)/shard_map/ppermute | solution.py:23
  24.2 0.0 slice-done
  24.2 0.4 slice-done.1
  24.6 0.4 contract_hidden.4.refs_2_
  25.1 1.4 %expand_rows.3.refs_0_ = bf16[128,512]{1,0:T(8,128)(2,1)S(1)} custom-call(bf16[128,4224]{1,0:T(8,128)(2,1)S(1)} %constant_dynamic-update-slice_fusion.rows_ref.refs_3_, bf16[4096,1024]{1,0:T(8,128)(2,1)S(1)} %bitcast.15, bf16[4096,1024]{1,0:T(8,128)(2,1)S(1)} %bitcast.17), custom_call_target="tpu_custom_call" | custom-call | bytes 65536 | tf_op jit(solution)/shard_map/expand_rows/pallas_call | solution.py:107
  26.4 1.5 %collective-permute-start.7 = (bf16[128,512]{1,0:T(8,128)(2,1)S(1)}, bf16[128,512]{1,0:T(8,128)(2,1)S(1)}, u32[]{:S(2)}, u32[]{:S(2)}) collective-permute-start(bf16[128,512]{1,0:T(8,128)(2,1)S(1)} %expand_rows.3.refs_0_), channel_id=1, source_target_pairs={{0,16},{1,17},{2,18},{3,19},{4,20},{5,21},{6,22},{7,23},{8,24},{9,... | collective-permute-start | bytes 393224 | tf_op jit(solution)/shard_map/ppermute | solution.py:23
  28.0 0.5 contract_hidden.5.refs_2_
  28.5 0.0 collective-permute-done.8.refs_0_
  28.5 0.5 contract_hidden.6.refs_2_
  28.9 3.1 %collective-permute-done.7.refs_0_ = bf16[128,512]{1,0:T(8,128)(2,1)S(1)} collective-permute-done((bf16[128,512]{1,0:T(8,128)(2,1)S(1)}, bf16[128,512]{1,0:T(8,128)(2,1)S(1)}, u32[]{:S(2)}, u32[]{:S(2)}) %collective-permute-start.7) | collective-permute-done | bytes 131104 | tf_op jit(solution)/shard_map/ppermute | solution.py:23
  32.0 0.5 contract_hidden.7.total_ref
  32.6 0.1 collective-permute-start.9
  32.6 1.5 %collective-permute-done.9.received_ref = bf16[64,2048]{1,0:T(8,128)(2,1)S(1)} collective-permute-done((bf16[64,2048]{1,0:T(8,128)(2,1)S(1)}, bf16[64,2048]{1,0:T(8,128)(2,1)S(1)}, u32[]{:S(2)}, u32[]{:S(2)}) %collective-permute-start.9) | collective-permute-done | bytes 262176 | tf_op jit(solution)/shard_map/ppermute | solution.py:23
  34.2 0.1 add_and_order.1
  34.3 15.0 %all_to_all.5 = bf16[16,4,2048]{2,1,0:T(4,128)(2,1)S(1)} all-to-all(bf16[16,4,2048]{2,1,0:T(4,128)(2,1)S(1)} %add_and_order.1), channel_id=1, replica_groups=mesh['dp'=2,'far'=8,'core'=2] {'dp','far'}, dimensions={0} | all-to-all | bytes 524288 | tf_op jit(solution)/shard_map/all_to_all | solution.py:242
  49.2 0.7 %bitcast_reduce_fusion = bf16[2,4,2048]{2,1,0:T(4,128)(2,1)} fusion(bf16[16,4,2048]{2,1,0:T(4,128)(2,1)S(1)} %all_to_all.5), kind=kLoop, calls=%fused_computation.2 | loop fusion | flops 114688 | bytes 294912 | tf_op jit(solution)/shard_map/reduce_sum | solution.py:244
  (9 shorter events, 0.2 us)
Async XLA Ops:
  0.0 21.2 %copy-start = (bf16[1,4096,1024]{2,1,0:T(8,128)(2,1)S(1)}, bf16[1,4096,1024]{2,1,0:T(8,128)(2,1)}, u32[]{:S(2)}) copy-start(bf16[1,4096,1024]{2,1,0:T(8,128)(2,1)} %param.9) | copy-start | bytes 25165828
  0.0 21.2 %copy-start.1 = (bf16[1,4096,1024]{2,1,0:T(8,128)(2,1)S(1)}, bf16[1,4096,1024]{2,1,0:T(8,128)(2,1)}, u32[]{:S(2)}) copy-start(bf16[1,4096,1024]{2,1,0:T(8,128)(2,1)} %param.10) | copy-start | bytes 25165828
  1.0 7.0 %collective-permute-start.2 = (bf16[4,4224]{1,0:T(4,128)(2,1)S(1)}, bf16[4,4224]{1,0:T(4,128)(2,1)S(1)}, u32[]{:S(2)}, u32[]{:S(2)}) collective-permute-start(bf16[4,4224]{1,0:T(4,128)(2,1)S(1)} %pack_block.1.refs_0_), channel_id=1, source_target_pairs={{0,12},{1,13},{2,14},{3,15},{4,8},{5,9},{6,10},{7,11},{8,4},{9,5},... | collective-permute-start | bytes 101384 | tf_op jit(solution)/shard_map/ppermute | solution.py:23
  6.1 4.8 %collective-permute-start.1 = (bf16[4,4224]{1,0:T(4,128)(2,1)S(1)}, bf16[4,4224]{1,0:T(4,128)(2,1)S(1)}, u32[]{:S(2)}, u32[]{:S(2)}) collective-permute-start(bf16[4,4224]{1,0:T(4,128)(2,1)S(1)} %pack_block.1.refs_0_), channel_id=1, source_target_pairs={{0,8},{1,9},{2,10},{3,11},{4,12},{5,13},{6,14},{7,15},{8,0},{9,1},... | collective-permute-start | bytes 101384 | tf_op jit(solution)/shard_map/ppermute | solution.py:23
  6.1 4.8 %collective-permute-start = (bf16[4,4224]{1,0:T(4,128)(2,1)S(1)}, bf16[4,4224]{1,0:T(4,128)(2,1)S(1)}, u32[]{:S(2)}, u32[]{:S(2)}) collective-permute-start(bf16[4,4224]{1,0:T(4,128)(2,1)S(1)} %pack_block.1.refs_0_), channel_id=1, source_target_pairs={{0,4},{1,5},{2,6},{3,7},{4,0},{5,1},{6,2},{7,3},{8,12},{9,13},{10,... | collective-permute-start | bytes 101384 | tf_op jit(solution)/shard_map/ppermute | solution.py:23
  11.0 6.4 %collective-permute-start.5 = (bf16[16,4224]{1,0:T(8,128)(2,1)S(1)}, bf16[16,4224]{1,0:T(8,128)(2,1)S(1)}, u32[]{:S(2)}, u32[]{:S(2)}) collective-permute-start(bf16[16,4224]{1,0:T(8,128)(2,1)S(1)} %stack_blocks.1), channel_id=1, source_target_pairs={{0,18},{1,19},{2,16},{3,17},{4,22},{5,23},{6,20},{7,21},{8,26},{9,... | collective-permute-start | bytes 405512 | tf_op jit(solution)/shard_map/ppermute | solution.py:23
  13.5 5.3 %collective-permute-start.4 = (bf16[16,4224]{1,0:T(8,128)(2,1)S(1)}, bf16[16,4224]{1,0:T(8,128)(2,1)S(1)}, u32[]{:S(2)}, u32[]{:S(2)}) collective-permute-start(bf16[16,4224]{1,0:T(8,128)(2,1)S(1)} %stack_blocks.1), channel_id=1, source_target_pairs={{0,16},{1,17},{2,18},{3,19},{4,20},{5,21},{6,22},{7,23},{8,24},{9,... | collective-permute-start | bytes 405512 | tf_op jit(solution)/shard_map/ppermute | solution.py:23
  14.1 5.0 %collective-permute-start.3 = (bf16[16,4224]{1,0:T(8,128)(2,1)S(1)}, bf16[16,4224]{1,0:T(8,128)(2,1)S(1)}, u32[]{:S(2)}, u32[]{:S(2)}) collective-permute-start(bf16[16,4224]{1,0:T(8,128)(2,1)S(1)} %stack_blocks.1), channel_id=1, source_target_pairs={{0,2},{1,3},{2,0},{3,1},{4,6},{5,7},{6,4},{7,5},{8,10},{9,11},{10,... | collective-permute-start | bytes 405512 | tf_op jit(solution)/shard_map/ppermute | solution.py:23
  19.1 2.0 %collective-permute-start.6 = (bf16[64,4224]{1,0:T(8,128)(2,1)S(1)}, bf16[64,4224]{1,0:T(8,128)(2,1)S(1)}, u32[]{:S(2)}, u32[]{:S(2)}) collective-permute-start(bf16[64,4224]{1,0:T(8,128)(2,1)S(1)} %pad_maximum_fusion), channel_id=1, source_target_pairs={{0,1},{1,0},{2,3},{3,2},{4,5},{5,4},{6,7},{7,6},{8,9},{9,8},{10,11... | collective-permute-start | bytes 1622024 | tf_op jit(solution)/shard_map/ppermute | solution.py:23
  21.1 3.0 %slice-start = ((s8[8388608]{0:T(1024)(128)(4,1)}), s8[4194304]{0:T(1024)(128)(4,1)S(1)}, s32[]{:S(2)}) async-start(s8[8388608]{0:T(1024)(128)(4,1)} %bitcast.8), calls=%async_computation.1 | async-start | bytes 8388608
  21.2 3.4 %slice-start.1 = ((s8[8388608]{0:T(1024)(128)(4,1)}), s8[4194304]{0:T(1024)(128)(4,1)S(1)}, s32[]{:S(2)}) async-start(s8[8388608]{0:T(1024)(128)(4,1)} %bitcast.8), calls=%async_computation.2 | async-start | bytes 8388608
  22.6 5.8 %collective-permute-start.8 = (bf16[128,512]{1,0:T(8,128)(2,1)S(1)}, bf16[128,512]{1,0:T(8,128)(2,1)S(1)}, u32[]{:S(2)}, u32[]{:S(2)}) collective-permute-start(bf16[128,512]{1,0:T(8,128)(2,1)S(1)} %expand_rows.2.refs_0_), channel_id=1, source_target_pairs={{0,16},{1,17},{2,18},{3,19},{4,20},{5,21},{6,22},{7,23},{8,24},{9,... | collective-permute-start | bytes 393224 | tf_op jit(solution)/shard_map/ppermute | solution.py:23
  26.4 5.6 %collective-permute-start.7 = (bf16[128,512]{1,0:T(8,128)(2,1)S(1)}, bf16[128,512]{1,0:T(8,128)(2,1)S(1)}, u32[]{:S(2)}, u32[]{:S(2)}) collective-permute-start(bf16[128,512]{1,0:T(8,128)(2,1)S(1)} %expand_rows.3.refs_0_), channel_id=1, source_target_pairs={{0,16},{1,17},{2,18},{3,19},{4,20},{5,21},{6,22},{7,23},{8,24},{9,... | collective-permute-start | bytes 393224 | tf_op jit(solution)/shard_map/ppermute | solution.py:23
  32.6 1.6 %collective-permute-start.9 = (bf16[64,2048]{1,0:T(8,128)(2,1)S(1)}, bf16[64,2048]{1,0:T(8,128)(2,1)S(1)}, u32[]{:S(2)}, u32[]{:S(2)}) collective-permute-start(bf16[64,2048]{1,0:T(8,128)(2,1)S(1)} %slice.7), channel_id=1, source_target_pairs={{0,1},{1,0},{2,3},{3,2},{4,5},{5,4},{6,7},{7,6},{8,9},{9,8},{10,11... | collective-permute-start | bytes 786440 | tf_op jit(solution)/shard_map/ppermute | solution.py:23

commit v8 on v7

--- a/solution.py
+++ b/solution.py
@@ -6,7 +6,6 @@
 from jax.sharding import Mesh
 from jax.sharding import PartitionSpec as P
 
-CHUNKS = 2
 TILE = 256
 BATCH = 128
 LANES = 128
@@ -88,87 +87,106 @@
     )(*blocks)
 
 
-def expand_rows(rows, w_gate, w_up, start, columns):
-    count, depth = rows.shape[0], w_gate.shape[0]
+def expand_rows(rows, w_gate, w_up):
+    count, depth, units = rows.shape[0], w_gate.shape[0], w_gate.shape[1]
 
     def body(rows_ref, gate_ref, up_ref, hidden_ref):
         def step(first, batch):
             x = rows_ref[pl.ds(first, batch), :depth]
-            tile = min(TILE, columns)
-            for i in range(0, columns, tile):
-                cut = slice(start + i, start + i + tile)
+            tile = min(TILE, units)
+            for i in range(0, units, tile):
+                cut = slice(i, i + tile)
                 gate = jnp.dot(x, gate_ref[:, cut], preferred_element_type=jnp.float32)
                 up = jnp.dot(x, up_ref[:, cut], preferred_element_type=jnp.float32)
                 value = gate / (1.0 + jnp.exp(-gate)) * up
-                hidden_ref[pl.ds(first, batch), i : i + tile] = value.astype(hidden_ref.dtype)
+                hidden_ref[pl.ds(first, batch), cut] = value.astype(hidden_ref.dtype)
 
         row_batches(count, step)
 
     return pl.pallas_call(
         body,
-        out_shape=jax.ShapeDtypeStruct((count, columns), rows.dtype),
+        out_shape=jax.ShapeDtypeStruct((count, units), rows.dtype),
         in_specs=[pl.BlockSpec(memory_space=pltpu.VMEM)] * 3,
         out_specs=pl.BlockSpec(memory_space=pltpu.VMEM),
-        cost_estimate=pl.CostEstimate(flops=0, bytes_accessed=count * columns, transcendentals=0),
+        cost_estimate=pl.CostEstimate(flops=0, bytes_accessed=count * units, transcendentals=0),
         compiler_params=pltpu.CompilerParams(vmem_limit_bytes=rows.nbytes + (6 << 20)),
         name="expand_rows",
     )(rows, in_vmem(w_gate), in_vmem(w_up))
 
 
-def contract_hidden(parts, w_down, units, before=None, rows=None, half=None):
-    count, width = parts[0][0].shape[0], w_down.shape[1]
-    experts = lax.axis_size(EXPERT)
-    operands = [part for part, _, _ in parts] + [in_vmem(w_down)]
-    operands += [value for value in (before, rows) if value is not None]
-
-    def body(*refs):
-        part_refs, down_ref = refs[: len(parts)], refs[len(parts)]
-        rest = list(refs[len(parts) + 1 : -1])
-        before_ref = rest.pop(0) if before is not None else None
-        rows_ref = rest.pop(0) if rows is not None else None
-        me, group = lax.axis_index(EXPERT), lax.axis_index("dp")
+def contract_own(halves, w_down):
+    count, units = halves[0].shape
+    width = w_down.shape[1]
+
+    def body(first_ref, second_ref, down_ref, total_ref):
+        start = pl.multiple_of(lax.axis_index("dp") * units, LANES)
 
         def step(first, batch):
             here = pl.ds(first, batch)
-            lefts = [ref[here, :] for ref in part_refs]
-            if half is not None:
-                order = [i ^ 1 for i in range(count // half)]
-                lefts = [
-                    jnp.concatenate([left[i * half : (i + 1) * half] for i in order])
-                    for left in lefts
-                ]
-            if rows is not None:
-                table = rows_ref[here, rows.shape[1] - LANES :].astype(jnp.float32)
-                lane = lax.broadcasted_iota(jnp.int32, table.shape, 1)
-                mine = (lax.rem(lane, experts) == me) & (lane < 3 * experts)
-                scale = jnp.sum(jnp.where(mine, table, 0.0), axis=1, keepdims=True)
+            left = jnp.concatenate([first_ref[here, :], second_ref[here, :]])
             tile = min(2 * TILE, width)
             for i in range(0, width, tile):
                 cut = slice(i, i + tile)
-                total = 0.0 if before is None else before_ref[here, cut]
-                for left, (_, mask, unit) in zip(lefts, parts):
-                    start = pl.multiple_of((group ^ mask) * units + unit, LANES)
-                    right = down_ref[pl.ds(start, left.shape[1]), cut]
+                right = down_ref[pl.ds(start, units), cut]
+                total = jnp.dot(left, right, preferred_element_type=jnp.float32)
+                total_ref[0, here, cut] = total[:batch]
+                total_ref[1, here, cut] = total[batch:]
+
+        row_batches(count, step)
+
+    return pl.pallas_call(
+        body,
+        out_shape=jax.ShapeDtypeStruct((2, count, width), jnp.float32),
+        in_specs=[pl.BlockSpec(memory_space=pltpu.VMEM)] * 3,
+        out_specs=pl.BlockSpec(memory_space=pltpu.VMEM),
+        cost_estimate=pl.CostEstimate(flops=0, bytes_accessed=count * width, transcendentals=0),
+        compiler_params=pltpu.CompilerParams(vmem_limit_bytes=12 * count * width + (6 << 20)),
+        name="contract_own",
+    )(*halves, in_vmem(w_down))
+
+
+def contract_others(parts, w_down, own, index, rows, kind, swapped):
+    count, units = parts[0].shape
+    width = w_down.shape[1]
+    experts = lax.axis_size(EXPERT)
+
+    def body(down_ref, own_ref, rows_ref, *refs):
+        me, group = lax.axis_index(EXPERT), lax.axis_index("dp")
+
+        def step(first, batch):
+            here = pl.ds(first, batch)
+            lefts = [ref[here, :] for ref in refs[:-1]]
+            if swapped:
+                half = count // 2
+                lefts = [jnp.concatenate([left[half:], left[:half]]) for left in lefts]
+            table = rows_ref[here, rows.shape[1] - LANES :].astype(jnp.float32)
+            lane = lax.broadcasted_iota(jnp.int32, table.shape, 1)
+            mine = (lax.rem(lane, experts) == me) & (lane < 3 * experts)
+            scale = jnp.sum(jnp.where(mine, table, 0.0), axis=1, keepdims=True)
+            tile = min(2 * TILE, width)
+            for i in range(0, width, tile):
+                cut = slice(i, i + tile)
+                total = own_ref[index, here, cut]
+                for mask, left in enumerate(lefts, 1):
+                    start = pl.multiple_of((group ^ mask) * units, LANES)
+                    right = down_ref[pl.ds(start, units), cut]
                     total = total + jnp.dot(left, right, preferred_element_type=jnp.float32)
-                if rows is not None:
-                    total = total.astype(jnp.bfloat16).astype(jnp.float32) * scale
-                refs[-1][here, cut] = total
+                total = total.astype(jnp.bfloat16).astype(jnp.float32) * scale
+                refs[-1][here, cut] = total.astype(kind)
 
         row_batches(count, step)
 
     return pl.pallas_call(
         body,
-        out_shape=jax.ShapeDtypeStruct((count, width), jnp.float32),
-        in_specs=[pl.BlockSpec(memory_space=pltpu.VMEM)] * len(operands),
+        out_shape=jax.ShapeDtypeStruct((count, width), kind),
+        in_specs=[pl.BlockSpec(memory_space=pltpu.VMEM)] * (3 + len(parts)),
         out_specs=pl.BlockSpec(memory_space=pltpu.VMEM),
         cost_estimate=pl.CostEstimate(flops=0, bytes_accessed=count * width, transcendentals=0),
         compiler_params=pltpu.CompilerParams(
-            vmem_limit_bytes=8 * count * width
-            + (6 << 20)
-            + (0 if rows is None else rows.nbytes)
+            vmem_limit_bytes=16 * count * width + (6 << 20) + rows.nbytes
         ),
-        name="contract_hidden",
-    )(*operands)
+        name="contract_others",
+    )(in_vmem(w_down), own, rows, *parts)
 
 
 def add_and_order(total, received, wide, high):
@@ -209,36 +227,37 @@
         near = jnp.concatenate([near] + [swap(near, 2 * i, 0) for i in range(1, wide)])
     chip = [near, swap(near, 0, 2), swap(near, 1, 0), swap(near, 1, 2)]
     chip = jnp.concatenate(chip)
-    rows = jnp.concatenate([chip, swap(chip, 0, 1)])
-
-    chunks = CHUNKS if units % (LANES * CHUNKS) == 0 else 1
-    step = units // chunks
-    half = rows.shape[0] // 4 if groups == 2 and rows.shape[0] <= BATCH else None
-
-    def from_group(value, mask):
+
+    swapped = groups == 2 and chip.shape[0] <= BATCH
+
+    def from_group(value, mask, as_sent):
         value = swap(value, mask, 0)
-        if half is not None:
+        if as_sent:
             return value
-        value = value.reshape(2, 2, 2, wide, high * token_count, step)
-        value = jnp.stack([value[:, i ^ (mask & 1)] for i in range(2)], axis=1)
-        value = jnp.stack([value[:, :, :, i ^ (mask >> 1)] for i in range(wide)], axis=3)
-        return value.reshape(-1, step)
-
-    total, others = None, [[] for _ in range(chunks)]
-    for i in range(chunks):
-        if total is not None:
-            rows, total = lax.optimization_barrier((rows, total))
-        hidden = expand_rows(rows, gate_weights, up_weights, i * step, step)
-        for mask in range(1, groups):
-            others[i].append((from_group(hidden, mask), mask, i * step))
-        total = contract_hidden([(hidden, 0, i * step)], down_weights, units, total)
-    for i in range(chunks):
-        weigh = rows if i == chunks - 1 else None
-        total = contract_hidden(others[i], down_weights, units, total, weigh, half)
-
-    count, columns = rows.shape[0] // 2, w_down.shape[2]
-    received = swap(total[count:].astype(jnp.bfloat16), 0, 1)
-    blocks = add_and_order(total, received, wide, high)
+        value = value.reshape(2, 2, wide, high * token_count, units)
+        value = jnp.stack([value[i ^ (mask & 1)] for i in range(2)])
+        value = jnp.stack([value[:, :, i ^ (mask >> 1)] for i in range(wide)], axis=2)
+        return value.reshape(-1, units)
+
+    halves = [chip, swap(chip, 0, 1)]
+    first = expand_rows(halves[0], gate_weights, up_weights)
+    first, halves[1] = lax.optimization_barrier((first, halves[1]))
+    hidden = [first, expand_rows(halves[1], gate_weights, up_weights)]
+    others = [
+        [from_group(value, mask, swapped and i == 1) for mask in range(1, groups)]
+        for i, value in enumerate(hidden)
+    ]
+    others = lax.optimization_barrier(others)
+    own = contract_own(hidden, down_weights)
+    kept, sent = (
+        contract_others(
+            others[i], down_weights, own, i, halves[i], kind, swapped and i == 1
+        )
+        for i, kind in enumerate((jnp.float32, jnp.bfloat16))
+    )
+
+    columns = w_down.shape[2]
+    blocks = add_and_order(kept, swap(sent, 0, 1), wide, high)
     blocks = lax.all_to_all(blocks, ("dp", "far"), split_axis=0, concat_axis=0, tiled=True)
     blocks = blocks.reshape(groups, -1, token_count, columns).astype(jnp.float32)
     combined = jnp.sum(blocks, axis=1).astype(jnp.bfloat16)

time: 50.2 us -> 50.2 us (level)
  Pallas kernels: 5.81 us -> 9.82 us
  waiting for transfers between devices: 15.2 us -> 13.6 us
  blocking collectives: 15 us -> 14 us
  starting transfers between devices: 12.5 us -> 11.6 us
  local copies, waits for them, and re-layouts: 0.59 us -> 0.03 us
    pallas_call x6 -> x5, Pallas kernels: 4.65 us -> 8.65 us  [the longest x2 6.2 us: expand_rows(): pl.pallas_call(body, out_shape=jax.ShapeDtypeStruct((count, units), rows....]
    ppermute x10, waiting for transfers between devices: 15.2 us -> 13.6 us  [swap(): return lax.ppermute(value, ('dp',) + EXPERT, pairs)]
    all_to_all x1, blocking collectives: 15 us -> 14 us  [local(): lax.all_to_all(blocks, ('dp', 'far'), split_axis=0, concat_axis=0, tiled=...]
    ppermute x10, starting transfers between devices: 12.5 us -> 11.6 us  [swap(): return lax.ppermute(value, ('dp',) + EXPERT, pairs)]
  transfers between devices with their start and end apart: 10 -> 10, of which waited for: 8 -> 7; matrix products, arithmetic and copies ran while one was open for 0% -> 0% of each run, Pallas kernels for 6% -> 16%
where the time goes in v8:
time: 50.2 us; the launch traced here: 50 us
  blocking collectives  14 us (28%)
  waiting for transfers between devices  13.6 us (27%)
  starting transfers between devices  11.6 us (23%)
  Pallas kernels  9.82 us (20%)
  other arithmetic  0.79 us (2%)
    all_to_all x1, blocking collectives, local(): lax.all_to_all(blocks, ('dp', 'far'), split_axis=0, concat_axis=0, tiled=...  14 us
    ppermute x10, waiting for transfers between devices, swap(): return lax.ppermute(value, ('dp',) + EXPERT, pairs)  13.6 us
    ppermute x10, starting transfers between devices, swap(): return lax.ppermute(value, ('dp',) + EXPERT, pairs)  11.6 us
    pallas_call x2, Pallas kernels, expand_rows(): pl.pallas_call(body, out_shape=jax.ShapeDtypeStruct((count, units), rows....  6.2 us
    pallas_call x2, Pallas kernels, contract_others(): pl.pallas_call(body, out_shape=jax.ShapeDtypeStruct((count, width), kind)...  1.73 us
    pallas_call x1, Pallas kernels, pack_block(): pl.pallas_call(body, out_shape=jax.ShapeDtypeStruct((count, width + LANES...  1.02 us
  transfers between devices with their start and end apart: 10, of which 7 were waited for; matrix products, arithmetic and copies ran while one was open for 0% of the time, Pallas kernels for 16%

profile of v8, /device:TPU:0, one launch (start us, length us, event | category | flops | bytes accessed | tf_op | source)
XLA Modules:
  0.0 50.0 jit_solution(14804201183597955652)
XLA Ops:
  0.0 0.0 copy-start
  0.0 0.0 copy-start.1
  0.0 1.0 %pack_block.1.refs_0_ = bf16[4,4224]{1,0:T(4,128)(2,1)S(1)} custom-call(bf16[4,4096]{1,0:T(4,128)(2,1)} %tokens_ref.1, s32[4,8]{1,0:T(4,128)} %ids_ref.1, f32[4,8]{1,0:T(4,128)} %probs_ref.1), custom_call_target="tpu_custom_call" | custom-call | flops 20000000000 | tf_op jit(solution)/shard_map/pack_block/pallas_call | solution.py:62
  1.0 5.1 %collective-permute-start.2 = (bf16[4,4224]{1,0:T(4,128)(2,1)S(1)}, bf16[4,4224]{1,0:T(4,128)(2,1)S(1)}, u32[]{:S(2)}, u32[]{:S(2)}) collective-permute-start(bf16[4,4224]{1,0:T(4,128)(2,1)S(1)} %pack_block.1.refs_0_), channel_id=1, source_target_pairs={{0,12},{1,13},{2,14},{3,15},{4,8},{5,9},{6,10},{7,11},{8,4},{9,5},... | collective-permute-start | bytes 101384 | tf_op jit(solution)/shard_map/ppermute | solution.py:22
  6.1 0.0 collective-permute-start.1
  6.1 0.6 %collective-permute-start = (bf16[4,4224]{1,0:T(4,128)(2,1)S(1)}, bf16[4,4224]{1,0:T(4,128)(2,1)S(1)}, u32[]{:S(2)}, u32[]{:S(2)}) collective-permute-start(bf16[4,4224]{1,0:T(4,128)(2,1)S(1)} %pack_block.1.refs_0_), channel_id=1, source_target_pairs={{0,4},{1,5},{2,6},{3,7},{4,0},{5,1},{6,2},{7,3},{8,12},{9,13},{10,... | collective-permute-start | bytes 101384 | tf_op jit(solution)/shard_map/ppermute | solution.py:22
  6.8 1.3 %collective-permute-done.2.refs_3_ = bf16[4,4224]{1,0:T(4,128)(2,1)S(1)} collective-permute-done((bf16[4,4224]{1,0:T(4,128)(2,1)S(1)}, bf16[4,4224]{1,0:T(4,128)(2,1)S(1)}, u32[]{:S(2)}, u32[]{:S(2)}) %collective-permute-start.2) | collective-permute-done | bytes 33824 | tf_op jit(solution)/shard_map/ppermute | solution.py:22
  8.0 2.9 %collective-permute-done.1.refs_2_ = bf16[4,4224]{1,0:T(4,128)(2,1)S(1)} collective-permute-done((bf16[4,4224]{1,0:T(4,128)(2,1)S(1)}, bf16[4,4224]{1,0:T(4,128)(2,1)S(1)}, u32[]{:S(2)}, u32[]{:S(2)}) %collective-permute-start.1) | collective-permute-done | bytes 33824 | tf_op jit(solution)/shard_map/ppermute | solution.py:22
  11.0 0.0 collective-permute-done.refs_1_
  11.0 2.5 %collective-permute-start.5 = (bf16[16,4224]{1,0:T(8,128)(2,1)S(1)}, bf16[16,4224]{1,0:T(8,128)(2,1)S(1)}, u32[]{:S(2)}, u32[]{:S(2)}) collective-permute-start(bf16[16,4224]{1,0:T(8,128)(2,1)S(1)} %stack_blocks.1), channel_id=1, source_target_pairs={{0,18},{1,19},{2,16},{3,17},{4,22},{5,23},{6,20},{7,21},{8,26},{9,... | collective-permute-start | bytes 405512 | tf_op jit(solution)/shard_map/ppermute | solution.py:22
  13.5 0.5 %collective-permute-start.4 = (bf16[16,4224]{1,0:T(8,128)(2,1)S(1)}, bf16[16,4224]{1,0:T(8,128)(2,1)S(1)}, u32[]{:S(2)}, u32[]{:S(2)}) collective-permute-start(bf16[16,4224]{1,0:T(8,128)(2,1)S(1)} %stack_blocks.1), channel_id=1, source_target_pairs={{0,16},{1,17},{2,18},{3,19},{4,20},{5,21},{6,22},{7,23},{8,24},{9,... | collective-permute-start | bytes 405512 | tf_op jit(solution)/shard_map/ppermute | solution.py:22
  14.1 0.5 %collective-permute-start.3 = (bf16[16,4224]{1,0:T(8,128)(2,1)S(1)}, bf16[16,4224]{1,0:T(8,128)(2,1)S(1)}, u32[]{:S(2)}, u32[]{:S(2)}) collective-permute-start(bf16[16,4224]{1,0:T(8,128)(2,1)S(1)} %stack_blocks.1), channel_id=1, source_target_pairs={{0,2},{1,3},{2,0},{3,1},{4,6},{5,7},{6,4},{7,5},{8,10},{9,11},{10,... | collective-permute-start | bytes 405512 | tf_op jit(solution)/shard_map/ppermute | solution.py:22
  14.6 2.8 %collective-permute-done.5 = bf16[16,4224]{1,0:T(8,128)(2,1)S(1)} collective-permute-done((bf16[16,4224]{1,0:T(8,128)(2,1)S(1)}, bf16[16,4224]{1,0:T(8,128)(2,1)S(1)}, u32[]{:S(2)}, u32[]{:S(2)}) %collective-permute-start.5) | collective-permute-done | bytes 135200 | tf_op jit(solution)/shard_map/ppermute | solution.py:22
  17.4 1.4 %collective-permute-done.4 = bf16[16,4224]{1,0:T(8,128)(2,1)S(1)} collective-permute-done((bf16[16,4224]{1,0:T(8,128)(2,1)S(1)}, bf16[16,4224]{1,0:T(8,128)(2,1)S(1)}, u32[]{:S(2)}, u32[]{:S(2)}) %collective-permute-start.4) | collective-permute-done | bytes 135200 | tf_op jit(solution)/shard_map/ppermute | solution.py:22
  18.8 0.2 collective-permute-done.3
  19.1 0.1 collective-permute-start.6
  19.2 0.0 copy-done
  19.2 0.0 copy-done.1
  19.2 0.0 slice-start
  19.2 3.1 %expand_rows.2.first_ref = bf16[64,1024]{1,0:T(8,128)(2,1)S(1)} custom-call(bf16[64,4224]{1,0:T(8,128)(2,1)S(1)} %pad_maximum_fusion.rows_ref, bf16[4096,1024]{1,0:T(8,128)(2,1)S(1)} %bitcast.20, bf16[4096,1024]{1,0:T(8,128)(2,1)S(1)} %bitcast.22), custom_call_target="tpu_custom_call" | custom-call | bytes 65536 | tf_op jit(solution)/shard_map/expand_rows/pallas_call | solution.py:106
  22.3 0.0 slice-start.1
  22.3 0.0 collective-permute-done.6.rows_ref
  22.4 1.6 %collective-permute-start.7 = (bf16[64,1024]{1,0:T(8,128)(2,1)S(1)}, bf16[64,1024]{1,0:T(8,128)(2,1)S(1)}, u32[]{:S(2)}, u32[]{:S(2)}) collective-permute-start(bf16[64,1024]{1,0:T(8,128)(2,1)S(1)} %expand_rows.2.first_ref), channel_id=1, source_target_pairs={{0,16},{1,17},{2,18},{3,19},{4,20},{5,21},{6,22},{7,23},{8,24},{9,... | collective-permute-start | bytes 393224 | tf_op jit(solution)/shard_map/ppermute | solution.py:22
  23.9 3.1 %expand_rows.3.second_ref = bf16[64,1024]{1,0:T(8,128)(2,1)S(1)} custom-call(bf16[64,4224]{1,0:T(8,128)(2,1)S(1)} %collective-permute-done.6.rows_ref, bf16[4096,1024]{1,0:T(8,128)(2,1)S(1)} %bitcast.21, bf16[4096,1024]{1,0:T(8,128)(2,1)S(1)} %bitcast.23), custom_call_target="tpu_custom_call" | custom-call | bytes 65536 | tf_op jit(solution)/shard_map/expand_rows/pallas_call | solution.py:106
  27.0 0.6 %collective-permute-start.8 = (bf16[64,1024]{1,0:T(8,128)(2,1)S(1)}, bf16[64,1024]{1,0:T(8,128)(2,1)S(1)}, u32[]{:S(2)}, u32[]{:S(2)}) collective-permute-start(bf16[64,1024]{1,0:T(8,128)(2,1)S(1)} %expand_rows.3.second_ref), channel_id=1, source_target_pairs={{0,16},{1,17},{2,18},{3,19},{4,20},{5,21},{6,22},{7,23},{8,24},{9,... | collective-permute-start | bytes 393224 | tf_op jit(solution)/shard_map/ppermute | solution.py:22
  27.6 0.0 slice-done
  27.6 0.0 slice-done.1
  27.6 0.7 %contract_own.1.own_ref = f32[2,64,2048]{2,1,0:T(8,128)S(1)} custom-call(bf16[64,1024]{1,0:T(8,128)(2,1)S(1)} %expand_rows.2.first_ref, bf16[64,1024]{1,0:T(8,128)(2,1)S(1)} %expand_rows.3.second_ref, bf16[2048,2048]{1,0:T(8,128)(2,1)S(1)} %bitcast.17), custom_call_target="tpu_custom_call" | custom-call | bytes 131072 | tf_op jit(solution)/shard_map/contract_own/pallas_call | solution.py:137
  28.4 0.0 collective-permute-done.7
  28.4 4.3 %collective-permute-done.8.refs_0_ = bf16[64,1024]{1,0:T(8,128)(2,1)S(1)} collective-permute-done((bf16[64,1024]{1,0:T(8,128)(2,1)S(1)}, bf16[64,1024]{1,0:T(8,128)(2,1)S(1)}, u32[]{:S(2)}, u32[]{:S(2)}) %collective-permute-start.8) | collective-permute-done | bytes 131104 | tf_op jit(solution)/shard_map/ppermute | solution.py:22
  32.7 0.9 %contract_others.3 = bf16[64,2048]{1,0:T(8,128)(2,1)S(1)} custom-call(bf16[2048,2048]{1,0:T(8,128)(2,1)S(1)} %bitcast.18, f32[2,64,2048]{2,1,0:T(8,128)S(1)} %contract_own.1.own_ref, bf16[64,4224]{1,0:T(8,128)(2,1)S(1)} %collective-permute-done.6.rows_ref, bf16[64,1024]{1,0:T(8,128)(2,1)S(1)} %collective-permute-done.8.refs_0_), custom_call_target="tpu_custom_call" | custom-call | bytes 131072 | tf_op jit(solution)/shard_map/contract_others/pallas_call | solution.py:179
  33.6 0.1 collective-permute-start.9
  33.6 0.9 %contract_others.2.total_ref = f32[64,2048]{1,0:T(8,128)S(1)} custom-call(bf16[2048,2048]{1,0:T(8,128)(2,1)S(1)} %bitcast.19, f32[2,64,2048]{2,1,0:T(8,128)S(1)} %contract_own.1.own_ref, bf16[64,4224]{1,0:T(8,128)(2,1)S(1)} %pad_maximum_fusion.rows_ref, bf16[64,1024]{1,0:T(8,128)(2,1)S(1)} %bitcast.24), custom_call_target="tpu_custom_call" | custom-call | bytes 131072 | tf_op jit(solution)/shard_map/contract_others/pallas_call | solution.py:179
  34.5 0.6 %collective-permute-done.9.received_ref = bf16[64,2048]{1,0:T(8,128)(2,1)S(1)} collective-permute-done((bf16[64,2048]{1,0:T(8,128)(2,1)S(1)}, bf16[64,2048]{1,0:T(8,128)(2,1)S(1)}, u32[]{:S(2)}, u32[]{:S(2)}) %collective-permute-start.9) | collective-permute-done | bytes 262176 | tf_op jit(solution)/shard_map/ppermute | solution.py:22
  35.2 0.1 add_and_order.1
  35.3 14.0 %all_to_all.5 = bf16[16,4,2048]{2,1,0:T(4,128)(2,1)S(1)} all-to-all(bf16[16,4,2048]{2,1,0:T(4,128)(2,1)S(1)} %add_and_order.1), channel_id=1, replica_groups=mesh['dp'=2,'far'=8,'core'=2] {'dp','far'}, dimensions={0} | all-to-all | bytes 524288 | tf_op jit(solution)/shard_map/all_to_all | solution.py:261
  49.3 0.7 %bitcast_reduce_fusion = bf16[2,4,2048]{2,1,0:T(4,128)(2,1)} fusion(bf16[16,4,2048]{2,1,0:T(4,128)(2,1)S(1)} %all_to_all.5), kind=kLoop, calls=%fused_computation.1 | loop fusion | flops 114688 | bytes 294912 | tf_op jit(solution)/shard_map/reduce_sum | solution.py:263
  (5 shorter events, 0.1 us)
Async XLA Ops:
  0.0 19.2 %copy-start = (bf16[1,4096,1024]{2,1,0:T(8,128)(2,1)S(1)}, bf16[1,4096,1024]{2,1,0:T(8,128)(2,1)}, u32[]{:S(2)}) copy-start(bf16[1,4096,1024]{2,1,0:T(8,128)(2,1)} %param.9) | copy-start | bytes 25165828
  0.0 19.2 %copy-start.1 = (bf16[1,4096,1024]{2,1,0:T(8,128)(2,1)S(1)}, bf16[1,4096,1024]{2,1,0:T(8,128)(2,1)}, u32[]{:S(2)}) copy-start(bf16[1,4096,1024]{2,1,0:T(8,128)(2,1)} %param.10) | copy-start | bytes 25165828
  1.0 7.0 %collective-permute-start.2 = (bf16[4,4224]{1,0:T(4,128)(2,1)S(1)}, bf16[4,4224]{1,0:T(4,128)(2,1)S(1)}, u32[]{:S(2)}, u32[]{:S(2)}) collective-permute-start(bf16[4,4224]{1,0:T(4,128)(2,1)S(1)} %pack_block.1.refs_0_), channel_id=1, source_target_pairs={{0,12},{1,13},{2,14},{3,15},{4,8},{5,9},{6,10},{7,11},{8,4},{9,5},... | collective-permute-start | bytes 101384 | tf_op jit(solution)/shard_map/ppermute | solution.py:22
  6.1 4.8 %collective-permute-start.1 = (bf16[4,4224]{1,0:T(4,128)(2,1)S(1)}, bf16[4,4224]{1,0:T(4,128)(2,1)S(1)}, u32[]{:S(2)}, u32[]{:S(2)}) collective-permute-start(bf16[4,4224]{1,0:T(4,128)(2,1)S(1)} %pack_block.1.refs_0_), channel_id=1, source_target_pairs={{0,8},{1,9},{2,10},{3,11},{4,12},{5,13},{6,14},{7,15},{8,0},{9,1},... | collective-permute-start | bytes 101384 | tf_op jit(solution)/shard_map/ppermute | solution.py:22
  6.1 4.8 %collective-permute-start = (bf16[4,4224]{1,0:T(4,128)(2,1)S(1)}, bf16[4,4224]{1,0:T(4,128)(2,1)S(1)}, u32[]{:S(2)}, u32[]{:S(2)}) collective-permute-start(bf16[4,4224]{1,0:T(4,128)(2,1)S(1)} %pack_block.1.refs_0_), channel_id=1, source_target_pairs={{0,4},{1,5},{2,6},{3,7},{4,0},{5,1},{6,2},{7,3},{8,12},{9,13},{10,... | collective-permute-start | bytes 101384 | tf_op jit(solution)/shard_map/ppermute | solution.py:22
  11.0 6.4 %collective-permute-start.5 = (bf16[16,4224]{1,0:T(8,128)(2,1)S(1)}, bf16[16,4224]{1,0:T(8,128)(2,1)S(1)}, u32[]{:S(2)}, u32[]{:S(2)}) collective-permute-start(bf16[16,4224]{1,0:T(8,128)(2,1)S(1)} %stack_blocks.1), channel_id=1, source_target_pairs={{0,18},{1,19},{2,16},{3,17},{4,22},{5,23},{6,20},{7,21},{8,26},{9,... | collective-permute-start | bytes 405512 | tf_op jit(solution)/shard_map/ppermute | solution.py:22
  13.5 5.3 %collective-permute-start.4 = (bf16[16,4224]{1,0:T(8,128)(2,1)S(1)}, bf16[16,4224]{1,0:T(8,128)(2,1)S(1)}, u32[]{:S(2)}, u32[]{:S(2)}) collective-permute-start(bf16[16,4224]{1,0:T(8,128)(2,1)S(1)} %stack_blocks.1), channel_id=1, source_target_pairs={{0,16},{1,17},{2,18},{3,19},{4,20},{5,21},{6,22},{7,23},{8,24},{9,... | collective-permute-start | bytes 405512 | tf_op jit(solution)/shard_map/ppermute | solution.py:22
  14.1 5.0 %collective-permute-start.3 = (bf16[16,4224]{1,0:T(8,128)(2,1)S(1)}, bf16[16,4224]{1,0:T(8,128)(2,1)S(1)}, u32[]{:S(2)}, u32[]{:S(2)}) collective-permute-start(bf16[16,4224]{1,0:T(8,128)(2,1)S(1)} %stack_blocks.1), channel_id=1, source_target_pairs={{0,2},{1,3},{2,0},{3,1},{4,6},{5,7},{6,4},{7,5},{8,10},{9,11},{10,... | collective-permute-start | bytes 405512 | tf_op jit(solution)/shard_map/ppermute | solution.py:22
  19.1 3.2 %collective-permute-start.6 = (bf16[64,4224]{1,0:T(8,128)(2,1)S(1)}, bf16[64,4224]{1,0:T(8,128)(2,1)S(1)}, u32[]{:S(2)}, u32[]{:S(2)}) collective-permute-start(bf16[64,4224]{1,0:T(8,128)(2,1)S(1)} %pad_maximum_fusion.rows_ref), channel_id=1, source_target_pairs={{0,1},{1,0},{2,3},{3,2},{4,5},{5,4},{6,7},{7,6},{8,9},{9,8},{10,11... | collective-permute-start | bytes 1622024 | tf_op jit(solution)/shard_map/ppermute | solution.py:22
  19.2 8.4 %slice-start = ((s8[8388608]{0:T(1024)(128)(4,1)}), s8[4194304]{0:T(1024)(128)(4,1)S(1)}, s32[]{:S(2)}) async-start(s8[8388608]{0:T(1024)(128)(4,1)} %bitcast.15), calls=%async_computation.1 | async-start | bytes 8388608
  22.3 5.3 %slice-start.1 = ((s8[8388608]{0:T(1024)(128)(4,1)}), s8[4194304]{0:T(1024)(128)(4,1)S(1)}, s32[]{:S(2)}) async-start(s8[8388608]{0:T(1024)(128)(4,1)} %bitcast.15), calls=%async_computation.2 | async-start | bytes 8388608
  22.4 6.0 %collective-permute-start.7 = (bf16[64,1024]{1,0:T(8,128)(2,1)S(1)}, bf16[64,1024]{1,0:T(8,128)(2,1)S(1)}, u32[]{:S(2)}, u32[]{:S(2)}) collective-permute-start(bf16[64,1024]{1,0:T(8,128)(2,1)S(1)} %expand_rows.2.first_ref), channel_id=1, source_target_pairs={{0,16},{1,17},{2,18},{3,19},{4,20},{5,21},{6,22},{7,23},{8,24},{9,... | collective-permute-start | bytes 393224 | tf_op jit(solution)/shard_map/ppermute | solution.py:22
  27.0 5.7 %collective-permute-start.8 = (bf16[64,1024]{1,0:T(8,128)(2,1)S(1)}, bf16[64,1024]{1,0:T(8,128)(2,1)S(1)}, u32[]{:S(2)}, u32[]{:S(2)}) collective-permute-start(bf16[64,1024]{1,0:T(8,128)(2,1)S(1)} %expand_rows.3.second_ref), channel_id=1, source_target_pairs={{0,16},{1,17},{2,18},{3,19},{4,20},{5,21},{6,22},{7,23},{8,24},{9,... | collective-permute-start | bytes 393224 | tf_op jit(solution)/shard_map/ppermute | solution.py:22
  33.6 1.6 %collective-permute-start.9 = (bf16[64,2048]{1,0:T(8,128)(2,1)S(1)}, bf16[64,2048]{1,0:T(8,128)(2,1)S(1)}, u32[]{:S(2)}, u32[]{:S(2)}) collective-permute-start(bf16[64,2048]{1,0:T(8,128)(2,1)S(1)} %contract_others.3), channel_id=1, source_target_pairs={{0,1},{1,0},{2,3},{3,2},{4,5},{5,4},{6,7},{7,6},{8,9},{9,8},{10,11... | collective-permute-start | bytes 786440 | tf_op jit(solution)/shard_map/ppermute | solution.py:22

commit v9 on v7

--- a/solution.py
+++ b/solution.py
@@ -65,27 +65,56 @@
         out_shape=jax.ShapeDtypeStruct((count, width + LANES), tokens.dtype),
         in_specs=[pl.BlockSpec(memory_space=pltpu.VMEM)] * 3,
         out_specs=pl.BlockSpec(memory_space=pltpu.VMEM),
-        cost_estimate=pl.CostEstimate(flops=20 * 10**9, bytes_accessed=0, transcendentals=0),
+        cost_estimate=pl.CostEstimate(flops=60 * 10**9, bytes_accessed=0, transcendentals=0),
         compiler_params=pltpu.CompilerParams(vmem_limit_bytes=1 << 20),
         name="pack_block",
     )(in_hbm(tokens), in_hbm(expert_ids), in_hbm(gate_probs))
 
 
 def stack_blocks(blocks):
-    count, width = blocks[0].shape
-
     def body(*refs):
-        values = [ref[...].astype(jnp.float32) for ref in refs[:-1]]
-        refs[-1][...] = jnp.concatenate(values).astype(refs[-1].dtype)
-
-    return pl.pallas_call(
-        body,
-        out_shape=jax.ShapeDtypeStruct((len(blocks) * count, width), blocks[0].dtype),
-        in_specs=[pl.BlockSpec(memory_space=pltpu.VMEM)] * len(blocks),
-        out_specs=pl.BlockSpec(memory_space=pltpu.VMEM),
+        for i, ref in enumerate(refs[:-2]):
+            refs[-2][i] = ref[...]
+            if i:
+                refs[-1][i - 1] = ref[...]
+
+    count, shape, dtype = len(blocks), blocks[0].shape, blocks[0].dtype
+    return pl.pallas_call(
+        body,
+        out_shape=[jax.ShapeDtypeStruct((n,) + shape, dtype) for n in (count, count - 1)],
+        in_specs=[pl.BlockSpec(memory_space=pltpu.VMEM)] * count,
+        out_specs=[pl.BlockSpec(memory_space=pltpu.VMEM)] * 2,
         compiler_params=pltpu.CompilerParams(vmem_limit_bytes=4 << 20),
         name="stack_blocks",
     )(*blocks)
+
+
+def join_rows(stacks):
+    _, tokens, width = stacks[0].shape
+    total = sum(1 if stack.ndim == 2 else stack.shape[0] for stack in stacks)
+    batch = max(1, 16 // tokens)
+
+    def body(*refs):
+        group, start = [], 0
+        for ref, stack in zip(refs, stacks):
+            for i in range(1 if stack.ndim == 2 else stack.shape[0]):
+                value = ref[...] if stack.ndim == 2 else ref[i]
+                group.append(value.astype(jnp.float32))
+                if len(group) == batch:
+                    rows = jnp.concatenate(group).astype(refs[-1].dtype)
+                    refs[-1][start : start + batch * tokens, :] = rows
+                    group, start = [], start + batch * tokens
+
+    return pl.pallas_call(
+        body,
+        out_shape=jax.ShapeDtypeStruct((total * tokens, width), stacks[0].dtype),
+        in_specs=[pl.BlockSpec(memory_space=pltpu.VMEM)] * len(stacks),
+        out_specs=pl.BlockSpec(memory_space=pltpu.VMEM),
+        compiler_params=pltpu.CompilerParams(
+            vmem_limit_bytes=5 * total * tokens * width + (4 << 20)
+        ),
+        name="join_rows",
+    )(*stacks)
 
 
 def expand_rows(rows, w_gate, w_up, start, columns):
@@ -115,8 +144,12 @@
     )(rows, in_vmem(w_gate), in_vmem(w_up))
 
 
-def contract_hidden(parts, w_down, units, before=None, rows=None, half=None):
-    count, width = parts[0][0].shape[0], w_down.shape[1]
+def contract_hidden(
+    parts, w_down, units, before=None, rows=None, half=None, index=None, kind=jnp.float32
+):
+    total_count, width = parts[0][0].shape[0], w_down.shape[1]
+    count = total_count if index is None else total_count // 2
+    offset = 0 if index is None else index * count
     experts = lax.axis_size(EXPERT)
     operands = [part for part, _, _ in parts] + [in_vmem(w_down)]
     operands += [value for value in (before, rows) if value is not None]
@@ -129,7 +162,7 @@
         me, group = lax.axis_index(EXPERT), lax.axis_index("dp")
 
         def step(first, batch):
-            here = pl.ds(first, batch)
+            here = pl.ds(offset + first, batch)
             lefts = [ref[here, :] for ref in part_refs]
             if half is not None:
                 order = [i ^ 1 for i in range(count // half)]
@@ -152,18 +185,18 @@
                     total = total + jnp.dot(left, right, preferred_element_type=jnp.float32)
                 if rows is not None:
                     total = total.astype(jnp.bfloat16).astype(jnp.float32) * scale
-                refs[-1][here, cut] = total
+                refs[-1][pl.ds(first, batch), cut] = total.astype(kind)
 
         row_batches(count, step)
 
     return pl.pallas_call(
         body,
-        out_shape=jax.ShapeDtypeStruct((count, width), jnp.float32),
+        out_shape=jax.ShapeDtypeStruct((count, width), kind),
         in_specs=[pl.BlockSpec(memory_space=pltpu.VMEM)] * len(operands),
         out_specs=pl.BlockSpec(memory_space=pltpu.VMEM),
         cost_estimate=pl.CostEstimate(flops=0, bytes_accessed=count * width, transcendentals=0),
         compiler_params=pltpu.CompilerParams(
-            vmem_limit_bytes=8 * count * width
+            vmem_limit_bytes=8 * total_count * width
             + (6 << 20)
             + (0 if rows is None else rows.nbytes)
         ),
@@ -204,11 +237,14 @@
     units = w_up.shape[2]
     weights = lax.optimization_barrier((block, w_gate[0], w_up[0], w_down[0]))
     block, gate_weights, up_weights, down_weights = weights
-    near = stack_blocks([block] + [swap(block, 0, 4 * i) for i in range(1, high)])
+    near = [block] + [swap(block, 0, 4 * i) for i in range(1, high)]
+    early = swap(block, 1, 2)
+    near[-1], early = lax.optimization_barrier((near[-1], early))
+    near, rest = stack_blocks(near)
     if wide > 1:
         near = jnp.concatenate([near] + [swap(near, 2 * i, 0) for i in range(1, wide)])
-    chip = [near, swap(near, 0, 2), swap(near, 1, 0), swap(near, 1, 2)]
-    chip = jnp.concatenate(chip)
+        rest = near[1:]
+    chip = join_rows([near, swap(near, 0, 2), swap(near, 1, 0), early, swap(rest, 1, 2)])
     rows = jnp.concatenate([chip, swap(chip, 0, 1)])
 
     chunks = CHUNKS if units % (LANES * CHUNKS) == 0 else 1
@@ -224,21 +260,25 @@
         value = jnp.stack([value[:, :, :, i ^ (mask >> 1)] for i in range(wide)], axis=3)
         return value.reshape(-1, step)
 
-    total, others = None, [[] for _ in range(chunks)]
+    hidden, others = [], []
     for i in range(chunks):
-        if total is not None:
-            rows, total = lax.optimization_barrier((rows, total))
-        hidden = expand_rows(rows, gate_weights, up_weights, i * step, step)
-        for mask in range(1, groups):
-            others[i].append((from_group(hidden, mask), mask, i * step))
-        total = contract_hidden([(hidden, 0, i * step)], down_weights, units, total)
-    for i in range(chunks):
-        weigh = rows if i == chunks - 1 else None
-        total = contract_hidden(others[i], down_weights, units, total, weigh, half)
-
-    count, columns = rows.shape[0] // 2, w_down.shape[2]
-    received = swap(total[count:].astype(jnp.bfloat16), 0, 1)
-    blocks = add_and_order(total, received, wide, high)
+        if hidden:
+            rows, hidden[-1] = lax.optimization_barrier((rows, hidden[-1]))
+        hidden.append(expand_rows(rows, gate_weights, up_weights, i * step, step))
+        others.append(
+            [(from_group(hidden[-1], mask), mask, i * step) for mask in range(1, groups)]
+        )
+    parts = [(value, 0, i * step) for i, value in enumerate(hidden)]
+    total = contract_hidden(parts, down_weights, units)
+    for i in range(chunks - 1):
+        total = contract_hidden(others[i], down_weights, units, total, half=half)
+    last = lambda index, kind: contract_hidden(
+        others[-1], down_weights, units, total, rows, half, index, kind
+    )
+    sent, kept = last(1, jnp.bfloat16), last(0, jnp.float32)
+
+    columns = w_down.shape[2]
+    blocks = add_and_order(kept, swap(sent, 0, 1), wide, high)
     blocks = lax.all_to_all(blocks, ("dp", "far"), split_axis=0, concat_axis=0, tiled=True)
     blocks = blocks.reshape(groups, -1, token_count, columns).astype(jnp.float32)
     combined = jnp.sum(blocks, axis=1).astype(jnp.bfloat16)

time: 50.2 us -> 50.5 us (level)
  starting transfers between devices: 12.5 us -> 14.2 us
  waiting for transfers between devices: 15.2 us -> 13.8 us
  local copies, waits for them, and re-layouts: 0.59 us -> 0.02 us
    ppermute x10 -> x11, starting transfers between devices: 12.5 us -> 14.2 us  [swap(): return lax.ppermute(value, ('dp',) + EXPERT, pairs)]
    ppermute x10 -> x11, waiting for transfers between devices: 15.2 us -> 13.8 us  [swap(): return lax.ppermute(value, ('dp',) + EXPERT, pairs)]
    pallas_call x5 -> x6, Pallas kernels: 1.88 us -> 2.31 us  [the longest x4 2.16 us: contract_hidden(): pl.pallas_call(body, out_shape=jax.ShapeDtypeStruct((count, width), kind)...]
  transfers between devices with their start and end apart: 10 -> 11, of which waited for: 8 -> 7; matrix products, arithmetic and copies ran while one was open for 0% -> 0% of each run, Pallas kernels for 6% -> 6%
where the time goes in v9:
time: 50.5 us; the launch traced here: 50.4 us
  blocking collectives  15.2 us (30%)
  starting transfers between devices  14.2 us (28%)
  waiting for transfers between devices  13.8 us (27%)
  Pallas kernels  6.22 us (12%)
  other arithmetic  0.8 us (2%)
    all_to_all x1, blocking collectives, local(): lax.all_to_all(blocks, ('dp', 'far'), split_axis=0, concat_axis=0, tiled=...  15.2 us
    ppermute x11, starting transfers between devices, swap(): return lax.ppermute(value, ('dp',) + EXPERT, pairs)  14.2 us
    ppermute x11, waiting for transfers between devices, swap(): return lax.ppermute(value, ('dp',) + EXPERT, pairs)  13.8 us
    pallas_call x2, Pallas kernels, expand_rows(): pl.pallas_call(body, out_shape=jax.ShapeDtypeStruct((count, columns), row...  2.78 us
    pallas_call x4, Pallas kernels, contract_hidden(): pl.pallas_call(body, out_shape=jax.ShapeDtypeStruct((count, width), kind)...  2.16 us
    pallas_call x1, Pallas kernels, pack_block(): pl.pallas_call(body, out_shape=jax.ShapeDtypeStruct((count, width + LANES...  1.02 us
  transfers between devices with their start and end apart: 11, of which 7 were waited for; matrix products, arithmetic and copies ran while one was open for 0% of the time, Pallas kernels for 6%

profile of v9, /device:TPU:0, one launch (start us, length us, event | category | flops | bytes accessed | tf_op | source)
XLA Modules:
  0.0 50.4 jit_solution(4948982774865583987)
XLA Ops:
  0.0 0.0 copy-start
  0.0 0.0 copy-start.1
  0.0 1.0 %pack_block.1.refs_0_ = bf16[4,4224]{1,0:T(4,128)(2,1)S(1)} custom-call(bf16[4,4096]{1,0:T(4,128)(2,1)} %tokens_ref.1, s32[4,8]{1,0:T(4,128)} %ids_ref.1, f32[4,8]{1,0:T(4,128)} %probs_ref.1), custom_call_target="tpu_custom_call" | custom-call | flops 60000002048 | tf_op jit(solution)/shard_map/pack_block/pallas_call | solution.py:63
  1.0 4.0 %collective-permute-start.3 = (bf16[4,4224]{1,0:T(4,128)(2,1)S(1)}, bf16[4,4224]{1,0:T(4,128)(2,1)S(1)}, u32[]{:S(2)}, u32[]{:S(2)}) collective-permute-start(bf16[4,4224]{1,0:T(4,128)(2,1)S(1)} %pack_block.1.refs_0_), channel_id=1, source_target_pairs={{0,18},{1,19},{2,16},{3,17},{4,22},{5,23},{6,20},{7,21},{8,26},{9,... | collective-permute-start | bytes 101384 | tf_op jit(solution)/shard_map/ppermute | solution.py:23
  5.0 3.6 %collective-permute-start.2 = (bf16[4,4224]{1,0:T(4,128)(2,1)S(1)}, bf16[4,4224]{1,0:T(4,128)(2,1)S(1)}, u32[]{:S(2)}, u32[]{:S(2)}) collective-permute-start(bf16[4,4224]{1,0:T(4,128)(2,1)S(1)} %pack_block.1.refs_0_), channel_id=1, source_target_pairs={{0,12},{1,13},{2,14},{3,15},{4,8},{5,9},{6,10},{7,11},{8,4},{9,5},... | collective-permute-start | bytes 101384 | tf_op jit(solution)/shard_map/ppermute | solution.py:23
  8.6 0.0 collective-permute-start.1
  8.6 0.8 %collective-permute-start = (bf16[4,4224]{1,0:T(4,128)(2,1)S(1)}, bf16[4,4224]{1,0:T(4,128)(2,1)S(1)}, u32[]{:S(2)}, u32[]{:S(2)}) collective-permute-start(bf16[4,4224]{1,0:T(4,128)(2,1)S(1)} %pack_block.1.refs_0_), channel_id=1, source_target_pairs={{0,4},{1,5},{2,6},{3,7},{4,0},{5,1},{6,2},{7,3},{8,12},{9,13},{10,... | collective-permute-start | bytes 101384 | tf_op jit(solution)/shard_map/ppermute | solution.py:23
  9.4 0.0 collective-permute-done.3.refs_3_
  9.4 1.7 %collective-permute-done.2.refs_3_ = bf16[4,4224]{1,0:T(4,128)(2,1)S(1)} collective-permute-done((bf16[4,4224]{1,0:T(4,128)(2,1)S(1)}, bf16[4,4224]{1,0:T(4,128)(2,1)S(1)}, u32[]{:S(2)}, u32[]{:S(2)}) %collective-permute-start.2) | collective-permute-done | bytes 33824 | tf_op jit(solution)/shard_map/ppermute | solution.py:23
  11.1 2.3 %collective-permute-done.1.refs_2_ = bf16[4,4224]{1,0:T(4,128)(2,1)S(1)} collective-permute-done((bf16[4,4224]{1,0:T(4,128)(2,1)S(1)}, bf16[4,4224]{1,0:T(4,128)(2,1)S(1)}, u32[]{:S(2)}, u32[]{:S(2)}) %collective-permute-start.1) | collective-permute-done | bytes 33824 | tf_op jit(solution)/shard_map/ppermute | solution.py:23
  13.4 0.0 collective-permute-done.refs_1_
  13.4 0.6 %collective-permute-start.5 = (bf16[4,4,4224]{2,1,0:T(4,128)(2,1)S(1)}, bf16[4,4,4224]{2,1,0:T(4,128)(2,1)S(1)}, u32[]{:S(2)}, u32[]{:S(2)}) collective-permute-start(bf16[4,4,4224]{2,1,0:T(4,128)(2,1)S(1)} %get-tuple-element.17.refs_0_), channel_id=1, source_target_pairs={{0,16},{1,17},{2,18},{3,19},{4,20},{5,21},{6,22},{7,23},{8,24},{9,... | collective-permute-start | bytes 405512 | tf_op jit(solution)/shard_map/ppermute | solution.py:23
  14.0 0.5 %collective-permute-start.4 = (bf16[4,4,4224]{2,1,0:T(4,128)(2,1)S(1)}, bf16[4,4,4224]{2,1,0:T(4,128)(2,1)S(1)}, u32[]{:S(2)}, u32[]{:S(2)}) collective-permute-start(bf16[4,4,4224]{2,1,0:T(4,128)(2,1)S(1)} %get-tuple-element.17.refs_0_), channel_id=1, source_target_pairs={{0,2},{1,3},{2,0},{3,1},{4,6},{5,7},{6,4},{7,5},{8,10},{9,11},{10,... | collective-permute-start | bytes 405512 | tf_op jit(solution)/shard_map/ppermute | solution.py:23
  14.5 2.4 %collective-permute-start.6 = (bf16[3,4,4224]{2,1,0:T(4,128)(2,1)S(1)}, bf16[3,4,4224]{2,1,0:T(4,128)(2,1)S(1)}, u32[]{:S(2)}, u32[]{:S(2)}) collective-permute-start(bf16[3,4,4224]{2,1,0:T(4,128)(2,1)S(1)} %get-tuple-element.19), channel_id=1, source_target_pairs={{0,18},{1,19},{2,16},{3,17},{4,22},{5,23},{6,20},{7,21},{8,26},{9,... | collective-permute-start | bytes 304136 | tf_op jit(solution)/shard_map/ppermute | solution.py:23
  17.0 3.1 %collective-permute-done.6.refs_4_ = bf16[3,4,4224]{2,1,0:T(4,128)(2,1)S(1)} collective-permute-done((bf16[3,4,4224]{2,1,0:T(4,128)(2,1)S(1)}, bf16[3,4,4224]{2,1,0:T(4,128)(2,1)S(1)}, u32[]{:S(2)}, u32[]{:S(2)}) %collective-permute-start.6) | collective-permute-done | bytes 101408 | tf_op jit(solution)/shard_map/ppermute | solution.py:23
  20.1 0.0 collective-permute-done.5.refs_2_
  20.1 0.0 collective-permute-done.4.refs_1_
  20.1 0.1 join_rows.1
  20.3 0.1 collective-permute-start.7
  20.4 1.9 %collective-permute-done.7 = bf16[64,4224]{1,0:T(8,128)(2,1)S(1)} collective-permute-done((bf16[64,4224]{1,0:T(8,128)(2,1)S(1)}, bf16[64,4224]{1,0:T(8,128)(2,1)S(1)}, u32[]{:S(2)}, u32[]{:S(2)}) %collective-permute-start.7) | collective-permute-done | bytes 540704 | tf_op jit(solution)/shard_map/ppermute | solution.py:23
  22.3 0.1 pad_maximum_fusion.rows_ref.refs_3_
  22.4 0.0 copy-done
  22.4 0.0 copy-done.1
  22.4 0.0 slice-start
  22.4 1.4 %expand_rows.2.refs_0_ = bf16[128,512]{1,0:T(8,128)(2,1)S(1)} custom-call(bf16[128,4224]{1,0:T(8,128)(2,1)S(1)} %pad_maximum_fusion.rows_ref.refs_3_, bf16[4096,1024]{1,0:T(8,128)(2,1)S(1)} %bitcast.14, bf16[4096,1024]{1,0:T(8,128)(2,1)S(1)} %bitcast.16), custom_call_target="tpu_custom_call" | custom-call | bytes 65536 | tf_op jit(solution)/shard_map/expand_rows/pallas_call | solution.py:136
  23.8 0.0 slice-start.1
  23.8 1.5 %collective-permute-start.9 = (bf16[128,512]{1,0:T(8,128)(2,1)S(1)}, bf16[128,512]{1,0:T(8,128)(2,1)S(1)}, u32[]{:S(2)}, u32[]{:S(2)}) collective-permute-start(bf16[128,512]{1,0:T(8,128)(2,1)S(1)} %expand_rows.2.refs_0_), channel_id=1, source_target_pairs={{0,16},{1,17},{2,18},{3,19},{4,20},{5,21},{6,22},{7,23},{8,24},{9,... | collective-permute-start | bytes 393224 | tf_op jit(solution)/shard_map/ppermute | solution.py:23
  25.3 1.4 %expand_rows.3.refs_1_ = bf16[128,512]{1,0:T(8,128)(2,1)S(1)} custom-call(bf16[128,4224]{1,0:T(8,128)(2,1)S(1)} %pad_maximum_fusion.rows_ref.refs_3_, bf16[4096,1024]{1,0:T(8,128)(2,1)S(1)} %bitcast.15, bf16[4096,1024]{1,0:T(8,128)(2,1)S(1)} %bitcast.17), custom_call_target="tpu_custom_call" | custom-call | bytes 65536 | tf_op jit(solution)/shard_map/expand_rows/pallas_call | solution.py:136
  26.7 0.6 %collective-permute-start.8 = (bf16[128,512]{1,0:T(8,128)(2,1)S(1)}, bf16[128,512]{1,0:T(8,128)(2,1)S(1)}, u32[]{:S(2)}, u32[]{:S(2)}) collective-permute-start(bf16[128,512]{1,0:T(8,128)(2,1)S(1)} %expand_rows.3.refs_1_), channel_id=1, source_target_pairs={{0,16},{1,17},{2,18},{3,19},{4,20},{5,21},{6,22},{7,23},{8,24},{9,... | collective-permute-start | bytes 393224 | tf_op jit(solution)/shard_map/ppermute | solution.py:23
  27.4 0.0 slice-done
  27.4 0.0 slice-done.1
  27.4 0.7 %contract_hidden.4.refs_2_ = f32[128,2048]{1,0:T(8,128)S(1)} custom-call(bf16[128,512]{1,0:T(8,128)(2,1)S(1)} %expand_rows.2.refs_0_, bf16[128,512]{1,0:T(8,128)(2,1)S(1)} %expand_rows.3.refs_1_, bf16[2048,2048]{1,0:T(8,128)(2,1)S(1)} %bitcast.10), custom_call_target="tpu_custom_call" | custom-call | bytes 262144 | tf_op jit(solution)/shard_map/contract_hidden/pallas_call | solution.py:192
  28.1 1.4 %collective-permute-done.9.refs_0_ = bf16[128,512]{1,0:T(8,128)(2,1)S(1)} collective-permute-done((bf16[128,512]{1,0:T(8,128)(2,1)S(1)}, bf16[128,512]{1,0:T(8,128)(2,1)S(1)}, u32[]{:S(2)}, u32[]{:S(2)}) %collective-permute-start.9) | collective-permute-done | bytes 131104 | tf_op jit(solution)/shard_map/ppermute | solution.py:23
  29.5 0.5 contract_hidden.5.refs_2_
  29.9 2.3 %collective-permute-done.8.refs_0_ = bf16[128,512]{1,0:T(8,128)(2,1)S(1)} collective-permute-done((bf16[128,512]{1,0:T(8,128)(2,1)S(1)}, bf16[128,512]{1,0:T(8,128)(2,1)S(1)}, u32[]{:S(2)}, u32[]{:S(2)}) %collective-permute-start.8) | collective-permute-done | bytes 131104 | tf_op jit(solution)/shard_map/ppermute | solution.py:23
  32.2 0.5 contract_hidden.7
  32.7 0.1 collective-permute-start.10
  32.8 0.5 contract_hidden.6.total_ref
  33.3 1.0 %collective-permute-done.10.received_ref = bf16[64,2048]{1,0:T(8,128)(2,1)S(1)} collective-permute-done((bf16[64,2048]{1,0:T(8,128)(2,1)S(1)}, bf16[64,2048]{1,0:T(8,128)(2,1)S(1)}, u32[]{:S(2)}, u32[]{:S(2)}) %collective-permute-start.10) | collective-permute-done | bytes 262176 | tf_op jit(solution)/shard_map/ppermute | solution.py:23
  34.3 0.1 add_and_order.1
  34.4 15.2 %all_to_all.5 = bf16[16,4,2048]{2,1,0:T(4,128)(2,1)S(1)} all-to-all(bf16[16,4,2048]{2,1,0:T(4,128)(2,1)S(1)} %add_and_order.1), channel_id=1, replica_groups=mesh['dp'=2,'far'=8,'core'=2] {'dp','far'}, dimensions={0} | all-to-all | bytes 524288 | tf_op jit(solution)/shard_map/all_to_all | solution.py:282
  49.6 0.7 %bitcast_reduce_fusion = bf16[2,4,2048]{2,1,0:T(4,128)(2,1)} fusion(bf16[16,4,2048]{2,1,0:T(4,128)(2,1)S(1)} %all_to_all.5), kind=kLoop, calls=%fused_computation.1 | loop fusion | flops 114688 | bytes 294912 | tf_op jit(solution)/shard_map/reduce_sum | solution.py:284
  (2 shorter events, 0.0 us)
Async XLA Ops:
  0.0 22.4 %copy-start = (bf16[1,4096,1024]{2,1,0:T(8,128)(2,1)S(1)}, bf16[1,4096,1024]{2,1,0:T(8,128)(2,1)}, u32[]{:S(2)}) copy-start(bf16[1,4096,1024]{2,1,0:T(8,128)(2,1)} %param.9) | copy-start | bytes 25165828
  0.0 22.4 %copy-start.1 = (bf16[1,4096,1024]{2,1,0:T(8,128)(2,1)S(1)}, bf16[1,4096,1024]{2,1,0:T(8,128)(2,1)}, u32[]{:S(2)}) copy-start(bf16[1,4096,1024]{2,1,0:T(8,128)(2,1)} %param.10) | copy-start | bytes 25165828
  1.0 8.4 %collective-permute-start.3 = (bf16[4,4224]{1,0:T(4,128)(2,1)S(1)}, bf16[4,4224]{1,0:T(4,128)(2,1)S(1)}, u32[]{:S(2)}, u32[]{:S(2)}) collective-permute-start(bf16[4,4224]{1,0:T(4,128)(2,1)S(1)} %pack_block.1.refs_0_), channel_id=1, source_target_pairs={{0,18},{1,19},{2,16},{3,17},{4,22},{5,23},{6,20},{7,21},{8,26},{9,... | collective-permute-start | bytes 101384 | tf_op jit(solution)/shard_map/ppermute | solution.py:23
  5.0 6.1 %collective-permute-start.2 = (bf16[4,4224]{1,0:T(4,128)(2,1)S(1)}, bf16[4,4224]{1,0:T(4,128)(2,1)S(1)}, u32[]{:S(2)}, u32[]{:S(2)}) collective-permute-start(bf16[4,4224]{1,0:T(4,128)(2,1)S(1)} %pack_block.1.refs_0_), channel_id=1, source_target_pairs={{0,12},{1,13},{2,14},{3,15},{4,8},{5,9},{6,10},{7,11},{8,4},{9,5},... | collective-permute-start | bytes 101384 | tf_op jit(solution)/shard_map/ppermute | solution.py:23
  8.6 4.8 %collective-permute-start.1 = (bf16[4,4224]{1,0:T(4,128)(2,1)S(1)}, bf16[4,4224]{1,0:T(4,128)(2,1)S(1)}, u32[]{:S(2)}, u32[]{:S(2)}) collective-permute-start(bf16[4,4224]{1,0:T(4,128)(2,1)S(1)} %pack_block.1.refs_0_), channel_id=1, source_target_pairs={{0,8},{1,9},{2,10},{3,11},{4,12},{5,13},{6,14},{7,15},{8,0},{9,1},... | collective-permute-start | bytes 101384 | tf_op jit(solution)/shard_map/ppermute | solution.py:23
  8.6 4.8 %collective-permute-start = (bf16[4,4224]{1,0:T(4,128)(2,1)S(1)}, bf16[4,4224]{1,0:T(4,128)(2,1)S(1)}, u32[]{:S(2)}, u32[]{:S(2)}) collective-permute-start(bf16[4,4224]{1,0:T(4,128)(2,1)S(1)} %pack_block.1.refs_0_), channel_id=1, source_target_pairs={{0,4},{1,5},{2,6},{3,7},{4,0},{5,1},{6,2},{7,3},{8,12},{9,13},{10,... | collective-permute-start | bytes 101384 | tf_op jit(solution)/shard_map/ppermute | solution.py:23
  13.4 6.7 %collective-permute-start.5 = (bf16[4,4,4224]{2,1,0:T(4,128)(2,1)S(1)}, bf16[4,4,4224]{2,1,0:T(4,128)(2,1)S(1)}, u32[]{:S(2)}, u32[]{:S(2)}) collective-permute-start(bf16[4,4,4224]{2,1,0:T(4,128)(2,1)S(1)} %get-tuple-element.17.refs_0_), channel_id=1, source_target_pairs={{0,16},{1,17},{2,18},{3,19},{4,20},{5,21},{6,22},{7,23},{8,24},{9,... | collective-permute-start | bytes 405512 | tf_op jit(solution)/shard_map/ppermute | solution.py:23
  14.0 6.1 %collective-permute-start.4 = (bf16[4,4,4224]{2,1,0:T(4,128)(2,1)S(1)}, bf16[4,4,4224]{2,1,0:T(4,128)(2,1)S(1)}, u32[]{:S(2)}, u32[]{:S(2)}) collective-permute-start(bf16[4,4,4224]{2,1,0:T(4,128)(2,1)S(1)} %get-tuple-element.17.refs_0_), channel_id=1, source_target_pairs={{0,2},{1,3},{2,0},{3,1},{4,6},{5,7},{6,4},{7,5},{8,10},{9,11},{10,... | collective-permute-start | bytes 405512 | tf_op jit(solution)/shard_map/ppermute | solution.py:23
  14.5 5.6 %collective-permute-start.6 = (bf16[3,4,4224]{2,1,0:T(4,128)(2,1)S(1)}, bf16[3,4,4224]{2,1,0:T(4,128)(2,1)S(1)}, u32[]{:S(2)}, u32[]{:S(2)}) collective-permute-start(bf16[3,4,4224]{2,1,0:T(4,128)(2,1)S(1)} %get-tuple-element.19), channel_id=1, source_target_pairs={{0,18},{1,19},{2,16},{3,17},{4,22},{5,23},{6,20},{7,21},{8,26},{9,... | collective-permute-start | bytes 304136 | tf_op jit(solution)/shard_map/ppermute | solution.py:23
  20.3 2.0 %collective-permute-start.7 = (bf16[64,4224]{1,0:T(8,128)(2,1)S(1)}, bf16[64,4224]{1,0:T(8,128)(2,1)S(1)}, u32[]{:S(2)}, u32[]{:S(2)}) collective-permute-start(bf16[64,4224]{1,0:T(8,128)(2,1)S(1)} %join_rows.1), channel_id=1, source_target_pairs={{0,1},{1,0},{2,3},{3,2},{4,5},{5,4},{6,7},{7,6},{8,9},{9,8},{10,11... | collective-permute-start | bytes 1622024 | tf_op jit(solution)/shard_map/ppermute | solution.py:23
  22.4 5.0 %slice-start = ((s8[8388608]{0:T(1024)(128)(4,1)}), s8[4194304]{0:T(1024)(128)(4,1)S(1)}, s32[]{:S(2)}) async-start(s8[8388608]{0:T(1024)(128)(4,1)} %bitcast.8), calls=%async_computation.1 | async-start | bytes 8388608
  23.8 3.6 %slice-start.1 = ((s8[8388608]{0:T(1024)(128)(4,1)}), s8[4194304]{0:T(1024)(128)(4,1)S(1)}, s32[]{:S(2)}) async-start(s8[8388608]{0:T(1024)(128)(4,1)} %bitcast.8), calls=%async_computation.2 | async-start | bytes 8388608
  23.8 5.7 %collective-permute-start.9 = (bf16[128,512]{1,0:T(8,128)(2,1)S(1)}, bf16[128,512]{1,0:T(8,128)(2,1)S(1)}, u32[]{:S(2)}, u32[]{:S(2)}) collective-permute-start(bf16[128,512]{1,0:T(8,128)(2,1)S(1)} %expand_rows.2.refs_0_), channel_id=1, source_target_pairs={{0,16},{1,17},{2,18},{3,19},{4,20},{5,21},{6,22},{7,23},{8,24},{9,... | collective-permute-start | bytes 393224 | tf_op jit(solution)/shard_map/ppermute | solution.py:23
  26.7 5.5 %collective-permute-start.8 = (bf16[128,512]{1,0:T(8,128)(2,1)S(1)}, bf16[128,512]{1,0:T(8,128)(2,1)S(1)}, u32[]{:S(2)}, u32[]{:S(2)}) collective-permute-start(bf16[128,512]{1,0:T(8,128)(2,1)S(1)} %expand_rows.3.refs_1_), channel_id=1, source_target_pairs={{0,16},{1,17},{2,18},{3,19},{4,20},{5,21},{6,22},{7,23},{8,24},{9,... | collective-permute-start | bytes 393224 | tf_op jit(solution)/shard_map/ppermute | solution.py:23
  32.7 1.6 %collective-permute-start.10 = (bf16[64,2048]{1,0:T(8,128)(2,1)S(1)}, bf16[64,2048]{1,0:T(8,128)(2,1)S(1)}, u32[]{:S(2)}, u32[]{:S(2)}) collective-permute-start(bf16[64,2048]{1,0:T(8,128)(2,1)S(1)} %contract_hidden.7), channel_id=1, source_target_pairs={{0,1},{1,0},{2,3},{3,2},{4,5},{5,4},{6,7},{7,6},{8,9},{9,8},{10,11... | collective-permute-start | bytes 786440 | tf_op jit(solution)/shard_map/ppermute | solution.py:23

commit v10 on v9

--- a/solution.py
+++ b/solution.py
@@ -73,37 +73,29 @@
 
 def stack_blocks(blocks):
     def body(*refs):
-        for i, ref in enumerate(refs[:-2]):
-            refs[-2][i] = ref[...]
-            if i:
-                refs[-1][i - 1] = ref[...]
-
-    count, shape, dtype = len(blocks), blocks[0].shape, blocks[0].dtype
-    return pl.pallas_call(
-        body,
-        out_shape=[jax.ShapeDtypeStruct((n,) + shape, dtype) for n in (count, count - 1)],
-        in_specs=[pl.BlockSpec(memory_space=pltpu.VMEM)] * count,
-        out_specs=[pl.BlockSpec(memory_space=pltpu.VMEM)] * 2,
+        for i, ref in enumerate(refs[:-1]):
+            refs[-1][i] = ref[...]
+
+    return pl.pallas_call(
+        body,
+        out_shape=jax.ShapeDtypeStruct((len(blocks),) + blocks[0].shape, blocks[0].dtype),
+        in_specs=[pl.BlockSpec(memory_space=pltpu.VMEM)] * len(blocks),
+        out_specs=pl.BlockSpec(memory_space=pltpu.VMEM),
         compiler_params=pltpu.CompilerParams(vmem_limit_bytes=4 << 20),
         name="stack_blocks",
     )(*blocks)
 
 
 def join_rows(stacks):
-    _, tokens, width = stacks[0].shape
-    total = sum(1 if stack.ndim == 2 else stack.shape[0] for stack in stacks)
+    blocks, tokens, width = stacks[0].shape
+    total = len(stacks) * blocks
     batch = max(1, 16 // tokens)
 
     def body(*refs):
-        group, start = [], 0
-        for ref, stack in zip(refs, stacks):
-            for i in range(1 if stack.ndim == 2 else stack.shape[0]):
-                value = ref[...] if stack.ndim == 2 else ref[i]
-                group.append(value.astype(jnp.float32))
-                if len(group) == batch:
-                    rows = jnp.concatenate(group).astype(refs[-1].dtype)
-                    refs[-1][start : start + batch * tokens, :] = rows
-                    group, start = [], start + batch * tokens
+        for i in range(0, total, batch):
+            group = [refs[j // blocks][j % blocks] for j in range(i, i + batch)]
+            rows = jnp.concatenate([value.astype(jnp.float32) for value in group])
+            refs[-1][i * tokens : (i + batch) * tokens, :] = rows.astype(refs[-1].dtype)
 
     return pl.pallas_call(
         body,
@@ -204,28 +196,55 @@
     )(*operands)
 
 
-def add_and_order(total, received, wide, high):
-    count, width = received.shape
-    blocks = 4 * wide * high
-    tokens, far_size = count // blocks, 2 * high
-
-    def body(total_ref, received_ref, out_ref):
-        group, far = lax.axis_index("dp"), lax.axis_index("far")
-        for i in range(blocks):
-            x, y, w, h = i // (blocks // 2), i // (wide * high) % 2, i // high % wide, i % high
-            slot = (group ^ (x + 2 * w)) * far_size + (far ^ (y + 2 * h))
-            here = slice(i * tokens, (i + 1) * tokens)
-            value = total_ref[here, :] + received_ref[here, :].astype(jnp.float32)
-            out_ref[slot] = value.astype(out_ref.dtype)
-
-    return pl.pallas_call(
-        body,
-        out_shape=jax.ShapeDtypeStruct((blocks, tokens, width), received.dtype),
-        in_specs=[pl.BlockSpec(memory_space=pltpu.VMEM)] * 2,
-        out_specs=pl.BlockSpec(memory_space=pltpu.VMEM),
-        compiler_params=pltpu.CompilerParams(vmem_limit_bytes=12 * total.size + (6 << 20)),
-        name="add_and_order",
-    )(total, received)
+def sum_stage(inputs, plan, shape, dtype):
+    def body(*refs):
+        sources, targets = refs[: len(inputs)], refs[len(inputs) :]
+        for target, blocks in zip(targets, plan):
+            for i, block in enumerate(blocks):
+                total = 0.0
+                for ref in sources:
+                    if len(ref.shape) == 2:
+                        value = ref[block * shape[0] : (block + 1) * shape[0], :]
+                    else:
+                        value = ref[block]
+                    total = total + value.astype(jnp.float32)
+                target[i] = total.astype(target.dtype)
+
+    return pl.pallas_call(
+        body,
+        out_shape=[
+            jax.ShapeDtypeStruct((len(blocks),) + shape, dtype if i else jnp.float32)
+            for i, blocks in enumerate(plan)
+        ],
+        in_specs=[pl.BlockSpec(memory_space=pltpu.VMEM)] * len(inputs),
+        out_specs=[pl.BlockSpec(memory_space=pltpu.VMEM)] * len(plan),
+        compiler_params=pltpu.CompilerParams(
+            vmem_limit_bytes=sum(value.nbytes for value in inputs) * 2 + (6 << 20)
+        ),
+        name="sum_stage",
+    )(*inputs)
+
+
+def finish(sums, groups, dtype):
+    tokens, columns = sums[0][0].shape[1:]
+    flat = [value for parts in sums for value in parts]
+
+    def body(*refs):
+        group = lax.axis_index("dp")
+        refs, out_ref = list(refs[:-1]), refs[-1]
+        for i, parts in enumerate(sums):
+            total = sum(refs.pop(0)[0].astype(jnp.float32) for _ in parts)
+            start = pl.multiple_of((group ^ i) * columns, LANES)
+            out_ref[:, pl.ds(start, columns)] = total.astype(dtype)
+
+    return pl.pallas_call(
+        body,
+        out_shape=jax.ShapeDtypeStruct((tokens, groups * columns), dtype),
+        in_specs=[pl.BlockSpec(memory_space=pltpu.VMEM)] * len(flat),
+        out_specs=pl.BlockSpec(memory_space=pltpu.VMEM),
+        compiler_params=pltpu.CompilerParams(vmem_limit_bytes=4 << 20),
+        name="finish",
+    )(*flat)
 
 
 def local(tokens, expert_ids, gate_probs, w_gate, w_up, w_down):
@@ -237,14 +256,10 @@
     units = w_up.shape[2]
     weights = lax.optimization_barrier((block, w_gate[0], w_up[0], w_down[0]))
     block, gate_weights, up_weights, down_weights = weights
-    near = [block] + [swap(block, 0, 4 * i) for i in range(1, high)]
-    early = swap(block, 1, 2)
-    near[-1], early = lax.optimization_barrier((near[-1], early))
-    near, rest = stack_blocks(near)
+    near = stack_blocks([block] + [swap(block, 0, 4 * i) for i in range(1, high)])
     if wide > 1:
         near = jnp.concatenate([near] + [swap(near, 2 * i, 0) for i in range(1, wide)])
-        rest = near[1:]
-    chip = join_rows([near, swap(near, 0, 2), swap(near, 1, 0), early, swap(rest, 1, 2)])
+    chip = join_rows([near, swap(near, 0, 2), swap(near, 1, 0), swap(near, 1, 2)])
     rows = jnp.concatenate([chip, swap(chip, 0, 1)])
 
     chunks = CHUNKS if units % (LANES * CHUNKS) == 0 else 1
@@ -277,12 +292,18 @@
     )
     sent, kept = last(1, jnp.bfloat16), last(0, jnp.float32)
 
-    columns = w_down.shape[2]
-    blocks = add_and_order(kept, swap(sent, 0, 1), wide, high)
-    blocks = lax.all_to_all(blocks, ("dp", "far"), split_axis=0, concat_axis=0, tiled=True)
-    blocks = blocks.reshape(groups, -1, token_count, columns).astype(jnp.float32)
-    combined = jnp.sum(blocks, axis=1).astype(jnp.bfloat16)
-    return combined.transpose(1, 0, 2).reshape(token_count, width)
+    shape = (token_count, w_down.shape[2])
+    rest = [(g, h) for g in range(groups) for h in range(0, high, 2)]
+    slot = lambda g, y, h: (((g & 1) * 2 + y) * wide + (g >> 1)) * high + h
+    plan = [[slot(g, y, h + z) for g, h in rest] for y, z in ((0, 0), (1, 0), (0, 1), (1, 1))]
+    mine, *away = sum_stage([kept, swap(sent, 0, 1)], plan, shape, jnp.bfloat16)
+    inputs = [mine] + [swap(value, 0, mask) for value, mask in zip(away, (2, 4, 6))]
+    mine, *away = sum_stage(inputs, [[i] for i in range(len(rest))], shape, jnp.bfloat16)
+    sums = [[] for _ in range(groups)]
+    sums[0].append(mine)
+    for value, (g, h) in zip(away, rest[1:]):
+        sums[g].append(swap(value, g, 4 * h))
+    return finish(sums, groups, tokens.dtype)
 
 
 def solution(mesh):

time: 50.5 us -> 50.1 us (level)
  blocking collectives: 15.2 us -> 0 us
  waiting for transfers between devices: 13.8 us -> 23.2 us
  starting transfers between devices: 14.2 us -> 19.6 us
  other arithmetic: 0.8 us -> 0.07 us
  Pallas kernels: 6.22 us -> 6.88 us
    all_to_all x1 -> x0, blocking collectives: 15.2 us -> none  [local(): lax.all_to_all(blocks, ('dp', 'far'), split_axis=0, concat_axis=0, tiled=...]
    ppermute x11 -> x16, waiting for transfers between devices: 13.8 us -> 23.2 us  [swap(): return lax.ppermute(value, ('dp',) + EXPERT, pairs)]
    ppermute x11 -> x16, starting transfers between devices: 14.2 us -> 19.6 us  [swap(): return lax.ppermute(value, ('dp',) + EXPERT, pairs)]
    reduce_sum x1 -> x0, other arithmetic: 0.73 us -> none  [local(): combined = jnp.sum(blocks, axis=1).astype(jnp.bfloat16)]
    pallas_call x2 -> x4, Pallas kernels: 0.13 us -> 0.8 us  [the longest x1 0.63 us: finish(): pl.pallas_call(body, out_shape=jax.ShapeDtypeStruct((tokens, groups * col...]
  transfers between devices with their start and end apart: 11 -> 16, of which waited for: 7 -> 15; matrix products, arithmetic and copies ran while one was open for 0% -> 0% of each run, Pallas kernels for 6% -> 6%
where the time goes in v10:
time: 50.1 us; the launch traced here: 50 us
  waiting for transfers between devices  23.2 us (46%)
  starting transfers between devices  19.6 us (39%)
  Pallas kernels  6.88 us (14%)
    ppermute x16, waiting for transfers between devices, swap(): return lax.ppermute(value, ('dp',) + EXPERT, pairs)  23.2 us
    ppermute x16, starting transfers between devices, swap(): return lax.ppermute(value, ('dp',) + EXPERT, pairs)  19.6 us
    pallas_call x2, Pallas kernels, expand_rows(): pl.pallas_call(body, out_shape=jax.ShapeDtypeStruct((count, columns), row...  2.78 us
    pallas_call x4, Pallas kernels, contract_hidden(): pl.pallas_call(body, out_shape=jax.ShapeDtypeStruct((count, width), kind)...  2.16 us
    pallas_call x1, Pallas kernels, pack_block(): pl.pallas_call(body, out_shape=jax.ShapeDtypeStruct((count, width + LANES...  1.02 us
  transfers between devices with their start and end apart: 16, of which 15 were waited for; matrix products, arithmetic and copies ran while one was open for 0% of the time, Pallas kernels for 6%

profile of v10, /device:TPU:0, one launch (start us, length us, event | category | flops | bytes accessed | tf_op | source)
XLA Modules:
  0.0 50.0 jit_solution(1063495319781940295)
XLA Ops:
  0.0 1.0 %pack_block.1.refs_0_ = bf16[4,4224]{1,0:T(4,128)(2,1)S(1)} custom-call(bf16[4,4096]{1,0:T(4,128)(2,1)} %tokens_ref.1, s32[4,8]{1,0:T(4,128)} %ids_ref.1, f32[4,8]{1,0:T(4,128)} %probs_ref.1), custom_call_target="tpu_custom_call" | custom-call | flops 60000002048 | tf_op jit(solution)/shard_map/pack_block/pallas_call | solution.py:63
  1.0 5.1 %collective-permute-start.2 = (bf16[4,4224]{1,0:T(4,128)(2,1)S(1)}, bf16[4,4224]{1,0:T(4,128)(2,1)S(1)}, u32[]{:S(2)}, u32[]{:S(2)}) collective-permute-start(bf16[4,4224]{1,0:T(4,128)(2,1)S(1)} %pack_block.1.refs_0_), channel_id=1, source_target_pairs={{0,12},{1,13},{2,14},{3,15},{4,8},{5,9},{6,10},{7,11},{8,4},{9,5},... | collective-permute-start | bytes 101384 | tf_op jit(solution)/shard_map/ppermute | solution.py:23
  6.1 0.0 collective-permute-start.1
  6.1 0.6 %collective-permute-start = (bf16[4,4224]{1,0:T(4,128)(2,1)S(1)}, bf16[4,4224]{1,0:T(4,128)(2,1)S(1)}, u32[]{:S(2)}, u32[]{:S(2)}) collective-permute-start(bf16[4,4224]{1,0:T(4,128)(2,1)S(1)} %pack_block.1.refs_0_), channel_id=1, source_target_pairs={{0,4},{1,5},{2,6},{3,7},{4,0},{5,1},{6,2},{7,3},{8,12},{9,13},{10,... | collective-permute-start | bytes 101384 | tf_op jit(solution)/shard_map/ppermute | solution.py:23
  6.8 1.3 %collective-permute-done.2.refs_3_ = bf16[4,4224]{1,0:T(4,128)(2,1)S(1)} collective-permute-done((bf16[4,4224]{1,0:T(4,128)(2,1)S(1)}, bf16[4,4224]{1,0:T(4,128)(2,1)S(1)}, u32[]{:S(2)}, u32[]{:S(2)}) %collective-permute-start.2) | collective-permute-done | bytes 33824 | tf_op jit(solution)/shard_map/ppermute | solution.py:23
  8.0 2.9 %collective-permute-done.1.refs_2_ = bf16[4,4224]{1,0:T(4,128)(2,1)S(1)} collective-permute-done((bf16[4,4224]{1,0:T(4,128)(2,1)S(1)}, bf16[4,4224]{1,0:T(4,128)(2,1)S(1)}, u32[]{:S(2)}, u32[]{:S(2)}) %collective-permute-start.1) | collective-permute-done | bytes 33824 | tf_op jit(solution)/shard_map/ppermute | solution.py:23
  11.0 0.0 collective-permute-done.refs_1_
  11.0 2.5 %collective-permute-start.5 = (bf16[4,4,4224]{2,1,0:T(4,128)(2,1)S(1)}, bf16[4,4,4224]{2,1,0:T(4,128)(2,1)S(1)}, u32[]{:S(2)}, u32[]{:S(2)}) collective-permute-start(bf16[4,4,4224]{2,1,0:T(4,128)(2,1)S(1)} %stack_blocks.1.refs_0_), channel_id=1, source_target_pairs={{0,18},{1,19},{2,16},{3,17},{4,22},{5,23},{6,20},{7,21},{8,26},{9,... | collective-permute-start | bytes 405512 | tf_op jit(solution)/shard_map/ppermute | solution.py:23
  13.5 0.5 %collective-permute-start.4 = (bf16[4,4,4224]{2,1,0:T(4,128)(2,1)S(1)}, bf16[4,4,4224]{2,1,0:T(4,128)(2,1)S(1)}, u32[]{:S(2)}, u32[]{:S(2)}) collective-permute-start(bf16[4,4,4224]{2,1,0:T(4,128)(2,1)S(1)} %stack_blocks.1.refs_0_), channel_id=1, source_target_pairs={{0,16},{1,17},{2,18},{3,19},{4,20},{5,21},{6,22},{7,23},{8,24},{9,... | collective-permute-start | bytes 405512 | tf_op jit(solution)/shard_map/ppermute | solution.py:23
  14.0 0.5 %collective-permute-start.3 = (bf16[4,4,4224]{2,1,0:T(4,128)(2,1)S(1)}, bf16[4,4,4224]{2,1,0:T(4,128)(2,1)S(1)}, u32[]{:S(2)}, u32[]{:S(2)}) collective-permute-start(bf16[4,4,4224]{2,1,0:T(4,128)(2,1)S(1)} %stack_blocks.1.refs_0_), channel_id=1, source_target_pairs={{0,2},{1,3},{2,0},{3,1},{4,6},{5,7},{6,4},{7,5},{8,10},{9,11},{10,... | collective-permute-start | bytes 405512 | tf_op jit(solution)/shard_map/ppermute | solution.py:23
  14.5 2.8 %collective-permute-done.5.refs_3_ = bf16[4,4,4224]{2,1,0:T(4,128)(2,1)S(1)} collective-permute-done((bf16[4,4,4224]{2,1,0:T(4,128)(2,1)S(1)}, bf16[4,4,4224]{2,1,0:T(4,128)(2,1)S(1)}, u32[]{:S(2)}, u32[]{:S(2)}) %collective-permute-start.5) | collective-permute-done | bytes 135200 | tf_op jit(solution)/shard_map/ppermute | solution.py:23
  17.4 1.4 %collective-permute-done.4.refs_2_ = bf16[4,4,4224]{2,1,0:T(4,128)(2,1)S(1)} collective-permute-done((bf16[4,4,4224]{2,1,0:T(4,128)(2,1)S(1)}, bf16[4,4,4224]{2,1,0:T(4,128)(2,1)S(1)}, u32[]{:S(2)}, u32[]{:S(2)}) %collective-permute-start.4) | collective-permute-done | bytes 135200 | tf_op jit(solution)/shard_map/ppermute | solution.py:23
  18.8 0.2 collective-permute-done.3.refs_1_
  19.0 0.1 join_rows.1
  19.2 0.1 collective-permute-start.6
  19.3 1.9 %collective-permute-done.6 = bf16[64,4224]{1,0:T(8,128)(2,1)S(1)} collective-permute-done((bf16[64,4224]{1,0:T(8,128)(2,1)S(1)}, bf16[64,4224]{1,0:T(8,128)(2,1)S(1)}, u32[]{:S(2)}, u32[]{:S(2)}) %collective-permute-start.6) | collective-permute-done | bytes 540704 | tf_op jit(solution)/shard_map/ppermute | solution.py:23
  21.2 0.1 pad_maximum_fusion.rows_ref.refs_3_
  21.3 0.0 copy-done
  21.3 0.0 copy-done.1
  21.3 0.0 slice-start
  21.3 1.4 %expand_rows.2.refs_0_ = bf16[128,512]{1,0:T(8,128)(2,1)S(1)} custom-call(bf16[128,4224]{1,0:T(8,128)(2,1)S(1)} %pad_maximum_fusion.rows_ref.refs_3_, bf16[4096,1024]{1,0:T(8,128)(2,1)S(1)} %bitcast.9, bf16[4096,1024]{1,0:T(8,128)(2,1)S(1)} %bitcast.11), custom_call_target="tpu_custom_call" | custom-call | bytes 65536 | tf_op jit(solution)/shard_map/expand_rows/pallas_call | solution.py:128
  22.7 0.0 slice-start.1
  22.7 1.5 %collective-permute-start.8 = (bf16[128,512]{1,0:T(8,128)(2,1)S(1)}, bf16[128,512]{1,0:T(8,128)(2,1)S(1)}, u32[]{:S(2)}, u32[]{:S(2)}) collective-permute-start(bf16[128,512]{1,0:T(8,128)(2,1)S(1)} %expand_rows.2.refs_0_), channel_id=1, source_target_pairs={{0,16},{1,17},{2,18},{3,19},{4,20},{5,21},{6,22},{7,23},{8,24},{9,... | collective-permute-start | bytes 393224 | tf_op jit(solution)/shard_map/ppermute | solution.py:23
  24.2 1.4 %expand_rows.3.refs_1_ = bf16[128,512]{1,0:T(8,128)(2,1)S(1)} custom-call(bf16[128,4224]{1,0:T(8,128)(2,1)S(1)} %pad_maximum_fusion.rows_ref.refs_3_, bf16[4096,1024]{1,0:T(8,128)(2,1)S(1)} %bitcast.10, bf16[4096,1024]{1,0:T(8,128)(2,1)S(1)} %bitcast.12), custom_call_target="tpu_custom_call" | custom-call | bytes 65536 | tf_op jit(solution)/shard_map/expand_rows/pallas_call | solution.py:128
  25.6 0.6 %collective-permute-start.7 = (bf16[128,512]{1,0:T(8,128)(2,1)S(1)}, bf16[128,512]{1,0:T(8,128)(2,1)S(1)}, u32[]{:S(2)}, u32[]{:S(2)}) collective-permute-start(bf16[128,512]{1,0:T(8,128)(2,1)S(1)} %expand_rows.3.refs_1_), channel_id=1, source_target_pairs={{0,16},{1,17},{2,18},{3,19},{4,20},{5,21},{6,22},{7,23},{8,24},{9,... | collective-permute-start | bytes 393224 | tf_op jit(solution)/shard_map/ppermute | solution.py:23
  26.3 0.0 slice-done
  26.3 0.7 %contract_hidden.4.refs_2_ = f32[128,2048]{1,0:T(8,128)S(1)} custom-call(bf16[128,512]{1,0:T(8,128)(2,1)S(1)} %expand_rows.2.refs_0_, bf16[128,512]{1,0:T(8,128)(2,1)S(1)} %expand_rows.3.refs_1_, bf16[2048,2048]{1,0:T(8,128)(2,1)S(1)} %bitcast.5), custom_call_target="tpu_custom_call" | custom-call | bytes 262144 | tf_op jit(solution)/shard_map/contract_hidden/pallas_call | solution.py:184
  27.0 1.4 %collective-permute-done.8.refs_0_ = bf16[128,512]{1,0:T(8,128)(2,1)S(1)} collective-permute-done((bf16[128,512]{1,0:T(8,128)(2,1)S(1)}, bf16[128,512]{1,0:T(8,128)(2,1)S(1)}, u32[]{:S(2)}, u32[]{:S(2)}) %collective-permute-start.8) | collective-permute-done | bytes 131104 | tf_op jit(solution)/shard_map/ppermute | solution.py:23
  28.4 0.5 contract_hidden.5.refs_2_
  28.8 2.3 %collective-permute-done.7.refs_0_ = bf16[128,512]{1,0:T(8,128)(2,1)S(1)} collective-permute-done((bf16[128,512]{1,0:T(8,128)(2,1)S(1)}, bf16[128,512]{1,0:T(8,128)(2,1)S(1)}, u32[]{:S(2)}, u32[]{:S(2)}) %collective-permute-start.7) | collective-permute-done | bytes 131104 | tf_op jit(solution)/shard_map/ppermute | solution.py:23
  31.1 0.5 contract_hidden.7
  31.6 0.1 collective-permute-start.9
  31.7 0.5 %contract_hidden.6.refs_0_ = f32[64,2048]{1,0:T(8,128)S(1)} custom-call(bf16[128,512]{1,0:T(8,128)(2,1)S(1)} %collective-permute-done.7.refs_0_, bf16[2048,2048]{1,0:T(8,128)(2,1)S(1)} %bitcast.8, f32[128,2048]{1,0:T(8,128)S(1)} %contract_hidden.5.refs_2_, bf16[128,4224]{1,0:T(8,128)(2,1)S(1)} %pad_maximum_fusion.rows_ref.refs_3_), custom_call_target="tpu_custom_call" | custom-call | bytes 131072 | tf_op jit(solution)/shard_map/contract_hidden/pallas_call | solution.py:184
  32.2 1.0 %collective-permute-done.9.refs_1_ = bf16[64,2048]{1,0:T(8,128)(2,1)S(1)} collective-permute-done((bf16[64,2048]{1,0:T(8,128)(2,1)S(1)}, bf16[64,2048]{1,0:T(8,128)(2,1)S(1)}, u32[]{:S(2)}, u32[]{:S(2)}) %collective-permute-start.9) | collective-permute-done | bytes 262176 | tf_op jit(solution)/shard_map/ppermute | solution.py:23
  33.2 0.1 sum_stage.2
  33.3 1.3 %collective-permute-start.10 = (bf16[4,4,2048]{2,1,0:T(4,128)(2,1)S(1)}, bf16[4,4,2048]{2,1,0:T(4,128)(2,1)S(1)}, u32[]{:S(2)}, u32[]{:S(2)}) collective-permute-start(bf16[4,4,2048]{2,1,0:T(4,128)(2,1)S(1)} %get-tuple-element.26), channel_id=1, source_target_pairs={{0,2},{1,3},{2,0},{3,1},{4,6},{5,7},{6,4},{7,5},{8,10},{9,11},{10,... | collective-permute-start | bytes 196616 | tf_op jit(solution)/shard_map/ppermute | solution.py:23
  34.6 0.1 collective-permute-start.11
  34.7 2.2 %collective-permute-start.12 = (bf16[4,4,2048]{2,1,0:T(4,128)(2,1)S(1)}, bf16[4,4,2048]{2,1,0:T(4,128)(2,1)S(1)}, u32[]{:S(2)}, u32[]{:S(2)}) collective-permute-start(bf16[4,4,2048]{2,1,0:T(4,128)(2,1)S(1)} %get-tuple-element.28), channel_id=1, source_target_pairs={{0,6},{1,7},{2,4},{3,5},{4,2},{5,3},{6,0},{7,1},{8,14},{9,15},{10,... | collective-permute-start | bytes 196616 | tf_op jit(solution)/shard_map/ppermute | solution.py:23
  36.9 0.8 %collective-permute-done.10.refs_1_ = bf16[4,4,2048]{2,1,0:T(4,128)(2,1)S(1)} collective-permute-done((bf16[4,4,2048]{2,1,0:T(4,128)(2,1)S(1)}, bf16[4,4,2048]{2,1,0:T(4,128)(2,1)S(1)}, u32[]{:S(2)}, u32[]{:S(2)}) %collective-permute-start.10) | collective-permute-done | bytes 65568 | tf_op jit(solution)/shard_map/ppermute | solution.py:23
  37.7 1.5 %collective-permute-done.11.refs_2_ = bf16[4,4,2048]{2,1,0:T(4,128)(2,1)S(1)} collective-permute-done((bf16[4,4,2048]{2,1,0:T(4,128)(2,1)S(1)}, bf16[4,4,2048]{2,1,0:T(4,128)(2,1)S(1)}, u32[]{:S(2)}, u32[]{:S(2)}) %collective-permute-start.11) | collective-permute-done | bytes 65568 | tf_op jit(solution)/shard_map/ppermute | solution.py:23
  39.2 0.9 %collective-permute-done.12.refs_3_ = bf16[4,4,2048]{2,1,0:T(4,128)(2,1)S(1)} collective-permute-done((bf16[4,4,2048]{2,1,0:T(4,128)(2,1)S(1)}, bf16[4,4,2048]{2,1,0:T(4,128)(2,1)S(1)}, u32[]{:S(2)}, u32[]{:S(2)}) %collective-permute-start.12) | collective-permute-done | bytes 65568 | tf_op jit(solution)/shard_map/ppermute | solution.py:23
  40.2 2.2 %collective-permute-start.13 = (bf16[1,4,2048]{2,1,0:T(4,128)(2,1)S(1)}, bf16[1,4,2048]{2,1,0:T(4,128)(2,1)S(1)}, u32[]{:S(2)}, u32[]{:S(2)}) collective-permute-start(bf16[1,4,2048]{2,1,0:T(4,128)(2,1)S(1)} %get-tuple-element.30), channel_id=1, source_target_pairs={{0,8},{1,9},{2,10},{3,11},{4,12},{5,13},{6,14},{7,15},{8,0},{9,1},... | collective-permute-start | bytes 49160 | tf_op jit(solution)/shard_map/ppermute | solution.py:23
  42.3 1.5 %collective-permute-start.14 = (bf16[1,4,2048]{2,1,0:T(4,128)(2,1)S(1)}, bf16[1,4,2048]{2,1,0:T(4,128)(2,1)S(1)}, u32[]{:S(2)}, u32[]{:S(2)}) collective-permute-start(bf16[1,4,2048]{2,1,0:T(4,128)(2,1)S(1)} %get-tuple-element.31), channel_id=1, source_target_pairs={{0,16},{1,17},{2,18},{3,19},{4,20},{5,21},{6,22},{7,23},{8,24},{9,... | collective-permute-start | bytes 49160 | tf_op jit(solution)/shard_map/ppermute | solution.py:23
  43.8 0.8 %collective-permute-start.15 = (bf16[1,4,2048]{2,1,0:T(4,128)(2,1)S(1)}, bf16[1,4,2048]{2,1,0:T(4,128)(2,1)S(1)}, u32[]{:S(2)}, u32[]{:S(2)}) collective-permute-start(bf16[1,4,2048]{2,1,0:T(4,128)(2,1)S(1)} %get-tuple-element.32), channel_id=1, source_target_pairs={{0,24},{1,25},{2,26},{3,27},{4,28},{5,29},{6,30},{7,31},{8,16},{9,... | collective-permute-start | bytes 49160 | tf_op jit(solution)/shard_map/ppermute | solution.py:23
  44.6 0.2 collective-permute-done.13.refs_1_
  44.9 1.2 %collective-permute-done.14.refs_2_ = bf16[1,4,2048]{2,1,0:T(4,128)(2,1)S(1)} collective-permute-done((bf16[1,4,2048]{2,1,0:T(4,128)(2,1)S(1)}, bf16[1,4,2048]{2,1,0:T(4,128)(2,1)S(1)}, u32[]{:S(2)}, u32[]{:S(2)}) %collective-permute-start.14) | collective-permute-done | bytes 16416 | tf_op jit(solution)/shard_map/ppermute | solution.py:23
  46.0 3.3 %collective-permute-done.15.refs_3_ = bf16[1,4,2048]{2,1,0:T(4,128)(2,1)S(1)} collective-permute-done((bf16[1,4,2048]{2,1,0:T(4,128)(2,1)S(1)}, bf16[1,4,2048]{2,1,0:T(4,128)(2,1)S(1)}, u32[]{:S(2)}, u32[]{:S(2)}) %collective-permute-start.15) | collective-permute-done | bytes 16416 | tf_op jit(solution)/shard_map/ppermute | solution.py:23
  49.3 0.6 %finish.1 = bf16[4,4096]{1,0:T(4,128)(2,1)} custom-call(f32[1,4,2048]{2,1,0:T(4,128)S(1)} %get-tuple-element.29.refs_0_, bf16[1,4,2048]{2,1,0:T(4,128)(2,1)S(1)} %collective-permute-done.13.refs_1_, bf16[1,4,2048]{2,1,0:T(4,128)(2,1)S(1)} %collective-permute-done.14.refs_2_, bf16[1,4,2048]{2,1,0:T(4,128)(2,1)S(1)} %collective-permute-done.15.refs_3_), custom_call_target="tpu_custom_call" | custom-call | tf_op jit(solution)/shard_map/finish/pallas_call | solution.py:240
  (6 shorter events, 0.1 us)
Async XLA Ops:
  0.0 21.3 %copy-start = (bf16[1,4096,1024]{2,1,0:T(8,128)(2,1)S(1)}, bf16[1,4096,1024]{2,1,0:T(8,128)(2,1)}, u32[]{:S(2)}) copy-start(bf16[1,4096,1024]{2,1,0:T(8,128)(2,1)} %param.9) | copy-start | bytes 25165828
  0.0 21.3 %copy-start.1 = (bf16[1,4096,1024]{2,1,0:T(8,128)(2,1)S(1)}, bf16[1,4096,1024]{2,1,0:T(8,128)(2,1)}, u32[]{:S(2)}) copy-start(bf16[1,4096,1024]{2,1,0:T(8,128)(2,1)} %param.10) | copy-start | bytes 25165828
  1.0 7.0 %collective-permute-start.2 = (bf16[4,4224]{1,0:T(4,128)(2,1)S(1)}, bf16[4,4224]{1,0:T(4,128)(2,1)S(1)}, u32[]{:S(2)}, u32[]{:S(2)}) collective-permute-start(bf16[4,4224]{1,0:T(4,128)(2,1)S(1)} %pack_block.1.refs_0_), channel_id=1, source_target_pairs={{0,12},{1,13},{2,14},{3,15},{4,8},{5,9},{6,10},{7,11},{8,4},{9,5},... | collective-permute-start | bytes 101384 | tf_op jit(solution)/shard_map/ppermute | solution.py:23
  6.1 4.8 %collective-permute-start.1 = (bf16[4,4224]{1,0:T(4,128)(2,1)S(1)}, bf16[4,4224]{1,0:T(4,128)(2,1)S(1)}, u32[]{:S(2)}, u32[]{:S(2)}) collective-permute-start(bf16[4,4224]{1,0:T(4,128)(2,1)S(1)} %pack_block.1.refs_0_), channel_id=1, source_target_pairs={{0,8},{1,9},{2,10},{3,11},{4,12},{5,13},{6,14},{7,15},{8,0},{9,1},... | collective-permute-start | bytes 101384 | tf_op jit(solution)/shard_map/ppermute | solution.py:23
  6.1 4.8 %collective-permute-start = (bf16[4,4224]{1,0:T(4,128)(2,1)S(1)}, bf16[4,4224]{1,0:T(4,128)(2,1)S(1)}, u32[]{:S(2)}, u32[]{:S(2)}) collective-permute-start(bf16[4,4224]{1,0:T(4,128)(2,1)S(1)} %pack_block.1.refs_0_), channel_id=1, source_target_pairs={{0,4},{1,5},{2,6},{3,7},{4,0},{5,1},{6,2},{7,3},{8,12},{9,13},{10,... | collective-permute-start | bytes 101384 | tf_op jit(solution)/shard_map/ppermute | solution.py:23
  11.0 6.4 %collective-permute-start.5 = (bf16[4,4,4224]{2,1,0:T(4,128)(2,1)S(1)}, bf16[4,4,4224]{2,1,0:T(4,128)(2,1)S(1)}, u32[]{:S(2)}, u32[]{:S(2)}) collective-permute-start(bf16[4,4,4224]{2,1,0:T(4,128)(2,1)S(1)} %stack_blocks.1.refs_0_), channel_id=1, source_target_pairs={{0,18},{1,19},{2,16},{3,17},{4,22},{5,23},{6,20},{7,21},{8,26},{9,... | collective-permute-start | bytes 405512 | tf_op jit(solution)/shard_map/ppermute | solution.py:23
  13.5 5.3 %collective-permute-start.4 = (bf16[4,4,4224]{2,1,0:T(4,128)(2,1)S(1)}, bf16[4,4,4224]{2,1,0:T(4,128)(2,1)S(1)}, u32[]{:S(2)}, u32[]{:S(2)}) collective-permute-start(bf16[4,4,4224]{2,1,0:T(4,128)(2,1)S(1)} %stack_blocks.1.refs_0_), channel_id=1, source_target_pairs={{0,16},{1,17},{2,18},{3,19},{4,20},{5,21},{6,22},{7,23},{8,24},{9,... | collective-permute-start | bytes 405512 | tf_op jit(solution)/shard_map/ppermute | solution.py:23
  14.0 5.0 %collective-permute-start.3 = (bf16[4,4,4224]{2,1,0:T(4,128)(2,1)S(1)}, bf16[4,4,4224]{2,1,0:T(4,128)(2,1)S(1)}, u32[]{:S(2)}, u32[]{:S(2)}) collective-permute-start(bf16[4,4,4224]{2,1,0:T(4,128)(2,1)S(1)} %stack_blocks.1.refs_0_), channel_id=1, source_target_pairs={{0,2},{1,3},{2,0},{3,1},{4,6},{5,7},{6,4},{7,5},{8,10},{9,11},{10,... | collective-permute-start | bytes 405512 | tf_op jit(solution)/shard_map/ppermute | solution.py:23
  19.2 2.0 %collective-permute-start.6 = (bf16[64,4224]{1,0:T(8,128)(2,1)S(1)}, bf16[64,4224]{1,0:T(8,128)(2,1)S(1)}, u32[]{:S(2)}, u32[]{:S(2)}) collective-permute-start(bf16[64,4224]{1,0:T(8,128)(2,1)S(1)} %join_rows.1), channel_id=1, source_target_pairs={{0,1},{1,0},{2,3},{3,2},{4,5},{5,4},{6,7},{7,6},{8,9},{9,8},{10,11... | collective-permute-start | bytes 1622024 | tf_op jit(solution)/shard_map/ppermute | solution.py:23
  21.3 5.0 %slice-start = ((s8[8388608]{0:T(1024)(128)(4,1)}), s8[4194304]{0:T(1024)(128)(4,1)S(1)}, s32[]{:S(2)}) async-start(s8[8388608]{0:T(1024)(128)(4,1)} %bitcast.3), calls=%async_computation | async-start | bytes 8388608
  22.7 3.6 %slice-start.1 = ((s8[8388608]{0:T(1024)(128)(4,1)}), s8[4194304]{0:T(1024)(128)(4,1)S(1)}, s32[]{:S(2)}) async-start(s8[8388608]{0:T(1024)(128)(4,1)} %bitcast.3), calls=%async_computation.1 | async-start | bytes 8388608
  22.7 5.7 %collective-permute-start.8 = (bf16[128,512]{1,0:T(8,128)(2,1)S(1)}, bf16[128,512]{1,0:T(8,128)(2,1)S(1)}, u32[]{:S(2)}, u32[]{:S(2)}) collective-permute-start(bf16[128,512]{1,0:T(8,128)(2,1)S(1)} %expand_rows.2.refs_0_), channel_id=1, source_target_pairs={{0,16},{1,17},{2,18},{3,19},{4,20},{5,21},{6,22},{7,23},{8,24},{9,... | collective-permute-start | bytes 393224 | tf_op jit(solution)/shard_map/ppermute | solution.py:23
  25.6 5.5 %collective-permute-start.7 = (bf16[128,512]{1,0:T(8,128)(2,1)S(1)}, bf16[128,512]{1,0:T(8,128)(2,1)S(1)}, u32[]{:S(2)}, u32[]{:S(2)}) collective-permute-start(bf16[128,512]{1,0:T(8,128)(2,1)S(1)} %expand_rows.3.refs_1_), channel_id=1, source_target_pairs={{0,16},{1,17},{2,18},{3,19},{4,20},{5,21},{6,22},{7,23},{8,24},{9,... | collective-permute-start | bytes 393224 | tf_op jit(solution)/shard_map/ppermute | solution.py:23
  31.6 1.6 %collective-permute-start.9 = (bf16[64,2048]{1,0:T(8,128)(2,1)S(1)}, bf16[64,2048]{1,0:T(8,128)(2,1)S(1)}, u32[]{:S(2)}, u32[]{:S(2)}) collective-permute-start(bf16[64,2048]{1,0:T(8,128)(2,1)S(1)} %contract_hidden.7), channel_id=1, source_target_pairs={{0,1},{1,0},{2,3},{3,2},{4,5},{5,4},{6,7},{7,6},{8,9},{9,8},{10,11... | collective-permute-start | bytes 786440 | tf_op jit(solution)/shard_map/ppermute | solution.py:23
  33.3 4.3 %collective-permute-start.10 = (bf16[4,4,2048]{2,1,0:T(4,128)(2,1)S(1)}, bf16[4,4,2048]{2,1,0:T(4,128)(2,1)S(1)}, u32[]{:S(2)}, u32[]{:S(2)}) collective-permute-start(bf16[4,4,2048]{2,1,0:T(4,128)(2,1)S(1)} %get-tuple-element.26), channel_id=1, source_target_pairs={{0,2},{1,3},{2,0},{3,1},{4,6},{5,7},{6,4},{7,5},{8,10},{9,11},{10,... | collective-permute-start | bytes 196616 | tf_op jit(solution)/shard_map/ppermute | solution.py:23
  34.6 4.6 %collective-permute-start.11 = (bf16[4,4,2048]{2,1,0:T(4,128)(2,1)S(1)}, bf16[4,4,2048]{2,1,0:T(4,128)(2,1)S(1)}, u32[]{:S(2)}, u32[]{:S(2)}) collective-permute-start(bf16[4,4,2048]{2,1,0:T(4,128)(2,1)S(1)} %get-tuple-element.27), channel_id=1, source_target_pairs={{0,4},{1,5},{2,6},{3,7},{4,0},{5,1},{6,2},{7,3},{8,12},{9,13},{10,... | collective-permute-start | bytes 196616 | tf_op jit(solution)/shard_map/ppermute | solution.py:23
  34.7 5.4 %collective-permute-start.12 = (bf16[4,4,2048]{2,1,0:T(4,128)(2,1)S(1)}, bf16[4,4,2048]{2,1,0:T(4,128)(2,1)S(1)}, u32[]{:S(2)}, u32[]{:S(2)}) collective-permute-start(bf16[4,4,2048]{2,1,0:T(4,128)(2,1)S(1)} %get-tuple-element.28), channel_id=1, source_target_pairs={{0,6},{1,7},{2,4},{3,5},{4,2},{5,3},{6,0},{7,1},{8,14},{9,15},{10,... | collective-permute-start | bytes 196616 | tf_op jit(solution)/shard_map/ppermute | solution.py:23
  40.2 4.7 %collective-permute-start.13 = (bf16[1,4,2048]{2,1,0:T(4,128)(2,1)S(1)}, bf16[1,4,2048]{2,1,0:T(4,128)(2,1)S(1)}, u32[]{:S(2)}, u32[]{:S(2)}) collective-permute-start(bf16[1,4,2048]{2,1,0:T(4,128)(2,1)S(1)} %get-tuple-element.30), channel_id=1, source_target_pairs={{0,8},{1,9},{2,10},{3,11},{4,12},{5,13},{6,14},{7,15},{8,0},{9,1},... | collective-permute-start | bytes 49160 | tf_op jit(solution)/shard_map/ppermute | solution.py:23
  42.3 3.7 %collective-permute-start.14 = (bf16[1,4,2048]{2,1,0:T(4,128)(2,1)S(1)}, bf16[1,4,2048]{2,1,0:T(4,128)(2,1)S(1)}, u32[]{:S(2)}, u32[]{:S(2)}) collective-permute-start(bf16[1,4,2048]{2,1,0:T(4,128)(2,1)S(1)} %get-tuple-element.31), channel_id=1, source_target_pairs={{0,16},{1,17},{2,18},{3,19},{4,20},{5,21},{6,22},{7,23},{8,24},{9,... | collective-permute-start | bytes 49160 | tf_op jit(solution)/shard_map/ppermute | solution.py:23
  43.8 5.5 %collective-permute-start.15 = (bf16[1,4,2048]{2,1,0:T(4,128)(2,1)S(1)}, bf16[1,4,2048]{2,1,0:T(4,128)(2,1)S(1)}, u32[]{:S(2)}, u32[]{:S(2)}) collective-permute-start(bf16[1,4,2048]{2,1,0:T(4,128)(2,1)S(1)} %get-tuple-element.32), channel_id=1, source_target_pairs={{0,24},{1,25},{2,26},{3,27},{4,28},{5,29},{6,30},{7,31},{8,16},{9,... | collective-permute-start | bytes 49160 | tf_op jit(solution)/shard_map/ppermute | solution.py:23

commit v11 on v10

--- a/solution.py
+++ b/solution.py
@@ -10,7 +10,7 @@
 TILE = 256
 BATCH = 128
 LANES = 128
-EXPERT = ("far", "core")
+EXPERT = ("far", "near", "core")
 
 
 def swap(value, group_mask, expert_mask):
@@ -196,8 +196,10 @@
     )(*operands)
 
 
-def sum_stage(inputs, plan, shape, dtype):
+def add_blocks(inputs, plan, shape, dtype, ordered):
     def body(*refs):
+        group, far = lax.axis_index("dp"), lax.axis_index("far")
+        far_size = lax.axis_size("far")
         sources, targets = refs[: len(inputs)], refs[len(inputs) :]
         for target, blocks in zip(targets, plan):
             for i, block in enumerate(blocks):
@@ -208,43 +210,45 @@
                     else:
                         value = ref[block]
                     total = total + value.astype(jnp.float32)
+                if ordered:
+                    i = (group ^ (i // far_size)) * far_size + (far ^ (i % far_size))
                 target[i] = total.astype(target.dtype)
 
+    kinds = [dtype if i or ordered else jnp.float32 for i in range(len(plan))]
     return pl.pallas_call(
         body,
         out_shape=[
-            jax.ShapeDtypeStruct((len(blocks),) + shape, dtype if i else jnp.float32)
-            for i, blocks in enumerate(plan)
+            jax.ShapeDtypeStruct((len(blocks),) + shape, kind)
+            for kind, blocks in zip(kinds, plan)
         ],
         in_specs=[pl.BlockSpec(memory_space=pltpu.VMEM)] * len(inputs),
         out_specs=[pl.BlockSpec(memory_space=pltpu.VMEM)] * len(plan),
         compiler_params=pltpu.CompilerParams(
             vmem_limit_bytes=sum(value.nbytes for value in inputs) * 2 + (6 << 20)
         ),
-        name="sum_stage",
+        name="add_blocks",
     )(*inputs)
 
 
-def finish(sums, groups, dtype):
-    tokens, columns = sums[0][0].shape[1:]
-    flat = [value for parts in sums for value in parts]
-
-    def body(*refs):
-        group = lax.axis_index("dp")
-        refs, out_ref = list(refs[:-1]), refs[-1]
-        for i, parts in enumerate(sums):
-            total = sum(refs.pop(0)[0].astype(jnp.float32) for _ in parts)
-            start = pl.multiple_of((group ^ i) * columns, LANES)
-            out_ref[:, pl.ds(start, columns)] = total.astype(dtype)
-
-    return pl.pallas_call(
-        body,
-        out_shape=jax.ShapeDtypeStruct((tokens, groups * columns), dtype),
-        in_specs=[pl.BlockSpec(memory_space=pltpu.VMEM)] * len(flat),
-        out_specs=pl.BlockSpec(memory_space=pltpu.VMEM),
-        compiler_params=pltpu.CompilerParams(vmem_limit_bytes=4 << 20),
+def finish(blocks, groups):
+    count, tokens, columns = blocks.shape
+    parts = count // groups
+
+    def body(blocks_ref, out_ref):
+        for g in range(groups):
+            total = blocks_ref[g * parts].astype(jnp.float32)
+            for i in range(1, parts):
+                total = total + blocks_ref[g * parts + i].astype(jnp.float32)
+            out_ref[:, g * columns : (g + 1) * columns] = total.astype(out_ref.dtype)
+
+    return pl.pallas_call(
+        body,
+        out_shape=jax.ShapeDtypeStruct((tokens, groups * columns), blocks.dtype),
+        in_specs=[pl.BlockSpec(memory_space=pltpu.VMEM)],
+        out_specs=pl.BlockSpec(memory_space=pltpu.VMEM),
+        compiler_params=pltpu.CompilerParams(vmem_limit_bytes=blocks.nbytes + (4 << 20)),
         name="finish",
-    )(*flat)
+    )(blocks)
 
 
 def local(tokens, expert_ids, gate_probs, w_gate, w_up, w_down):
@@ -295,21 +299,18 @@
     shape = (token_count, w_down.shape[2])
     rest = [(g, h) for g in range(groups) for h in range(0, high, 2)]
     slot = lambda g, y, h: (((g & 1) * 2 + y) * wide + (g >> 1)) * high + h
-    plan = [[slot(g, y, h + z) for g, h in rest] for y, z in ((0, 0), (1, 0), (0, 1), (1, 1))]
-    mine, *away = sum_stage([kept, swap(sent, 0, 1)], plan, shape, jnp.bfloat16)
-    inputs = [mine] + [swap(value, 0, mask) for value, mask in zip(away, (2, 4, 6))]
-    mine, *away = sum_stage(inputs, [[i] for i in range(len(rest))], shape, jnp.bfloat16)
-    sums = [[] for _ in range(groups)]
-    sums[0].append(mine)
-    for value, (g, h) in zip(away, rest[1:]):
-        sums[g].append(swap(value, g, 4 * h))
-    return finish(sums, groups, tokens.dtype)
+    plan = [[slot(g, y, h + z) for g, h in rest] for y, z in ((0, 0), (1, 1), (0, 1), (1, 0))]
+    mine, *away = add_blocks([kept, swap(sent, 0, 1)], plan, shape, jnp.bfloat16, False)
+    inputs = [mine] + [swap(value, 0, mask) for value, mask in zip(away, (6, 4, 2))]
+    (blocks,) = add_blocks(inputs, [range(len(rest))], shape, jnp.bfloat16, True)
+    blocks = lax.all_to_all(blocks, ("dp", "far"), split_axis=0, concat_axis=0, tiled=True)
+    return finish(blocks, groups)
 
 
 def solution(mesh):
     groups, experts = mesh.devices.shape
-    split = Mesh(mesh.devices.reshape(groups, experts // 2, 2), ("dp", "far", "core"))
-    row, expert = P(("dp", "far", "core"), None), P(EXPERT, None, "dp")
+    split = Mesh(mesh.devices.reshape(groups, experts // 8, 4, 2), ("dp",) + EXPERT)
+    row, expert = P(("dp",) + EXPERT, None), P(EXPERT, None, "dp")
     return jax.shard_map(
         local,
         mesh=split,

time: 50.1 us -> 51.2 us (1.022)
  blocking collectives: 0 us -> 9.95 us
  waiting for transfers between devices: 23.2 us -> 18.7 us
  starting transfers between devices: 19.6 us -> 15.2 us
    all_to_all x0 -> x1, blocking collectives: none -> 9.95 us  [local(): lax.all_to_all(blocks, ('dp', 'far'), split_axis=0, concat_axis=0, tiled=...]
    ppermute x16 -> x13, waiting for transfers between devices: 23.2 us -> 18.7 us  [swap(): return lax.ppermute(value, ('dp',) + EXPERT, pairs)]
    ppermute x16 -> x13, starting transfers between devices: 19.6 us -> 15.2 us  [swap(): return lax.ppermute(value, ('dp',) + EXPERT, pairs)]
  transfers between devices with their start and end apart: 16 -> 13, of which waited for: 15 -> 12; matrix products, arithmetic and copies ran while one was open for 0% -> 0% of each run, Pallas kernels for 6% -> 6%
where the time goes in v11:
time: 51.2 us; the launch traced here: 51 us
  waiting for transfers between devices  18.7 us (37%)
  starting transfers between devices  15.2 us (30%)
  blocking collectives  9.95 us (19%)
  Pallas kernels  6.89 us (13%)
    ppermute x13, waiting for transfers between devices, swap(): return lax.ppermute(value, ('dp',) + EXPERT, pairs)  18.7 us
    ppermute x13, starting transfers between devices, swap(): return lax.ppermute(value, ('dp',) + EXPERT, pairs)  15.2 us
    all_to_all x1, blocking collectives, local(): lax.all_to_all(blocks, ('dp', 'far'), split_axis=0, concat_axis=0, tiled=...  9.95 us
    pallas_call x2, Pallas kernels, expand_rows(): pl.pallas_call(body, out_shape=jax.ShapeDtypeStruct((count, columns), row...  2.78 us
    pallas_call x4, Pallas kernels, contract_hidden(): pl.pallas_call(body, out_shape=jax.ShapeDtypeStruct((count, width), kind)...  2.16 us
  transfers between devices with their start and end apart: 13, of which 12 were waited for; matrix products, arithmetic and copies ran while one was open for 0% of the time, Pallas kernels for 6%

profile of v11, /device:TPU:0, one launch (start us, length us, event | category | flops | bytes accessed | tf_op | source)
XLA Modules:
  0.0 51.0 jit_solution(1252604243402673874)
XLA Ops:
  0.0 0.0 copy-start
  0.0 0.0 copy-start.1
  0.0 1.0 %pack_block.1.refs_0_ = bf16[4,4224]{1,0:T(4,128)(2,1)S(1)} custom-call(bf16[4,4096]{1,0:T(4,128)(2,1)} %tokens_ref.1, s32[4,8]{1,0:T(4,128)} %ids_ref.1, f32[4,8]{1,0:T(4,128)} %probs_ref.1), custom_call_target="tpu_custom_call" | custom-call | flops 60000002048 | tf_op jit(solution)/shard_map/pack_block/pallas_call | solution.py:63
  1.0 5.1 %collective-permute-start.2 = (bf16[4,4224]{1,0:T(4,128)(2,1)S(1)}, bf16[4,4224]{1,0:T(4,128)(2,1)S(1)}, u32[]{:S(2)}, u32[]{:S(2)}) collective-permute-start(bf16[4,4224]{1,0:T(4,128)(2,1)S(1)} %pack_block.1.refs_0_), channel_id=1, source_target_pairs={{0,12},{1,13},{2,14},{3,15},{4,8},{5,9},{6,10},{7,11},{8,4},{9,5},... | collective-permute-start | bytes 101384 | tf_op jit(solution)/shard_map/ppermute | solution.py:23
  6.1 0.0 collective-permute-start.1
  6.1 0.6 %collective-permute-start = (bf16[4,4224]{1,0:T(4,128)(2,1)S(1)}, bf16[4,4224]{1,0:T(4,128)(2,1)S(1)}, u32[]{:S(2)}, u32[]{:S(2)}) collective-permute-start(bf16[4,4224]{1,0:T(4,128)(2,1)S(1)} %pack_block.1.refs_0_), channel_id=1, source_target_pairs={{0,4},{1,5},{2,6},{3,7},{4,0},{5,1},{6,2},{7,3},{8,12},{9,13},{10,... | collective-permute-start | bytes 101384 | tf_op jit(solution)/shard_map/ppermute | solution.py:23
  6.8 1.3 %collective-permute-done.2.refs_3_ = bf16[4,4224]{1,0:T(4,128)(2,1)S(1)} collective-permute-done((bf16[4,4224]{1,0:T(4,128)(2,1)S(1)}, bf16[4,4224]{1,0:T(4,128)(2,1)S(1)}, u32[]{:S(2)}, u32[]{:S(2)}) %collective-permute-start.2) | collective-permute-done | bytes 33824 | tf_op jit(solution)/shard_map/ppermute | solution.py:23
  8.0 2.9 %collective-permute-done.1.refs_2_ = bf16[4,4224]{1,0:T(4,128)(2,1)S(1)} collective-permute-done((bf16[4,4224]{1,0:T(4,128)(2,1)S(1)}, bf16[4,4224]{1,0:T(4,128)(2,1)S(1)}, u32[]{:S(2)}, u32[]{:S(2)}) %collective-permute-start.1) | collective-permute-done | bytes 33824 | tf_op jit(solution)/shard_map/ppermute | solution.py:23
  11.0 0.0 collective-permute-done.refs_1_
  11.0 2.5 %collective-permute-start.5 = (bf16[4,4,4224]{2,1,0:T(4,128)(2,1)S(1)}, bf16[4,4,4224]{2,1,0:T(4,128)(2,1)S(1)}, u32[]{:S(2)}, u32[]{:S(2)}) collective-permute-start(bf16[4,4,4224]{2,1,0:T(4,128)(2,1)S(1)} %stack_blocks.1.refs_0_), channel_id=1, source_target_pairs={{0,18},{1,19},{2,16},{3,17},{4,22},{5,23},{6,20},{7,21},{8,26},{9,... | collective-permute-start | bytes 405512 | tf_op jit(solution)/shard_map/ppermute | solution.py:23
  13.5 0.5 %collective-permute-start.4 = (bf16[4,4,4224]{2,1,0:T(4,128)(2,1)S(1)}, bf16[4,4,4224]{2,1,0:T(4,128)(2,1)S(1)}, u32[]{:S(2)}, u32[]{:S(2)}) collective-permute-start(bf16[4,4,4224]{2,1,0:T(4,128)(2,1)S(1)} %stack_blocks.1.refs_0_), channel_id=1, source_target_pairs={{0,16},{1,17},{2,18},{3,19},{4,20},{5,21},{6,22},{7,23},{8,24},{9,... | collective-permute-start | bytes 405512 | tf_op jit(solution)/shard_map/ppermute | solution.py:23
  14.0 0.5 collective-permute-start.3
  14.5 2.8 %collective-permute-done.5.refs_3_ = bf16[4,4,4224]{2,1,0:T(4,128)(2,1)S(1)} collective-permute-done((bf16[4,4,4224]{2,1,0:T(4,128)(2,1)S(1)}, bf16[4,4,4224]{2,1,0:T(4,128)(2,1)S(1)}, u32[]{:S(2)}, u32[]{:S(2)}) %collective-permute-start.5) | collective-permute-done | bytes 135200 | tf_op jit(solution)/shard_map/ppermute | solution.py:23
  17.4 1.4 %collective-permute-done.4.refs_2_ = bf16[4,4,4224]{2,1,0:T(4,128)(2,1)S(1)} collective-permute-done((bf16[4,4,4224]{2,1,0:T(4,128)(2,1)S(1)}, bf16[4,4,4224]{2,1,0:T(4,128)(2,1)S(1)}, u32[]{:S(2)}, u32[]{:S(2)}) %collective-permute-start.4) | collective-permute-done | bytes 135200 | tf_op jit(solution)/shard_map/ppermute | solution.py:23
  18.8 0.2 collective-permute-done.3.refs_1_
  19.0 0.1 join_rows.1
  19.2 0.1 collective-permute-start.6
  19.3 1.9 %collective-permute-done.6 = bf16[64,4224]{1,0:T(8,128)(2,1)S(1)} collective-permute-done((bf16[64,4224]{1,0:T(8,128)(2,1)S(1)}, bf16[64,4224]{1,0:T(8,128)(2,1)S(1)}, u32[]{:S(2)}, u32[]{:S(2)}) %collective-permute-start.6) | collective-permute-done | bytes 540704 | tf_op jit(solution)/shard_map/ppermute | solution.py:23
  21.2 0.1 pad_maximum_fusion.rows_ref.refs_3_
  21.3 0.0 copy-done
  21.3 0.0 copy-done.1
  21.3 0.0 slice-start
  21.3 1.4 %expand_rows.2.refs_0_ = bf16[128,512]{1,0:T(8,128)(2,1)S(1)} custom-call(bf16[128,4224]{1,0:T(8,128)(2,1)S(1)} %pad_maximum_fusion.rows_ref.refs_3_, bf16[4096,1024]{1,0:T(8,128)(2,1)S(1)} %bitcast.9, bf16[4096,1024]{1,0:T(8,128)(2,1)S(1)} %bitcast.11), custom_call_target="tpu_custom_call" | custom-call | bytes 65536 | tf_op jit(solution)/shard_map/expand_rows/pallas_call | solution.py:128
  22.7 0.0 slice-start.1
  22.7 1.5 %collective-permute-start.8 = (bf16[128,512]{1,0:T(8,128)(2,1)S(1)}, bf16[128,512]{1,0:T(8,128)(2,1)S(1)}, u32[]{:S(2)}, u32[]{:S(2)}) collective-permute-start(bf16[128,512]{1,0:T(8,128)(2,1)S(1)} %expand_rows.2.refs_0_), channel_id=1, source_target_pairs={{0,16},{1,17},{2,18},{3,19},{4,20},{5,21},{6,22},{7,23},{8,24},{9,... | collective-permute-start | bytes 393224 | tf_op jit(solution)/shard_map/ppermute | solution.py:23
  24.2 1.4 %expand_rows.3.refs_1_ = bf16[128,512]{1,0:T(8,128)(2,1)S(1)} custom-call(bf16[128,4224]{1,0:T(8,128)(2,1)S(1)} %pad_maximum_fusion.rows_ref.refs_3_, bf16[4096,1024]{1,0:T(8,128)(2,1)S(1)} %bitcast.10, bf16[4096,1024]{1,0:T(8,128)(2,1)S(1)} %bitcast.12), custom_call_target="tpu_custom_call" | custom-call | bytes 65536 | tf_op jit(solution)/shard_map/expand_rows/pallas_call | solution.py:128
  25.6 0.6 %collective-permute-start.7 = (bf16[128,512]{1,0:T(8,128)(2,1)S(1)}, bf16[128,512]{1,0:T(8,128)(2,1)S(1)}, u32[]{:S(2)}, u32[]{:S(2)}) collective-permute-start(bf16[128,512]{1,0:T(8,128)(2,1)S(1)} %expand_rows.3.refs_1_), channel_id=1, source_target_pairs={{0,16},{1,17},{2,18},{3,19},{4,20},{5,21},{6,22},{7,23},{8,24},{9,... | collective-permute-start | bytes 393224 | tf_op jit(solution)/shard_map/ppermute | solution.py:23
  26.3 0.0 slice-done
  26.3 0.0 slice-done.1
  26.3 0.7 %contract_hidden.4.refs_2_ = f32[128,2048]{1,0:T(8,128)S(1)} custom-call(bf16[128,512]{1,0:T(8,128)(2,1)S(1)} %expand_rows.2.refs_0_, bf16[128,512]{1,0:T(8,128)(2,1)S(1)} %expand_rows.3.refs_1_, bf16[2048,2048]{1,0:T(8,128)(2,1)S(1)} %bitcast.5), custom_call_target="tpu_custom_call" | custom-call | bytes 262144 | tf_op jit(solution)/shard_map/contract_hidden/pallas_call | solution.py:184
  27.0 1.4 %collective-permute-done.8.refs_0_ = bf16[128,512]{1,0:T(8,128)(2,1)S(1)} collective-permute-done((bf16[128,512]{1,0:T(8,128)(2,1)S(1)}, bf16[128,512]{1,0:T(8,128)(2,1)S(1)}, u32[]{:S(2)}, u32[]{:S(2)}) %collective-permute-start.8) | collective-permute-done | bytes 131104 | tf_op jit(solution)/shard_map/ppermute | solution.py:23
  28.4 0.5 contract_hidden.5.refs_2_
  28.8 2.3 %collective-permute-done.7.refs_0_ = bf16[128,512]{1,0:T(8,128)(2,1)S(1)} collective-permute-done((bf16[128,512]{1,0:T(8,128)(2,1)S(1)}, bf16[128,512]{1,0:T(8,128)(2,1)S(1)}, u32[]{:S(2)}, u32[]{:S(2)}) %collective-permute-start.7) | collective-permute-done | bytes 131104 | tf_op jit(solution)/shard_map/ppermute | solution.py:23
  31.1 0.5 contract_hidden.7
  31.6 0.1 collective-permute-start.9
  31.7 0.5 contract_hidden.6.refs_0_
  32.2 1.0 %collective-permute-done.9.refs_1_ = bf16[64,2048]{1,0:T(8,128)(2,1)S(1)} collective-permute-done((bf16[64,2048]{1,0:T(8,128)(2,1)S(1)}, bf16[64,2048]{1,0:T(8,128)(2,1)S(1)}, u32[]{:S(2)}, u32[]{:S(2)}) %collective-permute-start.9) | collective-permute-done | bytes 262176 | tf_op jit(solution)/shard_map/ppermute | solution.py:23
  33.2 0.1 add_blocks.2
  33.3 0.8 %collective-permute-start.10 = (bf16[4,4,2048]{2,1,0:T(4,128)(2,1)S(1)}, bf16[4,4,2048]{2,1,0:T(4,128)(2,1)S(1)}, u32[]{:S(2)}, u32[]{:S(2)}) collective-permute-start(bf16[4,4,2048]{2,1,0:T(4,128)(2,1)S(1)} %get-tuple-element.22), channel_id=1, source_target_pairs={{0,6},{1,7},{2,4},{3,5},{4,2},{5,3},{6,0},{7,1},{8,14},{9,15},{10,... | collective-permute-start | bytes 196616 | tf_op jit(solution)/shard_map/ppermute | solution.py:23
  34.1 1.9 %collective-permute-start.11 = (bf16[4,4,2048]{2,1,0:T(4,128)(2,1)S(1)}, bf16[4,4,2048]{2,1,0:T(4,128)(2,1)S(1)}, u32[]{:S(2)}, u32[]{:S(2)}) collective-permute-start(bf16[4,4,2048]{2,1,0:T(4,128)(2,1)S(1)} %get-tuple-element.23), channel_id=1, source_target_pairs={{0,4},{1,5},{2,6},{3,7},{4,0},{5,1},{6,2},{7,3},{8,12},{9,13},{10,... | collective-permute-start | bytes 196616 | tf_op jit(solution)/shard_map/ppermute | solution.py:23
  36.1 0.8 %collective-permute-start.12 = (bf16[4,4,2048]{2,1,0:T(4,128)(2,1)S(1)}, bf16[4,4,2048]{2,1,0:T(4,128)(2,1)S(1)}, u32[]{:S(2)}, u32[]{:S(2)}) collective-permute-start(bf16[4,4,2048]{2,1,0:T(4,128)(2,1)S(1)} %get-tuple-element.24), channel_id=1, source_target_pairs={{0,2},{1,3},{2,0},{3,1},{4,6},{5,7},{6,4},{7,5},{8,10},{9,11},{10,... | collective-permute-start | bytes 196616 | tf_op jit(solution)/shard_map/ppermute | solution.py:23
  36.9 2.4 %collective-permute-done.10.refs_1_ = bf16[4,4,2048]{2,1,0:T(4,128)(2,1)S(1)} collective-permute-done((bf16[4,4,2048]{2,1,0:T(4,128)(2,1)S(1)}, bf16[4,4,2048]{2,1,0:T(4,128)(2,1)S(1)}, u32[]{:S(2)}, u32[]{:S(2)}) %collective-permute-start.10) | collective-permute-done | bytes 65568 | tf_op jit(solution)/shard_map/ppermute | solution.py:23
  39.2 0.3 collective-permute-done.11.refs_2_
  39.6 0.8 %collective-permute-done.12.refs_3_ = bf16[4,4,2048]{2,1,0:T(4,128)(2,1)S(1)} collective-permute-done((bf16[4,4,2048]{2,1,0:T(4,128)(2,1)S(1)}, bf16[4,4,2048]{2,1,0:T(4,128)(2,1)S(1)}, u32[]{:S(2)}, u32[]{:S(2)}) %collective-permute-start.12) | collective-permute-done | bytes 65568 | tf_op jit(solution)/shard_map/ppermute | solution.py:23
  40.4 10.0 %all_to_all.5.blocks_ref = bf16[4,4,2048]{2,1,0:T(4,128)(2,1)S(1)} all-to-all(bf16[4,4,2048]{2,1,0:T(4,128)(2,1)S(1)} %add_blocks.3), channel_id=1, replica_groups=mesh['dp'=2,'far'=2,'near'=4,'core'=2] {'dp','far'}, dimensions={0} | all-to-all | bytes 131072 | tf_op jit(solution)/shard_map/all_to_all | solution.py:306
  50.3 0.6 %finish.1 = bf16[4,4096]{1,0:T(4,128)(2,1)} custom-call(bf16[4,4,2048]{2,1,0:T(4,128)(2,1)S(1)} %all_to_all.5.blocks_ref), custom_call_target="tpu_custom_call" | custom-call | tf_op jit(solution)/shard_map/finish/pallas_call | solution.py:244
  (3 shorter events, 0.1 us)
Async XLA Ops:
  0.0 21.3 %copy-start = (bf16[1,4096,1024]{2,1,0:T(8,128)(2,1)S(1)}, bf16[1,4096,1024]{2,1,0:T(8,128)(2,1)}, u32[]{:S(2)}) copy-start(bf16[1,4096,1024]{2,1,0:T(8,128)(2,1)} %param.9) | copy-start | bytes 25165828
  0.0 21.3 %copy-start.1 = (bf16[1,4096,1024]{2,1,0:T(8,128)(2,1)S(1)}, bf16[1,4096,1024]{2,1,0:T(8,128)(2,1)}, u32[]{:S(2)}) copy-start(bf16[1,4096,1024]{2,1,0:T(8,128)(2,1)} %param.10) | copy-start | bytes 25165828
  1.0 7.0 %collective-permute-start.2 = (bf16[4,4224]{1,0:T(4,128)(2,1)S(1)}, bf16[4,4224]{1,0:T(4,128)(2,1)S(1)}, u32[]{:S(2)}, u32[]{:S(2)}) collective-permute-start(bf16[4,4224]{1,0:T(4,128)(2,1)S(1)} %pack_block.1.refs_0_), channel_id=1, source_target_pairs={{0,12},{1,13},{2,14},{3,15},{4,8},{5,9},{6,10},{7,11},{8,4},{9,5},... | collective-permute-start | bytes 101384 | tf_op jit(solution)/shard_map/ppermute | solution.py:23
  6.1 4.8 %collective-permute-start.1 = (bf16[4,4224]{1,0:T(4,128)(2,1)S(1)}, bf16[4,4224]{1,0:T(4,128)(2,1)S(1)}, u32[]{:S(2)}, u32[]{:S(2)}) collective-permute-start(bf16[4,4224]{1,0:T(4,128)(2,1)S(1)} %pack_block.1.refs_0_), channel_id=1, source_target_pairs={{0,8},{1,9},{2,10},{3,11},{4,12},{5,13},{6,14},{7,15},{8,0},{9,1},... | collective-permute-start | bytes 101384 | tf_op jit(solution)/shard_map/ppermute | solution.py:23
  6.1 4.8 %collective-permute-start = (bf16[4,4224]{1,0:T(4,128)(2,1)S(1)}, bf16[4,4224]{1,0:T(4,128)(2,1)S(1)}, u32[]{:S(2)}, u32[]{:S(2)}) collective-permute-start(bf16[4,4224]{1,0:T(4,128)(2,1)S(1)} %pack_block.1.refs_0_), channel_id=1, source_target_pairs={{0,4},{1,5},{2,6},{3,7},{4,0},{5,1},{6,2},{7,3},{8,12},{9,13},{10,... | collective-permute-start | bytes 101384 | tf_op jit(solution)/shard_map/ppermute | solution.py:23
  11.0 6.4 %collective-permute-start.5 = (bf16[4,4,4224]{2,1,0:T(4,128)(2,1)S(1)}, bf16[4,4,4224]{2,1,0:T(4,128)(2,1)S(1)}, u32[]{:S(2)}, u32[]{:S(2)}) collective-permute-start(bf16[4,4,4224]{2,1,0:T(4,128)(2,1)S(1)} %stack_blocks.1.refs_0_), channel_id=1, source_target_pairs={{0,18},{1,19},{2,16},{3,17},{4,22},{5,23},{6,20},{7,21},{8,26},{9,... | collective-permute-start | bytes 405512 | tf_op jit(solution)/shard_map/ppermute | solution.py:23
  13.5 5.3 %collective-permute-start.4 = (bf16[4,4,4224]{2,1,0:T(4,128)(2,1)S(1)}, bf16[4,4,4224]{2,1,0:T(4,128)(2,1)S(1)}, u32[]{:S(2)}, u32[]{:S(2)}) collective-permute-start(bf16[4,4,4224]{2,1,0:T(4,128)(2,1)S(1)} %stack_blocks.1.refs_0_), channel_id=1, source_target_pairs={{0,16},{1,17},{2,18},{3,19},{4,20},{5,21},{6,22},{7,23},{8,24},{9,... | collective-permute-start | bytes 405512 | tf_op jit(solution)/shard_map/ppermute | solution.py:23
  14.0 5.0 %collective-permute-start.3 = (bf16[4,4,4224]{2,1,0:T(4,128)(2,1)S(1)}, bf16[4,4,4224]{2,1,0:T(4,128)(2,1)S(1)}, u32[]{:S(2)}, u32[]{:S(2)}) collective-permute-start(bf16[4,4,4224]{2,1,0:T(4,128)(2,1)S(1)} %stack_blocks.1.refs_0_), channel_id=1, source_target_pairs={{0,2},{1,3},{2,0},{3,1},{4,6},{5,7},{6,4},{7,5},{8,10},{9,11},{10,... | collective-permute-start | bytes 405512 | tf_op jit(solution)/shard_map/ppermute | solution.py:23
  19.2 2.0 %collective-permute-start.6 = (bf16[64,4224]{1,0:T(8,128)(2,1)S(1)}, bf16[64,4224]{1,0:T(8,128)(2,1)S(1)}, u32[]{:S(2)}, u32[]{:S(2)}) collective-permute-start(bf16[64,4224]{1,0:T(8,128)(2,1)S(1)} %join_rows.1), channel_id=1, source_target_pairs={{0,1},{1,0},{2,3},{3,2},{4,5},{5,4},{6,7},{7,6},{8,9},{9,8},{10,11... | collective-permute-start | bytes 1622024 | tf_op jit(solution)/shard_map/ppermute | solution.py:23
  21.3 5.0 %slice-start = ((s8[8388608]{0:T(1024)(128)(4,1)}), s8[4194304]{0:T(1024)(128)(4,1)S(1)}, s32[]{:S(2)}) async-start(s8[8388608]{0:T(1024)(128)(4,1)} %bitcast.3), calls=%async_computation.1 | async-start | bytes 8388608
  22.7 3.6 %slice-start.1 = ((s8[8388608]{0:T(1024)(128)(4,1)}), s8[4194304]{0:T(1024)(128)(4,1)S(1)}, s32[]{:S(2)}) async-start(s8[8388608]{0:T(1024)(128)(4,1)} %bitcast.3), calls=%async_computation.2 | async-start | bytes 8388608
  22.7 5.7 %collective-permute-start.8 = (bf16[128,512]{1,0:T(8,128)(2,1)S(1)}, bf16[128,512]{1,0:T(8,128)(2,1)S(1)}, u32[]{:S(2)}, u32[]{:S(2)}) collective-permute-start(bf16[128,512]{1,0:T(8,128)(2,1)S(1)} %expand_rows.2.refs_0_), channel_id=1, source_target_pairs={{0,16},{1,17},{2,18},{3,19},{4,20},{5,21},{6,22},{7,23},{8,24},{9,... | collective-permute-start | bytes 393224 | tf_op jit(solution)/shard_map/ppermute | solution.py:23
  25.6 5.5 %collective-permute-start.7 = (bf16[128,512]{1,0:T(8,128)(2,1)S(1)}, bf16[128,512]{1,0:T(8,128)(2,1)S(1)}, u32[]{:S(2)}, u32[]{:S(2)}) collective-permute-start(bf16[128,512]{1,0:T(8,128)(2,1)S(1)} %expand_rows.3.refs_1_), channel_id=1, source_target_pairs={{0,16},{1,17},{2,18},{3,19},{4,20},{5,21},{6,22},{7,23},{8,24},{9,... | collective-permute-start | bytes 393224 | tf_op jit(solution)/shard_map/ppermute | solution.py:23
  31.6 1.6 %collective-permute-start.9 = (bf16[64,2048]{1,0:T(8,128)(2,1)S(1)}, bf16[64,2048]{1,0:T(8,128)(2,1)S(1)}, u32[]{:S(2)}, u32[]{:S(2)}) collective-permute-start(bf16[64,2048]{1,0:T(8,128)(2,1)S(1)} %contract_hidden.7), channel_id=1, source_target_pairs={{0,1},{1,0},{2,3},{3,2},{4,5},{5,4},{6,7},{7,6},{8,9},{9,8},{10,11... | collective-permute-start | bytes 786440 | tf_op jit(solution)/shard_map/ppermute | solution.py:23
  33.3 5.9 %collective-permute-start.10 = (bf16[4,4,2048]{2,1,0:T(4,128)(2,1)S(1)}, bf16[4,4,2048]{2,1,0:T(4,128)(2,1)S(1)}, u32[]{:S(2)}, u32[]{:S(2)}) collective-permute-start(bf16[4,4,2048]{2,1,0:T(4,128)(2,1)S(1)} %get-tuple-element.22), channel_id=1, source_target_pairs={{0,6},{1,7},{2,4},{3,5},{4,2},{5,3},{6,0},{7,1},{8,14},{9,15},{10,... | collective-permute-start | bytes 196616 | tf_op jit(solution)/shard_map/ppermute | solution.py:23
  34.1 5.4 %collective-permute-start.11 = (bf16[4,4,2048]{2,1,0:T(4,128)(2,1)S(1)}, bf16[4,4,2048]{2,1,0:T(4,128)(2,1)S(1)}, u32[]{:S(2)}, u32[]{:S(2)}) collective-permute-start(bf16[4,4,2048]{2,1,0:T(4,128)(2,1)S(1)} %get-tuple-element.23), channel_id=1, source_target_pairs={{0,4},{1,5},{2,6},{3,7},{4,0},{5,1},{6,2},{7,3},{8,12},{9,13},{10,... | collective-permute-start | bytes 196616 | tf_op jit(solution)/shard_map/ppermute | solution.py:23
  36.1 4.3 %collective-permute-start.12 = (bf16[4,4,2048]{2,1,0:T(4,128)(2,1)S(1)}, bf16[4,4,2048]{2,1,0:T(4,128)(2,1)S(1)}, u32[]{:S(2)}, u32[]{:S(2)}) collective-permute-start(bf16[4,4,2048]{2,1,0:T(4,128)(2,1)S(1)} %get-tuple-element.24), channel_id=1, source_target_pairs={{0,2},{1,3},{2,0},{3,1},{4,6},{5,7},{6,4},{7,5},{8,10},{9,11},{10,... | collective-permute-start | bytes 196616 | tf_op jit(solution)/shard_map/ppermute | solution.py:23

commit v12 on v10

--- a/solution.py
+++ b/solution.py
@@ -10,10 +10,20 @@
 TILE = 256
 BATCH = 128
 LANES = 128
+X, Y = (1, 1), (0, 3)
 EXPERT = ("far", "core")
 
 
-def swap(value, group_mask, expert_mask):
+def far(i):
+    return (0, 4 * i + bin(i).count("1") % 2)
+
+
+def both(a, b):
+    return (a[0] ^ b[0], a[1] ^ b[1])
+
+
+def swap(value, masks):
+    group_mask, expert_mask = masks
     groups, experts = lax.axis_size("dp"), lax.axis_size(EXPERT)
     pairs = [
         (g * experts + e, (g ^ group_mask) * experts + (e ^ expert_mask))
@@ -155,12 +165,13 @@
 
         def step(first, batch):
             here = pl.ds(offset + first, batch)
-            lefts = [ref[here, :] for ref in part_refs]
-            if half is not None:
-                order = [i ^ 1 for i in range(count // half)]
+            if half is None:
+                lefts = [ref[here, :] for ref in part_refs]
+            else:
+                order = [i ^ 3 for i in range(offset // half, (offset + count) // half)]
                 lefts = [
-                    jnp.concatenate([left[i * half : (i + 1) * half] for i in order])
-                    for left in lefts
+                    jnp.concatenate([ref[i * half : (i + 1) * half, :] for i in order])
+                    for ref in part_refs
                 ]
             if rows is not None:
                 table = rows_ref[here, rows.shape[1] - LANES :].astype(jnp.float32)
@@ -256,22 +267,24 @@
     units = w_up.shape[2]
     weights = lax.optimization_barrier((block, w_gate[0], w_up[0], w_down[0]))
     block, gate_weights, up_weights, down_weights = weights
-    near = stack_blocks([block] + [swap(block, 0, 4 * i) for i in range(1, high)])
+    near = stack_blocks([block] + [swap(block, far(i)) for i in range(1, high)])
     if wide > 1:
-        near = jnp.concatenate([near] + [swap(near, 2 * i, 0) for i in range(1, wide)])
-    chip = join_rows([near, swap(near, 0, 2), swap(near, 1, 0), swap(near, 1, 2)])
-    rows = jnp.concatenate([chip, swap(chip, 0, 1)])
+        near = jnp.concatenate([near] + [swap(near, (2 * i, 0)) for i in range(1, wide)])
+    chip = join_rows([near, swap(near, Y), swap(near, X), swap(near, both(X, Y))])
+    rows = jnp.concatenate([chip, swap(chip, (0, 1))])
 
     chunks = CHUNKS if units % (LANES * CHUNKS) == 0 else 1
     step = units // chunks
     half = rows.shape[0] // 4 if groups == 2 and rows.shape[0] <= BATCH else None
 
     def from_group(value, mask):
-        value = swap(value, mask, 0)
+        value = swap(value, (mask, 0))
         if half is not None:
             return value
         value = value.reshape(2, 2, 2, wide, high * token_count, step)
-        value = jnp.stack([value[:, i ^ (mask & 1)] for i in range(2)], axis=1)
+        for axis in range(2):
+            order = [i ^ (mask & 1) for i in range(2)]
+            value = jnp.stack([lax.index_in_dim(value, i, axis, False) for i in order], axis)
         value = jnp.stack([value[:, :, :, i ^ (mask >> 1)] for i in range(wide)], axis=3)
         return value.reshape(-1, step)
 
@@ -295,14 +308,17 @@
     shape = (token_count, w_down.shape[2])
     rest = [(g, h) for g in range(groups) for h in range(0, high, 2)]
     slot = lambda g, y, h: (((g & 1) * 2 + y) * wide + (g >> 1)) * high + h
-    plan = [[slot(g, y, h + z) for g, h in rest] for y, z in ((0, 0), (1, 0), (0, 1), (1, 1))]
-    mine, *away = sum_stage([kept, swap(sent, 0, 1)], plan, shape, jnp.bfloat16)
-    inputs = [mine] + [swap(value, 0, mask) for value, mask in zip(away, (2, 4, 6))]
-    mine, *away = sum_stage(inputs, [[i] for i in range(len(rest))], shape, jnp.bfloat16)
+    plan = [[slot(g, y, h + z) for g, h in rest] for y, z in ((0, 0), (1, 1), (0, 1), (1, 0))]
+    mine, *away = sum_stage([kept, swap(sent, (0, 1))], plan, shape, jnp.bfloat16)
+    masks = (both(Y, far(1)), far(1), Y)
+    inputs = [mine] + [swap(value, mask) for value, mask in zip(away, masks)]
+    order = [0] + list(range(len(rest) - 1, 0, -1))
+    mine, *away = sum_stage(inputs, [[i] for i in order], shape, jnp.bfloat16)
     sums = [[] for _ in range(groups)]
     sums[0].append(mine)
-    for value, (g, h) in zip(away, rest[1:]):
-        sums[g].append(swap(value, g, 4 * h))
+    for value, (g, h) in zip(away, [rest[i] for i in order[1:]]):
+        mask = both((g - g % 2, 0), far(h))
+        sums[g].append(swap(value, both(mask, X) if g % 2 else mask))
     return finish(sums, groups, tokens.dtype)
 
 

time: 50.1 us -> 49.4 us (0.986)
  starting transfers between devices: 19.6 us -> 18.6 us
    ppermute x16, starting transfers between devices: 19.6 us -> 18.6 us  [swap(): return lax.ppermute(value, ('dp',) + EXPERT, pairs)]
  transfers between devices with their start and end apart: 16 -> 16, of which waited for: 15 -> 13; matrix products, arithmetic and copies ran while one was open for 0% -> 0% of each run, Pallas kernels for 6% -> 6%
where the time goes in v12:
time: 49.4 us; the launch traced here: 49.2 us
  waiting for transfers between devices  23.5 us (48%)
  starting transfers between devices  18.6 us (38%)
  Pallas kernels  6.86 us (14%)
    ppermute x16, waiting for transfers between devices, swap(): return lax.ppermute(value, ('dp',) + EXPERT, pairs)  23.5 us
    ppermute x16, starting transfers between devices, swap(): return lax.ppermute(value, ('dp',) + EXPERT, pairs)  18.6 us
    pallas_call x2, Pallas kernels, expand_rows(): pl.pallas_call(body, out_shape=jax.ShapeDtypeStruct((count, columns), row...  2.76 us
    pallas_call x4, Pallas kernels, contract_hidden(): pl.pallas_call(body, out_shape=jax.ShapeDtypeStruct((count, width), kind)...  2.17 us
    pallas_call x1, Pallas kernels, pack_block(): pl.pallas_call(body, out_shape=jax.ShapeDtypeStruct((count, width + LANES...  1.02 us
  transfers between devices with their start and end apart: 16, of which 13 were waited for; matrix products, arithmetic and copies ran while one was open for 0% of the time, Pallas kernels for 6%

profile of v12, /device:TPU:0, one launch (start us, length us, event | category | flops | bytes accessed | tf_op | source)
XLA Modules:
  0.0 49.2 jit_solution(9346112798156140110)
XLA Ops:
  0.0 1.0 %pack_block.1.refs_0_ = bf16[4,4224]{1,0:T(4,128)(2,1)S(1)} custom-call(bf16[4,4096]{1,0:T(4,128)(2,1)} %tokens_ref.1, s32[4,8]{1,0:T(4,128)} %ids_ref.1, f32[4,8]{1,0:T(4,128)} %probs_ref.1), custom_call_target="tpu_custom_call" | custom-call | flops 60000002048 | tf_op jit(solution)/shard_map/pack_block/pallas_call | solution.py:73
  1.0 5.1 %collective-permute-start.2 = (bf16[4,4224]{1,0:T(4,128)(2,1)S(1)}, bf16[4,4224]{1,0:T(4,128)(2,1)S(1)}, u32[]{:S(2)}, u32[]{:S(2)}) collective-permute-start(bf16[4,4224]{1,0:T(4,128)(2,1)S(1)} %pack_block.1.refs_0_), channel_id=1, source_target_pairs={{0,12},{1,13},{2,14},{3,15},{4,8},{5,9},{6,10},{7,11},{8,4},{9,5},... | collective-permute-start | bytes 101384 | tf_op jit(solution)/shard_map/ppermute | solution.py:33
  6.1 0.0 collective-permute-start.1
  6.1 0.4 collective-permute-start
  6.5 1.5 %collective-permute-done.2.refs_3_ = bf16[4,4224]{1,0:T(4,128)(2,1)S(1)} collective-permute-done((bf16[4,4224]{1,0:T(4,128)(2,1)S(1)}, bf16[4,4224]{1,0:T(4,128)(2,1)S(1)}, u32[]{:S(2)}, u32[]{:S(2)}) %collective-permute-start.2) | collective-permute-done | bytes 33824 | tf_op jit(solution)/shard_map/ppermute | solution.py:33
  8.0 2.4 %collective-permute-done.1.refs_2_ = bf16[4,4224]{1,0:T(4,128)(2,1)S(1)} collective-permute-done((bf16[4,4224]{1,0:T(4,128)(2,1)S(1)}, bf16[4,4224]{1,0:T(4,128)(2,1)S(1)}, u32[]{:S(2)}, u32[]{:S(2)}) %collective-permute-start.1) | collective-permute-done | bytes 33824 | tf_op jit(solution)/shard_map/ppermute | solution.py:33
  10.5 0.0 collective-permute-done.refs_1_
  10.5 2.5 %collective-permute-start.5 = (bf16[4,4,4224]{2,1,0:T(4,128)(2,1)S(1)}, bf16[4,4,4224]{2,1,0:T(4,128)(2,1)S(1)}, u32[]{:S(2)}, u32[]{:S(2)}) collective-permute-start(bf16[4,4,4224]{2,1,0:T(4,128)(2,1)S(1)} %stack_blocks.1.refs_0_), channel_id=1, source_target_pairs={{0,18},{1,19},{2,16},{3,17},{4,22},{5,23},{6,20},{7,21},{8,26},{9,... | collective-permute-start | bytes 405512 | tf_op jit(solution)/shard_map/ppermute | solution.py:33
  13.0 0.0 collective-permute-start.4
  13.0 0.8 %collective-permute-start.3 = (bf16[4,4,4224]{2,1,0:T(4,128)(2,1)S(1)}, bf16[4,4,4224]{2,1,0:T(4,128)(2,1)S(1)}, u32[]{:S(2)}, u32[]{:S(2)}) collective-permute-start(bf16[4,4,4224]{2,1,0:T(4,128)(2,1)S(1)} %stack_blocks.1.refs_0_), channel_id=1, source_target_pairs={{0,3},{1,2},{2,1},{3,0},{4,7},{5,6},{6,5},{7,4},{8,11},{9,10},{10,... | collective-permute-start | bytes 405512 | tf_op jit(solution)/shard_map/ppermute | solution.py:33
  13.8 3.9 %collective-permute-done.5.refs_3_ = bf16[4,4,4224]{2,1,0:T(4,128)(2,1)S(1)} collective-permute-done((bf16[4,4,4224]{2,1,0:T(4,128)(2,1)S(1)}, bf16[4,4,4224]{2,1,0:T(4,128)(2,1)S(1)}, u32[]{:S(2)}, u32[]{:S(2)}) %collective-permute-start.5) | collective-permute-done | bytes 135200 | tf_op jit(solution)/shard_map/ppermute | solution.py:33
  17.7 1.2 %collective-permute-done.4.refs_2_ = bf16[4,4,4224]{2,1,0:T(4,128)(2,1)S(1)} collective-permute-done((bf16[4,4,4224]{2,1,0:T(4,128)(2,1)S(1)}, bf16[4,4,4224]{2,1,0:T(4,128)(2,1)S(1)}, u32[]{:S(2)}, u32[]{:S(2)}) %collective-permute-start.4) | collective-permute-done | bytes 135200 | tf_op jit(solution)/shard_map/ppermute | solution.py:33
  18.9 0.5 collective-permute-done.3.refs_1_
  19.4 0.1 join_rows.1
  19.5 0.3 collective-permute-start.6
  19.8 1.7 %collective-permute-done.6 = bf16[64,4224]{1,0:T(8,128)(2,1)S(1)} collective-permute-done((bf16[64,4224]{1,0:T(8,128)(2,1)S(1)}, bf16[64,4224]{1,0:T(8,128)(2,1)S(1)}, u32[]{:S(2)}, u32[]{:S(2)}) %collective-permute-start.6) | collective-permute-done | bytes 540704 | tf_op jit(solution)/shard_map/ppermute | solution.py:33
  21.5 0.1 pad_maximum_fusion.rows_ref.refs_3_
  21.6 0.0 copy-done
  21.6 0.0 copy-done.1
  21.6 0.0 slice-start
  21.6 1.4 %expand_rows.2.refs_0_ = bf16[128,512]{1,0:T(8,128)(2,1)S(1)} custom-call(bf16[128,4224]{1,0:T(8,128)(2,1)S(1)} %pad_maximum_fusion.rows_ref.refs_3_, bf16[4096,1024]{1,0:T(8,128)(2,1)S(1)} %bitcast.9, bf16[4096,1024]{1,0:T(8,128)(2,1)S(1)} %bitcast.11), custom_call_target="tpu_custom_call" | custom-call | bytes 65536 | tf_op jit(solution)/shard_map/expand_rows/pallas_call | solution.py:138
  23.0 0.0 slice-start.1
  23.0 1.4 %collective-permute-start.8 = (bf16[128,512]{1,0:T(8,128)(2,1)S(1)}, bf16[128,512]{1,0:T(8,128)(2,1)S(1)}, u32[]{:S(2)}, u32[]{:S(2)}) collective-permute-start(bf16[128,512]{1,0:T(8,128)(2,1)S(1)} %expand_rows.2.refs_0_), channel_id=1, source_target_pairs={{0,16},{1,17},{2,18},{3,19},{4,20},{5,21},{6,22},{7,23},{8,24},{9,... | collective-permute-start | bytes 393224 | tf_op jit(solution)/shard_map/ppermute | solution.py:33
  24.4 1.4 %expand_rows.3.refs_1_ = bf16[128,512]{1,0:T(8,128)(2,1)S(1)} custom-call(bf16[128,4224]{1,0:T(8,128)(2,1)S(1)} %pad_maximum_fusion.rows_ref.refs_3_, bf16[4096,1024]{1,0:T(8,128)(2,1)S(1)} %bitcast.10, bf16[4096,1024]{1,0:T(8,128)(2,1)S(1)} %bitcast.12), custom_call_target="tpu_custom_call" | custom-call | bytes 65536 | tf_op jit(solution)/shard_map/expand_rows/pallas_call | solution.py:138
  25.8 0.8 %collective-permute-start.7 = (bf16[128,512]{1,0:T(8,128)(2,1)S(1)}, bf16[128,512]{1,0:T(8,128)(2,1)S(1)}, u32[]{:S(2)}, u32[]{:S(2)}) collective-permute-start(bf16[128,512]{1,0:T(8,128)(2,1)S(1)} %expand_rows.3.refs_1_), channel_id=1, source_target_pairs={{0,16},{1,17},{2,18},{3,19},{4,20},{5,21},{6,22},{7,23},{8,24},{9,... | collective-permute-start | bytes 393224 | tf_op jit(solution)/shard_map/ppermute | solution.py:33
  26.6 0.0 slice-done
  26.6 0.7 %contract_hidden.4.refs_2_ = f32[128,2048]{1,0:T(8,128)S(1)} custom-call(bf16[128,512]{1,0:T(8,128)(2,1)S(1)} %expand_rows.2.refs_0_, bf16[128,512]{1,0:T(8,128)(2,1)S(1)} %expand_rows.3.refs_1_, bf16[2048,2048]{1,0:T(8,128)(2,1)S(1)} %bitcast.5), custom_call_target="tpu_custom_call" | custom-call | bytes 262144 | tf_op jit(solution)/shard_map/contract_hidden/pallas_call | solution.py:195
  27.3 1.4 %collective-permute-done.8.refs_0_ = bf16[128,512]{1,0:T(8,128)(2,1)S(1)} collective-permute-done((bf16[128,512]{1,0:T(8,128)(2,1)S(1)}, bf16[128,512]{1,0:T(8,128)(2,1)S(1)}, u32[]{:S(2)}, u32[]{:S(2)}) %collective-permute-start.8) | collective-permute-done | bytes 131104 | tf_op jit(solution)/shard_map/ppermute | solution.py:33
  28.8 0.5 contract_hidden.5.refs_2_
  29.2 2.3 %collective-permute-done.7.refs_0_ = bf16[128,512]{1,0:T(8,128)(2,1)S(1)} collective-permute-done((bf16[128,512]{1,0:T(8,128)(2,1)S(1)}, bf16[128,512]{1,0:T(8,128)(2,1)S(1)}, u32[]{:S(2)}, u32[]{:S(2)}) %collective-permute-start.7) | collective-permute-done | bytes 131104 | tf_op jit(solution)/shard_map/ppermute | solution.py:33
  31.5 0.5 contract_hidden.7
  32.0 0.1 collective-permute-start.9
  32.1 0.5 %contract_hidden.6.refs_0_ = f32[64,2048]{1,0:T(8,128)S(1)} custom-call(bf16[128,512]{1,0:T(8,128)(2,1)S(1)} %collective-permute-done.7.refs_0_, bf16[2048,2048]{1,0:T(8,128)(2,1)S(1)} %bitcast.8, f32[128,2048]{1,0:T(8,128)S(1)} %contract_hidden.5.refs_2_, bf16[128,4224]{1,0:T(8,128)(2,1)S(1)} %pad_maximum_fusion.rows_ref.refs_3_), custom_call_target="tpu_custom_call" | custom-call | bytes 131072 | tf_op jit(solution)/shard_map/contract_hidden/pallas_call | solution.py:195
  32.6 1.0 %collective-permute-done.9.refs_1_ = bf16[64,2048]{1,0:T(8,128)(2,1)S(1)} collective-permute-done((bf16[64,2048]{1,0:T(8,128)(2,1)S(1)}, bf16[64,2048]{1,0:T(8,128)(2,1)S(1)}, u32[]{:S(2)}, u32[]{:S(2)}) %collective-permute-start.9) | collective-permute-done | bytes 262176 | tf_op jit(solution)/shard_map/ppermute | solution.py:33
  33.6 0.1 sum_stage.2
  33.7 1.5 %collective-permute-start.10 = (bf16[4,4,2048]{2,1,0:T(4,128)(2,1)S(1)}, bf16[4,4,2048]{2,1,0:T(4,128)(2,1)S(1)}, u32[]{:S(2)}, u32[]{:S(2)}) collective-permute-start(bf16[4,4,2048]{2,1,0:T(4,128)(2,1)S(1)} %get-tuple-element.26), channel_id=1, source_target_pairs={{0,6},{1,7},{2,4},{3,5},{4,2},{5,3},{6,0},{7,1},{8,14},{9,15},{10,... | collective-permute-start | bytes 196616 | tf_op jit(solution)/shard_map/ppermute | solution.py:33
  35.2 1.2 %collective-permute-start.11 = (bf16[4,4,2048]{2,1,0:T(4,128)(2,1)S(1)}, bf16[4,4,2048]{2,1,0:T(4,128)(2,1)S(1)}, u32[]{:S(2)}, u32[]{:S(2)}) collective-permute-start(bf16[4,4,2048]{2,1,0:T(4,128)(2,1)S(1)} %get-tuple-element.27), channel_id=1, source_target_pairs={{0,5},{1,4},{2,7},{3,6},{4,1},{5,0},{6,3},{7,2},{8,13},{9,12},{10,... | collective-permute-start | bytes 196616 | tf_op jit(solution)/shard_map/ppermute | solution.py:33
  36.4 0.6 %collective-permute-start.12 = (bf16[4,4,2048]{2,1,0:T(4,128)(2,1)S(1)}, bf16[4,4,2048]{2,1,0:T(4,128)(2,1)S(1)}, u32[]{:S(2)}, u32[]{:S(2)}) collective-permute-start(bf16[4,4,2048]{2,1,0:T(4,128)(2,1)S(1)} %get-tuple-element.28), channel_id=1, source_target_pairs={{0,3},{1,2},{2,1},{3,0},{4,7},{5,6},{6,5},{7,4},{8,11},{9,10},{10,... | collective-permute-start | bytes 196616 | tf_op jit(solution)/shard_map/ppermute | solution.py:33
  37.0 2.7 %collective-permute-done.10.refs_1_ = bf16[4,4,2048]{2,1,0:T(4,128)(2,1)S(1)} collective-permute-done((bf16[4,4,2048]{2,1,0:T(4,128)(2,1)S(1)}, bf16[4,4,2048]{2,1,0:T(4,128)(2,1)S(1)}, u32[]{:S(2)}, u32[]{:S(2)}) %collective-permute-start.10) | collective-permute-done | bytes 65568 | tf_op jit(solution)/shard_map/ppermute | solution.py:33
  39.7 0.0 collective-permute-done.11.refs_2_
  39.7 0.6 %collective-permute-done.12.refs_3_ = bf16[4,4,2048]{2,1,0:T(4,128)(2,1)S(1)} collective-permute-done((bf16[4,4,2048]{2,1,0:T(4,128)(2,1)S(1)}, bf16[4,4,2048]{2,1,0:T(4,128)(2,1)S(1)}, u32[]{:S(2)}, u32[]{:S(2)}) %collective-permute-start.12) | collective-permute-done | bytes 65568 | tf_op jit(solution)/shard_map/ppermute | solution.py:33
  40.3 2.6 %collective-permute-start.13 = (bf16[1,4,2048]{2,1,0:T(4,128)(2,1)S(1)}, bf16[1,4,2048]{2,1,0:T(4,128)(2,1)S(1)}, u32[]{:S(2)}, u32[]{:S(2)}) collective-permute-start(bf16[1,4,2048]{2,1,0:T(4,128)(2,1)S(1)} %get-tuple-element.30), channel_id=1, source_target_pairs={{0,9},{1,8},{2,11},{3,10},{4,13},{5,12},{6,15},{7,14},{8,1},{9,0},... | collective-permute-start | bytes 49160 | tf_op jit(solution)/shard_map/ppermute | solution.py:33
  42.9 1.5 %collective-permute-start.14 = (bf16[1,4,2048]{2,1,0:T(4,128)(2,1)S(1)}, bf16[1,4,2048]{2,1,0:T(4,128)(2,1)S(1)}, u32[]{:S(2)}, u32[]{:S(2)}) collective-permute-start(bf16[1,4,2048]{2,1,0:T(4,128)(2,1)S(1)} %get-tuple-element.31), channel_id=1, source_target_pairs={{0,24},{1,25},{2,26},{3,27},{4,28},{5,29},{6,30},{7,31},{8,16},{9,... | collective-permute-start | bytes 49160 | tf_op jit(solution)/shard_map/ppermute | solution.py:33
  44.3 0.0 collective-permute-start.15
  44.3 0.1 collective-permute-done.13.refs_1_
  44.4 4.2 %collective-permute-done.14.refs_2_ = bf16[1,4,2048]{2,1,0:T(4,128)(2,1)S(1)} collective-permute-done((bf16[1,4,2048]{2,1,0:T(4,128)(2,1)S(1)}, bf16[1,4,2048]{2,1,0:T(4,128)(2,1)S(1)}, u32[]{:S(2)}, u32[]{:S(2)}) %collective-permute-start.14) | collective-permute-done | bytes 16416 | tf_op jit(solution)/shard_map/ppermute | solution.py:33
  48.6 0.0 collective-permute-done.15.refs_3_
  48.6 0.6 %finish.1 = bf16[4,4096]{1,0:T(4,128)(2,1)} custom-call(f32[1,4,2048]{2,1,0:T(4,128)S(1)} %get-tuple-element.29.refs_0_, bf16[1,4,2048]{2,1,0:T(4,128)(2,1)S(1)} %collective-permute-done.13.refs_1_, bf16[1,4,2048]{2,1,0:T(4,128)(2,1)S(1)} %collective-permute-done.14.refs_2_, bf16[1,4,2048]{2,1,0:T(4,128)(2,1)S(1)} %collective-permute-done.15.refs_3_), custom_call_target="tpu_custom_call" | custom-call | tf_op jit(solution)/shard_map/finish/pallas_call | solution.py:251
  (6 shorter events, 0.1 us)
Async XLA Ops:
  0.0 21.6 %copy-start = (bf16[1,4096,1024]{2,1,0:T(8,128)(2,1)S(1)}, bf16[1,4096,1024]{2,1,0:T(8,128)(2,1)}, u32[]{:S(2)}) copy-start(bf16[1,4096,1024]{2,1,0:T(8,128)(2,1)} %param.9) | copy-start | bytes 25165828
  0.0 21.6 %copy-start.1 = (bf16[1,4096,1024]{2,1,0:T(8,128)(2,1)S(1)}, bf16[1,4096,1024]{2,1,0:T(8,128)(2,1)}, u32[]{:S(2)}) copy-start(bf16[1,4096,1024]{2,1,0:T(8,128)(2,1)} %param.10) | copy-start | bytes 25165828
  1.0 7.0 %collective-permute-start.2 = (bf16[4,4224]{1,0:T(4,128)(2,1)S(1)}, bf16[4,4224]{1,0:T(4,128)(2,1)S(1)}, u32[]{:S(2)}, u32[]{:S(2)}) collective-permute-start(bf16[4,4224]{1,0:T(4,128)(2,1)S(1)} %pack_block.1.refs_0_), channel_id=1, source_target_pairs={{0,12},{1,13},{2,14},{3,15},{4,8},{5,9},{6,10},{7,11},{8,4},{9,5},... | collective-permute-start | bytes 101384 | tf_op jit(solution)/shard_map/ppermute | solution.py:33
  6.1 4.3 %collective-permute-start.1 = (bf16[4,4224]{1,0:T(4,128)(2,1)S(1)}, bf16[4,4224]{1,0:T(4,128)(2,1)S(1)}, u32[]{:S(2)}, u32[]{:S(2)}) collective-permute-start(bf16[4,4224]{1,0:T(4,128)(2,1)S(1)} %pack_block.1.refs_0_), channel_id=1, source_target_pairs={{0,9},{1,8},{2,11},{3,10},{4,13},{5,12},{6,15},{7,14},{8,1},{9,0},... | collective-permute-start | bytes 101384 | tf_op jit(solution)/shard_map/ppermute | solution.py:33
  6.1 4.3 %collective-permute-start = (bf16[4,4224]{1,0:T(4,128)(2,1)S(1)}, bf16[4,4224]{1,0:T(4,128)(2,1)S(1)}, u32[]{:S(2)}, u32[]{:S(2)}) collective-permute-start(bf16[4,4224]{1,0:T(4,128)(2,1)S(1)} %pack_block.1.refs_0_), channel_id=1, source_target_pairs={{0,5},{1,4},{2,7},{3,6},{4,1},{5,0},{6,3},{7,2},{8,13},{9,12},{10,... | collective-permute-start | bytes 101384 | tf_op jit(solution)/shard_map/ppermute | solution.py:33
  10.5 7.2 %collective-permute-start.5 = (bf16[4,4,4224]{2,1,0:T(4,128)(2,1)S(1)}, bf16[4,4,4224]{2,1,0:T(4,128)(2,1)S(1)}, u32[]{:S(2)}, u32[]{:S(2)}) collective-permute-start(bf16[4,4,4224]{2,1,0:T(4,128)(2,1)S(1)} %stack_blocks.1.refs_0_), channel_id=1, source_target_pairs={{0,18},{1,19},{2,16},{3,17},{4,22},{5,23},{6,20},{7,21},{8,26},{9,... | collective-permute-start | bytes 405512 | tf_op jit(solution)/shard_map/ppermute | solution.py:33
  13.0 5.9 %collective-permute-start.4 = (bf16[4,4,4224]{2,1,0:T(4,128)(2,1)S(1)}, bf16[4,4,4224]{2,1,0:T(4,128)(2,1)S(1)}, u32[]{:S(2)}, u32[]{:S(2)}) collective-permute-start(bf16[4,4,4224]{2,1,0:T(4,128)(2,1)S(1)} %stack_blocks.1.refs_0_), channel_id=1, source_target_pairs={{0,17},{1,16},{2,19},{3,18},{4,21},{5,20},{6,23},{7,22},{8,25},{9,... | collective-permute-start | bytes 405512 | tf_op jit(solution)/shard_map/ppermute | solution.py:33
  13.0 6.3 %collective-permute-start.3 = (bf16[4,4,4224]{2,1,0:T(4,128)(2,1)S(1)}, bf16[4,4,4224]{2,1,0:T(4,128)(2,1)S(1)}, u32[]{:S(2)}, u32[]{:S(2)}) collective-permute-start(bf16[4,4,4224]{2,1,0:T(4,128)(2,1)S(1)} %stack_blocks.1.refs_0_), channel_id=1, source_target_pairs={{0,3},{1,2},{2,1},{3,0},{4,7},{5,6},{6,5},{7,4},{8,11},{9,10},{10,... | collective-permute-start | bytes 405512 | tf_op jit(solution)/shard_map/ppermute | solution.py:33
  19.5 2.0 %collective-permute-start.6 = (bf16[64,4224]{1,0:T(8,128)(2,1)S(1)}, bf16[64,4224]{1,0:T(8,128)(2,1)S(1)}, u32[]{:S(2)}, u32[]{:S(2)}) collective-permute-start(bf16[64,4224]{1,0:T(8,128)(2,1)S(1)} %join_rows.1), channel_id=1, source_target_pairs={{0,1},{1,0},{2,3},{3,2},{4,5},{5,4},{6,7},{7,6},{8,9},{9,8},{10,11... | collective-permute-start | bytes 1622024 | tf_op jit(solution)/shard_map/ppermute | solution.py:33
  21.6 5.0 %slice-start = ((s8[8388608]{0:T(1024)(128)(4,1)}), s8[4194304]{0:T(1024)(128)(4,1)S(1)}, s32[]{:S(2)}) async-start(s8[8388608]{0:T(1024)(128)(4,1)} %bitcast.3), calls=%async_computation | async-start | bytes 8388608
  23.0 3.6 %slice-start.1 = ((s8[8388608]{0:T(1024)(128)(4,1)}), s8[4194304]{0:T(1024)(128)(4,1)S(1)}, s32[]{:S(2)}) async-start(s8[8388608]{0:T(1024)(128)(4,1)} %bitcast.3), calls=%async_computation.1 | async-start | bytes 8388608
  23.0 5.8 %collective-permute-start.8 = (bf16[128,512]{1,0:T(8,128)(2,1)S(1)}, bf16[128,512]{1,0:T(8,128)(2,1)S(1)}, u32[]{:S(2)}, u32[]{:S(2)}) collective-permute-start(bf16[128,512]{1,0:T(8,128)(2,1)S(1)} %expand_rows.2.refs_0_), channel_id=1, source_target_pairs={{0,16},{1,17},{2,18},{3,19},{4,20},{5,21},{6,22},{7,23},{8,24},{9,... | collective-permute-start | bytes 393224 | tf_op jit(solution)/shard_map/ppermute | solution.py:33
  25.8 5.7 %collective-permute-start.7 = (bf16[128,512]{1,0:T(8,128)(2,1)S(1)}, bf16[128,512]{1,0:T(8,128)(2,1)S(1)}, u32[]{:S(2)}, u32[]{:S(2)}) collective-permute-start(bf16[128,512]{1,0:T(8,128)(2,1)S(1)} %expand_rows.3.refs_1_), channel_id=1, source_target_pairs={{0,16},{1,17},{2,18},{3,19},{4,20},{5,21},{6,22},{7,23},{8,24},{9,... | collective-permute-start | bytes 393224 | tf_op jit(solution)/shard_map/ppermute | solution.py:33
  32.0 1.6 %collective-permute-start.9 = (bf16[64,2048]{1,0:T(8,128)(2,1)S(1)}, bf16[64,2048]{1,0:T(8,128)(2,1)S(1)}, u32[]{:S(2)}, u32[]{:S(2)}) collective-permute-start(bf16[64,2048]{1,0:T(8,128)(2,1)S(1)} %contract_hidden.7), channel_id=1, source_target_pairs={{0,1},{1,0},{2,3},{3,2},{4,5},{5,4},{6,7},{7,6},{8,9},{9,8},{10,11... | collective-permute-start | bytes 786440 | tf_op jit(solution)/shard_map/ppermute | solution.py:33
  33.7 6.0 %collective-permute-start.10 = (bf16[4,4,2048]{2,1,0:T(4,128)(2,1)S(1)}, bf16[4,4,2048]{2,1,0:T(4,128)(2,1)S(1)}, u32[]{:S(2)}, u32[]{:S(2)}) collective-permute-start(bf16[4,4,2048]{2,1,0:T(4,128)(2,1)S(1)} %get-tuple-element.26), channel_id=1, source_target_pairs={{0,6},{1,7},{2,4},{3,5},{4,2},{5,3},{6,0},{7,1},{8,14},{9,15},{10,... | collective-permute-start | bytes 196616 | tf_op jit(solution)/shard_map/ppermute | solution.py:33
  35.2 4.4 %collective-permute-start.11 = (bf16[4,4,2048]{2,1,0:T(4,128)(2,1)S(1)}, bf16[4,4,2048]{2,1,0:T(4,128)(2,1)S(1)}, u32[]{:S(2)}, u32[]{:S(2)}) collective-permute-start(bf16[4,4,2048]{2,1,0:T(4,128)(2,1)S(1)} %get-tuple-element.27), channel_id=1, source_target_pairs={{0,5},{1,4},{2,7},{3,6},{4,1},{5,0},{6,3},{7,2},{8,13},{9,12},{10,... | collective-permute-start | bytes 196616 | tf_op jit(solution)/shard_map/ppermute | solution.py:33
  36.4 3.8 %collective-permute-start.12 = (bf16[4,4,2048]{2,1,0:T(4,128)(2,1)S(1)}, bf16[4,4,2048]{2,1,0:T(4,128)(2,1)S(1)}, u32[]{:S(2)}, u32[]{:S(2)}) collective-permute-start(bf16[4,4,2048]{2,1,0:T(4,128)(2,1)S(1)} %get-tuple-element.28), channel_id=1, source_target_pairs={{0,3},{1,2},{2,1},{3,0},{4,7},{5,6},{6,5},{7,4},{8,11},{9,10},{10,... | collective-permute-start | bytes 196616 | tf_op jit(solution)/shard_map/ppermute | solution.py:33
  40.3 4.1 %collective-permute-start.13 = (bf16[1,4,2048]{2,1,0:T(4,128)(2,1)S(1)}, bf16[1,4,2048]{2,1,0:T(4,128)(2,1)S(1)}, u32[]{:S(2)}, u32[]{:S(2)}) collective-permute-start(bf16[1,4,2048]{2,1,0:T(4,128)(2,1)S(1)} %get-tuple-element.30), channel_id=1, source_target_pairs={{0,9},{1,8},{2,11},{3,10},{4,13},{5,12},{6,15},{7,14},{8,1},{9,0},... | collective-permute-start | bytes 49160 | tf_op jit(solution)/shard_map/ppermute | solution.py:33
  42.9 5.7 %collective-permute-start.14 = (bf16[1,4,2048]{2,1,0:T(4,128)(2,1)S(1)}, bf16[1,4,2048]{2,1,0:T(4,128)(2,1)S(1)}, u32[]{:S(2)}, u32[]{:S(2)}) collective-permute-start(bf16[1,4,2048]{2,1,0:T(4,128)(2,1)S(1)} %get-tuple-element.31), channel_id=1, source_target_pairs={{0,24},{1,25},{2,26},{3,27},{4,28},{5,29},{6,30},{7,31},{8,16},{9,... | collective-permute-start | bytes 49160 | tf_op jit(solution)/shard_map/ppermute | solution.py:33
  44.3 4.3 %collective-permute-start.15 = (bf16[1,4,2048]{2,1,0:T(4,128)(2,1)S(1)}, bf16[1,4,2048]{2,1,0:T(4,128)(2,1)S(1)}, u32[]{:S(2)}, u32[]{:S(2)}) collective-permute-start(bf16[1,4,2048]{2,1,0:T(4,128)(2,1)S(1)} %get-tuple-element.32), channel_id=1, source_target_pairs={{0,17},{1,16},{2,19},{3,18},{4,21},{5,20},{6,23},{7,22},{8,25},{9,... | collective-permute-start | bytes 49160 | tf_op jit(solution)/shard_map/ppermute | solution.py:33

commit v13 on v12

--- a/solution.py
+++ b/solution.py
@@ -10,7 +10,7 @@
 TILE = 256
 BATCH = 128
 LANES = 128
-X, Y = (1, 1), (0, 3)
+X, Y = (1, 0), (0, 2)
 EXPERT = ("far", "core")
 
 
@@ -168,7 +168,7 @@
             if half is None:
                 lefts = [ref[here, :] for ref in part_refs]
             else:
-                order = [i ^ 3 for i in range(offset // half, (offset + count) // half)]
+                order = [i ^ 1 for i in range(offset // half, (offset + count) // half)]
                 lefts = [
                     jnp.concatenate([ref[i * half : (i + 1) * half, :] for i in order])
                     for ref in part_refs
@@ -282,9 +282,7 @@
         if half is not None:
             return value
         value = value.reshape(2, 2, 2, wide, high * token_count, step)
-        for axis in range(2):
-            order = [i ^ (mask & 1) for i in range(2)]
-            value = jnp.stack([lax.index_in_dim(value, i, axis, False) for i in order], axis)
+        value = jnp.stack([value[:, i ^ (mask & 1)] for i in range(2)], axis=1)
         value = jnp.stack([value[:, :, :, i ^ (mask >> 1)] for i in range(wide)], axis=3)
         return value.reshape(-1, step)
 

time: 49.4 us -> 49.2 us (level)
  transfers between devices with their start and end apart: 16 -> 16, of which waited for: 13 -> 14; matrix products, arithmetic and copies ran while one was open for 0% -> 0% of each run, Pallas kernels for 6% -> 6%
where the time goes in v13:
time: 49.2 us; the launch traced here: 49.1 us
  waiting for transfers between devices  23.2 us (47%)
  starting transfers between devices  18.8 us (38%)
  Pallas kernels  6.85 us (14%)
    ppermute x16, waiting for transfers between devices, swap(): return lax.ppermute(value, ('dp',) + EXPERT, pairs)  23.2 us
    ppermute x16, starting transfers between devices, swap(): return lax.ppermute(value, ('dp',) + EXPERT, pairs)  18.8 us
    pallas_call x2, Pallas kernels, expand_rows(): pl.pallas_call(body, out_shape=jax.ShapeDtypeStruct((count, columns), row...  2.76 us
    pallas_call x4, Pallas kernels, contract_hidden(): pl.pallas_call(body, out_shape=jax.ShapeDtypeStruct((count, width), kind)...  2.16 us
    pallas_call x1, Pallas kernels, pack_block(): pl.pallas_call(body, out_shape=jax.ShapeDtypeStruct((count, width + LANES...  1.02 us
  transfers between devices with their start and end apart: 16, of which 14 were waited for; matrix products, arithmetic and copies ran while one was open for 0% of the time, Pallas kernels for 6%

profile of v13, /device:TPU:0, one launch (start us, length us, event | category | flops | bytes accessed | tf_op | source)
XLA Modules:
  0.0 49.1 jit_solution(832875751408444870)
XLA Ops:
  0.0 1.0 %pack_block.1.refs_0_ = bf16[4,4224]{1,0:T(4,128)(2,1)S(1)} custom-call(bf16[4,4096]{1,0:T(4,128)(2,1)} %tokens_ref.1, s32[4,8]{1,0:T(4,128)} %ids_ref.1, f32[4,8]{1,0:T(4,128)} %probs_ref.1), custom_call_target="tpu_custom_call" | custom-call | flops 60000002048 | tf_op jit(solution)/shard_map/pack_block/pallas_call | solution.py:73
  1.0 5.1 %collective-permute-start.2 = (bf16[4,4224]{1,0:T(4,128)(2,1)S(1)}, bf16[4,4224]{1,0:T(4,128)(2,1)S(1)}, u32[]{:S(2)}, u32[]{:S(2)}) collective-permute-start(bf16[4,4224]{1,0:T(4,128)(2,1)S(1)} %pack_block.1.refs_0_), channel_id=1, source_target_pairs={{0,12},{1,13},{2,14},{3,15},{4,8},{5,9},{6,10},{7,11},{8,4},{9,5},... | collective-permute-start | bytes 101384 | tf_op jit(solution)/shard_map/ppermute | solution.py:33
  6.1 0.0 collective-permute-start.1
  6.1 0.4 collective-permute-start
  6.5 1.5 %collective-permute-done.2.refs_3_ = bf16[4,4224]{1,0:T(4,128)(2,1)S(1)} collective-permute-done((bf16[4,4224]{1,0:T(4,128)(2,1)S(1)}, bf16[4,4224]{1,0:T(4,128)(2,1)S(1)}, u32[]{:S(2)}, u32[]{:S(2)}) %collective-permute-start.2) | collective-permute-done | bytes 33824 | tf_op jit(solution)/shard_map/ppermute | solution.py:33
  8.0 2.4 %collective-permute-done.1.refs_2_ = bf16[4,4224]{1,0:T(4,128)(2,1)S(1)} collective-permute-done((bf16[4,4224]{1,0:T(4,128)(2,1)S(1)}, bf16[4,4224]{1,0:T(4,128)(2,1)S(1)}, u32[]{:S(2)}, u32[]{:S(2)}) %collective-permute-start.1) | collective-permute-done | bytes 33824 | tf_op jit(solution)/shard_map/ppermute | solution.py:33
  10.5 0.0 collective-permute-done.refs_1_
  10.5 2.5 %collective-permute-start.5 = (bf16[4,4,4224]{2,1,0:T(4,128)(2,1)S(1)}, bf16[4,4,4224]{2,1,0:T(4,128)(2,1)S(1)}, u32[]{:S(2)}, u32[]{:S(2)}) collective-permute-start(bf16[4,4,4224]{2,1,0:T(4,128)(2,1)S(1)} %stack_blocks.1.refs_0_), channel_id=1, source_target_pairs={{0,18},{1,19},{2,16},{3,17},{4,22},{5,23},{6,20},{7,21},{8,26},{9,... | collective-permute-start | bytes 405512 | tf_op jit(solution)/shard_map/ppermute | solution.py:33
  13.0 0.5 %collective-permute-start.4 = (bf16[4,4,4224]{2,1,0:T(4,128)(2,1)S(1)}, bf16[4,4,4224]{2,1,0:T(4,128)(2,1)S(1)}, u32[]{:S(2)}, u32[]{:S(2)}) collective-permute-start(bf16[4,4,4224]{2,1,0:T(4,128)(2,1)S(1)} %stack_blocks.1.refs_0_), channel_id=1, source_target_pairs={{0,16},{1,17},{2,18},{3,19},{4,20},{5,21},{6,22},{7,23},{8,24},{9,... | collective-permute-start | bytes 405512 | tf_op jit(solution)/shard_map/ppermute | solution.py:33
  13.6 0.5 %collective-permute-start.3 = (bf16[4,4,4224]{2,1,0:T(4,128)(2,1)S(1)}, bf16[4,4,4224]{2,1,0:T(4,128)(2,1)S(1)}, u32[]{:S(2)}, u32[]{:S(2)}) collective-permute-start(bf16[4,4,4224]{2,1,0:T(4,128)(2,1)S(1)} %stack_blocks.1.refs_0_), channel_id=1, source_target_pairs={{0,2},{1,3},{2,0},{3,1},{4,6},{5,7},{6,4},{7,5},{8,10},{9,11},{10,... | collective-permute-start | bytes 405512 | tf_op jit(solution)/shard_map/ppermute | solution.py:33
  14.1 3.9 %collective-permute-done.5.refs_3_ = bf16[4,4,4224]{2,1,0:T(4,128)(2,1)S(1)} collective-permute-done((bf16[4,4,4224]{2,1,0:T(4,128)(2,1)S(1)}, bf16[4,4,4224]{2,1,0:T(4,128)(2,1)S(1)}, u32[]{:S(2)}, u32[]{:S(2)}) %collective-permute-start.5) | collective-permute-done | bytes 135200 | tf_op jit(solution)/shard_map/ppermute | solution.py:33
  17.9 1.8 %collective-permute-done.4.refs_2_ = bf16[4,4,4224]{2,1,0:T(4,128)(2,1)S(1)} collective-permute-done((bf16[4,4,4224]{2,1,0:T(4,128)(2,1)S(1)}, bf16[4,4,4224]{2,1,0:T(4,128)(2,1)S(1)}, u32[]{:S(2)}, u32[]{:S(2)}) %collective-permute-start.4) | collective-permute-done | bytes 135200 | tf_op jit(solution)/shard_map/ppermute | solution.py:33
  19.8 0.0 collective-permute-done.3.refs_1_
  19.8 0.1 join_rows.1
  19.9 0.1 collective-permute-start.6
  20.0 1.9 %collective-permute-done.6 = bf16[64,4224]{1,0:T(8,128)(2,1)S(1)} collective-permute-done((bf16[64,4224]{1,0:T(8,128)(2,1)S(1)}, bf16[64,4224]{1,0:T(8,128)(2,1)S(1)}, u32[]{:S(2)}, u32[]{:S(2)}) %collective-permute-start.6) | collective-permute-done | bytes 540704 | tf_op jit(solution)/shard_map/ppermute | solution.py:33
  21.9 0.1 pad_maximum_fusion.rows_ref.refs_3_
  22.0 0.0 copy-done
  22.0 0.0 copy-done.1
  22.0 0.0 slice-start
  22.0 1.4 %expand_rows.2.refs_0_ = bf16[128,512]{1,0:T(8,128)(2,1)S(1)} custom-call(bf16[128,4224]{1,0:T(8,128)(2,1)S(1)} %pad_maximum_fusion.rows_ref.refs_3_, bf16[4096,1024]{1,0:T(8,128)(2,1)S(1)} %bitcast.9, bf16[4096,1024]{1,0:T(8,128)(2,1)S(1)} %bitcast.11), custom_call_target="tpu_custom_call" | custom-call | bytes 65536 | tf_op jit(solution)/shard_map/expand_rows/pallas_call | solution.py:138
  23.4 0.0 slice-start.1
  23.4 1.6 %collective-permute-start.8 = (bf16[128,512]{1,0:T(8,128)(2,1)S(1)}, bf16[128,512]{1,0:T(8,128)(2,1)S(1)}, u32[]{:S(2)}, u32[]{:S(2)}) collective-permute-start(bf16[128,512]{1,0:T(8,128)(2,1)S(1)} %expand_rows.2.refs_0_), channel_id=1, source_target_pairs={{0,16},{1,17},{2,18},{3,19},{4,20},{5,21},{6,22},{7,23},{8,24},{9,... | collective-permute-start | bytes 393224 | tf_op jit(solution)/shard_map/ppermute | solution.py:33
  25.0 1.4 %expand_rows.3.refs_1_ = bf16[128,512]{1,0:T(8,128)(2,1)S(1)} custom-call(bf16[128,4224]{1,0:T(8,128)(2,1)S(1)} %pad_maximum_fusion.rows_ref.refs_3_, bf16[4096,1024]{1,0:T(8,128)(2,1)S(1)} %bitcast.10, bf16[4096,1024]{1,0:T(8,128)(2,1)S(1)} %bitcast.12), custom_call_target="tpu_custom_call" | custom-call | bytes 65536 | tf_op jit(solution)/shard_map/expand_rows/pallas_call | solution.py:138
  26.4 0.6 %collective-permute-start.7 = (bf16[128,512]{1,0:T(8,128)(2,1)S(1)}, bf16[128,512]{1,0:T(8,128)(2,1)S(1)}, u32[]{:S(2)}, u32[]{:S(2)}) collective-permute-start(bf16[128,512]{1,0:T(8,128)(2,1)S(1)} %expand_rows.3.refs_1_), channel_id=1, source_target_pairs={{0,16},{1,17},{2,18},{3,19},{4,20},{5,21},{6,22},{7,23},{8,24},{9,... | collective-permute-start | bytes 393224 | tf_op jit(solution)/shard_map/ppermute | solution.py:33
  27.0 0.0 slice-done
  27.0 0.7 %contract_hidden.4.refs_2_ = f32[128,2048]{1,0:T(8,128)S(1)} custom-call(bf16[128,512]{1,0:T(8,128)(2,1)S(1)} %expand_rows.2.refs_0_, bf16[128,512]{1,0:T(8,128)(2,1)S(1)} %expand_rows.3.refs_1_, bf16[2048,2048]{1,0:T(8,128)(2,1)S(1)} %bitcast.5), custom_call_target="tpu_custom_call" | custom-call | bytes 262144 | tf_op jit(solution)/shard_map/contract_hidden/pallas_call | solution.py:195
  27.7 1.4 %collective-permute-done.8.refs_0_ = bf16[128,512]{1,0:T(8,128)(2,1)S(1)} collective-permute-done((bf16[128,512]{1,0:T(8,128)(2,1)S(1)}, bf16[128,512]{1,0:T(8,128)(2,1)S(1)}, u32[]{:S(2)}, u32[]{:S(2)}) %collective-permute-start.8) | collective-permute-done | bytes 131104 | tf_op jit(solution)/shard_map/ppermute | solution.py:33
  29.1 0.5 contract_hidden.5.refs_2_
  29.5 2.3 %collective-permute-done.7.refs_0_ = bf16[128,512]{1,0:T(8,128)(2,1)S(1)} collective-permute-done((bf16[128,512]{1,0:T(8,128)(2,1)S(1)}, bf16[128,512]{1,0:T(8,128)(2,1)S(1)}, u32[]{:S(2)}, u32[]{:S(2)}) %collective-permute-start.7) | collective-permute-done | bytes 131104 | tf_op jit(solution)/shard_map/ppermute | solution.py:33
  31.8 0.5 contract_hidden.7
  32.3 0.1 collective-permute-start.9
  32.4 0.5 %contract_hidden.6.refs_0_ = f32[64,2048]{1,0:T(8,128)S(1)} custom-call(bf16[128,512]{1,0:T(8,128)(2,1)S(1)} %collective-permute-done.7.refs_0_, bf16[2048,2048]{1,0:T(8,128)(2,1)S(1)} %bitcast.8, f32[128,2048]{1,0:T(8,128)S(1)} %contract_hidden.5.refs_2_, bf16[128,4224]{1,0:T(8,128)(2,1)S(1)} %pad_maximum_fusion.rows_ref.refs_3_), custom_call_target="tpu_custom_call" | custom-call | bytes 131072 | tf_op jit(solution)/shard_map/contract_hidden/pallas_call | solution.py:195
  32.9 1.0 %collective-permute-done.9.refs_1_ = bf16[64,2048]{1,0:T(8,128)(2,1)S(1)} collective-permute-done((bf16[64,2048]{1,0:T(8,128)(2,1)S(1)}, bf16[64,2048]{1,0:T(8,128)(2,1)S(1)}, u32[]{:S(2)}, u32[]{:S(2)}) %collective-permute-start.9) | collective-permute-done | bytes 262176 | tf_op jit(solution)/shard_map/ppermute | solution.py:33
  33.9 0.1 sum_stage.2
  34.0 1.0 %collective-permute-start.10 = (bf16[4,4,2048]{2,1,0:T(4,128)(2,1)S(1)}, bf16[4,4,2048]{2,1,0:T(4,128)(2,1)S(1)}, u32[]{:S(2)}, u32[]{:S(2)}) collective-permute-start(bf16[4,4,2048]{2,1,0:T(4,128)(2,1)S(1)} %get-tuple-element.26), channel_id=1, source_target_pairs={{0,7},{1,6},{2,5},{3,4},{4,3},{5,2},{6,1},{7,0},{8,15},{9,14},{10,... | collective-permute-start | bytes 196616 | tf_op jit(solution)/shard_map/ppermute | solution.py:33
  35.0 1.7 %collective-permute-start.11 = (bf16[4,4,2048]{2,1,0:T(4,128)(2,1)S(1)}, bf16[4,4,2048]{2,1,0:T(4,128)(2,1)S(1)}, u32[]{:S(2)}, u32[]{:S(2)}) collective-permute-start(bf16[4,4,2048]{2,1,0:T(4,128)(2,1)S(1)} %get-tuple-element.27), channel_id=1, source_target_pairs={{0,5},{1,4},{2,7},{3,6},{4,1},{5,0},{6,3},{7,2},{8,13},{9,12},{10,... | collective-permute-start | bytes 196616 | tf_op jit(solution)/shard_map/ppermute | solution.py:33
  36.7 0.6 %collective-permute-start.12 = (bf16[4,4,2048]{2,1,0:T(4,128)(2,1)S(1)}, bf16[4,4,2048]{2,1,0:T(4,128)(2,1)S(1)}, u32[]{:S(2)}, u32[]{:S(2)}) collective-permute-start(bf16[4,4,2048]{2,1,0:T(4,128)(2,1)S(1)} %get-tuple-element.28), channel_id=1, source_target_pairs={{0,2},{1,3},{2,0},{3,1},{4,6},{5,7},{6,4},{7,5},{8,10},{9,11},{10,... | collective-permute-start | bytes 196616 | tf_op jit(solution)/shard_map/ppermute | solution.py:33
  37.3 1.8 %collective-permute-done.10.refs_1_ = bf16[4,4,2048]{2,1,0:T(4,128)(2,1)S(1)} collective-permute-done((bf16[4,4,2048]{2,1,0:T(4,128)(2,1)S(1)}, bf16[4,4,2048]{2,1,0:T(4,128)(2,1)S(1)}, u32[]{:S(2)}, u32[]{:S(2)}) %collective-permute-start.10) | collective-permute-done | bytes 65568 | tf_op jit(solution)/shard_map/ppermute | solution.py:33
  39.1 1.4 %collective-permute-done.11.refs_2_ = bf16[4,4,2048]{2,1,0:T(4,128)(2,1)S(1)} collective-permute-done((bf16[4,4,2048]{2,1,0:T(4,128)(2,1)S(1)}, bf16[4,4,2048]{2,1,0:T(4,128)(2,1)S(1)}, u32[]{:S(2)}, u32[]{:S(2)}) %collective-permute-start.11) | collective-permute-done | bytes 65568 | tf_op jit(solution)/shard_map/ppermute | solution.py:33
  40.5 0.5 %collective-permute-done.12.refs_3_ = bf16[4,4,2048]{2,1,0:T(4,128)(2,1)S(1)} collective-permute-done((bf16[4,4,2048]{2,1,0:T(4,128)(2,1)S(1)}, bf16[4,4,2048]{2,1,0:T(4,128)(2,1)S(1)}, u32[]{:S(2)}, u32[]{:S(2)}) %collective-permute-start.12) | collective-permute-done | bytes 65568 | tf_op jit(solution)/shard_map/ppermute | solution.py:33
  41.1 1.8 %collective-permute-start.13 = (bf16[1,4,2048]{2,1,0:T(4,128)(2,1)S(1)}, bf16[1,4,2048]{2,1,0:T(4,128)(2,1)S(1)}, u32[]{:S(2)}, u32[]{:S(2)}) collective-permute-start(bf16[1,4,2048]{2,1,0:T(4,128)(2,1)S(1)} %get-tuple-element.30), channel_id=1, source_target_pairs={{0,9},{1,8},{2,11},{3,10},{4,13},{5,12},{6,15},{7,14},{8,1},{9,0},... | collective-permute-start | bytes 49160 | tf_op jit(solution)/shard_map/ppermute | solution.py:33
  42.8 1.9 %collective-permute-start.14 = (bf16[1,4,2048]{2,1,0:T(4,128)(2,1)S(1)}, bf16[1,4,2048]{2,1,0:T(4,128)(2,1)S(1)}, u32[]{:S(2)}, u32[]{:S(2)}) collective-permute-start(bf16[1,4,2048]{2,1,0:T(4,128)(2,1)S(1)} %get-tuple-element.31), channel_id=1, source_target_pairs={{0,25},{1,24},{2,27},{3,26},{4,29},{5,28},{6,31},{7,30},{8,17},{9,... | collective-permute-start | bytes 49160 | tf_op jit(solution)/shard_map/ppermute | solution.py:33
  44.7 0.5 %collective-permute-start.15 = (bf16[1,4,2048]{2,1,0:T(4,128)(2,1)S(1)}, bf16[1,4,2048]{2,1,0:T(4,128)(2,1)S(1)}, u32[]{:S(2)}, u32[]{:S(2)}) collective-permute-start(bf16[1,4,2048]{2,1,0:T(4,128)(2,1)S(1)} %get-tuple-element.32), channel_id=1, source_target_pairs={{0,16},{1,17},{2,18},{3,19},{4,20},{5,21},{6,22},{7,23},{8,24},{9,... | collective-permute-start | bytes 49160 | tf_op jit(solution)/shard_map/ppermute | solution.py:33
  45.2 0.2 collective-permute-done.13.refs_1_
  45.4 2.3 %collective-permute-done.14.refs_2_ = bf16[1,4,2048]{2,1,0:T(4,128)(2,1)S(1)} collective-permute-done((bf16[1,4,2048]{2,1,0:T(4,128)(2,1)S(1)}, bf16[1,4,2048]{2,1,0:T(4,128)(2,1)S(1)}, u32[]{:S(2)}, u32[]{:S(2)}) %collective-permute-start.14) | collective-permute-done | bytes 16416 | tf_op jit(solution)/shard_map/ppermute | solution.py:33
  47.8 0.6 %collective-permute-done.15.refs_3_ = bf16[1,4,2048]{2,1,0:T(4,128)(2,1)S(1)} collective-permute-done((bf16[1,4,2048]{2,1,0:T(4,128)(2,1)S(1)}, bf16[1,4,2048]{2,1,0:T(4,128)(2,1)S(1)}, u32[]{:S(2)}, u32[]{:S(2)}) %collective-permute-start.15) | collective-permute-done | bytes 16416 | tf_op jit(solution)/shard_map/ppermute | solution.py:33
  48.4 0.6 %finish.1 = bf16[4,4096]{1,0:T(4,128)(2,1)} custom-call(f32[1,4,2048]{2,1,0:T(4,128)S(1)} %get-tuple-element.29.refs_0_, bf16[1,4,2048]{2,1,0:T(4,128)(2,1)S(1)} %collective-permute-done.13.refs_1_, bf16[1,4,2048]{2,1,0:T(4,128)(2,1)S(1)} %collective-permute-done.14.refs_2_, bf16[1,4,2048]{2,1,0:T(4,128)(2,1)S(1)} %collective-permute-done.15.refs_3_), custom_call_target="tpu_custom_call" | custom-call | tf_op jit(solution)/shard_map/finish/pallas_call | solution.py:251
  (6 shorter events, 0.1 us)
Async XLA Ops:
  0.0 22.0 %copy-start = (bf16[1,4096,1024]{2,1,0:T(8,128)(2,1)S(1)}, bf16[1,4096,1024]{2,1,0:T(8,128)(2,1)}, u32[]{:S(2)}) copy-start(bf16[1,4096,1024]{2,1,0:T(8,128)(2,1)} %param.9) | copy-start | bytes 25165828
  0.0 22.0 %copy-start.1 = (bf16[1,4096,1024]{2,1,0:T(8,128)(2,1)S(1)}, bf16[1,4096,1024]{2,1,0:T(8,128)(2,1)}, u32[]{:S(2)}) copy-start(bf16[1,4096,1024]{2,1,0:T(8,128)(2,1)} %param.10) | copy-start | bytes 25165828
  1.0 7.0 %collective-permute-start.2 = (bf16[4,4224]{1,0:T(4,128)(2,1)S(1)}, bf16[4,4224]{1,0:T(4,128)(2,1)S(1)}, u32[]{:S(2)}, u32[]{:S(2)}) collective-permute-start(bf16[4,4224]{1,0:T(4,128)(2,1)S(1)} %pack_block.1.refs_0_), channel_id=1, source_target_pairs={{0,12},{1,13},{2,14},{3,15},{4,8},{5,9},{6,10},{7,11},{8,4},{9,5},... | collective-permute-start | bytes 101384 | tf_op jit(solution)/shard_map/ppermute | solution.py:33
  6.1 4.3 %collective-permute-start.1 = (bf16[4,4224]{1,0:T(4,128)(2,1)S(1)}, bf16[4,4224]{1,0:T(4,128)(2,1)S(1)}, u32[]{:S(2)}, u32[]{:S(2)}) collective-permute-start(bf16[4,4224]{1,0:T(4,128)(2,1)S(1)} %pack_block.1.refs_0_), channel_id=1, source_target_pairs={{0,9},{1,8},{2,11},{3,10},{4,13},{5,12},{6,15},{7,14},{8,1},{9,0},... | collective-permute-start | bytes 101384 | tf_op jit(solution)/shard_map/ppermute | solution.py:33
  6.1 4.3 %collective-permute-start = (bf16[4,4224]{1,0:T(4,128)(2,1)S(1)}, bf16[4,4224]{1,0:T(4,128)(2,1)S(1)}, u32[]{:S(2)}, u32[]{:S(2)}) collective-permute-start(bf16[4,4224]{1,0:T(4,128)(2,1)S(1)} %pack_block.1.refs_0_), channel_id=1, source_target_pairs={{0,5},{1,4},{2,7},{3,6},{4,1},{5,0},{6,3},{7,2},{8,13},{9,12},{10,... | collective-permute-start | bytes 101384 | tf_op jit(solution)/shard_map/ppermute | solution.py:33
  10.5 7.4 %collective-permute-start.5 = (bf16[4,4,4224]{2,1,0:T(4,128)(2,1)S(1)}, bf16[4,4,4224]{2,1,0:T(4,128)(2,1)S(1)}, u32[]{:S(2)}, u32[]{:S(2)}) collective-permute-start(bf16[4,4,4224]{2,1,0:T(4,128)(2,1)S(1)} %stack_blocks.1.refs_0_), channel_id=1, source_target_pairs={{0,18},{1,19},{2,16},{3,17},{4,22},{5,23},{6,20},{7,21},{8,26},{9,... | collective-permute-start | bytes 405512 | tf_op jit(solution)/shard_map/ppermute | solution.py:33
  13.0 6.7 %collective-permute-start.4 = (bf16[4,4,4224]{2,1,0:T(4,128)(2,1)S(1)}, bf16[4,4,4224]{2,1,0:T(4,128)(2,1)S(1)}, u32[]{:S(2)}, u32[]{:S(2)}) collective-permute-start(bf16[4,4,4224]{2,1,0:T(4,128)(2,1)S(1)} %stack_blocks.1.refs_0_), channel_id=1, source_target_pairs={{0,16},{1,17},{2,18},{3,19},{4,20},{5,21},{6,22},{7,23},{8,24},{9,... | collective-permute-start | bytes 405512 | tf_op jit(solution)/shard_map/ppermute | solution.py:33
  13.6 6.2 %collective-permute-start.3 = (bf16[4,4,4224]{2,1,0:T(4,128)(2,1)S(1)}, bf16[4,4,4224]{2,1,0:T(4,128)(2,1)S(1)}, u32[]{:S(2)}, u32[]{:S(2)}) collective-permute-start(bf16[4,4,4224]{2,1,0:T(4,128)(2,1)S(1)} %stack_blocks.1.refs_0_), channel_id=1, source_target_pairs={{0,2},{1,3},{2,0},{3,1},{4,6},{5,7},{6,4},{7,5},{8,10},{9,11},{10,... | collective-permute-start | bytes 405512 | tf_op jit(solution)/shard_map/ppermute | solution.py:33
  19.9 2.0 %collective-permute-start.6 = (bf16[64,4224]{1,0:T(8,128)(2,1)S(1)}, bf16[64,4224]{1,0:T(8,128)(2,1)S(1)}, u32[]{:S(2)}, u32[]{:S(2)}) collective-permute-start(bf16[64,4224]{1,0:T(8,128)(2,1)S(1)} %join_rows.1), channel_id=1, source_target_pairs={{0,1},{1,0},{2,3},{3,2},{4,5},{5,4},{6,7},{7,6},{8,9},{9,8},{10,11... | collective-permute-start | bytes 1622024 | tf_op jit(solution)/shard_map/ppermute | solution.py:33
  22.0 5.0 %slice-start = ((s8[8388608]{0:T(1024)(128)(4,1)}), s8[4194304]{0:T(1024)(128)(4,1)S(1)}, s32[]{:S(2)}) async-start(s8[8388608]{0:T(1024)(128)(4,1)} %bitcast.3), calls=%async_computation | async-start | bytes 8388608
  23.4 3.6 %slice-start.1 = ((s8[8388608]{0:T(1024)(128)(4,1)}), s8[4194304]{0:T(1024)(128)(4,1)S(1)}, s32[]{:S(2)}) async-start(s8[8388608]{0:T(1024)(128)(4,1)} %bitcast.3), calls=%async_computation.1 | async-start | bytes 8388608
  23.4 5.7 %collective-permute-start.8 = (bf16[128,512]{1,0:T(8,128)(2,1)S(1)}, bf16[128,512]{1,0:T(8,128)(2,1)S(1)}, u32[]{:S(2)}, u32[]{:S(2)}) collective-permute-start(bf16[128,512]{1,0:T(8,128)(2,1)S(1)} %expand_rows.2.refs_0_), channel_id=1, source_target_pairs={{0,16},{1,17},{2,18},{3,19},{4,20},{5,21},{6,22},{7,23},{8,24},{9,... | collective-permute-start | bytes 393224 | tf_op jit(solution)/shard_map/ppermute | solution.py:33
  26.4 5.5 %collective-permute-start.7 = (bf16[128,512]{1,0:T(8,128)(2,1)S(1)}, bf16[128,512]{1,0:T(8,128)(2,1)S(1)}, u32[]{:S(2)}, u32[]{:S(2)}) collective-permute-start(bf16[128,512]{1,0:T(8,128)(2,1)S(1)} %expand_rows.3.refs_1_), channel_id=1, source_target_pairs={{0,16},{1,17},{2,18},{3,19},{4,20},{5,21},{6,22},{7,23},{8,24},{9,... | collective-permute-start | bytes 393224 | tf_op jit(solution)/shard_map/ppermute | solution.py:33
  32.3 1.6 %collective-permute-start.9 = (bf16[64,2048]{1,0:T(8,128)(2,1)S(1)}, bf16[64,2048]{1,0:T(8,128)(2,1)S(1)}, u32[]{:S(2)}, u32[]{:S(2)}) collective-permute-start(bf16[64,2048]{1,0:T(8,128)(2,1)S(1)} %contract_hidden.7), channel_id=1, source_target_pairs={{0,1},{1,0},{2,3},{3,2},{4,5},{5,4},{6,7},{7,6},{8,9},{9,8},{10,11... | collective-permute-start | bytes 786440 | tf_op jit(solution)/shard_map/ppermute | solution.py:33
  34.0 5.0 %collective-permute-start.10 = (bf16[4,4,2048]{2,1,0:T(4,128)(2,1)S(1)}, bf16[4,4,2048]{2,1,0:T(4,128)(2,1)S(1)}, u32[]{:S(2)}, u32[]{:S(2)}) collective-permute-start(bf16[4,4,2048]{2,1,0:T(4,128)(2,1)S(1)} %get-tuple-element.26), channel_id=1, source_target_pairs={{0,7},{1,6},{2,5},{3,4},{4,3},{5,2},{6,1},{7,0},{8,15},{9,14},{10,... | collective-permute-start | bytes 196616 | tf_op jit(solution)/shard_map/ppermute | solution.py:33
  35.0 5.5 %collective-permute-start.11 = (bf16[4,4,2048]{2,1,0:T(4,128)(2,1)S(1)}, bf16[4,4,2048]{2,1,0:T(4,128)(2,1)S(1)}, u32[]{:S(2)}, u32[]{:S(2)}) collective-permute-start(bf16[4,4,2048]{2,1,0:T(4,128)(2,1)S(1)} %get-tuple-element.27), channel_id=1, source_target_pairs={{0,5},{1,4},{2,7},{3,6},{4,1},{5,0},{6,3},{7,2},{8,13},{9,12},{10,... | collective-permute-start | bytes 196616 | tf_op jit(solution)/shard_map/ppermute | solution.py:33
  36.7 4.3 %collective-permute-start.12 = (bf16[4,4,2048]{2,1,0:T(4,128)(2,1)S(1)}, bf16[4,4,2048]{2,1,0:T(4,128)(2,1)S(1)}, u32[]{:S(2)}, u32[]{:S(2)}) collective-permute-start(bf16[4,4,2048]{2,1,0:T(4,128)(2,1)S(1)} %get-tuple-element.28), channel_id=1, source_target_pairs={{0,2},{1,3},{2,0},{3,1},{4,6},{5,7},{6,4},{7,5},{8,10},{9,11},{10,... | collective-permute-start | bytes 196616 | tf_op jit(solution)/shard_map/ppermute | solution.py:33
  41.1 4.4 %collective-permute-start.13 = (bf16[1,4,2048]{2,1,0:T(4,128)(2,1)S(1)}, bf16[1,4,2048]{2,1,0:T(4,128)(2,1)S(1)}, u32[]{:S(2)}, u32[]{:S(2)}) collective-permute-start(bf16[1,4,2048]{2,1,0:T(4,128)(2,1)S(1)} %get-tuple-element.30), channel_id=1, source_target_pairs={{0,9},{1,8},{2,11},{3,10},{4,13},{5,12},{6,15},{7,14},{8,1},{9,0},... | collective-permute-start | bytes 49160 | tf_op jit(solution)/shard_map/ppermute | solution.py:33
  42.8 5.0 %collective-permute-start.14 = (bf16[1,4,2048]{2,1,0:T(4,128)(2,1)S(1)}, bf16[1,4,2048]{2,1,0:T(4,128)(2,1)S(1)}, u32[]{:S(2)}, u32[]{:S(2)}) collective-permute-start(bf16[1,4,2048]{2,1,0:T(4,128)(2,1)S(1)} %get-tuple-element.31), channel_id=1, source_target_pairs={{0,25},{1,24},{2,27},{3,26},{4,29},{5,28},{6,31},{7,30},{8,17},{9,... | collective-permute-start | bytes 49160 | tf_op jit(solution)/shard_map/ppermute | solution.py:33
  44.7 3.8 %collective-permute-start.15 = (bf16[1,4,2048]{2,1,0:T(4,128)(2,1)S(1)}, bf16[1,4,2048]{2,1,0:T(4,128)(2,1)S(1)}, u32[]{:S(2)}, u32[]{:S(2)}) collective-permute-start(bf16[1,4,2048]{2,1,0:T(4,128)(2,1)S(1)} %get-tuple-element.32), channel_id=1, source_target_pairs={{0,16},{1,17},{2,18},{3,19},{4,20},{5,21},{6,22},{7,23},{8,24},{9,... | collective-permute-start | bytes 49160 | tf_op jit(solution)/shard_map/ppermute | solution.py:33

commit v14 on v10

--- a/solution.py
+++ b/solution.py
@@ -155,12 +155,13 @@
 
         def step(first, batch):
             here = pl.ds(offset + first, batch)
-            lefts = [ref[here, :] for ref in part_refs]
-            if half is not None:
-                order = [i ^ 1 for i in range(count // half)]
+            if half is None:
+                lefts = [ref[here, :] for ref in part_refs]
+            else:
+                order = [i ^ 1 for i in range(offset // half, (offset + count) // half)]
                 lefts = [
-                    jnp.concatenate([left[i * half : (i + 1) * half] for i in order])
-                    for left in lefts
+                    jnp.concatenate([ref[i * half : (i + 1) * half, :] for i in order])
+                    for ref in part_refs
                 ]
             if rows is not None:
                 table = rows_ref[here, rows.shape[1] - LANES :].astype(jnp.float32)
@@ -225,26 +226,25 @@
     )(*inputs)
 
 
-def finish(sums, groups, dtype):
-    tokens, columns = sums[0][0].shape[1:]
-    flat = [value for parts in sums for value in parts]
+def finish(parts, groups, dtype):
+    tokens, columns = parts[0][0].shape[1:]
 
     def body(*refs):
         group = lax.axis_index("dp")
-        refs, out_ref = list(refs[:-1]), refs[-1]
-        for i, parts in enumerate(sums):
-            total = sum(refs.pop(0)[0].astype(jnp.float32) for _ in parts)
+        for i in range(groups):
+            mine = [ref[0] for ref, (_, j) in zip(refs, parts) if i == j]
+            total = sum(value.astype(jnp.float32) for value in mine)
             start = pl.multiple_of((group ^ i) * columns, LANES)
-            out_ref[:, pl.ds(start, columns)] = total.astype(dtype)
+            refs[-1][:, pl.ds(start, columns)] = total.astype(dtype)
 
     return pl.pallas_call(
         body,
         out_shape=jax.ShapeDtypeStruct((tokens, groups * columns), dtype),
-        in_specs=[pl.BlockSpec(memory_space=pltpu.VMEM)] * len(flat),
+        in_specs=[pl.BlockSpec(memory_space=pltpu.VMEM)] * len(parts),
         out_specs=pl.BlockSpec(memory_space=pltpu.VMEM),
         compiler_params=pltpu.CompilerParams(vmem_limit_bytes=4 << 20),
         name="finish",
-    )(*flat)
+    )(*[value for value, _ in parts])
 
 
 def local(tokens, expert_ids, gate_probs, w_gate, w_up, w_down):
@@ -295,15 +295,15 @@
     shape = (token_count, w_down.shape[2])
     rest = [(g, h) for g in range(groups) for h in range(0, high, 2)]
     slot = lambda g, y, h: (((g & 1) * 2 + y) * wide + (g >> 1)) * high + h
-    plan = [[slot(g, y, h + z) for g, h in rest] for y, z in ((0, 0), (1, 0), (0, 1), (1, 1))]
+    plan = [[slot(g, y, h + z) for g, h in rest] for y, z in ((0, 0), (1, 1), (0, 1), (1, 0))]
     mine, *away = sum_stage([kept, swap(sent, 0, 1)], plan, shape, jnp.bfloat16)
-    inputs = [mine] + [swap(value, 0, mask) for value, mask in zip(away, (2, 4, 6))]
-    mine, *away = sum_stage(inputs, [[i] for i in range(len(rest))], shape, jnp.bfloat16)
-    sums = [[] for _ in range(groups)]
-    sums[0].append(mine)
-    for value, (g, h) in zip(away, rest[1:]):
-        sums[g].append(swap(value, g, 4 * h))
-    return finish(sums, groups, tokens.dtype)
+    inputs = [mine] + [swap(value, 0, mask) for value, mask in zip(away, (6, 4, 2))]
+    order = sorted(range(1, len(rest)), key=lambda i: (rest[i][1], rest[i][0]), reverse=True)
+    mine, *away = sum_stage(inputs, [[i] for i in [0] + order], shape, jnp.bfloat16)
+    parts = [
+        (swap(value, rest[i][0], 4 * rest[i][1]), rest[i][0]) for value, i in zip(away, order)
+    ]
+    return finish(parts + [(mine, 0)], groups, tokens.dtype)
 
 
 def solution(mesh):

time: 50.1 us -> 48.8 us (0.974)
  waiting for transfers between devices: 23.2 us -> 21.9 us
    ppermute x16, waiting for transfers between devices: 23.2 us -> 21.9 us  [swap(): return lax.ppermute(value, ('dp',) + EXPERT, pairs)]
  transfers between devices with their start and end apart: 16 -> 16, of which waited for: 15 -> 14; matrix products, arithmetic and copies ran while one was open for 0% -> 0% of each run, Pallas kernels for 6% -> 6%
where the time goes in v14:
time: 48.8 us; the launch traced here: 48.7 us
  waiting for transfers between devices  21.9 us (45%)
  starting transfers between devices  19.6 us (40%)
  Pallas kernels  6.88 us (14%)
    ppermute x16, waiting for transfers between devices, swap(): return lax.ppermute(value, ('dp',) + EXPERT, pairs)  21.9 us
    ppermute x16, starting transfers between devices, swap(): return lax.ppermute(value, ('dp',) + EXPERT, pairs)  19.6 us
    pallas_call x2, Pallas kernels, expand_rows(): pl.pallas_call(body, out_shape=jax.ShapeDtypeStruct((count, columns), row...  2.78 us
    pallas_call x4, Pallas kernels, contract_hidden(): pl.pallas_call(body, out_shape=jax.ShapeDtypeStruct((count, width), kind)...  2.16 us
    pallas_call x1, Pallas kernels, pack_block(): pl.pallas_call(body, out_shape=jax.ShapeDtypeStruct((count, width + LANES...  1.02 us
  transfers between devices with their start and end apart: 16, of which 14 were waited for; matrix products, arithmetic and copies ran while one was open for 0% of the time, Pallas kernels for 6%

profile of v14, /device:TPU:0, one launch (start us, length us, event | category | flops | bytes accessed | tf_op | source)
XLA Modules:
  0.0 48.7 jit_solution(3206979022016045531)
XLA Ops:
  0.0 1.0 %pack_block.1.refs_0_ = bf16[4,4224]{1,0:T(4,128)(2,1)S(1)} custom-call(bf16[4,4096]{1,0:T(4,128)(2,1)} %tokens_ref.1, s32[4,8]{1,0:T(4,128)} %ids_ref.1, f32[4,8]{1,0:T(4,128)} %probs_ref.1), custom_call_target="tpu_custom_call" | custom-call | flops 60000002048 | tf_op jit(solution)/shard_map/pack_block/pallas_call | solution.py:63
  1.0 5.1 %collective-permute-start.2 = (bf16[4,4224]{1,0:T(4,128)(2,1)S(1)}, bf16[4,4224]{1,0:T(4,128)(2,1)S(1)}, u32[]{:S(2)}, u32[]{:S(2)}) collective-permute-start(bf16[4,4224]{1,0:T(4,128)(2,1)S(1)} %pack_block.1.refs_0_), channel_id=1, source_target_pairs={{0,12},{1,13},{2,14},{3,15},{4,8},{5,9},{6,10},{7,11},{8,4},{9,5},... | collective-permute-start | bytes 101384 | tf_op jit(solution)/shard_map/ppermute | solution.py:23
  6.1 0.0 collective-permute-start.1
  6.1 0.6 %collective-permute-start = (bf16[4,4224]{1,0:T(4,128)(2,1)S(1)}, bf16[4,4224]{1,0:T(4,128)(2,1)S(1)}, u32[]{:S(2)}, u32[]{:S(2)}) collective-permute-start(bf16[4,4224]{1,0:T(4,128)(2,1)S(1)} %pack_block.1.refs_0_), channel_id=1, source_target_pairs={{0,4},{1,5},{2,6},{3,7},{4,0},{5,1},{6,2},{7,3},{8,12},{9,13},{10,... | collective-permute-start | bytes 101384 | tf_op jit(solution)/shard_map/ppermute | solution.py:23
  6.8 1.3 %collective-permute-done.2.refs_3_ = bf16[4,4224]{1,0:T(4,128)(2,1)S(1)} collective-permute-done((bf16[4,4224]{1,0:T(4,128)(2,1)S(1)}, bf16[4,4224]{1,0:T(4,128)(2,1)S(1)}, u32[]{:S(2)}, u32[]{:S(2)}) %collective-permute-start.2) | collective-permute-done | bytes 33824 | tf_op jit(solution)/shard_map/ppermute | solution.py:23
  8.0 2.9 %collective-permute-done.1.refs_2_ = bf16[4,4224]{1,0:T(4,128)(2,1)S(1)} collective-permute-done((bf16[4,4224]{1,0:T(4,128)(2,1)S(1)}, bf16[4,4224]{1,0:T(4,128)(2,1)S(1)}, u32[]{:S(2)}, u32[]{:S(2)}) %collective-permute-start.1) | collective-permute-done | bytes 33824 | tf_op jit(solution)/shard_map/ppermute | solution.py:23
  11.0 0.0 collective-permute-done.refs_1_
  11.0 2.5 %collective-permute-start.5 = (bf16[4,4,4224]{2,1,0:T(4,128)(2,1)S(1)}, bf16[4,4,4224]{2,1,0:T(4,128)(2,1)S(1)}, u32[]{:S(2)}, u32[]{:S(2)}) collective-permute-start(bf16[4,4,4224]{2,1,0:T(4,128)(2,1)S(1)} %stack_blocks.1.refs_0_), channel_id=1, source_target_pairs={{0,18},{1,19},{2,16},{3,17},{4,22},{5,23},{6,20},{7,21},{8,26},{9,... | collective-permute-start | bytes 405512 | tf_op jit(solution)/shard_map/ppermute | solution.py:23
  13.5 0.5 %collective-permute-start.4 = (bf16[4,4,4224]{2,1,0:T(4,128)(2,1)S(1)}, bf16[4,4,4224]{2,1,0:T(4,128)(2,1)S(1)}, u32[]{:S(2)}, u32[]{:S(2)}) collective-permute-start(bf16[4,4,4224]{2,1,0:T(4,128)(2,1)S(1)} %stack_blocks.1.refs_0_), channel_id=1, source_target_pairs={{0,16},{1,17},{2,18},{3,19},{4,20},{5,21},{6,22},{7,23},{8,24},{9,... | collective-permute-start | bytes 405512 | tf_op jit(solution)/shard_map/ppermute | solution.py:23
  14.0 0.5 %collective-permute-start.3 = (bf16[4,4,4224]{2,1,0:T(4,128)(2,1)S(1)}, bf16[4,4,4224]{2,1,0:T(4,128)(2,1)S(1)}, u32[]{:S(2)}, u32[]{:S(2)}) collective-permute-start(bf16[4,4,4224]{2,1,0:T(4,128)(2,1)S(1)} %stack_blocks.1.refs_0_), channel_id=1, source_target_pairs={{0,2},{1,3},{2,0},{3,1},{4,6},{5,7},{6,4},{7,5},{8,10},{9,11},{10,... | collective-permute-start | bytes 405512 | tf_op jit(solution)/shard_map/ppermute | solution.py:23
  14.5 2.8 %collective-permute-done.5.refs_3_ = bf16[4,4,4224]{2,1,0:T(4,128)(2,1)S(1)} collective-permute-done((bf16[4,4,4224]{2,1,0:T(4,128)(2,1)S(1)}, bf16[4,4,4224]{2,1,0:T(4,128)(2,1)S(1)}, u32[]{:S(2)}, u32[]{:S(2)}) %collective-permute-start.5) | collective-permute-done | bytes 135200 | tf_op jit(solution)/shard_map/ppermute | solution.py:23
  17.4 1.4 %collective-permute-done.4.refs_2_ = bf16[4,4,4224]{2,1,0:T(4,128)(2,1)S(1)} collective-permute-done((bf16[4,4,4224]{2,1,0:T(4,128)(2,1)S(1)}, bf16[4,4,4224]{2,1,0:T(4,128)(2,1)S(1)}, u32[]{:S(2)}, u32[]{:S(2)}) %collective-permute-start.4) | collective-permute-done | bytes 135200 | tf_op jit(solution)/shard_map/ppermute | solution.py:23
  18.8 0.2 collective-permute-done.3.refs_1_
  19.0 0.1 join_rows.1
  19.2 0.1 collective-permute-start.6
  19.3 1.9 %collective-permute-done.6 = bf16[64,4224]{1,0:T(8,128)(2,1)S(1)} collective-permute-done((bf16[64,4224]{1,0:T(8,128)(2,1)S(1)}, bf16[64,4224]{1,0:T(8,128)(2,1)S(1)}, u32[]{:S(2)}, u32[]{:S(2)}) %collective-permute-start.6) | collective-permute-done | bytes 540704 | tf_op jit(solution)/shard_map/ppermute | solution.py:23
  21.2 0.1 pad_maximum_fusion.rows_ref.refs_3_
  21.3 0.0 copy-done
  21.3 0.0 copy-done.1
  21.3 0.0 slice-start
  21.3 1.4 %expand_rows.2.refs_0_ = bf16[128,512]{1,0:T(8,128)(2,1)S(1)} custom-call(bf16[128,4224]{1,0:T(8,128)(2,1)S(1)} %pad_maximum_fusion.rows_ref.refs_3_, bf16[4096,1024]{1,0:T(8,128)(2,1)S(1)} %bitcast.9, bf16[4096,1024]{1,0:T(8,128)(2,1)S(1)} %bitcast.11), custom_call_target="tpu_custom_call" | custom-call | bytes 65536 | tf_op jit(solution)/shard_map/expand_rows/pallas_call | solution.py:128
  22.7 0.0 slice-start.1
  22.7 1.5 %collective-permute-start.8 = (bf16[128,512]{1,0:T(8,128)(2,1)S(1)}, bf16[128,512]{1,0:T(8,128)(2,1)S(1)}, u32[]{:S(2)}, u32[]{:S(2)}) collective-permute-start(bf16[128,512]{1,0:T(8,128)(2,1)S(1)} %expand_rows.2.refs_0_), channel_id=1, source_target_pairs={{0,16},{1,17},{2,18},{3,19},{4,20},{5,21},{6,22},{7,23},{8,24},{9,... | collective-permute-start | bytes 393224 | tf_op jit(solution)/shard_map/ppermute | solution.py:23
  24.2 1.4 %expand_rows.3.refs_1_ = bf16[128,512]{1,0:T(8,128)(2,1)S(1)} custom-call(bf16[128,4224]{1,0:T(8,128)(2,1)S(1)} %pad_maximum_fusion.rows_ref.refs_3_, bf16[4096,1024]{1,0:T(8,128)(2,1)S(1)} %bitcast.10, bf16[4096,1024]{1,0:T(8,128)(2,1)S(1)} %bitcast.12), custom_call_target="tpu_custom_call" | custom-call | bytes 65536 | tf_op jit(solution)/shard_map/expand_rows/pallas_call | solution.py:128
  25.6 0.6 %collective-permute-start.7 = (bf16[128,512]{1,0:T(8,128)(2,1)S(1)}, bf16[128,512]{1,0:T(8,128)(2,1)S(1)}, u32[]{:S(2)}, u32[]{:S(2)}) collective-permute-start(bf16[128,512]{1,0:T(8,128)(2,1)S(1)} %expand_rows.3.refs_1_), channel_id=1, source_target_pairs={{0,16},{1,17},{2,18},{3,19},{4,20},{5,21},{6,22},{7,23},{8,24},{9,... | collective-permute-start | bytes 393224 | tf_op jit(solution)/shard_map/ppermute | solution.py:23
  26.3 0.0 slice-done
  26.3 0.7 %contract_hidden.4.refs_2_ = f32[128,2048]{1,0:T(8,128)S(1)} custom-call(bf16[128,512]{1,0:T(8,128)(2,1)S(1)} %expand_rows.2.refs_0_, bf16[128,512]{1,0:T(8,128)(2,1)S(1)} %expand_rows.3.refs_1_, bf16[2048,2048]{1,0:T(8,128)(2,1)S(1)} %bitcast.5), custom_call_target="tpu_custom_call" | custom-call | bytes 262144 | tf_op jit(solution)/shard_map/contract_hidden/pallas_call | solution.py:185
  27.0 1.4 %collective-permute-done.8.refs_0_ = bf16[128,512]{1,0:T(8,128)(2,1)S(1)} collective-permute-done((bf16[128,512]{1,0:T(8,128)(2,1)S(1)}, bf16[128,512]{1,0:T(8,128)(2,1)S(1)}, u32[]{:S(2)}, u32[]{:S(2)}) %collective-permute-start.8) | collective-permute-done | bytes 131104 | tf_op jit(solution)/shard_map/ppermute | solution.py:23
  28.4 0.5 contract_hidden.5.refs_2_
  28.8 2.3 %collective-permute-done.7.refs_0_ = bf16[128,512]{1,0:T(8,128)(2,1)S(1)} collective-permute-done((bf16[128,512]{1,0:T(8,128)(2,1)S(1)}, bf16[128,512]{1,0:T(8,128)(2,1)S(1)}, u32[]{:S(2)}, u32[]{:S(2)}) %collective-permute-start.7) | collective-permute-done | bytes 131104 | tf_op jit(solution)/shard_map/ppermute | solution.py:23
  31.1 0.5 %contract_hidden.7 = bf16[64,2048]{1,0:T(8,128)(2,1)S(1)} custom-call(bf16[128,512]{1,0:T(8,128)(2,1)S(1)} %collective-permute-done.7.refs_0_, bf16[2048,2048]{1,0:T(8,128)(2,1)S(1)} %bitcast.7, f32[128,2048]{1,0:T(8,128)S(1)} %contract_hidden.5.refs_2_, bf16[128,4224]{1,0:T(8,128)(2,1)S(1)} %pad_maximum_fusion.rows_ref.refs_3_), custom_call_target="tpu_custom_call" | custom-call | bytes 131072 | tf_op jit(solution)/shard_map/contract_hidden/pallas_call | solution.py:185
  31.6 0.1 collective-permute-start.9
  31.7 0.5 %contract_hidden.6.refs_0_ = f32[64,2048]{1,0:T(8,128)S(1)} custom-call(bf16[128,512]{1,0:T(8,128)(2,1)S(1)} %collective-permute-done.7.refs_0_, bf16[2048,2048]{1,0:T(8,128)(2,1)S(1)} %bitcast.8, f32[128,2048]{1,0:T(8,128)S(1)} %contract_hidden.5.refs_2_, bf16[128,4224]{1,0:T(8,128)(2,1)S(1)} %pad_maximum_fusion.rows_ref.refs_3_), custom_call_target="tpu_custom_call" | custom-call | bytes 131072 | tf_op jit(solution)/shard_map/contract_hidden/pallas_call | solution.py:185
  32.2 1.0 %collective-permute-done.9.refs_1_ = bf16[64,2048]{1,0:T(8,128)(2,1)S(1)} collective-permute-done((bf16[64,2048]{1,0:T(8,128)(2,1)S(1)}, bf16[64,2048]{1,0:T(8,128)(2,1)S(1)}, u32[]{:S(2)}, u32[]{:S(2)}) %collective-permute-start.9) | collective-permute-done | bytes 262176 | tf_op jit(solution)/shard_map/ppermute | solution.py:23
  33.2 0.1 sum_stage.2
  33.3 0.8 %collective-permute-start.10 = (bf16[4,4,2048]{2,1,0:T(4,128)(2,1)S(1)}, bf16[4,4,2048]{2,1,0:T(4,128)(2,1)S(1)}, u32[]{:S(2)}, u32[]{:S(2)}) collective-permute-start(bf16[4,4,2048]{2,1,0:T(4,128)(2,1)S(1)} %get-tuple-element.26), channel_id=1, source_target_pairs={{0,6},{1,7},{2,4},{3,5},{4,2},{5,3},{6,0},{7,1},{8,14},{9,15},{10,... | collective-permute-start | bytes 196616 | tf_op jit(solution)/shard_map/ppermute | solution.py:23
  34.1 1.9 %collective-permute-start.11 = (bf16[4,4,2048]{2,1,0:T(4,128)(2,1)S(1)}, bf16[4,4,2048]{2,1,0:T(4,128)(2,1)S(1)}, u32[]{:S(2)}, u32[]{:S(2)}) collective-permute-start(bf16[4,4,2048]{2,1,0:T(4,128)(2,1)S(1)} %get-tuple-element.27), channel_id=1, source_target_pairs={{0,4},{1,5},{2,6},{3,7},{4,0},{5,1},{6,2},{7,3},{8,12},{9,13},{10,... | collective-permute-start | bytes 196616 | tf_op jit(solution)/shard_map/ppermute | solution.py:23
  36.1 0.8 %collective-permute-start.12 = (bf16[4,4,2048]{2,1,0:T(4,128)(2,1)S(1)}, bf16[4,4,2048]{2,1,0:T(4,128)(2,1)S(1)}, u32[]{:S(2)}, u32[]{:S(2)}) collective-permute-start(bf16[4,4,2048]{2,1,0:T(4,128)(2,1)S(1)} %get-tuple-element.28), channel_id=1, source_target_pairs={{0,2},{1,3},{2,0},{3,1},{4,6},{5,7},{6,4},{7,5},{8,10},{9,11},{10,... | collective-permute-start | bytes 196616 | tf_op jit(solution)/shard_map/ppermute | solution.py:23
  36.9 2.4 %collective-permute-done.10.refs_1_ = bf16[4,4,2048]{2,1,0:T(4,128)(2,1)S(1)} collective-permute-done((bf16[4,4,2048]{2,1,0:T(4,128)(2,1)S(1)}, bf16[4,4,2048]{2,1,0:T(4,128)(2,1)S(1)}, u32[]{:S(2)}, u32[]{:S(2)}) %collective-permute-start.10) | collective-permute-done | bytes 65568 | tf_op jit(solution)/shard_map/ppermute | solution.py:23
  39.2 0.3 collective-permute-done.11.refs_2_
  39.6 0.8 %collective-permute-done.12.refs_3_ = bf16[4,4,2048]{2,1,0:T(4,128)(2,1)S(1)} collective-permute-done((bf16[4,4,2048]{2,1,0:T(4,128)(2,1)S(1)}, bf16[4,4,2048]{2,1,0:T(4,128)(2,1)S(1)}, u32[]{:S(2)}, u32[]{:S(2)}) %collective-permute-start.12) | collective-permute-done | bytes 65568 | tf_op jit(solution)/shard_map/ppermute | solution.py:23
  40.4 3.0 %collective-permute-start.13 = (bf16[1,4,2048]{2,1,0:T(4,128)(2,1)S(1)}, bf16[1,4,2048]{2,1,0:T(4,128)(2,1)S(1)}, u32[]{:S(2)}, u32[]{:S(2)}) collective-permute-start(bf16[1,4,2048]{2,1,0:T(4,128)(2,1)S(1)} %get-tuple-element.29), channel_id=1, source_target_pairs={{0,24},{1,25},{2,26},{3,27},{4,28},{5,29},{6,30},{7,31},{8,16},{9,... | collective-permute-start | bytes 49160 | tf_op jit(solution)/shard_map/ppermute | solution.py:23
  43.4 0.9 %collective-permute-start.14 = (bf16[1,4,2048]{2,1,0:T(4,128)(2,1)S(1)}, bf16[1,4,2048]{2,1,0:T(4,128)(2,1)S(1)}, u32[]{:S(2)}, u32[]{:S(2)}) collective-permute-start(bf16[1,4,2048]{2,1,0:T(4,128)(2,1)S(1)} %get-tuple-element.30), channel_id=1, source_target_pairs={{0,8},{1,9},{2,10},{3,11},{4,12},{5,13},{6,14},{7,15},{8,0},{9,1},... | collective-permute-start | bytes 49160 | tf_op jit(solution)/shard_map/ppermute | solution.py:23
  44.3 0.5 %collective-permute-start.15 = (bf16[1,4,2048]{2,1,0:T(4,128)(2,1)S(1)}, bf16[1,4,2048]{2,1,0:T(4,128)(2,1)S(1)}, u32[]{:S(2)}, u32[]{:S(2)}) collective-permute-start(bf16[1,4,2048]{2,1,0:T(4,128)(2,1)S(1)} %get-tuple-element.31), channel_id=1, source_target_pairs={{0,16},{1,17},{2,18},{3,19},{4,20},{5,21},{6,22},{7,23},{8,24},{9,... | collective-permute-start | bytes 49160 | tf_op jit(solution)/shard_map/ppermute | solution.py:23
  44.8 1.3 %collective-permute-done.13.refs_0_ = bf16[1,4,2048]{2,1,0:T(4,128)(2,1)S(1)} collective-permute-done((bf16[1,4,2048]{2,1,0:T(4,128)(2,1)S(1)}, bf16[1,4,2048]{2,1,0:T(4,128)(2,1)S(1)}, u32[]{:S(2)}, u32[]{:S(2)}) %collective-permute-start.13) | collective-permute-done | bytes 16416 | tf_op jit(solution)/shard_map/ppermute | solution.py:23
  46.2 1.9 %collective-permute-done.14.refs_1_ = bf16[1,4,2048]{2,1,0:T(4,128)(2,1)S(1)} collective-permute-done((bf16[1,4,2048]{2,1,0:T(4,128)(2,1)S(1)}, bf16[1,4,2048]{2,1,0:T(4,128)(2,1)S(1)}, u32[]{:S(2)}, u32[]{:S(2)}) %collective-permute-start.14) | collective-permute-done | bytes 16416 | tf_op jit(solution)/shard_map/ppermute | solution.py:23
  48.0 0.0 collective-permute-done.15.refs_2_
  48.0 0.6 %finish.1 = bf16[4,4096]{1,0:T(4,128)(2,1)} custom-call(bf16[1,4,2048]{2,1,0:T(4,128)(2,1)S(1)} %collective-permute-done.13.refs_0_, bf16[1,4,2048]{2,1,0:T(4,128)(2,1)S(1)} %collective-permute-done.14.refs_1_, bf16[1,4,2048]{2,1,0:T(4,128)(2,1)S(1)} %collective-permute-done.15.refs_2_, f32[1,4,2048]{2,1,0:T(4,128)S(1)} %get-tuple-element.32.refs_3_), custom_call_target="tpu_custom_call" | custom-call | tf_op jit(solution)/shard_map/finish/pallas_call | solution.py:240
  (6 shorter events, 0.1 us)
Async XLA Ops:
  0.0 21.3 %copy-start = (bf16[1,4096,1024]{2,1,0:T(8,128)(2,1)S(1)}, bf16[1,4096,1024]{2,1,0:T(8,128)(2,1)}, u32[]{:S(2)}) copy-start(bf16[1,4096,1024]{2,1,0:T(8,128)(2,1)} %param.9) | copy-start | bytes 25165828
  0.0 21.3 %copy-start.1 = (bf16[1,4096,1024]{2,1,0:T(8,128)(2,1)S(1)}, bf16[1,4096,1024]{2,1,0:T(8,128)(2,1)}, u32[]{:S(2)}) copy-start(bf16[1,4096,1024]{2,1,0:T(8,128)(2,1)} %param.10) | copy-start | bytes 25165828
  1.0 7.0 %collective-permute-start.2 = (bf16[4,4224]{1,0:T(4,128)(2,1)S(1)}, bf16[4,4224]{1,0:T(4,128)(2,1)S(1)}, u32[]{:S(2)}, u32[]{:S(2)}) collective-permute-start(bf16[4,4224]{1,0:T(4,128)(2,1)S(1)} %pack_block.1.refs_0_), channel_id=1, source_target_pairs={{0,12},{1,13},{2,14},{3,15},{4,8},{5,9},{6,10},{7,11},{8,4},{9,5},... | collective-permute-start | bytes 101384 | tf_op jit(solution)/shard_map/ppermute | solution.py:23
  6.1 4.8 %collective-permute-start.1 = (bf16[4,4224]{1,0:T(4,128)(2,1)S(1)}, bf16[4,4224]{1,0:T(4,128)(2,1)S(1)}, u32[]{:S(2)}, u32[]{:S(2)}) collective-permute-start(bf16[4,4224]{1,0:T(4,128)(2,1)S(1)} %pack_block.1.refs_0_), channel_id=1, source_target_pairs={{0,8},{1,9},{2,10},{3,11},{4,12},{5,13},{6,14},{7,15},{8,0},{9,1},... | collective-permute-start | bytes 101384 | tf_op jit(solution)/shard_map/ppermute | solution.py:23
  6.1 4.8 %collective-permute-start = (bf16[4,4224]{1,0:T(4,128)(2,1)S(1)}, bf16[4,4224]{1,0:T(4,128)(2,1)S(1)}, u32[]{:S(2)}, u32[]{:S(2)}) collective-permute-start(bf16[4,4224]{1,0:T(4,128)(2,1)S(1)} %pack_block.1.refs_0_), channel_id=1, source_target_pairs={{0,4},{1,5},{2,6},{3,7},{4,0},{5,1},{6,2},{7,3},{8,12},{9,13},{10,... | collective-permute-start | bytes 101384 | tf_op jit(solution)/shard_map/ppermute | solution.py:23
  11.0 6.4 %collective-permute-start.5 = (bf16[4,4,4224]{2,1,0:T(4,128)(2,1)S(1)}, bf16[4,4,4224]{2,1,0:T(4,128)(2,1)S(1)}, u32[]{:S(2)}, u32[]{:S(2)}) collective-permute-start(bf16[4,4,4224]{2,1,0:T(4,128)(2,1)S(1)} %stack_blocks.1.refs_0_), channel_id=1, source_target_pairs={{0,18},{1,19},{2,16},{3,17},{4,22},{5,23},{6,20},{7,21},{8,26},{9,... | collective-permute-start | bytes 405512 | tf_op jit(solution)/shard_map/ppermute | solution.py:23
  13.5 5.3 %collective-permute-start.4 = (bf16[4,4,4224]{2,1,0:T(4,128)(2,1)S(1)}, bf16[4,4,4224]{2,1,0:T(4,128)(2,1)S(1)}, u32[]{:S(2)}, u32[]{:S(2)}) collective-permute-start(bf16[4,4,4224]{2,1,0:T(4,128)(2,1)S(1)} %stack_blocks.1.refs_0_), channel_id=1, source_target_pairs={{0,16},{1,17},{2,18},{3,19},{4,20},{5,21},{6,22},{7,23},{8,24},{9,... | collective-permute-start | bytes 405512 | tf_op jit(solution)/shard_map/ppermute | solution.py:23
  14.0 5.0 %collective-permute-start.3 = (bf16[4,4,4224]{2,1,0:T(4,128)(2,1)S(1)}, bf16[4,4,4224]{2,1,0:T(4,128)(2,1)S(1)}, u32[]{:S(2)}, u32[]{:S(2)}) collective-permute-start(bf16[4,4,4224]{2,1,0:T(4,128)(2,1)S(1)} %stack_blocks.1.refs_0_), channel_id=1, source_target_pairs={{0,2},{1,3},{2,0},{3,1},{4,6},{5,7},{6,4},{7,5},{8,10},{9,11},{10,... | collective-permute-start | bytes 405512 | tf_op jit(solution)/shard_map/ppermute | solution.py:23
  19.2 2.0 %collective-permute-start.6 = (bf16[64,4224]{1,0:T(8,128)(2,1)S(1)}, bf16[64,4224]{1,0:T(8,128)(2,1)S(1)}, u32[]{:S(2)}, u32[]{:S(2)}) collective-permute-start(bf16[64,4224]{1,0:T(8,128)(2,1)S(1)} %join_rows.1), channel_id=1, source_target_pairs={{0,1},{1,0},{2,3},{3,2},{4,5},{5,4},{6,7},{7,6},{8,9},{9,8},{10,11... | collective-permute-start | bytes 1622024 | tf_op jit(solution)/shard_map/ppermute | solution.py:23
  21.3 5.0 %slice-start = ((s8[8388608]{0:T(1024)(128)(4,1)}), s8[4194304]{0:T(1024)(128)(4,1)S(1)}, s32[]{:S(2)}) async-start(s8[8388608]{0:T(1024)(128)(4,1)} %bitcast.3), calls=%async_computation | async-start | bytes 8388608
  22.7 3.6 %slice-start.1 = ((s8[8388608]{0:T(1024)(128)(4,1)}), s8[4194304]{0:T(1024)(128)(4,1)S(1)}, s32[]{:S(2)}) async-start(s8[8388608]{0:T(1024)(128)(4,1)} %bitcast.3), calls=%async_computation.1 | async-start | bytes 8388608
  22.7 5.7 %collective-permute-start.8 = (bf16[128,512]{1,0:T(8,128)(2,1)S(1)}, bf16[128,512]{1,0:T(8,128)(2,1)S(1)}, u32[]{:S(2)}, u32[]{:S(2)}) collective-permute-start(bf16[128,512]{1,0:T(8,128)(2,1)S(1)} %expand_rows.2.refs_0_), channel_id=1, source_target_pairs={{0,16},{1,17},{2,18},{3,19},{4,20},{5,21},{6,22},{7,23},{8,24},{9,... | collective-permute-start | bytes 393224 | tf_op jit(solution)/shard_map/ppermute | solution.py:23
  25.6 5.5 %collective-permute-start.7 = (bf16[128,512]{1,0:T(8,128)(2,1)S(1)}, bf16[128,512]{1,0:T(8,128)(2,1)S(1)}, u32[]{:S(2)}, u32[]{:S(2)}) collective-permute-start(bf16[128,512]{1,0:T(8,128)(2,1)S(1)} %expand_rows.3.refs_1_), channel_id=1, source_target_pairs={{0,16},{1,17},{2,18},{3,19},{4,20},{5,21},{6,22},{7,23},{8,24},{9,... | collective-permute-start | bytes 393224 | tf_op jit(solution)/shard_map/ppermute | solution.py:23
  31.6 1.6 %collective-permute-start.9 = (bf16[64,2048]{1,0:T(8,128)(2,1)S(1)}, bf16[64,2048]{1,0:T(8,128)(2,1)S(1)}, u32[]{:S(2)}, u32[]{:S(2)}) collective-permute-start(bf16[64,2048]{1,0:T(8,128)(2,1)S(1)} %contract_hidden.7), channel_id=1, source_target_pairs={{0,1},{1,0},{2,3},{3,2},{4,5},{5,4},{6,7},{7,6},{8,9},{9,8},{10,11... | collective-permute-start | bytes 786440 | tf_op jit(solution)/shard_map/ppermute | solution.py:23
  33.3 5.9 %collective-permute-start.10 = (bf16[4,4,2048]{2,1,0:T(4,128)(2,1)S(1)}, bf16[4,4,2048]{2,1,0:T(4,128)(2,1)S(1)}, u32[]{:S(2)}, u32[]{:S(2)}) collective-permute-start(bf16[4,4,2048]{2,1,0:T(4,128)(2,1)S(1)} %get-tuple-element.26), channel_id=1, source_target_pairs={{0,6},{1,7},{2,4},{3,5},{4,2},{5,3},{6,0},{7,1},{8,14},{9,15},{10,... | collective-permute-start | bytes 196616 | tf_op jit(solution)/shard_map/ppermute | solution.py:23
  34.1 5.4 %collective-permute-start.11 = (bf16[4,4,2048]{2,1,0:T(4,128)(2,1)S(1)}, bf16[4,4,2048]{2,1,0:T(4,128)(2,1)S(1)}, u32[]{:S(2)}, u32[]{:S(2)}) collective-permute-start(bf16[4,4,2048]{2,1,0:T(4,128)(2,1)S(1)} %get-tuple-element.27), channel_id=1, source_target_pairs={{0,4},{1,5},{2,6},{3,7},{4,0},{5,1},{6,2},{7,3},{8,12},{9,13},{10,... | collective-permute-start | bytes 196616 | tf_op jit(solution)/shard_map/ppermute | solution.py:23
  36.1 4.3 %collective-permute-start.12 = (bf16[4,4,2048]{2,1,0:T(4,128)(2,1)S(1)}, bf16[4,4,2048]{2,1,0:T(4,128)(2,1)S(1)}, u32[]{:S(2)}, u32[]{:S(2)}) collective-permute-start(bf16[4,4,2048]{2,1,0:T(4,128)(2,1)S(1)} %get-tuple-element.28), channel_id=1, source_target_pairs={{0,2},{1,3},{2,0},{3,1},{4,6},{5,7},{6,4},{7,5},{8,10},{9,11},{10,... | collective-permute-start | bytes 196616 | tf_op jit(solution)/shard_map/ppermute | solution.py:23
  40.4 5.8 %collective-permute-start.13 = (bf16[1,4,2048]{2,1,0:T(4,128)(2,1)S(1)}, bf16[1,4,2048]{2,1,0:T(4,128)(2,1)S(1)}, u32[]{:S(2)}, u32[]{:S(2)}) collective-permute-start(bf16[1,4,2048]{2,1,0:T(4,128)(2,1)S(1)} %get-tuple-element.29), channel_id=1, source_target_pairs={{0,24},{1,25},{2,26},{3,27},{4,28},{5,29},{6,30},{7,31},{8,16},{9,... | collective-permute-start | bytes 49160 | tf_op jit(solution)/shard_map/ppermute | solution.py:23
  43.4 4.6 %collective-permute-start.14 = (bf16[1,4,2048]{2,1,0:T(4,128)(2,1)S(1)}, bf16[1,4,2048]{2,1,0:T(4,128)(2,1)S(1)}, u32[]{:S(2)}, u32[]{:S(2)}) collective-permute-start(bf16[1,4,2048]{2,1,0:T(4,128)(2,1)S(1)} %get-tuple-element.30), channel_id=1, source_target_pairs={{0,8},{1,9},{2,10},{3,11},{4,12},{5,13},{6,14},{7,15},{8,0},{9,1},... | collective-permute-start | bytes 49160 | tf_op jit(solution)/shard_map/ppermute | solution.py:23
  44.3 3.8 %collective-permute-start.15 = (bf16[1,4,2048]{2,1,0:T(4,128)(2,1)S(1)}, bf16[1,4,2048]{2,1,0:T(4,128)(2,1)S(1)}, u32[]{:S(2)}, u32[]{:S(2)}) collective-permute-start(bf16[1,4,2048]{2,1,0:T(4,128)(2,1)S(1)} %get-tuple-element.31), channel_id=1, source_target_pairs={{0,16},{1,17},{2,18},{3,19},{4,20},{5,21},{6,22},{7,23},{8,24},{9,... | collective-permute-start | bytes 49160 | tf_op jit(solution)/shard_map/ppermute | solution.py:23

commit v15 on v14

--- a/solution.py
+++ b/solution.py
@@ -13,14 +13,19 @@
 EXPERT = ("far", "core")
 
 
+def permute(value, masks_of):
+    groups, experts = lax.axis_size("dp"), lax.axis_size(EXPERT)
+    pairs = []
+    for g in range(groups):
+        for e in range(experts):
+            masks = masks_of[e % 2]
+            if masks is not None:
+                pairs.append((g * experts + e, (g ^ masks[0]) * experts + (e ^ masks[1])))
+    return lax.ppermute(value, ("dp",) + EXPERT, pairs)
+
+
 def swap(value, group_mask, expert_mask):
-    groups, experts = lax.axis_size("dp"), lax.axis_size(EXPERT)
-    pairs = [
-        (g * experts + e, (g ^ group_mask) * experts + (e ^ expert_mask))
-        for g in range(groups)
-        for e in range(experts)
-    ]
-    return lax.ppermute(value, ("dp",) + EXPERT, pairs)
+    return permute(value, ((group_mask, expert_mask),) * 2)
 
 
 def in_vmem(value):
@@ -136,29 +141,26 @@
     )(rows, in_vmem(w_gate), in_vmem(w_up))
 
 
-def contract_hidden(
-    parts, w_down, units, before=None, rows=None, half=None, index=None, kind=jnp.float32
-):
-    total_count, width = parts[0][0].shape[0], w_down.shape[1]
-    count = total_count if index is None else total_count // 2
-    offset = 0 if index is None else index * count
+def contract_hidden(parts, w_down, units, before=None, rows=None, half=None, split=False):
+    count, width = parts[0][0].shape[0], w_down.shape[1]
     experts = lax.axis_size(EXPERT)
     operands = [part for part, _, _ in parts] + [in_vmem(w_down)]
     operands += [value for value in (before, rows) if value is not None]
 
     def body(*refs):
         part_refs, down_ref = refs[: len(parts)], refs[len(parts)]
-        rest = list(refs[len(parts) + 1 : -1])
+        rest = list(refs[len(parts) + 1 : len(operands)])
+        outs = refs[len(operands) :]
         before_ref = rest.pop(0) if before is not None else None
         rows_ref = rest.pop(0) if rows is not None else None
         me, group = lax.axis_index(EXPERT), lax.axis_index("dp")
 
         def step(first, batch):
-            here = pl.ds(offset + first, batch)
+            here = pl.ds(first, batch)
             if half is None:
                 lefts = [ref[here, :] for ref in part_refs]
             else:
-                order = [i ^ 1 for i in range(offset // half, (offset + count) // half)]
+                order = [i ^ 1 for i in range(count // half)]
                 lefts = [
                     jnp.concatenate([ref[i * half : (i + 1) * half, :] for i in order])
                     for ref in part_refs
@@ -178,18 +180,35 @@
                     total = total + jnp.dot(left, right, preferred_element_type=jnp.float32)
                 if rows is not None:
                     total = total.astype(jnp.bfloat16).astype(jnp.float32) * scale
-                refs[-1][pl.ds(first, batch), cut] = total.astype(kind)
+                if not split:
+                    outs[0][here, cut] = total
+                    continue
+                size, core = count // 8, lax.axis_index("core")
+                for j in range(4):
+                    near = total[2 * j * size : (2 * j + 1) * size]
+                    away = total[(2 * j + 1) * size : (2 * j + 2) * size]
+                    kept, sent = slice(j * size, (j + 1) * size), (j ^ 2) * size
+                    outs[0][kept, cut] = jnp.where(core == 0, near, away)
+                    other = jnp.where(core == 0, away, near).astype(jnp.bfloat16)
+                    outs[1][sent : sent + size, cut] = other
 
         row_batches(count, step)
 
-    return pl.pallas_call(
-        body,
-        out_shape=jax.ShapeDtypeStruct((count, width), kind),
+    shape = jax.ShapeDtypeStruct((count, width), jnp.float32)
+    if split:
+        kinds = (jnp.float32, jnp.bfloat16)
+        shape = [jax.ShapeDtypeStruct((count // 2, width), kind) for kind in kinds]
+
+    return pl.pallas_call(
+        body,
+        out_shape=shape,
         in_specs=[pl.BlockSpec(memory_space=pltpu.VMEM)] * len(operands),
-        out_specs=pl.BlockSpec(memory_space=pltpu.VMEM),
+        out_specs=[pl.BlockSpec(memory_space=pltpu.VMEM)] * 2
+        if split
+        else pl.BlockSpec(memory_space=pltpu.VMEM),
         cost_estimate=pl.CostEstimate(flops=0, bytes_accessed=count * width, transcendentals=0),
         compiler_params=pltpu.CompilerParams(
-            vmem_limit_bytes=8 * total_count * width
+            vmem_limit_bytes=8 * count * width
             + (6 << 20)
             + (0 if rows is None else rows.nbytes)
         ),
@@ -226,25 +245,70 @@
     )(*inputs)
 
 
-def finish(parts, groups, dtype):
-    tokens, columns = parts[0][0].shape[1:]
-
-    def body(*refs):
+def add_to_own(own, one, two, shape):
+    count = own.shape[0] // 2
+
+    def body(own_ref, one_ref, two_ref, kept_ref, sent_ref):
+        core = lax.axis_index("core")
+
+        def block(i):
+            mine = jnp.where(core == 0, own_ref[i], two_ref[i].astype(jnp.float32))
+            return mine + one_ref[i].astype(jnp.float32)
+
+        for i in range(count):
+            kept_ref[i] = block(2 * i + core)
+            sent_ref[i ^ (count // 2)] = block(2 * i + 1 - core).astype(sent_ref.dtype)
+
+    return pl.pallas_call(
+        body,
+        out_shape=[
+            jax.ShapeDtypeStruct((count,) + shape, kind) for kind in (jnp.float32, one.dtype)
+        ],
+        in_specs=[pl.BlockSpec(memory_space=pltpu.VMEM)] * 3,
+        out_specs=[pl.BlockSpec(memory_space=pltpu.VMEM)] * 2,
+        compiler_params=pltpu.CompilerParams(vmem_limit_bytes=4 * own.nbytes + (4 << 20)),
+        name="add_to_own",
+    )(own, one, two)
+
+
+def pick_columns(own, one, two, shape):
+    def body(own_ref, one_ref, two_ref, kept_ref, sent_ref):
+        core = lax.axis_index("core")
+        for i, ref in enumerate((kept_ref, sent_ref)):
+            mine = jnp.where(core == 0, own_ref[i], two_ref[i].astype(jnp.float32))
+            ref[0] = mine.astype(ref.dtype)
+            ref[1] = one_ref[i].astype(ref.dtype)
+
+    return pl.pallas_call(
+        body,
+        out_shape=[jax.ShapeDtypeStruct((2,) + shape, kind) for kind in (jnp.float32, one.dtype)],
+        in_specs=[pl.BlockSpec(memory_space=pltpu.VMEM)] * 3,
+        out_specs=[pl.BlockSpec(memory_space=pltpu.VMEM)] * 2,
+        compiler_params=pltpu.CompilerParams(vmem_limit_bytes=4 * own.nbytes + (4 << 20)),
+        name="pick_columns",
+    )(own, one, two)
+
+
+def finish(kept, received, groups):
+    _, tokens, wide_columns = kept.shape
+    columns = 2 * wide_columns // groups
+
+    def body(kept_ref, received_ref, out_ref):
         group = lax.axis_index("dp")
-        for i in range(groups):
-            mine = [ref[0] for ref, (_, j) in zip(refs, parts) if i == j]
-            total = sum(value.astype(jnp.float32) for value in mine)
-            start = pl.multiple_of((group ^ i) * columns, LANES)
-            refs[-1][:, pl.ds(start, columns)] = total.astype(dtype)
-
-    return pl.pallas_call(
-        body,
-        out_shape=jax.ShapeDtypeStruct((tokens, groups * columns), dtype),
-        in_specs=[pl.BlockSpec(memory_space=pltpu.VMEM)] * len(parts),
+        for g in range(groups):
+            place = slice((g >> 1) * columns, ((g >> 1) + 1) * columns)
+            total = kept_ref[g & 1, :, place] + received_ref[g & 1, :, place].astype(jnp.float32)
+            start = pl.multiple_of((group ^ g) * columns, LANES)
+            out_ref[:, pl.ds(start, columns)] = total.astype(out_ref.dtype)
+
+    return pl.pallas_call(
+        body,
+        out_shape=jax.ShapeDtypeStruct((tokens, groups * columns), received.dtype),
+        in_specs=[pl.BlockSpec(memory_space=pltpu.VMEM)] * 2,
         out_specs=pl.BlockSpec(memory_space=pltpu.VMEM),
         compiler_params=pltpu.CompilerParams(vmem_limit_bytes=4 << 20),
         name="finish",
-    )(*[value for value, _ in parts])
+    )(kept, received)
 
 
 def local(tokens, expert_ids, gate_probs, w_gate, w_up, w_down):
@@ -287,23 +351,40 @@
     total = contract_hidden(parts, down_weights, units)
     for i in range(chunks - 1):
         total = contract_hidden(others[i], down_weights, units, total, half=half)
-    last = lambda index, kind: contract_hidden(
-        others[-1], down_weights, units, total, rows, half, index, kind
-    )
-    sent, kept = last(1, jnp.bfloat16), last(0, jnp.float32)
-
-    shape = (token_count, w_down.shape[2])
-    rest = [(g, h) for g in range(groups) for h in range(0, high, 2)]
-    slot = lambda g, y, h: (((g & 1) * 2 + y) * wide + (g >> 1)) * high + h
-    plan = [[slot(g, y, h + z) for g, h in rest] for y, z in ((0, 0), (1, 1), (0, 1), (1, 0))]
-    mine, *away = sum_stage([kept, swap(sent, 0, 1)], plan, shape, jnp.bfloat16)
-    inputs = [mine] + [swap(value, 0, mask) for value, mask in zip(away, (6, 4, 2))]
-    order = sorted(range(1, len(rest)), key=lambda i: (rest[i][1], rest[i][0]), reverse=True)
-    mine, *away = sum_stage(inputs, [[i] for i in [0] + order], shape, jnp.bfloat16)
-    parts = [
-        (swap(value, rest[i][0], 4 * rest[i][1]), rest[i][0]) for value, i in zip(away, order)
-    ]
-    return finish(parts + [(mine, 0)], groups, tokens.dtype)
+    columns = w_down.shape[2]
+    if rows.shape[0] <= BATCH:
+        kept, sent = contract_hidden(
+            others[-1], down_weights, units, total, rows, half, split=True
+        )
+    else:
+        total = contract_hidden(others[-1], down_weights, units, total, rows, half)
+        total = total.reshape(2, 2, 2, -1, columns)
+        core = lax.axis_index("core")
+        kept = lax.dynamic_index_in_dim(total, core, 2, False).reshape(-1, columns)
+        sent = lax.dynamic_index_in_dim(total, 1 - core, 2, False)[::-1]
+        sent = sent.reshape(-1, columns).astype(jnp.bfloat16)
+    inputs = [kept, swap(sent, 0, 1)]
+    if wide * high > 4:
+        total = kept + inputs[1].astype(jnp.float32)
+        total = total.reshape(4, wide, high // 4, 4 * token_count, columns)
+        send = lambda value, g, e: swap(value.astype(jnp.bfloat16), g, e).astype(jnp.float32)
+        total = total[:, :, 0] + sum(
+            send(total[:, :, i], 0, 16 * i) for i in range(1, high // 4)
+        )
+        total = [total[:, 0]] + [send(total[:, i], 2 * i, 0) for i in range(1, wide)]
+        inputs = [jnp.concatenate(total, axis=2).reshape(16, token_count, wide * columns)]
+    shape = (token_count, wide * columns)
+    low, up = range(0, 16, 2), range(1, 16, 2)
+    own, near, away = sum_stage(inputs, [low, low, up], shape, jnp.bfloat16)
+    one = permute(away, ((0, 4), (0, 6)))
+    two = permute(near, (None, (0, 2)))
+    kept, sent = add_to_own(own, one, two, shape)
+    inputs = [kept, swap(sent, 0, 1)]
+    own, near, away = sum_stage(inputs, [(0, 2), (0, 2), (1, 3)], shape, jnp.bfloat16)
+    one = permute(away, ((1, 0), (1, 8)))
+    two = permute(near, (None, (0, 8)))
+    kept, sent = pick_columns(own, one, two, shape)
+    return finish(kept, swap(sent, 0, 1), groups)
 
 
 def solution(mesh):

time: 48.8 us -> 51.7 us (1.059)
  waiting for transfers between devices: 21.9 us -> 24.8 us
    ppermute x16, waiting for transfers between devices: 21.9 us -> 24.8 us  [permute(): return lax.ppermute(value, ('dp',) + EXPERT, pairs)]
    pallas_call x4 -> x5, Pallas kernels: 2.16 us -> 1.74 us  [the longest x3 1.67 us: contract_hidden(): pl.pallas_call(body, out_shape=shape, in_specs=[pl.BlockSpec(memory_space...]
  transfers between devices with their start and end apart: 16 -> 16, of which waited for: 14 -> 13; matrix products, arithmetic and copies ran while one was open for 0% -> 0% of each run, Pallas kernels for 6% -> 5%
where the time goes in v15:
time: 51.7 us; the launch traced here: 51.6 us
  waiting for transfers between devices  24.8 us (48%)
  starting transfers between devices  20 us (39%)
  Pallas kernels  6.49 us (13%)
    ppermute x16, waiting for transfers between devices, permute(): return lax.ppermute(value, ('dp',) + EXPERT, pairs)  24.8 us
    ppermute x16, starting transfers between devices, permute(): return lax.ppermute(value, ('dp',) + EXPERT, pairs)  20 us
    pallas_call x2, Pallas kernels, expand_rows(): pl.pallas_call(body, out_shape=jax.ShapeDtypeStruct((count, columns), row...  2.78 us
    pallas_call x3, Pallas kernels, contract_hidden(): pl.pallas_call(body, out_shape=shape, in_specs=[pl.BlockSpec(memory_space...  1.67 us
  transfers between devices with their start and end apart: 16, of which 13 were waited for; matrix products, arithmetic and copies ran while one was open for 0% of the time, Pallas kernels for 5%

profile of v15, /device:TPU:0, one launch (start us, length us, event | category | flops | bytes accessed | tf_op | source)
XLA Modules:
  0.0 51.6 jit_solution(6606491931608827300)
XLA Ops:
  0.0 1.0 %pack_block.1.refs_0_ = bf16[4,4224]{1,0:T(4,128)(2,1)S(1)} custom-call(bf16[4,4096]{1,0:T(4,128)(2,1)} %tokens_ref.1, s32[4,8]{1,0:T(4,128)} %ids_ref.1, f32[4,8]{1,0:T(4,128)} %probs_ref.1), custom_call_target="tpu_custom_call" | custom-call | flops 60000002048 | tf_op jit(solution)/shard_map/pack_block/pallas_call | solution.py:68
  1.0 5.1 %collective-permute-start.2 = (bf16[4,4224]{1,0:T(4,128)(2,1)S(1)}, bf16[4,4224]{1,0:T(4,128)(2,1)S(1)}, u32[]{:S(2)}, u32[]{:S(2)}) collective-permute-start(bf16[4,4224]{1,0:T(4,128)(2,1)S(1)} %pack_block.1.refs_0_), channel_id=1, source_target_pairs={{0,12},{1,13},{2,14},{3,15},{4,8},{5,9},{6,10},{7,11},{8,4},{9,5},... | collective-permute-start | bytes 101384 | tf_op jit(solution)/shard_map/ppermute | solution.py:24
  6.1 0.0 collective-permute-start.1
  6.1 0.6 %collective-permute-start = (bf16[4,4224]{1,0:T(4,128)(2,1)S(1)}, bf16[4,4224]{1,0:T(4,128)(2,1)S(1)}, u32[]{:S(2)}, u32[]{:S(2)}) collective-permute-start(bf16[4,4224]{1,0:T(4,128)(2,1)S(1)} %pack_block.1.refs_0_), channel_id=1, source_target_pairs={{0,4},{1,5},{2,6},{3,7},{4,0},{5,1},{6,2},{7,3},{8,12},{9,13},{10,... | collective-permute-start | bytes 101384 | tf_op jit(solution)/shard_map/ppermute | solution.py:24
  6.8 1.3 %collective-permute-done.2.refs_3_ = bf16[4,4224]{1,0:T(4,128)(2,1)S(1)} collective-permute-done((bf16[4,4224]{1,0:T(4,128)(2,1)S(1)}, bf16[4,4224]{1,0:T(4,128)(2,1)S(1)}, u32[]{:S(2)}, u32[]{:S(2)}) %collective-permute-start.2) | collective-permute-done | bytes 33824 | tf_op jit(solution)/shard_map/ppermute | solution.py:24
  8.0 2.9 %collective-permute-done.1.refs_2_ = bf16[4,4224]{1,0:T(4,128)(2,1)S(1)} collective-permute-done((bf16[4,4224]{1,0:T(4,128)(2,1)S(1)}, bf16[4,4224]{1,0:T(4,128)(2,1)S(1)}, u32[]{:S(2)}, u32[]{:S(2)}) %collective-permute-start.1) | collective-permute-done | bytes 33824 | tf_op jit(solution)/shard_map/ppermute | solution.py:24
  11.0 0.0 collective-permute-done.refs_1_
  11.0 2.5 %collective-permute-start.5 = (bf16[4,4,4224]{2,1,0:T(4,128)(2,1)S(1)}, bf16[4,4,4224]{2,1,0:T(4,128)(2,1)S(1)}, u32[]{:S(2)}, u32[]{:S(2)}) collective-permute-start(bf16[4,4,4224]{2,1,0:T(4,128)(2,1)S(1)} %stack_blocks.1.refs_0_), channel_id=1, source_target_pairs={{0,18},{1,19},{2,16},{3,17},{4,22},{5,23},{6,20},{7,21},{8,26},{9,... | collective-permute-start | bytes 405512 | tf_op jit(solution)/shard_map/ppermute | solution.py:24
  13.5 0.5 %collective-permute-start.4 = (bf16[4,4,4224]{2,1,0:T(4,128)(2,1)S(1)}, bf16[4,4,4224]{2,1,0:T(4,128)(2,1)S(1)}, u32[]{:S(2)}, u32[]{:S(2)}) collective-permute-start(bf16[4,4,4224]{2,1,0:T(4,128)(2,1)S(1)} %stack_blocks.1.refs_0_), channel_id=1, source_target_pairs={{0,16},{1,17},{2,18},{3,19},{4,20},{5,21},{6,22},{7,23},{8,24},{9,... | collective-permute-start | bytes 405512 | tf_op jit(solution)/shard_map/ppermute | solution.py:24
  14.0 0.5 collective-permute-start.3
  14.5 2.8 %collective-permute-done.5.refs_3_ = bf16[4,4,4224]{2,1,0:T(4,128)(2,1)S(1)} collective-permute-done((bf16[4,4,4224]{2,1,0:T(4,128)(2,1)S(1)}, bf16[4,4,4224]{2,1,0:T(4,128)(2,1)S(1)}, u32[]{:S(2)}, u32[]{:S(2)}) %collective-permute-start.5) | collective-permute-done | bytes 135200 | tf_op jit(solution)/shard_map/ppermute | solution.py:24
  17.4 1.4 %collective-permute-done.4.refs_2_ = bf16[4,4,4224]{2,1,0:T(4,128)(2,1)S(1)} collective-permute-done((bf16[4,4,4224]{2,1,0:T(4,128)(2,1)S(1)}, bf16[4,4,4224]{2,1,0:T(4,128)(2,1)S(1)}, u32[]{:S(2)}, u32[]{:S(2)}) %collective-permute-start.4) | collective-permute-done | bytes 135200 | tf_op jit(solution)/shard_map/ppermute | solution.py:24
  18.8 0.2 collective-permute-done.3.refs_1_
  19.0 0.1 join_rows.1
  19.2 0.1 collective-permute-start.6
  19.3 1.9 %collective-permute-done.6 = bf16[64,4224]{1,0:T(8,128)(2,1)S(1)} collective-permute-done((bf16[64,4224]{1,0:T(8,128)(2,1)S(1)}, bf16[64,4224]{1,0:T(8,128)(2,1)S(1)}, u32[]{:S(2)}, u32[]{:S(2)}) %collective-permute-start.6) | collective-permute-done | bytes 540704 | tf_op jit(solution)/shard_map/ppermute | solution.py:24
  21.2 0.1 pad_maximum_fusion.rows_ref.refs_3_
  21.3 0.0 copy-done
  21.3 0.0 copy-done.1
  21.3 0.0 slice-start
  21.3 1.4 %expand_rows.2.refs_0_ = bf16[128,512]{1,0:T(8,128)(2,1)S(1)} custom-call(bf16[128,4224]{1,0:T(8,128)(2,1)S(1)} %pad_maximum_fusion.rows_ref.refs_3_, bf16[4096,1024]{1,0:T(8,128)(2,1)S(1)} %bitcast.8, bf16[4096,1024]{1,0:T(8,128)(2,1)S(1)} %bitcast.10), custom_call_target="tpu_custom_call" | custom-call | bytes 65536 | tf_op jit(solution)/shard_map/expand_rows/pallas_call | solution.py:133
  22.7 0.0 slice-start.1
  22.7 1.5 %collective-permute-start.8 = (bf16[128,512]{1,0:T(8,128)(2,1)S(1)}, bf16[128,512]{1,0:T(8,128)(2,1)S(1)}, u32[]{:S(2)}, u32[]{:S(2)}) collective-permute-start(bf16[128,512]{1,0:T(8,128)(2,1)S(1)} %expand_rows.2.refs_0_), channel_id=1, source_target_pairs={{0,16},{1,17},{2,18},{3,19},{4,20},{5,21},{6,22},{7,23},{8,24},{9,... | collective-permute-start | bytes 393224 | tf_op jit(solution)/shard_map/ppermute | solution.py:24
  24.2 1.4 %expand_rows.3.refs_1_ = bf16[128,512]{1,0:T(8,128)(2,1)S(1)} custom-call(bf16[128,4224]{1,0:T(8,128)(2,1)S(1)} %pad_maximum_fusion.rows_ref.refs_3_, bf16[4096,1024]{1,0:T(8,128)(2,1)S(1)} %bitcast.9, bf16[4096,1024]{1,0:T(8,128)(2,1)S(1)} %bitcast.11), custom_call_target="tpu_custom_call" | custom-call | bytes 65536 | tf_op jit(solution)/shard_map/expand_rows/pallas_call | solution.py:133
  25.6 0.6 %collective-permute-start.7 = (bf16[128,512]{1,0:T(8,128)(2,1)S(1)}, bf16[128,512]{1,0:T(8,128)(2,1)S(1)}, u32[]{:S(2)}, u32[]{:S(2)}) collective-permute-start(bf16[128,512]{1,0:T(8,128)(2,1)S(1)} %expand_rows.3.refs_1_), channel_id=1, source_target_pairs={{0,16},{1,17},{2,18},{3,19},{4,20},{5,21},{6,22},{7,23},{8,24},{9,... | collective-permute-start | bytes 393224 | tf_op jit(solution)/shard_map/ppermute | solution.py:24
  26.3 0.0 slice-done.1
  26.3 0.7 %contract_hidden.3.refs_2_ = f32[128,2048]{1,0:T(8,128)S(1)} custom-call(bf16[128,512]{1,0:T(8,128)(2,1)S(1)} %expand_rows.2.refs_0_, bf16[128,512]{1,0:T(8,128)(2,1)S(1)} %expand_rows.3.refs_1_, bf16[2048,2048]{1,0:T(8,128)(2,1)S(1)} %bitcast.5), custom_call_target="tpu_custom_call" | custom-call | bytes 262144 | tf_op jit(solution)/shard_map/contract_hidden/pallas_call | solution.py:202
  27.0 1.4 %collective-permute-done.8.refs_0_ = bf16[128,512]{1,0:T(8,128)(2,1)S(1)} collective-permute-done((bf16[128,512]{1,0:T(8,128)(2,1)S(1)}, bf16[128,512]{1,0:T(8,128)(2,1)S(1)}, u32[]{:S(2)}, u32[]{:S(2)}) %collective-permute-start.8) | collective-permute-done | bytes 131104 | tf_op jit(solution)/shard_map/ppermute | solution.py:24
  28.4 0.5 contract_hidden.4.refs_2_
  28.8 2.3 %collective-permute-done.7.refs_0_ = bf16[128,512]{1,0:T(8,128)(2,1)S(1)} collective-permute-done((bf16[128,512]{1,0:T(8,128)(2,1)S(1)}, bf16[128,512]{1,0:T(8,128)(2,1)S(1)}, u32[]{:S(2)}, u32[]{:S(2)}) %collective-permute-start.7) | collective-permute-done | bytes 131104 | tf_op jit(solution)/shard_map/ppermute | solution.py:24
  31.1 0.5 contract_hidden.5
  31.6 0.1 collective-permute-start.9
  31.7 1.5 %collective-permute-done.9.refs_1_ = bf16[64,2048]{1,0:T(8,128)(2,1)S(1)} collective-permute-done((bf16[64,2048]{1,0:T(8,128)(2,1)S(1)}, bf16[64,2048]{1,0:T(8,128)(2,1)S(1)}, u32[]{:S(2)}, u32[]{:S(2)}) %collective-permute-start.9) | collective-permute-done | bytes 262176 | tf_op jit(solution)/shard_map/ppermute | solution.py:24
  33.2 0.2 sum_stage.2
  33.4 0.1 collective-permute-start.10
  33.5 0.7 %collective-permute-start.11 = (bf16[8,4,2048]{2,1,0:T(4,128)(2,1)S(1)}, bf16[8,4,2048]{2,1,0:T(4,128)(2,1)S(1)}, u32[]{:S(2)}, u32[]{:S(2)}) collective-permute-start(bf16[8,4,2048]{2,1,0:T(4,128)(2,1)S(1)} %get-tuple-element.33), channel_id=1, source_target_pairs={{1,3},{3,1},{5,7},{7,5},{9,11},{11,9},{13,15},{15,13},{17,19},{19,... | collective-permute-start | bytes 393224 | tf_op jit(solution)/shard_map/ppermute | solution.py:24
  34.1 5.5 %collective-permute-done.10.one_ref = bf16[8,4,2048]{2,1,0:T(4,128)(2,1)S(1)} collective-permute-done((bf16[8,4,2048]{2,1,0:T(4,128)(2,1)S(1)}, bf16[8,4,2048]{2,1,0:T(4,128)(2,1)S(1)}, u32[]{:S(2)}, u32[]{:S(2)}) %collective-permute-start.10) | collective-permute-done | bytes 131104 | tf_op jit(solution)/shard_map/ppermute | solution.py:24
  39.6 0.0 collective-permute-done.11.two_ref
  39.6 0.1 add_to_own.1
  39.7 0.6 %collective-permute-start.12 = (bf16[4,4,2048]{2,1,0:T(4,128)(2,1)S(1)}, bf16[4,4,2048]{2,1,0:T(4,128)(2,1)S(1)}, u32[]{:S(2)}, u32[]{:S(2)}) collective-permute-start(bf16[4,4,2048]{2,1,0:T(4,128)(2,1)S(1)} %get-tuple-element.35), channel_id=1, source_target_pairs={{0,1},{1,0},{2,3},{3,2},{4,5},{5,4},{6,7},{7,6},{8,9},{9,8},{10,11... | collective-permute-start | bytes 196616 | tf_op jit(solution)/shard_map/ppermute | solution.py:24
  40.3 0.9 %collective-permute-done.12.refs_1_ = bf16[4,4,2048]{2,1,0:T(4,128)(2,1)S(1)} collective-permute-done((bf16[4,4,2048]{2,1,0:T(4,128)(2,1)S(1)}, bf16[4,4,2048]{2,1,0:T(4,128)(2,1)S(1)}, u32[]{:S(2)}, u32[]{:S(2)}) %collective-permute-start.12) | collective-permute-done | bytes 65568 | tf_op jit(solution)/shard_map/ppermute | solution.py:24
  41.2 1.6 %collective-permute-start.13 = (bf16[2,4,2048]{2,1,0:T(4,128)(2,1)S(1)}, bf16[2,4,2048]{2,1,0:T(4,128)(2,1)S(1)}, u32[]{:S(2)}, u32[]{:S(2)}) collective-permute-start(bf16[2,4,2048]{2,1,0:T(4,128)(2,1)S(1)} %get-tuple-element.37), channel_id=1, source_target_pairs={{0,16},{1,25},{2,18},{3,27},{4,20},{5,29},{6,22},{7,31},{8,24},{9,... | collective-permute-start | bytes 98312 | tf_op jit(solution)/shard_map/ppermute | solution.py:24
  42.8 0.7 %collective-permute-start.14 = (bf16[2,4,2048]{2,1,0:T(4,128)(2,1)S(1)}, bf16[2,4,2048]{2,1,0:T(4,128)(2,1)S(1)}, u32[]{:S(2)}, u32[]{:S(2)}) collective-permute-start(bf16[2,4,2048]{2,1,0:T(4,128)(2,1)S(1)} %get-tuple-element.38), channel_id=1, source_target_pairs={{1,9},{3,11},{5,13},{7,15},{9,1},{11,3},{13,5},{15,7},{17,25},{19,... | collective-permute-start | bytes 98312 | tf_op jit(solution)/shard_map/ppermute | solution.py:24
  43.4 1.8 %collective-permute-done.13.one_ref = bf16[2,4,2048]{2,1,0:T(4,128)(2,1)S(1)} collective-permute-done((bf16[2,4,2048]{2,1,0:T(4,128)(2,1)S(1)}, bf16[2,4,2048]{2,1,0:T(4,128)(2,1)S(1)}, u32[]{:S(2)}, u32[]{:S(2)}) %collective-permute-start.13) | collective-permute-done | bytes 32800 | tf_op jit(solution)/shard_map/ppermute | solution.py:24
  45.2 0.0 collective-permute-done.14.two_ref
  45.2 4.9 %collective-permute-start.15 = (bf16[2,4,2048]{2,1,0:T(4,128)(2,1)S(1)}, bf16[2,4,2048]{2,1,0:T(4,128)(2,1)S(1)}, u32[]{:S(2)}, u32[]{:S(2)}) collective-permute-start(bf16[2,4,2048]{2,1,0:T(4,128)(2,1)S(1)} %get-tuple-element.40), channel_id=1, source_target_pairs={{0,1},{1,0},{2,3},{3,2},{4,5},{5,4},{6,7},{7,6},{8,9},{9,8},{10,11... | collective-permute-start | bytes 98312 | tf_op jit(solution)/shard_map/ppermute | solution.py:24
  50.1 0.9 %collective-permute-done.15.received_ref = bf16[2,4,2048]{2,1,0:T(4,128)(2,1)S(1)} collective-permute-done((bf16[2,4,2048]{2,1,0:T(4,128)(2,1)S(1)}, bf16[2,4,2048]{2,1,0:T(4,128)(2,1)S(1)}, u32[]{:S(2)}, u32[]{:S(2)}) %collective-permute-start.15) | collective-permute-done | bytes 32800 | tf_op jit(solution)/shard_map/ppermute | solution.py:24
  50.9 0.6 %finish.1 = bf16[4,4096]{1,0:T(4,128)(2,1)} custom-call(f32[2,4,2048]{2,1,0:T(4,128)S(1)} %get-tuple-element.39.kept_ref, bf16[2,4,2048]{2,1,0:T(4,128)(2,1)S(1)} %collective-permute-done.15.received_ref), custom_call_target="tpu_custom_call" | custom-call | tf_op jit(solution)/shard_map/finish/pallas_call | solution.py:304
  (7 shorter events, 0.1 us)
Async XLA Ops:
  0.0 21.3 %copy-start = (bf16[1,4096,1024]{2,1,0:T(8,128)(2,1)S(1)}, bf16[1,4096,1024]{2,1,0:T(8,128)(2,1)}, u32[]{:S(2)}) copy-start(bf16[1,4096,1024]{2,1,0:T(8,128)(2,1)} %param.9) | copy-start | bytes 25165828
  0.0 21.3 %copy-start.1 = (bf16[1,4096,1024]{2,1,0:T(8,128)(2,1)S(1)}, bf16[1,4096,1024]{2,1,0:T(8,128)(2,1)}, u32[]{:S(2)}) copy-start(bf16[1,4096,1024]{2,1,0:T(8,128)(2,1)} %param.10) | copy-start | bytes 25165828
  1.0 7.0 %collective-permute-start.2 = (bf16[4,4224]{1,0:T(4,128)(2,1)S(1)}, bf16[4,4224]{1,0:T(4,128)(2,1)S(1)}, u32[]{:S(2)}, u32[]{:S(2)}) collective-permute-start(bf16[4,4224]{1,0:T(4,128)(2,1)S(1)} %pack_block.1.refs_0_), channel_id=1, source_target_pairs={{0,12},{1,13},{2,14},{3,15},{4,8},{5,9},{6,10},{7,11},{8,4},{9,5},... | collective-permute-start | bytes 101384 | tf_op jit(solution)/shard_map/ppermute | solution.py:24
  6.1 4.8 %collective-permute-start.1 = (bf16[4,4224]{1,0:T(4,128)(2,1)S(1)}, bf16[4,4224]{1,0:T(4,128)(2,1)S(1)}, u32[]{:S(2)}, u32[]{:S(2)}) collective-permute-start(bf16[4,4224]{1,0:T(4,128)(2,1)S(1)} %pack_block.1.refs_0_), channel_id=1, source_target_pairs={{0,8},{1,9},{2,10},{3,11},{4,12},{5,13},{6,14},{7,15},{8,0},{9,1},... | collective-permute-start | bytes 101384 | tf_op jit(solution)/shard_map/ppermute | solution.py:24
  6.1 4.8 %collective-permute-start = (bf16[4,4224]{1,0:T(4,128)(2,1)S(1)}, bf16[4,4224]{1,0:T(4,128)(2,1)S(1)}, u32[]{:S(2)}, u32[]{:S(2)}) collective-permute-start(bf16[4,4224]{1,0:T(4,128)(2,1)S(1)} %pack_block.1.refs_0_), channel_id=1, source_target_pairs={{0,4},{1,5},{2,6},{3,7},{4,0},{5,1},{6,2},{7,3},{8,12},{9,13},{10,... | collective-permute-start | bytes 101384 | tf_op jit(solution)/shard_map/ppermute | solution.py:24
  11.0 6.4 %collective-permute-start.5 = (bf16[4,4,4224]{2,1,0:T(4,128)(2,1)S(1)}, bf16[4,4,4224]{2,1,0:T(4,128)(2,1)S(1)}, u32[]{:S(2)}, u32[]{:S(2)}) collective-permute-start(bf16[4,4,4224]{2,1,0:T(4,128)(2,1)S(1)} %stack_blocks.1.refs_0_), channel_id=1, source_target_pairs={{0,18},{1,19},{2,16},{3,17},{4,22},{5,23},{6,20},{7,21},{8,26},{9,... | collective-permute-start | bytes 405512 | tf_op jit(solution)/shard_map/ppermute | solution.py:24
  13.5 5.3 %collective-permute-start.4 = (bf16[4,4,4224]{2,1,0:T(4,128)(2,1)S(1)}, bf16[4,4,4224]{2,1,0:T(4,128)(2,1)S(1)}, u32[]{:S(2)}, u32[]{:S(2)}) collective-permute-start(bf16[4,4,4224]{2,1,0:T(4,128)(2,1)S(1)} %stack_blocks.1.refs_0_), channel_id=1, source_target_pairs={{0,16},{1,17},{2,18},{3,19},{4,20},{5,21},{6,22},{7,23},{8,24},{9,... | collective-permute-start | bytes 405512 | tf_op jit(solution)/shard_map/ppermute | solution.py:24
  14.0 5.0 %collective-permute-start.3 = (bf16[4,4,4224]{2,1,0:T(4,128)(2,1)S(1)}, bf16[4,4,4224]{2,1,0:T(4,128)(2,1)S(1)}, u32[]{:S(2)}, u32[]{:S(2)}) collective-permute-start(bf16[4,4,4224]{2,1,0:T(4,128)(2,1)S(1)} %stack_blocks.1.refs_0_), channel_id=1, source_target_pairs={{0,2},{1,3},{2,0},{3,1},{4,6},{5,7},{6,4},{7,5},{8,10},{9,11},{10,... | collective-permute-start | bytes 405512 | tf_op jit(solution)/shard_map/ppermute | solution.py:24
  19.2 2.0 %collective-permute-start.6 = (bf16[64,4224]{1,0:T(8,128)(2,1)S(1)}, bf16[64,4224]{1,0:T(8,128)(2,1)S(1)}, u32[]{:S(2)}, u32[]{:S(2)}) collective-permute-start(bf16[64,4224]{1,0:T(8,128)(2,1)S(1)} %join_rows.1), channel_id=1, source_target_pairs={{0,1},{1,0},{2,3},{3,2},{4,5},{5,4},{6,7},{7,6},{8,9},{9,8},{10,11... | collective-permute-start | bytes 1622024 | tf_op jit(solution)/shard_map/ppermute | solution.py:24
  21.3 5.0 %slice-start = ((s8[8388608]{0:T(1024)(128)(4,1)}), s8[4194304]{0:T(1024)(128)(4,1)S(1)}, s32[]{:S(2)}) async-start(s8[8388608]{0:T(1024)(128)(4,1)} %bitcast.3), calls=%async_computation | async-start | bytes 8388608
  22.7 3.6 %slice-start.1 = ((s8[8388608]{0:T(1024)(128)(4,1)}), s8[4194304]{0:T(1024)(128)(4,1)S(1)}, s32[]{:S(2)}) async-start(s8[8388608]{0:T(1024)(128)(4,1)} %bitcast.3), calls=%async_computation.1 | async-start | bytes 8388608
  22.7 5.7 %collective-permute-start.8 = (bf16[128,512]{1,0:T(8,128)(2,1)S(1)}, bf16[128,512]{1,0:T(8,128)(2,1)S(1)}, u32[]{:S(2)}, u32[]{:S(2)}) collective-permute-start(bf16[128,512]{1,0:T(8,128)(2,1)S(1)} %expand_rows.2.refs_0_), channel_id=1, source_target_pairs={{0,16},{1,17},{2,18},{3,19},{4,20},{5,21},{6,22},{7,23},{8,24},{9,... | collective-permute-start | bytes 393224 | tf_op jit(solution)/shard_map/ppermute | solution.py:24
  25.6 5.5 %collective-permute-start.7 = (bf16[128,512]{1,0:T(8,128)(2,1)S(1)}, bf16[128,512]{1,0:T(8,128)(2,1)S(1)}, u32[]{:S(2)}, u32[]{:S(2)}) collective-permute-start(bf16[128,512]{1,0:T(8,128)(2,1)S(1)} %expand_rows.3.refs_1_), channel_id=1, source_target_pairs={{0,16},{1,17},{2,18},{3,19},{4,20},{5,21},{6,22},{7,23},{8,24},{9,... | collective-permute-start | bytes 393224 | tf_op jit(solution)/shard_map/ppermute | solution.py:24
  31.6 1.6 %collective-permute-start.9 = (bf16[64,2048]{1,0:T(8,128)(2,1)S(1)}, bf16[64,2048]{1,0:T(8,128)(2,1)S(1)}, u32[]{:S(2)}, u32[]{:S(2)}) collective-permute-start(bf16[64,2048]{1,0:T(8,128)(2,1)S(1)} %get-tuple-element.30), channel_id=1, source_target_pairs={{0,1},{1,0},{2,3},{3,2},{4,5},{5,4},{6,7},{7,6},{8,9},{9,8},{10,11... | collective-permute-start | bytes 786440 | tf_op jit(solution)/shard_map/ppermute | solution.py:24
  33.4 6.3 %collective-permute-start.10 = (bf16[8,4,2048]{2,1,0:T(4,128)(2,1)S(1)}, bf16[8,4,2048]{2,1,0:T(4,128)(2,1)S(1)}, u32[]{:S(2)}, u32[]{:S(2)}) collective-permute-start(bf16[8,4,2048]{2,1,0:T(4,128)(2,1)S(1)} %get-tuple-element.32), channel_id=1, source_target_pairs={{0,4},{1,7},{2,6},{3,5},{4,0},{5,3},{6,2},{7,1},{8,12},{9,15},{10,... | collective-permute-start | bytes 393224 | tf_op jit(solution)/shard_map/ppermute | solution.py:24
  33.5 6.2 %collective-permute-start.11 = (bf16[8,4,2048]{2,1,0:T(4,128)(2,1)S(1)}, bf16[8,4,2048]{2,1,0:T(4,128)(2,1)S(1)}, u32[]{:S(2)}, u32[]{:S(2)}) collective-permute-start(bf16[8,4,2048]{2,1,0:T(4,128)(2,1)S(1)} %get-tuple-element.33), channel_id=1, source_target_pairs={{1,3},{3,1},{5,7},{7,5},{9,11},{11,9},{13,15},{15,13},{17,19},{19,... | collective-permute-start | bytes 393224 | tf_op jit(solution)/shard_map/ppermute | solution.py:24
  39.7 1.5 %collective-permute-start.12 = (bf16[4,4,2048]{2,1,0:T(4,128)(2,1)S(1)}, bf16[4,4,2048]{2,1,0:T(4,128)(2,1)S(1)}, u32[]{:S(2)}, u32[]{:S(2)}) collective-permute-start(bf16[4,4,2048]{2,1,0:T(4,128)(2,1)S(1)} %get-tuple-element.35), channel_id=1, source_target_pairs={{0,1},{1,0},{2,3},{3,2},{4,5},{5,4},{6,7},{7,6},{8,9},{9,8},{10,11... | collective-permute-start | bytes 196616 | tf_op jit(solution)/shard_map/ppermute | solution.py:24
  41.2 4.0 %collective-permute-start.13 = (bf16[2,4,2048]{2,1,0:T(4,128)(2,1)S(1)}, bf16[2,4,2048]{2,1,0:T(4,128)(2,1)S(1)}, u32[]{:S(2)}, u32[]{:S(2)}) collective-permute-start(bf16[2,4,2048]{2,1,0:T(4,128)(2,1)S(1)} %get-tuple-element.37), channel_id=1, source_target_pairs={{0,16},{1,25},{2,18},{3,27},{4,20},{5,29},{6,22},{7,31},{8,24},{9,... | collective-permute-start | bytes 98312 | tf_op jit(solution)/shard_map/ppermute | solution.py:24
  42.8 2.4 %collective-permute-start.14 = (bf16[2,4,2048]{2,1,0:T(4,128)(2,1)S(1)}, bf16[2,4,2048]{2,1,0:T(4,128)(2,1)S(1)}, u32[]{:S(2)}, u32[]{:S(2)}) collective-permute-start(bf16[2,4,2048]{2,1,0:T(4,128)(2,1)S(1)} %get-tuple-element.38), channel_id=1, source_target_pairs={{1,9},{3,11},{5,13},{7,15},{9,1},{11,3},{13,5},{15,7},{17,25},{19,... | collective-permute-start | bytes 98312 | tf_op jit(solution)/shard_map/ppermute | solution.py:24
  45.2 5.7 %collective-permute-start.15 = (bf16[2,4,2048]{2,1,0:T(4,128)(2,1)S(1)}, bf16[2,4,2048]{2,1,0:T(4,128)(2,1)S(1)}, u32[]{:S(2)}, u32[]{:S(2)}) collective-permute-start(bf16[2,4,2048]{2,1,0:T(4,128)(2,1)S(1)} %get-tuple-element.40), channel_id=1, source_target_pairs={{0,1},{1,0},{2,3},{3,2},{4,5},{5,4},{6,7},{7,6},{8,9},{9,8},{10,11... | collective-permute-start | bytes 98312 | tf_op jit(solution)/shard_map/ppermute | solution.py:24

commit v16 on v14

--- a/solution.py
+++ b/solution.py
@@ -259,8 +259,14 @@
     near = stack_blocks([block] + [swap(block, 0, 4 * i) for i in range(1, high)])
     if wide > 1:
         near = jnp.concatenate([near] + [swap(near, 2 * i, 0) for i in range(1, wide)])
-    chip = join_rows([near, swap(near, 0, 2), swap(near, 1, 0), swap(near, 1, 2)])
-    rows = jnp.concatenate([chip, swap(chip, 0, 1)])
+    over_y = swap(near, 0, 2)
+    first = join_rows([near, swap(near, 1, 0), swap(near, 1, 2)])
+    last = join_rows([over_y])
+    size = last.shape[0]
+    rows = []
+    for one, two in ((first, last), (swap(first, 0, 1), swap(last, 0, 1))):
+        rows += [one[:size], two, one[size:]]
+    rows = jnp.concatenate(rows)
 
     chunks = CHUNKS if units % (LANES * CHUNKS) == 0 else 1
     step = units // chunks

time: 48.8 us -> 48.2 us (0.988)
  waiting for transfers between devices: 21.9 us -> 20.6 us
  starting transfers between devices: 19.6 us -> 20.2 us
    ppermute x16 -> x17, waiting for transfers between devices: 21.9 us -> 20.6 us  [swap(): return lax.ppermute(value, ('dp',) + EXPERT, pairs)]
    ppermute x16 -> x17, starting transfers between devices: 19.6 us -> 20.2 us  [swap(): return lax.ppermute(value, ('dp',) + EXPERT, pairs)]
  transfers between devices with their start and end apart: 16 -> 17, of which waited for: 14 -> 14; matrix products, arithmetic and copies ran while one was open for 0% -> 0% of each run, Pallas kernels for 6% -> 7%
where the time goes in v16:
time: 48.2 us; the launch traced here: 48.1 us
  waiting for transfers between devices  20.6 us (43%)
  starting transfers between devices  20.2 us (42%)
  Pallas kernels  7.04 us (15%)
    ppermute x17, waiting for transfers between devices, swap(): return lax.ppermute(value, ('dp',) + EXPERT, pairs)  20.6 us
    ppermute x17, starting transfers between devices, swap(): return lax.ppermute(value, ('dp',) + EXPERT, pairs)  20.2 us
    pallas_call x2, Pallas kernels, expand_rows(): pl.pallas_call(body, out_shape=jax.ShapeDtypeStruct((count, columns), row...  2.82 us
    pallas_call x4, Pallas kernels, contract_hidden(): pl.pallas_call(body, out_shape=jax.ShapeDtypeStruct((count, width), kind)...  2.25 us
    pallas_call x1, Pallas kernels, pack_block(): pl.pallas_call(body, out_shape=jax.ShapeDtypeStruct((count, width + LANES...  1.02 us
  transfers between devices with their start and end apart: 17, of which 14 were waited for; matrix products, arithmetic and copies ran while one was open for 0% of the time, Pallas kernels for 7%

profile of v16, /device:TPU:0, one launch (start us, length us, event | category | flops | bytes accessed | tf_op | source)
XLA Modules:
  0.0 48.1 jit_solution(3550418951675814928)
XLA Ops:
  0.0 1.0 %pack_block.1.refs_0_ = bf16[4,4224]{1,0:T(4,128)(2,1)S(1)} custom-call(bf16[4,4096]{1,0:T(4,128)(2,1)} %tokens_ref.1, s32[4,8]{1,0:T(4,128)} %ids_ref.1, f32[4,8]{1,0:T(4,128)} %probs_ref.1), custom_call_target="tpu_custom_call" | custom-call | flops 60000002048 | tf_op jit(solution)/shard_map/pack_block/pallas_call | solution.py:63
  1.0 5.1 %collective-permute-start.2 = (bf16[4,4224]{1,0:T(4,128)(2,1)S(1)}, bf16[4,4224]{1,0:T(4,128)(2,1)S(1)}, u32[]{:S(2)}, u32[]{:S(2)}) collective-permute-start(bf16[4,4224]{1,0:T(4,128)(2,1)S(1)} %pack_block.1.refs_0_), channel_id=1, source_target_pairs={{0,12},{1,13},{2,14},{3,15},{4,8},{5,9},{6,10},{7,11},{8,4},{9,5},... | collective-permute-start | bytes 101384 | tf_op jit(solution)/shard_map/ppermute | solution.py:23
  6.1 0.0 collective-permute-start.1
  6.1 0.6 %collective-permute-start = (bf16[4,4224]{1,0:T(4,128)(2,1)S(1)}, bf16[4,4224]{1,0:T(4,128)(2,1)S(1)}, u32[]{:S(2)}, u32[]{:S(2)}) collective-permute-start(bf16[4,4224]{1,0:T(4,128)(2,1)S(1)} %pack_block.1.refs_0_), channel_id=1, source_target_pairs={{0,4},{1,5},{2,6},{3,7},{4,0},{5,1},{6,2},{7,3},{8,12},{9,13},{10,... | collective-permute-start | bytes 101384 | tf_op jit(solution)/shard_map/ppermute | solution.py:23
  6.8 1.3 %collective-permute-done.2.refs_3_ = bf16[4,4224]{1,0:T(4,128)(2,1)S(1)} collective-permute-done((bf16[4,4224]{1,0:T(4,128)(2,1)S(1)}, bf16[4,4224]{1,0:T(4,128)(2,1)S(1)}, u32[]{:S(2)}, u32[]{:S(2)}) %collective-permute-start.2) | collective-permute-done | bytes 33824 | tf_op jit(solution)/shard_map/ppermute | solution.py:23
  8.0 2.9 %collective-permute-done.1.refs_2_ = bf16[4,4224]{1,0:T(4,128)(2,1)S(1)} collective-permute-done((bf16[4,4224]{1,0:T(4,128)(2,1)S(1)}, bf16[4,4224]{1,0:T(4,128)(2,1)S(1)}, u32[]{:S(2)}, u32[]{:S(2)}) %collective-permute-start.1) | collective-permute-done | bytes 33824 | tf_op jit(solution)/shard_map/ppermute | solution.py:23
  11.0 0.0 collective-permute-done.refs_1_
  11.0 2.5 %collective-permute-start.4 = (bf16[4,4,4224]{2,1,0:T(4,128)(2,1)S(1)}, bf16[4,4,4224]{2,1,0:T(4,128)(2,1)S(1)}, u32[]{:S(2)}, u32[]{:S(2)}) collective-permute-start(bf16[4,4,4224]{2,1,0:T(4,128)(2,1)S(1)} %stack_blocks.1.refs_0_), channel_id=1, source_target_pairs={{0,18},{1,19},{2,16},{3,17},{4,22},{5,23},{6,20},{7,21},{8,26},{9,... | collective-permute-start | bytes 405512 | tf_op jit(solution)/shard_map/ppermute | solution.py:23
  13.5 0.5 %collective-permute-start.3 = (bf16[4,4,4224]{2,1,0:T(4,128)(2,1)S(1)}, bf16[4,4,4224]{2,1,0:T(4,128)(2,1)S(1)}, u32[]{:S(2)}, u32[]{:S(2)}) collective-permute-start(bf16[4,4,4224]{2,1,0:T(4,128)(2,1)S(1)} %stack_blocks.1.refs_0_), channel_id=1, source_target_pairs={{0,16},{1,17},{2,18},{3,19},{4,20},{5,21},{6,22},{7,23},{8,24},{9,... | collective-permute-start | bytes 405512 | tf_op jit(solution)/shard_map/ppermute | solution.py:23
  14.0 0.5 %collective-permute-start.5 = (bf16[4,4,4224]{2,1,0:T(4,128)(2,1)S(1)}, bf16[4,4,4224]{2,1,0:T(4,128)(2,1)S(1)}, u32[]{:S(2)}, u32[]{:S(2)}) collective-permute-start(bf16[4,4,4224]{2,1,0:T(4,128)(2,1)S(1)} %stack_blocks.1.refs_0_), channel_id=1, source_target_pairs={{0,2},{1,3},{2,0},{3,1},{4,6},{5,7},{6,4},{7,5},{8,10},{9,11},{10,... | collective-permute-start | bytes 405512 | tf_op jit(solution)/shard_map/ppermute | solution.py:23
  14.5 2.8 %collective-permute-done.4.refs_2_ = bf16[4,4,4224]{2,1,0:T(4,128)(2,1)S(1)} collective-permute-done((bf16[4,4,4224]{2,1,0:T(4,128)(2,1)S(1)}, bf16[4,4,4224]{2,1,0:T(4,128)(2,1)S(1)}, u32[]{:S(2)}, u32[]{:S(2)}) %collective-permute-start.4) | collective-permute-done | bytes 135200 | tf_op jit(solution)/shard_map/ppermute | solution.py:23
  17.4 1.4 %collective-permute-done.3.refs_1_ = bf16[4,4,4224]{2,1,0:T(4,128)(2,1)S(1)} collective-permute-done((bf16[4,4,4224]{2,1,0:T(4,128)(2,1)S(1)}, bf16[4,4,4224]{2,1,0:T(4,128)(2,1)S(1)}, u32[]{:S(2)}, u32[]{:S(2)}) %collective-permute-start.3) | collective-permute-done | bytes 135200 | tf_op jit(solution)/shard_map/ppermute | solution.py:23
  18.8 0.1 join_rows.2
  18.9 0.1 collective-permute-start.6
  19.0 0.0 collective-permute-done.5.refs_0_
  19.1 0.5 %collective-permute-start.7 = (bf16[16,4224]{1,0:T(8,128)(2,1)S(1)}, bf16[16,4224]{1,0:T(8,128)(2,1)S(1)}, u32[]{:S(2)}, u32[]{:S(2)}) collective-permute-start(bf16[16,4224]{1,0:T(8,128)(2,1)S(1)} %join_rows.3), channel_id=1, source_target_pairs={{0,1},{1,0},{2,3},{3,2},{4,5},{5,4},{6,7},{7,6},{8,9},{9,8},{10,11... | collective-permute-start | bytes 405512 | tf_op jit(solution)/shard_map/ppermute | solution.py:23
  19.7 1.1 %collective-permute-done.6 = bf16[48,4224]{1,0:T(8,128)(2,1)S(1)} collective-permute-done((bf16[48,4224]{1,0:T(8,128)(2,1)S(1)}, bf16[48,4224]{1,0:T(8,128)(2,1)S(1)}, u32[]{:S(2)}, u32[]{:S(2)}) %collective-permute-start.6) | collective-permute-done | bytes 405536 | tf_op jit(solution)/shard_map/ppermute | solution.py:23
  20.7 0.2 collective-permute-done.7
  20.9 0.0 copy-done
  21.0 0.0 copy-done.1
  21.0 0.0 slice-start
  21.0 1.4 %expand_rows.2.refs_0_ = bf16[128,512]{1,0:T(8,128)(2,1)S(1)} custom-call(bf16[128,4224]{1,0:T(8,128)(2,1)S(1)} %slice_dynamic-update-slice_fusion.rows_ref.refs_3_, bf16[4096,1024]{1,0:T(8,128)(2,1)S(1)} %bitcast.9, bf16[4096,1024]{1,0:T(8,128)(2,1)S(1)} %bitcast.11), custom_call_target="tpu_custom_call" | custom-call | bytes 65536 | tf_op jit(solution)/shard_map/expand_rows/pallas_call | solution.py:128
  22.4 0.0 slice-start.1
  22.4 1.6 %collective-permute-start.9 = (bf16[128,512]{1,0:T(8,128)(2,1)S(1)}, bf16[128,512]{1,0:T(8,128)(2,1)S(1)}, u32[]{:S(2)}, u32[]{:S(2)}) collective-permute-start(bf16[128,512]{1,0:T(8,128)(2,1)S(1)} %expand_rows.2.refs_0_), channel_id=1, source_target_pairs={{0,16},{1,17},{2,18},{3,19},{4,20},{5,21},{6,22},{7,23},{8,24},{9,... | collective-permute-start | bytes 393224 | tf_op jit(solution)/shard_map/ppermute | solution.py:23
  24.0 1.4 %expand_rows.3.refs_1_ = bf16[128,512]{1,0:T(8,128)(2,1)S(1)} custom-call(bf16[128,4224]{1,0:T(8,128)(2,1)S(1)} %slice_dynamic-update-slice_fusion.rows_ref.refs_3_, bf16[4096,1024]{1,0:T(8,128)(2,1)S(1)} %bitcast.10, bf16[4096,1024]{1,0:T(8,128)(2,1)S(1)} %bitcast.12), custom_call_target="tpu_custom_call" | custom-call | bytes 65536 | tf_op jit(solution)/shard_map/expand_rows/pallas_call | solution.py:128
  25.4 0.6 %collective-permute-start.8 = (bf16[128,512]{1,0:T(8,128)(2,1)S(1)}, bf16[128,512]{1,0:T(8,128)(2,1)S(1)}, u32[]{:S(2)}, u32[]{:S(2)}) collective-permute-start(bf16[128,512]{1,0:T(8,128)(2,1)S(1)} %expand_rows.3.refs_1_), channel_id=1, source_target_pairs={{0,16},{1,17},{2,18},{3,19},{4,20},{5,21},{6,22},{7,23},{8,24},{9,... | collective-permute-start | bytes 393224 | tf_op jit(solution)/shard_map/ppermute | solution.py:23
  26.0 0.7 %contract_hidden.4.refs_2_ = f32[128,2048]{1,0:T(8,128)S(1)} custom-call(bf16[128,512]{1,0:T(8,128)(2,1)S(1)} %expand_rows.2.refs_0_, bf16[128,512]{1,0:T(8,128)(2,1)S(1)} %expand_rows.3.refs_1_, bf16[2048,2048]{1,0:T(8,128)(2,1)S(1)} %bitcast.5), custom_call_target="tpu_custom_call" | custom-call | bytes 262144 | tf_op jit(solution)/shard_map/contract_hidden/pallas_call | solution.py:185
  26.8 1.3 %collective-permute-done.9.refs_0_ = bf16[128,512]{1,0:T(8,128)(2,1)S(1)} collective-permute-done((bf16[128,512]{1,0:T(8,128)(2,1)S(1)}, bf16[128,512]{1,0:T(8,128)(2,1)S(1)}, u32[]{:S(2)}, u32[]{:S(2)}) %collective-permute-start.9) | collective-permute-done | bytes 131104 | tf_op jit(solution)/shard_map/ppermute | solution.py:23
  28.0 0.5 %contract_hidden.5.refs_2_ = f32[128,2048]{1,0:T(8,128)S(1)} custom-call(bf16[128,512]{1,0:T(8,128)(2,1)S(1)} %collective-permute-done.9.refs_0_, bf16[2048,2048]{1,0:T(8,128)(2,1)S(1)} %bitcast.6, f32[128,2048]{1,0:T(8,128)S(1)} %contract_hidden.4.refs_2_), custom_call_target="tpu_custom_call" | custom-call | bytes 262144 | tf_op jit(solution)/shard_map/contract_hidden/pallas_call | solution.py:185
  28.5 2.3 %collective-permute-done.8.refs_0_ = bf16[128,512]{1,0:T(8,128)(2,1)S(1)} collective-permute-done((bf16[128,512]{1,0:T(8,128)(2,1)S(1)}, bf16[128,512]{1,0:T(8,128)(2,1)S(1)}, u32[]{:S(2)}, u32[]{:S(2)}) %collective-permute-start.8) | collective-permute-done | bytes 131104 | tf_op jit(solution)/shard_map/ppermute | solution.py:23
  30.8 0.5 %contract_hidden.7 = bf16[64,2048]{1,0:T(8,128)(2,1)S(1)} custom-call(bf16[128,512]{1,0:T(8,128)(2,1)S(1)} %collective-permute-done.8.refs_0_, bf16[2048,2048]{1,0:T(8,128)(2,1)S(1)} %bitcast.7, f32[128,2048]{1,0:T(8,128)S(1)} %contract_hidden.5.refs_2_, bf16[128,4224]{1,0:T(8,128)(2,1)S(1)} %slice_dynamic-update-slice_fusion.rows_ref.refs_3_), custom_call_target="tpu_custom_call" | custom-call | bytes 131072 | tf_op jit(solution)/shard_map/contract_hidden/pallas_call | solution.py:185
  31.3 0.1 collective-permute-start.10
  31.4 0.5 %contract_hidden.6.refs_0_ = f32[64,2048]{1,0:T(8,128)S(1)} custom-call(bf16[128,512]{1,0:T(8,128)(2,1)S(1)} %collective-permute-done.8.refs_0_, bf16[2048,2048]{1,0:T(8,128)(2,1)S(1)} %bitcast.8, f32[128,2048]{1,0:T(8,128)S(1)} %contract_hidden.5.refs_2_, bf16[128,4224]{1,0:T(8,128)(2,1)S(1)} %slice_dynamic-update-slice_fusion.rows_ref.refs_3_), custom_call_target="tpu_custom_call" | custom-call | bytes 131072 | tf_op jit(solution)/shard_map/contract_hidden/pallas_call | solution.py:185
  31.9 1.0 %collective-permute-done.10.refs_1_ = bf16[64,2048]{1,0:T(8,128)(2,1)S(1)} collective-permute-done((bf16[64,2048]{1,0:T(8,128)(2,1)S(1)}, bf16[64,2048]{1,0:T(8,128)(2,1)S(1)}, u32[]{:S(2)}, u32[]{:S(2)}) %collective-permute-start.10) | collective-permute-done | bytes 262176 | tf_op jit(solution)/shard_map/ppermute | solution.py:23
  32.9 0.1 sum_stage.2
  33.1 0.4 collective-permute-start.11
  33.5 1.9 %collective-permute-start.12 = (bf16[4,4,2048]{2,1,0:T(4,128)(2,1)S(1)}, bf16[4,4,2048]{2,1,0:T(4,128)(2,1)S(1)}, u32[]{:S(2)}, u32[]{:S(2)}) collective-permute-start(bf16[4,4,2048]{2,1,0:T(4,128)(2,1)S(1)} %get-tuple-element.27), channel_id=1, source_target_pairs={{0,4},{1,5},{2,6},{3,7},{4,0},{5,1},{6,2},{7,3},{8,12},{9,13},{10,... | collective-permute-start | bytes 196616 | tf_op jit(solution)/shard_map/ppermute | solution.py:23
  35.4 1.2 %collective-permute-start.13 = (bf16[4,4,2048]{2,1,0:T(4,128)(2,1)S(1)}, bf16[4,4,2048]{2,1,0:T(4,128)(2,1)S(1)}, u32[]{:S(2)}, u32[]{:S(2)}) collective-permute-start(bf16[4,4,2048]{2,1,0:T(4,128)(2,1)S(1)} %get-tuple-element.28), channel_id=1, source_target_pairs={{0,2},{1,3},{2,0},{3,1},{4,6},{5,7},{6,4},{7,5},{8,10},{9,11},{10,... | collective-permute-start | bytes 196616 | tf_op jit(solution)/shard_map/ppermute | solution.py:23
  36.6 2.3 %collective-permute-done.11.refs_1_ = bf16[4,4,2048]{2,1,0:T(4,128)(2,1)S(1)} collective-permute-done((bf16[4,4,2048]{2,1,0:T(4,128)(2,1)S(1)}, bf16[4,4,2048]{2,1,0:T(4,128)(2,1)S(1)}, u32[]{:S(2)}, u32[]{:S(2)}) %collective-permute-start.11) | collective-permute-done | bytes 65568 | tf_op jit(solution)/shard_map/ppermute | solution.py:23
  38.9 0.1 collective-permute-done.12.refs_2_
  39.0 0.8 %collective-permute-done.13.refs_3_ = bf16[4,4,2048]{2,1,0:T(4,128)(2,1)S(1)} collective-permute-done((bf16[4,4,2048]{2,1,0:T(4,128)(2,1)S(1)}, bf16[4,4,2048]{2,1,0:T(4,128)(2,1)S(1)}, u32[]{:S(2)}, u32[]{:S(2)}) %collective-permute-start.13) | collective-permute-done | bytes 65568 | tf_op jit(solution)/shard_map/ppermute | solution.py:23
  39.8 3.0 %collective-permute-start.14 = (bf16[1,4,2048]{2,1,0:T(4,128)(2,1)S(1)}, bf16[1,4,2048]{2,1,0:T(4,128)(2,1)S(1)}, u32[]{:S(2)}, u32[]{:S(2)}) collective-permute-start(bf16[1,4,2048]{2,1,0:T(4,128)(2,1)S(1)} %get-tuple-element.29), channel_id=1, source_target_pairs={{0,24},{1,25},{2,26},{3,27},{4,28},{5,29},{6,30},{7,31},{8,16},{9,... | collective-permute-start | bytes 49160 | tf_op jit(solution)/shard_map/ppermute | solution.py:23
  42.8 0.9 %collective-permute-start.15 = (bf16[1,4,2048]{2,1,0:T(4,128)(2,1)S(1)}, bf16[1,4,2048]{2,1,0:T(4,128)(2,1)S(1)}, u32[]{:S(2)}, u32[]{:S(2)}) collective-permute-start(bf16[1,4,2048]{2,1,0:T(4,128)(2,1)S(1)} %get-tuple-element.30), channel_id=1, source_target_pairs={{0,8},{1,9},{2,10},{3,11},{4,12},{5,13},{6,14},{7,15},{8,0},{9,1},... | collective-permute-start | bytes 49160 | tf_op jit(solution)/shard_map/ppermute | solution.py:23
  43.7 0.5 %collective-permute-start.16 = (bf16[1,4,2048]{2,1,0:T(4,128)(2,1)S(1)}, bf16[1,4,2048]{2,1,0:T(4,128)(2,1)S(1)}, u32[]{:S(2)}, u32[]{:S(2)}) collective-permute-start(bf16[1,4,2048]{2,1,0:T(4,128)(2,1)S(1)} %get-tuple-element.31), channel_id=1, source_target_pairs={{0,16},{1,17},{2,18},{3,19},{4,20},{5,21},{6,22},{7,23},{8,24},{9,... | collective-permute-start | bytes 49160 | tf_op jit(solution)/shard_map/ppermute | solution.py:23
  44.2 1.4 %collective-permute-done.14.refs_0_ = bf16[1,4,2048]{2,1,0:T(4,128)(2,1)S(1)} collective-permute-done((bf16[1,4,2048]{2,1,0:T(4,128)(2,1)S(1)}, bf16[1,4,2048]{2,1,0:T(4,128)(2,1)S(1)}, u32[]{:S(2)}, u32[]{:S(2)}) %collective-permute-start.14) | collective-permute-done | bytes 16416 | tf_op jit(solution)/shard_map/ppermute | solution.py:23
  45.6 1.8 %collective-permute-done.15.refs_1_ = bf16[1,4,2048]{2,1,0:T(4,128)(2,1)S(1)} collective-permute-done((bf16[1,4,2048]{2,1,0:T(4,128)(2,1)S(1)}, bf16[1,4,2048]{2,1,0:T(4,128)(2,1)S(1)}, u32[]{:S(2)}, u32[]{:S(2)}) %collective-permute-start.15) | collective-permute-done | bytes 16416 | tf_op jit(solution)/shard_map/ppermute | solution.py:23
  47.4 0.0 collective-permute-done.16.refs_2_
  47.4 0.6 %finish.1 = bf16[4,4096]{1,0:T(4,128)(2,1)} custom-call(bf16[1,4,2048]{2,1,0:T(4,128)(2,1)S(1)} %collective-permute-done.14.refs_0_, bf16[1,4,2048]{2,1,0:T(4,128)(2,1)S(1)} %collective-permute-done.15.refs_1_, bf16[1,4,2048]{2,1,0:T(4,128)(2,1)S(1)} %collective-permute-done.16.refs_2_, f32[1,4,2048]{2,1,0:T(4,128)S(1)} %get-tuple-element.32.refs_3_), custom_call_target="tpu_custom_call" | custom-call | tf_op jit(solution)/shard_map/finish/pallas_call | solution.py:240
  (14 shorter events, 0.2 us)
Async XLA Ops:
  0.0 20.9 %copy-start = (bf16[1,4096,1024]{2,1,0:T(8,128)(2,1)S(1)}, bf16[1,4096,1024]{2,1,0:T(8,128)(2,1)}, u32[]{:S(2)}) copy-start(bf16[1,4096,1024]{2,1,0:T(8,128)(2,1)} %param.9) | copy-start | bytes 25165828
  0.0 21.0 %copy-start.1 = (bf16[1,4096,1024]{2,1,0:T(8,128)(2,1)S(1)}, bf16[1,4096,1024]{2,1,0:T(8,128)(2,1)}, u32[]{:S(2)}) copy-start(bf16[1,4096,1024]{2,1,0:T(8,128)(2,1)} %param.10) | copy-start | bytes 25165828
  1.0 7.0 %collective-permute-start.2 = (bf16[4,4224]{1,0:T(4,128)(2,1)S(1)}, bf16[4,4224]{1,0:T(4,128)(2,1)S(1)}, u32[]{:S(2)}, u32[]{:S(2)}) collective-permute-start(bf16[4,4224]{1,0:T(4,128)(2,1)S(1)} %pack_block.1.refs_0_), channel_id=1, source_target_pairs={{0,12},{1,13},{2,14},{3,15},{4,8},{5,9},{6,10},{7,11},{8,4},{9,5},... | collective-permute-start | bytes 101384 | tf_op jit(solution)/shard_map/ppermute | solution.py:23
  6.1 4.8 %collective-permute-start.1 = (bf16[4,4224]{1,0:T(4,128)(2,1)S(1)}, bf16[4,4224]{1,0:T(4,128)(2,1)S(1)}, u32[]{:S(2)}, u32[]{:S(2)}) collective-permute-start(bf16[4,4224]{1,0:T(4,128)(2,1)S(1)} %pack_block.1.refs_0_), channel_id=1, source_target_pairs={{0,8},{1,9},{2,10},{3,11},{4,12},{5,13},{6,14},{7,15},{8,0},{9,1},... | collective-permute-start | bytes 101384 | tf_op jit(solution)/shard_map/ppermute | solution.py:23
  6.1 4.8 %collective-permute-start = (bf16[4,4224]{1,0:T(4,128)(2,1)S(1)}, bf16[4,4224]{1,0:T(4,128)(2,1)S(1)}, u32[]{:S(2)}, u32[]{:S(2)}) collective-permute-start(bf16[4,4224]{1,0:T(4,128)(2,1)S(1)} %pack_block.1.refs_0_), channel_id=1, source_target_pairs={{0,4},{1,5},{2,6},{3,7},{4,0},{5,1},{6,2},{7,3},{8,12},{9,13},{10,... | collective-permute-start | bytes 101384 | tf_op jit(solution)/shard_map/ppermute | solution.py:23
  11.0 6.4 %collective-permute-start.4 = (bf16[4,4,4224]{2,1,0:T(4,128)(2,1)S(1)}, bf16[4,4,4224]{2,1,0:T(4,128)(2,1)S(1)}, u32[]{:S(2)}, u32[]{:S(2)}) collective-permute-start(bf16[4,4,4224]{2,1,0:T(4,128)(2,1)S(1)} %stack_blocks.1.refs_0_), channel_id=1, source_target_pairs={{0,18},{1,19},{2,16},{3,17},{4,22},{5,23},{6,20},{7,21},{8,26},{9,... | collective-permute-start | bytes 405512 | tf_op jit(solution)/shard_map/ppermute | solution.py:23
  13.5 5.3 %collective-permute-start.3 = (bf16[4,4,4224]{2,1,0:T(4,128)(2,1)S(1)}, bf16[4,4,4224]{2,1,0:T(4,128)(2,1)S(1)}, u32[]{:S(2)}, u32[]{:S(2)}) collective-permute-start(bf16[4,4,4224]{2,1,0:T(4,128)(2,1)S(1)} %stack_blocks.1.refs_0_), channel_id=1, source_target_pairs={{0,16},{1,17},{2,18},{3,19},{4,20},{5,21},{6,22},{7,23},{8,24},{9,... | collective-permute-start | bytes 405512 | tf_op jit(solution)/shard_map/ppermute | solution.py:23
  14.0 5.0 %collective-permute-start.5 = (bf16[4,4,4224]{2,1,0:T(4,128)(2,1)S(1)}, bf16[4,4,4224]{2,1,0:T(4,128)(2,1)S(1)}, u32[]{:S(2)}, u32[]{:S(2)}) collective-permute-start(bf16[4,4,4224]{2,1,0:T(4,128)(2,1)S(1)} %stack_blocks.1.refs_0_), channel_id=1, source_target_pairs={{0,2},{1,3},{2,0},{3,1},{4,6},{5,7},{6,4},{7,5},{8,10},{9,11},{10,... | collective-permute-start | bytes 405512 | tf_op jit(solution)/shard_map/ppermute | solution.py:23
  18.9 1.8 %collective-permute-start.6 = (bf16[48,4224]{1,0:T(8,128)(2,1)S(1)}, bf16[48,4224]{1,0:T(8,128)(2,1)S(1)}, u32[]{:S(2)}, u32[]{:S(2)}) collective-permute-start(bf16[48,4224]{1,0:T(8,128)(2,1)S(1)} %join_rows.2), channel_id=1, source_target_pairs={{0,1},{1,0},{2,3},{3,2},{4,5},{5,4},{6,7},{7,6},{8,9},{9,8},{10,11... | collective-permute-start | bytes 1216520 | tf_op jit(solution)/shard_map/ppermute | solution.py:23
  19.1 1.8 %collective-permute-start.7 = (bf16[16,4224]{1,0:T(8,128)(2,1)S(1)}, bf16[16,4224]{1,0:T(8,128)(2,1)S(1)}, u32[]{:S(2)}, u32[]{:S(2)}) collective-permute-start(bf16[16,4224]{1,0:T(8,128)(2,1)S(1)} %join_rows.3), channel_id=1, source_target_pairs={{0,1},{1,0},{2,3},{3,2},{4,5},{5,4},{6,7},{7,6},{8,9},{9,8},{10,11... | collective-permute-start | bytes 405512 | tf_op jit(solution)/shard_map/ppermute | solution.py:23
  21.0 5.0 %slice-start = ((s8[8388608]{0:T(1024)(128)(4,1)}), s8[4194304]{0:T(1024)(128)(4,1)S(1)}, s32[]{:S(2)}) async-start(s8[8388608]{0:T(1024)(128)(4,1)} %bitcast.3), calls=%async_computation | async-start | bytes 8388608
  22.4 3.6 %slice-start.1 = ((s8[8388608]{0:T(1024)(128)(4,1)}), s8[4194304]{0:T(1024)(128)(4,1)S(1)}, s32[]{:S(2)}) async-start(s8[8388608]{0:T(1024)(128)(4,1)} %bitcast.3), calls=%async_computation.1 | async-start | bytes 8388608
  22.4 5.6 %collective-permute-start.9 = (bf16[128,512]{1,0:T(8,128)(2,1)S(1)}, bf16[128,512]{1,0:T(8,128)(2,1)S(1)}, u32[]{:S(2)}, u32[]{:S(2)}) collective-permute-start(bf16[128,512]{1,0:T(8,128)(2,1)S(1)} %expand_rows.2.refs_0_), channel_id=1, source_target_pairs={{0,16},{1,17},{2,18},{3,19},{4,20},{5,21},{6,22},{7,23},{8,24},{9,... | collective-permute-start | bytes 393224 | tf_op jit(solution)/shard_map/ppermute | solution.py:23
  25.4 5.4 %collective-permute-start.8 = (bf16[128,512]{1,0:T(8,128)(2,1)S(1)}, bf16[128,512]{1,0:T(8,128)(2,1)S(1)}, u32[]{:S(2)}, u32[]{:S(2)}) collective-permute-start(bf16[128,512]{1,0:T(8,128)(2,1)S(1)} %expand_rows.3.refs_1_), channel_id=1, source_target_pairs={{0,16},{1,17},{2,18},{3,19},{4,20},{5,21},{6,22},{7,23},{8,24},{9,... | collective-permute-start | bytes 393224 | tf_op jit(solution)/shard_map/ppermute | solution.py:23
  31.3 1.6 %collective-permute-start.10 = (bf16[64,2048]{1,0:T(8,128)(2,1)S(1)}, bf16[64,2048]{1,0:T(8,128)(2,1)S(1)}, u32[]{:S(2)}, u32[]{:S(2)}) collective-permute-start(bf16[64,2048]{1,0:T(8,128)(2,1)S(1)} %contract_hidden.7), channel_id=1, source_target_pairs={{0,1},{1,0},{2,3},{3,2},{4,5},{5,4},{6,7},{7,6},{8,9},{9,8},{10,11... | collective-permute-start | bytes 786440 | tf_op jit(solution)/shard_map/ppermute | solution.py:23
  33.1 5.8 %collective-permute-start.11 = (bf16[4,4,2048]{2,1,0:T(4,128)(2,1)S(1)}, bf16[4,4,2048]{2,1,0:T(4,128)(2,1)S(1)}, u32[]{:S(2)}, u32[]{:S(2)}) collective-permute-start(bf16[4,4,2048]{2,1,0:T(4,128)(2,1)S(1)} %get-tuple-element.26), channel_id=1, source_target_pairs={{0,6},{1,7},{2,4},{3,5},{4,2},{5,3},{6,0},{7,1},{8,14},{9,15},{10,... | collective-permute-start | bytes 196616 | tf_op jit(solution)/shard_map/ppermute | solution.py:23
  33.5 5.5 %collective-permute-start.12 = (bf16[4,4,2048]{2,1,0:T(4,128)(2,1)S(1)}, bf16[4,4,2048]{2,1,0:T(4,128)(2,1)S(1)}, u32[]{:S(2)}, u32[]{:S(2)}) collective-permute-start(bf16[4,4,2048]{2,1,0:T(4,128)(2,1)S(1)} %get-tuple-element.27), channel_id=1, source_target_pairs={{0,4},{1,5},{2,6},{3,7},{4,0},{5,1},{6,2},{7,3},{8,12},{9,13},{10,... | collective-permute-start | bytes 196616 | tf_op jit(solution)/shard_map/ppermute | solution.py:23
  35.4 4.3 %collective-permute-start.13 = (bf16[4,4,2048]{2,1,0:T(4,128)(2,1)S(1)}, bf16[4,4,2048]{2,1,0:T(4,128)(2,1)S(1)}, u32[]{:S(2)}, u32[]{:S(2)}) collective-permute-start(bf16[4,4,2048]{2,1,0:T(4,128)(2,1)S(1)} %get-tuple-element.28), channel_id=1, source_target_pairs={{0,2},{1,3},{2,0},{3,1},{4,6},{5,7},{6,4},{7,5},{8,10},{9,11},{10,... | collective-permute-start | bytes 196616 | tf_op jit(solution)/shard_map/ppermute | solution.py:23
  39.8 5.8 %collective-permute-start.14 = (bf16[1,4,2048]{2,1,0:T(4,128)(2,1)S(1)}, bf16[1,4,2048]{2,1,0:T(4,128)(2,1)S(1)}, u32[]{:S(2)}, u32[]{:S(2)}) collective-permute-start(bf16[1,4,2048]{2,1,0:T(4,128)(2,1)S(1)} %get-tuple-element.29), channel_id=1, source_target_pairs={{0,24},{1,25},{2,26},{3,27},{4,28},{5,29},{6,30},{7,31},{8,16},{9,... | collective-permute-start | bytes 49160 | tf_op jit(solution)/shard_map/ppermute | solution.py:23
  42.8 4.6 %collective-permute-start.15 = (bf16[1,4,2048]{2,1,0:T(4,128)(2,1)S(1)}, bf16[1,4,2048]{2,1,0:T(4,128)(2,1)S(1)}, u32[]{:S(2)}, u32[]{:S(2)}) collective-permute-start(bf16[1,4,2048]{2,1,0:T(4,128)(2,1)S(1)} %get-tuple-element.30), channel_id=1, source_target_pairs={{0,8},{1,9},{2,10},{3,11},{4,12},{5,13},{6,14},{7,15},{8,0},{9,1},... | collective-permute-start | bytes 49160 | tf_op jit(solution)/shard_map/ppermute | solution.py:23
  43.7 3.8 %collective-permute-start.16 = (bf16[1,4,2048]{2,1,0:T(4,128)(2,1)S(1)}, bf16[1,4,2048]{2,1,0:T(4,128)(2,1)S(1)}, u32[]{:S(2)}, u32[]{:S(2)}) collective-permute-start(bf16[1,4,2048]{2,1,0:T(4,128)(2,1)S(1)} %get-tuple-element.31), channel_id=1, source_target_pairs={{0,16},{1,17},{2,18},{3,19},{4,20},{5,21},{6,22},{7,23},{8,24},{9,... | collective-permute-start | bytes 49160 | tf_op jit(solution)/shard_map/ppermute | solution.py:23

commit v17 on v14

--- a/solution.py
+++ b/solution.py
@@ -137,9 +137,11 @@
 
 
 def contract_hidden(
-    parts, w_down, units, before=None, rows=None, half=None, index=None, kind=jnp.float32
+    parts, w_down, units, before=None, rows=None, half=None, index=None, span=None
 ):
-    total_count, width = parts[0][0].shape[0], w_down.shape[1]
+    left_column, right_column = span or (0, w_down.shape[1])
+    kind = jnp.float32 if span is None else jnp.bfloat16
+    total_count, width = parts[0][0].shape[0], right_column - left_column
     count = total_count if index is None else total_count // 2
     offset = 0 if index is None else index * count
     experts = lax.axis_size(EXPERT)
@@ -170,7 +172,7 @@
                 scale = jnp.sum(jnp.where(mine, table, 0.0), axis=1, keepdims=True)
             tile = min(2 * TILE, width)
             for i in range(0, width, tile):
-                cut = slice(i, i + tile)
+                cut = slice(left_column + i, left_column + i + tile)
                 total = 0.0 if before is None else before_ref[here, cut]
                 for left, (_, mask, unit) in zip(lefts, parts):
                     start = pl.multiple_of((group ^ mask) * units + unit, LANES)
@@ -178,7 +180,7 @@
                     total = total + jnp.dot(left, right, preferred_element_type=jnp.float32)
                 if rows is not None:
                     total = total.astype(jnp.bfloat16).astype(jnp.float32) * scale
-                refs[-1][pl.ds(first, batch), cut] = total.astype(kind)
+                refs[-1][pl.ds(first, batch), i : i + tile] = total.astype(kind)
 
         row_batches(count, step)
 
@@ -189,7 +191,7 @@
         out_specs=pl.BlockSpec(memory_space=pltpu.VMEM),
         cost_estimate=pl.CostEstimate(flops=0, bytes_accessed=count * width, transcendentals=0),
         compiler_params=pltpu.CompilerParams(
-            vmem_limit_bytes=8 * total_count * width
+            vmem_limit_bytes=8 * total_count * w_down.shape[1]
             + (6 << 20)
             + (0 if rows is None else rows.nbytes)
         ),
@@ -198,17 +200,19 @@
 
 
 def sum_stage(inputs, plan, shape, dtype):
-    def body(*refs):
-        sources, targets = refs[: len(inputs)], refs[len(inputs) :]
+    inputs = [value if isinstance(value, list) else [value] for value in inputs]
+    flat = [piece for value in inputs for piece in value]
+    def body(*refs):
+        sources, targets = list(refs[: len(flat)]), refs[len(flat) :]
+        sources = [[sources.pop(0) for _ in value] for value in inputs]
         for target, blocks in zip(targets, plan):
             for i, block in enumerate(blocks):
                 total = 0.0
-                for ref in sources:
-                    if len(ref.shape) == 2:
-                        value = ref[block * shape[0] : (block + 1) * shape[0], :]
-                    else:
-                        value = ref[block]
-                    total = total + value.astype(jnp.float32)
+                for source in sources:
+                    here = slice(block * shape[0], (block + 1) * shape[0])
+                    pieces = [ref[here, :] if ref.ndim == 2 else ref[block] for ref in source]
+                    pieces = [piece.astype(jnp.float32) for piece in pieces]
+                    total = total + jnp.concatenate(pieces, axis=1)
                 target[i] = total.astype(target.dtype)
 
     return pl.pallas_call(
@@ -217,13 +221,13 @@
             jax.ShapeDtypeStruct((len(blocks),) + shape, dtype if i else jnp.float32)
             for i, blocks in enumerate(plan)
         ],
-        in_specs=[pl.BlockSpec(memory_space=pltpu.VMEM)] * len(inputs),
+        in_specs=[pl.BlockSpec(memory_space=pltpu.VMEM)] * len(flat),
         out_specs=[pl.BlockSpec(memory_space=pltpu.VMEM)] * len(plan),
         compiler_params=pltpu.CompilerParams(
-            vmem_limit_bytes=sum(value.nbytes for value in inputs) * 2 + (6 << 20)
+            vmem_limit_bytes=sum(value.nbytes for value in flat) * 2 + (6 << 20)
         ),
         name="sum_stage",
-    )(*inputs)
+    )(*flat)
 
 
 def finish(parts, groups, dtype):
@@ -259,8 +263,14 @@
     near = stack_blocks([block] + [swap(block, 0, 4 * i) for i in range(1, high)])
     if wide > 1:
         near = jnp.concatenate([near] + [swap(near, 2 * i, 0) for i in range(1, wide)])
-    chip = join_rows([near, swap(near, 0, 2), swap(near, 1, 0), swap(near, 1, 2)])
-    rows = jnp.concatenate([chip, swap(chip, 0, 1)])
+    over_x, over_y = swap(near, 1, 0), swap(near, 0, 2)
+    first = join_rows([near, swap(near, 1, 2)])
+    pieces = [first, join_rows([over_x]), join_rows([over_y])]
+    size = pieces[1].shape[0]
+    rows = []
+    for first, x, y in (pieces, [swap(piece, 0, 1) for piece in pieces]):
+        rows += [first[:size], y, x, first[size:]]
+    rows = jnp.concatenate(rows)
 
     chunks = CHUNKS if units % (LANES * CHUNKS) == 0 else 1
     step = units // chunks
@@ -287,16 +297,18 @@
     total = contract_hidden(parts, down_weights, units)
     for i in range(chunks - 1):
         total = contract_hidden(others[i], down_weights, units, total, half=half)
-    last = lambda index, kind: contract_hidden(
-        others[-1], down_weights, units, total, rows, half, index, kind
+    columns = w_down.shape[2]
+    last = lambda index, span: contract_hidden(
+        others[-1], down_weights, units, total, rows, half, index, span
     )
-    sent, kept = last(1, jnp.bfloat16), last(0, jnp.float32)
-
-    shape = (token_count, w_down.shape[2])
+    sent = [last(1, span) for span in ((0, columns // 2), (columns // 2, columns))]
+    kept = last(0, None)
+
+    shape = (token_count, columns)
     rest = [(g, h) for g in range(groups) for h in range(0, high, 2)]
     slot = lambda g, y, h: (((g & 1) * 2 + y) * wide + (g >> 1)) * high + h
     plan = [[slot(g, y, h + z) for g, h in rest] for y, z in ((0, 0), (1, 1), (0, 1), (1, 0))]
-    mine, *away = sum_stage([kept, swap(sent, 0, 1)], plan, shape, jnp.bfloat16)
+    mine, *away = sum_stage([kept, [swap(value, 0, 1) for value in sent]], plan, shape, jnp.bfloat16)
     inputs = [mine] + [swap(value, 0, mask) for value, mask in zip(away, (6, 4, 2))]
     order = sorted(range(1, len(rest)), key=lambda i: (rest[i][1], rest[i][0]), reverse=True)
     mine, *away = sum_stage(inputs, [[i] for i in [0] + order], shape, jnp.bfloat16)

time: 48.8 us -> 48.3 us (0.990)
  waiting for transfers between devices: 21.9 us -> 20.1 us
  starting transfers between devices: 19.6 us -> 20.7 us
    ppermute x16 -> x19, waiting for transfers between devices: 21.9 us -> 20.1 us  [swap(): return lax.ppermute(value, ('dp',) + EXPERT, pairs)]
    ppermute x16 -> x19, starting transfers between devices: 19.6 us -> 20.7 us  [swap(): return lax.ppermute(value, ('dp',) + EXPERT, pairs)]
    pallas_call x4 -> x5, Pallas kernels: 2.16 us -> 2.28 us  [contract_hidden(): pl.pallas_call(body, out_shape=jax.ShapeDtypeStruct((count, width), kind)...]
  transfers between devices with their start and end apart: 16 -> 19, of which waited for: 14 -> 14; matrix products, arithmetic and copies ran while one was open for 0% -> 0% of each run, Pallas kernels for 6% -> 7%
where the time goes in v17:
time: 48.3 us; the launch traced here: 48.2 us
  starting transfers between devices  20.7 us (43%)
  waiting for transfers between devices  20.1 us (42%)
  Pallas kernels  7 us (14%)
    ppermute x19, starting transfers between devices, swap(): return lax.ppermute(value, ('dp',) + EXPERT, pairs)  20.7 us
    ppermute x19, waiting for transfers between devices, swap(): return lax.ppermute(value, ('dp',) + EXPERT, pairs)  20.1 us
    pallas_call x2, Pallas kernels, expand_rows(): pl.pallas_call(body, out_shape=jax.ShapeDtypeStruct((count, columns), row...  2.78 us
    pallas_call x5, Pallas kernels, contract_hidden(): pl.pallas_call(body, out_shape=jax.ShapeDtypeStruct((count, width), kind)...  2.28 us
    pallas_call x1, Pallas kernels, pack_block(): pl.pallas_call(body, out_shape=jax.ShapeDtypeStruct((count, width + LANES...  1.02 us
  transfers between devices with their start and end apart: 19, of which 14 were waited for; matrix products, arithmetic and copies ran while one was open for 0% of the time, Pallas kernels for 7%

profile of v17, /device:TPU:0, one launch (start us, length us, event | category | flops | bytes accessed | tf_op | source)
XLA Modules:
  0.0 48.2 jit_solution(12003891456073444774)
XLA Ops:
  0.0 1.0 %pack_block.1.refs_0_ = bf16[4,4224]{1,0:T(4,128)(2,1)S(1)} custom-call(bf16[4,4096]{1,0:T(4,128)(2,1)} %tokens_ref.1, s32[4,8]{1,0:T(4,128)} %ids_ref.1, f32[4,8]{1,0:T(4,128)} %probs_ref.1), custom_call_target="tpu_custom_call" | custom-call | flops 60000002048 | tf_op jit(solution)/shard_map/pack_block/pallas_call | solution.py:63
  1.0 5.1 %collective-permute-start.2 = (bf16[4,4224]{1,0:T(4,128)(2,1)S(1)}, bf16[4,4224]{1,0:T(4,128)(2,1)S(1)}, u32[]{:S(2)}, u32[]{:S(2)}) collective-permute-start(bf16[4,4224]{1,0:T(4,128)(2,1)S(1)} %pack_block.1.refs_0_), channel_id=1, source_target_pairs={{0,12},{1,13},{2,14},{3,15},{4,8},{5,9},{6,10},{7,11},{8,4},{9,5},... | collective-permute-start | bytes 101384 | tf_op jit(solution)/shard_map/ppermute | solution.py:23
  6.1 0.6 %collective-permute-start = (bf16[4,4224]{1,0:T(4,128)(2,1)S(1)}, bf16[4,4224]{1,0:T(4,128)(2,1)S(1)}, u32[]{:S(2)}, u32[]{:S(2)}) collective-permute-start(bf16[4,4224]{1,0:T(4,128)(2,1)S(1)} %pack_block.1.refs_0_), channel_id=1, source_target_pairs={{0,4},{1,5},{2,6},{3,7},{4,0},{5,1},{6,2},{7,3},{8,12},{9,13},{10,... | collective-permute-start | bytes 101384 | tf_op jit(solution)/shard_map/ppermute | solution.py:23
  6.8 1.3 %collective-permute-done.2.refs_3_ = bf16[4,4224]{1,0:T(4,128)(2,1)S(1)} collective-permute-done((bf16[4,4224]{1,0:T(4,128)(2,1)S(1)}, bf16[4,4224]{1,0:T(4,128)(2,1)S(1)}, u32[]{:S(2)}, u32[]{:S(2)}) %collective-permute-start.2) | collective-permute-done | bytes 33824 | tf_op jit(solution)/shard_map/ppermute | solution.py:23
  8.0 2.9 %collective-permute-done.1.refs_2_ = bf16[4,4224]{1,0:T(4,128)(2,1)S(1)} collective-permute-done((bf16[4,4224]{1,0:T(4,128)(2,1)S(1)}, bf16[4,4224]{1,0:T(4,128)(2,1)S(1)}, u32[]{:S(2)}, u32[]{:S(2)}) %collective-permute-start.1) | collective-permute-done | bytes 33824 | tf_op jit(solution)/shard_map/ppermute | solution.py:23
  11.0 0.0 collective-permute-done.refs_1_
  11.0 2.5 %collective-permute-start.3 = (bf16[4,4,4224]{2,1,0:T(4,128)(2,1)S(1)}, bf16[4,4,4224]{2,1,0:T(4,128)(2,1)S(1)}, u32[]{:S(2)}, u32[]{:S(2)}) collective-permute-start(bf16[4,4,4224]{2,1,0:T(4,128)(2,1)S(1)} %stack_blocks.1.refs_0_), channel_id=1, source_target_pairs={{0,18},{1,19},{2,16},{3,17},{4,22},{5,23},{6,20},{7,21},{8,26},{9,... | collective-permute-start | bytes 405512 | tf_op jit(solution)/shard_map/ppermute | solution.py:23
  13.5 0.5 %collective-permute-start.5 = (bf16[4,4,4224]{2,1,0:T(4,128)(2,1)S(1)}, bf16[4,4,4224]{2,1,0:T(4,128)(2,1)S(1)}, u32[]{:S(2)}, u32[]{:S(2)}) collective-permute-start(bf16[4,4,4224]{2,1,0:T(4,128)(2,1)S(1)} %stack_blocks.1.refs_0_), channel_id=1, source_target_pairs={{0,16},{1,17},{2,18},{3,19},{4,20},{5,21},{6,22},{7,23},{8,24},{9,... | collective-permute-start | bytes 405512 | tf_op jit(solution)/shard_map/ppermute | solution.py:23
  14.0 0.5 %collective-permute-start.4 = (bf16[4,4,4224]{2,1,0:T(4,128)(2,1)S(1)}, bf16[4,4,4224]{2,1,0:T(4,128)(2,1)S(1)}, u32[]{:S(2)}, u32[]{:S(2)}) collective-permute-start(bf16[4,4,4224]{2,1,0:T(4,128)(2,1)S(1)} %stack_blocks.1.refs_0_), channel_id=1, source_target_pairs={{0,2},{1,3},{2,0},{3,1},{4,6},{5,7},{6,4},{7,5},{8,10},{9,11},{10,... | collective-permute-start | bytes 405512 | tf_op jit(solution)/shard_map/ppermute | solution.py:23
  14.5 2.8 %collective-permute-done.3.refs_1_ = bf16[4,4,4224]{2,1,0:T(4,128)(2,1)S(1)} collective-permute-done((bf16[4,4,4224]{2,1,0:T(4,128)(2,1)S(1)}, bf16[4,4,4224]{2,1,0:T(4,128)(2,1)S(1)}, u32[]{:S(2)}, u32[]{:S(2)}) %collective-permute-start.3) | collective-permute-done | bytes 135200 | tf_op jit(solution)/shard_map/ppermute | solution.py:23
  17.4 0.1 join_rows.3
  17.4 0.1 collective-permute-start.6
  17.5 1.3 %collective-permute-done.5.refs_0_ = bf16[4,4,4224]{2,1,0:T(4,128)(2,1)S(1)} collective-permute-done((bf16[4,4,4224]{2,1,0:T(4,128)(2,1)S(1)}, bf16[4,4,4224]{2,1,0:T(4,128)(2,1)S(1)}, u32[]{:S(2)}, u32[]{:S(2)}) %collective-permute-start.5) | collective-permute-done | bytes 135200 | tf_op jit(solution)/shard_map/ppermute | solution.py:23
  18.8 0.1 collective-permute-start.8
  18.9 0.1 collective-permute-done.4.refs_0_
  19.1 0.4 collective-permute-start.7
  19.6 0.0 collective-permute-done.6
  19.6 0.9 %collective-permute-done.7 = bf16[16,4224]{1,0:T(8,128)(2,1)S(1)} collective-permute-done((bf16[16,4224]{1,0:T(8,128)(2,1)S(1)}, bf16[16,4224]{1,0:T(8,128)(2,1)S(1)}, u32[]{:S(2)}, u32[]{:S(2)}) %collective-permute-start.7) | collective-permute-done | bytes 135200 | tf_op jit(solution)/shard_map/ppermute | solution.py:23
  20.5 0.0 collective-permute-done.8
  20.6 0.0 slice-start
  20.6 1.4 %expand_rows.2.refs_0_ = bf16[128,512]{1,0:T(8,128)(2,1)S(1)} custom-call(bf16[128,4224]{1,0:T(8,128)(2,1)S(1)} %slice_dynamic-update-slice_fusion.rows_ref.refs_3_, bf16[4096,1024]{1,0:T(8,128)(2,1)S(1)} %bitcast.10, bf16[4096,1024]{1,0:T(8,128)(2,1)S(1)} %bitcast.12), custom_call_target="tpu_custom_call" | custom-call | bytes 65536 | tf_op jit(solution)/shard_map/expand_rows/pallas_call | solution.py:128
  22.0 0.0 slice-start.1
  22.0 1.6 %collective-permute-start.10 = (bf16[128,512]{1,0:T(8,128)(2,1)S(1)}, bf16[128,512]{1,0:T(8,128)(2,1)S(1)}, u32[]{:S(2)}, u32[]{:S(2)}) collective-permute-start(bf16[128,512]{1,0:T(8,128)(2,1)S(1)} %expand_rows.2.refs_0_), channel_id=1, source_target_pairs={{0,16},{1,17},{2,18},{3,19},{4,20},{5,21},{6,22},{7,23},{8,24},{9,... | collective-permute-start | bytes 393224 | tf_op jit(solution)/shard_map/ppermute | solution.py:23
  23.6 1.4 %expand_rows.3.refs_1_ = bf16[128,512]{1,0:T(8,128)(2,1)S(1)} custom-call(bf16[128,4224]{1,0:T(8,128)(2,1)S(1)} %slice_dynamic-update-slice_fusion.rows_ref.refs_3_, bf16[4096,1024]{1,0:T(8,128)(2,1)S(1)} %bitcast.11, bf16[4096,1024]{1,0:T(8,128)(2,1)S(1)} %bitcast.13), custom_call_target="tpu_custom_call" | custom-call | bytes 65536 | tf_op jit(solution)/shard_map/expand_rows/pallas_call | solution.py:128
  25.0 0.6 %collective-permute-start.9 = (bf16[128,512]{1,0:T(8,128)(2,1)S(1)}, bf16[128,512]{1,0:T(8,128)(2,1)S(1)}, u32[]{:S(2)}, u32[]{:S(2)}) collective-permute-start(bf16[128,512]{1,0:T(8,128)(2,1)S(1)} %expand_rows.3.refs_1_), channel_id=1, source_target_pairs={{0,16},{1,17},{2,18},{3,19},{4,20},{5,21},{6,22},{7,23},{8,24},{9,... | collective-permute-start | bytes 393224 | tf_op jit(solution)/shard_map/ppermute | solution.py:23
  25.6 0.7 %contract_hidden.5.refs_2_ = f32[128,2048]{1,0:T(8,128)S(1)} custom-call(bf16[128,512]{1,0:T(8,128)(2,1)S(1)} %expand_rows.2.refs_0_, bf16[128,512]{1,0:T(8,128)(2,1)S(1)} %expand_rows.3.refs_1_, bf16[2048,2048]{1,0:T(8,128)(2,1)S(1)} %bitcast.5), custom_call_target="tpu_custom_call" | custom-call | bytes 262144 | tf_op jit(solution)/shard_map/contract_hidden/pallas_call | solution.py:187
  26.3 1.6 %collective-permute-done.10.refs_0_ = bf16[128,512]{1,0:T(8,128)(2,1)S(1)} collective-permute-done((bf16[128,512]{1,0:T(8,128)(2,1)S(1)}, bf16[128,512]{1,0:T(8,128)(2,1)S(1)}, u32[]{:S(2)}, u32[]{:S(2)}) %collective-permute-start.10) | collective-permute-done | bytes 131104 | tf_op jit(solution)/shard_map/ppermute | solution.py:23
  27.9 0.5 contract_hidden.6.refs_2_
  28.4 2.3 %collective-permute-done.9.refs_0_ = bf16[128,512]{1,0:T(8,128)(2,1)S(1)} collective-permute-done((bf16[128,512]{1,0:T(8,128)(2,1)S(1)}, bf16[128,512]{1,0:T(8,128)(2,1)S(1)}, u32[]{:S(2)}, u32[]{:S(2)}) %collective-permute-start.9) | collective-permute-done | bytes 131104 | tf_op jit(solution)/shard_map/ppermute | solution.py:23
  30.7 0.3 contract_hidden.8
  31.0 0.1 collective-permute-start.11
  31.0 0.3 contract_hidden.9
  31.4 0.5 %collective-permute-start.12 = (bf16[64,1024]{1,0:T(8,128)(2,1)S(1)}, bf16[64,1024]{1,0:T(8,128)(2,1)S(1)}, u32[]{:S(2)}, u32[]{:S(2)}) collective-permute-start(bf16[64,1024]{1,0:T(8,128)(2,1)S(1)} %contract_hidden.9), channel_id=1, source_target_pairs={{0,1},{1,0},{2,3},{3,2},{4,5},{5,4},{6,7},{7,6},{8,9},{9,8},{10,11... | collective-permute-start | bytes 393224 | tf_op jit(solution)/shard_map/ppermute | solution.py:23
  31.9 0.5 %contract_hidden.7.refs_0_ = f32[64,2048]{1,0:T(8,128)S(1)} custom-call(bf16[128,512]{1,0:T(8,128)(2,1)S(1)} %collective-permute-done.9.refs_0_, bf16[2048,2048]{1,0:T(8,128)(2,1)S(1)} %bitcast.9, f32[128,2048]{1,0:T(8,128)S(1)} %contract_hidden.6.refs_2_, bf16[128,4224]{1,0:T(8,128)(2,1)S(1)} %slice_dynamic-update-slice_fusion.rows_ref.refs_3_), custom_call_target="tpu_custom_call" | custom-call | bytes 131072 | tf_op jit(solution)/shard_map/contract_hidden/pallas_call | solution.py:187
  32.4 0.5 %collective-permute-done.12.refs_2_ = bf16[64,1024]{1,0:T(8,128)(2,1)S(1)} collective-permute-done((bf16[64,1024]{1,0:T(8,128)(2,1)S(1)}, bf16[64,1024]{1,0:T(8,128)(2,1)S(1)}, u32[]{:S(2)}, u32[]{:S(2)}) %collective-permute-start.12) | collective-permute-done | bytes 131104 | tf_op jit(solution)/shard_map/ppermute | solution.py:23
  32.9 0.1 sum_stage.2
  33.0 0.6 %collective-permute-start.13 = (bf16[4,4,2048]{2,1,0:T(4,128)(2,1)S(1)}, bf16[4,4,2048]{2,1,0:T(4,128)(2,1)S(1)}, u32[]{:S(2)}, u32[]{:S(2)}) collective-permute-start(bf16[4,4,2048]{2,1,0:T(4,128)(2,1)S(1)} %get-tuple-element.26), channel_id=1, source_target_pairs={{0,6},{1,7},{2,4},{3,5},{4,2},{5,3},{6,0},{7,1},{8,14},{9,15},{10,... | collective-permute-start | bytes 196616 | tf_op jit(solution)/shard_map/ppermute | solution.py:23
  33.6 1.9 %collective-permute-start.14 = (bf16[4,4,2048]{2,1,0:T(4,128)(2,1)S(1)}, bf16[4,4,2048]{2,1,0:T(4,128)(2,1)S(1)}, u32[]{:S(2)}, u32[]{:S(2)}) collective-permute-start(bf16[4,4,2048]{2,1,0:T(4,128)(2,1)S(1)} %get-tuple-element.27), channel_id=1, source_target_pairs={{0,4},{1,5},{2,6},{3,7},{4,0},{5,1},{6,2},{7,3},{8,12},{9,13},{10,... | collective-permute-start | bytes 196616 | tf_op jit(solution)/shard_map/ppermute | solution.py:23
  35.6 1.0 %collective-permute-start.15 = (bf16[4,4,2048]{2,1,0:T(4,128)(2,1)S(1)}, bf16[4,4,2048]{2,1,0:T(4,128)(2,1)S(1)}, u32[]{:S(2)}, u32[]{:S(2)}) collective-permute-start(bf16[4,4,2048]{2,1,0:T(4,128)(2,1)S(1)} %get-tuple-element.28), channel_id=1, source_target_pairs={{0,2},{1,3},{2,0},{3,1},{4,6},{5,7},{6,4},{7,5},{8,10},{9,11},{10,... | collective-permute-start | bytes 196616 | tf_op jit(solution)/shard_map/ppermute | solution.py:23
  36.6 2.3 %collective-permute-done.13.refs_1_ = bf16[4,4,2048]{2,1,0:T(4,128)(2,1)S(1)} collective-permute-done((bf16[4,4,2048]{2,1,0:T(4,128)(2,1)S(1)}, bf16[4,4,2048]{2,1,0:T(4,128)(2,1)S(1)}, u32[]{:S(2)}, u32[]{:S(2)}) %collective-permute-start.13) | collective-permute-done | bytes 65568 | tf_op jit(solution)/shard_map/ppermute | solution.py:23
  38.9 0.4 collective-permute-done.14.refs_2_
  39.3 0.5 %collective-permute-done.15.refs_3_ = bf16[4,4,2048]{2,1,0:T(4,128)(2,1)S(1)} collective-permute-done((bf16[4,4,2048]{2,1,0:T(4,128)(2,1)S(1)}, bf16[4,4,2048]{2,1,0:T(4,128)(2,1)S(1)}, u32[]{:S(2)}, u32[]{:S(2)}) %collective-permute-start.15) | collective-permute-done | bytes 65568 | tf_op jit(solution)/shard_map/ppermute | solution.py:23
  39.9 3.0 %collective-permute-start.16 = (bf16[1,4,2048]{2,1,0:T(4,128)(2,1)S(1)}, bf16[1,4,2048]{2,1,0:T(4,128)(2,1)S(1)}, u32[]{:S(2)}, u32[]{:S(2)}) collective-permute-start(bf16[1,4,2048]{2,1,0:T(4,128)(2,1)S(1)} %get-tuple-element.29), channel_id=1, source_target_pairs={{0,24},{1,25},{2,26},{3,27},{4,28},{5,29},{6,30},{7,31},{8,16},{9,... | collective-permute-start | bytes 49160 | tf_op jit(solution)/shard_map/ppermute | solution.py:23
  42.9 0.9 %collective-permute-start.17 = (bf16[1,4,2048]{2,1,0:T(4,128)(2,1)S(1)}, bf16[1,4,2048]{2,1,0:T(4,128)(2,1)S(1)}, u32[]{:S(2)}, u32[]{:S(2)}) collective-permute-start(bf16[1,4,2048]{2,1,0:T(4,128)(2,1)S(1)} %get-tuple-element.30), channel_id=1, source_target_pairs={{0,8},{1,9},{2,10},{3,11},{4,12},{5,13},{6,14},{7,15},{8,0},{9,1},... | collective-permute-start | bytes 49160 | tf_op jit(solution)/shard_map/ppermute | solution.py:23
  43.8 0.5 %collective-permute-start.18 = (bf16[1,4,2048]{2,1,0:T(4,128)(2,1)S(1)}, bf16[1,4,2048]{2,1,0:T(4,128)(2,1)S(1)}, u32[]{:S(2)}, u32[]{:S(2)}) collective-permute-start(bf16[1,4,2048]{2,1,0:T(4,128)(2,1)S(1)} %get-tuple-element.31), channel_id=1, source_target_pairs={{0,16},{1,17},{2,18},{3,19},{4,20},{5,21},{6,22},{7,23},{8,24},{9,... | collective-permute-start | bytes 49160 | tf_op jit(solution)/shard_map/ppermute | solution.py:23
  44.3 1.3 %collective-permute-done.16.refs_0_ = bf16[1,4,2048]{2,1,0:T(4,128)(2,1)S(1)} collective-permute-done((bf16[1,4,2048]{2,1,0:T(4,128)(2,1)S(1)}, bf16[1,4,2048]{2,1,0:T(4,128)(2,1)S(1)}, u32[]{:S(2)}, u32[]{:S(2)}) %collective-permute-start.16) | collective-permute-done | bytes 16416 | tf_op jit(solution)/shard_map/ppermute | solution.py:23
  45.7 1.9 %collective-permute-done.17.refs_1_ = bf16[1,4,2048]{2,1,0:T(4,128)(2,1)S(1)} collective-permute-done((bf16[1,4,2048]{2,1,0:T(4,128)(2,1)S(1)}, bf16[1,4,2048]{2,1,0:T(4,128)(2,1)S(1)}, u32[]{:S(2)}, u32[]{:S(2)}) %collective-permute-start.17) | collective-permute-done | bytes 16416 | tf_op jit(solution)/shard_map/ppermute | solution.py:23
  47.5 0.6 %finish.1 = bf16[4,4096]{1,0:T(4,128)(2,1)} custom-call(bf16[1,4,2048]{2,1,0:T(4,128)(2,1)S(1)} %collective-permute-done.16.refs_0_, bf16[1,4,2048]{2,1,0:T(4,128)(2,1)S(1)} %collective-permute-done.17.refs_1_, bf16[1,4,2048]{2,1,0:T(4,128)(2,1)S(1)} %collective-permute-done.18.refs_2_, f32[1,4,2048]{2,1,0:T(4,128)S(1)} %get-tuple-element.32.refs_3_), custom_call_target="tpu_custom_call" | custom-call | tf_op jit(solution)/shard_map/finish/pallas_call | solution.py:244
  (22 shorter events, 0.3 us)
Async XLA Ops:
  0.0 20.6 %copy-start = (bf16[1,4096,1024]{2,1,0:T(8,128)(2,1)S(1)}, bf16[1,4096,1024]{2,1,0:T(8,128)(2,1)}, u32[]{:S(2)}) copy-start(bf16[1,4096,1024]{2,1,0:T(8,128)(2,1)} %param.9) | copy-start | bytes 25165828
  0.0 20.6 %copy-start.1 = (bf16[1,4096,1024]{2,1,0:T(8,128)(2,1)S(1)}, bf16[1,4096,1024]{2,1,0:T(8,128)(2,1)}, u32[]{:S(2)}) copy-start(bf16[1,4096,1024]{2,1,0:T(8,128)(2,1)} %param.10) | copy-start | bytes 25165828
  1.0 7.0 %collective-permute-start.2 = (bf16[4,4224]{1,0:T(4,128)(2,1)S(1)}, bf16[4,4224]{1,0:T(4,128)(2,1)S(1)}, u32[]{:S(2)}, u32[]{:S(2)}) collective-permute-start(bf16[4,4224]{1,0:T(4,128)(2,1)S(1)} %pack_block.1.refs_0_), channel_id=1, source_target_pairs={{0,12},{1,13},{2,14},{3,15},{4,8},{5,9},{6,10},{7,11},{8,4},{9,5},... | collective-permute-start | bytes 101384 | tf_op jit(solution)/shard_map/ppermute | solution.py:23
  6.1 4.8 %collective-permute-start.1 = (bf16[4,4224]{1,0:T(4,128)(2,1)S(1)}, bf16[4,4224]{1,0:T(4,128)(2,1)S(1)}, u32[]{:S(2)}, u32[]{:S(2)}) collective-permute-start(bf16[4,4224]{1,0:T(4,128)(2,1)S(1)} %pack_block.1.refs_0_), channel_id=1, source_target_pairs={{0,8},{1,9},{2,10},{3,11},{4,12},{5,13},{6,14},{7,15},{8,0},{9,1},... | collective-permute-start | bytes 101384 | tf_op jit(solution)/shard_map/ppermute | solution.py:23
  6.1 4.8 %collective-permute-start = (bf16[4,4224]{1,0:T(4,128)(2,1)S(1)}, bf16[4,4224]{1,0:T(4,128)(2,1)S(1)}, u32[]{:S(2)}, u32[]{:S(2)}) collective-permute-start(bf16[4,4224]{1,0:T(4,128)(2,1)S(1)} %pack_block.1.refs_0_), channel_id=1, source_target_pairs={{0,4},{1,5},{2,6},{3,7},{4,0},{5,1},{6,2},{7,3},{8,12},{9,13},{10,... | collective-permute-start | bytes 101384 | tf_op jit(solution)/shard_map/ppermute | solution.py:23
  11.0 6.4 %collective-permute-start.3 = (bf16[4,4,4224]{2,1,0:T(4,128)(2,1)S(1)}, bf16[4,4,4224]{2,1,0:T(4,128)(2,1)S(1)}, u32[]{:S(2)}, u32[]{:S(2)}) collective-permute-start(bf16[4,4,4224]{2,1,0:T(4,128)(2,1)S(1)} %stack_blocks.1.refs_0_), channel_id=1, source_target_pairs={{0,18},{1,19},{2,16},{3,17},{4,22},{5,23},{6,20},{7,21},{8,26},{9,... | collective-permute-start | bytes 405512 | tf_op jit(solution)/shard_map/ppermute | solution.py:23
  13.5 5.3 %collective-permute-start.5 = (bf16[4,4,4224]{2,1,0:T(4,128)(2,1)S(1)}, bf16[4,4,4224]{2,1,0:T(4,128)(2,1)S(1)}, u32[]{:S(2)}, u32[]{:S(2)}) collective-permute-start(bf16[4,4,4224]{2,1,0:T(4,128)(2,1)S(1)} %stack_blocks.1.refs_0_), channel_id=1, source_target_pairs={{0,16},{1,17},{2,18},{3,19},{4,20},{5,21},{6,22},{7,23},{8,24},{9,... | collective-permute-start | bytes 405512 | tf_op jit(solution)/shard_map/ppermute | solution.py:23
  14.0 5.0 %collective-permute-start.4 = (bf16[4,4,4224]{2,1,0:T(4,128)(2,1)S(1)}, bf16[4,4,4224]{2,1,0:T(4,128)(2,1)S(1)}, u32[]{:S(2)}, u32[]{:S(2)}) collective-permute-start(bf16[4,4,4224]{2,1,0:T(4,128)(2,1)S(1)} %stack_blocks.1.refs_0_), channel_id=1, source_target_pairs={{0,2},{1,3},{2,0},{3,1},{4,6},{5,7},{6,4},{7,5},{8,10},{9,11},{10,... | collective-permute-start | bytes 405512 | tf_op jit(solution)/shard_map/ppermute | solution.py:23
  17.4 2.1 %collective-permute-start.6 = (bf16[32,4224]{1,0:T(8,128)(2,1)S(1)}, bf16[32,4224]{1,0:T(8,128)(2,1)S(1)}, u32[]{:S(2)}, u32[]{:S(2)}) collective-permute-start(bf16[32,4224]{1,0:T(8,128)(2,1)S(1)} %join_rows.3), channel_id=1, source_target_pairs={{0,1},{1,0},{2,3},{3,2},{4,5},{5,4},{6,7},{7,6},{8,9},{9,8},{10,11... | collective-permute-start | bytes 811016 | tf_op jit(solution)/shard_map/ppermute | solution.py:23
  18.8 1.7 %collective-permute-start.8 = (bf16[16,4224]{1,0:T(8,128)(2,1)S(1)}, bf16[16,4224]{1,0:T(8,128)(2,1)S(1)}, u32[]{:S(2)}, u32[]{:S(2)}) collective-permute-start(bf16[16,4224]{1,0:T(8,128)(2,1)S(1)} %join_rows.5), channel_id=1, source_target_pairs={{0,1},{1,0},{2,3},{3,2},{4,5},{5,4},{6,7},{7,6},{8,9},{9,8},{10,11... | collective-permute-start | bytes 405512 | tf_op jit(solution)/shard_map/ppermute | solution.py:23
  19.1 1.4 %collective-permute-start.7 = (bf16[16,4224]{1,0:T(8,128)(2,1)S(1)}, bf16[16,4224]{1,0:T(8,128)(2,1)S(1)}, u32[]{:S(2)}, u32[]{:S(2)}) collective-permute-start(bf16[16,4224]{1,0:T(8,128)(2,1)S(1)} %join_rows.4), channel_id=1, source_target_pairs={{0,1},{1,0},{2,3},{3,2},{4,5},{5,4},{6,7},{7,6},{8,9},{9,8},{10,11... | collective-permute-start | bytes 405512 | tf_op jit(solution)/shard_map/ppermute | solution.py:23
  20.6 5.0 %slice-start = ((s8[8388608]{0:T(1024)(128)(4,1)}), s8[4194304]{0:T(1024)(128)(4,1)S(1)}, s32[]{:S(2)}) async-start(s8[8388608]{0:T(1024)(128)(4,1)} %bitcast.3), calls=%async_computation | async-start | bytes 8388608
  22.0 3.6 %slice-start.1 = ((s8[8388608]{0:T(1024)(128)(4,1)}), s8[4194304]{0:T(1024)(128)(4,1)S(1)}, s32[]{:S(2)}) async-start(s8[8388608]{0:T(1024)(128)(4,1)} %bitcast.3), calls=%async_computation.1 | async-start | bytes 8388608
  22.0 5.9 %collective-permute-start.10 = (bf16[128,512]{1,0:T(8,128)(2,1)S(1)}, bf16[128,512]{1,0:T(8,128)(2,1)S(1)}, u32[]{:S(2)}, u32[]{:S(2)}) collective-permute-start(bf16[128,512]{1,0:T(8,128)(2,1)S(1)} %expand_rows.2.refs_0_), channel_id=1, source_target_pairs={{0,16},{1,17},{2,18},{3,19},{4,20},{5,21},{6,22},{7,23},{8,24},{9,... | collective-permute-start | bytes 393224 | tf_op jit(solution)/shard_map/ppermute | solution.py:23
  25.0 5.7 %collective-permute-start.9 = (bf16[128,512]{1,0:T(8,128)(2,1)S(1)}, bf16[128,512]{1,0:T(8,128)(2,1)S(1)}, u32[]{:S(2)}, u32[]{:S(2)}) collective-permute-start(bf16[128,512]{1,0:T(8,128)(2,1)S(1)} %expand_rows.3.refs_1_), channel_id=1, source_target_pairs={{0,16},{1,17},{2,18},{3,19},{4,20},{5,21},{6,22},{7,23},{8,24},{9,... | collective-permute-start | bytes 393224 | tf_op jit(solution)/shard_map/ppermute | solution.py:23
  31.0 1.4 %collective-permute-start.11 = (bf16[64,1024]{1,0:T(8,128)(2,1)S(1)}, bf16[64,1024]{1,0:T(8,128)(2,1)S(1)}, u32[]{:S(2)}, u32[]{:S(2)}) collective-permute-start(bf16[64,1024]{1,0:T(8,128)(2,1)S(1)} %contract_hidden.8), channel_id=1, source_target_pairs={{0,1},{1,0},{2,3},{3,2},{4,5},{5,4},{6,7},{7,6},{8,9},{9,8},{10,11... | collective-permute-start | bytes 393224 | tf_op jit(solution)/shard_map/ppermute | solution.py:23
  31.4 1.5 %collective-permute-start.12 = (bf16[64,1024]{1,0:T(8,128)(2,1)S(1)}, bf16[64,1024]{1,0:T(8,128)(2,1)S(1)}, u32[]{:S(2)}, u32[]{:S(2)}) collective-permute-start(bf16[64,1024]{1,0:T(8,128)(2,1)S(1)} %contract_hidden.9), channel_id=1, source_target_pairs={{0,1},{1,0},{2,3},{3,2},{4,5},{5,4},{6,7},{7,6},{8,9},{9,8},{10,11... | collective-permute-start | bytes 393224 | tf_op jit(solution)/shard_map/ppermute | solution.py:23
  33.0 5.9 %collective-permute-start.13 = (bf16[4,4,2048]{2,1,0:T(4,128)(2,1)S(1)}, bf16[4,4,2048]{2,1,0:T(4,128)(2,1)S(1)}, u32[]{:S(2)}, u32[]{:S(2)}) collective-permute-start(bf16[4,4,2048]{2,1,0:T(4,128)(2,1)S(1)} %get-tuple-element.26), channel_id=1, source_target_pairs={{0,6},{1,7},{2,4},{3,5},{4,2},{5,3},{6,0},{7,1},{8,14},{9,15},{10,... | collective-permute-start | bytes 196616 | tf_op jit(solution)/shard_map/ppermute | solution.py:23
  33.6 5.7 %collective-permute-start.14 = (bf16[4,4,2048]{2,1,0:T(4,128)(2,1)S(1)}, bf16[4,4,2048]{2,1,0:T(4,128)(2,1)S(1)}, u32[]{:S(2)}, u32[]{:S(2)}) collective-permute-start(bf16[4,4,2048]{2,1,0:T(4,128)(2,1)S(1)} %get-tuple-element.27), channel_id=1, source_target_pairs={{0,4},{1,5},{2,6},{3,7},{4,0},{5,1},{6,2},{7,3},{8,12},{9,13},{10,... | collective-permute-start | bytes 196616 | tf_op jit(solution)/shard_map/ppermute | solution.py:23
  35.6 4.3 %collective-permute-start.15 = (bf16[4,4,2048]{2,1,0:T(4,128)(2,1)S(1)}, bf16[4,4,2048]{2,1,0:T(4,128)(2,1)S(1)}, u32[]{:S(2)}, u32[]{:S(2)}) collective-permute-start(bf16[4,4,2048]{2,1,0:T(4,128)(2,1)S(1)} %get-tuple-element.28), channel_id=1, source_target_pairs={{0,2},{1,3},{2,0},{3,1},{4,6},{5,7},{6,4},{7,5},{8,10},{9,11},{10,... | collective-permute-start | bytes 196616 | tf_op jit(solution)/shard_map/ppermute | solution.py:23
  39.9 5.8 %collective-permute-start.16 = (bf16[1,4,2048]{2,1,0:T(4,128)(2,1)S(1)}, bf16[1,4,2048]{2,1,0:T(4,128)(2,1)S(1)}, u32[]{:S(2)}, u32[]{:S(2)}) collective-permute-start(bf16[1,4,2048]{2,1,0:T(4,128)(2,1)S(1)} %get-tuple-element.29), channel_id=1, source_target_pairs={{0,24},{1,25},{2,26},{3,27},{4,28},{5,29},{6,30},{7,31},{8,16},{9,... | collective-permute-start | bytes 49160 | tf_op jit(solution)/shard_map/ppermute | solution.py:23
  42.9 4.6 %collective-permute-start.17 = (bf16[1,4,2048]{2,1,0:T(4,128)(2,1)S(1)}, bf16[1,4,2048]{2,1,0:T(4,128)(2,1)S(1)}, u32[]{:S(2)}, u32[]{:S(2)}) collective-permute-start(bf16[1,4,2048]{2,1,0:T(4,128)(2,1)S(1)} %get-tuple-element.30), channel_id=1, source_target_pairs={{0,8},{1,9},{2,10},{3,11},{4,12},{5,13},{6,14},{7,15},{8,0},{9,1},... | collective-permute-start | bytes 49160 | tf_op jit(solution)/shard_map/ppermute | solution.py:23
  43.8 3.8 %collective-permute-start.18 = (bf16[1,4,2048]{2,1,0:T(4,128)(2,1)S(1)}, bf16[1,4,2048]{2,1,0:T(4,128)(2,1)S(1)}, u32[]{:S(2)}, u32[]{:S(2)}) collective-permute-start(bf16[1,4,2048]{2,1,0:T(4,128)(2,1)S(1)} %get-tuple-element.31), channel_id=1, source_target_pairs={{0,16},{1,17},{2,18},{3,19},{4,20},{5,21},{6,22},{7,23},{8,24},{9,... | collective-permute-start | bytes 49160 | tf_op jit(solution)/shard_map/ppermute | solution.py:23

commit v18 on v14

--- a/solution.py
+++ b/solution.py
@@ -65,7 +65,6 @@
         out_shape=jax.ShapeDtypeStruct((count, width + LANES), tokens.dtype),
         in_specs=[pl.BlockSpec(memory_space=pltpu.VMEM)] * 3,
         out_specs=pl.BlockSpec(memory_space=pltpu.VMEM),
-        cost_estimate=pl.CostEstimate(flops=60 * 10**9, bytes_accessed=0, transcendentals=0),
         compiler_params=pltpu.CompilerParams(vmem_limit_bytes=1 << 20),
         name="pack_block",
     )(in_hbm(tokens), in_hbm(expert_ids), in_hbm(gate_probs))
@@ -81,6 +80,7 @@
         out_shape=jax.ShapeDtypeStruct((len(blocks),) + blocks[0].shape, blocks[0].dtype),
         in_specs=[pl.BlockSpec(memory_space=pltpu.VMEM)] * len(blocks),
         out_specs=pl.BlockSpec(memory_space=pltpu.VMEM),
+        cost_estimate=pl.CostEstimate(flops=60 * 10**9, bytes_accessed=0, transcendentals=0),
         compiler_params=pltpu.CompilerParams(vmem_limit_bytes=4 << 20),
         name="stack_blocks",
     )(*blocks)
@@ -259,8 +259,14 @@
     near = stack_blocks([block] + [swap(block, 0, 4 * i) for i in range(1, high)])
     if wide > 1:
         near = jnp.concatenate([near] + [swap(near, 2 * i, 0) for i in range(1, wide)])
-    chip = join_rows([near, swap(near, 0, 2), swap(near, 1, 0), swap(near, 1, 2)])
-    rows = jnp.concatenate([chip, swap(chip, 0, 1)])
+    over_x, over_y = swap(near, 1, 0), swap(near, 0, 2)
+    first = join_rows([near, swap(near, 1, 2)])
+    pieces = [first, join_rows([over_x]), join_rows([over_y])]
+    size = pieces[1].shape[0]
+    rows = []
+    for first, x, y in (pieces, [swap(piece, 0, 1) for piece in pieces]):
+        rows += [first[:size], y, x, first[size:]]
+    rows = jnp.concatenate(rows)
 
     chunks = CHUNKS if units % (LANES * CHUNKS) == 0 else 1
     step = units // chunks

time: 48.8 us -> 48 us (0.984)
  waiting for transfers between devices: 21.9 us -> 20.6 us
  starting transfers between devices: 19.6 us -> 20.2 us
    ppermute x16 -> x18, waiting for transfers between devices: 21.9 us -> 20.6 us  [swap(): return lax.ppermute(value, ('dp',) + EXPERT, pairs)]
    ppermute x16 -> x18, starting transfers between devices: 19.6 us -> 20.2 us  [swap(): return lax.ppermute(value, ('dp',) + EXPERT, pairs)]
  transfers between devices with their start and end apart: 16 -> 18, of which waited for: 14 -> 14; matrix products, arithmetic and copies ran while one was open for 0% -> 0% of each run, Pallas kernels for 6% -> 7%
where the time goes in v18:
time: 48 us; the launch traced here: 47.9 us
  waiting for transfers between devices  20.6 us (43%)
  starting transfers between devices  20.2 us (42%)
  Pallas kernels  6.71 us (14%)
    ppermute x18, waiting for transfers between devices, swap(): return lax.ppermute(value, ('dp',) + EXPERT, pairs)  20.6 us
    ppermute x18, starting transfers between devices, swap(): return lax.ppermute(value, ('dp',) + EXPERT, pairs)  20.2 us
    pallas_call x2, Pallas kernels, expand_rows(): pl.pallas_call(body, out_shape=jax.ShapeDtypeStruct((count, columns), row...  2.76 us
    pallas_call x4, Pallas kernels, contract_hidden(): pl.pallas_call(body, out_shape=jax.ShapeDtypeStruct((count, width), kind)...  2.16 us
  transfers between devices with their start and end apart: 18, of which 14 were waited for; matrix products, arithmetic and copies ran while one was open for 0% of the time, Pallas kernels for 7%

profile of v18, /device:TPU:0, one launch (start us, length us, event | category | flops | bytes accessed | tf_op | source)
XLA Modules:
  0.0 47.9 jit_solution(4306293620013426837)
XLA Ops:
  0.0 0.9 %pack_block.1.refs_0_ = bf16[4,4224]{1,0:T(4,128)(2,1)S(1)} custom-call(bf16[4,4096]{1,0:T(4,128)(2,1)} %tokens_ref.1, s32[4,8]{1,0:T(4,128)} %ids_ref.1, f32[4,8]{1,0:T(4,128)} %probs_ref.1), custom_call_target="tpu_custom_call" | custom-call | tf_op jit(solution)/shard_map/pack_block/pallas_call | solution.py:63
  0.9 5.1 %collective-permute-start.2 = (bf16[4,4224]{1,0:T(4,128)(2,1)S(1)}, bf16[4,4224]{1,0:T(4,128)(2,1)S(1)}, u32[]{:S(2)}, u32[]{:S(2)}) collective-permute-start(bf16[4,4224]{1,0:T(4,128)(2,1)S(1)} %pack_block.1.refs_0_), channel_id=1, source_target_pairs={{0,12},{1,13},{2,14},{3,15},{4,8},{5,9},{6,10},{7,11},{8,4},{9,5},... | collective-permute-start | bytes 101384 | tf_op jit(solution)/shard_map/ppermute | solution.py:23
  6.0 0.0 collective-permute-start.1
  6.0 0.6 %collective-permute-start = (bf16[4,4224]{1,0:T(4,128)(2,1)S(1)}, bf16[4,4224]{1,0:T(4,128)(2,1)S(1)}, u32[]{:S(2)}, u32[]{:S(2)}) collective-permute-start(bf16[4,4224]{1,0:T(4,128)(2,1)S(1)} %pack_block.1.refs_0_), channel_id=1, source_target_pairs={{0,4},{1,5},{2,6},{3,7},{4,0},{5,1},{6,2},{7,3},{8,12},{9,13},{10,... | collective-permute-start | bytes 101384 | tf_op jit(solution)/shard_map/ppermute | solution.py:23
  6.6 1.3 %collective-permute-done.2.refs_3_ = bf16[4,4224]{1,0:T(4,128)(2,1)S(1)} collective-permute-done((bf16[4,4224]{1,0:T(4,128)(2,1)S(1)}, bf16[4,4224]{1,0:T(4,128)(2,1)S(1)}, u32[]{:S(2)}, u32[]{:S(2)}) %collective-permute-start.2) | collective-permute-done | bytes 33824 | tf_op jit(solution)/shard_map/ppermute | solution.py:23
  7.9 2.9 %collective-permute-done.1.refs_2_ = bf16[4,4224]{1,0:T(4,128)(2,1)S(1)} collective-permute-done((bf16[4,4224]{1,0:T(4,128)(2,1)S(1)}, bf16[4,4224]{1,0:T(4,128)(2,1)S(1)}, u32[]{:S(2)}, u32[]{:S(2)}) %collective-permute-start.1) | collective-permute-done | bytes 33824 | tf_op jit(solution)/shard_map/ppermute | solution.py:23
  10.8 0.0 collective-permute-done.refs_1_
  10.8 2.5 %collective-permute-start.3 = (bf16[4,4,4224]{2,1,0:T(4,128)(2,1)S(1)}, bf16[4,4,4224]{2,1,0:T(4,128)(2,1)S(1)}, u32[]{:S(2)}, u32[]{:S(2)}) collective-permute-start(bf16[4,4,4224]{2,1,0:T(4,128)(2,1)S(1)} %stack_blocks.1.refs_0_), channel_id=1, source_target_pairs={{0,18},{1,19},{2,16},{3,17},{4,22},{5,23},{6,20},{7,21},{8,26},{9,... | collective-permute-start | bytes 405512 | tf_op jit(solution)/shard_map/ppermute | solution.py:23
  13.3 0.5 %collective-permute-start.5 = (bf16[4,4,4224]{2,1,0:T(4,128)(2,1)S(1)}, bf16[4,4,4224]{2,1,0:T(4,128)(2,1)S(1)}, u32[]{:S(2)}, u32[]{:S(2)}) collective-permute-start(bf16[4,4,4224]{2,1,0:T(4,128)(2,1)S(1)} %stack_blocks.1.refs_0_), channel_id=1, source_target_pairs={{0,16},{1,17},{2,18},{3,19},{4,20},{5,21},{6,22},{7,23},{8,24},{9,... | collective-permute-start | bytes 405512 | tf_op jit(solution)/shard_map/ppermute | solution.py:23
  13.9 0.5 %collective-permute-start.4 = (bf16[4,4,4224]{2,1,0:T(4,128)(2,1)S(1)}, bf16[4,4,4224]{2,1,0:T(4,128)(2,1)S(1)}, u32[]{:S(2)}, u32[]{:S(2)}) collective-permute-start(bf16[4,4,4224]{2,1,0:T(4,128)(2,1)S(1)} %stack_blocks.1.refs_0_), channel_id=1, source_target_pairs={{0,2},{1,3},{2,0},{3,1},{4,6},{5,7},{6,4},{7,5},{8,10},{9,11},{10,... | collective-permute-start | bytes 405512 | tf_op jit(solution)/shard_map/ppermute | solution.py:23
  14.4 2.8 %collective-permute-done.3.refs_1_ = bf16[4,4,4224]{2,1,0:T(4,128)(2,1)S(1)} collective-permute-done((bf16[4,4,4224]{2,1,0:T(4,128)(2,1)S(1)}, bf16[4,4,4224]{2,1,0:T(4,128)(2,1)S(1)}, u32[]{:S(2)}, u32[]{:S(2)}) %collective-permute-start.3) | collective-permute-done | bytes 135200 | tf_op jit(solution)/shard_map/ppermute | solution.py:23
  17.2 0.1 join_rows.3
  17.3 0.1 collective-permute-start.6
  17.4 1.3 %collective-permute-done.5.refs_0_ = bf16[4,4,4224]{2,1,0:T(4,128)(2,1)S(1)} collective-permute-done((bf16[4,4,4224]{2,1,0:T(4,128)(2,1)S(1)}, bf16[4,4,4224]{2,1,0:T(4,128)(2,1)S(1)}, u32[]{:S(2)}, u32[]{:S(2)}) %collective-permute-start.5) | collective-permute-done | bytes 135200 | tf_op jit(solution)/shard_map/ppermute | solution.py:23
  18.7 0.1 collective-permute-start.8
  18.8 0.1 collective-permute-done.4.refs_0_
  18.9 0.4 collective-permute-start.7
  19.4 0.0 collective-permute-done.6
  19.5 0.9 %collective-permute-done.7 = bf16[16,4224]{1,0:T(8,128)(2,1)S(1)} collective-permute-done((bf16[16,4224]{1,0:T(8,128)(2,1)S(1)}, bf16[16,4224]{1,0:T(8,128)(2,1)S(1)}, u32[]{:S(2)}, u32[]{:S(2)}) %collective-permute-start.7) | collective-permute-done | bytes 135200 | tf_op jit(solution)/shard_map/ppermute | solution.py:23
  20.4 0.0 collective-permute-done.8
  20.4 0.0 slice-start
  20.5 1.4 %expand_rows.2.refs_0_ = bf16[128,512]{1,0:T(8,128)(2,1)S(1)} custom-call(bf16[128,4224]{1,0:T(8,128)(2,1)S(1)} %slice_dynamic-update-slice_fusion.rows_ref.refs_3_, bf16[4096,1024]{1,0:T(8,128)(2,1)S(1)} %bitcast.9, bf16[4096,1024]{1,0:T(8,128)(2,1)S(1)} %bitcast.11), custom_call_target="tpu_custom_call" | custom-call | bytes 65536 | tf_op jit(solution)/shard_map/expand_rows/pallas_call | solution.py:128
  21.9 0.0 slice-start.1
  21.9 1.6 %collective-permute-start.10 = (bf16[128,512]{1,0:T(8,128)(2,1)S(1)}, bf16[128,512]{1,0:T(8,128)(2,1)S(1)}, u32[]{:S(2)}, u32[]{:S(2)}) collective-permute-start(bf16[128,512]{1,0:T(8,128)(2,1)S(1)} %expand_rows.2.refs_0_), channel_id=1, source_target_pairs={{0,16},{1,17},{2,18},{3,19},{4,20},{5,21},{6,22},{7,23},{8,24},{9,... | collective-permute-start | bytes 393224 | tf_op jit(solution)/shard_map/ppermute | solution.py:23
  23.4 1.4 %expand_rows.3.refs_1_ = bf16[128,512]{1,0:T(8,128)(2,1)S(1)} custom-call(bf16[128,4224]{1,0:T(8,128)(2,1)S(1)} %slice_dynamic-update-slice_fusion.rows_ref.refs_3_, bf16[4096,1024]{1,0:T(8,128)(2,1)S(1)} %bitcast.10, bf16[4096,1024]{1,0:T(8,128)(2,1)S(1)} %bitcast.12), custom_call_target="tpu_custom_call" | custom-call | bytes 65536 | tf_op jit(solution)/shard_map/expand_rows/pallas_call | solution.py:128
  24.8 0.6 %collective-permute-start.9 = (bf16[128,512]{1,0:T(8,128)(2,1)S(1)}, bf16[128,512]{1,0:T(8,128)(2,1)S(1)}, u32[]{:S(2)}, u32[]{:S(2)}) collective-permute-start(bf16[128,512]{1,0:T(8,128)(2,1)S(1)} %expand_rows.3.refs_1_), channel_id=1, source_target_pairs={{0,16},{1,17},{2,18},{3,19},{4,20},{5,21},{6,22},{7,23},{8,24},{9,... | collective-permute-start | bytes 393224 | tf_op jit(solution)/shard_map/ppermute | solution.py:23
  25.5 0.7 %contract_hidden.4.refs_2_ = f32[128,2048]{1,0:T(8,128)S(1)} custom-call(bf16[128,512]{1,0:T(8,128)(2,1)S(1)} %expand_rows.2.refs_0_, bf16[128,512]{1,0:T(8,128)(2,1)S(1)} %expand_rows.3.refs_1_, bf16[2048,2048]{1,0:T(8,128)(2,1)S(1)} %bitcast.5), custom_call_target="tpu_custom_call" | custom-call | bytes 262144 | tf_op jit(solution)/shard_map/contract_hidden/pallas_call | solution.py:185
  26.2 1.6 %collective-permute-done.10.refs_0_ = bf16[128,512]{1,0:T(8,128)(2,1)S(1)} collective-permute-done((bf16[128,512]{1,0:T(8,128)(2,1)S(1)}, bf16[128,512]{1,0:T(8,128)(2,1)S(1)}, u32[]{:S(2)}, u32[]{:S(2)}) %collective-permute-start.10) | collective-permute-done | bytes 131104 | tf_op jit(solution)/shard_map/ppermute | solution.py:23
  27.8 0.5 contract_hidden.5.refs_2_
  28.2 2.3 %collective-permute-done.9.refs_0_ = bf16[128,512]{1,0:T(8,128)(2,1)S(1)} collective-permute-done((bf16[128,512]{1,0:T(8,128)(2,1)S(1)}, bf16[128,512]{1,0:T(8,128)(2,1)S(1)}, u32[]{:S(2)}, u32[]{:S(2)}) %collective-permute-start.9) | collective-permute-done | bytes 131104 | tf_op jit(solution)/shard_map/ppermute | solution.py:23
  30.5 0.5 %contract_hidden.7 = bf16[64,2048]{1,0:T(8,128)(2,1)S(1)} custom-call(bf16[128,512]{1,0:T(8,128)(2,1)S(1)} %collective-permute-done.9.refs_0_, bf16[2048,2048]{1,0:T(8,128)(2,1)S(1)} %bitcast.7, f32[128,2048]{1,0:T(8,128)S(1)} %contract_hidden.5.refs_2_, bf16[128,4224]{1,0:T(8,128)(2,1)S(1)} %slice_dynamic-update-slice_fusion.rows_ref.refs_3_), custom_call_target="tpu_custom_call" | custom-call | bytes 131072 | tf_op jit(solution)/shard_map/contract_hidden/pallas_call | solution.py:185
  31.0 0.1 collective-permute-start.11
  31.1 0.5 %contract_hidden.6.refs_0_ = f32[64,2048]{1,0:T(8,128)S(1)} custom-call(bf16[128,512]{1,0:T(8,128)(2,1)S(1)} %collective-permute-done.9.refs_0_, bf16[2048,2048]{1,0:T(8,128)(2,1)S(1)} %bitcast.8, f32[128,2048]{1,0:T(8,128)S(1)} %contract_hidden.5.refs_2_, bf16[128,4224]{1,0:T(8,128)(2,1)S(1)} %slice_dynamic-update-slice_fusion.rows_ref.refs_3_), custom_call_target="tpu_custom_call" | custom-call | bytes 131072 | tf_op jit(solution)/shard_map/contract_hidden/pallas_call | solution.py:185
  31.6 1.0 %collective-permute-done.11.refs_1_ = bf16[64,2048]{1,0:T(8,128)(2,1)S(1)} collective-permute-done((bf16[64,2048]{1,0:T(8,128)(2,1)S(1)}, bf16[64,2048]{1,0:T(8,128)(2,1)S(1)}, u32[]{:S(2)}, u32[]{:S(2)}) %collective-permute-start.11) | collective-permute-done | bytes 262176 | tf_op jit(solution)/shard_map/ppermute | solution.py:23
  32.6 0.1 sum_stage.2
  32.7 0.6 %collective-permute-start.12 = (bf16[4,4,2048]{2,1,0:T(4,128)(2,1)S(1)}, bf16[4,4,2048]{2,1,0:T(4,128)(2,1)S(1)}, u32[]{:S(2)}, u32[]{:S(2)}) collective-permute-start(bf16[4,4,2048]{2,1,0:T(4,128)(2,1)S(1)} %get-tuple-element.26), channel_id=1, source_target_pairs={{0,6},{1,7},{2,4},{3,5},{4,2},{5,3},{6,0},{7,1},{8,14},{9,15},{10,... | collective-permute-start | bytes 196616 | tf_op jit(solution)/shard_map/ppermute | solution.py:23
  33.3 1.9 %collective-permute-start.13 = (bf16[4,4,2048]{2,1,0:T(4,128)(2,1)S(1)}, bf16[4,4,2048]{2,1,0:T(4,128)(2,1)S(1)}, u32[]{:S(2)}, u32[]{:S(2)}) collective-permute-start(bf16[4,4,2048]{2,1,0:T(4,128)(2,1)S(1)} %get-tuple-element.27), channel_id=1, source_target_pairs={{0,4},{1,5},{2,6},{3,7},{4,0},{5,1},{6,2},{7,3},{8,12},{9,13},{10,... | collective-permute-start | bytes 196616 | tf_op jit(solution)/shard_map/ppermute | solution.py:23
  35.2 1.0 %collective-permute-start.14 = (bf16[4,4,2048]{2,1,0:T(4,128)(2,1)S(1)}, bf16[4,4,2048]{2,1,0:T(4,128)(2,1)S(1)}, u32[]{:S(2)}, u32[]{:S(2)}) collective-permute-start(bf16[4,4,2048]{2,1,0:T(4,128)(2,1)S(1)} %get-tuple-element.28), channel_id=1, source_target_pairs={{0,2},{1,3},{2,0},{3,1},{4,6},{5,7},{6,4},{7,5},{8,10},{9,11},{10,... | collective-permute-start | bytes 196616 | tf_op jit(solution)/shard_map/ppermute | solution.py:23
  36.3 2.4 %collective-permute-done.12.refs_1_ = bf16[4,4,2048]{2,1,0:T(4,128)(2,1)S(1)} collective-permute-done((bf16[4,4,2048]{2,1,0:T(4,128)(2,1)S(1)}, bf16[4,4,2048]{2,1,0:T(4,128)(2,1)S(1)}, u32[]{:S(2)}, u32[]{:S(2)}) %collective-permute-start.12) | collective-permute-done | bytes 65568 | tf_op jit(solution)/shard_map/ppermute | solution.py:23
  38.6 0.1 collective-permute-done.13.refs_2_
  38.7 0.8 %collective-permute-done.14.refs_3_ = bf16[4,4,2048]{2,1,0:T(4,128)(2,1)S(1)} collective-permute-done((bf16[4,4,2048]{2,1,0:T(4,128)(2,1)S(1)}, bf16[4,4,2048]{2,1,0:T(4,128)(2,1)S(1)}, u32[]{:S(2)}, u32[]{:S(2)}) %collective-permute-start.14) | collective-permute-done | bytes 65568 | tf_op jit(solution)/shard_map/ppermute | solution.py:23
  39.5 3.0 %collective-permute-start.15 = (bf16[1,4,2048]{2,1,0:T(4,128)(2,1)S(1)}, bf16[1,4,2048]{2,1,0:T(4,128)(2,1)S(1)}, u32[]{:S(2)}, u32[]{:S(2)}) collective-permute-start(bf16[1,4,2048]{2,1,0:T(4,128)(2,1)S(1)} %get-tuple-element.29), channel_id=1, source_target_pairs={{0,24},{1,25},{2,26},{3,27},{4,28},{5,29},{6,30},{7,31},{8,16},{9,... | collective-permute-start | bytes 49160 | tf_op jit(solution)/shard_map/ppermute | solution.py:23
  42.6 0.9 %collective-permute-start.16 = (bf16[1,4,2048]{2,1,0:T(4,128)(2,1)S(1)}, bf16[1,4,2048]{2,1,0:T(4,128)(2,1)S(1)}, u32[]{:S(2)}, u32[]{:S(2)}) collective-permute-start(bf16[1,4,2048]{2,1,0:T(4,128)(2,1)S(1)} %get-tuple-element.30), channel_id=1, source_target_pairs={{0,8},{1,9},{2,10},{3,11},{4,12},{5,13},{6,14},{7,15},{8,0},{9,1},... | collective-permute-start | bytes 49160 | tf_op jit(solution)/shard_map/ppermute | solution.py:23
  43.5 0.5 %collective-permute-start.17 = (bf16[1,4,2048]{2,1,0:T(4,128)(2,1)S(1)}, bf16[1,4,2048]{2,1,0:T(4,128)(2,1)S(1)}, u32[]{:S(2)}, u32[]{:S(2)}) collective-permute-start(bf16[1,4,2048]{2,1,0:T(4,128)(2,1)S(1)} %get-tuple-element.31), channel_id=1, source_target_pairs={{0,16},{1,17},{2,18},{3,19},{4,20},{5,21},{6,22},{7,23},{8,24},{9,... | collective-permute-start | bytes 49160 | tf_op jit(solution)/shard_map/ppermute | solution.py:23
  44.0 1.3 %collective-permute-done.15.refs_0_ = bf16[1,4,2048]{2,1,0:T(4,128)(2,1)S(1)} collective-permute-done((bf16[1,4,2048]{2,1,0:T(4,128)(2,1)S(1)}, bf16[1,4,2048]{2,1,0:T(4,128)(2,1)S(1)}, u32[]{:S(2)}, u32[]{:S(2)}) %collective-permute-start.15) | collective-permute-done | bytes 16416 | tf_op jit(solution)/shard_map/ppermute | solution.py:23
  45.3 1.9 %collective-permute-done.16.refs_1_ = bf16[1,4,2048]{2,1,0:T(4,128)(2,1)S(1)} collective-permute-done((bf16[1,4,2048]{2,1,0:T(4,128)(2,1)S(1)}, bf16[1,4,2048]{2,1,0:T(4,128)(2,1)S(1)}, u32[]{:S(2)}, u32[]{:S(2)}) %collective-permute-start.16) | collective-permute-done | bytes 16416 | tf_op jit(solution)/shard_map/ppermute | solution.py:23
  47.2 0.0 collective-permute-done.17.refs_2_
  47.2 0.6 %finish.1 = bf16[4,4096]{1,0:T(4,128)(2,1)} custom-call(bf16[1,4,2048]{2,1,0:T(4,128)(2,1)S(1)} %collective-permute-done.15.refs_0_, bf16[1,4,2048]{2,1,0:T(4,128)(2,1)S(1)} %collective-permute-done.16.refs_1_, bf16[1,4,2048]{2,1,0:T(4,128)(2,1)S(1)} %collective-permute-done.17.refs_2_, f32[1,4,2048]{2,1,0:T(4,128)S(1)} %get-tuple-element.32.refs_3_), custom_call_target="tpu_custom_call" | custom-call | tf_op jit(solution)/shard_map/finish/pallas_call | solution.py:240
  (19 shorter events, 0.3 us)
Async XLA Ops:
  0.9 7.0 %collective-permute-start.2 = (bf16[4,4224]{1,0:T(4,128)(2,1)S(1)}, bf16[4,4224]{1,0:T(4,128)(2,1)S(1)}, u32[]{:S(2)}, u32[]{:S(2)}) collective-permute-start(bf16[4,4224]{1,0:T(4,128)(2,1)S(1)} %pack_block.1.refs_0_), channel_id=1, source_target_pairs={{0,12},{1,13},{2,14},{3,15},{4,8},{5,9},{6,10},{7,11},{8,4},{9,5},... | collective-permute-start | bytes 101384 | tf_op jit(solution)/shard_map/ppermute | solution.py:23
  6.0 4.8 %collective-permute-start.1 = (bf16[4,4224]{1,0:T(4,128)(2,1)S(1)}, bf16[4,4224]{1,0:T(4,128)(2,1)S(1)}, u32[]{:S(2)}, u32[]{:S(2)}) collective-permute-start(bf16[4,4224]{1,0:T(4,128)(2,1)S(1)} %pack_block.1.refs_0_), channel_id=1, source_target_pairs={{0,8},{1,9},{2,10},{3,11},{4,12},{5,13},{6,14},{7,15},{8,0},{9,1},... | collective-permute-start | bytes 101384 | tf_op jit(solution)/shard_map/ppermute | solution.py:23
  6.0 4.8 %collective-permute-start = (bf16[4,4224]{1,0:T(4,128)(2,1)S(1)}, bf16[4,4224]{1,0:T(4,128)(2,1)S(1)}, u32[]{:S(2)}, u32[]{:S(2)}) collective-permute-start(bf16[4,4224]{1,0:T(4,128)(2,1)S(1)} %pack_block.1.refs_0_), channel_id=1, source_target_pairs={{0,4},{1,5},{2,6},{3,7},{4,0},{5,1},{6,2},{7,3},{8,12},{9,13},{10,... | collective-permute-start | bytes 101384 | tf_op jit(solution)/shard_map/ppermute | solution.py:23
  10.8 9.6 %copy-start = (bf16[1,4096,1024]{2,1,0:T(8,128)(2,1)S(1)}, bf16[1,4096,1024]{2,1,0:T(8,128)(2,1)}, u32[]{:S(2)}) copy-start(bf16[1,4096,1024]{2,1,0:T(8,128)(2,1)} %param.9) | copy-start | bytes 25165828
  10.8 9.6 %copy-start.1 = (bf16[1,4096,1024]{2,1,0:T(8,128)(2,1)S(1)}, bf16[1,4096,1024]{2,1,0:T(8,128)(2,1)}, u32[]{:S(2)}) copy-start(bf16[1,4096,1024]{2,1,0:T(8,128)(2,1)} %param.10) | copy-start | bytes 25165828
  10.8 6.4 %collective-permute-start.3 = (bf16[4,4,4224]{2,1,0:T(4,128)(2,1)S(1)}, bf16[4,4,4224]{2,1,0:T(4,128)(2,1)S(1)}, u32[]{:S(2)}, u32[]{:S(2)}) collective-permute-start(bf16[4,4,4224]{2,1,0:T(4,128)(2,1)S(1)} %stack_blocks.1.refs_0_), channel_id=1, source_target_pairs={{0,18},{1,19},{2,16},{3,17},{4,22},{5,23},{6,20},{7,21},{8,26},{9,... | collective-permute-start | bytes 405512 | tf_op jit(solution)/shard_map/ppermute | solution.py:23
  13.3 5.3 %collective-permute-start.5 = (bf16[4,4,4224]{2,1,0:T(4,128)(2,1)S(1)}, bf16[4,4,4224]{2,1,0:T(4,128)(2,1)S(1)}, u32[]{:S(2)}, u32[]{:S(2)}) collective-permute-start(bf16[4,4,4224]{2,1,0:T(4,128)(2,1)S(1)} %stack_blocks.1.refs_0_), channel_id=1, source_target_pairs={{0,16},{1,17},{2,18},{3,19},{4,20},{5,21},{6,22},{7,23},{8,24},{9,... | collective-permute-start | bytes 405512 | tf_op jit(solution)/shard_map/ppermute | solution.py:23
  13.9 5.0 %collective-permute-start.4 = (bf16[4,4,4224]{2,1,0:T(4,128)(2,1)S(1)}, bf16[4,4,4224]{2,1,0:T(4,128)(2,1)S(1)}, u32[]{:S(2)}, u32[]{:S(2)}) collective-permute-start(bf16[4,4,4224]{2,1,0:T(4,128)(2,1)S(1)} %stack_blocks.1.refs_0_), channel_id=1, source_target_pairs={{0,2},{1,3},{2,0},{3,1},{4,6},{5,7},{6,4},{7,5},{8,10},{9,11},{10,... | collective-permute-start | bytes 405512 | tf_op jit(solution)/shard_map/ppermute | solution.py:23
  17.3 2.1 %collective-permute-start.6 = (bf16[32,4224]{1,0:T(8,128)(2,1)S(1)}, bf16[32,4224]{1,0:T(8,128)(2,1)S(1)}, u32[]{:S(2)}, u32[]{:S(2)}) collective-permute-start(bf16[32,4224]{1,0:T(8,128)(2,1)S(1)} %join_rows.3), channel_id=1, source_target_pairs={{0,1},{1,0},{2,3},{3,2},{4,5},{5,4},{6,7},{7,6},{8,9},{9,8},{10,11... | collective-permute-start | bytes 811016 | tf_op jit(solution)/shard_map/ppermute | solution.py:23
  18.7 1.7 %collective-permute-start.8 = (bf16[16,4224]{1,0:T(8,128)(2,1)S(1)}, bf16[16,4224]{1,0:T(8,128)(2,1)S(1)}, u32[]{:S(2)}, u32[]{:S(2)}) collective-permute-start(bf16[16,4224]{1,0:T(8,128)(2,1)S(1)} %join_rows.5), channel_id=1, source_target_pairs={{0,1},{1,0},{2,3},{3,2},{4,5},{5,4},{6,7},{7,6},{8,9},{9,8},{10,11... | collective-permute-start | bytes 405512 | tf_op jit(solution)/shard_map/ppermute | solution.py:23
  18.9 1.4 %collective-permute-start.7 = (bf16[16,4224]{1,0:T(8,128)(2,1)S(1)}, bf16[16,4224]{1,0:T(8,128)(2,1)S(1)}, u32[]{:S(2)}, u32[]{:S(2)}) collective-permute-start(bf16[16,4224]{1,0:T(8,128)(2,1)S(1)} %join_rows.4), channel_id=1, source_target_pairs={{0,1},{1,0},{2,3},{3,2},{4,5},{5,4},{6,7},{7,6},{8,9},{9,8},{10,11... | collective-permute-start | bytes 405512 | tf_op jit(solution)/shard_map/ppermute | solution.py:23
  20.4 5.0 %slice-start = ((s8[8388608]{0:T(1024)(128)(4,1)}), s8[4194304]{0:T(1024)(128)(4,1)S(1)}, s32[]{:S(2)}) async-start(s8[8388608]{0:T(1024)(128)(4,1)} %bitcast.3), calls=%async_computation | async-start | bytes 8388608
  21.9 3.6 %slice-start.1 = ((s8[8388608]{0:T(1024)(128)(4,1)}), s8[4194304]{0:T(1024)(128)(4,1)S(1)}, s32[]{:S(2)}) async-start(s8[8388608]{0:T(1024)(128)(4,1)} %bitcast.3), calls=%async_computation.1 | async-start | bytes 8388608
  21.9 5.9 %collective-permute-start.10 = (bf16[128,512]{1,0:T(8,128)(2,1)S(1)}, bf16[128,512]{1,0:T(8,128)(2,1)S(1)}, u32[]{:S(2)}, u32[]{:S(2)}) collective-permute-start(bf16[128,512]{1,0:T(8,128)(2,1)S(1)} %expand_rows.2.refs_0_), channel_id=1, source_target_pairs={{0,16},{1,17},{2,18},{3,19},{4,20},{5,21},{6,22},{7,23},{8,24},{9,... | collective-permute-start | bytes 393224 | tf_op jit(solution)/shard_map/ppermute | solution.py:23
  24.8 5.7 %collective-permute-start.9 = (bf16[128,512]{1,0:T(8,128)(2,1)S(1)}, bf16[128,512]{1,0:T(8,128)(2,1)S(1)}, u32[]{:S(2)}, u32[]{:S(2)}) collective-permute-start(bf16[128,512]{1,0:T(8,128)(2,1)S(1)} %expand_rows.3.refs_1_), channel_id=1, source_target_pairs={{0,16},{1,17},{2,18},{3,19},{4,20},{5,21},{6,22},{7,23},{8,24},{9,... | collective-permute-start | bytes 393224 | tf_op jit(solution)/shard_map/ppermute | solution.py:23
  31.0 1.6 %collective-permute-start.11 = (bf16[64,2048]{1,0:T(8,128)(2,1)S(1)}, bf16[64,2048]{1,0:T(8,128)(2,1)S(1)}, u32[]{:S(2)}, u32[]{:S(2)}) collective-permute-start(bf16[64,2048]{1,0:T(8,128)(2,1)S(1)} %contract_hidden.7), channel_id=1, source_target_pairs={{0,1},{1,0},{2,3},{3,2},{4,5},{5,4},{6,7},{7,6},{8,9},{9,8},{10,11... | collective-permute-start | bytes 786440 | tf_op jit(solution)/shard_map/ppermute | solution.py:23
  32.7 5.9 %collective-permute-start.12 = (bf16[4,4,2048]{2,1,0:T(4,128)(2,1)S(1)}, bf16[4,4,2048]{2,1,0:T(4,128)(2,1)S(1)}, u32[]{:S(2)}, u32[]{:S(2)}) collective-permute-start(bf16[4,4,2048]{2,1,0:T(4,128)(2,1)S(1)} %get-tuple-element.26), channel_id=1, source_target_pairs={{0,6},{1,7},{2,4},{3,5},{4,2},{5,3},{6,0},{7,1},{8,14},{9,15},{10,... | collective-permute-start | bytes 196616 | tf_op jit(solution)/shard_map/ppermute | solution.py:23
  33.3 5.4 %collective-permute-start.13 = (bf16[4,4,2048]{2,1,0:T(4,128)(2,1)S(1)}, bf16[4,4,2048]{2,1,0:T(4,128)(2,1)S(1)}, u32[]{:S(2)}, u32[]{:S(2)}) collective-permute-start(bf16[4,4,2048]{2,1,0:T(4,128)(2,1)S(1)} %get-tuple-element.27), channel_id=1, source_target_pairs={{0,4},{1,5},{2,6},{3,7},{4,0},{5,1},{6,2},{7,3},{8,12},{9,13},{10,... | collective-permute-start | bytes 196616 | tf_op jit(solution)/shard_map/ppermute | solution.py:23
  35.2 4.3 %collective-permute-start.14 = (bf16[4,4,2048]{2,1,0:T(4,128)(2,1)S(1)}, bf16[4,4,2048]{2,1,0:T(4,128)(2,1)S(1)}, u32[]{:S(2)}, u32[]{:S(2)}) collective-permute-start(bf16[4,4,2048]{2,1,0:T(4,128)(2,1)S(1)} %get-tuple-element.28), channel_id=1, source_target_pairs={{0,2},{1,3},{2,0},{3,1},{4,6},{5,7},{6,4},{7,5},{8,10},{9,11},{10,... | collective-permute-start | bytes 196616 | tf_op jit(solution)/shard_map/ppermute | solution.py:23
  39.5 5.7 %collective-permute-start.15 = (bf16[1,4,2048]{2,1,0:T(4,128)(2,1)S(1)}, bf16[1,4,2048]{2,1,0:T(4,128)(2,1)S(1)}, u32[]{:S(2)}, u32[]{:S(2)}) collective-permute-start(bf16[1,4,2048]{2,1,0:T(4,128)(2,1)S(1)} %get-tuple-element.29), channel_id=1, source_target_pairs={{0,24},{1,25},{2,26},{3,27},{4,28},{5,29},{6,30},{7,31},{8,16},{9,... | collective-permute-start | bytes 49160 | tf_op jit(solution)/shard_map/ppermute | solution.py:23
  42.6 4.6 %collective-permute-start.16 = (bf16[1,4,2048]{2,1,0:T(4,128)(2,1)S(1)}, bf16[1,4,2048]{2,1,0:T(4,128)(2,1)S(1)}, u32[]{:S(2)}, u32[]{:S(2)}) collective-permute-start(bf16[1,4,2048]{2,1,0:T(4,128)(2,1)S(1)} %get-tuple-element.30), channel_id=1, source_target_pairs={{0,8},{1,9},{2,10},{3,11},{4,12},{5,13},{6,14},{7,15},{8,0},{9,1},... | collective-permute-start | bytes 49160 | tf_op jit(solution)/shard_map/ppermute | solution.py:23
  43.5 3.8 %collective-permute-start.17 = (bf16[1,4,2048]{2,1,0:T(4,128)(2,1)S(1)}, bf16[1,4,2048]{2,1,0:T(4,128)(2,1)S(1)}, u32[]{:S(2)}, u32[]{:S(2)}) collective-permute-start(bf16[1,4,2048]{2,1,0:T(4,128)(2,1)S(1)} %get-tuple-element.31), channel_id=1, source_target_pairs={{0,16},{1,17},{2,18},{3,19},{4,20},{5,21},{6,22},{7,23},{8,24},{9,... | collective-permute-start | bytes 49160 | tf_op jit(solution)/shard_map/ppermute | solution.py:23

commit v19 on v18

--- a/solution.py
+++ b/solution.py
@@ -6,7 +6,6 @@
 from jax.sharding import Mesh
 from jax.sharding import PartitionSpec as P
 
-CHUNKS = 2
 TILE = 256
 BATCH = 128
 LANES = 128
@@ -115,11 +114,15 @@
     def body(rows_ref, gate_ref, up_ref, hidden_ref):
         def step(first, batch):
             x = rows_ref[pl.ds(first, batch), :depth]
-            tile = min(TILE, columns)
-            for i in range(0, columns, tile):
+            dot = lambda right: jnp.dot(x, right, preferred_element_type=jnp.float32)
+            for i in range(0, columns, TILE):
+                tile = min(TILE, columns - i)
                 cut = slice(start + i, start + i + tile)
-                gate = jnp.dot(x, gate_ref[:, cut], preferred_element_type=jnp.float32)
-                up = jnp.dot(x, up_ref[:, cut], preferred_element_type=jnp.float32)
+                if 2 * tile <= TILE:
+                    both = dot(jnp.concatenate([gate_ref[:, cut], up_ref[:, cut]], axis=1))
+                    gate, up = both[:, :tile], both[:, tile:]
+                else:
+                    gate, up = dot(gate_ref[:, cut]), dot(up_ref[:, cut])
                 value = gate / (1.0 + jnp.exp(-gate)) * up
                 hidden_ref[pl.ds(first, batch), i : i + tile] = value.astype(hidden_ref.dtype)
 
@@ -139,16 +142,17 @@
 def contract_hidden(
     parts, w_down, units, before=None, rows=None, half=None, index=None, kind=jnp.float32
 ):
-    total_count, width = parts[0][0].shape[0], w_down.shape[1]
+    total_count, width = parts[0][0][0].shape[0], w_down.shape[1]
     count = total_count if index is None else total_count // 2
     offset = 0 if index is None else index * count
     experts = lax.axis_size(EXPERT)
-    operands = [part for part, _, _ in parts] + [in_vmem(w_down)]
+    values = [value for part, _, _ in parts for value in part]
+    operands = values + [in_vmem(w_down)]
     operands += [value for value in (before, rows) if value is not None]
 
     def body(*refs):
-        part_refs, down_ref = refs[: len(parts)], refs[len(parts)]
-        rest = list(refs[len(parts) + 1 : -1])
+        part_refs, down_ref = refs[: len(values)], refs[len(values)]
+        rest = list(refs[len(values) + 1 : -1])
         before_ref = rest.pop(0) if before is not None else None
         rows_ref = rest.pop(0) if rows is not None else None
         me, group = lax.axis_index(EXPERT), lax.axis_index("dp")
@@ -163,6 +167,9 @@
                     jnp.concatenate([ref[i * half : (i + 1) * half, :] for i in order])
                     for ref in part_refs
                 ]
+            lefts = [
+                jnp.concatenate([lefts.pop(0) for _ in part], axis=1) for part, _, _ in parts
+            ]
             if rows is not None:
                 table = rows_ref[here, rows.shape[1] - LANES :].astype(jnp.float32)
                 lane = lax.broadcasted_iota(jnp.int32, table.shape, 1)
@@ -268,31 +275,31 @@
         rows += [first[:size], y, x, first[size:]]
     rows = jnp.concatenate(rows)
 
-    chunks = CHUNKS if units % (LANES * CHUNKS) == 0 else 1
-    step = units // chunks
+    eighth = units // 8
+    steps = (3 * eighth, 3 * eighth, 2 * eighth) if eighth % LANES == 0 else (units,)
+    starts = [sum(steps[:i]) for i in range(len(steps))]
     half = rows.shape[0] // 4 if groups == 2 and rows.shape[0] <= BATCH else None
 
     def from_group(value, mask):
         value = swap(value, mask, 0)
         if half is not None:
             return value
-        value = value.reshape(2, 2, 2, wide, high * token_count, step)
+        value = value.reshape(2, 2, 2, wide, high * token_count, value.shape[1])
         value = jnp.stack([value[:, i ^ (mask & 1)] for i in range(2)], axis=1)
         value = jnp.stack([value[:, :, :, i ^ (mask >> 1)] for i in range(wide)], axis=3)
-        return value.reshape(-1, step)
+        return value.reshape(-1, value.shape[-1])
 
     hidden, others = [], []
-    for i in range(chunks):
+    for start, step in zip(starts, steps):
         if hidden:
             rows, hidden[-1] = lax.optimization_barrier((rows, hidden[-1]))
-        hidden.append(expand_rows(rows, gate_weights, up_weights, i * step, step))
+        hidden.append(expand_rows(rows, gate_weights, up_weights, start, step))
         others.append(
-            [(from_group(hidden[-1], mask), mask, i * step) for mask in range(1, groups)]
+            [([from_group(hidden[-1], mask)], mask, start) for mask in range(1, groups)]
         )
-    parts = [(value, 0, i * step) for i, value in enumerate(hidden)]
-    total = contract_hidden(parts, down_weights, units)
-    for i in range(chunks - 1):
-        total = contract_hidden(others[i], down_weights, units, total, half=half)
+    total = contract_hidden([(hidden, 0, 0)], down_weights, units)
+    for parts in others[:-1]:
+        total = contract_hidden(parts, down_weights, units, total, half=half)
     last = lambda index, kind: contract_hidden(
         others[-1], down_weights, units, total, rows, half, index, kind
     )

time: 48 us -> 47.5 us (0.990)
  waiting for transfers between devices: 20.6 us -> 18.4 us
  starting transfers between devices: 20.2 us -> 21.7 us
    ppermute x18 -> x19, waiting for transfers between devices: 20.6 us -> 18.4 us  [swap(): return lax.ppermute(value, ('dp',) + EXPERT, pairs)]
    ppermute x18 -> x19, starting transfers between devices: 20.2 us -> 21.7 us  [swap(): return lax.ppermute(value, ('dp',) + EXPERT, pairs)]
    pallas_call x2 -> x3, Pallas kernels: 2.76 us -> 2.91 us  [expand_rows(): pl.pallas_call(body, out_shape=jax.ShapeDtypeStruct((count, columns), row...]
    pallas_call x4 -> x5, Pallas kernels: 2.16 us -> 2.26 us  [contract_hidden(): pl.pallas_call(body, out_shape=jax.ShapeDtypeStruct((count, width), kind)...]
  transfers between devices with their start and end apart: 18 -> 19, of which waited for: 14 -> 14; matrix products, arithmetic and copies ran while one was open for 0% -> 0% of each run, Pallas kernels for 7% -> 8%
where the time goes in v19:
time: 47.5 us; the launch traced here: 47.4 us
  starting transfers between devices  21.7 us (46%)
  waiting for transfers between devices  18.4 us (39%)
  Pallas kernels  6.97 us (15%)
    ppermute x19, starting transfers between devices, swap(): return lax.ppermute(value, ('dp',) + EXPERT, pairs)  21.7 us
    ppermute x19, waiting for transfers between devices, swap(): return lax.ppermute(value, ('dp',) + EXPERT, pairs)  18.4 us
    pallas_call x3, Pallas kernels, expand_rows(): pl.pallas_call(body, out_shape=jax.ShapeDtypeStruct((count, columns), row...  2.91 us
    pallas_call x5, Pallas kernels, contract_hidden(): pl.pallas_call(body, out_shape=jax.ShapeDtypeStruct((count, width), kind)...  2.26 us
  transfers between devices with their start and end apart: 19, of which 14 were waited for; matrix products, arithmetic and copies ran while one was open for 0% of the time, Pallas kernels for 8%

profile of v19, /device:TPU:0, one launch (start us, length us, event | category | flops | bytes accessed | tf_op | source)
XLA Modules:
  0.0 47.4 jit_solution(2076752242496577861)
XLA Ops:
  0.0 0.9 %pack_block.1.refs_0_ = bf16[4,4224]{1,0:T(4,128)(2,1)S(1)} custom-call(bf16[4,4096]{1,0:T(4,128)(2,1)} %tokens_ref.1, s32[4,8]{1,0:T(4,128)} %ids_ref.1, f32[4,8]{1,0:T(4,128)} %probs_ref.1), custom_call_target="tpu_custom_call" | custom-call | tf_op jit(solution)/shard_map/pack_block/pallas_call | solution.py:62
  0.9 5.1 %collective-permute-start.2 = (bf16[4,4224]{1,0:T(4,128)(2,1)S(1)}, bf16[4,4224]{1,0:T(4,128)(2,1)S(1)}, u32[]{:S(2)}, u32[]{:S(2)}) collective-permute-start(bf16[4,4224]{1,0:T(4,128)(2,1)S(1)} %pack_block.1.refs_0_), channel_id=1, source_target_pairs={{0,12},{1,13},{2,14},{3,15},{4,8},{5,9},{6,10},{7,11},{8,4},{9,5},... | collective-permute-start | bytes 101384 | tf_op jit(solution)/shard_map/ppermute | solution.py:22
  6.0 0.6 %collective-permute-start = (bf16[4,4224]{1,0:T(4,128)(2,1)S(1)}, bf16[4,4224]{1,0:T(4,128)(2,1)S(1)}, u32[]{:S(2)}, u32[]{:S(2)}) collective-permute-start(bf16[4,4224]{1,0:T(4,128)(2,1)S(1)} %pack_block.1.refs_0_), channel_id=1, source_target_pairs={{0,4},{1,5},{2,6},{3,7},{4,0},{5,1},{6,2},{7,3},{8,12},{9,13},{10,... | collective-permute-start | bytes 101384 | tf_op jit(solution)/shard_map/ppermute | solution.py:22
  6.6 1.3 %collective-permute-done.2.refs_3_ = bf16[4,4224]{1,0:T(4,128)(2,1)S(1)} collective-permute-done((bf16[4,4224]{1,0:T(4,128)(2,1)S(1)}, bf16[4,4224]{1,0:T(4,128)(2,1)S(1)}, u32[]{:S(2)}, u32[]{:S(2)}) %collective-permute-start.2) | collective-permute-done | bytes 33824 | tf_op jit(solution)/shard_map/ppermute | solution.py:22
  7.9 2.9 %collective-permute-done.1.refs_2_ = bf16[4,4224]{1,0:T(4,128)(2,1)S(1)} collective-permute-done((bf16[4,4224]{1,0:T(4,128)(2,1)S(1)}, bf16[4,4224]{1,0:T(4,128)(2,1)S(1)}, u32[]{:S(2)}, u32[]{:S(2)}) %collective-permute-start.1) | collective-permute-done | bytes 33824 | tf_op jit(solution)/shard_map/ppermute | solution.py:22
  10.8 2.5 %collective-permute-start.3 = (bf16[4,4,4224]{2,1,0:T(4,128)(2,1)S(1)}, bf16[4,4,4224]{2,1,0:T(4,128)(2,1)S(1)}, u32[]{:S(2)}, u32[]{:S(2)}) collective-permute-start(bf16[4,4,4224]{2,1,0:T(4,128)(2,1)S(1)} %stack_blocks.1.refs_0_), channel_id=1, source_target_pairs={{0,18},{1,19},{2,16},{3,17},{4,22},{5,23},{6,20},{7,21},{8,26},{9,... | collective-permute-start | bytes 405512 | tf_op jit(solution)/shard_map/ppermute | solution.py:22
  13.3 0.5 %collective-permute-start.5 = (bf16[4,4,4224]{2,1,0:T(4,128)(2,1)S(1)}, bf16[4,4,4224]{2,1,0:T(4,128)(2,1)S(1)}, u32[]{:S(2)}, u32[]{:S(2)}) collective-permute-start(bf16[4,4,4224]{2,1,0:T(4,128)(2,1)S(1)} %stack_blocks.1.refs_0_), channel_id=1, source_target_pairs={{0,16},{1,17},{2,18},{3,19},{4,20},{5,21},{6,22},{7,23},{8,24},{9,... | collective-permute-start | bytes 405512 | tf_op jit(solution)/shard_map/ppermute | solution.py:22
  13.9 0.5 %collective-permute-start.4 = (bf16[4,4,4224]{2,1,0:T(4,128)(2,1)S(1)}, bf16[4,4,4224]{2,1,0:T(4,128)(2,1)S(1)}, u32[]{:S(2)}, u32[]{:S(2)}) collective-permute-start(bf16[4,4,4224]{2,1,0:T(4,128)(2,1)S(1)} %stack_blocks.1.refs_0_), channel_id=1, source_target_pairs={{0,2},{1,3},{2,0},{3,1},{4,6},{5,7},{6,4},{7,5},{8,10},{9,11},{10,... | collective-permute-start | bytes 405512 | tf_op jit(solution)/shard_map/ppermute | solution.py:22
  14.4 2.8 %collective-permute-done.3.refs_1_ = bf16[4,4,4224]{2,1,0:T(4,128)(2,1)S(1)} collective-permute-done((bf16[4,4,4224]{2,1,0:T(4,128)(2,1)S(1)}, bf16[4,4,4224]{2,1,0:T(4,128)(2,1)S(1)}, u32[]{:S(2)}, u32[]{:S(2)}) %collective-permute-start.3) | collective-permute-done | bytes 135200 | tf_op jit(solution)/shard_map/ppermute | solution.py:22
  17.2 0.1 join_rows.3
  17.3 0.1 collective-permute-start.6
  17.4 1.3 %collective-permute-done.5.refs_0_ = bf16[4,4,4224]{2,1,0:T(4,128)(2,1)S(1)} collective-permute-done((bf16[4,4,4224]{2,1,0:T(4,128)(2,1)S(1)}, bf16[4,4,4224]{2,1,0:T(4,128)(2,1)S(1)}, u32[]{:S(2)}, u32[]{:S(2)}) %collective-permute-start.5) | collective-permute-done | bytes 135200 | tf_op jit(solution)/shard_map/ppermute | solution.py:22
  18.7 0.1 collective-permute-start.8
  18.8 0.1 collective-permute-done.4.refs_0_
  18.9 0.4 collective-permute-start.7
  19.4 0.0 collective-permute-done.6
  19.5 0.9 %collective-permute-done.7 = bf16[16,4224]{1,0:T(8,128)(2,1)S(1)} collective-permute-done((bf16[16,4224]{1,0:T(8,128)(2,1)S(1)}, bf16[16,4224]{1,0:T(8,128)(2,1)S(1)}, u32[]{:S(2)}, u32[]{:S(2)}) %collective-permute-start.7) | collective-permute-done | bytes 135200 | tf_op jit(solution)/shard_map/ppermute | solution.py:22
  20.4 0.0 collective-permute-done.8
  20.4 0.0 slice-start
  20.5 1.1 %expand_rows.3.refs_0_ = bf16[128,384]{1,0:T(8,128)(2,1)S(1)} custom-call(bf16[128,4224]{1,0:T(8,128)(2,1)S(1)} %slice_dynamic-update-slice_fusion.rows_ref.refs_3_, bf16[4096,1024]{1,0:T(8,128)(2,1)S(1)} %bitcast.10, bf16[4096,1024]{1,0:T(8,128)(2,1)S(1)} %bitcast.13), custom_call_target="tpu_custom_call" | custom-call | bytes 49152 | tf_op jit(solution)/shard_map/expand_rows/pallas_call | solution.py:131
  21.6 0.0 slice-start.1
  21.6 1.6 %collective-permute-start.11 = (bf16[128,384]{1,0:T(8,128)(2,1)S(1)}, bf16[128,384]{1,0:T(8,128)(2,1)S(1)}, u32[]{:S(2)}, u32[]{:S(2)}) collective-permute-start(bf16[128,384]{1,0:T(8,128)(2,1)S(1)} %expand_rows.3.refs_0_), channel_id=1, source_target_pairs={{0,16},{1,17},{2,18},{3,19},{4,20},{5,21},{6,22},{7,23},{8,24},{9,... | collective-permute-start | bytes 294920 | tf_op jit(solution)/shard_map/ppermute | solution.py:22
  23.1 1.0 %expand_rows.4.refs_1_ = bf16[128,384]{1,0:T(8,128)(2,1)S(1)} custom-call(bf16[128,4224]{1,0:T(8,128)(2,1)S(1)} %slice_dynamic-update-slice_fusion.rows_ref.refs_3_, bf16[4096,1024]{1,0:T(8,128)(2,1)S(1)} %bitcast.11, bf16[4096,1024]{1,0:T(8,128)(2,1)S(1)} %bitcast.14), custom_call_target="tpu_custom_call" | custom-call | bytes 49152 | tf_op jit(solution)/shard_map/expand_rows/pallas_call | solution.py:131
  24.2 0.6 %collective-permute-start.10 = (bf16[128,384]{1,0:T(8,128)(2,1)S(1)}, bf16[128,384]{1,0:T(8,128)(2,1)S(1)}, u32[]{:S(2)}, u32[]{:S(2)}) collective-permute-start(bf16[128,384]{1,0:T(8,128)(2,1)S(1)} %expand_rows.4.refs_1_), channel_id=1, source_target_pairs={{0,16},{1,17},{2,18},{3,19},{4,20},{5,21},{6,22},{7,23},{8,24},{9,... | collective-permute-start | bytes 294920 | tf_op jit(solution)/shard_map/ppermute | solution.py:22
  24.8 0.8 %expand_rows.5.refs_2_ = bf16[128,256]{1,0:T(8,128)(2,1)S(1)} custom-call(bf16[128,4224]{1,0:T(8,128)(2,1)S(1)} %slice_dynamic-update-slice_fusion.rows_ref.refs_3_, bf16[4096,1024]{1,0:T(8,128)(2,1)S(1)} %bitcast.12, bf16[4096,1024]{1,0:T(8,128)(2,1)S(1)} %bitcast.15), custom_call_target="tpu_custom_call" | custom-call | bytes 32768 | tf_op jit(solution)/shard_map/expand_rows/pallas_call | solution.py:131
  25.6 1.5 %collective-permute-start.9 = (bf16[128,256]{1,0:T(8,128)(2,1)S(1)}, bf16[128,256]{1,0:T(8,128)(2,1)S(1)}, u32[]{:S(2)}, u32[]{:S(2)}) collective-permute-start(bf16[128,256]{1,0:T(8,128)(2,1)S(1)} %expand_rows.5.refs_2_), channel_id=1, source_target_pairs={{0,16},{1,17},{2,18},{3,19},{4,20},{5,21},{6,22},{7,23},{8,24},{9,... | collective-permute-start | bytes 196616 | tf_op jit(solution)/shard_map/ppermute | solution.py:22
  27.1 0.7 %contract_hidden.5.refs_2_ = f32[128,2048]{1,0:T(8,128)S(1)} custom-call(bf16[128,384]{1,0:T(8,128)(2,1)S(1)} %expand_rows.3.refs_0_, bf16[128,384]{1,0:T(8,128)(2,1)S(1)} %expand_rows.4.refs_1_, bf16[128,256]{1,0:T(8,128)(2,1)S(1)} %expand_rows.5.refs_2_, bf16[2048,2048]{1,0:T(8,128)(2,1)S(1)} %bitcast.5), custom_call_target="tpu_custom_call" | custom-call | bytes 262144 | tf_op jit(solution)/shard_map/contract_hidden/pallas_call | solution.py:192
  27.9 0.5 contract_hidden.6.refs_2_
  28.4 1.4 %collective-permute-done.10.refs_0_ = bf16[128,384]{1,0:T(8,128)(2,1)S(1)} collective-permute-done((bf16[128,384]{1,0:T(8,128)(2,1)S(1)}, bf16[128,384]{1,0:T(8,128)(2,1)S(1)}, u32[]{:S(2)}, u32[]{:S(2)}) %collective-permute-start.10) | collective-permute-done | bytes 98336 | tf_op jit(solution)/shard_map/ppermute | solution.py:22
  29.8 0.4 contract_hidden.7.refs_2_
  30.2 0.2 collective-permute-done.9.refs_0_
  30.5 0.3 contract_hidden.9
  30.8 0.1 collective-permute-start.12
  30.8 0.3 contract_hidden.8.refs_0_
  31.2 1.2 %collective-permute-done.12.refs_1_ = bf16[64,2048]{1,0:T(8,128)(2,1)S(1)} collective-permute-done((bf16[64,2048]{1,0:T(8,128)(2,1)S(1)}, bf16[64,2048]{1,0:T(8,128)(2,1)S(1)}, u32[]{:S(2)}, u32[]{:S(2)}) %collective-permute-start.12) | collective-permute-done | bytes 262176 | tf_op jit(solution)/shard_map/ppermute | solution.py:22
  32.4 0.1 sum_stage.2
  32.5 0.6 %collective-permute-start.13 = (bf16[4,4,2048]{2,1,0:T(4,128)(2,1)S(1)}, bf16[4,4,2048]{2,1,0:T(4,128)(2,1)S(1)}, u32[]{:S(2)}, u32[]{:S(2)}) collective-permute-start(bf16[4,4,2048]{2,1,0:T(4,128)(2,1)S(1)} %get-tuple-element.30), channel_id=1, source_target_pairs={{0,6},{1,7},{2,4},{3,5},{4,2},{5,3},{6,0},{7,1},{8,14},{9,15},{10,... | collective-permute-start | bytes 196616 | tf_op jit(solution)/shard_map/ppermute | solution.py:22
  33.1 1.9 %collective-permute-start.14 = (bf16[4,4,2048]{2,1,0:T(4,128)(2,1)S(1)}, bf16[4,4,2048]{2,1,0:T(4,128)(2,1)S(1)}, u32[]{:S(2)}, u32[]{:S(2)}) collective-permute-start(bf16[4,4,2048]{2,1,0:T(4,128)(2,1)S(1)} %get-tuple-element.31), channel_id=1, source_target_pairs={{0,4},{1,5},{2,6},{3,7},{4,0},{5,1},{6,2},{7,3},{8,12},{9,13},{10,... | collective-permute-start | bytes 196616 | tf_op jit(solution)/shard_map/ppermute | solution.py:22
  35.0 1.0 %collective-permute-start.15 = (bf16[4,4,2048]{2,1,0:T(4,128)(2,1)S(1)}, bf16[4,4,2048]{2,1,0:T(4,128)(2,1)S(1)}, u32[]{:S(2)}, u32[]{:S(2)}) collective-permute-start(bf16[4,4,2048]{2,1,0:T(4,128)(2,1)S(1)} %get-tuple-element.32), channel_id=1, source_target_pairs={{0,2},{1,3},{2,0},{3,1},{4,6},{5,7},{6,4},{7,5},{8,10},{9,11},{10,... | collective-permute-start | bytes 196616 | tf_op jit(solution)/shard_map/ppermute | solution.py:22
  36.0 2.3 %collective-permute-done.13.refs_1_ = bf16[4,4,2048]{2,1,0:T(4,128)(2,1)S(1)} collective-permute-done((bf16[4,4,2048]{2,1,0:T(4,128)(2,1)S(1)}, bf16[4,4,2048]{2,1,0:T(4,128)(2,1)S(1)}, u32[]{:S(2)}, u32[]{:S(2)}) %collective-permute-start.13) | collective-permute-done | bytes 65568 | tf_op jit(solution)/shard_map/ppermute | solution.py:22
  38.4 0.2 collective-permute-done.14.refs_2_
  38.5 0.8 %collective-permute-done.15.refs_3_ = bf16[4,4,2048]{2,1,0:T(4,128)(2,1)S(1)} collective-permute-done((bf16[4,4,2048]{2,1,0:T(4,128)(2,1)S(1)}, bf16[4,4,2048]{2,1,0:T(4,128)(2,1)S(1)}, u32[]{:S(2)}, u32[]{:S(2)}) %collective-permute-start.15) | collective-permute-done | bytes 65568 | tf_op jit(solution)/shard_map/ppermute | solution.py:22
  39.3 2.8 %collective-permute-start.16 = (bf16[1,4,2048]{2,1,0:T(4,128)(2,1)S(1)}, bf16[1,4,2048]{2,1,0:T(4,128)(2,1)S(1)}, u32[]{:S(2)}, u32[]{:S(2)}) collective-permute-start(bf16[1,4,2048]{2,1,0:T(4,128)(2,1)S(1)} %get-tuple-element.33), channel_id=1, source_target_pairs={{0,24},{1,25},{2,26},{3,27},{4,28},{5,29},{6,30},{7,31},{8,16},{9,... | collective-permute-start | bytes 49160 | tf_op jit(solution)/shard_map/ppermute | solution.py:22
  42.1 0.9 %collective-permute-start.17 = (bf16[1,4,2048]{2,1,0:T(4,128)(2,1)S(1)}, bf16[1,4,2048]{2,1,0:T(4,128)(2,1)S(1)}, u32[]{:S(2)}, u32[]{:S(2)}) collective-permute-start(bf16[1,4,2048]{2,1,0:T(4,128)(2,1)S(1)} %get-tuple-element.34), channel_id=1, source_target_pairs={{0,8},{1,9},{2,10},{3,11},{4,12},{5,13},{6,14},{7,15},{8,0},{9,1},... | collective-permute-start | bytes 49160 | tf_op jit(solution)/shard_map/ppermute | solution.py:22
  43.0 0.8 %collective-permute-start.18 = (bf16[1,4,2048]{2,1,0:T(4,128)(2,1)S(1)}, bf16[1,4,2048]{2,1,0:T(4,128)(2,1)S(1)}, u32[]{:S(2)}, u32[]{:S(2)}) collective-permute-start(bf16[1,4,2048]{2,1,0:T(4,128)(2,1)S(1)} %get-tuple-element.35), channel_id=1, source_target_pairs={{0,16},{1,17},{2,18},{3,19},{4,20},{5,21},{6,22},{7,23},{8,24},{9,... | collective-permute-start | bytes 49160 | tf_op jit(solution)/shard_map/ppermute | solution.py:22
  43.8 1.2 %collective-permute-done.16.refs_0_ = bf16[1,4,2048]{2,1,0:T(4,128)(2,1)S(1)} collective-permute-done((bf16[1,4,2048]{2,1,0:T(4,128)(2,1)S(1)}, bf16[1,4,2048]{2,1,0:T(4,128)(2,1)S(1)}, u32[]{:S(2)}, u32[]{:S(2)}) %collective-permute-start.16) | collective-permute-done | bytes 16416 | tf_op jit(solution)/shard_map/ppermute | solution.py:22
  45.0 1.7 %collective-permute-done.17.refs_1_ = bf16[1,4,2048]{2,1,0:T(4,128)(2,1)S(1)} collective-permute-done((bf16[1,4,2048]{2,1,0:T(4,128)(2,1)S(1)}, bf16[1,4,2048]{2,1,0:T(4,128)(2,1)S(1)}, u32[]{:S(2)}, u32[]{:S(2)}) %collective-permute-start.17) | collective-permute-done | bytes 16416 | tf_op jit(solution)/shard_map/ppermute | solution.py:22
  46.7 0.6 %finish.1 = bf16[4,4096]{1,0:T(4,128)(2,1)} custom-call(bf16[1,4,2048]{2,1,0:T(4,128)(2,1)S(1)} %collective-permute-done.16.refs_0_, bf16[1,4,2048]{2,1,0:T(4,128)(2,1)S(1)} %collective-permute-done.17.refs_1_, bf16[1,4,2048]{2,1,0:T(4,128)(2,1)S(1)} %collective-permute-done.18.refs_2_, f32[1,4,2048]{2,1,0:T(4,128)S(1)} %get-tuple-element.36.refs_3_), custom_call_target="tpu_custom_call" | custom-call | tf_op jit(solution)/shard_map/finish/pallas_call | solution.py:247
  (23 shorter events, 0.3 us)
Async XLA Ops:
  0.9 7.0 %collective-permute-start.2 = (bf16[4,4224]{1,0:T(4,128)(2,1)S(1)}, bf16[4,4224]{1,0:T(4,128)(2,1)S(1)}, u32[]{:S(2)}, u32[]{:S(2)}) collective-permute-start(bf16[4,4224]{1,0:T(4,128)(2,1)S(1)} %pack_block.1.refs_0_), channel_id=1, source_target_pairs={{0,12},{1,13},{2,14},{3,15},{4,8},{5,9},{6,10},{7,11},{8,4},{9,5},... | collective-permute-start | bytes 101384 | tf_op jit(solution)/shard_map/ppermute | solution.py:22
  6.0 4.8 %collective-permute-start.1 = (bf16[4,4224]{1,0:T(4,128)(2,1)S(1)}, bf16[4,4224]{1,0:T(4,128)(2,1)S(1)}, u32[]{:S(2)}, u32[]{:S(2)}) collective-permute-start(bf16[4,4224]{1,0:T(4,128)(2,1)S(1)} %pack_block.1.refs_0_), channel_id=1, source_target_pairs={{0,8},{1,9},{2,10},{3,11},{4,12},{5,13},{6,14},{7,15},{8,0},{9,1},... | collective-permute-start | bytes 101384 | tf_op jit(solution)/shard_map/ppermute | solution.py:22
  6.0 4.8 %collective-permute-start = (bf16[4,4224]{1,0:T(4,128)(2,1)S(1)}, bf16[4,4224]{1,0:T(4,128)(2,1)S(1)}, u32[]{:S(2)}, u32[]{:S(2)}) collective-permute-start(bf16[4,4224]{1,0:T(4,128)(2,1)S(1)} %pack_block.1.refs_0_), channel_id=1, source_target_pairs={{0,4},{1,5},{2,6},{3,7},{4,0},{5,1},{6,2},{7,3},{8,12},{9,13},{10,... | collective-permute-start | bytes 101384 | tf_op jit(solution)/shard_map/ppermute | solution.py:22
  10.8 9.6 %copy-start = (bf16[1,4096,1024]{2,1,0:T(8,128)(2,1)S(1)}, bf16[1,4096,1024]{2,1,0:T(8,128)(2,1)}, u32[]{:S(2)}) copy-start(bf16[1,4096,1024]{2,1,0:T(8,128)(2,1)} %param.9) | copy-start | bytes 25165828
  10.8 9.6 %copy-start.1 = (bf16[1,4096,1024]{2,1,0:T(8,128)(2,1)S(1)}, bf16[1,4096,1024]{2,1,0:T(8,128)(2,1)}, u32[]{:S(2)}) copy-start(bf16[1,4096,1024]{2,1,0:T(8,128)(2,1)} %param.10) | copy-start | bytes 25165828
  10.8 6.4 %collective-permute-start.3 = (bf16[4,4,4224]{2,1,0:T(4,128)(2,1)S(1)}, bf16[4,4,4224]{2,1,0:T(4,128)(2,1)S(1)}, u32[]{:S(2)}, u32[]{:S(2)}) collective-permute-start(bf16[4,4,4224]{2,1,0:T(4,128)(2,1)S(1)} %stack_blocks.1.refs_0_), channel_id=1, source_target_pairs={{0,18},{1,19},{2,16},{3,17},{4,22},{5,23},{6,20},{7,21},{8,26},{9,... | collective-permute-start | bytes 405512 | tf_op jit(solution)/shard_map/ppermute | solution.py:22
  13.3 5.3 %collective-permute-start.5 = (bf16[4,4,4224]{2,1,0:T(4,128)(2,1)S(1)}, bf16[4,4,4224]{2,1,0:T(4,128)(2,1)S(1)}, u32[]{:S(2)}, u32[]{:S(2)}) collective-permute-start(bf16[4,4,4224]{2,1,0:T(4,128)(2,1)S(1)} %stack_blocks.1.refs_0_), channel_id=1, source_target_pairs={{0,16},{1,17},{2,18},{3,19},{4,20},{5,21},{6,22},{7,23},{8,24},{9,... | collective-permute-start | bytes 405512 | tf_op jit(solution)/shard_map/ppermute | solution.py:22
  13.9 5.0 %collective-permute-start.4 = (bf16[4,4,4224]{2,1,0:T(4,128)(2,1)S(1)}, bf16[4,4,4224]{2,1,0:T(4,128)(2,1)S(1)}, u32[]{:S(2)}, u32[]{:S(2)}) collective-permute-start(bf16[4,4,4224]{2,1,0:T(4,128)(2,1)S(1)} %stack_blocks.1.refs_0_), channel_id=1, source_target_pairs={{0,2},{1,3},{2,0},{3,1},{4,6},{5,7},{6,4},{7,5},{8,10},{9,11},{10,... | collective-permute-start | bytes 405512 | tf_op jit(solution)/shard_map/ppermute | solution.py:22
  17.3 2.1 %collective-permute-start.6 = (bf16[32,4224]{1,0:T(8,128)(2,1)S(1)}, bf16[32,4224]{1,0:T(8,128)(2,1)S(1)}, u32[]{:S(2)}, u32[]{:S(2)}) collective-permute-start(bf16[32,4224]{1,0:T(8,128)(2,1)S(1)} %join_rows.3), channel_id=1, source_target_pairs={{0,1},{1,0},{2,3},{3,2},{4,5},{5,4},{6,7},{7,6},{8,9},{9,8},{10,11... | collective-permute-start | bytes 811016 | tf_op jit(solution)/shard_map/ppermute | solution.py:22
  18.7 1.7 %collective-permute-start.8 = (bf16[16,4224]{1,0:T(8,128)(2,1)S(1)}, bf16[16,4224]{1,0:T(8,128)(2,1)S(1)}, u32[]{:S(2)}, u32[]{:S(2)}) collective-permute-start(bf16[16,4224]{1,0:T(8,128)(2,1)S(1)} %join_rows.5), channel_id=1, source_target_pairs={{0,1},{1,0},{2,3},{3,2},{4,5},{5,4},{6,7},{7,6},{8,9},{9,8},{10,11... | collective-permute-start | bytes 405512 | tf_op jit(solution)/shard_map/ppermute | solution.py:22
  18.9 1.4 %collective-permute-start.7 = (bf16[16,4224]{1,0:T(8,128)(2,1)S(1)}, bf16[16,4224]{1,0:T(8,128)(2,1)S(1)}, u32[]{:S(2)}, u32[]{:S(2)}) collective-permute-start(bf16[16,4224]{1,0:T(8,128)(2,1)S(1)} %join_rows.4), channel_id=1, source_target_pairs={{0,1},{1,0},{2,3},{3,2},{4,5},{5,4},{6,7},{7,6},{8,9},{9,8},{10,11... | collective-permute-start | bytes 405512 | tf_op jit(solution)/shard_map/ppermute | solution.py:22
  20.4 6.7 %slice-start = ((s8[8388608]{0:T(1024)(128)(4,1)}), s8[4194304]{0:T(1024)(128)(4,1)S(1)}, s32[]{:S(2)}) async-start(s8[8388608]{0:T(1024)(128)(4,1)} %bitcast.3), calls=%async_computation | async-start | bytes 8388608
  21.6 5.6 %slice-start.1 = ((s8[8388608]{0:T(1024)(128)(4,1)}), s8[4194304]{0:T(1024)(128)(4,1)S(1)}, s32[]{:S(2)}) async-start(s8[8388608]{0:T(1024)(128)(4,1)} %bitcast.3), calls=%async_computation.1 | async-start | bytes 8388608
  21.6 6.3 %collective-permute-start.11 = (bf16[128,384]{1,0:T(8,128)(2,1)S(1)}, bf16[128,384]{1,0:T(8,128)(2,1)S(1)}, u32[]{:S(2)}, u32[]{:S(2)}) collective-permute-start(bf16[128,384]{1,0:T(8,128)(2,1)S(1)} %expand_rows.3.refs_0_), channel_id=1, source_target_pairs={{0,16},{1,17},{2,18},{3,19},{4,20},{5,21},{6,22},{7,23},{8,24},{9,... | collective-permute-start | bytes 294920 | tf_op jit(solution)/shard_map/ppermute | solution.py:22
  24.2 5.6 %collective-permute-start.10 = (bf16[128,384]{1,0:T(8,128)(2,1)S(1)}, bf16[128,384]{1,0:T(8,128)(2,1)S(1)}, u32[]{:S(2)}, u32[]{:S(2)}) collective-permute-start(bf16[128,384]{1,0:T(8,128)(2,1)S(1)} %expand_rows.4.refs_1_), channel_id=1, source_target_pairs={{0,16},{1,17},{2,18},{3,19},{4,20},{5,21},{6,22},{7,23},{8,24},{9,... | collective-permute-start | bytes 294920 | tf_op jit(solution)/shard_map/ppermute | solution.py:22
  25.6 4.8 %collective-permute-start.9 = (bf16[128,256]{1,0:T(8,128)(2,1)S(1)}, bf16[128,256]{1,0:T(8,128)(2,1)S(1)}, u32[]{:S(2)}, u32[]{:S(2)}) collective-permute-start(bf16[128,256]{1,0:T(8,128)(2,1)S(1)} %expand_rows.5.refs_2_), channel_id=1, source_target_pairs={{0,16},{1,17},{2,18},{3,19},{4,20},{5,21},{6,22},{7,23},{8,24},{9,... | collective-permute-start | bytes 196616 | tf_op jit(solution)/shard_map/ppermute | solution.py:22
  30.8 1.6 %collective-permute-start.12 = (bf16[64,2048]{1,0:T(8,128)(2,1)S(1)}, bf16[64,2048]{1,0:T(8,128)(2,1)S(1)}, u32[]{:S(2)}, u32[]{:S(2)}) collective-permute-start(bf16[64,2048]{1,0:T(8,128)(2,1)S(1)} %contract_hidden.9), channel_id=1, source_target_pairs={{0,1},{1,0},{2,3},{3,2},{4,5},{5,4},{6,7},{7,6},{8,9},{9,8},{10,11... | collective-permute-start | bytes 786440 | tf_op jit(solution)/shard_map/ppermute | solution.py:22
  32.5 5.9 %collective-permute-start.13 = (bf16[4,4,2048]{2,1,0:T(4,128)(2,1)S(1)}, bf16[4,4,2048]{2,1,0:T(4,128)(2,1)S(1)}, u32[]{:S(2)}, u32[]{:S(2)}) collective-permute-start(bf16[4,4,2048]{2,1,0:T(4,128)(2,1)S(1)} %get-tuple-element.30), channel_id=1, source_target_pairs={{0,6},{1,7},{2,4},{3,5},{4,2},{5,3},{6,0},{7,1},{8,14},{9,15},{10,... | collective-permute-start | bytes 196616 | tf_op jit(solution)/shard_map/ppermute | solution.py:22
  33.1 5.4 %collective-permute-start.14 = (bf16[4,4,2048]{2,1,0:T(4,128)(2,1)S(1)}, bf16[4,4,2048]{2,1,0:T(4,128)(2,1)S(1)}, u32[]{:S(2)}, u32[]{:S(2)}) collective-permute-start(bf16[4,4,2048]{2,1,0:T(4,128)(2,1)S(1)} %get-tuple-element.31), channel_id=1, source_target_pairs={{0,4},{1,5},{2,6},{3,7},{4,0},{5,1},{6,2},{7,3},{8,12},{9,13},{10,... | collective-permute-start | bytes 196616 | tf_op jit(solution)/shard_map/ppermute | solution.py:22
  35.0 4.3 %collective-permute-start.15 = (bf16[4,4,2048]{2,1,0:T(4,128)(2,1)S(1)}, bf16[4,4,2048]{2,1,0:T(4,128)(2,1)S(1)}, u32[]{:S(2)}, u32[]{:S(2)}) collective-permute-start(bf16[4,4,2048]{2,1,0:T(4,128)(2,1)S(1)} %get-tuple-element.32), channel_id=1, source_target_pairs={{0,2},{1,3},{2,0},{3,1},{4,6},{5,7},{6,4},{7,5},{8,10},{9,11},{10,... | collective-permute-start | bytes 196616 | tf_op jit(solution)/shard_map/ppermute | solution.py:22
  39.3 5.7 %collective-permute-start.16 = (bf16[1,4,2048]{2,1,0:T(4,128)(2,1)S(1)}, bf16[1,4,2048]{2,1,0:T(4,128)(2,1)S(1)}, u32[]{:S(2)}, u32[]{:S(2)}) collective-permute-start(bf16[1,4,2048]{2,1,0:T(4,128)(2,1)S(1)} %get-tuple-element.33), channel_id=1, source_target_pairs={{0,24},{1,25},{2,26},{3,27},{4,28},{5,29},{6,30},{7,31},{8,16},{9,... | collective-permute-start | bytes 49160 | tf_op jit(solution)/shard_map/ppermute | solution.py:22
  42.1 4.6 %collective-permute-start.17 = (bf16[1,4,2048]{2,1,0:T(4,128)(2,1)S(1)}, bf16[1,4,2048]{2,1,0:T(4,128)(2,1)S(1)}, u32[]{:S(2)}, u32[]{:S(2)}) collective-permute-start(bf16[1,4,2048]{2,1,0:T(4,128)(2,1)S(1)} %get-tuple-element.34), channel_id=1, source_target_pairs={{0,8},{1,9},{2,10},{3,11},{4,12},{5,13},{6,14},{7,15},{8,0},{9,1},... | collective-permute-start | bytes 49160 | tf_op jit(solution)/shard_map/ppermute | solution.py:22
  43.0 3.8 %collective-permute-start.18 = (bf16[1,4,2048]{2,1,0:T(4,128)(2,1)S(1)}, bf16[1,4,2048]{2,1,0:T(4,128)(2,1)S(1)}, u32[]{:S(2)}, u32[]{:S(2)}) collective-permute-start(bf16[1,4,2048]{2,1,0:T(4,128)(2,1)S(1)} %get-tuple-element.35), channel_id=1, source_target_pairs={{0,16},{1,17},{2,18},{3,19},{4,20},{5,21},{6,22},{7,23},{8,24},{9,... | collective-permute-start | bytes 49160 | tf_op jit(solution)/shard_map/ppermute | solution.py:22

commit v20 on v19

--- a/solution.py
+++ b/solution.py
@@ -204,7 +204,7 @@
     )(*operands)
 
 
-def sum_stage(inputs, plan, shape, dtype):
+def sum_stage(inputs, plan, shape, dtype, wide=1):
     def body(*refs):
         sources, targets = refs[: len(inputs)], refs[len(inputs) :]
         for target, blocks in zip(targets, plan):
@@ -221,7 +221,7 @@
     return pl.pallas_call(
         body,
         out_shape=[
-            jax.ShapeDtypeStruct((len(blocks),) + shape, dtype if i else jnp.float32)
+            jax.ShapeDtypeStruct((len(blocks),) + shape, jnp.float32 if i < wide else dtype)
             for i, blocks in enumerate(plan)
         ],
         in_specs=[pl.BlockSpec(memory_space=pltpu.VMEM)] * len(inputs),
@@ -308,15 +308,25 @@
     shape = (token_count, w_down.shape[2])
     rest = [(g, h) for g in range(groups) for h in range(0, high, 2)]
     slot = lambda g, y, h: (((g & 1) * 2 + y) * wide + (g >> 1)) * high + h
-    plan = [[slot(g, y, h + z) for g, h in rest] for y, z in ((0, 0), (1, 1), (0, 1), (1, 0))]
-    mine, *away = sum_stage([kept, swap(sent, 0, 1)], plan, shape, jnp.bfloat16)
-    inputs = [mine] + [swap(value, 0, mask) for value, mask in zip(away, (6, 4, 2))]
-    order = sorted(range(1, len(rest)), key=lambda i: (rest[i][1], rest[i][0]), reverse=True)
-    mine, *away = sum_stage(inputs, [[i] for i in [0] + order], shape, jnp.bfloat16)
-    parts = [
-        (swap(value, rest[i][0], 4 * rest[i][1]), rest[i][0]) for value, i in zip(away, order)
+    rest.sort(key=lambda masks: (masks[1], masks[0]), reverse=True)
+    sets = ([masks for masks in rest if masks[1]], [masks for masks in rest if not masks[1]])
+    near = [[slot(g, 0, h) for g, h in blocks] for blocks in sets]
+    away = [
+        [slot(g, y, h + z) for g, h in blocks]
+        for blocks in sets
+        for y, z in ((1, 1), (0, 1), (1, 0))
     ]
-    return finish(parts + [(mine, 0)], groups, tokens.dtype)
+    inputs = [kept, swap(sent, 0, 1)]
+    sums = sum_stage(inputs, near + away, shape, jnp.bfloat16, 2)
+    got = [swap(value, 0, mask) for value, mask in zip(sums[2:], (6, 4, 2) * 2)]
+    parts = []
+    for i, blocks in enumerate(sets):
+        inputs = [sums[i]] + got[3 * i : 3 * i + 3]
+        order = range(len(blocks) - 1, -1, -1) if i else range(len(blocks))
+        values = sum_stage(inputs, [[j] for j in order], shape, jnp.bfloat16, i)
+        for value, (g, h) in zip(values, [blocks[j] for j in order]):
+            parts.append((swap(value, g, 4 * h) if g or h else value, g))
+    return finish(parts, groups, tokens.dtype)
 
 
 def solution(mesh):

time: 47.5 us -> 47.9 us (level)
  starting transfers between devices: 21.7 us -> 25.2 us
  waiting for transfers between devices: 18.4 us -> 15.1 us
    ppermute x19 -> x22, starting transfers between devices: 21.7 us -> 25.2 us  [swap(): return lax.ppermute(value, ('dp',) + EXPERT, pairs)]
    ppermute x19 -> x22, waiting for transfers between devices: 18.4 us -> 15.1 us  [swap(): return lax.ppermute(value, ('dp',) + EXPERT, pairs)]
  transfers between devices with their start and end apart: 19 -> 22, of which waited for: 14 -> 12; matrix products, arithmetic and copies ran while one was open for 0% -> 0% of each run, Pallas kernels for 8% -> 8%
where the time goes in v20:
time: 47.9 us; the launch traced here: 47.7 us
  starting transfers between devices  25.2 us (53%)
  waiting for transfers between devices  15.1 us (32%)
  Pallas kernels  6.97 us (15%)
    ppermute x22, starting transfers between devices, swap(): return lax.ppermute(value, ('dp',) + EXPERT, pairs)  25.2 us
    ppermute x22, waiting for transfers between devices, swap(): return lax.ppermute(value, ('dp',) + EXPERT, pairs)  15.1 us
    pallas_call x3, Pallas kernels, expand_rows(): pl.pallas_call(body, out_shape=jax.ShapeDtypeStruct((count, columns), row...  2.91 us
    pallas_call x5, Pallas kernels, contract_hidden(): pl.pallas_call(body, out_shape=jax.ShapeDtypeStruct((count, width), kind)...  2.26 us
  transfers between devices with their start and end apart: 22, of which 12 were waited for; matrix products, arithmetic and copies ran while one was open for 0% of the time, Pallas kernels for 8%

profile of v20, /device:TPU:0, one launch (start us, length us, event | category | flops | bytes accessed | tf_op | source)
XLA Modules:
  0.0 47.7 jit_solution(11190570235502954998)
XLA Ops:
  0.0 0.9 %pack_block.1.refs_0_ = bf16[4,4224]{1,0:T(4,128)(2,1)S(1)} custom-call(bf16[4,4096]{1,0:T(4,128)(2,1)} %tokens_ref.1, s32[4,8]{1,0:T(4,128)} %ids_ref.1, f32[4,8]{1,0:T(4,128)} %probs_ref.1), custom_call_target="tpu_custom_call" | custom-call | tf_op jit(solution)/shard_map/pack_block/pallas_call | solution.py:62
  0.9 5.1 %collective-permute-start.2 = (bf16[4,4224]{1,0:T(4,128)(2,1)S(1)}, bf16[4,4224]{1,0:T(4,128)(2,1)S(1)}, u32[]{:S(2)}, u32[]{:S(2)}) collective-permute-start(bf16[4,4224]{1,0:T(4,128)(2,1)S(1)} %pack_block.1.refs_0_), channel_id=1, source_target_pairs={{0,12},{1,13},{2,14},{3,15},{4,8},{5,9},{6,10},{7,11},{8,4},{9,5},... | collective-permute-start | bytes 101384 | tf_op jit(solution)/shard_map/ppermute | solution.py:22
  6.0 0.6 %collective-permute-start = (bf16[4,4224]{1,0:T(4,128)(2,1)S(1)}, bf16[4,4224]{1,0:T(4,128)(2,1)S(1)}, u32[]{:S(2)}, u32[]{:S(2)}) collective-permute-start(bf16[4,4224]{1,0:T(4,128)(2,1)S(1)} %pack_block.1.refs_0_), channel_id=1, source_target_pairs={{0,4},{1,5},{2,6},{3,7},{4,0},{5,1},{6,2},{7,3},{8,12},{9,13},{10,... | collective-permute-start | bytes 101384 | tf_op jit(solution)/shard_map/ppermute | solution.py:22
  6.6 1.3 %collective-permute-done.2.refs_3_ = bf16[4,4224]{1,0:T(4,128)(2,1)S(1)} collective-permute-done((bf16[4,4224]{1,0:T(4,128)(2,1)S(1)}, bf16[4,4224]{1,0:T(4,128)(2,1)S(1)}, u32[]{:S(2)}, u32[]{:S(2)}) %collective-permute-start.2) | collective-permute-done | bytes 33824 | tf_op jit(solution)/shard_map/ppermute | solution.py:22
  7.9 2.9 %collective-permute-done.1.refs_2_ = bf16[4,4224]{1,0:T(4,128)(2,1)S(1)} collective-permute-done((bf16[4,4224]{1,0:T(4,128)(2,1)S(1)}, bf16[4,4224]{1,0:T(4,128)(2,1)S(1)}, u32[]{:S(2)}, u32[]{:S(2)}) %collective-permute-start.1) | collective-permute-done | bytes 33824 | tf_op jit(solution)/shard_map/ppermute | solution.py:22
  10.8 0.0 collective-permute-done.refs_1_
  10.8 2.5 %collective-permute-start.3 = (bf16[4,4,4224]{2,1,0:T(4,128)(2,1)S(1)}, bf16[4,4,4224]{2,1,0:T(4,128)(2,1)S(1)}, u32[]{:S(2)}, u32[]{:S(2)}) collective-permute-start(bf16[4,4,4224]{2,1,0:T(4,128)(2,1)S(1)} %stack_blocks.1.refs_0_), channel_id=1, source_target_pairs={{0,18},{1,19},{2,16},{3,17},{4,22},{5,23},{6,20},{7,21},{8,26},{9,... | collective-permute-start | bytes 405512 | tf_op jit(solution)/shard_map/ppermute | solution.py:22
  13.3 0.5 %collective-permute-start.5 = (bf16[4,4,4224]{2,1,0:T(4,128)(2,1)S(1)}, bf16[4,4,4224]{2,1,0:T(4,128)(2,1)S(1)}, u32[]{:S(2)}, u32[]{:S(2)}) collective-permute-start(bf16[4,4,4224]{2,1,0:T(4,128)(2,1)S(1)} %stack_blocks.1.refs_0_), channel_id=1, source_target_pairs={{0,16},{1,17},{2,18},{3,19},{4,20},{5,21},{6,22},{7,23},{8,24},{9,... | collective-permute-start | bytes 405512 | tf_op jit(solution)/shard_map/ppermute | solution.py:22
  13.9 0.5 %collective-permute-start.4 = (bf16[4,4,4224]{2,1,0:T(4,128)(2,1)S(1)}, bf16[4,4,4224]{2,1,0:T(4,128)(2,1)S(1)}, u32[]{:S(2)}, u32[]{:S(2)}) collective-permute-start(bf16[4,4,4224]{2,1,0:T(4,128)(2,1)S(1)} %stack_blocks.1.refs_0_), channel_id=1, source_target_pairs={{0,2},{1,3},{2,0},{3,1},{4,6},{5,7},{6,4},{7,5},{8,10},{9,11},{10,... | collective-permute-start | bytes 405512 | tf_op jit(solution)/shard_map/ppermute | solution.py:22
  14.4 2.8 %collective-permute-done.3.refs_1_ = bf16[4,4,4224]{2,1,0:T(4,128)(2,1)S(1)} collective-permute-done((bf16[4,4,4224]{2,1,0:T(4,128)(2,1)S(1)}, bf16[4,4,4224]{2,1,0:T(4,128)(2,1)S(1)}, u32[]{:S(2)}, u32[]{:S(2)}) %collective-permute-start.3) | collective-permute-done | bytes 135200 | tf_op jit(solution)/shard_map/ppermute | solution.py:22
  17.2 0.1 join_rows.3
  17.3 0.1 collective-permute-start.6
  17.4 1.3 %collective-permute-done.5.refs_0_ = bf16[4,4,4224]{2,1,0:T(4,128)(2,1)S(1)} collective-permute-done((bf16[4,4,4224]{2,1,0:T(4,128)(2,1)S(1)}, bf16[4,4,4224]{2,1,0:T(4,128)(2,1)S(1)}, u32[]{:S(2)}, u32[]{:S(2)}) %collective-permute-start.5) | collective-permute-done | bytes 135200 | tf_op jit(solution)/shard_map/ppermute | solution.py:22
  18.7 0.1 collective-permute-start.8
  18.8 0.1 collective-permute-done.4.refs_0_
  18.9 0.4 collective-permute-start.7
  19.5 0.9 %collective-permute-done.7 = bf16[16,4224]{1,0:T(8,128)(2,1)S(1)} collective-permute-done((bf16[16,4224]{1,0:T(8,128)(2,1)S(1)}, bf16[16,4224]{1,0:T(8,128)(2,1)S(1)}, u32[]{:S(2)}, u32[]{:S(2)}) %collective-permute-start.7) | collective-permute-done | bytes 135200 | tf_op jit(solution)/shard_map/ppermute | solution.py:22
  20.4 0.0 slice-start
  20.5 1.1 %expand_rows.3.refs_0_ = bf16[128,384]{1,0:T(8,128)(2,1)S(1)} custom-call(bf16[128,4224]{1,0:T(8,128)(2,1)S(1)} %slice_dynamic-update-slice_fusion.rows_ref.refs_3_, bf16[4096,1024]{1,0:T(8,128)(2,1)S(1)} %bitcast.10, bf16[4096,1024]{1,0:T(8,128)(2,1)S(1)} %bitcast.13), custom_call_target="tpu_custom_call" | custom-call | bytes 49152 | tf_op jit(solution)/shard_map/expand_rows/pallas_call | solution.py:131
  21.6 0.0 slice-start.1
  21.6 1.6 %collective-permute-start.11 = (bf16[128,384]{1,0:T(8,128)(2,1)S(1)}, bf16[128,384]{1,0:T(8,128)(2,1)S(1)}, u32[]{:S(2)}, u32[]{:S(2)}) collective-permute-start(bf16[128,384]{1,0:T(8,128)(2,1)S(1)} %expand_rows.3.refs_0_), channel_id=1, source_target_pairs={{0,16},{1,17},{2,18},{3,19},{4,20},{5,21},{6,22},{7,23},{8,24},{9,... | collective-permute-start | bytes 294920 | tf_op jit(solution)/shard_map/ppermute | solution.py:22
  23.1 1.0 %expand_rows.4.refs_1_ = bf16[128,384]{1,0:T(8,128)(2,1)S(1)} custom-call(bf16[128,4224]{1,0:T(8,128)(2,1)S(1)} %slice_dynamic-update-slice_fusion.rows_ref.refs_3_, bf16[4096,1024]{1,0:T(8,128)(2,1)S(1)} %bitcast.11, bf16[4096,1024]{1,0:T(8,128)(2,1)S(1)} %bitcast.14), custom_call_target="tpu_custom_call" | custom-call | bytes 49152 | tf_op jit(solution)/shard_map/expand_rows/pallas_call | solution.py:131
  24.2 0.6 %collective-permute-start.10 = (bf16[128,384]{1,0:T(8,128)(2,1)S(1)}, bf16[128,384]{1,0:T(8,128)(2,1)S(1)}, u32[]{:S(2)}, u32[]{:S(2)}) collective-permute-start(bf16[128,384]{1,0:T(8,128)(2,1)S(1)} %expand_rows.4.refs_1_), channel_id=1, source_target_pairs={{0,16},{1,17},{2,18},{3,19},{4,20},{5,21},{6,22},{7,23},{8,24},{9,... | collective-permute-start | bytes 294920 | tf_op jit(solution)/shard_map/ppermute | solution.py:22
  24.8 0.8 %expand_rows.5.refs_2_ = bf16[128,256]{1,0:T(8,128)(2,1)S(1)} custom-call(bf16[128,4224]{1,0:T(8,128)(2,1)S(1)} %slice_dynamic-update-slice_fusion.rows_ref.refs_3_, bf16[4096,1024]{1,0:T(8,128)(2,1)S(1)} %bitcast.12, bf16[4096,1024]{1,0:T(8,128)(2,1)S(1)} %bitcast.15), custom_call_target="tpu_custom_call" | custom-call | bytes 32768 | tf_op jit(solution)/shard_map/expand_rows/pallas_call | solution.py:131
  25.6 1.5 %collective-permute-start.9 = (bf16[128,256]{1,0:T(8,128)(2,1)S(1)}, bf16[128,256]{1,0:T(8,128)(2,1)S(1)}, u32[]{:S(2)}, u32[]{:S(2)}) collective-permute-start(bf16[128,256]{1,0:T(8,128)(2,1)S(1)} %expand_rows.5.refs_2_), channel_id=1, source_target_pairs={{0,16},{1,17},{2,18},{3,19},{4,20},{5,21},{6,22},{7,23},{8,24},{9,... | collective-permute-start | bytes 196616 | tf_op jit(solution)/shard_map/ppermute | solution.py:22
  27.1 0.7 %contract_hidden.5.refs_2_ = f32[128,2048]{1,0:T(8,128)S(1)} custom-call(bf16[128,384]{1,0:T(8,128)(2,1)S(1)} %expand_rows.3.refs_0_, bf16[128,384]{1,0:T(8,128)(2,1)S(1)} %expand_rows.4.refs_1_, bf16[128,256]{1,0:T(8,128)(2,1)S(1)} %expand_rows.5.refs_2_, bf16[2048,2048]{1,0:T(8,128)(2,1)S(1)} %bitcast.5), custom_call_target="tpu_custom_call" | custom-call | bytes 262144 | tf_op jit(solution)/shard_map/contract_hidden/pallas_call | solution.py:192
  27.9 0.5 contract_hidden.6.refs_2_
  28.4 1.4 %collective-permute-done.10.refs_0_ = bf16[128,384]{1,0:T(8,128)(2,1)S(1)} collective-permute-done((bf16[128,384]{1,0:T(8,128)(2,1)S(1)}, bf16[128,384]{1,0:T(8,128)(2,1)S(1)}, u32[]{:S(2)}, u32[]{:S(2)}) %collective-permute-start.10) | collective-permute-done | bytes 98336 | tf_op jit(solution)/shard_map/ppermute | solution.py:22
  29.8 0.4 contract_hidden.7.refs_2_
  30.2 0.2 collective-permute-done.9.refs_0_
  30.5 0.3 contract_hidden.9
  30.8 0.1 collective-permute-start.12
  30.8 0.3 contract_hidden.8.refs_0_
  31.2 1.2 %collective-permute-done.12.refs_1_ = bf16[64,2048]{1,0:T(8,128)(2,1)S(1)} collective-permute-done((bf16[64,2048]{1,0:T(8,128)(2,1)S(1)}, bf16[64,2048]{1,0:T(8,128)(2,1)S(1)}, u32[]{:S(2)}, u32[]{:S(2)}) %collective-permute-start.12) | collective-permute-done | bytes 262176 | tf_op jit(solution)/shard_map/ppermute | solution.py:22
  32.4 0.1 sum_stage.3
  32.5 0.6 %collective-permute-start.13 = (bf16[2,4,2048]{2,1,0:T(4,128)(2,1)S(1)}, bf16[2,4,2048]{2,1,0:T(4,128)(2,1)S(1)}, u32[]{:S(2)}, u32[]{:S(2)}) collective-permute-start(bf16[2,4,2048]{2,1,0:T(4,128)(2,1)S(1)} %get-tuple-element.34), channel_id=1, source_target_pairs={{0,6},{1,7},{2,4},{3,5},{4,2},{5,3},{6,0},{7,1},{8,14},{9,15},{10,... | collective-permute-start | bytes 98312 | tf_op jit(solution)/shard_map/ppermute | solution.py:22
  33.1 1.9 %collective-permute-start.14 = (bf16[2,4,2048]{2,1,0:T(4,128)(2,1)S(1)}, bf16[2,4,2048]{2,1,0:T(4,128)(2,1)S(1)}, u32[]{:S(2)}, u32[]{:S(2)}) collective-permute-start(bf16[2,4,2048]{2,1,0:T(4,128)(2,1)S(1)} %get-tuple-element.35), channel_id=1, source_target_pairs={{0,4},{1,5},{2,6},{3,7},{4,0},{5,1},{6,2},{7,3},{8,12},{9,13},{10,... | collective-permute-start | bytes 98312 | tf_op jit(solution)/shard_map/ppermute | solution.py:22
  35.0 1.0 %collective-permute-start.15 = (bf16[2,4,2048]{2,1,0:T(4,128)(2,1)S(1)}, bf16[2,4,2048]{2,1,0:T(4,128)(2,1)S(1)}, u32[]{:S(2)}, u32[]{:S(2)}) collective-permute-start(bf16[2,4,2048]{2,1,0:T(4,128)(2,1)S(1)} %get-tuple-element.36), channel_id=1, source_target_pairs={{0,2},{1,3},{2,0},{3,1},{4,6},{5,7},{6,4},{7,5},{8,10},{9,11},{10,... | collective-permute-start | bytes 98312 | tf_op jit(solution)/shard_map/ppermute | solution.py:22
  36.0 0.6 %collective-permute-start.18 = (bf16[2,4,2048]{2,1,0:T(4,128)(2,1)S(1)}, bf16[2,4,2048]{2,1,0:T(4,128)(2,1)S(1)}, u32[]{:S(2)}, u32[]{:S(2)}) collective-permute-start(bf16[2,4,2048]{2,1,0:T(4,128)(2,1)S(1)} %get-tuple-element.40), channel_id=1, source_target_pairs={{0,6},{1,7},{2,4},{3,5},{4,2},{5,3},{6,0},{7,1},{8,14},{9,15},{10,... | collective-permute-start | bytes 98312 | tf_op jit(solution)/shard_map/ppermute | solution.py:22
  36.6 1.9 %collective-permute-start.19 = (bf16[2,4,2048]{2,1,0:T(4,128)(2,1)S(1)}, bf16[2,4,2048]{2,1,0:T(4,128)(2,1)S(1)}, u32[]{:S(2)}, u32[]{:S(2)}) collective-permute-start(bf16[2,4,2048]{2,1,0:T(4,128)(2,1)S(1)} %get-tuple-element.41), channel_id=1, source_target_pairs={{0,4},{1,5},{2,6},{3,7},{4,0},{5,1},{6,2},{7,3},{8,12},{9,13},{10,... | collective-permute-start | bytes 98312 | tf_op jit(solution)/shard_map/ppermute | solution.py:22
  38.5 1.0 %collective-permute-start.20 = (bf16[2,4,2048]{2,1,0:T(4,128)(2,1)S(1)}, bf16[2,4,2048]{2,1,0:T(4,128)(2,1)S(1)}, u32[]{:S(2)}, u32[]{:S(2)}) collective-permute-start(bf16[2,4,2048]{2,1,0:T(4,128)(2,1)S(1)} %get-tuple-element.42), channel_id=1, source_target_pairs={{0,2},{1,3},{2,0},{3,1},{4,6},{5,7},{6,4},{7,5},{8,10},{9,11},{10,... | collective-permute-start | bytes 98312 | tf_op jit(solution)/shard_map/ppermute | solution.py:22
  39.6 2.8 %collective-permute-start.16 = (bf16[1,4,2048]{2,1,0:T(4,128)(2,1)S(1)}, bf16[1,4,2048]{2,1,0:T(4,128)(2,1)S(1)}, u32[]{:S(2)}, u32[]{:S(2)}) collective-permute-start(bf16[1,4,2048]{2,1,0:T(4,128)(2,1)S(1)} %get-tuple-element.37), channel_id=1, source_target_pairs={{0,24},{1,25},{2,26},{3,27},{4,28},{5,29},{6,30},{7,31},{8,16},{9,... | collective-permute-start | bytes 49160 | tf_op jit(solution)/shard_map/ppermute | solution.py:22
  42.3 0.9 %collective-permute-start.17 = (bf16[1,4,2048]{2,1,0:T(4,128)(2,1)S(1)}, bf16[1,4,2048]{2,1,0:T(4,128)(2,1)S(1)}, u32[]{:S(2)}, u32[]{:S(2)}) collective-permute-start(bf16[1,4,2048]{2,1,0:T(4,128)(2,1)S(1)} %get-tuple-element.38), channel_id=1, source_target_pairs={{0,8},{1,9},{2,10},{3,11},{4,12},{5,13},{6,14},{7,15},{8,0},{9,1},... | collective-permute-start | bytes 49160 | tf_op jit(solution)/shard_map/ppermute | solution.py:22
  43.3 0.9 %collective-permute-start.21 = (bf16[1,4,2048]{2,1,0:T(4,128)(2,1)S(1)}, bf16[1,4,2048]{2,1,0:T(4,128)(2,1)S(1)}, u32[]{:S(2)}, u32[]{:S(2)}) collective-permute-start(bf16[1,4,2048]{2,1,0:T(4,128)(2,1)S(1)} %get-tuple-element.44), channel_id=1, source_target_pairs={{0,16},{1,17},{2,18},{3,19},{4,20},{5,21},{6,22},{7,23},{8,24},{9,... | collective-permute-start | bytes 49160 | tf_op jit(solution)/shard_map/ppermute | solution.py:22
  44.1 1.0 %collective-permute-done.16.refs_0_ = bf16[1,4,2048]{2,1,0:T(4,128)(2,1)S(1)} collective-permute-done((bf16[1,4,2048]{2,1,0:T(4,128)(2,1)S(1)}, bf16[1,4,2048]{2,1,0:T(4,128)(2,1)S(1)}, u32[]{:S(2)}, u32[]{:S(2)}) %collective-permute-start.16) | collective-permute-done | bytes 16416 | tf_op jit(solution)/shard_map/ppermute | solution.py:22
  45.2 1.8 %collective-permute-done.17.refs_1_ = bf16[1,4,2048]{2,1,0:T(4,128)(2,1)S(1)} collective-permute-done((bf16[1,4,2048]{2,1,0:T(4,128)(2,1)S(1)}, bf16[1,4,2048]{2,1,0:T(4,128)(2,1)S(1)}, u32[]{:S(2)}, u32[]{:S(2)}) %collective-permute-start.17) | collective-permute-done | bytes 16416 | tf_op jit(solution)/shard_map/ppermute | solution.py:22
  47.0 0.1 collective-permute-done.21.refs_3_
  47.1 0.6 %finish.1 = bf16[4,4096]{1,0:T(4,128)(2,1)} custom-call(bf16[1,4,2048]{2,1,0:T(4,128)(2,1)S(1)} %collective-permute-done.16.refs_0_, bf16[1,4,2048]{2,1,0:T(4,128)(2,1)S(1)} %collective-permute-done.17.refs_1_, f32[1,4,2048]{2,1,0:T(4,128)S(1)} %get-tuple-element.43.refs_2_, bf16[1,4,2048]{2,1,0:T(4,128)(2,1)S(1)} %collective-permute-done.21.refs_3_), custom_call_target="tpu_custom_call" | custom-call | tf_op jit(solution)/shard_map/finish/pallas_call | solution.py:247
  (30 shorter events, 0.3 us)
Async XLA Ops:
  0.9 7.0 %collective-permute-start.2 = (bf16[4,4224]{1,0:T(4,128)(2,1)S(1)}, bf16[4,4224]{1,0:T(4,128)(2,1)S(1)}, u32[]{:S(2)}, u32[]{:S(2)}) collective-permute-start(bf16[4,4224]{1,0:T(4,128)(2,1)S(1)} %pack_block.1.refs_0_), channel_id=1, source_target_pairs={{0,12},{1,13},{2,14},{3,15},{4,8},{5,9},{6,10},{7,11},{8,4},{9,5},... | collective-permute-start | bytes 101384 | tf_op jit(solution)/shard_map/ppermute | solution.py:22
  6.0 4.8 %collective-permute-start.1 = (bf16[4,4224]{1,0:T(4,128)(2,1)S(1)}, bf16[4,4224]{1,0:T(4,128)(2,1)S(1)}, u32[]{:S(2)}, u32[]{:S(2)}) collective-permute-start(bf16[4,4224]{1,0:T(4,128)(2,1)S(1)} %pack_block.1.refs_0_), channel_id=1, source_target_pairs={{0,8},{1,9},{2,10},{3,11},{4,12},{5,13},{6,14},{7,15},{8,0},{9,1},... | collective-permute-start | bytes 101384 | tf_op jit(solution)/shard_map/ppermute | solution.py:22
  6.0 4.8 %collective-permute-start = (bf16[4,4224]{1,0:T(4,128)(2,1)S(1)}, bf16[4,4224]{1,0:T(4,128)(2,1)S(1)}, u32[]{:S(2)}, u32[]{:S(2)}) collective-permute-start(bf16[4,4224]{1,0:T(4,128)(2,1)S(1)} %pack_block.1.refs_0_), channel_id=1, source_target_pairs={{0,4},{1,5},{2,6},{3,7},{4,0},{5,1},{6,2},{7,3},{8,12},{9,13},{10,... | collective-permute-start | bytes 101384 | tf_op jit(solution)/shard_map/ppermute | solution.py:22
  10.8 9.6 %copy-start = (bf16[1,4096,1024]{2,1,0:T(8,128)(2,1)S(1)}, bf16[1,4096,1024]{2,1,0:T(8,128)(2,1)}, u32[]{:S(2)}) copy-start(bf16[1,4096,1024]{2,1,0:T(8,128)(2,1)} %param.9) | copy-start | bytes 25165828
  10.8 9.6 %copy-start.1 = (bf16[1,4096,1024]{2,1,0:T(8,128)(2,1)S(1)}, bf16[1,4096,1024]{2,1,0:T(8,128)(2,1)}, u32[]{:S(2)}) copy-start(bf16[1,4096,1024]{2,1,0:T(8,128)(2,1)} %param.10) | copy-start | bytes 25165828
  10.8 6.4 %collective-permute-start.3 = (bf16[4,4,4224]{2,1,0:T(4,128)(2,1)S(1)}, bf16[4,4,4224]{2,1,0:T(4,128)(2,1)S(1)}, u32[]{:S(2)}, u32[]{:S(2)}) collective-permute-start(bf16[4,4,4224]{2,1,0:T(4,128)(2,1)S(1)} %stack_blocks.1.refs_0_), channel_id=1, source_target_pairs={{0,18},{1,19},{2,16},{3,17},{4,22},{5,23},{6,20},{7,21},{8,26},{9,... | collective-permute-start | bytes 405512 | tf_op jit(solution)/shard_map/ppermute | solution.py:22
  13.3 5.3 %collective-permute-start.5 = (bf16[4,4,4224]{2,1,0:T(4,128)(2,1)S(1)}, bf16[4,4,4224]{2,1,0:T(4,128)(2,1)S(1)}, u32[]{:S(2)}, u32[]{:S(2)}) collective-permute-start(bf16[4,4,4224]{2,1,0:T(4,128)(2,1)S(1)} %stack_blocks.1.refs_0_), channel_id=1, source_target_pairs={{0,16},{1,17},{2,18},{3,19},{4,20},{5,21},{6,22},{7,23},{8,24},{9,... | collective-permute-start | bytes 405512 | tf_op jit(solution)/shard_map/ppermute | solution.py:22
  13.9 5.0 %collective-permute-start.4 = (bf16[4,4,4224]{2,1,0:T(4,128)(2,1)S(1)}, bf16[4,4,4224]{2,1,0:T(4,128)(2,1)S(1)}, u32[]{:S(2)}, u32[]{:S(2)}) collective-permute-start(bf16[4,4,4224]{2,1,0:T(4,128)(2,1)S(1)} %stack_blocks.1.refs_0_), channel_id=1, source_target_pairs={{0,2},{1,3},{2,0},{3,1},{4,6},{5,7},{6,4},{7,5},{8,10},{9,11},{10,... | collective-permute-start | bytes 405512 | tf_op jit(solution)/shard_map/ppermute | solution.py:22
  17.3 2.1 %collective-permute-start.6 = (bf16[32,4224]{1,0:T(8,128)(2,1)S(1)}, bf16[32,4224]{1,0:T(8,128)(2,1)S(1)}, u32[]{:S(2)}, u32[]{:S(2)}) collective-permute-start(bf16[32,4224]{1,0:T(8,128)(2,1)S(1)} %join_rows.3), channel_id=1, source_target_pairs={{0,1},{1,0},{2,3},{3,2},{4,5},{5,4},{6,7},{7,6},{8,9},{9,8},{10,11... | collective-permute-start | bytes 811016 | tf_op jit(solution)/shard_map/ppermute | solution.py:22
  18.7 1.7 %collective-permute-start.8 = (bf16[16,4224]{1,0:T(8,128)(2,1)S(1)}, bf16[16,4224]{1,0:T(8,128)(2,1)S(1)}, u32[]{:S(2)}, u32[]{:S(2)}) collective-permute-start(bf16[16,4224]{1,0:T(8,128)(2,1)S(1)} %join_rows.5), channel_id=1, source_target_pairs={{0,1},{1,0},{2,3},{3,2},{4,5},{5,4},{6,7},{7,6},{8,9},{9,8},{10,11... | collective-permute-start | bytes 405512 | tf_op jit(solution)/shard_map/ppermute | solution.py:22
  18.9 1.4 %collective-permute-start.7 = (bf16[16,4224]{1,0:T(8,128)(2,1)S(1)}, bf16[16,4224]{1,0:T(8,128)(2,1)S(1)}, u32[]{:S(2)}, u32[]{:S(2)}) collective-permute-start(bf16[16,4224]{1,0:T(8,128)(2,1)S(1)} %join_rows.4), channel_id=1, source_target_pairs={{0,1},{1,0},{2,3},{3,2},{4,5},{5,4},{6,7},{7,6},{8,9},{9,8},{10,11... | collective-permute-start | bytes 405512 | tf_op jit(solution)/shard_map/ppermute | solution.py:22
  20.4 6.7 %slice-start = ((s8[8388608]{0:T(1024)(128)(4,1)}), s8[4194304]{0:T(1024)(128)(4,1)S(1)}, s32[]{:S(2)}) async-start(s8[8388608]{0:T(1024)(128)(4,1)} %bitcast.3), calls=%async_computation | async-start | bytes 8388608
  21.6 5.6 %slice-start.1 = ((s8[8388608]{0:T(1024)(128)(4,1)}), s8[4194304]{0:T(1024)(128)(4,1)S(1)}, s32[]{:S(2)}) async-start(s8[8388608]{0:T(1024)(128)(4,1)} %bitcast.3), calls=%async_computation.1 | async-start | bytes 8388608
  21.6 6.3 %collective-permute-start.11 = (bf16[128,384]{1,0:T(8,128)(2,1)S(1)}, bf16[128,384]{1,0:T(8,128)(2,1)S(1)}, u32[]{:S(2)}, u32[]{:S(2)}) collective-permute-start(bf16[128,384]{1,0:T(8,128)(2,1)S(1)} %expand_rows.3.refs_0_), channel_id=1, source_target_pairs={{0,16},{1,17},{2,18},{3,19},{4,20},{5,21},{6,22},{7,23},{8,24},{9,... | collective-permute-start | bytes 294920 | tf_op jit(solution)/shard_map/ppermute | solution.py:22
  24.2 5.6 %collective-permute-start.10 = (bf16[128,384]{1,0:T(8,128)(2,1)S(1)}, bf16[128,384]{1,0:T(8,128)(2,1)S(1)}, u32[]{:S(2)}, u32[]{:S(2)}) collective-permute-start(bf16[128,384]{1,0:T(8,128)(2,1)S(1)} %expand_rows.4.refs_1_), channel_id=1, source_target_pairs={{0,16},{1,17},{2,18},{3,19},{4,20},{5,21},{6,22},{7,23},{8,24},{9,... | collective-permute-start | bytes 294920 | tf_op jit(solution)/shard_map/ppermute | solution.py:22
  25.6 4.8 %collective-permute-start.9 = (bf16[128,256]{1,0:T(8,128)(2,1)S(1)}, bf16[128,256]{1,0:T(8,128)(2,1)S(1)}, u32[]{:S(2)}, u32[]{:S(2)}) collective-permute-start(bf16[128,256]{1,0:T(8,128)(2,1)S(1)} %expand_rows.5.refs_2_), channel_id=1, source_target_pairs={{0,16},{1,17},{2,18},{3,19},{4,20},{5,21},{6,22},{7,23},{8,24},{9,... | collective-permute-start | bytes 196616 | tf_op jit(solution)/shard_map/ppermute | solution.py:22
  30.8 1.6 %collective-permute-start.12 = (bf16[64,2048]{1,0:T(8,128)(2,1)S(1)}, bf16[64,2048]{1,0:T(8,128)(2,1)S(1)}, u32[]{:S(2)}, u32[]{:S(2)}) collective-permute-start(bf16[64,2048]{1,0:T(8,128)(2,1)S(1)} %contract_hidden.9), channel_id=1, source_target_pairs={{0,1},{1,0},{2,3},{3,2},{4,5},{5,4},{6,7},{7,6},{8,9},{9,8},{10,11... | collective-permute-start | bytes 786440 | tf_op jit(solution)/shard_map/ppermute | solution.py:22
  32.5 6.0 %collective-permute-start.13 = (bf16[2,4,2048]{2,1,0:T(4,128)(2,1)S(1)}, bf16[2,4,2048]{2,1,0:T(4,128)(2,1)S(1)}, u32[]{:S(2)}, u32[]{:S(2)}) collective-permute-start(bf16[2,4,2048]{2,1,0:T(4,128)(2,1)S(1)} %get-tuple-element.34), channel_id=1, source_target_pairs={{0,6},{1,7},{2,4},{3,5},{4,2},{5,3},{6,0},{7,1},{8,14},{9,15},{10,... | collective-permute-start | bytes 98312 | tf_op jit(solution)/shard_map/ppermute | solution.py:22
  33.1 6.4 %collective-permute-start.14 = (bf16[2,4,2048]{2,1,0:T(4,128)(2,1)S(1)}, bf16[2,4,2048]{2,1,0:T(4,128)(2,1)S(1)}, u32[]{:S(2)}, u32[]{:S(2)}) collective-permute-start(bf16[2,4,2048]{2,1,0:T(4,128)(2,1)S(1)} %get-tuple-element.35), channel_id=1, source_target_pairs={{0,4},{1,5},{2,6},{3,7},{4,0},{5,1},{6,2},{7,3},{8,12},{9,13},{10,... | collective-permute-start | bytes 98312 | tf_op jit(solution)/shard_map/ppermute | solution.py:22
  35.0 4.5 %collective-permute-start.15 = (bf16[2,4,2048]{2,1,0:T(4,128)(2,1)S(1)}, bf16[2,4,2048]{2,1,0:T(4,128)(2,1)S(1)}, u32[]{:S(2)}, u32[]{:S(2)}) collective-permute-start(bf16[2,4,2048]{2,1,0:T(4,128)(2,1)S(1)} %get-tuple-element.36), channel_id=1, source_target_pairs={{0,2},{1,3},{2,0},{3,1},{4,6},{5,7},{6,4},{7,5},{8,10},{9,11},{10,... | collective-permute-start | bytes 98312 | tf_op jit(solution)/shard_map/ppermute | solution.py:22
  36.0 7.2 %collective-permute-start.18 = (bf16[2,4,2048]{2,1,0:T(4,128)(2,1)S(1)}, bf16[2,4,2048]{2,1,0:T(4,128)(2,1)S(1)}, u32[]{:S(2)}, u32[]{:S(2)}) collective-permute-start(bf16[2,4,2048]{2,1,0:T(4,128)(2,1)S(1)} %get-tuple-element.40), channel_id=1, source_target_pairs={{0,6},{1,7},{2,4},{3,5},{4,2},{5,3},{6,0},{7,1},{8,14},{9,15},{10,... | collective-permute-start | bytes 98312 | tf_op jit(solution)/shard_map/ppermute | solution.py:22
  36.6 6.6 %collective-permute-start.19 = (bf16[2,4,2048]{2,1,0:T(4,128)(2,1)S(1)}, bf16[2,4,2048]{2,1,0:T(4,128)(2,1)S(1)}, u32[]{:S(2)}, u32[]{:S(2)}) collective-permute-start(bf16[2,4,2048]{2,1,0:T(4,128)(2,1)S(1)} %get-tuple-element.41), channel_id=1, source_target_pairs={{0,4},{1,5},{2,6},{3,7},{4,0},{5,1},{6,2},{7,3},{8,12},{9,13},{10,... | collective-permute-start | bytes 98312 | tf_op jit(solution)/shard_map/ppermute | solution.py:22
  38.5 4.7 %collective-permute-start.20 = (bf16[2,4,2048]{2,1,0:T(4,128)(2,1)S(1)}, bf16[2,4,2048]{2,1,0:T(4,128)(2,1)S(1)}, u32[]{:S(2)}, u32[]{:S(2)}) collective-permute-start(bf16[2,4,2048]{2,1,0:T(4,128)(2,1)S(1)} %get-tuple-element.42), channel_id=1, source_target_pairs={{0,2},{1,3},{2,0},{3,1},{4,6},{5,7},{6,4},{7,5},{8,10},{9,11},{10,... | collective-permute-start | bytes 98312 | tf_op jit(solution)/shard_map/ppermute | solution.py:22
  39.6 5.6 %collective-permute-start.16 = (bf16[1,4,2048]{2,1,0:T(4,128)(2,1)S(1)}, bf16[1,4,2048]{2,1,0:T(4,128)(2,1)S(1)}, u32[]{:S(2)}, u32[]{:S(2)}) collective-permute-start(bf16[1,4,2048]{2,1,0:T(4,128)(2,1)S(1)} %get-tuple-element.37), channel_id=1, source_target_pairs={{0,24},{1,25},{2,26},{3,27},{4,28},{5,29},{6,30},{7,31},{8,16},{9,... | collective-permute-start | bytes 49160 | tf_op jit(solution)/shard_map/ppermute | solution.py:22
  42.3 4.6 %collective-permute-start.17 = (bf16[1,4,2048]{2,1,0:T(4,128)(2,1)S(1)}, bf16[1,4,2048]{2,1,0:T(4,128)(2,1)S(1)}, u32[]{:S(2)}, u32[]{:S(2)}) collective-permute-start(bf16[1,4,2048]{2,1,0:T(4,128)(2,1)S(1)} %get-tuple-element.38), channel_id=1, source_target_pairs={{0,8},{1,9},{2,10},{3,11},{4,12},{5,13},{6,14},{7,15},{8,0},{9,1},... | collective-permute-start | bytes 49160 | tf_op jit(solution)/shard_map/ppermute | solution.py:22
  43.3 3.8 %collective-permute-start.21 = (bf16[1,4,2048]{2,1,0:T(4,128)(2,1)S(1)}, bf16[1,4,2048]{2,1,0:T(4,128)(2,1)S(1)}, u32[]{:S(2)}, u32[]{:S(2)}) collective-permute-start(bf16[1,4,2048]{2,1,0:T(4,128)(2,1)S(1)} %get-tuple-element.44), channel_id=1, source_target_pairs={{0,16},{1,17},{2,18},{3,19},{4,20},{5,21},{6,22},{7,23},{8,24},{9,... | collective-permute-start | bytes 49160 | tf_op jit(solution)/shard_map/ppermute | solution.py:22

commit v21 on v19

--- a/solution.py
+++ b/solution.py
@@ -88,7 +88,7 @@
 def join_rows(stacks):
     blocks, tokens, width = stacks[0].shape
     total = len(stacks) * blocks
-    batch = max(1, 16 // tokens)
+    batch = min(total, max(1, 16 // tokens))
 
     def body(*refs):
         for i in range(0, total, batch):
@@ -263,28 +263,36 @@
     units = w_up.shape[2]
     weights = lax.optimization_barrier((block, w_gate[0], w_up[0], w_down[0]))
     block, gate_weights, up_weights, down_weights = weights
+    order = [0] + list(range(high - 1, 0, -1))
+    blocks = [swap(block, 0, 4 * i) if i else block for i in order]
+    units = w_up.shape[2]
+    weights = lax.optimization_barrier((block, w_gate[0], w_up[0], w_down[0]))
+    block, gate_weights, up_weights, down_weights = weights
     near = stack_blocks([block] + [swap(block, 0, 4 * i) for i in range(1, high)])
-    if wide > 1:
-        near = jnp.concatenate([near] + [swap(near, 2 * i, 0) for i in range(1, wide)])
-    over_x, over_y = swap(near, 1, 0), swap(near, 0, 2)
-    first = join_rows([near, swap(near, 1, 2)])
-    pieces = [first, join_rows([over_x]), join_rows([over_y])]
-    size = pieces[1].shape[0]
+    sets = []
+    for part in (blocks[: high // 2], blocks[high // 2 :]):
+        near = stack_blocks(part)
+        if wide > 1:
+            near = jnp.concatenate([near] + [swap(near, 2 * i, 0) for i in range(1, wide)])
+        sets.append((near, swap(near, 0, 2), swap(near, 1, 0), swap(near, 1, 2)))
+    near, over_y, over_x, corner = sets[1]
+    pieces = [join_rows(sets[0]), join_rows([near, corner]), join_rows([over_y, over_x])]
+    size = pieces[0].shape[0] // 4
     rows = []
-    for first, x, y in (pieces, [swap(piece, 0, 1) for piece in pieces]):
-        rows += [first[:size], y, x, first[size:]]
+    for first, outer, inner in (pieces, [swap(piece, 0, 1) for piece in pieces]):
+        rows += [first, outer[:size], inner, outer[size:]]
     rows = jnp.concatenate(rows)
 
     eighth = units // 8
     steps = (3 * eighth, 3 * eighth, 2 * eighth) if eighth % LANES == 0 else (units,)
     starts = [sum(steps[:i]) for i in range(len(steps))]
-    half = rows.shape[0] // 4 if groups == 2 and rows.shape[0] <= BATCH else None
+    half = rows.shape[0] // 8 if groups == 2 and rows.shape[0] <= BATCH else None
 
     def from_group(value, mask):
         value = swap(value, mask, 0)
         if half is not None:
             return value
-        value = value.reshape(2, 2, 2, wide, high * token_count, value.shape[1])
+        value = value.reshape(4, 2, 2, wide, -1, value.shape[1])
         value = jnp.stack([value[:, i ^ (mask & 1)] for i in range(2)], axis=1)
         value = jnp.stack([value[:, :, :, i ^ (mask >> 1)] for i in range(wide)], axis=3)
         return value.reshape(-1, value.shape[-1])
@@ -307,15 +315,17 @@
 
     shape = (token_count, w_down.shape[2])
     rest = [(g, h) for g in range(groups) for h in range(0, high, 2)]
-    slot = lambda g, y, h: (((g & 1) * 2 + y) * wide + (g >> 1)) * high + h
+
+    def slot(g, y, h):
+        which, place = divmod(order.index(h), high // 2)
+        return (((which * 2 + (g & 1)) * 2 + y) * wide + (g >> 1)) * (high // 2) + place
+
     plan = [[slot(g, y, h + z) for g, h in rest] for y, z in ((0, 0), (1, 1), (0, 1), (1, 0))]
     mine, *away = sum_stage([kept, swap(sent, 0, 1)], plan, shape, jnp.bfloat16)
     inputs = [mine] + [swap(value, 0, mask) for value, mask in zip(away, (6, 4, 2))]
-    order = sorted(range(1, len(rest)), key=lambda i: (rest[i][1], rest[i][0]), reverse=True)
-    mine, *away = sum_stage(inputs, [[i] for i in [0] + order], shape, jnp.bfloat16)
-    parts = [
-        (swap(value, rest[i][0], 4 * rest[i][1]), rest[i][0]) for value, i in zip(away, order)
-    ]
+    last = sorted(range(1, len(rest)), key=lambda i: (rest[i][1], rest[i][0]), reverse=True)
+    mine, *away = sum_stage(inputs, [[i] for i in [0] + last], shape, jnp.bfloat16)
+    parts = [(swap(value, rest[i][0], 4 * rest[i][1]), rest[i][0]) for value, i in zip(away, last)]
     return finish(parts + [(mine, 0)], groups, tokens.dtype)
 
 

time: 47.5 us -> 48.5 us (1.021)
  starting transfers between devices: 21.7 us -> 25.5 us
  waiting for transfers between devices: 18.4 us -> 15.2 us
    ppermute x19 -> x22, starting transfers between devices: 21.7 us -> 25.5 us  [swap(): return lax.ppermute(value, ('dp',) + EXPERT, pairs)]
    ppermute x19 -> x22, waiting for transfers between devices: 18.4 us -> 15.2 us  [swap(): return lax.ppermute(value, ('dp',) + EXPERT, pairs)]
  transfers between devices with their start and end apart: 19 -> 22, of which waited for: 14 -> 12; matrix products, arithmetic and copies ran while one was open for 0% -> 0% of each run, Pallas kernels for 8% -> 8%
where the time goes in v21:
time: 48.5 us; the launch traced here: 48.3 us
  starting transfers between devices  25.5 us (53%)
  waiting for transfers between devices  15.2 us (31%)
  Pallas kernels  7.18 us (15%)
    ppermute x22, starting transfers between devices, swap(): return lax.ppermute(value, ('dp',) + EXPERT, pairs)  25.5 us
    ppermute x22, waiting for transfers between devices, swap(): return lax.ppermute(value, ('dp',) + EXPERT, pairs)  15.2 us
    pallas_call x3, Pallas kernels, expand_rows(): pl.pallas_call(body, out_shape=jax.ShapeDtypeStruct((count, columns), row...  3.04 us
    pallas_call x5, Pallas kernels, contract_hidden(): pl.pallas_call(body, out_shape=jax.ShapeDtypeStruct((count, width), kind)...  2.31 us
  transfers between devices with their start and end apart: 22, of which 12 were waited for; matrix products, arithmetic and copies ran while one was open for 0% of the time, Pallas kernels for 8%

profile of v21, /device:TPU:0, one launch (start us, length us, event | category | flops | bytes accessed | tf_op | source)
XLA Modules:
  0.0 48.3 jit_solution(13955983117313102495)
XLA Ops:
  0.0 0.9 %pack_block.1.refs_0_ = bf16[4,4224]{1,0:T(4,128)(2,1)S(1)} custom-call(bf16[4,4096]{1,0:T(4,128)(2,1)} %tokens_ref.1, s32[4,8]{1,0:T(4,128)} %ids_ref.1, f32[4,8]{1,0:T(4,128)} %probs_ref.1), custom_call_target="tpu_custom_call" | custom-call | tf_op jit(solution)/shard_map/pack_block/pallas_call | solution.py:62
  0.9 5.1 %collective-permute-start = (bf16[4,4224]{1,0:T(4,128)(2,1)S(1)}, bf16[4,4224]{1,0:T(4,128)(2,1)S(1)}, u32[]{:S(2)}, u32[]{:S(2)}) collective-permute-start(bf16[4,4224]{1,0:T(4,128)(2,1)S(1)} %pack_block.1.refs_0_), channel_id=1, source_target_pairs={{0,12},{1,13},{2,14},{3,15},{4,8},{5,9},{6,10},{7,11},{8,4},{9,5},... | collective-permute-start | bytes 101384 | tf_op jit(solution)/shard_map/ppermute | solution.py:22
  6.0 0.6 %collective-permute-start.4 = (bf16[4,4224]{1,0:T(4,128)(2,1)S(1)}, bf16[4,4224]{1,0:T(4,128)(2,1)S(1)}, u32[]{:S(2)}, u32[]{:S(2)}) collective-permute-start(bf16[4,4224]{1,0:T(4,128)(2,1)S(1)} %pack_block.1.refs_0_), channel_id=1, source_target_pairs={{0,8},{1,9},{2,10},{3,11},{4,12},{5,13},{6,14},{7,15},{8,0},{9,1},... | collective-permute-start | bytes 101384 | tf_op jit(solution)/shard_map/ppermute | solution.py:22
  6.6 1.3 %collective-permute-done.refs_1_ = bf16[4,4224]{1,0:T(4,128)(2,1)S(1)} collective-permute-done((bf16[4,4224]{1,0:T(4,128)(2,1)S(1)}, bf16[4,4224]{1,0:T(4,128)(2,1)S(1)}, u32[]{:S(2)}, u32[]{:S(2)}) %collective-permute-start) | collective-permute-done | bytes 33824 | tf_op jit(solution)/shard_map/ppermute | solution.py:22
  7.9 0.0 slice-start.3
  7.9 0.0 slice-start.5
  7.9 2.7 %collective-permute-start.3 = (bf16[2,4,4224]{2,1,0:T(4,128)(2,1)S(1)}, bf16[2,4,4224]{2,1,0:T(4,128)(2,1)S(1)}, u32[]{:S(2)}, u32[]{:S(2)}) collective-permute-start(bf16[2,4,4224]{2,1,0:T(4,128)(2,1)S(1)} %stack_blocks.2.refs_0_), channel_id=1, source_target_pairs={{0,18},{1,19},{2,16},{3,17},{4,22},{5,23},{6,20},{7,21},{8,26},{9,... | collective-permute-start | bytes 202760 | tf_op jit(solution)/shard_map/ppermute | solution.py:22
  10.7 0.5 %collective-permute-start.2 = (bf16[2,4,4224]{2,1,0:T(4,128)(2,1)S(1)}, bf16[2,4,4224]{2,1,0:T(4,128)(2,1)S(1)}, u32[]{:S(2)}, u32[]{:S(2)}) collective-permute-start(bf16[2,4,4224]{2,1,0:T(4,128)(2,1)S(1)} %stack_blocks.2.refs_0_), channel_id=1, source_target_pairs={{0,16},{1,17},{2,18},{3,19},{4,20},{5,21},{6,22},{7,23},{8,24},{9,... | collective-permute-start | bytes 202760 | tf_op jit(solution)/shard_map/ppermute | solution.py:22
  11.2 0.3 collective-permute-start.1
  11.5 1.8 %collective-permute-start.8 = (bf16[2,4,4224]{2,1,0:T(4,128)(2,1)S(1)}, bf16[2,4,4224]{2,1,0:T(4,128)(2,1)S(1)}, u32[]{:S(2)}, u32[]{:S(2)}) collective-permute-start(bf16[2,4,4224]{2,1,0:T(4,128)(2,1)S(1)} %stack_blocks.3.refs_0_), channel_id=1, source_target_pairs={{0,16},{1,17},{2,18},{3,19},{4,20},{5,21},{6,22},{7,23},{8,24},{9,... | collective-permute-start | bytes 202760 | tf_op jit(solution)/shard_map/ppermute | solution.py:22
  13.3 1.5 %collective-permute-start.7 = (bf16[2,4,4224]{2,1,0:T(4,128)(2,1)S(1)}, bf16[2,4,4224]{2,1,0:T(4,128)(2,1)S(1)}, u32[]{:S(2)}, u32[]{:S(2)}) collective-permute-start(bf16[2,4,4224]{2,1,0:T(4,128)(2,1)S(1)} %stack_blocks.3.refs_0_), channel_id=1, source_target_pairs={{0,2},{1,3},{2,0},{3,1},{4,6},{5,7},{6,4},{7,5},{8,10},{9,11},{10,... | collective-permute-start | bytes 202760 | tf_op jit(solution)/shard_map/ppermute | solution.py:22
  14.8 1.4 %collective-permute-start.6 = (bf16[2,4,4224]{2,1,0:T(4,128)(2,1)S(1)}, bf16[2,4,4224]{2,1,0:T(4,128)(2,1)S(1)}, u32[]{:S(2)}, u32[]{:S(2)}) collective-permute-start(bf16[2,4,4224]{2,1,0:T(4,128)(2,1)S(1)} %stack_blocks.3.refs_0_), channel_id=1, source_target_pairs={{0,18},{1,19},{2,16},{3,17},{4,22},{5,23},{6,20},{7,21},{8,26},{9,... | collective-permute-start | bytes 202760 | tf_op jit(solution)/shard_map/ppermute | solution.py:22
  16.2 0.1 join_rows.3
  16.3 0.1 collective-permute-start.9
  16.4 3.6 %collective-permute-done.6.refs_1_ = bf16[2,4,4224]{2,1,0:T(4,128)(2,1)S(1)} collective-permute-done((bf16[2,4,4224]{2,1,0:T(4,128)(2,1)S(1)}, bf16[2,4,4224]{2,1,0:T(4,128)(2,1)S(1)}, u32[]{:S(2)}, u32[]{:S(2)}) %collective-permute-start.6) | collective-permute-done | bytes 67616 | tf_op jit(solution)/shard_map/ppermute | solution.py:22
  20.0 0.1 collective-permute-start.10
  20.2 0.5 %collective-permute-start.11 = (bf16[16,4224]{1,0:T(8,128)(2,1)S(1)}, bf16[16,4224]{1,0:T(8,128)(2,1)S(1)}, u32[]{:S(2)}, u32[]{:S(2)}) collective-permute-start(bf16[16,4224]{1,0:T(8,128)(2,1)S(1)} %join_rows.5), channel_id=1, source_target_pairs={{0,1},{1,0},{2,3},{3,2},{4,5},{5,4},{6,7},{7,6},{8,9},{9,8},{10,11... | collective-permute-start | bytes 405512 | tf_op jit(solution)/shard_map/ppermute | solution.py:22
  20.8 0.6 %collective-permute-done.10 = bf16[16,4224]{1,0:T(8,128)(2,1)S(1)} collective-permute-done((bf16[16,4224]{1,0:T(8,128)(2,1)S(1)}, bf16[16,4224]{1,0:T(8,128)(2,1)S(1)}, u32[]{:S(2)}, u32[]{:S(2)}) %collective-permute-start.10) | collective-permute-done | bytes 135200 | tf_op jit(solution)/shard_map/ppermute | solution.py:22
  21.5 0.2 collective-permute-done.11
  21.8 1.1 %expand_rows.3.refs_0_ = bf16[128,384]{1,0:T(8,128)(2,1)S(1)} custom-call(bf16[128,4224]{1,0:T(8,128)(2,1)S(1)} %slice_dynamic-update-slice_fusion.rows_ref.refs_3_, bf16[4096,1024]{1,0:T(8,128)(2,1)S(1)} %bitcast.12, bf16[4096,1024]{1,0:T(8,128)(2,1)S(1)} %bitcast.17), custom_call_target="tpu_custom_call" | custom-call | bytes 49152 | tf_op jit(solution)/shard_map/expand_rows/pallas_call | solution.py:131
  22.9 0.0 slice-start.1
  23.0 0.6 %collective-permute-start.14 = (bf16[128,384]{1,0:T(8,128)(2,1)S(1)}, bf16[128,384]{1,0:T(8,128)(2,1)S(1)}, u32[]{:S(2)}, u32[]{:S(2)}) collective-permute-start(bf16[128,384]{1,0:T(8,128)(2,1)S(1)} %expand_rows.3.refs_0_), channel_id=1, source_target_pairs={{0,16},{1,17},{2,18},{3,19},{4,20},{5,21},{6,22},{7,23},{8,24},{9,... | collective-permute-start | bytes 294920 | tf_op jit(solution)/shard_map/ppermute | solution.py:22
  23.6 1.1 %expand_rows.4.refs_1_ = bf16[128,384]{1,0:T(8,128)(2,1)S(1)} custom-call(bf16[128,4224]{1,0:T(8,128)(2,1)S(1)} %slice_dynamic-update-slice_fusion.rows_ref.refs_3_, bf16[4096,1024]{1,0:T(8,128)(2,1)S(1)} %bitcast.13, bf16[4096,1024]{1,0:T(8,128)(2,1)S(1)} %bitcast.18), custom_call_target="tpu_custom_call" | custom-call | bytes 49152 | tf_op jit(solution)/shard_map/expand_rows/pallas_call | solution.py:131
  24.7 1.6 %collective-permute-start.13 = (bf16[128,384]{1,0:T(8,128)(2,1)S(1)}, bf16[128,384]{1,0:T(8,128)(2,1)S(1)}, u32[]{:S(2)}, u32[]{:S(2)}) collective-permute-start(bf16[128,384]{1,0:T(8,128)(2,1)S(1)} %expand_rows.4.refs_1_), channel_id=1, source_target_pairs={{0,16},{1,17},{2,18},{3,19},{4,20},{5,21},{6,22},{7,23},{8,24},{9,... | collective-permute-start | bytes 294920 | tf_op jit(solution)/shard_map/ppermute | solution.py:22
  26.2 0.8 %expand_rows.5.refs_2_ = bf16[128,256]{1,0:T(8,128)(2,1)S(1)} custom-call(bf16[128,4224]{1,0:T(8,128)(2,1)S(1)} %slice_dynamic-update-slice_fusion.rows_ref.refs_3_, bf16[4096,1024]{1,0:T(8,128)(2,1)S(1)} %bitcast.14, bf16[4096,1024]{1,0:T(8,128)(2,1)S(1)} %bitcast.19), custom_call_target="tpu_custom_call" | custom-call | bytes 32768 | tf_op jit(solution)/shard_map/expand_rows/pallas_call | solution.py:131
  27.0 0.6 %collective-permute-start.12 = (bf16[128,256]{1,0:T(8,128)(2,1)S(1)}, bf16[128,256]{1,0:T(8,128)(2,1)S(1)}, u32[]{:S(2)}, u32[]{:S(2)}) collective-permute-start(bf16[128,256]{1,0:T(8,128)(2,1)S(1)} %expand_rows.5.refs_2_), channel_id=1, source_target_pairs={{0,16},{1,17},{2,18},{3,19},{4,20},{5,21},{6,22},{7,23},{8,24},{9,... | collective-permute-start | bytes 196616 | tf_op jit(solution)/shard_map/ppermute | solution.py:22
  27.6 0.7 %contract_hidden.5.refs_2_ = f32[128,2048]{1,0:T(8,128)S(1)} custom-call(bf16[128,384]{1,0:T(8,128)(2,1)S(1)} %expand_rows.3.refs_0_, bf16[128,384]{1,0:T(8,128)(2,1)S(1)} %expand_rows.4.refs_1_, bf16[128,256]{1,0:T(8,128)(2,1)S(1)} %expand_rows.5.refs_2_, bf16[2048,2048]{1,0:T(8,128)(2,1)S(1)} %bitcast.5), custom_call_target="tpu_custom_call" | custom-call | bytes 262144 | tf_op jit(solution)/shard_map/contract_hidden/pallas_call | solution.py:192
  28.4 0.3 collective-permute-done.14.refs_0_
  28.6 0.5 contract_hidden.6.refs_2_
  29.1 1.6 %collective-permute-done.13.refs_0_ = bf16[128,384]{1,0:T(8,128)(2,1)S(1)} collective-permute-done((bf16[128,384]{1,0:T(8,128)(2,1)S(1)}, bf16[128,384]{1,0:T(8,128)(2,1)S(1)}, u32[]{:S(2)}, u32[]{:S(2)}) %collective-permute-start.13) | collective-permute-done | bytes 98336 | tf_op jit(solution)/shard_map/ppermute | solution.py:22
  30.8 0.5 %contract_hidden.7.refs_2_ = f32[128,2048]{1,0:T(8,128)S(1)} custom-call(bf16[128,384]{1,0:T(8,128)(2,1)S(1)} %collective-permute-done.13.refs_0_, bf16[2048,2048]{1,0:T(8,128)(2,1)S(1)} %bitcast.7, f32[128,2048]{1,0:T(8,128)S(1)} %contract_hidden.6.refs_2_), custom_call_target="tpu_custom_call" | custom-call | bytes 262144 | tf_op jit(solution)/shard_map/contract_hidden/pallas_call | solution.py:192
  31.2 0.3 collective-permute-done.12.refs_0_
  31.6 0.3 contract_hidden.9
  31.9 0.1 collective-permute-start.15
  32.0 0.3 contract_hidden.8.refs_0_
  32.3 1.2 %collective-permute-done.15.refs_1_ = bf16[64,2048]{1,0:T(8,128)(2,1)S(1)} collective-permute-done((bf16[64,2048]{1,0:T(8,128)(2,1)S(1)}, bf16[64,2048]{1,0:T(8,128)(2,1)S(1)}, u32[]{:S(2)}, u32[]{:S(2)}) %collective-permute-start.15) | collective-permute-done | bytes 262176 | tf_op jit(solution)/shard_map/ppermute | solution.py:22
  33.5 0.1 sum_stage.2
  33.7 1.1 %collective-permute-start.16 = (bf16[4,4,2048]{2,1,0:T(4,128)(2,1)S(1)}, bf16[4,4,2048]{2,1,0:T(4,128)(2,1)S(1)}, u32[]{:S(2)}, u32[]{:S(2)}) collective-permute-start(bf16[4,4,2048]{2,1,0:T(4,128)(2,1)S(1)} %get-tuple-element.30), channel_id=1, source_target_pairs={{0,6},{1,7},{2,4},{3,5},{4,2},{5,3},{6,0},{7,1},{8,14},{9,15},{10,... | collective-permute-start | bytes 196616 | tf_op jit(solution)/shard_map/ppermute | solution.py:22
  34.7 1.2 %collective-permute-start.17 = (bf16[4,4,2048]{2,1,0:T(4,128)(2,1)S(1)}, bf16[4,4,2048]{2,1,0:T(4,128)(2,1)S(1)}, u32[]{:S(2)}, u32[]{:S(2)}) collective-permute-start(bf16[4,4,2048]{2,1,0:T(4,128)(2,1)S(1)} %get-tuple-element.31), channel_id=1, source_target_pairs={{0,4},{1,5},{2,6},{3,7},{4,0},{5,1},{6,2},{7,3},{8,12},{9,13},{10,... | collective-permute-start | bytes 196616 | tf_op jit(solution)/shard_map/ppermute | solution.py:22
  35.9 1.3 %collective-permute-start.18 = (bf16[4,4,2048]{2,1,0:T(4,128)(2,1)S(1)}, bf16[4,4,2048]{2,1,0:T(4,128)(2,1)S(1)}, u32[]{:S(2)}, u32[]{:S(2)}) collective-permute-start(bf16[4,4,2048]{2,1,0:T(4,128)(2,1)S(1)} %get-tuple-element.32), channel_id=1, source_target_pairs={{0,2},{1,3},{2,0},{3,1},{4,6},{5,7},{6,4},{7,5},{8,10},{9,11},{10,... | collective-permute-start | bytes 196616 | tf_op jit(solution)/shard_map/ppermute | solution.py:22
  37.2 2.3 %collective-permute-done.16.refs_1_ = bf16[4,4,2048]{2,1,0:T(4,128)(2,1)S(1)} collective-permute-done((bf16[4,4,2048]{2,1,0:T(4,128)(2,1)S(1)}, bf16[4,4,2048]{2,1,0:T(4,128)(2,1)S(1)}, u32[]{:S(2)}, u32[]{:S(2)}) %collective-permute-start.16) | collective-permute-done | bytes 65568 | tf_op jit(solution)/shard_map/ppermute | solution.py:22
  39.5 0.7 %collective-permute-done.18.refs_3_ = bf16[4,4,2048]{2,1,0:T(4,128)(2,1)S(1)} collective-permute-done((bf16[4,4,2048]{2,1,0:T(4,128)(2,1)S(1)}, bf16[4,4,2048]{2,1,0:T(4,128)(2,1)S(1)}, u32[]{:S(2)}, u32[]{:S(2)}) %collective-permute-start.18) | collective-permute-done | bytes 65568 | tf_op jit(solution)/shard_map/ppermute | solution.py:22
  40.3 2.7 %collective-permute-start.19 = (bf16[1,4,2048]{2,1,0:T(4,128)(2,1)S(1)}, bf16[1,4,2048]{2,1,0:T(4,128)(2,1)S(1)}, u32[]{:S(2)}, u32[]{:S(2)}) collective-permute-start(bf16[1,4,2048]{2,1,0:T(4,128)(2,1)S(1)} %get-tuple-element.33), channel_id=1, source_target_pairs={{0,24},{1,25},{2,26},{3,27},{4,28},{5,29},{6,30},{7,31},{8,16},{9,... | collective-permute-start | bytes 49160 | tf_op jit(solution)/shard_map/ppermute | solution.py:22
  43.0 0.8 %collective-permute-start.20 = (bf16[1,4,2048]{2,1,0:T(4,128)(2,1)S(1)}, bf16[1,4,2048]{2,1,0:T(4,128)(2,1)S(1)}, u32[]{:S(2)}, u32[]{:S(2)}) collective-permute-start(bf16[1,4,2048]{2,1,0:T(4,128)(2,1)S(1)} %get-tuple-element.34), channel_id=1, source_target_pairs={{0,8},{1,9},{2,10},{3,11},{4,12},{5,13},{6,14},{7,15},{8,0},{9,1},... | collective-permute-start | bytes 49160 | tf_op jit(solution)/shard_map/ppermute | solution.py:22
  43.9 0.9 %collective-permute-start.21 = (bf16[1,4,2048]{2,1,0:T(4,128)(2,1)S(1)}, bf16[1,4,2048]{2,1,0:T(4,128)(2,1)S(1)}, u32[]{:S(2)}, u32[]{:S(2)}) collective-permute-start(bf16[1,4,2048]{2,1,0:T(4,128)(2,1)S(1)} %get-tuple-element.35), channel_id=1, source_target_pairs={{0,16},{1,17},{2,18},{3,19},{4,20},{5,21},{6,22},{7,23},{8,24},{9,... | collective-permute-start | bytes 49160 | tf_op jit(solution)/shard_map/ppermute | solution.py:22
  44.7 1.1 %collective-permute-done.19.refs_0_ = bf16[1,4,2048]{2,1,0:T(4,128)(2,1)S(1)} collective-permute-done((bf16[1,4,2048]{2,1,0:T(4,128)(2,1)S(1)}, bf16[1,4,2048]{2,1,0:T(4,128)(2,1)S(1)}, u32[]{:S(2)}, u32[]{:S(2)}) %collective-permute-start.19) | collective-permute-done | bytes 16416 | tf_op jit(solution)/shard_map/ppermute | solution.py:22
  45.9 1.8 %collective-permute-done.20.refs_1_ = bf16[1,4,2048]{2,1,0:T(4,128)(2,1)S(1)} collective-permute-done((bf16[1,4,2048]{2,1,0:T(4,128)(2,1)S(1)}, bf16[1,4,2048]{2,1,0:T(4,128)(2,1)S(1)}, u32[]{:S(2)}, u32[]{:S(2)}) %collective-permute-start.20) | collective-permute-done | bytes 16416 | tf_op jit(solution)/shard_map/ppermute | solution.py:22
  47.7 0.6 %finish.1 = bf16[4,4096]{1,0:T(4,128)(2,1)} custom-call(bf16[1,4,2048]{2,1,0:T(4,128)(2,1)S(1)} %collective-permute-done.19.refs_0_, bf16[1,4,2048]{2,1,0:T(4,128)(2,1)S(1)} %collective-permute-done.20.refs_1_, bf16[1,4,2048]{2,1,0:T(4,128)(2,1)S(1)} %collective-permute-done.21.refs_2_, f32[1,4,2048]{2,1,0:T(4,128)S(1)} %get-tuple-element.36.refs_3_), custom_call_target="tpu_custom_call" | custom-call | tf_op jit(solution)/shard_map/finish/pallas_call | solution.py:247
  (36 shorter events, 0.3 us)
Async XLA Ops:
  0.9 7.0 %collective-permute-start = (bf16[4,4224]{1,0:T(4,128)(2,1)S(1)}, bf16[4,4224]{1,0:T(4,128)(2,1)S(1)}, u32[]{:S(2)}, u32[]{:S(2)}) collective-permute-start(bf16[4,4224]{1,0:T(4,128)(2,1)S(1)} %pack_block.1.refs_0_), channel_id=1, source_target_pairs={{0,12},{1,13},{2,14},{3,15},{4,8},{5,9},{6,10},{7,11},{8,4},{9,5},... | collective-permute-start | bytes 101384 | tf_op jit(solution)/shard_map/ppermute | solution.py:22
  6.0 5.5 %collective-permute-start.5 = (bf16[4,4224]{1,0:T(4,128)(2,1)S(1)}, bf16[4,4224]{1,0:T(4,128)(2,1)S(1)}, u32[]{:S(2)}, u32[]{:S(2)}) collective-permute-start(bf16[4,4224]{1,0:T(4,128)(2,1)S(1)} %pack_block.1.refs_0_), channel_id=1, source_target_pairs={{0,4},{1,5},{2,6},{3,7},{4,0},{5,1},{6,2},{7,3},{8,12},{9,13},{10,... | collective-permute-start | bytes 101384 | tf_op jit(solution)/shard_map/ppermute | solution.py:22
  6.0 5.5 %collective-permute-start.4 = (bf16[4,4224]{1,0:T(4,128)(2,1)S(1)}, bf16[4,4224]{1,0:T(4,128)(2,1)S(1)}, u32[]{:S(2)}, u32[]{:S(2)}) collective-permute-start(bf16[4,4224]{1,0:T(4,128)(2,1)S(1)} %pack_block.1.refs_0_), channel_id=1, source_target_pairs={{0,8},{1,9},{2,10},{3,11},{4,12},{5,13},{6,14},{7,15},{8,0},{9,1},... | collective-permute-start | bytes 101384 | tf_op jit(solution)/shard_map/ppermute | solution.py:22
  7.9 13.8 %slice-start.2 = ((s8[8388608]{0:T(1024)(128)(4,1)}), s8[4194304]{0:T(1024)(128)(4,1)S(1)}, s32[]{:S(2)}) async-start(s8[8388608]{0:T(1024)(128)(4,1)} %bitcast.10), calls=%async_computation.2 | async-start | bytes 8388608
  7.9 13.9 %slice-start.4 = ((s8[8388608]{0:T(1024)(128)(4,1)}), s8[4194304]{0:T(1024)(128)(4,1)S(1)}, s32[]{:S(2)}) async-start(s8[8388608]{0:T(1024)(128)(4,1)} %bitcast.15), calls=%async_computation.4 | async-start | bytes 8388608
  7.9 13.9 %slice-start.3 = ((s8[8388608]{0:T(1024)(128)(4,1)}), s8[4194304]{0:T(1024)(128)(4,1)S(1)}, s32[]{:S(2)}) async-start(s8[8388608]{0:T(1024)(128)(4,1)} %bitcast.10), calls=%async_computation.3 | async-start | bytes 8388608
  7.9 13.8 %slice-start.5 = ((s8[8388608]{0:T(1024)(128)(4,1)}), s8[4194304]{0:T(1024)(128)(4,1)S(1)}, s32[]{:S(2)}) async-start(s8[8388608]{0:T(1024)(128)(4,1)} %bitcast.15), calls=%async_computation.5 | async-start | bytes 8388608
  7.9 6.9 %collective-permute-start.3 = (bf16[2,4,4224]{2,1,0:T(4,128)(2,1)S(1)}, bf16[2,4,4224]{2,1,0:T(4,128)(2,1)S(1)}, u32[]{:S(2)}, u32[]{:S(2)}) collective-permute-start(bf16[2,4,4224]{2,1,0:T(4,128)(2,1)S(1)} %stack_blocks.2.refs_0_), channel_id=1, source_target_pairs={{0,18},{1,19},{2,16},{3,17},{4,22},{5,23},{6,20},{7,21},{8,26},{9,... | collective-permute-start | bytes 202760 | tf_op jit(solution)/shard_map/ppermute | solution.py:22
  10.7 5.5 %collective-permute-start.2 = (bf16[2,4,4224]{2,1,0:T(4,128)(2,1)S(1)}, bf16[2,4,4224]{2,1,0:T(4,128)(2,1)S(1)}, u32[]{:S(2)}, u32[]{:S(2)}) collective-permute-start(bf16[2,4,4224]{2,1,0:T(4,128)(2,1)S(1)} %stack_blocks.2.refs_0_), channel_id=1, source_target_pairs={{0,16},{1,17},{2,18},{3,19},{4,20},{5,21},{6,22},{7,23},{8,24},{9,... | collective-permute-start | bytes 202760 | tf_op jit(solution)/shard_map/ppermute | solution.py:22
  11.2 5.0 %collective-permute-start.1 = (bf16[2,4,4224]{2,1,0:T(4,128)(2,1)S(1)}, bf16[2,4,4224]{2,1,0:T(4,128)(2,1)S(1)}, u32[]{:S(2)}, u32[]{:S(2)}) collective-permute-start(bf16[2,4,4224]{2,1,0:T(4,128)(2,1)S(1)} %stack_blocks.2.refs_0_), channel_id=1, source_target_pairs={{0,2},{1,3},{2,0},{3,1},{4,6},{5,7},{6,4},{7,5},{8,10},{9,11},{10,... | collective-permute-start | bytes 202760 | tf_op jit(solution)/shard_map/ppermute | solution.py:22
  11.5 8.6 %collective-permute-start.8 = (bf16[2,4,4224]{2,1,0:T(4,128)(2,1)S(1)}, bf16[2,4,4224]{2,1,0:T(4,128)(2,1)S(1)}, u32[]{:S(2)}, u32[]{:S(2)}) collective-permute-start(bf16[2,4,4224]{2,1,0:T(4,128)(2,1)S(1)} %stack_blocks.3.refs_0_), channel_id=1, source_target_pairs={{0,16},{1,17},{2,18},{3,19},{4,20},{5,21},{6,22},{7,23},{8,24},{9,... | collective-permute-start | bytes 202760 | tf_op jit(solution)/shard_map/ppermute | solution.py:22
  13.3 6.8 %collective-permute-start.7 = (bf16[2,4,4224]{2,1,0:T(4,128)(2,1)S(1)}, bf16[2,4,4224]{2,1,0:T(4,128)(2,1)S(1)}, u32[]{:S(2)}, u32[]{:S(2)}) collective-permute-start(bf16[2,4,4224]{2,1,0:T(4,128)(2,1)S(1)} %stack_blocks.3.refs_0_), channel_id=1, source_target_pairs={{0,2},{1,3},{2,0},{3,1},{4,6},{5,7},{6,4},{7,5},{8,10},{9,11},{10,... | collective-permute-start | bytes 202760 | tf_op jit(solution)/shard_map/ppermute | solution.py:22
  14.8 5.2 %collective-permute-start.6 = (bf16[2,4,4224]{2,1,0:T(4,128)(2,1)S(1)}, bf16[2,4,4224]{2,1,0:T(4,128)(2,1)S(1)}, u32[]{:S(2)}, u32[]{:S(2)}) collective-permute-start(bf16[2,4,4224]{2,1,0:T(4,128)(2,1)S(1)} %stack_blocks.3.refs_0_), channel_id=1, source_target_pairs={{0,18},{1,19},{2,16},{3,17},{4,22},{5,23},{6,20},{7,21},{8,26},{9,... | collective-permute-start | bytes 202760 | tf_op jit(solution)/shard_map/ppermute | solution.py:22
  16.3 4.5 %collective-permute-start.9 = (bf16[32,4224]{1,0:T(8,128)(2,1)S(1)}, bf16[32,4224]{1,0:T(8,128)(2,1)S(1)}, u32[]{:S(2)}, u32[]{:S(2)}) collective-permute-start(bf16[32,4224]{1,0:T(8,128)(2,1)S(1)} %join_rows.3), channel_id=1, source_target_pairs={{0,1},{1,0},{2,3},{3,2},{4,5},{5,4},{6,7},{7,6},{8,9},{9,8},{10,11... | collective-permute-start | bytes 811016 | tf_op jit(solution)/shard_map/ppermute | solution.py:22
  20.0 1.4 %collective-permute-start.10 = (bf16[16,4224]{1,0:T(8,128)(2,1)S(1)}, bf16[16,4224]{1,0:T(8,128)(2,1)S(1)}, u32[]{:S(2)}, u32[]{:S(2)}) collective-permute-start(bf16[16,4224]{1,0:T(8,128)(2,1)S(1)} %join_rows.4), channel_id=1, source_target_pairs={{0,1},{1,0},{2,3},{3,2},{4,5},{5,4},{6,7},{7,6},{8,9},{9,8},{10,11... | collective-permute-start | bytes 405512 | tf_op jit(solution)/shard_map/ppermute | solution.py:22
  20.2 1.5 %collective-permute-start.11 = (bf16[16,4224]{1,0:T(8,128)(2,1)S(1)}, bf16[16,4224]{1,0:T(8,128)(2,1)S(1)}, u32[]{:S(2)}, u32[]{:S(2)}) collective-permute-start(bf16[16,4224]{1,0:T(8,128)(2,1)S(1)} %join_rows.5), channel_id=1, source_target_pairs={{0,1},{1,0},{2,3},{3,2},{4,5},{5,4},{6,7},{7,6},{8,9},{9,8},{10,11... | collective-permute-start | bytes 405512 | tf_op jit(solution)/shard_map/ppermute | solution.py:22
  21.8 5.9 %slice-start = ((s8[8388608]{0:T(1024)(128)(4,1)}), s8[4194304]{0:T(1024)(128)(4,1)S(1)}, s32[]{:S(2)}) async-start(s8[8388608]{0:T(1024)(128)(4,1)} %bitcast.3), calls=%async_computation | async-start | bytes 8388608
  22.9 4.7 %slice-start.1 = ((s8[8388608]{0:T(1024)(128)(4,1)}), s8[4194304]{0:T(1024)(128)(4,1)S(1)}, s32[]{:S(2)}) async-start(s8[8388608]{0:T(1024)(128)(4,1)} %bitcast.3), calls=%async_computation.1 | async-start | bytes 8388608
  23.0 5.7 %collective-permute-start.14 = (bf16[128,384]{1,0:T(8,128)(2,1)S(1)}, bf16[128,384]{1,0:T(8,128)(2,1)S(1)}, u32[]{:S(2)}, u32[]{:S(2)}) collective-permute-start(bf16[128,384]{1,0:T(8,128)(2,1)S(1)} %expand_rows.3.refs_0_), channel_id=1, source_target_pairs={{0,16},{1,17},{2,18},{3,19},{4,20},{5,21},{6,22},{7,23},{8,24},{9,... | collective-permute-start | bytes 294920 | tf_op jit(solution)/shard_map/ppermute | solution.py:22
  24.7 6.1 %collective-permute-start.13 = (bf16[128,384]{1,0:T(8,128)(2,1)S(1)}, bf16[128,384]{1,0:T(8,128)(2,1)S(1)}, u32[]{:S(2)}, u32[]{:S(2)}) collective-permute-start(bf16[128,384]{1,0:T(8,128)(2,1)S(1)} %expand_rows.4.refs_1_), channel_id=1, source_target_pairs={{0,16},{1,17},{2,18},{3,19},{4,20},{5,21},{6,22},{7,23},{8,24},{9,... | collective-permute-start | bytes 294920 | tf_op jit(solution)/shard_map/ppermute | solution.py:22
  27.0 4.5 %collective-permute-start.12 = (bf16[128,256]{1,0:T(8,128)(2,1)S(1)}, bf16[128,256]{1,0:T(8,128)(2,1)S(1)}, u32[]{:S(2)}, u32[]{:S(2)}) collective-permute-start(bf16[128,256]{1,0:T(8,128)(2,1)S(1)} %expand_rows.5.refs_2_), channel_id=1, source_target_pairs={{0,16},{1,17},{2,18},{3,19},{4,20},{5,21},{6,22},{7,23},{8,24},{9,... | collective-permute-start | bytes 196616 | tf_op jit(solution)/shard_map/ppermute | solution.py:22
  31.9 1.6 %collective-permute-start.15 = (bf16[64,2048]{1,0:T(8,128)(2,1)S(1)}, bf16[64,2048]{1,0:T(8,128)(2,1)S(1)}, u32[]{:S(2)}, u32[]{:S(2)}) collective-permute-start(bf16[64,2048]{1,0:T(8,128)(2,1)S(1)} %contract_hidden.9), channel_id=1, source_target_pairs={{0,1},{1,0},{2,3},{3,2},{4,5},{5,4},{6,7},{7,6},{8,9},{9,8},{10,11... | collective-permute-start | bytes 786440 | tf_op jit(solution)/shard_map/ppermute | solution.py:22
  33.7 5.9 %collective-permute-start.16 = (bf16[4,4,2048]{2,1,0:T(4,128)(2,1)S(1)}, bf16[4,4,2048]{2,1,0:T(4,128)(2,1)S(1)}, u32[]{:S(2)}, u32[]{:S(2)}) collective-permute-start(bf16[4,4,2048]{2,1,0:T(4,128)(2,1)S(1)} %get-tuple-element.30), channel_id=1, source_target_pairs={{0,6},{1,7},{2,4},{3,5},{4,2},{5,3},{6,0},{7,1},{8,14},{9,15},{10,... | collective-permute-start | bytes 196616 | tf_op jit(solution)/shard_map/ppermute | solution.py:22
  34.7 4.8 %collective-permute-start.17 = (bf16[4,4,2048]{2,1,0:T(4,128)(2,1)S(1)}, bf16[4,4,2048]{2,1,0:T(4,128)(2,1)S(1)}, u32[]{:S(2)}, u32[]{:S(2)}) collective-permute-start(bf16[4,4,2048]{2,1,0:T(4,128)(2,1)S(1)} %get-tuple-element.31), channel_id=1, source_target_pairs={{0,4},{1,5},{2,6},{3,7},{4,0},{5,1},{6,2},{7,3},{8,12},{9,13},{10,... | collective-permute-start | bytes 196616 | tf_op jit(solution)/shard_map/ppermute | solution.py:22
  35.9 4.3 %collective-permute-start.18 = (bf16[4,4,2048]{2,1,0:T(4,128)(2,1)S(1)}, bf16[4,4,2048]{2,1,0:T(4,128)(2,1)S(1)}, u32[]{:S(2)}, u32[]{:S(2)}) collective-permute-start(bf16[4,4,2048]{2,1,0:T(4,128)(2,1)S(1)} %get-tuple-element.32), channel_id=1, source_target_pairs={{0,2},{1,3},{2,0},{3,1},{4,6},{5,7},{6,4},{7,5},{8,10},{9,11},{10,... | collective-permute-start | bytes 196616 | tf_op jit(solution)/shard_map/ppermute | solution.py:22
  40.3 5.6 %collective-permute-start.19 = (bf16[1,4,2048]{2,1,0:T(4,128)(2,1)S(1)}, bf16[1,4,2048]{2,1,0:T(4,128)(2,1)S(1)}, u32[]{:S(2)}, u32[]{:S(2)}) collective-permute-start(bf16[1,4,2048]{2,1,0:T(4,128)(2,1)S(1)} %get-tuple-element.33), channel_id=1, source_target_pairs={{0,24},{1,25},{2,26},{3,27},{4,28},{5,29},{6,30},{7,31},{8,16},{9,... | collective-permute-start | bytes 49160 | tf_op jit(solution)/shard_map/ppermute | solution.py:22
  43.0 4.6 %collective-permute-start.20 = (bf16[1,4,2048]{2,1,0:T(4,128)(2,1)S(1)}, bf16[1,4,2048]{2,1,0:T(4,128)(2,1)S(1)}, u32[]{:S(2)}, u32[]{:S(2)}) collective-permute-start(bf16[1,4,2048]{2,1,0:T(4,128)(2,1)S(1)} %get-tuple-element.34), channel_id=1, source_target_pairs={{0,8},{1,9},{2,10},{3,11},{4,12},{5,13},{6,14},{7,15},{8,0},{9,1},... | collective-permute-start | bytes 49160 | tf_op jit(solution)/shard_map/ppermute | solution.py:22
  43.9 3.8 %collective-permute-start.21 = (bf16[1,4,2048]{2,1,0:T(4,128)(2,1)S(1)}, bf16[1,4,2048]{2,1,0:T(4,128)(2,1)S(1)}, u32[]{:S(2)}, u32[]{:S(2)}) collective-permute-start(bf16[1,4,2048]{2,1,0:T(4,128)(2,1)S(1)} %get-tuple-element.35), channel_id=1, source_target_pairs={{0,16},{1,17},{2,18},{3,19},{4,20},{5,21},{6,22},{7,23},{8,24},{9,... | collective-permute-start | bytes 49160 | tf_op jit(solution)/shard_map/ppermute | solution.py:22

commit v22 on v21

--- a/solution.py
+++ b/solution.py
@@ -271,17 +271,14 @@
     near = stack_blocks([block] + [swap(block, 0, 4 * i) for i in range(1, high)])
     sets = []
     for part in (blocks[: high // 2], blocks[high // 2 :]):
+        if sets:
+            part[0], sets[0][0] = lax.optimization_barrier((part[0], sets[0][0]))
         near = stack_blocks(part)
         if wide > 1:
             near = jnp.concatenate([near] + [swap(near, 2 * i, 0) for i in range(1, wide)])
-        sets.append((near, swap(near, 0, 2), swap(near, 1, 0), swap(near, 1, 2)))
-    near, over_y, over_x, corner = sets[1]
-    pieces = [join_rows(sets[0]), join_rows([near, corner]), join_rows([over_y, over_x])]
-    size = pieces[0].shape[0] // 4
-    rows = []
-    for first, outer, inner in (pieces, [swap(piece, 0, 1) for piece in pieces]):
-        rows += [first, outer[:size], inner, outer[size:]]
-    rows = jnp.concatenate(rows)
+        sets.append([near, swap(near, 0, 2), swap(near, 1, 0), swap(near, 1, 2)])
+    pieces = [join_rows(blocks) for blocks in sets]
+    rows = jnp.concatenate(pieces + [swap(piece, 0, 1) for piece in pieces])
 
     eighth = units // 8
     steps = (3 * eighth, 3 * eighth, 2 * eighth) if eighth % LANES == 0 else (units,)

time: 48.5 us -> 47.7 us (0.984)
  starting transfers between devices: 25.5 us -> 24.9 us
    ppermute x22 -> x21, starting transfers between devices: 25.5 us -> 24.9 us  [swap(): return lax.ppermute(value, ('dp',) + EXPERT, pairs)]
    ppermute x22 -> x21, waiting for transfers between devices: 15.2 us -> 15 us  [swap(): return lax.ppermute(value, ('dp',) + EXPERT, pairs)]
  transfers between devices with their start and end apart: 22 -> 21, of which waited for: 12 -> 13; matrix products, arithmetic and copies ran while one was open for 0% -> 0% of each run, Pallas kernels for 8% -> 9%
where the time goes in v22:
time: 47.7 us; the launch traced here: 47.5 us
  starting transfers between devices  24.9 us (52%)
  waiting for transfers between devices  15 us (31%)
  Pallas kernels  7.2 us (15%)
    ppermute x21, starting transfers between devices, swap(): return lax.ppermute(value, ('dp',) + EXPERT, pairs)  24.9 us
    ppermute x21, waiting for transfers between devices, swap(): return lax.ppermute(value, ('dp',) + EXPERT, pairs)  15 us
    pallas_call x3, Pallas kernels, expand_rows(): pl.pallas_call(body, out_shape=jax.ShapeDtypeStruct((count, columns), row...  3.11 us
    pallas_call x5, Pallas kernels, contract_hidden(): pl.pallas_call(body, out_shape=jax.ShapeDtypeStruct((count, width), kind)...  2.28 us
  transfers between devices with their start and end apart: 21, of which 13 were waited for; matrix products, arithmetic and copies ran while one was open for 0% of the time, Pallas kernels for 9%

profile of v22, /device:TPU:0, one launch (start us, length us, event | category | flops | bytes accessed | tf_op | source)
XLA Modules:
  0.0 47.5 jit_solution(2670499443999592887)
XLA Ops:
  0.0 0.9 %pack_block.1.refs_0_ = bf16[4,4224]{1,0:T(4,128)(2,1)S(1)} custom-call(bf16[4,4096]{1,0:T(4,128)(2,1)} %tokens_ref.1, s32[4,8]{1,0:T(4,128)} %ids_ref.1, f32[4,8]{1,0:T(4,128)} %probs_ref.1), custom_call_target="tpu_custom_call" | custom-call | tf_op jit(solution)/shard_map/pack_block/pallas_call | solution.py:62
  0.9 5.1 %collective-permute-start.1 = (bf16[4,4224]{1,0:T(4,128)(2,1)S(1)}, bf16[4,4224]{1,0:T(4,128)(2,1)S(1)}, u32[]{:S(2)}, u32[]{:S(2)}) collective-permute-start(bf16[4,4224]{1,0:T(4,128)(2,1)S(1)} %pack_block.1.refs_0_), channel_id=1, source_target_pairs={{0,12},{1,13},{2,14},{3,15},{4,8},{5,9},{6,10},{7,11},{8,4},{9,5},... | collective-permute-start | bytes 101384 | tf_op jit(solution)/shard_map/ppermute | solution.py:22
  6.0 0.6 %collective-permute-start = (bf16[4,4224]{1,0:T(4,128)(2,1)S(1)}, bf16[4,4224]{1,0:T(4,128)(2,1)S(1)}, u32[]{:S(2)}, u32[]{:S(2)}) collective-permute-start(bf16[4,4224]{1,0:T(4,128)(2,1)S(1)} %pack_block.1.refs_0_), channel_id=1, source_target_pairs={{0,8},{1,9},{2,10},{3,11},{4,12},{5,13},{6,14},{7,15},{8,0},{9,1},... | collective-permute-start | bytes 101384 | tf_op jit(solution)/shard_map/ppermute | solution.py:22
  6.6 1.3 %collective-permute-done.1.refs_1_ = bf16[4,4224]{1,0:T(4,128)(2,1)S(1)} collective-permute-done((bf16[4,4224]{1,0:T(4,128)(2,1)S(1)}, bf16[4,4224]{1,0:T(4,128)(2,1)S(1)}, u32[]{:S(2)}, u32[]{:S(2)}) %collective-permute-start.1) | collective-permute-done | bytes 33824 | tf_op jit(solution)/shard_map/ppermute | solution.py:22
  7.9 0.0 slice-start.5
  7.9 2.7 %collective-permute-start.4 = (bf16[2,4,4224]{2,1,0:T(4,128)(2,1)S(1)}, bf16[2,4,4224]{2,1,0:T(4,128)(2,1)S(1)}, u32[]{:S(2)}, u32[]{:S(2)}) collective-permute-start(bf16[2,4,4224]{2,1,0:T(4,128)(2,1)S(1)} %stack_blocks.2.refs_0_), channel_id=1, source_target_pairs={{0,18},{1,19},{2,16},{3,17},{4,22},{5,23},{6,20},{7,21},{8,26},{9,... | collective-permute-start | bytes 202760 | tf_op jit(solution)/shard_map/ppermute | solution.py:22
  10.7 0.5 %collective-permute-start.3 = (bf16[2,4,4224]{2,1,0:T(4,128)(2,1)S(1)}, bf16[2,4,4224]{2,1,0:T(4,128)(2,1)S(1)}, u32[]{:S(2)}, u32[]{:S(2)}) collective-permute-start(bf16[2,4,4224]{2,1,0:T(4,128)(2,1)S(1)} %stack_blocks.2.refs_0_), channel_id=1, source_target_pairs={{0,16},{1,17},{2,18},{3,19},{4,20},{5,21},{6,22},{7,23},{8,24},{9,... | collective-permute-start | bytes 202760 | tf_op jit(solution)/shard_map/ppermute | solution.py:22
  11.2 0.3 collective-permute-start.2
  11.5 2.7 %collective-permute-start.8 = (bf16[2,4,4224]{2,1,0:T(4,128)(2,1)S(1)}, bf16[2,4,4224]{2,1,0:T(4,128)(2,1)S(1)}, u32[]{:S(2)}, u32[]{:S(2)}) collective-permute-start(bf16[2,4,4224]{2,1,0:T(4,128)(2,1)S(1)} %stack_blocks.3.refs_0_), channel_id=1, source_target_pairs={{0,18},{1,19},{2,16},{3,17},{4,22},{5,23},{6,20},{7,21},{8,26},{9,... | collective-permute-start | bytes 202760 | tf_op jit(solution)/shard_map/ppermute | solution.py:22
  14.2 0.5 %collective-permute-start.7 = (bf16[2,4,4224]{2,1,0:T(4,128)(2,1)S(1)}, bf16[2,4,4224]{2,1,0:T(4,128)(2,1)S(1)}, u32[]{:S(2)}, u32[]{:S(2)}) collective-permute-start(bf16[2,4,4224]{2,1,0:T(4,128)(2,1)S(1)} %stack_blocks.3.refs_0_), channel_id=1, source_target_pairs={{0,16},{1,17},{2,18},{3,19},{4,20},{5,21},{6,22},{7,23},{8,24},{9,... | collective-permute-start | bytes 202760 | tf_op jit(solution)/shard_map/ppermute | solution.py:22
  14.8 0.4 collective-permute-start.6
  15.2 0.2 collective-permute-done.3.refs_2_
  15.4 1.5 %collective-permute-done.2.refs_1_ = bf16[2,4,4224]{2,1,0:T(4,128)(2,1)S(1)} collective-permute-done((bf16[2,4,4224]{2,1,0:T(4,128)(2,1)S(1)}, bf16[2,4,4224]{2,1,0:T(4,128)(2,1)S(1)}, u32[]{:S(2)}, u32[]{:S(2)}) %collective-permute-start.2) | collective-permute-done | bytes 67616 | tf_op jit(solution)/shard_map/ppermute | solution.py:22
  16.9 0.1 join_rows.2
  17.0 0.1 collective-permute-start.9
  17.1 1.5 %collective-permute-done.7.refs_2_ = bf16[2,4,4224]{2,1,0:T(4,128)(2,1)S(1)} collective-permute-done((bf16[2,4,4224]{2,1,0:T(4,128)(2,1)S(1)}, bf16[2,4,4224]{2,1,0:T(4,128)(2,1)S(1)}, u32[]{:S(2)}, u32[]{:S(2)}) %collective-permute-start.7) | collective-permute-done | bytes 67616 | tf_op jit(solution)/shard_map/ppermute | solution.py:22
  18.5 0.5 %collective-permute-done.6.refs_1_ = bf16[2,4,4224]{2,1,0:T(4,128)(2,1)S(1)} collective-permute-done((bf16[2,4,4224]{2,1,0:T(4,128)(2,1)S(1)}, bf16[2,4,4224]{2,1,0:T(4,128)(2,1)S(1)}, u32[]{:S(2)}, u32[]{:S(2)}) %collective-permute-start.6) | collective-permute-done | bytes 67616 | tf_op jit(solution)/shard_map/ppermute | solution.py:22
  19.1 0.1 join_rows.3
  19.1 0.1 collective-permute-start.10
  19.2 1.5 %collective-permute-done.10 = bf16[32,4224]{1,0:T(8,128)(2,1)S(1)} collective-permute-done((bf16[32,4224]{1,0:T(8,128)(2,1)S(1)}, bf16[32,4224]{1,0:T(8,128)(2,1)S(1)}, u32[]{:S(2)}, u32[]{:S(2)}) %collective-permute-start.10) | collective-permute-done | bytes 270368 | tf_op jit(solution)/shard_map/ppermute | solution.py:22
  20.7 0.1 pad_maximum_fusion.rows_ref.refs_3_
  20.9 1.2 %expand_rows.3.refs_0_ = bf16[128,384]{1,0:T(8,128)(2,1)S(1)} custom-call(bf16[128,4224]{1,0:T(8,128)(2,1)S(1)} %pad_maximum_fusion.rows_ref.refs_3_, bf16[4096,1024]{1,0:T(8,128)(2,1)S(1)} %bitcast.12, bf16[4096,1024]{1,0:T(8,128)(2,1)S(1)} %bitcast.17), custom_call_target="tpu_custom_call" | custom-call | bytes 49152 | tf_op jit(solution)/shard_map/expand_rows/pallas_call | solution.py:131
  22.1 1.6 %collective-permute-start.13 = (bf16[128,384]{1,0:T(8,128)(2,1)S(1)}, bf16[128,384]{1,0:T(8,128)(2,1)S(1)}, u32[]{:S(2)}, u32[]{:S(2)}) collective-permute-start(bf16[128,384]{1,0:T(8,128)(2,1)S(1)} %expand_rows.3.refs_0_), channel_id=1, source_target_pairs={{0,16},{1,17},{2,18},{3,19},{4,20},{5,21},{6,22},{7,23},{8,24},{9,... | collective-permute-start | bytes 294920 | tf_op jit(solution)/shard_map/ppermute | solution.py:22
  23.6 1.1 %expand_rows.4.refs_1_ = bf16[128,384]{1,0:T(8,128)(2,1)S(1)} custom-call(bf16[128,4224]{1,0:T(8,128)(2,1)S(1)} %pad_maximum_fusion.rows_ref.refs_3_, bf16[4096,1024]{1,0:T(8,128)(2,1)S(1)} %bitcast.13, bf16[4096,1024]{1,0:T(8,128)(2,1)S(1)} %bitcast.18), custom_call_target="tpu_custom_call" | custom-call | bytes 49152 | tf_op jit(solution)/shard_map/expand_rows/pallas_call | solution.py:131
  24.8 0.6 %collective-permute-start.12 = (bf16[128,384]{1,0:T(8,128)(2,1)S(1)}, bf16[128,384]{1,0:T(8,128)(2,1)S(1)}, u32[]{:S(2)}, u32[]{:S(2)}) collective-permute-start(bf16[128,384]{1,0:T(8,128)(2,1)S(1)} %expand_rows.4.refs_1_), channel_id=1, source_target_pairs={{0,16},{1,17},{2,18},{3,19},{4,20},{5,21},{6,22},{7,23},{8,24},{9,... | collective-permute-start | bytes 294920 | tf_op jit(solution)/shard_map/ppermute | solution.py:22
  25.4 0.8 %expand_rows.5.refs_2_ = bf16[128,256]{1,0:T(8,128)(2,1)S(1)} custom-call(bf16[128,4224]{1,0:T(8,128)(2,1)S(1)} %pad_maximum_fusion.rows_ref.refs_3_, bf16[4096,1024]{1,0:T(8,128)(2,1)S(1)} %bitcast.14, bf16[4096,1024]{1,0:T(8,128)(2,1)S(1)} %bitcast.19), custom_call_target="tpu_custom_call" | custom-call | bytes 32768 | tf_op jit(solution)/shard_map/expand_rows/pallas_call | solution.py:131
  26.2 1.5 %collective-permute-start.11 = (bf16[128,256]{1,0:T(8,128)(2,1)S(1)}, bf16[128,256]{1,0:T(8,128)(2,1)S(1)}, u32[]{:S(2)}, u32[]{:S(2)}) collective-permute-start(bf16[128,256]{1,0:T(8,128)(2,1)S(1)} %expand_rows.5.refs_2_), channel_id=1, source_target_pairs={{0,16},{1,17},{2,18},{3,19},{4,20},{5,21},{6,22},{7,23},{8,24},{9,... | collective-permute-start | bytes 196616 | tf_op jit(solution)/shard_map/ppermute | solution.py:22
  27.8 0.7 %contract_hidden.5.refs_2_ = f32[128,2048]{1,0:T(8,128)S(1)} custom-call(bf16[128,384]{1,0:T(8,128)(2,1)S(1)} %expand_rows.3.refs_0_, bf16[128,384]{1,0:T(8,128)(2,1)S(1)} %expand_rows.4.refs_1_, bf16[128,256]{1,0:T(8,128)(2,1)S(1)} %expand_rows.5.refs_2_, bf16[2048,2048]{1,0:T(8,128)(2,1)S(1)} %bitcast.5), custom_call_target="tpu_custom_call" | custom-call | bytes 262144 | tf_op jit(solution)/shard_map/contract_hidden/pallas_call | solution.py:192
  28.5 0.5 contract_hidden.6.refs_2_
  29.0 1.2 %collective-permute-done.12.refs_0_ = bf16[128,384]{1,0:T(8,128)(2,1)S(1)} collective-permute-done((bf16[128,384]{1,0:T(8,128)(2,1)S(1)}, bf16[128,384]{1,0:T(8,128)(2,1)S(1)}, u32[]{:S(2)}, u32[]{:S(2)}) %collective-permute-start.12) | collective-permute-done | bytes 98336 | tf_op jit(solution)/shard_map/ppermute | solution.py:22
  30.2 0.5 contract_hidden.7.refs_2_
  30.6 0.2 collective-permute-done.11.refs_0_
  30.9 0.3 contract_hidden.9
  31.2 0.1 collective-permute-start.14
  31.2 0.3 contract_hidden.8.refs_0_
  31.6 1.2 %collective-permute-done.14.refs_1_ = bf16[64,2048]{1,0:T(8,128)(2,1)S(1)} collective-permute-done((bf16[64,2048]{1,0:T(8,128)(2,1)S(1)}, bf16[64,2048]{1,0:T(8,128)(2,1)S(1)}, u32[]{:S(2)}, u32[]{:S(2)}) %collective-permute-start.14) | collective-permute-done | bytes 262176 | tf_op jit(solution)/shard_map/ppermute | solution.py:22
  32.8 0.1 sum_stage.2
  32.9 1.1 %collective-permute-start.15 = (bf16[4,4,2048]{2,1,0:T(4,128)(2,1)S(1)}, bf16[4,4,2048]{2,1,0:T(4,128)(2,1)S(1)}, u32[]{:S(2)}, u32[]{:S(2)}) collective-permute-start(bf16[4,4,2048]{2,1,0:T(4,128)(2,1)S(1)} %get-tuple-element.34), channel_id=1, source_target_pairs={{0,6},{1,7},{2,4},{3,5},{4,2},{5,3},{6,0},{7,1},{8,14},{9,15},{10,... | collective-permute-start | bytes 196616 | tf_op jit(solution)/shard_map/ppermute | solution.py:22
  34.0 0.9 %collective-permute-start.16 = (bf16[4,4,2048]{2,1,0:T(4,128)(2,1)S(1)}, bf16[4,4,2048]{2,1,0:T(4,128)(2,1)S(1)}, u32[]{:S(2)}, u32[]{:S(2)}) collective-permute-start(bf16[4,4,2048]{2,1,0:T(4,128)(2,1)S(1)} %get-tuple-element.35), channel_id=1, source_target_pairs={{0,4},{1,5},{2,6},{3,7},{4,0},{5,1},{6,2},{7,3},{8,12},{9,13},{10,... | collective-permute-start | bytes 196616 | tf_op jit(solution)/shard_map/ppermute | solution.py:22
  34.9 1.5 %collective-permute-start.17 = (bf16[4,4,2048]{2,1,0:T(4,128)(2,1)S(1)}, bf16[4,4,2048]{2,1,0:T(4,128)(2,1)S(1)}, u32[]{:S(2)}, u32[]{:S(2)}) collective-permute-start(bf16[4,4,2048]{2,1,0:T(4,128)(2,1)S(1)} %get-tuple-element.36), channel_id=1, source_target_pairs={{0,2},{1,3},{2,0},{3,1},{4,6},{5,7},{6,4},{7,5},{8,10},{9,11},{10,... | collective-permute-start | bytes 196616 | tf_op jit(solution)/shard_map/ppermute | solution.py:22
  36.5 2.4 %collective-permute-done.15.refs_1_ = bf16[4,4,2048]{2,1,0:T(4,128)(2,1)S(1)} collective-permute-done((bf16[4,4,2048]{2,1,0:T(4,128)(2,1)S(1)}, bf16[4,4,2048]{2,1,0:T(4,128)(2,1)S(1)}, u32[]{:S(2)}, u32[]{:S(2)}) %collective-permute-start.15) | collective-permute-done | bytes 65568 | tf_op jit(solution)/shard_map/ppermute | solution.py:22
  38.8 0.6 %collective-permute-done.17.refs_3_ = bf16[4,4,2048]{2,1,0:T(4,128)(2,1)S(1)} collective-permute-done((bf16[4,4,2048]{2,1,0:T(4,128)(2,1)S(1)}, bf16[4,4,2048]{2,1,0:T(4,128)(2,1)S(1)}, u32[]{:S(2)}, u32[]{:S(2)}) %collective-permute-start.17) | collective-permute-done | bytes 65568 | tf_op jit(solution)/shard_map/ppermute | solution.py:22
  39.5 2.7 %collective-permute-start.18 = (bf16[1,4,2048]{2,1,0:T(4,128)(2,1)S(1)}, bf16[1,4,2048]{2,1,0:T(4,128)(2,1)S(1)}, u32[]{:S(2)}, u32[]{:S(2)}) collective-permute-start(bf16[1,4,2048]{2,1,0:T(4,128)(2,1)S(1)} %get-tuple-element.37), channel_id=1, source_target_pairs={{0,24},{1,25},{2,26},{3,27},{4,28},{5,29},{6,30},{7,31},{8,16},{9,... | collective-permute-start | bytes 49160 | tf_op jit(solution)/shard_map/ppermute | solution.py:22
  42.2 0.8 %collective-permute-start.19 = (bf16[1,4,2048]{2,1,0:T(4,128)(2,1)S(1)}, bf16[1,4,2048]{2,1,0:T(4,128)(2,1)S(1)}, u32[]{:S(2)}, u32[]{:S(2)}) collective-permute-start(bf16[1,4,2048]{2,1,0:T(4,128)(2,1)S(1)} %get-tuple-element.38), channel_id=1, source_target_pairs={{0,8},{1,9},{2,10},{3,11},{4,12},{5,13},{6,14},{7,15},{8,0},{9,1},... | collective-permute-start | bytes 49160 | tf_op jit(solution)/shard_map/ppermute | solution.py:22
  43.0 0.9 %collective-permute-start.20 = (bf16[1,4,2048]{2,1,0:T(4,128)(2,1)S(1)}, bf16[1,4,2048]{2,1,0:T(4,128)(2,1)S(1)}, u32[]{:S(2)}, u32[]{:S(2)}) collective-permute-start(bf16[1,4,2048]{2,1,0:T(4,128)(2,1)S(1)} %get-tuple-element.39), channel_id=1, source_target_pairs={{0,16},{1,17},{2,18},{3,19},{4,20},{5,21},{6,22},{7,23},{8,24},{9,... | collective-permute-start | bytes 49160 | tf_op jit(solution)/shard_map/ppermute | solution.py:22
  43.9 1.1 %collective-permute-done.18.refs_0_ = bf16[1,4,2048]{2,1,0:T(4,128)(2,1)S(1)} collective-permute-done((bf16[1,4,2048]{2,1,0:T(4,128)(2,1)S(1)}, bf16[1,4,2048]{2,1,0:T(4,128)(2,1)S(1)}, u32[]{:S(2)}, u32[]{:S(2)}) %collective-permute-start.18) | collective-permute-done | bytes 16416 | tf_op jit(solution)/shard_map/ppermute | solution.py:22
  45.1 1.8 %collective-permute-done.19.refs_1_ = bf16[1,4,2048]{2,1,0:T(4,128)(2,1)S(1)} collective-permute-done((bf16[1,4,2048]{2,1,0:T(4,128)(2,1)S(1)}, bf16[1,4,2048]{2,1,0:T(4,128)(2,1)S(1)}, u32[]{:S(2)}, u32[]{:S(2)}) %collective-permute-start.19) | collective-permute-done | bytes 16416 | tf_op jit(solution)/shard_map/ppermute | solution.py:22
  46.8 0.6 %finish.1 = bf16[4,4096]{1,0:T(4,128)(2,1)} custom-call(bf16[1,4,2048]{2,1,0:T(4,128)(2,1)S(1)} %collective-permute-done.18.refs_0_, bf16[1,4,2048]{2,1,0:T(4,128)(2,1)S(1)} %collective-permute-done.19.refs_1_, bf16[1,4,2048]{2,1,0:T(4,128)(2,1)S(1)} %collective-permute-done.20.refs_2_, f32[1,4,2048]{2,1,0:T(4,128)S(1)} %get-tuple-element.40.refs_3_), custom_call_target="tpu_custom_call" | custom-call | tf_op jit(solution)/shard_map/finish/pallas_call | solution.py:247
  (26 shorter events, 0.1 us)
Async XLA Ops:
  0.9 7.0 %collective-permute-start.1 = (bf16[4,4224]{1,0:T(4,128)(2,1)S(1)}, bf16[4,4224]{1,0:T(4,128)(2,1)S(1)}, u32[]{:S(2)}, u32[]{:S(2)}) collective-permute-start(bf16[4,4224]{1,0:T(4,128)(2,1)S(1)} %pack_block.1.refs_0_), channel_id=1, source_target_pairs={{0,12},{1,13},{2,14},{3,15},{4,8},{5,9},{6,10},{7,11},{8,4},{9,5},... | collective-permute-start | bytes 101384 | tf_op jit(solution)/shard_map/ppermute | solution.py:22
  6.0 5.5 %collective-permute-start.5 = (bf16[4,4224]{1,0:T(4,128)(2,1)S(1)}, bf16[4,4224]{1,0:T(4,128)(2,1)S(1)}, u32[]{:S(2)}, u32[]{:S(2)}) collective-permute-start(bf16[4,4224]{1,0:T(4,128)(2,1)S(1)} %pack_block.1.refs_0_), channel_id=1, source_target_pairs={{0,4},{1,5},{2,6},{3,7},{4,0},{5,1},{6,2},{7,3},{8,12},{9,13},{10,... | collective-permute-start | bytes 101384 | tf_op jit(solution)/shard_map/ppermute | solution.py:22
  6.0 5.5 %collective-permute-start = (bf16[4,4224]{1,0:T(4,128)(2,1)S(1)}, bf16[4,4224]{1,0:T(4,128)(2,1)S(1)}, u32[]{:S(2)}, u32[]{:S(2)}) collective-permute-start(bf16[4,4224]{1,0:T(4,128)(2,1)S(1)} %pack_block.1.refs_0_), channel_id=1, source_target_pairs={{0,8},{1,9},{2,10},{3,11},{4,12},{5,13},{6,14},{7,15},{8,0},{9,1},... | collective-permute-start | bytes 101384 | tf_op jit(solution)/shard_map/ppermute | solution.py:22
  7.9 12.9 %slice-start.2 = ((s8[8388608]{0:T(1024)(128)(4,1)}), s8[4194304]{0:T(1024)(128)(4,1)S(1)}, s32[]{:S(2)}) async-start(s8[8388608]{0:T(1024)(128)(4,1)} %bitcast.10), calls=%async_computation.2 | async-start | bytes 8388608
  7.9 12.9 %slice-start.4 = ((s8[8388608]{0:T(1024)(128)(4,1)}), s8[4194304]{0:T(1024)(128)(4,1)S(1)}, s32[]{:S(2)}) async-start(s8[8388608]{0:T(1024)(128)(4,1)} %bitcast.15), calls=%async_computation.4 | async-start | bytes 8388608
  7.9 12.9 %slice-start.3 = ((s8[8388608]{0:T(1024)(128)(4,1)}), s8[4194304]{0:T(1024)(128)(4,1)S(1)}, s32[]{:S(2)}) async-start(s8[8388608]{0:T(1024)(128)(4,1)} %bitcast.10), calls=%async_computation.3 | async-start | bytes 8388608
  7.9 12.9 %slice-start.5 = ((s8[8388608]{0:T(1024)(128)(4,1)}), s8[4194304]{0:T(1024)(128)(4,1)S(1)}, s32[]{:S(2)}) async-start(s8[8388608]{0:T(1024)(128)(4,1)} %bitcast.15), calls=%async_computation.5 | async-start | bytes 8388608
  7.9 6.8 %collective-permute-start.4 = (bf16[2,4,4224]{2,1,0:T(4,128)(2,1)S(1)}, bf16[2,4,4224]{2,1,0:T(4,128)(2,1)S(1)}, u32[]{:S(2)}, u32[]{:S(2)}) collective-permute-start(bf16[2,4,4224]{2,1,0:T(4,128)(2,1)S(1)} %stack_blocks.2.refs_0_), channel_id=1, source_target_pairs={{0,18},{1,19},{2,16},{3,17},{4,22},{5,23},{6,20},{7,21},{8,26},{9,... | collective-permute-start | bytes 202760 | tf_op jit(solution)/shard_map/ppermute | solution.py:22
  10.7 4.8 %collective-permute-start.3 = (bf16[2,4,4224]{2,1,0:T(4,128)(2,1)S(1)}, bf16[2,4,4224]{2,1,0:T(4,128)(2,1)S(1)}, u32[]{:S(2)}, u32[]{:S(2)}) collective-permute-start(bf16[2,4,4224]{2,1,0:T(4,128)(2,1)S(1)} %stack_blocks.2.refs_0_), channel_id=1, source_target_pairs={{0,16},{1,17},{2,18},{3,19},{4,20},{5,21},{6,22},{7,23},{8,24},{9,... | collective-permute-start | bytes 202760 | tf_op jit(solution)/shard_map/ppermute | solution.py:22
  11.2 5.7 %collective-permute-start.2 = (bf16[2,4,4224]{2,1,0:T(4,128)(2,1)S(1)}, bf16[2,4,4224]{2,1,0:T(4,128)(2,1)S(1)}, u32[]{:S(2)}, u32[]{:S(2)}) collective-permute-start(bf16[2,4,4224]{2,1,0:T(4,128)(2,1)S(1)} %stack_blocks.2.refs_0_), channel_id=1, source_target_pairs={{0,2},{1,3},{2,0},{3,1},{4,6},{5,7},{6,4},{7,5},{8,10},{9,11},{10,... | collective-permute-start | bytes 202760 | tf_op jit(solution)/shard_map/ppermute | solution.py:22
  11.5 5.5 %collective-permute-start.8 = (bf16[2,4,4224]{2,1,0:T(4,128)(2,1)S(1)}, bf16[2,4,4224]{2,1,0:T(4,128)(2,1)S(1)}, u32[]{:S(2)}, u32[]{:S(2)}) collective-permute-start(bf16[2,4,4224]{2,1,0:T(4,128)(2,1)S(1)} %stack_blocks.3.refs_0_), channel_id=1, source_target_pairs={{0,18},{1,19},{2,16},{3,17},{4,22},{5,23},{6,20},{7,21},{8,26},{9,... | collective-permute-start | bytes 202760 | tf_op jit(solution)/shard_map/ppermute | solution.py:22
  14.2 4.3 %collective-permute-start.7 = (bf16[2,4,4224]{2,1,0:T(4,128)(2,1)S(1)}, bf16[2,4,4224]{2,1,0:T(4,128)(2,1)S(1)}, u32[]{:S(2)}, u32[]{:S(2)}) collective-permute-start(bf16[2,4,4224]{2,1,0:T(4,128)(2,1)S(1)} %stack_blocks.3.refs_0_), channel_id=1, source_target_pairs={{0,16},{1,17},{2,18},{3,19},{4,20},{5,21},{6,22},{7,23},{8,24},{9,... | collective-permute-start | bytes 202760 | tf_op jit(solution)/shard_map/ppermute | solution.py:22
  14.8 4.3 %collective-permute-start.6 = (bf16[2,4,4224]{2,1,0:T(4,128)(2,1)S(1)}, bf16[2,4,4224]{2,1,0:T(4,128)(2,1)S(1)}, u32[]{:S(2)}, u32[]{:S(2)}) collective-permute-start(bf16[2,4,4224]{2,1,0:T(4,128)(2,1)S(1)} %stack_blocks.3.refs_0_), channel_id=1, source_target_pairs={{0,2},{1,3},{2,0},{3,1},{4,6},{5,7},{6,4},{7,5},{8,10},{9,11},{10,... | collective-permute-start | bytes 202760 | tf_op jit(solution)/shard_map/ppermute | solution.py:22
  17.0 2.2 %collective-permute-start.9 = (bf16[32,4224]{1,0:T(8,128)(2,1)S(1)}, bf16[32,4224]{1,0:T(8,128)(2,1)S(1)}, u32[]{:S(2)}, u32[]{:S(2)}) collective-permute-start(bf16[32,4224]{1,0:T(8,128)(2,1)S(1)} %join_rows.2), channel_id=1, source_target_pairs={{0,1},{1,0},{2,3},{3,2},{4,5},{5,4},{6,7},{7,6},{8,9},{9,8},{10,11... | collective-permute-start | bytes 811016 | tf_op jit(solution)/shard_map/ppermute | solution.py:22
  19.1 1.6 %collective-permute-start.10 = (bf16[32,4224]{1,0:T(8,128)(2,1)S(1)}, bf16[32,4224]{1,0:T(8,128)(2,1)S(1)}, u32[]{:S(2)}, u32[]{:S(2)}) collective-permute-start(bf16[32,4224]{1,0:T(8,128)(2,1)S(1)} %join_rows.3), channel_id=1, source_target_pairs={{0,1},{1,0},{2,3},{3,2},{4,5},{5,4},{6,7},{7,6},{8,9},{9,8},{10,11... | collective-permute-start | bytes 811016 | tf_op jit(solution)/shard_map/ppermute | solution.py:22
  20.9 6.9 %slice-start = ((s8[8388608]{0:T(1024)(128)(4,1)}), s8[4194304]{0:T(1024)(128)(4,1)S(1)}, s32[]{:S(2)}) async-start(s8[8388608]{0:T(1024)(128)(4,1)} %bitcast.3), calls=%async_computation | async-start | bytes 8388608
  22.1 5.7 %slice-start.1 = ((s8[8388608]{0:T(1024)(128)(4,1)}), s8[4194304]{0:T(1024)(128)(4,1)S(1)}, s32[]{:S(2)}) async-start(s8[8388608]{0:T(1024)(128)(4,1)} %bitcast.3), calls=%async_computation.1 | async-start | bytes 8388608
  22.1 6.4 %collective-permute-start.13 = (bf16[128,384]{1,0:T(8,128)(2,1)S(1)}, bf16[128,384]{1,0:T(8,128)(2,1)S(1)}, u32[]{:S(2)}, u32[]{:S(2)}) collective-permute-start(bf16[128,384]{1,0:T(8,128)(2,1)S(1)} %expand_rows.3.refs_0_), channel_id=1, source_target_pairs={{0,16},{1,17},{2,18},{3,19},{4,20},{5,21},{6,22},{7,23},{8,24},{9,... | collective-permute-start | bytes 294920 | tf_op jit(solution)/shard_map/ppermute | solution.py:22
  24.8 5.4 %collective-permute-start.12 = (bf16[128,384]{1,0:T(8,128)(2,1)S(1)}, bf16[128,384]{1,0:T(8,128)(2,1)S(1)}, u32[]{:S(2)}, u32[]{:S(2)}) collective-permute-start(bf16[128,384]{1,0:T(8,128)(2,1)S(1)} %expand_rows.4.refs_1_), channel_id=1, source_target_pairs={{0,16},{1,17},{2,18},{3,19},{4,20},{5,21},{6,22},{7,23},{8,24},{9,... | collective-permute-start | bytes 294920 | tf_op jit(solution)/shard_map/ppermute | solution.py:22
  26.2 4.7 %collective-permute-start.11 = (bf16[128,256]{1,0:T(8,128)(2,1)S(1)}, bf16[128,256]{1,0:T(8,128)(2,1)S(1)}, u32[]{:S(2)}, u32[]{:S(2)}) collective-permute-start(bf16[128,256]{1,0:T(8,128)(2,1)S(1)} %expand_rows.5.refs_2_), channel_id=1, source_target_pairs={{0,16},{1,17},{2,18},{3,19},{4,20},{5,21},{6,22},{7,23},{8,24},{9,... | collective-permute-start | bytes 196616 | tf_op jit(solution)/shard_map/ppermute | solution.py:22
  31.2 1.6 %collective-permute-start.14 = (bf16[64,2048]{1,0:T(8,128)(2,1)S(1)}, bf16[64,2048]{1,0:T(8,128)(2,1)S(1)}, u32[]{:S(2)}, u32[]{:S(2)}) collective-permute-start(bf16[64,2048]{1,0:T(8,128)(2,1)S(1)} %contract_hidden.9), channel_id=1, source_target_pairs={{0,1},{1,0},{2,3},{3,2},{4,5},{5,4},{6,7},{7,6},{8,9},{9,8},{10,11... | collective-permute-start | bytes 786440 | tf_op jit(solution)/shard_map/ppermute | solution.py:22
  32.9 5.9 %collective-permute-start.15 = (bf16[4,4,2048]{2,1,0:T(4,128)(2,1)S(1)}, bf16[4,4,2048]{2,1,0:T(4,128)(2,1)S(1)}, u32[]{:S(2)}, u32[]{:S(2)}) collective-permute-start(bf16[4,4,2048]{2,1,0:T(4,128)(2,1)S(1)} %get-tuple-element.34), channel_id=1, source_target_pairs={{0,6},{1,7},{2,4},{3,5},{4,2},{5,3},{6,0},{7,1},{8,14},{9,15},{10,... | collective-permute-start | bytes 196616 | tf_op jit(solution)/shard_map/ppermute | solution.py:22
  34.0 4.8 %collective-permute-start.16 = (bf16[4,4,2048]{2,1,0:T(4,128)(2,1)S(1)}, bf16[4,4,2048]{2,1,0:T(4,128)(2,1)S(1)}, u32[]{:S(2)}, u32[]{:S(2)}) collective-permute-start(bf16[4,4,2048]{2,1,0:T(4,128)(2,1)S(1)} %get-tuple-element.35), channel_id=1, source_target_pairs={{0,4},{1,5},{2,6},{3,7},{4,0},{5,1},{6,2},{7,3},{8,12},{9,13},{10,... | collective-permute-start | bytes 196616 | tf_op jit(solution)/shard_map/ppermute | solution.py:22
  34.9 4.5 %collective-permute-start.17 = (bf16[4,4,2048]{2,1,0:T(4,128)(2,1)S(1)}, bf16[4,4,2048]{2,1,0:T(4,128)(2,1)S(1)}, u32[]{:S(2)}, u32[]{:S(2)}) collective-permute-start(bf16[4,4,2048]{2,1,0:T(4,128)(2,1)S(1)} %get-tuple-element.36), channel_id=1, source_target_pairs={{0,2},{1,3},{2,0},{3,1},{4,6},{5,7},{6,4},{7,5},{8,10},{9,11},{10,... | collective-permute-start | bytes 196616 | tf_op jit(solution)/shard_map/ppermute | solution.py:22
  39.5 5.6 %collective-permute-start.18 = (bf16[1,4,2048]{2,1,0:T(4,128)(2,1)S(1)}, bf16[1,4,2048]{2,1,0:T(4,128)(2,1)S(1)}, u32[]{:S(2)}, u32[]{:S(2)}) collective-permute-start(bf16[1,4,2048]{2,1,0:T(4,128)(2,1)S(1)} %get-tuple-element.37), channel_id=1, source_target_pairs={{0,24},{1,25},{2,26},{3,27},{4,28},{5,29},{6,30},{7,31},{8,16},{9,... | collective-permute-start | bytes 49160 | tf_op jit(solution)/shard_map/ppermute | solution.py:22
  42.2 4.6 %collective-permute-start.19 = (bf16[1,4,2048]{2,1,0:T(4,128)(2,1)S(1)}, bf16[1,4,2048]{2,1,0:T(4,128)(2,1)S(1)}, u32[]{:S(2)}, u32[]{:S(2)}) collective-permute-start(bf16[1,4,2048]{2,1,0:T(4,128)(2,1)S(1)} %get-tuple-element.38), channel_id=1, source_target_pairs={{0,8},{1,9},{2,10},{3,11},{4,12},{5,13},{6,14},{7,15},{8,0},{9,1},... | collective-permute-start | bytes 49160 | tf_op jit(solution)/shard_map/ppermute | solution.py:22
  43.0 3.8 %collective-permute-start.20 = (bf16[1,4,2048]{2,1,0:T(4,128)(2,1)S(1)}, bf16[1,4,2048]{2,1,0:T(4,128)(2,1)S(1)}, u32[]{:S(2)}, u32[]{:S(2)}) collective-permute-start(bf16[1,4,2048]{2,1,0:T(4,128)(2,1)S(1)} %get-tuple-element.39), channel_id=1, source_target_pairs={{0,16},{1,17},{2,18},{3,19},{4,20},{5,21},{6,22},{7,23},{8,24},{9,... | collective-permute-start | bytes 49160 | tf_op jit(solution)/shard_map/ppermute | solution.py:22

commit v23 on v19

--- a/solution.py
+++ b/solution.py
@@ -276,7 +276,7 @@
     rows = jnp.concatenate(rows)
 
     eighth = units // 8
-    steps = (3 * eighth, 3 * eighth, 2 * eighth) if eighth % LANES == 0 else (units,)
+    steps = (3 * eighth, 3 * eighth, eighth, eighth) if eighth % LANES == 0 else (units,)
     starts = [sum(steps[:i]) for i in range(len(steps))]
     half = rows.shape[0] // 4 if groups == 2 and rows.shape[0] <= BATCH else None
 

time: 47.5 us -> 48.5 us (1.021)
  Pallas kernels: 6.97 us -> 8.02 us
  waiting for transfers between devices: 18.4 us -> 17.7 us
  starting transfers between devices: 21.7 us -> 22.3 us
    pallas_call x3 -> x4, Pallas kernels: 2.91 us -> 3.82 us  [expand_rows(): pl.pallas_call(body, out_shape=jax.ShapeDtypeStruct((count, columns), row...]
    ppermute x19 -> x20, waiting for transfers between devices: 18.4 us -> 17.7 us  [swap(): return lax.ppermute(value, ('dp',) + EXPERT, pairs)]
    ppermute x19 -> x20, starting transfers between devices: 21.7 us -> 22.3 us  [swap(): return lax.ppermute(value, ('dp',) + EXPERT, pairs)]
    pallas_call x5 -> x6, Pallas kernels: 2.26 us -> 2.4 us  [contract_hidden(): pl.pallas_call(body, out_shape=jax.ShapeDtypeStruct((count, width), kind)...]
  transfers between devices with their start and end apart: 19 -> 20, of which waited for: 14 -> 13; matrix products, arithmetic and copies ran while one was open for 0% -> 0% of each run, Pallas kernels for 8% -> 10%
where the time goes in v23:
time: 48.5 us; the launch traced here: 48.4 us
  starting transfers between devices  22.3 us (46%)
  waiting for transfers between devices  17.7 us (36%)
  Pallas kernels  8.02 us (17%)
    ppermute x20, starting transfers between devices, swap(): return lax.ppermute(value, ('dp',) + EXPERT, pairs)  22.3 us
    ppermute x20, waiting for transfers between devices, swap(): return lax.ppermute(value, ('dp',) + EXPERT, pairs)  17.7 us
    pallas_call x4, Pallas kernels, expand_rows(): pl.pallas_call(body, out_shape=jax.ShapeDtypeStruct((count, columns), row...  3.82 us
    pallas_call x6, Pallas kernels, contract_hidden(): pl.pallas_call(body, out_shape=jax.ShapeDtypeStruct((count, width), kind)...  2.4 us
  transfers between devices with their start and end apart: 20, of which 13 were waited for; matrix products, arithmetic and copies ran while one was open for 0% of the time, Pallas kernels for 10%

profile of v23, /device:TPU:0, one launch (start us, length us, event | category | flops | bytes accessed | tf_op | source)
XLA Modules:
  0.0 48.4 jit_solution(10660823064261193752)
XLA Ops:
  0.0 0.9 %pack_block.1.refs_0_ = bf16[4,4224]{1,0:T(4,128)(2,1)S(1)} custom-call(bf16[4,4096]{1,0:T(4,128)(2,1)} %tokens_ref.1, s32[4,8]{1,0:T(4,128)} %ids_ref.1, f32[4,8]{1,0:T(4,128)} %probs_ref.1), custom_call_target="tpu_custom_call" | custom-call | tf_op jit(solution)/shard_map/pack_block/pallas_call | solution.py:62
  0.9 5.1 %collective-permute-start.2 = (bf16[4,4224]{1,0:T(4,128)(2,1)S(1)}, bf16[4,4224]{1,0:T(4,128)(2,1)S(1)}, u32[]{:S(2)}, u32[]{:S(2)}) collective-permute-start(bf16[4,4224]{1,0:T(4,128)(2,1)S(1)} %pack_block.1.refs_0_), channel_id=1, source_target_pairs={{0,12},{1,13},{2,14},{3,15},{4,8},{5,9},{6,10},{7,11},{8,4},{9,5},... | collective-permute-start | bytes 101384 | tf_op jit(solution)/shard_map/ppermute | solution.py:22
  6.0 0.0 collective-permute-start.1
  6.0 0.6 %collective-permute-start = (bf16[4,4224]{1,0:T(4,128)(2,1)S(1)}, bf16[4,4224]{1,0:T(4,128)(2,1)S(1)}, u32[]{:S(2)}, u32[]{:S(2)}) collective-permute-start(bf16[4,4224]{1,0:T(4,128)(2,1)S(1)} %pack_block.1.refs_0_), channel_id=1, source_target_pairs={{0,4},{1,5},{2,6},{3,7},{4,0},{5,1},{6,2},{7,3},{8,12},{9,13},{10,... | collective-permute-start | bytes 101384 | tf_op jit(solution)/shard_map/ppermute | solution.py:22
  6.6 1.3 %collective-permute-done.2.refs_3_ = bf16[4,4224]{1,0:T(4,128)(2,1)S(1)} collective-permute-done((bf16[4,4224]{1,0:T(4,128)(2,1)S(1)}, bf16[4,4224]{1,0:T(4,128)(2,1)S(1)}, u32[]{:S(2)}, u32[]{:S(2)}) %collective-permute-start.2) | collective-permute-done | bytes 33824 | tf_op jit(solution)/shard_map/ppermute | solution.py:22
  7.9 2.9 %collective-permute-done.1.refs_2_ = bf16[4,4224]{1,0:T(4,128)(2,1)S(1)} collective-permute-done((bf16[4,4224]{1,0:T(4,128)(2,1)S(1)}, bf16[4,4224]{1,0:T(4,128)(2,1)S(1)}, u32[]{:S(2)}, u32[]{:S(2)}) %collective-permute-start.1) | collective-permute-done | bytes 33824 | tf_op jit(solution)/shard_map/ppermute | solution.py:22
  10.8 2.5 %collective-permute-start.3 = (bf16[4,4,4224]{2,1,0:T(4,128)(2,1)S(1)}, bf16[4,4,4224]{2,1,0:T(4,128)(2,1)S(1)}, u32[]{:S(2)}, u32[]{:S(2)}) collective-permute-start(bf16[4,4,4224]{2,1,0:T(4,128)(2,1)S(1)} %stack_blocks.1.refs_0_), channel_id=1, source_target_pairs={{0,18},{1,19},{2,16},{3,17},{4,22},{5,23},{6,20},{7,21},{8,26},{9,... | collective-permute-start | bytes 405512 | tf_op jit(solution)/shard_map/ppermute | solution.py:22
  13.3 0.5 %collective-permute-start.5 = (bf16[4,4,4224]{2,1,0:T(4,128)(2,1)S(1)}, bf16[4,4,4224]{2,1,0:T(4,128)(2,1)S(1)}, u32[]{:S(2)}, u32[]{:S(2)}) collective-permute-start(bf16[4,4,4224]{2,1,0:T(4,128)(2,1)S(1)} %stack_blocks.1.refs_0_), channel_id=1, source_target_pairs={{0,16},{1,17},{2,18},{3,19},{4,20},{5,21},{6,22},{7,23},{8,24},{9,... | collective-permute-start | bytes 405512 | tf_op jit(solution)/shard_map/ppermute | solution.py:22
  13.9 0.5 %collective-permute-start.4 = (bf16[4,4,4224]{2,1,0:T(4,128)(2,1)S(1)}, bf16[4,4,4224]{2,1,0:T(4,128)(2,1)S(1)}, u32[]{:S(2)}, u32[]{:S(2)}) collective-permute-start(bf16[4,4,4224]{2,1,0:T(4,128)(2,1)S(1)} %stack_blocks.1.refs_0_), channel_id=1, source_target_pairs={{0,2},{1,3},{2,0},{3,1},{4,6},{5,7},{6,4},{7,5},{8,10},{9,11},{10,... | collective-permute-start | bytes 405512 | tf_op jit(solution)/shard_map/ppermute | solution.py:22
  14.4 2.8 %collective-permute-done.3.refs_1_ = bf16[4,4,4224]{2,1,0:T(4,128)(2,1)S(1)} collective-permute-done((bf16[4,4,4224]{2,1,0:T(4,128)(2,1)S(1)}, bf16[4,4,4224]{2,1,0:T(4,128)(2,1)S(1)}, u32[]{:S(2)}, u32[]{:S(2)}) %collective-permute-start.3) | collective-permute-done | bytes 135200 | tf_op jit(solution)/shard_map/ppermute | solution.py:22
  17.2 0.1 join_rows.3
  17.3 0.1 collective-permute-start.6
  17.4 1.3 %collective-permute-done.5.refs_0_ = bf16[4,4,4224]{2,1,0:T(4,128)(2,1)S(1)} collective-permute-done((bf16[4,4,4224]{2,1,0:T(4,128)(2,1)S(1)}, bf16[4,4,4224]{2,1,0:T(4,128)(2,1)S(1)}, u32[]{:S(2)}, u32[]{:S(2)}) %collective-permute-start.5) | collective-permute-done | bytes 135200 | tf_op jit(solution)/shard_map/ppermute | solution.py:22
  18.7 0.1 collective-permute-start.8
  18.8 0.1 collective-permute-done.4.refs_0_
  18.9 0.4 collective-permute-start.7
  19.5 0.9 %collective-permute-done.7 = bf16[16,4224]{1,0:T(8,128)(2,1)S(1)} collective-permute-done((bf16[16,4224]{1,0:T(8,128)(2,1)S(1)}, bf16[16,4224]{1,0:T(8,128)(2,1)S(1)}, u32[]{:S(2)}, u32[]{:S(2)}) %collective-permute-start.7) | collective-permute-done | bytes 135200 | tf_op jit(solution)/shard_map/ppermute | solution.py:22
  20.4 1.1 %expand_rows.4.refs_0_ = bf16[128,384]{1,0:T(8,128)(2,1)S(1)} custom-call(bf16[128,4224]{1,0:T(8,128)(2,1)S(1)} %slice_dynamic-update-slice_fusion.rows_ref.refs_3_, bf16[4096,1024]{1,0:T(8,128)(2,1)S(1)} %bitcast.11, bf16[4096,1024]{1,0:T(8,128)(2,1)S(1)} %bitcast.15), custom_call_target="tpu_custom_call" | custom-call | bytes 49152 | tf_op jit(solution)/shard_map/expand_rows/pallas_call | solution.py:131
  21.5 1.6 %collective-permute-start.12 = (bf16[128,384]{1,0:T(8,128)(2,1)S(1)}, bf16[128,384]{1,0:T(8,128)(2,1)S(1)}, u32[]{:S(2)}, u32[]{:S(2)}) collective-permute-start(bf16[128,384]{1,0:T(8,128)(2,1)S(1)} %expand_rows.4.refs_0_), channel_id=1, source_target_pairs={{0,16},{1,17},{2,18},{3,19},{4,20},{5,21},{6,22},{7,23},{8,24},{9,... | collective-permute-start | bytes 294920 | tf_op jit(solution)/shard_map/ppermute | solution.py:22
  23.1 1.0 %expand_rows.5.refs_1_ = bf16[128,384]{1,0:T(8,128)(2,1)S(1)} custom-call(bf16[128,4224]{1,0:T(8,128)(2,1)S(1)} %slice_dynamic-update-slice_fusion.rows_ref.refs_3_, bf16[4096,1024]{1,0:T(8,128)(2,1)S(1)} %bitcast.12, bf16[4096,1024]{1,0:T(8,128)(2,1)S(1)} %bitcast.16), custom_call_target="tpu_custom_call" | custom-call | bytes 49152 | tf_op jit(solution)/shard_map/expand_rows/pallas_call | solution.py:131
  24.1 0.6 %collective-permute-start.11 = (bf16[128,384]{1,0:T(8,128)(2,1)S(1)}, bf16[128,384]{1,0:T(8,128)(2,1)S(1)}, u32[]{:S(2)}, u32[]{:S(2)}) collective-permute-start(bf16[128,384]{1,0:T(8,128)(2,1)S(1)} %expand_rows.5.refs_1_), channel_id=1, source_target_pairs={{0,16},{1,17},{2,18},{3,19},{4,20},{5,21},{6,22},{7,23},{8,24},{9,... | collective-permute-start | bytes 294920 | tf_op jit(solution)/shard_map/ppermute | solution.py:22
  24.7 0.8 %expand_rows.6.refs_2_ = bf16[128,128]{1,0:T(8,128)(2,1)S(1)} custom-call(bf16[128,4224]{1,0:T(8,128)(2,1)S(1)} %slice_dynamic-update-slice_fusion.rows_ref.refs_3_, bf16[4096,1024]{1,0:T(8,128)(2,1)S(1)} %bitcast.13, bf16[4096,1024]{1,0:T(8,128)(2,1)S(1)} %bitcast.17), custom_call_target="tpu_custom_call" | custom-call | bytes 16384 | tf_op jit(solution)/shard_map/expand_rows/pallas_call | solution.py:131
  25.6 0.0 slice-start.1
  25.6 1.6 %collective-permute-start.10 = (bf16[128,128]{1,0:T(8,128)(2,1)S(1)}, bf16[128,128]{1,0:T(8,128)(2,1)S(1)}, u32[]{:S(2)}, u32[]{:S(2)}) collective-permute-start(bf16[128,128]{1,0:T(8,128)(2,1)S(1)} %expand_rows.6.refs_2_), channel_id=1, source_target_pairs={{0,16},{1,17},{2,18},{3,19},{4,20},{5,21},{6,22},{7,23},{8,24},{9,... | collective-permute-start | bytes 98312 | tf_op jit(solution)/shard_map/ppermute | solution.py:22
  27.1 0.9 %expand_rows.7.refs_3_ = bf16[128,128]{1,0:T(8,128)(2,1)S(1)} custom-call(bf16[128,4224]{1,0:T(8,128)(2,1)S(1)} %slice_dynamic-update-slice_fusion.rows_ref.refs_3_, bf16[4096,1024]{1,0:T(8,128)(2,1)S(1)} %bitcast.14, bf16[4096,1024]{1,0:T(8,128)(2,1)S(1)} %bitcast.18), custom_call_target="tpu_custom_call" | custom-call | bytes 16384 | tf_op jit(solution)/shard_map/expand_rows/pallas_call | solution.py:131
  28.0 0.6 %collective-permute-start.9 = (bf16[128,128]{1,0:T(8,128)(2,1)S(1)}, bf16[128,128]{1,0:T(8,128)(2,1)S(1)}, u32[]{:S(2)}, u32[]{:S(2)}) collective-permute-start(bf16[128,128]{1,0:T(8,128)(2,1)S(1)} %expand_rows.7.refs_3_), channel_id=1, source_target_pairs={{0,16},{1,17},{2,18},{3,19},{4,20},{5,21},{6,22},{7,23},{8,24},{9,... | collective-permute-start | bytes 98312 | tf_op jit(solution)/shard_map/ppermute | solution.py:22
  28.6 0.7 %contract_hidden.6.refs_2_ = f32[128,2048]{1,0:T(8,128)S(1)} custom-call(bf16[128,384]{1,0:T(8,128)(2,1)S(1)} %expand_rows.4.refs_0_, bf16[128,384]{1,0:T(8,128)(2,1)S(1)} %expand_rows.5.refs_1_, bf16[128,128]{1,0:T(8,128)(2,1)S(1)} %expand_rows.6.refs_2_, bf16[128,128]{1,0:T(8,128)(2,1)S(1)} %expand_rows.7.refs_3_, bf16[2048,2048]{1,0:T(8,128)(2,1)S(1)} %bitcast.5), custom_call_target="tpu_custom_call" | custom-call | bytes 262144 | tf_op jit(solution)/shard_map/contract_hidden/pallas_call | solution.py:192
  29.4 0.5 contract_hidden.7.refs_2_
  29.9 0.5 contract_hidden.8.refs_2_
  30.3 0.3 contract_hidden.9.refs_2_
  30.6 1.4 %collective-permute-done.9.refs_0_ = bf16[128,128]{1,0:T(8,128)(2,1)S(1)} collective-permute-done((bf16[128,128]{1,0:T(8,128)(2,1)S(1)}, bf16[128,128]{1,0:T(8,128)(2,1)S(1)}, u32[]{:S(2)}, u32[]{:S(2)}) %collective-permute-start.9) | collective-permute-done | bytes 32800 | tf_op jit(solution)/shard_map/ppermute | solution.py:22
  32.0 0.2 contract_hidden.11
  32.3 0.1 collective-permute-start.13
  32.3 0.2 contract_hidden.10.refs_0_
  32.6 1.3 %collective-permute-done.13.refs_1_ = bf16[64,2048]{1,0:T(8,128)(2,1)S(1)} collective-permute-done((bf16[64,2048]{1,0:T(8,128)(2,1)S(1)}, bf16[64,2048]{1,0:T(8,128)(2,1)S(1)}, u32[]{:S(2)}, u32[]{:S(2)}) %collective-permute-start.13) | collective-permute-done | bytes 262176 | tf_op jit(solution)/shard_map/ppermute | solution.py:22
  33.9 0.1 sum_stage.2
  34.0 0.8 %collective-permute-start.14 = (bf16[4,4,2048]{2,1,0:T(4,128)(2,1)S(1)}, bf16[4,4,2048]{2,1,0:T(4,128)(2,1)S(1)}, u32[]{:S(2)}, u32[]{:S(2)}) collective-permute-start(bf16[4,4,2048]{2,1,0:T(4,128)(2,1)S(1)} %get-tuple-element.34), channel_id=1, source_target_pairs={{0,6},{1,7},{2,4},{3,5},{4,2},{5,3},{6,0},{7,1},{8,14},{9,15},{10,... | collective-permute-start | bytes 196616 | tf_op jit(solution)/shard_map/ppermute | solution.py:22
  34.8 1.9 %collective-permute-start.15 = (bf16[4,4,2048]{2,1,0:T(4,128)(2,1)S(1)}, bf16[4,4,2048]{2,1,0:T(4,128)(2,1)S(1)}, u32[]{:S(2)}, u32[]{:S(2)}) collective-permute-start(bf16[4,4,2048]{2,1,0:T(4,128)(2,1)S(1)} %get-tuple-element.35), channel_id=1, source_target_pairs={{0,4},{1,5},{2,6},{3,7},{4,0},{5,1},{6,2},{7,3},{8,12},{9,13},{10,... | collective-permute-start | bytes 196616 | tf_op jit(solution)/shard_map/ppermute | solution.py:22
  36.7 0.8 %collective-permute-start.16 = (bf16[4,4,2048]{2,1,0:T(4,128)(2,1)S(1)}, bf16[4,4,2048]{2,1,0:T(4,128)(2,1)S(1)}, u32[]{:S(2)}, u32[]{:S(2)}) collective-permute-start(bf16[4,4,2048]{2,1,0:T(4,128)(2,1)S(1)} %get-tuple-element.36), channel_id=1, source_target_pairs={{0,2},{1,3},{2,0},{3,1},{4,6},{5,7},{6,4},{7,5},{8,10},{9,11},{10,... | collective-permute-start | bytes 196616 | tf_op jit(solution)/shard_map/ppermute | solution.py:22
  37.5 2.4 %collective-permute-done.14.refs_1_ = bf16[4,4,2048]{2,1,0:T(4,128)(2,1)S(1)} collective-permute-done((bf16[4,4,2048]{2,1,0:T(4,128)(2,1)S(1)}, bf16[4,4,2048]{2,1,0:T(4,128)(2,1)S(1)}, u32[]{:S(2)}, u32[]{:S(2)}) %collective-permute-start.14) | collective-permute-done | bytes 65568 | tf_op jit(solution)/shard_map/ppermute | solution.py:22
  39.9 0.3 collective-permute-done.15.refs_2_
  40.2 0.8 %collective-permute-done.16.refs_3_ = bf16[4,4,2048]{2,1,0:T(4,128)(2,1)S(1)} collective-permute-done((bf16[4,4,2048]{2,1,0:T(4,128)(2,1)S(1)}, bf16[4,4,2048]{2,1,0:T(4,128)(2,1)S(1)}, u32[]{:S(2)}, u32[]{:S(2)}) %collective-permute-start.16) | collective-permute-done | bytes 65568 | tf_op jit(solution)/shard_map/ppermute | solution.py:22
  41.0 2.1 %collective-permute-start.17 = (bf16[1,4,2048]{2,1,0:T(4,128)(2,1)S(1)}, bf16[1,4,2048]{2,1,0:T(4,128)(2,1)S(1)}, u32[]{:S(2)}, u32[]{:S(2)}) collective-permute-start(bf16[1,4,2048]{2,1,0:T(4,128)(2,1)S(1)} %get-tuple-element.37), channel_id=1, source_target_pairs={{0,24},{1,25},{2,26},{3,27},{4,28},{5,29},{6,30},{7,31},{8,16},{9,... | collective-permute-start | bytes 49160 | tf_op jit(solution)/shard_map/ppermute | solution.py:22
  43.1 0.9 %collective-permute-start.18 = (bf16[1,4,2048]{2,1,0:T(4,128)(2,1)S(1)}, bf16[1,4,2048]{2,1,0:T(4,128)(2,1)S(1)}, u32[]{:S(2)}, u32[]{:S(2)}) collective-permute-start(bf16[1,4,2048]{2,1,0:T(4,128)(2,1)S(1)} %get-tuple-element.38), channel_id=1, source_target_pairs={{0,8},{1,9},{2,10},{3,11},{4,12},{5,13},{6,14},{7,15},{8,0},{9,1},... | collective-permute-start | bytes 49160 | tf_op jit(solution)/shard_map/ppermute | solution.py:22
  44.0 1.5 %collective-permute-start.19 = (bf16[1,4,2048]{2,1,0:T(4,128)(2,1)S(1)}, bf16[1,4,2048]{2,1,0:T(4,128)(2,1)S(1)}, u32[]{:S(2)}, u32[]{:S(2)}) collective-permute-start(bf16[1,4,2048]{2,1,0:T(4,128)(2,1)S(1)} %get-tuple-element.39), channel_id=1, source_target_pairs={{0,16},{1,17},{2,18},{3,19},{4,20},{5,21},{6,22},{7,23},{8,24},{9,... | collective-permute-start | bytes 49160 | tf_op jit(solution)/shard_map/ppermute | solution.py:22
  45.5 1.3 %collective-permute-done.17.refs_0_ = bf16[1,4,2048]{2,1,0:T(4,128)(2,1)S(1)} collective-permute-done((bf16[1,4,2048]{2,1,0:T(4,128)(2,1)S(1)}, bf16[1,4,2048]{2,1,0:T(4,128)(2,1)S(1)}, u32[]{:S(2)}, u32[]{:S(2)}) %collective-permute-start.17) | collective-permute-done | bytes 16416 | tf_op jit(solution)/shard_map/ppermute | solution.py:22
  46.8 1.0 %collective-permute-done.18.refs_1_ = bf16[1,4,2048]{2,1,0:T(4,128)(2,1)S(1)} collective-permute-done((bf16[1,4,2048]{2,1,0:T(4,128)(2,1)S(1)}, bf16[1,4,2048]{2,1,0:T(4,128)(2,1)S(1)}, u32[]{:S(2)}, u32[]{:S(2)}) %collective-permute-start.18) | collective-permute-done | bytes 16416 | tf_op jit(solution)/shard_map/ppermute | solution.py:22
  47.7 0.6 %finish.1 = bf16[4,4096]{1,0:T(4,128)(2,1)} custom-call(bf16[1,4,2048]{2,1,0:T(4,128)(2,1)S(1)} %collective-permute-done.17.refs_0_, bf16[1,4,2048]{2,1,0:T(4,128)(2,1)S(1)} %collective-permute-done.18.refs_1_, bf16[1,4,2048]{2,1,0:T(4,128)(2,1)S(1)} %collective-permute-done.19.refs_2_, f32[1,4,2048]{2,1,0:T(4,128)S(1)} %get-tuple-element.40.refs_3_), custom_call_target="tpu_custom_call" | custom-call | tf_op jit(solution)/shard_map/finish/pallas_call | solution.py:247
  (27 shorter events, 0.3 us)
Async XLA Ops:
  0.9 7.0 %collective-permute-start.2 = (bf16[4,4224]{1,0:T(4,128)(2,1)S(1)}, bf16[4,4224]{1,0:T(4,128)(2,1)S(1)}, u32[]{:S(2)}, u32[]{:S(2)}) collective-permute-start(bf16[4,4224]{1,0:T(4,128)(2,1)S(1)} %pack_block.1.refs_0_), channel_id=1, source_target_pairs={{0,12},{1,13},{2,14},{3,15},{4,8},{5,9},{6,10},{7,11},{8,4},{9,5},... | collective-permute-start | bytes 101384 | tf_op jit(solution)/shard_map/ppermute | solution.py:22
  6.0 4.8 %collective-permute-start.1 = (bf16[4,4224]{1,0:T(4,128)(2,1)S(1)}, bf16[4,4224]{1,0:T(4,128)(2,1)S(1)}, u32[]{:S(2)}, u32[]{:S(2)}) collective-permute-start(bf16[4,4224]{1,0:T(4,128)(2,1)S(1)} %pack_block.1.refs_0_), channel_id=1, source_target_pairs={{0,8},{1,9},{2,10},{3,11},{4,12},{5,13},{6,14},{7,15},{8,0},{9,1},... | collective-permute-start | bytes 101384 | tf_op jit(solution)/shard_map/ppermute | solution.py:22
  6.0 4.8 %collective-permute-start = (bf16[4,4224]{1,0:T(4,128)(2,1)S(1)}, bf16[4,4224]{1,0:T(4,128)(2,1)S(1)}, u32[]{:S(2)}, u32[]{:S(2)}) collective-permute-start(bf16[4,4224]{1,0:T(4,128)(2,1)S(1)} %pack_block.1.refs_0_), channel_id=1, source_target_pairs={{0,4},{1,5},{2,6},{3,7},{4,0},{5,1},{6,2},{7,3},{8,12},{9,13},{10,... | collective-permute-start | bytes 101384 | tf_op jit(solution)/shard_map/ppermute | solution.py:22
  10.8 9.6 %copy-start = (bf16[1,4096,1024]{2,1,0:T(8,128)(2,1)S(1)}, bf16[1,4096,1024]{2,1,0:T(8,128)(2,1)}, u32[]{:S(2)}) copy-start(bf16[1,4096,1024]{2,1,0:T(8,128)(2,1)} %param.9) | copy-start | bytes 25165828
  10.8 9.6 %copy-start.1 = (bf16[1,4096,1024]{2,1,0:T(8,128)(2,1)S(1)}, bf16[1,4096,1024]{2,1,0:T(8,128)(2,1)}, u32[]{:S(2)}) copy-start(bf16[1,4096,1024]{2,1,0:T(8,128)(2,1)} %param.10) | copy-start | bytes 25165828
  10.8 6.4 %collective-permute-start.3 = (bf16[4,4,4224]{2,1,0:T(4,128)(2,1)S(1)}, bf16[4,4,4224]{2,1,0:T(4,128)(2,1)S(1)}, u32[]{:S(2)}, u32[]{:S(2)}) collective-permute-start(bf16[4,4,4224]{2,1,0:T(4,128)(2,1)S(1)} %stack_blocks.1.refs_0_), channel_id=1, source_target_pairs={{0,18},{1,19},{2,16},{3,17},{4,22},{5,23},{6,20},{7,21},{8,26},{9,... | collective-permute-start | bytes 405512 | tf_op jit(solution)/shard_map/ppermute | solution.py:22
  13.3 5.3 %collective-permute-start.5 = (bf16[4,4,4224]{2,1,0:T(4,128)(2,1)S(1)}, bf16[4,4,4224]{2,1,0:T(4,128)(2,1)S(1)}, u32[]{:S(2)}, u32[]{:S(2)}) collective-permute-start(bf16[4,4,4224]{2,1,0:T(4,128)(2,1)S(1)} %stack_blocks.1.refs_0_), channel_id=1, source_target_pairs={{0,16},{1,17},{2,18},{3,19},{4,20},{5,21},{6,22},{7,23},{8,24},{9,... | collective-permute-start | bytes 405512 | tf_op jit(solution)/shard_map/ppermute | solution.py:22
  13.9 5.0 %collective-permute-start.4 = (bf16[4,4,4224]{2,1,0:T(4,128)(2,1)S(1)}, bf16[4,4,4224]{2,1,0:T(4,128)(2,1)S(1)}, u32[]{:S(2)}, u32[]{:S(2)}) collective-permute-start(bf16[4,4,4224]{2,1,0:T(4,128)(2,1)S(1)} %stack_blocks.1.refs_0_), channel_id=1, source_target_pairs={{0,2},{1,3},{2,0},{3,1},{4,6},{5,7},{6,4},{7,5},{8,10},{9,11},{10,... | collective-permute-start | bytes 405512 | tf_op jit(solution)/shard_map/ppermute | solution.py:22
  17.3 2.1 %collective-permute-start.6 = (bf16[32,4224]{1,0:T(8,128)(2,1)S(1)}, bf16[32,4224]{1,0:T(8,128)(2,1)S(1)}, u32[]{:S(2)}, u32[]{:S(2)}) collective-permute-start(bf16[32,4224]{1,0:T(8,128)(2,1)S(1)} %join_rows.3), channel_id=1, source_target_pairs={{0,1},{1,0},{2,3},{3,2},{4,5},{5,4},{6,7},{7,6},{8,9},{9,8},{10,11... | collective-permute-start | bytes 811016 | tf_op jit(solution)/shard_map/ppermute | solution.py:22
  18.7 1.7 %collective-permute-start.8 = (bf16[16,4224]{1,0:T(8,128)(2,1)S(1)}, bf16[16,4224]{1,0:T(8,128)(2,1)S(1)}, u32[]{:S(2)}, u32[]{:S(2)}) collective-permute-start(bf16[16,4224]{1,0:T(8,128)(2,1)S(1)} %join_rows.5), channel_id=1, source_target_pairs={{0,1},{1,0},{2,3},{3,2},{4,5},{5,4},{6,7},{7,6},{8,9},{9,8},{10,11... | collective-permute-start | bytes 405512 | tf_op jit(solution)/shard_map/ppermute | solution.py:22
  18.9 1.4 %collective-permute-start.7 = (bf16[16,4224]{1,0:T(8,128)(2,1)S(1)}, bf16[16,4224]{1,0:T(8,128)(2,1)S(1)}, u32[]{:S(2)}, u32[]{:S(2)}) collective-permute-start(bf16[16,4224]{1,0:T(8,128)(2,1)S(1)} %join_rows.4), channel_id=1, source_target_pairs={{0,1},{1,0},{2,3},{3,2},{4,5},{5,4},{6,7},{7,6},{8,9},{9,8},{10,11... | collective-permute-start | bytes 405512 | tf_op jit(solution)/shard_map/ppermute | solution.py:22
  21.5 7.9 %collective-permute-start.12 = (bf16[128,384]{1,0:T(8,128)(2,1)S(1)}, bf16[128,384]{1,0:T(8,128)(2,1)S(1)}, u32[]{:S(2)}, u32[]{:S(2)}) collective-permute-start(bf16[128,384]{1,0:T(8,128)(2,1)S(1)} %expand_rows.4.refs_0_), channel_id=1, source_target_pairs={{0,16},{1,17},{2,18},{3,19},{4,20},{5,21},{6,22},{7,23},{8,24},{9,... | collective-permute-start | bytes 294920 | tf_op jit(solution)/shard_map/ppermute | solution.py:22
  24.1 5.7 %collective-permute-start.11 = (bf16[128,384]{1,0:T(8,128)(2,1)S(1)}, bf16[128,384]{1,0:T(8,128)(2,1)S(1)}, u32[]{:S(2)}, u32[]{:S(2)}) collective-permute-start(bf16[128,384]{1,0:T(8,128)(2,1)S(1)} %expand_rows.5.refs_1_), channel_id=1, source_target_pairs={{0,16},{1,17},{2,18},{3,19},{4,20},{5,21},{6,22},{7,23},{8,24},{9,... | collective-permute-start | bytes 294920 | tf_op jit(solution)/shard_map/ppermute | solution.py:22
  24.7 3.9 %slice-start = ((s8[8388608]{0:T(1024)(128)(4,1)}), s8[4194304]{0:T(1024)(128)(4,1)S(1)}, s32[]{:S(2)}) async-start(s8[8388608]{0:T(1024)(128)(4,1)} %bitcast.3), calls=%async_computation | async-start | bytes 8388608
  25.6 3.1 %slice-start.1 = ((s8[8388608]{0:T(1024)(128)(4,1)}), s8[4194304]{0:T(1024)(128)(4,1)S(1)}, s32[]{:S(2)}) async-start(s8[8388608]{0:T(1024)(128)(4,1)} %bitcast.3), calls=%async_computation.1 | async-start | bytes 8388608
  25.6 4.8 %collective-permute-start.10 = (bf16[128,128]{1,0:T(8,128)(2,1)S(1)}, bf16[128,128]{1,0:T(8,128)(2,1)S(1)}, u32[]{:S(2)}, u32[]{:S(2)}) collective-permute-start(bf16[128,128]{1,0:T(8,128)(2,1)S(1)} %expand_rows.6.refs_2_), channel_id=1, source_target_pairs={{0,16},{1,17},{2,18},{3,19},{4,20},{5,21},{6,22},{7,23},{8,24},{9,... | collective-permute-start | bytes 98312 | tf_op jit(solution)/shard_map/ppermute | solution.py:22
  28.0 4.0 %collective-permute-start.9 = (bf16[128,128]{1,0:T(8,128)(2,1)S(1)}, bf16[128,128]{1,0:T(8,128)(2,1)S(1)}, u32[]{:S(2)}, u32[]{:S(2)}) collective-permute-start(bf16[128,128]{1,0:T(8,128)(2,1)S(1)} %expand_rows.7.refs_3_), channel_id=1, source_target_pairs={{0,16},{1,17},{2,18},{3,19},{4,20},{5,21},{6,22},{7,23},{8,24},{9,... | collective-permute-start | bytes 98312 | tf_op jit(solution)/shard_map/ppermute | solution.py:22
  32.3 1.6 %collective-permute-start.13 = (bf16[64,2048]{1,0:T(8,128)(2,1)S(1)}, bf16[64,2048]{1,0:T(8,128)(2,1)S(1)}, u32[]{:S(2)}, u32[]{:S(2)}) collective-permute-start(bf16[64,2048]{1,0:T(8,128)(2,1)S(1)} %contract_hidden.11), channel_id=1, source_target_pairs={{0,1},{1,0},{2,3},{3,2},{4,5},{5,4},{6,7},{7,6},{8,9},{9,8},{10,11... | collective-permute-start | bytes 786440 | tf_op jit(solution)/shard_map/ppermute | solution.py:22
  34.0 5.9 %collective-permute-start.14 = (bf16[4,4,2048]{2,1,0:T(4,128)(2,1)S(1)}, bf16[4,4,2048]{2,1,0:T(4,128)(2,1)S(1)}, u32[]{:S(2)}, u32[]{:S(2)}) collective-permute-start(bf16[4,4,2048]{2,1,0:T(4,128)(2,1)S(1)} %get-tuple-element.34), channel_id=1, source_target_pairs={{0,6},{1,7},{2,4},{3,5},{4,2},{5,3},{6,0},{7,1},{8,14},{9,15},{10,... | collective-permute-start | bytes 196616 | tf_op jit(solution)/shard_map/ppermute | solution.py:22
  34.8 5.4 %collective-permute-start.15 = (bf16[4,4,2048]{2,1,0:T(4,128)(2,1)S(1)}, bf16[4,4,2048]{2,1,0:T(4,128)(2,1)S(1)}, u32[]{:S(2)}, u32[]{:S(2)}) collective-permute-start(bf16[4,4,2048]{2,1,0:T(4,128)(2,1)S(1)} %get-tuple-element.35), channel_id=1, source_target_pairs={{0,4},{1,5},{2,6},{3,7},{4,0},{5,1},{6,2},{7,3},{8,12},{9,13},{10,... | collective-permute-start | bytes 196616 | tf_op jit(solution)/shard_map/ppermute | solution.py:22
  36.7 4.3 %collective-permute-start.16 = (bf16[4,4,2048]{2,1,0:T(4,128)(2,1)S(1)}, bf16[4,4,2048]{2,1,0:T(4,128)(2,1)S(1)}, u32[]{:S(2)}, u32[]{:S(2)}) collective-permute-start(bf16[4,4,2048]{2,1,0:T(4,128)(2,1)S(1)} %get-tuple-element.36), channel_id=1, source_target_pairs={{0,2},{1,3},{2,0},{3,1},{4,6},{5,7},{6,4},{7,5},{8,10},{9,11},{10,... | collective-permute-start | bytes 196616 | tf_op jit(solution)/shard_map/ppermute | solution.py:22
  41.0 5.8 %collective-permute-start.17 = (bf16[1,4,2048]{2,1,0:T(4,128)(2,1)S(1)}, bf16[1,4,2048]{2,1,0:T(4,128)(2,1)S(1)}, u32[]{:S(2)}, u32[]{:S(2)}) collective-permute-start(bf16[1,4,2048]{2,1,0:T(4,128)(2,1)S(1)} %get-tuple-element.37), channel_id=1, source_target_pairs={{0,24},{1,25},{2,26},{3,27},{4,28},{5,29},{6,30},{7,31},{8,16},{9,... | collective-permute-start | bytes 49160 | tf_op jit(solution)/shard_map/ppermute | solution.py:22
  43.1 4.6 %collective-permute-start.18 = (bf16[1,4,2048]{2,1,0:T(4,128)(2,1)S(1)}, bf16[1,4,2048]{2,1,0:T(4,128)(2,1)S(1)}, u32[]{:S(2)}, u32[]{:S(2)}) collective-permute-start(bf16[1,4,2048]{2,1,0:T(4,128)(2,1)S(1)} %get-tuple-element.38), channel_id=1, source_target_pairs={{0,8},{1,9},{2,10},{3,11},{4,12},{5,13},{6,14},{7,15},{8,0},{9,1},... | collective-permute-start | bytes 49160 | tf_op jit(solution)/shard_map/ppermute | solution.py:22
  44.0 3.8 %collective-permute-start.19 = (bf16[1,4,2048]{2,1,0:T(4,128)(2,1)S(1)}, bf16[1,4,2048]{2,1,0:T(4,128)(2,1)S(1)}, u32[]{:S(2)}, u32[]{:S(2)}) collective-permute-start(bf16[1,4,2048]{2,1,0:T(4,128)(2,1)S(1)} %get-tuple-element.39), channel_id=1, source_target_pairs={{0,16},{1,17},{2,18},{3,19},{4,20},{5,21},{6,22},{7,23},{8,24},{9,... | collective-permute-start | bytes 49160 | tf_op jit(solution)/shard_map/ppermute | solution.py:22

commit v24 on v19

--- a/solution.py
+++ b/solution.py
@@ -266,13 +266,14 @@
     near = stack_blocks([block] + [swap(block, 0, 4 * i) for i in range(1, high)])
     if wide > 1:
         near = jnp.concatenate([near] + [swap(near, 2 * i, 0) for i in range(1, wide)])
-    over_x, over_y = swap(near, 1, 0), swap(near, 0, 2)
-    first = join_rows([near, swap(near, 1, 2)])
+    over_x, over_y = swap(near, 1, 1), swap(near, 0, 3)
+    first = join_rows([near, swap(near, 1, 3)])
     pieces = [first, join_rows([over_x]), join_rows([over_y])]
     size = pieces[1].shape[0]
+    here, there = pieces, [swap(piece, 0, 1) for piece in pieces]
     rows = []
-    for first, x, y in (pieces, [swap(piece, 0, 1) for piece in pieces]):
-        rows += [first[:size], y, x, first[size:]]
+    for near, (first, x, y) in ((here[0], there), (there[0], here)):
+        rows += [near[:size], y, x, first[size:]]
     rows = jnp.concatenate(rows)
 
     eighth = units // 8

time: 47.5 us -> 48.7 us (1.025)
  waiting for transfers between devices: 18.4 us -> 19.9 us
    ppermute x19, waiting for transfers between devices: 18.4 us -> 19.9 us  [swap(): return lax.ppermute(value, ('dp',) + EXPERT, pairs)]
  transfers between devices with their start and end apart: 19 -> 19, of which waited for: 14 -> 12; matrix products, arithmetic and copies ran while one was open for 0% -> 0% of each run, Pallas kernels for 8% -> 8%
where the time goes in v24:
time: 48.7 us; the launch traced here: 48.5 us
  starting transfers between devices  21.3 us (44%)
  waiting for transfers between devices  19.9 us (41%)
  Pallas kernels  6.98 us (14%)
    ppermute x19, starting transfers between devices, swap(): return lax.ppermute(value, ('dp',) + EXPERT, pairs)  21.3 us
    ppermute x19, waiting for transfers between devices, swap(): return lax.ppermute(value, ('dp',) + EXPERT, pairs)  19.9 us
    pallas_call x3, Pallas kernels, expand_rows(): pl.pallas_call(body, out_shape=jax.ShapeDtypeStruct((count, columns), row...  2.91 us
    pallas_call x5, Pallas kernels, contract_hidden(): pl.pallas_call(body, out_shape=jax.ShapeDtypeStruct((count, width), kind)...  2.27 us
  transfers between devices with their start and end apart: 19, of which 12 were waited for; matrix products, arithmetic and copies ran while one was open for 0% of the time, Pallas kernels for 8%

profile of v24, /device:TPU:0, one launch (start us, length us, event | category | flops | bytes accessed | tf_op | source)
XLA Modules:
  0.0 48.5 jit_solution(6721750329248865992)
XLA Ops:
  0.0 0.9 %pack_block.1.refs_0_ = bf16[4,4224]{1,0:T(4,128)(2,1)S(1)} custom-call(bf16[4,4096]{1,0:T(4,128)(2,1)} %tokens_ref.1, s32[4,8]{1,0:T(4,128)} %ids_ref.1, f32[4,8]{1,0:T(4,128)} %probs_ref.1), custom_call_target="tpu_custom_call" | custom-call | tf_op jit(solution)/shard_map/pack_block/pallas_call | solution.py:62
  0.9 5.1 %collective-permute-start.2 = (bf16[4,4224]{1,0:T(4,128)(2,1)S(1)}, bf16[4,4224]{1,0:T(4,128)(2,1)S(1)}, u32[]{:S(2)}, u32[]{:S(2)}) collective-permute-start(bf16[4,4224]{1,0:T(4,128)(2,1)S(1)} %pack_block.1.refs_0_), channel_id=1, source_target_pairs={{0,12},{1,13},{2,14},{3,15},{4,8},{5,9},{6,10},{7,11},{8,4},{9,5},... | collective-permute-start | bytes 101384 | tf_op jit(solution)/shard_map/ppermute | solution.py:22
  6.0 0.6 %collective-permute-start = (bf16[4,4224]{1,0:T(4,128)(2,1)S(1)}, bf16[4,4224]{1,0:T(4,128)(2,1)S(1)}, u32[]{:S(2)}, u32[]{:S(2)}) collective-permute-start(bf16[4,4224]{1,0:T(4,128)(2,1)S(1)} %pack_block.1.refs_0_), channel_id=1, source_target_pairs={{0,4},{1,5},{2,6},{3,7},{4,0},{5,1},{6,2},{7,3},{8,12},{9,13},{10,... | collective-permute-start | bytes 101384 | tf_op jit(solution)/shard_map/ppermute | solution.py:22
  6.6 1.3 %collective-permute-done.2.refs_3_ = bf16[4,4224]{1,0:T(4,128)(2,1)S(1)} collective-permute-done((bf16[4,4224]{1,0:T(4,128)(2,1)S(1)}, bf16[4,4224]{1,0:T(4,128)(2,1)S(1)}, u32[]{:S(2)}, u32[]{:S(2)}) %collective-permute-start.2) | collective-permute-done | bytes 33824 | tf_op jit(solution)/shard_map/ppermute | solution.py:22
  7.9 2.9 %collective-permute-done.1.refs_2_ = bf16[4,4224]{1,0:T(4,128)(2,1)S(1)} collective-permute-done((bf16[4,4224]{1,0:T(4,128)(2,1)S(1)}, bf16[4,4224]{1,0:T(4,128)(2,1)S(1)}, u32[]{:S(2)}, u32[]{:S(2)}) %collective-permute-start.1) | collective-permute-done | bytes 33824 | tf_op jit(solution)/shard_map/ppermute | solution.py:22
  10.8 0.1 collective-permute-start.4
  10.9 2.7 %collective-permute-start.3 = (bf16[4,4,4224]{2,1,0:T(4,128)(2,1)S(1)}, bf16[4,4,4224]{2,1,0:T(4,128)(2,1)S(1)}, u32[]{:S(2)}, u32[]{:S(2)}) collective-permute-start(bf16[4,4,4224]{2,1,0:T(4,128)(2,1)S(1)} %stack_blocks.1.refs_0_), channel_id=1, source_target_pairs={{0,19},{1,18},{2,17},{3,16},{4,23},{5,22},{6,21},{7,20},{8,27},{9,... | collective-permute-start | bytes 405512 | tf_op jit(solution)/shard_map/ppermute | solution.py:22
  13.6 0.1 collective-permute-start.6
  13.7 5.9 %collective-permute-done.4.refs_0_ = bf16[4,4,4224]{2,1,0:T(4,128)(2,1)S(1)} collective-permute-done((bf16[4,4,4224]{2,1,0:T(4,128)(2,1)S(1)}, bf16[4,4,4224]{2,1,0:T(4,128)(2,1)S(1)}, u32[]{:S(2)}, u32[]{:S(2)}) %collective-permute-start.4) | collective-permute-done | bytes 135200 | tf_op jit(solution)/shard_map/ppermute | solution.py:22
  19.6 0.3 collective-permute-start.5
  19.9 0.1 join_rows.3
  20.0 0.4 collective-permute-start.8
  20.4 0.0 collective-permute-done.6.refs_0_
  20.4 0.3 collective-permute-start.7
  20.7 0.4 collective-permute-done.5
  21.1 0.8 %collective-permute-done.7 = bf16[16,4224]{1,0:T(8,128)(2,1)S(1)} collective-permute-done((bf16[16,4224]{1,0:T(8,128)(2,1)S(1)}, bf16[16,4224]{1,0:T(8,128)(2,1)S(1)}, u32[]{:S(2)}, u32[]{:S(2)}) %collective-permute-start.7) | collective-permute-done | bytes 135200 | tf_op jit(solution)/shard_map/ppermute | solution.py:22
  22.0 0.0 slice-start
  22.0 1.1 %expand_rows.3.refs_0_ = bf16[128,384]{1,0:T(8,128)(2,1)S(1)} custom-call(bf16[128,4224]{1,0:T(8,128)(2,1)S(1)} %slice_dynamic-update-slice_fusion.rows_ref.refs_3_, bf16[4096,1024]{1,0:T(8,128)(2,1)S(1)} %bitcast.10, bf16[4096,1024]{1,0:T(8,128)(2,1)S(1)} %bitcast.13), custom_call_target="tpu_custom_call" | custom-call | bytes 49152 | tf_op jit(solution)/shard_map/expand_rows/pallas_call | solution.py:131
  23.1 0.0 slice-start.1
  23.1 1.6 %collective-permute-start.11 = (bf16[128,384]{1,0:T(8,128)(2,1)S(1)}, bf16[128,384]{1,0:T(8,128)(2,1)S(1)}, u32[]{:S(2)}, u32[]{:S(2)}) collective-permute-start(bf16[128,384]{1,0:T(8,128)(2,1)S(1)} %expand_rows.3.refs_0_), channel_id=1, source_target_pairs={{0,16},{1,17},{2,18},{3,19},{4,20},{5,21},{6,22},{7,23},{8,24},{9,... | collective-permute-start | bytes 294920 | tf_op jit(solution)/shard_map/ppermute | solution.py:22
  24.7 1.1 %expand_rows.4.refs_1_ = bf16[128,384]{1,0:T(8,128)(2,1)S(1)} custom-call(bf16[128,4224]{1,0:T(8,128)(2,1)S(1)} %slice_dynamic-update-slice_fusion.rows_ref.refs_3_, bf16[4096,1024]{1,0:T(8,128)(2,1)S(1)} %bitcast.11, bf16[4096,1024]{1,0:T(8,128)(2,1)S(1)} %bitcast.14), custom_call_target="tpu_custom_call" | custom-call | bytes 49152 | tf_op jit(solution)/shard_map/expand_rows/pallas_call | solution.py:131
  25.7 0.6 %collective-permute-start.10 = (bf16[128,384]{1,0:T(8,128)(2,1)S(1)}, bf16[128,384]{1,0:T(8,128)(2,1)S(1)}, u32[]{:S(2)}, u32[]{:S(2)}) collective-permute-start(bf16[128,384]{1,0:T(8,128)(2,1)S(1)} %expand_rows.4.refs_1_), channel_id=1, source_target_pairs={{0,16},{1,17},{2,18},{3,19},{4,20},{5,21},{6,22},{7,23},{8,24},{9,... | collective-permute-start | bytes 294920 | tf_op jit(solution)/shard_map/ppermute | solution.py:22
  26.4 0.8 %expand_rows.5.refs_2_ = bf16[128,256]{1,0:T(8,128)(2,1)S(1)} custom-call(bf16[128,4224]{1,0:T(8,128)(2,1)S(1)} %slice_dynamic-update-slice_fusion.rows_ref.refs_3_, bf16[4096,1024]{1,0:T(8,128)(2,1)S(1)} %bitcast.12, bf16[4096,1024]{1,0:T(8,128)(2,1)S(1)} %bitcast.15), custom_call_target="tpu_custom_call" | custom-call | bytes 32768 | tf_op jit(solution)/shard_map/expand_rows/pallas_call | solution.py:131
  27.1 1.5 %collective-permute-start.9 = (bf16[128,256]{1,0:T(8,128)(2,1)S(1)}, bf16[128,256]{1,0:T(8,128)(2,1)S(1)}, u32[]{:S(2)}, u32[]{:S(2)}) collective-permute-start(bf16[128,256]{1,0:T(8,128)(2,1)S(1)} %expand_rows.5.refs_2_), channel_id=1, source_target_pairs={{0,16},{1,17},{2,18},{3,19},{4,20},{5,21},{6,22},{7,23},{8,24},{9,... | collective-permute-start | bytes 196616 | tf_op jit(solution)/shard_map/ppermute | solution.py:22
  28.7 0.7 %contract_hidden.5.refs_2_ = f32[128,2048]{1,0:T(8,128)S(1)} custom-call(bf16[128,384]{1,0:T(8,128)(2,1)S(1)} %expand_rows.3.refs_0_, bf16[128,384]{1,0:T(8,128)(2,1)S(1)} %expand_rows.4.refs_1_, bf16[128,256]{1,0:T(8,128)(2,1)S(1)} %expand_rows.5.refs_2_, bf16[2048,2048]{1,0:T(8,128)(2,1)S(1)} %bitcast.5), custom_call_target="tpu_custom_call" | custom-call | bytes 262144 | tf_op jit(solution)/shard_map/contract_hidden/pallas_call | solution.py:192
  29.4 0.0 collective-permute-done.11.refs_0_
  29.4 0.5 contract_hidden.6.refs_2_
  29.9 1.3 %collective-permute-done.10.refs_0_ = bf16[128,384]{1,0:T(8,128)(2,1)S(1)} collective-permute-done((bf16[128,384]{1,0:T(8,128)(2,1)S(1)}, bf16[128,384]{1,0:T(8,128)(2,1)S(1)}, u32[]{:S(2)}, u32[]{:S(2)}) %collective-permute-start.10) | collective-permute-done | bytes 98336 | tf_op jit(solution)/shard_map/ppermute | solution.py:22
  31.2 0.5 contract_hidden.7.refs_2_
  31.7 0.2 collective-permute-done.9.refs_0_
  31.9 0.3 contract_hidden.9
  32.2 0.1 collective-permute-start.12
  32.3 0.3 contract_hidden.8.refs_0_
  32.6 1.2 %collective-permute-done.12.refs_1_ = bf16[64,2048]{1,0:T(8,128)(2,1)S(1)} collective-permute-done((bf16[64,2048]{1,0:T(8,128)(2,1)S(1)}, bf16[64,2048]{1,0:T(8,128)(2,1)S(1)}, u32[]{:S(2)}, u32[]{:S(2)}) %collective-permute-start.12) | collective-permute-done | bytes 262176 | tf_op jit(solution)/shard_map/ppermute | solution.py:22
  33.8 0.1 sum_stage.2
  33.9 0.1 collective-permute-start.13
  34.0 2.1 %collective-permute-start.14 = (bf16[4,4,2048]{2,1,0:T(4,128)(2,1)S(1)}, bf16[4,4,2048]{2,1,0:T(4,128)(2,1)S(1)}, u32[]{:S(2)}, u32[]{:S(2)}) collective-permute-start(bf16[4,4,2048]{2,1,0:T(4,128)(2,1)S(1)} %get-tuple-element.31), channel_id=1, source_target_pairs={{0,4},{1,5},{2,6},{3,7},{4,0},{5,1},{6,2},{7,3},{8,12},{9,13},{10,... | collective-permute-start | bytes 196616 | tf_op jit(solution)/shard_map/ppermute | solution.py:22
  36.1 1.4 %collective-permute-start.15 = (bf16[4,4,2048]{2,1,0:T(4,128)(2,1)S(1)}, bf16[4,4,2048]{2,1,0:T(4,128)(2,1)S(1)}, u32[]{:S(2)}, u32[]{:S(2)}) collective-permute-start(bf16[4,4,2048]{2,1,0:T(4,128)(2,1)S(1)} %get-tuple-element.32), channel_id=1, source_target_pairs={{0,2},{1,3},{2,0},{3,1},{4,6},{5,7},{6,4},{7,5},{8,10},{9,11},{10,... | collective-permute-start | bytes 196616 | tf_op jit(solution)/shard_map/ppermute | solution.py:22
  37.5 2.3 %collective-permute-done.13.refs_1_ = bf16[4,4,2048]{2,1,0:T(4,128)(2,1)S(1)} collective-permute-done((bf16[4,4,2048]{2,1,0:T(4,128)(2,1)S(1)}, bf16[4,4,2048]{2,1,0:T(4,128)(2,1)S(1)}, u32[]{:S(2)}, u32[]{:S(2)}) %collective-permute-start.13) | collective-permute-done | bytes 65568 | tf_op jit(solution)/shard_map/ppermute | solution.py:22
  39.7 0.0 collective-permute-done.14.refs_2_
  39.7 0.7 %collective-permute-done.15.refs_3_ = bf16[4,4,2048]{2,1,0:T(4,128)(2,1)S(1)} collective-permute-done((bf16[4,4,2048]{2,1,0:T(4,128)(2,1)S(1)}, bf16[4,4,2048]{2,1,0:T(4,128)(2,1)S(1)}, u32[]{:S(2)}, u32[]{:S(2)}) %collective-permute-start.15) | collective-permute-done | bytes 65568 | tf_op jit(solution)/shard_map/ppermute | solution.py:22
  40.5 2.8 %collective-permute-start.16 = (bf16[1,4,2048]{2,1,0:T(4,128)(2,1)S(1)}, bf16[1,4,2048]{2,1,0:T(4,128)(2,1)S(1)}, u32[]{:S(2)}, u32[]{:S(2)}) collective-permute-start(bf16[1,4,2048]{2,1,0:T(4,128)(2,1)S(1)} %get-tuple-element.33), channel_id=1, source_target_pairs={{0,24},{1,25},{2,26},{3,27},{4,28},{5,29},{6,30},{7,31},{8,16},{9,... | collective-permute-start | bytes 49160 | tf_op jit(solution)/shard_map/ppermute | solution.py:22
  43.2 0.9 %collective-permute-start.17 = (bf16[1,4,2048]{2,1,0:T(4,128)(2,1)S(1)}, bf16[1,4,2048]{2,1,0:T(4,128)(2,1)S(1)}, u32[]{:S(2)}, u32[]{:S(2)}) collective-permute-start(bf16[1,4,2048]{2,1,0:T(4,128)(2,1)S(1)} %get-tuple-element.34), channel_id=1, source_target_pairs={{0,8},{1,9},{2,10},{3,11},{4,12},{5,13},{6,14},{7,15},{8,0},{9,1},... | collective-permute-start | bytes 49160 | tf_op jit(solution)/shard_map/ppermute | solution.py:22
  44.1 0.8 %collective-permute-start.18 = (bf16[1,4,2048]{2,1,0:T(4,128)(2,1)S(1)}, bf16[1,4,2048]{2,1,0:T(4,128)(2,1)S(1)}, u32[]{:S(2)}, u32[]{:S(2)}) collective-permute-start(bf16[1,4,2048]{2,1,0:T(4,128)(2,1)S(1)} %get-tuple-element.35), channel_id=1, source_target_pairs={{0,16},{1,17},{2,18},{3,19},{4,20},{5,21},{6,22},{7,23},{8,24},{9,... | collective-permute-start | bytes 49160 | tf_op jit(solution)/shard_map/ppermute | solution.py:22
  44.9 1.4 %collective-permute-done.16.refs_0_ = bf16[1,4,2048]{2,1,0:T(4,128)(2,1)S(1)} collective-permute-done((bf16[1,4,2048]{2,1,0:T(4,128)(2,1)S(1)}, bf16[1,4,2048]{2,1,0:T(4,128)(2,1)S(1)}, u32[]{:S(2)}, u32[]{:S(2)}) %collective-permute-start.16) | collective-permute-done | bytes 16416 | tf_op jit(solution)/shard_map/ppermute | solution.py:22
  46.3 1.5 %collective-permute-done.17.refs_1_ = bf16[1,4,2048]{2,1,0:T(4,128)(2,1)S(1)} collective-permute-done((bf16[1,4,2048]{2,1,0:T(4,128)(2,1)S(1)}, bf16[1,4,2048]{2,1,0:T(4,128)(2,1)S(1)}, u32[]{:S(2)}, u32[]{:S(2)}) %collective-permute-start.17) | collective-permute-done | bytes 16416 | tf_op jit(solution)/shard_map/ppermute | solution.py:22
  47.9 0.0 collective-permute-done.18.refs_2_
  47.9 0.6 %finish.1 = bf16[4,4096]{1,0:T(4,128)(2,1)} custom-call(bf16[1,4,2048]{2,1,0:T(4,128)(2,1)S(1)} %collective-permute-done.16.refs_0_, bf16[1,4,2048]{2,1,0:T(4,128)(2,1)S(1)} %collective-permute-done.17.refs_1_, bf16[1,4,2048]{2,1,0:T(4,128)(2,1)S(1)} %collective-permute-done.18.refs_2_, f32[1,4,2048]{2,1,0:T(4,128)S(1)} %get-tuple-element.36.refs_3_), custom_call_target="tpu_custom_call" | custom-call | tf_op jit(solution)/shard_map/finish/pallas_call | solution.py:247
  (23 shorter events, 0.3 us)
Async XLA Ops:
  0.9 7.0 %collective-permute-start.2 = (bf16[4,4224]{1,0:T(4,128)(2,1)S(1)}, bf16[4,4224]{1,0:T(4,128)(2,1)S(1)}, u32[]{:S(2)}, u32[]{:S(2)}) collective-permute-start(bf16[4,4224]{1,0:T(4,128)(2,1)S(1)} %pack_block.1.refs_0_), channel_id=1, source_target_pairs={{0,12},{1,13},{2,14},{3,15},{4,8},{5,9},{6,10},{7,11},{8,4},{9,5},... | collective-permute-start | bytes 101384 | tf_op jit(solution)/shard_map/ppermute | solution.py:22
  6.0 4.8 %collective-permute-start.1 = (bf16[4,4224]{1,0:T(4,128)(2,1)S(1)}, bf16[4,4224]{1,0:T(4,128)(2,1)S(1)}, u32[]{:S(2)}, u32[]{:S(2)}) collective-permute-start(bf16[4,4224]{1,0:T(4,128)(2,1)S(1)} %pack_block.1.refs_0_), channel_id=1, source_target_pairs={{0,8},{1,9},{2,10},{3,11},{4,12},{5,13},{6,14},{7,15},{8,0},{9,1},... | collective-permute-start | bytes 101384 | tf_op jit(solution)/shard_map/ppermute | solution.py:22
  6.0 4.8 %collective-permute-start = (bf16[4,4224]{1,0:T(4,128)(2,1)S(1)}, bf16[4,4224]{1,0:T(4,128)(2,1)S(1)}, u32[]{:S(2)}, u32[]{:S(2)}) collective-permute-start(bf16[4,4224]{1,0:T(4,128)(2,1)S(1)} %pack_block.1.refs_0_), channel_id=1, source_target_pairs={{0,4},{1,5},{2,6},{3,7},{4,0},{5,1},{6,2},{7,3},{8,12},{9,13},{10,... | collective-permute-start | bytes 101384 | tf_op jit(solution)/shard_map/ppermute | solution.py:22
  10.8 11.2 %copy-start = (bf16[1,4096,1024]{2,1,0:T(8,128)(2,1)S(1)}, bf16[1,4096,1024]{2,1,0:T(8,128)(2,1)}, u32[]{:S(2)}) copy-start(bf16[1,4096,1024]{2,1,0:T(8,128)(2,1)} %param.9) | copy-start | bytes 25165828
  10.8 11.2 %copy-start.1 = (bf16[1,4096,1024]{2,1,0:T(8,128)(2,1)S(1)}, bf16[1,4096,1024]{2,1,0:T(8,128)(2,1)}, u32[]{:S(2)}) copy-start(bf16[1,4096,1024]{2,1,0:T(8,128)(2,1)} %param.10) | copy-start | bytes 25165828
  10.8 8.8 %collective-permute-start.4 = (bf16[4,4,4224]{2,1,0:T(4,128)(2,1)S(1)}, bf16[4,4,4224]{2,1,0:T(4,128)(2,1)S(1)}, u32[]{:S(2)}, u32[]{:S(2)}) collective-permute-start(bf16[4,4,4224]{2,1,0:T(4,128)(2,1)S(1)} %stack_blocks.1.refs_0_), channel_id=1, source_target_pairs={{0,3},{1,2},{2,1},{3,0},{4,7},{5,6},{6,5},{7,4},{8,11},{9,10},{10,... | collective-permute-start | bytes 405512 | tf_op jit(solution)/shard_map/ppermute | solution.py:22
  10.9 9.0 %collective-permute-start.3 = (bf16[4,4,4224]{2,1,0:T(4,128)(2,1)S(1)}, bf16[4,4,4224]{2,1,0:T(4,128)(2,1)S(1)}, u32[]{:S(2)}, u32[]{:S(2)}) collective-permute-start(bf16[4,4,4224]{2,1,0:T(4,128)(2,1)S(1)} %stack_blocks.1.refs_0_), channel_id=1, source_target_pairs={{0,19},{1,18},{2,17},{3,16},{4,23},{5,22},{6,21},{7,20},{8,27},{9,... | collective-permute-start | bytes 405512 | tf_op jit(solution)/shard_map/ppermute | solution.py:22
  13.6 6.8 %collective-permute-start.6 = (bf16[4,4,4224]{2,1,0:T(4,128)(2,1)S(1)}, bf16[4,4,4224]{2,1,0:T(4,128)(2,1)S(1)}, u32[]{:S(2)}, u32[]{:S(2)}) collective-permute-start(bf16[4,4,4224]{2,1,0:T(4,128)(2,1)S(1)} %stack_blocks.1.refs_0_), channel_id=1, source_target_pairs={{0,17},{1,16},{2,19},{3,18},{4,21},{5,20},{6,23},{7,22},{8,25},{9,... | collective-permute-start | bytes 405512 | tf_op jit(solution)/shard_map/ppermute | solution.py:22
  19.6 1.4 %collective-permute-start.5 = (bf16[16,4224]{1,0:T(8,128)(2,1)S(1)}, bf16[16,4224]{1,0:T(8,128)(2,1)S(1)}, u32[]{:S(2)}, u32[]{:S(2)}) collective-permute-start(bf16[16,4224]{1,0:T(8,128)(2,1)S(1)} %join_rows.4), channel_id=1, source_target_pairs={{0,1},{1,0},{2,3},{3,2},{4,5},{5,4},{6,7},{7,6},{8,9},{9,8},{10,11... | collective-permute-start | bytes 405512 | tf_op jit(solution)/shard_map/ppermute | solution.py:22
  20.0 1.9 %collective-permute-start.8 = (bf16[32,4224]{1,0:T(8,128)(2,1)S(1)}, bf16[32,4224]{1,0:T(8,128)(2,1)S(1)}, u32[]{:S(2)}, u32[]{:S(2)}) collective-permute-start(bf16[32,4224]{1,0:T(8,128)(2,1)S(1)} %join_rows.3), channel_id=1, source_target_pairs={{0,1},{1,0},{2,3},{3,2},{4,5},{5,4},{6,7},{7,6},{8,9},{9,8},{10,11... | collective-permute-start | bytes 811016 | tf_op jit(solution)/shard_map/ppermute | solution.py:22
  20.4 1.4 %collective-permute-start.7 = (bf16[16,4224]{1,0:T(8,128)(2,1)S(1)}, bf16[16,4224]{1,0:T(8,128)(2,1)S(1)}, u32[]{:S(2)}, u32[]{:S(2)}) collective-permute-start(bf16[16,4224]{1,0:T(8,128)(2,1)S(1)} %join_rows.5), channel_id=1, source_target_pairs={{0,1},{1,0},{2,3},{3,2},{4,5},{5,4},{6,7},{7,6},{8,9},{9,8},{10,11... | collective-permute-start | bytes 405512 | tf_op jit(solution)/shard_map/ppermute | solution.py:22
  22.0 6.7 %slice-start = ((s8[8388608]{0:T(1024)(128)(4,1)}), s8[4194304]{0:T(1024)(128)(4,1)S(1)}, s32[]{:S(2)}) async-start(s8[8388608]{0:T(1024)(128)(4,1)} %bitcast.3), calls=%async_computation | async-start | bytes 8388608
  23.1 5.6 %slice-start.1 = ((s8[8388608]{0:T(1024)(128)(4,1)}), s8[4194304]{0:T(1024)(128)(4,1)S(1)}, s32[]{:S(2)}) async-start(s8[8388608]{0:T(1024)(128)(4,1)} %bitcast.3), calls=%async_computation.1 | async-start | bytes 8388608
  23.1 6.3 %collective-permute-start.11 = (bf16[128,384]{1,0:T(8,128)(2,1)S(1)}, bf16[128,384]{1,0:T(8,128)(2,1)S(1)}, u32[]{:S(2)}, u32[]{:S(2)}) collective-permute-start(bf16[128,384]{1,0:T(8,128)(2,1)S(1)} %expand_rows.3.refs_0_), channel_id=1, source_target_pairs={{0,16},{1,17},{2,18},{3,19},{4,20},{5,21},{6,22},{7,23},{8,24},{9,... | collective-permute-start | bytes 294920 | tf_op jit(solution)/shard_map/ppermute | solution.py:22
  25.7 5.5 %collective-permute-start.10 = (bf16[128,384]{1,0:T(8,128)(2,1)S(1)}, bf16[128,384]{1,0:T(8,128)(2,1)S(1)}, u32[]{:S(2)}, u32[]{:S(2)}) collective-permute-start(bf16[128,384]{1,0:T(8,128)(2,1)S(1)} %expand_rows.4.refs_1_), channel_id=1, source_target_pairs={{0,16},{1,17},{2,18},{3,19},{4,20},{5,21},{6,22},{7,23},{8,24},{9,... | collective-permute-start | bytes 294920 | tf_op jit(solution)/shard_map/ppermute | solution.py:22
  27.1 4.8 %collective-permute-start.9 = (bf16[128,256]{1,0:T(8,128)(2,1)S(1)}, bf16[128,256]{1,0:T(8,128)(2,1)S(1)}, u32[]{:S(2)}, u32[]{:S(2)}) collective-permute-start(bf16[128,256]{1,0:T(8,128)(2,1)S(1)} %expand_rows.5.refs_2_), channel_id=1, source_target_pairs={{0,16},{1,17},{2,18},{3,19},{4,20},{5,21},{6,22},{7,23},{8,24},{9,... | collective-permute-start | bytes 196616 | tf_op jit(solution)/shard_map/ppermute | solution.py:22
  32.2 1.6 %collective-permute-start.12 = (bf16[64,2048]{1,0:T(8,128)(2,1)S(1)}, bf16[64,2048]{1,0:T(8,128)(2,1)S(1)}, u32[]{:S(2)}, u32[]{:S(2)}) collective-permute-start(bf16[64,2048]{1,0:T(8,128)(2,1)S(1)} %contract_hidden.9), channel_id=1, source_target_pairs={{0,1},{1,0},{2,3},{3,2},{4,5},{5,4},{6,7},{7,6},{8,9},{9,8},{10,11... | collective-permute-start | bytes 786440 | tf_op jit(solution)/shard_map/ppermute | solution.py:22
  33.9 5.8 %collective-permute-start.13 = (bf16[4,4,2048]{2,1,0:T(4,128)(2,1)S(1)}, bf16[4,4,2048]{2,1,0:T(4,128)(2,1)S(1)}, u32[]{:S(2)}, u32[]{:S(2)}) collective-permute-start(bf16[4,4,2048]{2,1,0:T(4,128)(2,1)S(1)} %get-tuple-element.30), channel_id=1, source_target_pairs={{0,6},{1,7},{2,4},{3,5},{4,2},{5,3},{6,0},{7,1},{8,14},{9,15},{10,... | collective-permute-start | bytes 196616 | tf_op jit(solution)/shard_map/ppermute | solution.py:22
  34.0 5.7 %collective-permute-start.14 = (bf16[4,4,2048]{2,1,0:T(4,128)(2,1)S(1)}, bf16[4,4,2048]{2,1,0:T(4,128)(2,1)S(1)}, u32[]{:S(2)}, u32[]{:S(2)}) collective-permute-start(bf16[4,4,2048]{2,1,0:T(4,128)(2,1)S(1)} %get-tuple-element.31), channel_id=1, source_target_pairs={{0,4},{1,5},{2,6},{3,7},{4,0},{5,1},{6,2},{7,3},{8,12},{9,13},{10,... | collective-permute-start | bytes 196616 | tf_op jit(solution)/shard_map/ppermute | solution.py:22
  36.1 4.3 %collective-permute-start.15 = (bf16[4,4,2048]{2,1,0:T(4,128)(2,1)S(1)}, bf16[4,4,2048]{2,1,0:T(4,128)(2,1)S(1)}, u32[]{:S(2)}, u32[]{:S(2)}) collective-permute-start(bf16[4,4,2048]{2,1,0:T(4,128)(2,1)S(1)} %get-tuple-element.32), channel_id=1, source_target_pairs={{0,2},{1,3},{2,0},{3,1},{4,6},{5,7},{6,4},{7,5},{8,10},{9,11},{10,... | collective-permute-start | bytes 196616 | tf_op jit(solution)/shard_map/ppermute | solution.py:22
  40.5 5.9 %collective-permute-start.16 = (bf16[1,4,2048]{2,1,0:T(4,128)(2,1)S(1)}, bf16[1,4,2048]{2,1,0:T(4,128)(2,1)S(1)}, u32[]{:S(2)}, u32[]{:S(2)}) collective-permute-start(bf16[1,4,2048]{2,1,0:T(4,128)(2,1)S(1)} %get-tuple-element.33), channel_id=1, source_target_pairs={{0,24},{1,25},{2,26},{3,27},{4,28},{5,29},{6,30},{7,31},{8,16},{9,... | collective-permute-start | bytes 49160 | tf_op jit(solution)/shard_map/ppermute | solution.py:22
  43.2 4.6 %collective-permute-start.17 = (bf16[1,4,2048]{2,1,0:T(4,128)(2,1)S(1)}, bf16[1,4,2048]{2,1,0:T(4,128)(2,1)S(1)}, u32[]{:S(2)}, u32[]{:S(2)}) collective-permute-start(bf16[1,4,2048]{2,1,0:T(4,128)(2,1)S(1)} %get-tuple-element.34), channel_id=1, source_target_pairs={{0,8},{1,9},{2,10},{3,11},{4,12},{5,13},{6,14},{7,15},{8,0},{9,1},... | collective-permute-start | bytes 49160 | tf_op jit(solution)/shard_map/ppermute | solution.py:22
  44.1 3.7 %collective-permute-start.18 = (bf16[1,4,2048]{2,1,0:T(4,128)(2,1)S(1)}, bf16[1,4,2048]{2,1,0:T(4,128)(2,1)S(1)}, u32[]{:S(2)}, u32[]{:S(2)}) collective-permute-start(bf16[1,4,2048]{2,1,0:T(4,128)(2,1)S(1)} %get-tuple-element.35), channel_id=1, source_target_pairs={{0,16},{1,17},{2,18},{3,19},{4,20},{5,21},{6,22},{7,23},{8,24},{9,... | collective-permute-start | bytes 49160 | tf_op jit(solution)/shard_map/ppermute | solution.py:22

commit v25 on v19

--- a/solution.py
+++ b/solution.py
@@ -69,9 +69,9 @@
     )(in_hbm(tokens), in_hbm(expert_ids), in_hbm(gate_probs))
 
 
-def stack_blocks(blocks):
-    def body(*refs):
-        for i, ref in enumerate(refs[:-1]):
+def stack_blocks(blocks, places):
+    def body(*refs):
+        for i, ref in zip(places, refs):
             refs[-1][i] = ref[...]
 
     return pl.pallas_call(
@@ -263,7 +263,8 @@
     units = w_up.shape[2]
     weights = lax.optimization_barrier((block, w_gate[0], w_up[0], w_down[0]))
     block, gate_weights, up_weights, down_weights = weights
-    near = stack_blocks([block] + [swap(block, 0, 4 * i) for i in range(1, high)])
+    places = [0] + [i for i in range(1, high) if i != 2] + [2]
+    near = stack_blocks([block] + [swap(block, 0, 4 * i) for i in places[1:]], places)
     if wide > 1:
         near = jnp.concatenate([near] + [swap(near, 2 * i, 0) for i in range(1, wide)])
     over_x, over_y = swap(near, 1, 0), swap(near, 0, 2)

time: 47.5 us -> 47.4 us (level)
  transfers between devices with their start and end apart: 19 -> 19, of which waited for: 14 -> 15; matrix products, arithmetic and copies ran while one was open for 0% -> 0% of each run, Pallas kernels for 8% -> 8%
where the time goes in v25:
time: 47.4 us; the launch traced here: 47.2 us
  starting transfers between devices  21.6 us (46%)
  waiting for transfers between devices  18.3 us (39%)
  Pallas kernels  6.95 us (15%)
    ppermute x19, starting transfers between devices, swap(): return lax.ppermute(value, ('dp',) + EXPERT, pairs)  21.6 us
    ppermute x19, waiting for transfers between devices, swap(): return lax.ppermute(value, ('dp',) + EXPERT, pairs)  18.3 us
    pallas_call x3, Pallas kernels, expand_rows(): pl.pallas_call(body, out_shape=jax.ShapeDtypeStruct((count, columns), row...  2.91 us
    pallas_call x5, Pallas kernels, contract_hidden(): pl.pallas_call(body, out_shape=jax.ShapeDtypeStruct((count, width), kind)...  2.25 us
  transfers between devices with their start and end apart: 19, of which 15 were waited for; matrix products, arithmetic and copies ran while one was open for 0% of the time, Pallas kernels for 8%

profile of v25, /device:TPU:0, one launch (start us, length us, event | category | flops | bytes accessed | tf_op | source)
XLA Modules:
  0.0 47.2 jit_solution(2920426615547455047)
XLA Ops:
  0.0 0.9 %pack_block.1.refs_0_ = bf16[4,4224]{1,0:T(4,128)(2,1)S(1)} custom-call(bf16[4,4096]{1,0:T(4,128)(2,1)} %tokens_ref.1, s32[4,8]{1,0:T(4,128)} %ids_ref.1, f32[4,8]{1,0:T(4,128)} %probs_ref.1), custom_call_target="tpu_custom_call" | custom-call | tf_op jit(solution)/shard_map/pack_block/pallas_call | solution.py:62
  0.9 4.1 %collective-permute-start.2 = (bf16[4,4224]{1,0:T(4,128)(2,1)S(1)}, bf16[4,4224]{1,0:T(4,128)(2,1)S(1)}, u32[]{:S(2)}, u32[]{:S(2)}) collective-permute-start(bf16[4,4224]{1,0:T(4,128)(2,1)S(1)} %pack_block.1.refs_0_), channel_id=1, source_target_pairs={{0,8},{1,9},{2,10},{3,11},{4,12},{5,13},{6,14},{7,15},{8,0},{9,1},... | collective-permute-start | bytes 101384 | tf_op jit(solution)/shard_map/ppermute | solution.py:22
  5.0 1.3 %collective-permute-start.1 = (bf16[4,4224]{1,0:T(4,128)(2,1)S(1)}, bf16[4,4224]{1,0:T(4,128)(2,1)S(1)}, u32[]{:S(2)}, u32[]{:S(2)}) collective-permute-start(bf16[4,4224]{1,0:T(4,128)(2,1)S(1)} %pack_block.1.refs_0_), channel_id=1, source_target_pairs={{0,12},{1,13},{2,14},{3,15},{4,8},{5,9},{6,10},{7,11},{8,4},{9,5},... | collective-permute-start | bytes 101384 | tf_op jit(solution)/shard_map/ppermute | solution.py:22
  6.3 0.2 collective-permute-start
  6.6 0.7 %collective-permute-done.2.refs_3_ = bf16[4,4224]{1,0:T(4,128)(2,1)S(1)} collective-permute-done((bf16[4,4224]{1,0:T(4,128)(2,1)S(1)}, bf16[4,4224]{1,0:T(4,128)(2,1)S(1)}, u32[]{:S(2)}, u32[]{:S(2)}) %collective-permute-start.2) | collective-permute-done | bytes 33824 | tf_op jit(solution)/shard_map/ppermute | solution.py:22
  7.2 3.5 %collective-permute-done.1.refs_2_ = bf16[4,4224]{1,0:T(4,128)(2,1)S(1)} collective-permute-done((bf16[4,4224]{1,0:T(4,128)(2,1)S(1)}, bf16[4,4224]{1,0:T(4,128)(2,1)S(1)}, u32[]{:S(2)}, u32[]{:S(2)}) %collective-permute-start.1) | collective-permute-done | bytes 33824 | tf_op jit(solution)/shard_map/ppermute | solution.py:22
  10.7 2.5 %collective-permute-start.3 = (bf16[4,4,4224]{2,1,0:T(4,128)(2,1)S(1)}, bf16[4,4,4224]{2,1,0:T(4,128)(2,1)S(1)}, u32[]{:S(2)}, u32[]{:S(2)}) collective-permute-start(bf16[4,4,4224]{2,1,0:T(4,128)(2,1)S(1)} %stack_blocks.1.refs_0_), channel_id=1, source_target_pairs={{0,18},{1,19},{2,16},{3,17},{4,22},{5,23},{6,20},{7,21},{8,26},{9,... | collective-permute-start | bytes 405512 | tf_op jit(solution)/shard_map/ppermute | solution.py:22
  13.2 0.5 %collective-permute-start.5 = (bf16[4,4,4224]{2,1,0:T(4,128)(2,1)S(1)}, bf16[4,4,4224]{2,1,0:T(4,128)(2,1)S(1)}, u32[]{:S(2)}, u32[]{:S(2)}) collective-permute-start(bf16[4,4,4224]{2,1,0:T(4,128)(2,1)S(1)} %stack_blocks.1.refs_0_), channel_id=1, source_target_pairs={{0,16},{1,17},{2,18},{3,19},{4,20},{5,21},{6,22},{7,23},{8,24},{9,... | collective-permute-start | bytes 405512 | tf_op jit(solution)/shard_map/ppermute | solution.py:22
  13.8 0.5 %collective-permute-start.4 = (bf16[4,4,4224]{2,1,0:T(4,128)(2,1)S(1)}, bf16[4,4,4224]{2,1,0:T(4,128)(2,1)S(1)}, u32[]{:S(2)}, u32[]{:S(2)}) collective-permute-start(bf16[4,4,4224]{2,1,0:T(4,128)(2,1)S(1)} %stack_blocks.1.refs_0_), channel_id=1, source_target_pairs={{0,2},{1,3},{2,0},{3,1},{4,6},{5,7},{6,4},{7,5},{8,10},{9,11},{10,... | collective-permute-start | bytes 405512 | tf_op jit(solution)/shard_map/ppermute | solution.py:22
  14.3 2.8 %collective-permute-done.3.refs_1_ = bf16[4,4,4224]{2,1,0:T(4,128)(2,1)S(1)} collective-permute-done((bf16[4,4,4224]{2,1,0:T(4,128)(2,1)S(1)}, bf16[4,4,4224]{2,1,0:T(4,128)(2,1)S(1)}, u32[]{:S(2)}, u32[]{:S(2)}) %collective-permute-start.3) | collective-permute-done | bytes 135200 | tf_op jit(solution)/shard_map/ppermute | solution.py:22
  17.1 0.1 join_rows.3
  17.2 0.1 collective-permute-start.6
  17.3 1.3 %collective-permute-done.5.refs_0_ = bf16[4,4,4224]{2,1,0:T(4,128)(2,1)S(1)} collective-permute-done((bf16[4,4,4224]{2,1,0:T(4,128)(2,1)S(1)}, bf16[4,4,4224]{2,1,0:T(4,128)(2,1)S(1)}, u32[]{:S(2)}, u32[]{:S(2)}) %collective-permute-start.5) | collective-permute-done | bytes 135200 | tf_op jit(solution)/shard_map/ppermute | solution.py:22
  18.6 0.1 collective-permute-start.8
  18.7 0.1 collective-permute-done.4.refs_0_
  18.8 0.4 collective-permute-start.7
  19.3 0.9 %collective-permute-done.7 = bf16[16,4224]{1,0:T(8,128)(2,1)S(1)} collective-permute-done((bf16[16,4224]{1,0:T(8,128)(2,1)S(1)}, bf16[16,4224]{1,0:T(8,128)(2,1)S(1)}, u32[]{:S(2)}, u32[]{:S(2)}) %collective-permute-start.7) | collective-permute-done | bytes 135200 | tf_op jit(solution)/shard_map/ppermute | solution.py:22
  20.3 0.0 slice-start
  20.3 1.1 %expand_rows.3.refs_0_ = bf16[128,384]{1,0:T(8,128)(2,1)S(1)} custom-call(bf16[128,4224]{1,0:T(8,128)(2,1)S(1)} %slice_dynamic-update-slice_fusion.rows_ref.refs_3_, bf16[4096,1024]{1,0:T(8,128)(2,1)S(1)} %bitcast.10, bf16[4096,1024]{1,0:T(8,128)(2,1)S(1)} %bitcast.13), custom_call_target="tpu_custom_call" | custom-call | bytes 49152 | tf_op jit(solution)/shard_map/expand_rows/pallas_call | solution.py:131
  21.4 0.0 slice-start.1
  21.5 1.6 %collective-permute-start.11 = (bf16[128,384]{1,0:T(8,128)(2,1)S(1)}, bf16[128,384]{1,0:T(8,128)(2,1)S(1)}, u32[]{:S(2)}, u32[]{:S(2)}) collective-permute-start(bf16[128,384]{1,0:T(8,128)(2,1)S(1)} %expand_rows.3.refs_0_), channel_id=1, source_target_pairs={{0,16},{1,17},{2,18},{3,19},{4,20},{5,21},{6,22},{7,23},{8,24},{9,... | collective-permute-start | bytes 294920 | tf_op jit(solution)/shard_map/ppermute | solution.py:22
  23.0 1.0 %expand_rows.4.refs_1_ = bf16[128,384]{1,0:T(8,128)(2,1)S(1)} custom-call(bf16[128,4224]{1,0:T(8,128)(2,1)S(1)} %slice_dynamic-update-slice_fusion.rows_ref.refs_3_, bf16[4096,1024]{1,0:T(8,128)(2,1)S(1)} %bitcast.11, bf16[4096,1024]{1,0:T(8,128)(2,1)S(1)} %bitcast.14), custom_call_target="tpu_custom_call" | custom-call | bytes 49152 | tf_op jit(solution)/shard_map/expand_rows/pallas_call | solution.py:131
  24.1 0.6 %collective-permute-start.10 = (bf16[128,384]{1,0:T(8,128)(2,1)S(1)}, bf16[128,384]{1,0:T(8,128)(2,1)S(1)}, u32[]{:S(2)}, u32[]{:S(2)}) collective-permute-start(bf16[128,384]{1,0:T(8,128)(2,1)S(1)} %expand_rows.4.refs_1_), channel_id=1, source_target_pairs={{0,16},{1,17},{2,18},{3,19},{4,20},{5,21},{6,22},{7,23},{8,24},{9,... | collective-permute-start | bytes 294920 | tf_op jit(solution)/shard_map/ppermute | solution.py:22
  24.7 0.8 %expand_rows.5.refs_2_ = bf16[128,256]{1,0:T(8,128)(2,1)S(1)} custom-call(bf16[128,4224]{1,0:T(8,128)(2,1)S(1)} %slice_dynamic-update-slice_fusion.rows_ref.refs_3_, bf16[4096,1024]{1,0:T(8,128)(2,1)S(1)} %bitcast.12, bf16[4096,1024]{1,0:T(8,128)(2,1)S(1)} %bitcast.15), custom_call_target="tpu_custom_call" | custom-call | bytes 32768 | tf_op jit(solution)/shard_map/expand_rows/pallas_call | solution.py:131
  25.5 1.5 %collective-permute-start.9 = (bf16[128,256]{1,0:T(8,128)(2,1)S(1)}, bf16[128,256]{1,0:T(8,128)(2,1)S(1)}, u32[]{:S(2)}, u32[]{:S(2)}) collective-permute-start(bf16[128,256]{1,0:T(8,128)(2,1)S(1)} %expand_rows.5.refs_2_), channel_id=1, source_target_pairs={{0,16},{1,17},{2,18},{3,19},{4,20},{5,21},{6,22},{7,23},{8,24},{9,... | collective-permute-start | bytes 196616 | tf_op jit(solution)/shard_map/ppermute | solution.py:22
  27.0 0.7 %contract_hidden.5.refs_2_ = f32[128,2048]{1,0:T(8,128)S(1)} custom-call(bf16[128,384]{1,0:T(8,128)(2,1)S(1)} %expand_rows.3.refs_0_, bf16[128,384]{1,0:T(8,128)(2,1)S(1)} %expand_rows.4.refs_1_, bf16[128,256]{1,0:T(8,128)(2,1)S(1)} %expand_rows.5.refs_2_, bf16[2048,2048]{1,0:T(8,128)(2,1)S(1)} %bitcast.5), custom_call_target="tpu_custom_call" | custom-call | bytes 262144 | tf_op jit(solution)/shard_map/contract_hidden/pallas_call | solution.py:192
  27.8 0.5 %contract_hidden.6.refs_2_ = f32[128,2048]{1,0:T(8,128)S(1)} custom-call(bf16[128,384]{1,0:T(8,128)(2,1)S(1)} %collective-permute-done.11.refs_0_, bf16[2048,2048]{1,0:T(8,128)(2,1)S(1)} %bitcast.6, f32[128,2048]{1,0:T(8,128)S(1)} %contract_hidden.5.refs_2_), custom_call_target="tpu_custom_call" | custom-call | bytes 262144 | tf_op jit(solution)/shard_map/contract_hidden/pallas_call | solution.py:192
  28.2 1.4 %collective-permute-done.10.refs_0_ = bf16[128,384]{1,0:T(8,128)(2,1)S(1)} collective-permute-done((bf16[128,384]{1,0:T(8,128)(2,1)S(1)}, bf16[128,384]{1,0:T(8,128)(2,1)S(1)}, u32[]{:S(2)}, u32[]{:S(2)}) %collective-permute-start.10) | collective-permute-done | bytes 98336 | tf_op jit(solution)/shard_map/ppermute | solution.py:22
  29.6 0.4 contract_hidden.7.refs_2_
  30.1 0.3 collective-permute-done.9.refs_0_
  30.3 0.3 contract_hidden.9
  30.6 0.1 collective-permute-start.12
  30.7 0.3 contract_hidden.8.refs_0_
  31.0 1.2 %collective-permute-done.12.refs_1_ = bf16[64,2048]{1,0:T(8,128)(2,1)S(1)} collective-permute-done((bf16[64,2048]{1,0:T(8,128)(2,1)S(1)}, bf16[64,2048]{1,0:T(8,128)(2,1)S(1)}, u32[]{:S(2)}, u32[]{:S(2)}) %collective-permute-start.12) | collective-permute-done | bytes 262176 | tf_op jit(solution)/shard_map/ppermute | solution.py:22
  32.2 0.1 sum_stage.2
  32.4 0.8 %collective-permute-start.13 = (bf16[4,4,2048]{2,1,0:T(4,128)(2,1)S(1)}, bf16[4,4,2048]{2,1,0:T(4,128)(2,1)S(1)}, u32[]{:S(2)}, u32[]{:S(2)}) collective-permute-start(bf16[4,4,2048]{2,1,0:T(4,128)(2,1)S(1)} %get-tuple-element.30), channel_id=1, source_target_pairs={{0,6},{1,7},{2,4},{3,5},{4,2},{5,3},{6,0},{7,1},{8,14},{9,15},{10,... | collective-permute-start | bytes 196616 | tf_op jit(solution)/shard_map/ppermute | solution.py:22
  33.2 1.7 %collective-permute-start.14 = (bf16[4,4,2048]{2,1,0:T(4,128)(2,1)S(1)}, bf16[4,4,2048]{2,1,0:T(4,128)(2,1)S(1)}, u32[]{:S(2)}, u32[]{:S(2)}) collective-permute-start(bf16[4,4,2048]{2,1,0:T(4,128)(2,1)S(1)} %get-tuple-element.31), channel_id=1, source_target_pairs={{0,4},{1,5},{2,6},{3,7},{4,0},{5,1},{6,2},{7,3},{8,12},{9,13},{10,... | collective-permute-start | bytes 196616 | tf_op jit(solution)/shard_map/ppermute | solution.py:22
  34.9 1.0 %collective-permute-start.15 = (bf16[4,4,2048]{2,1,0:T(4,128)(2,1)S(1)}, bf16[4,4,2048]{2,1,0:T(4,128)(2,1)S(1)}, u32[]{:S(2)}, u32[]{:S(2)}) collective-permute-start(bf16[4,4,2048]{2,1,0:T(4,128)(2,1)S(1)} %get-tuple-element.32), channel_id=1, source_target_pairs={{0,2},{1,3},{2,0},{3,1},{4,6},{5,7},{6,4},{7,5},{8,10},{9,11},{10,... | collective-permute-start | bytes 196616 | tf_op jit(solution)/shard_map/ppermute | solution.py:22
  35.9 2.4 %collective-permute-done.13.refs_1_ = bf16[4,4,2048]{2,1,0:T(4,128)(2,1)S(1)} collective-permute-done((bf16[4,4,2048]{2,1,0:T(4,128)(2,1)S(1)}, bf16[4,4,2048]{2,1,0:T(4,128)(2,1)S(1)}, u32[]{:S(2)}, u32[]{:S(2)}) %collective-permute-start.13) | collective-permute-done | bytes 65568 | tf_op jit(solution)/shard_map/ppermute | solution.py:22
  38.3 0.2 collective-permute-done.14.refs_2_
  38.4 0.8 %collective-permute-done.15.refs_3_ = bf16[4,4,2048]{2,1,0:T(4,128)(2,1)S(1)} collective-permute-done((bf16[4,4,2048]{2,1,0:T(4,128)(2,1)S(1)}, bf16[4,4,2048]{2,1,0:T(4,128)(2,1)S(1)}, u32[]{:S(2)}, u32[]{:S(2)}) %collective-permute-start.15) | collective-permute-done | bytes 65568 | tf_op jit(solution)/shard_map/ppermute | solution.py:22
  39.2 1.9 %collective-permute-start.16 = (bf16[1,4,2048]{2,1,0:T(4,128)(2,1)S(1)}, bf16[1,4,2048]{2,1,0:T(4,128)(2,1)S(1)}, u32[]{:S(2)}, u32[]{:S(2)}) collective-permute-start(bf16[1,4,2048]{2,1,0:T(4,128)(2,1)S(1)} %get-tuple-element.33), channel_id=1, source_target_pairs={{0,24},{1,25},{2,26},{3,27},{4,28},{5,29},{6,30},{7,31},{8,16},{9,... | collective-permute-start | bytes 49160 | tf_op jit(solution)/shard_map/ppermute | solution.py:22
  41.1 1.8 %collective-permute-start.17 = (bf16[1,4,2048]{2,1,0:T(4,128)(2,1)S(1)}, bf16[1,4,2048]{2,1,0:T(4,128)(2,1)S(1)}, u32[]{:S(2)}, u32[]{:S(2)}) collective-permute-start(bf16[1,4,2048]{2,1,0:T(4,128)(2,1)S(1)} %get-tuple-element.34), channel_id=1, source_target_pairs={{0,8},{1,9},{2,10},{3,11},{4,12},{5,13},{6,14},{7,15},{8,0},{9,1},... | collective-permute-start | bytes 49160 | tf_op jit(solution)/shard_map/ppermute | solution.py:22
  42.9 0.8 %collective-permute-start.18 = (bf16[1,4,2048]{2,1,0:T(4,128)(2,1)S(1)}, bf16[1,4,2048]{2,1,0:T(4,128)(2,1)S(1)}, u32[]{:S(2)}, u32[]{:S(2)}) collective-permute-start(bf16[1,4,2048]{2,1,0:T(4,128)(2,1)S(1)} %get-tuple-element.35), channel_id=1, source_target_pairs={{0,16},{1,17},{2,18},{3,19},{4,20},{5,21},{6,22},{7,23},{8,24},{9,... | collective-permute-start | bytes 49160 | tf_op jit(solution)/shard_map/ppermute | solution.py:22
  43.7 1.1 %collective-permute-done.16.refs_0_ = bf16[1,4,2048]{2,1,0:T(4,128)(2,1)S(1)} collective-permute-done((bf16[1,4,2048]{2,1,0:T(4,128)(2,1)S(1)}, bf16[1,4,2048]{2,1,0:T(4,128)(2,1)S(1)}, u32[]{:S(2)}, u32[]{:S(2)}) %collective-permute-start.16) | collective-permute-done | bytes 16416 | tf_op jit(solution)/shard_map/ppermute | solution.py:22
  44.8 0.9 %collective-permute-done.17.refs_1_ = bf16[1,4,2048]{2,1,0:T(4,128)(2,1)S(1)} collective-permute-done((bf16[1,4,2048]{2,1,0:T(4,128)(2,1)S(1)}, bf16[1,4,2048]{2,1,0:T(4,128)(2,1)S(1)}, u32[]{:S(2)}, u32[]{:S(2)}) %collective-permute-start.17) | collective-permute-done | bytes 16416 | tf_op jit(solution)/shard_map/ppermute | solution.py:22
  45.7 0.9 %collective-permute-done.18.refs_2_ = bf16[1,4,2048]{2,1,0:T(4,128)(2,1)S(1)} collective-permute-done((bf16[1,4,2048]{2,1,0:T(4,128)(2,1)S(1)}, bf16[1,4,2048]{2,1,0:T(4,128)(2,1)S(1)}, u32[]{:S(2)}, u32[]{:S(2)}) %collective-permute-start.18) | collective-permute-done | bytes 16416 | tf_op jit(solution)/shard_map/ppermute | solution.py:22
  46.6 0.6 %finish.1 = bf16[4,4096]{1,0:T(4,128)(2,1)} custom-call(bf16[1,4,2048]{2,1,0:T(4,128)(2,1)S(1)} %collective-permute-done.16.refs_0_, bf16[1,4,2048]{2,1,0:T(4,128)(2,1)S(1)} %collective-permute-done.17.refs_1_, bf16[1,4,2048]{2,1,0:T(4,128)(2,1)S(1)} %collective-permute-done.18.refs_2_, f32[1,4,2048]{2,1,0:T(4,128)S(1)} %get-tuple-element.36.refs_3_), custom_call_target="tpu_custom_call" | custom-call | tf_op jit(solution)/shard_map/finish/pallas_call | solution.py:247
  (23 shorter events, 0.3 us)
Async XLA Ops:
  0.9 6.4 %collective-permute-start.2 = (bf16[4,4224]{1,0:T(4,128)(2,1)S(1)}, bf16[4,4224]{1,0:T(4,128)(2,1)S(1)}, u32[]{:S(2)}, u32[]{:S(2)}) collective-permute-start(bf16[4,4224]{1,0:T(4,128)(2,1)S(1)} %pack_block.1.refs_0_), channel_id=1, source_target_pairs={{0,8},{1,9},{2,10},{3,11},{4,12},{5,13},{6,14},{7,15},{8,0},{9,1},... | collective-permute-start | bytes 101384 | tf_op jit(solution)/shard_map/ppermute | solution.py:22
  5.0 5.7 %collective-permute-start.1 = (bf16[4,4224]{1,0:T(4,128)(2,1)S(1)}, bf16[4,4224]{1,0:T(4,128)(2,1)S(1)}, u32[]{:S(2)}, u32[]{:S(2)}) collective-permute-start(bf16[4,4224]{1,0:T(4,128)(2,1)S(1)} %pack_block.1.refs_0_), channel_id=1, source_target_pairs={{0,12},{1,13},{2,14},{3,15},{4,8},{5,9},{6,10},{7,11},{8,4},{9,5},... | collective-permute-start | bytes 101384 | tf_op jit(solution)/shard_map/ppermute | solution.py:22
  6.3 4.4 %collective-permute-start = (bf16[4,4224]{1,0:T(4,128)(2,1)S(1)}, bf16[4,4224]{1,0:T(4,128)(2,1)S(1)}, u32[]{:S(2)}, u32[]{:S(2)}) collective-permute-start(bf16[4,4224]{1,0:T(4,128)(2,1)S(1)} %pack_block.1.refs_0_), channel_id=1, source_target_pairs={{0,4},{1,5},{2,6},{3,7},{4,0},{5,1},{6,2},{7,3},{8,12},{9,13},{10,... | collective-permute-start | bytes 101384 | tf_op jit(solution)/shard_map/ppermute | solution.py:22
  10.7 9.6 %copy-start = (bf16[1,4096,1024]{2,1,0:T(8,128)(2,1)S(1)}, bf16[1,4096,1024]{2,1,0:T(8,128)(2,1)}, u32[]{:S(2)}) copy-start(bf16[1,4096,1024]{2,1,0:T(8,128)(2,1)} %param.9) | copy-start | bytes 25165828
  10.7 9.6 %copy-start.1 = (bf16[1,4096,1024]{2,1,0:T(8,128)(2,1)S(1)}, bf16[1,4096,1024]{2,1,0:T(8,128)(2,1)}, u32[]{:S(2)}) copy-start(bf16[1,4096,1024]{2,1,0:T(8,128)(2,1)} %param.10) | copy-start | bytes 25165828
  10.7 6.4 %collective-permute-start.3 = (bf16[4,4,4224]{2,1,0:T(4,128)(2,1)S(1)}, bf16[4,4,4224]{2,1,0:T(4,128)(2,1)S(1)}, u32[]{:S(2)}, u32[]{:S(2)}) collective-permute-start(bf16[4,4,4224]{2,1,0:T(4,128)(2,1)S(1)} %stack_blocks.1.refs_0_), channel_id=1, source_target_pairs={{0,18},{1,19},{2,16},{3,17},{4,22},{5,23},{6,20},{7,21},{8,26},{9,... | collective-permute-start | bytes 405512 | tf_op jit(solution)/shard_map/ppermute | solution.py:22
  13.2 5.3 %collective-permute-start.5 = (bf16[4,4,4224]{2,1,0:T(4,128)(2,1)S(1)}, bf16[4,4,4224]{2,1,0:T(4,128)(2,1)S(1)}, u32[]{:S(2)}, u32[]{:S(2)}) collective-permute-start(bf16[4,4,4224]{2,1,0:T(4,128)(2,1)S(1)} %stack_blocks.1.refs_0_), channel_id=1, source_target_pairs={{0,16},{1,17},{2,18},{3,19},{4,20},{5,21},{6,22},{7,23},{8,24},{9,... | collective-permute-start | bytes 405512 | tf_op jit(solution)/shard_map/ppermute | solution.py:22
  13.8 5.0 %collective-permute-start.4 = (bf16[4,4,4224]{2,1,0:T(4,128)(2,1)S(1)}, bf16[4,4,4224]{2,1,0:T(4,128)(2,1)S(1)}, u32[]{:S(2)}, u32[]{:S(2)}) collective-permute-start(bf16[4,4,4224]{2,1,0:T(4,128)(2,1)S(1)} %stack_blocks.1.refs_0_), channel_id=1, source_target_pairs={{0,2},{1,3},{2,0},{3,1},{4,6},{5,7},{6,4},{7,5},{8,10},{9,11},{10,... | collective-permute-start | bytes 405512 | tf_op jit(solution)/shard_map/ppermute | solution.py:22
  17.2 2.1 %collective-permute-start.6 = (bf16[32,4224]{1,0:T(8,128)(2,1)S(1)}, bf16[32,4224]{1,0:T(8,128)(2,1)S(1)}, u32[]{:S(2)}, u32[]{:S(2)}) collective-permute-start(bf16[32,4224]{1,0:T(8,128)(2,1)S(1)} %join_rows.3), channel_id=1, source_target_pairs={{0,1},{1,0},{2,3},{3,2},{4,5},{5,4},{6,7},{7,6},{8,9},{9,8},{10,11... | collective-permute-start | bytes 811016 | tf_op jit(solution)/shard_map/ppermute | solution.py:22
  18.6 1.7 %collective-permute-start.8 = (bf16[16,4224]{1,0:T(8,128)(2,1)S(1)}, bf16[16,4224]{1,0:T(8,128)(2,1)S(1)}, u32[]{:S(2)}, u32[]{:S(2)}) collective-permute-start(bf16[16,4224]{1,0:T(8,128)(2,1)S(1)} %join_rows.5), channel_id=1, source_target_pairs={{0,1},{1,0},{2,3},{3,2},{4,5},{5,4},{6,7},{7,6},{8,9},{9,8},{10,11... | collective-permute-start | bytes 405512 | tf_op jit(solution)/shard_map/ppermute | solution.py:22
  18.8 1.4 %collective-permute-start.7 = (bf16[16,4224]{1,0:T(8,128)(2,1)S(1)}, bf16[16,4224]{1,0:T(8,128)(2,1)S(1)}, u32[]{:S(2)}, u32[]{:S(2)}) collective-permute-start(bf16[16,4224]{1,0:T(8,128)(2,1)S(1)} %join_rows.4), channel_id=1, source_target_pairs={{0,1},{1,0},{2,3},{3,2},{4,5},{5,4},{6,7},{7,6},{8,9},{9,8},{10,11... | collective-permute-start | bytes 405512 | tf_op jit(solution)/shard_map/ppermute | solution.py:22
  20.3 6.7 %slice-start = ((s8[8388608]{0:T(1024)(128)(4,1)}), s8[4194304]{0:T(1024)(128)(4,1)S(1)}, s32[]{:S(2)}) async-start(s8[8388608]{0:T(1024)(128)(4,1)} %bitcast.3), calls=%async_computation | async-start | bytes 8388608
  21.4 5.6 %slice-start.1 = ((s8[8388608]{0:T(1024)(128)(4,1)}), s8[4194304]{0:T(1024)(128)(4,1)S(1)}, s32[]{:S(2)}) async-start(s8[8388608]{0:T(1024)(128)(4,1)} %bitcast.3), calls=%async_computation.1 | async-start | bytes 8388608
  21.5 6.3 %collective-permute-start.11 = (bf16[128,384]{1,0:T(8,128)(2,1)S(1)}, bf16[128,384]{1,0:T(8,128)(2,1)S(1)}, u32[]{:S(2)}, u32[]{:S(2)}) collective-permute-start(bf16[128,384]{1,0:T(8,128)(2,1)S(1)} %expand_rows.3.refs_0_), channel_id=1, source_target_pairs={{0,16},{1,17},{2,18},{3,19},{4,20},{5,21},{6,22},{7,23},{8,24},{9,... | collective-permute-start | bytes 294920 | tf_op jit(solution)/shard_map/ppermute | solution.py:22
  24.1 5.6 %collective-permute-start.10 = (bf16[128,384]{1,0:T(8,128)(2,1)S(1)}, bf16[128,384]{1,0:T(8,128)(2,1)S(1)}, u32[]{:S(2)}, u32[]{:S(2)}) collective-permute-start(bf16[128,384]{1,0:T(8,128)(2,1)S(1)} %expand_rows.4.refs_1_), channel_id=1, source_target_pairs={{0,16},{1,17},{2,18},{3,19},{4,20},{5,21},{6,22},{7,23},{8,24},{9,... | collective-permute-start | bytes 294920 | tf_op jit(solution)/shard_map/ppermute | solution.py:22
  25.5 4.8 %collective-permute-start.9 = (bf16[128,256]{1,0:T(8,128)(2,1)S(1)}, bf16[128,256]{1,0:T(8,128)(2,1)S(1)}, u32[]{:S(2)}, u32[]{:S(2)}) collective-permute-start(bf16[128,256]{1,0:T(8,128)(2,1)S(1)} %expand_rows.5.refs_2_), channel_id=1, source_target_pairs={{0,16},{1,17},{2,18},{3,19},{4,20},{5,21},{6,22},{7,23},{8,24},{9,... | collective-permute-start | bytes 196616 | tf_op jit(solution)/shard_map/ppermute | solution.py:22
  30.6 1.6 %collective-permute-start.12 = (bf16[64,2048]{1,0:T(8,128)(2,1)S(1)}, bf16[64,2048]{1,0:T(8,128)(2,1)S(1)}, u32[]{:S(2)}, u32[]{:S(2)}) collective-permute-start(bf16[64,2048]{1,0:T(8,128)(2,1)S(1)} %contract_hidden.9), channel_id=1, source_target_pairs={{0,1},{1,0},{2,3},{3,2},{4,5},{5,4},{6,7},{7,6},{8,9},{9,8},{10,11... | collective-permute-start | bytes 786440 | tf_op jit(solution)/shard_map/ppermute | solution.py:22
  32.4 5.9 %collective-permute-start.13 = (bf16[4,4,2048]{2,1,0:T(4,128)(2,1)S(1)}, bf16[4,4,2048]{2,1,0:T(4,128)(2,1)S(1)}, u32[]{:S(2)}, u32[]{:S(2)}) collective-permute-start(bf16[4,4,2048]{2,1,0:T(4,128)(2,1)S(1)} %get-tuple-element.30), channel_id=1, source_target_pairs={{0,6},{1,7},{2,4},{3,5},{4,2},{5,3},{6,0},{7,1},{8,14},{9,15},{10,... | collective-permute-start | bytes 196616 | tf_op jit(solution)/shard_map/ppermute | solution.py:22
  33.2 5.2 %collective-permute-start.14 = (bf16[4,4,2048]{2,1,0:T(4,128)(2,1)S(1)}, bf16[4,4,2048]{2,1,0:T(4,128)(2,1)S(1)}, u32[]{:S(2)}, u32[]{:S(2)}) collective-permute-start(bf16[4,4,2048]{2,1,0:T(4,128)(2,1)S(1)} %get-tuple-element.31), channel_id=1, source_target_pairs={{0,4},{1,5},{2,6},{3,7},{4,0},{5,1},{6,2},{7,3},{8,12},{9,13},{10,... | collective-permute-start | bytes 196616 | tf_op jit(solution)/shard_map/ppermute | solution.py:22
  34.9 4.3 %collective-permute-start.15 = (bf16[4,4,2048]{2,1,0:T(4,128)(2,1)S(1)}, bf16[4,4,2048]{2,1,0:T(4,128)(2,1)S(1)}, u32[]{:S(2)}, u32[]{:S(2)}) collective-permute-start(bf16[4,4,2048]{2,1,0:T(4,128)(2,1)S(1)} %get-tuple-element.32), channel_id=1, source_target_pairs={{0,2},{1,3},{2,0},{3,1},{4,6},{5,7},{6,4},{7,5},{8,10},{9,11},{10,... | collective-permute-start | bytes 196616 | tf_op jit(solution)/shard_map/ppermute | solution.py:22
  39.2 5.6 %collective-permute-start.16 = (bf16[1,4,2048]{2,1,0:T(4,128)(2,1)S(1)}, bf16[1,4,2048]{2,1,0:T(4,128)(2,1)S(1)}, u32[]{:S(2)}, u32[]{:S(2)}) collective-permute-start(bf16[1,4,2048]{2,1,0:T(4,128)(2,1)S(1)} %get-tuple-element.33), channel_id=1, source_target_pairs={{0,24},{1,25},{2,26},{3,27},{4,28},{5,29},{6,30},{7,31},{8,16},{9,... | collective-permute-start | bytes 49160 | tf_op jit(solution)/shard_map/ppermute | solution.py:22
  41.1 4.6 %collective-permute-start.17 = (bf16[1,4,2048]{2,1,0:T(4,128)(2,1)S(1)}, bf16[1,4,2048]{2,1,0:T(4,128)(2,1)S(1)}, u32[]{:S(2)}, u32[]{:S(2)}) collective-permute-start(bf16[1,4,2048]{2,1,0:T(4,128)(2,1)S(1)} %get-tuple-element.34), channel_id=1, source_target_pairs={{0,8},{1,9},{2,10},{3,11},{4,12},{5,13},{6,14},{7,15},{8,0},{9,1},... | collective-permute-start | bytes 49160 | tf_op jit(solution)/shard_map/ppermute | solution.py:22
  42.9 3.7 %collective-permute-start.18 = (bf16[1,4,2048]{2,1,0:T(4,128)(2,1)S(1)}, bf16[1,4,2048]{2,1,0:T(4,128)(2,1)S(1)}, u32[]{:S(2)}, u32[]{:S(2)}) collective-permute-start(bf16[1,4,2048]{2,1,0:T(4,128)(2,1)S(1)} %get-tuple-element.35), channel_id=1, source_target_pairs={{0,16},{1,17},{2,18},{3,19},{4,20},{5,21},{6,22},{7,23},{8,24},{9,... | collective-permute-start | bytes 49160 | tf_op jit(solution)/shard_map/ppermute | solution.py:22
